TPU v7x, 32 devices: a whole 2x2x4 slice. The times are simulated.
32 devices in a mesh: seq: 4 (over y, core), tensor: 8 (over z, x).
Axes of the slice: x: 2, y: 2, z: 4, core: 2. Of those that a mesh axis runs over, the one named last changes fastest.
Arguments:
- tokens: bfloat16 [2048, 3584], P('seq', 'tensor'), may hold values from -6 to 6
- w_zx: bfloat16 [2, 3584, 1024], P(None, None, 'tensor'), may hold values from -0.09375 to 0.09375
- w_bc: bfloat16 [3584, 128], replicated, may hold values from -0.09375 to 0.09375
- w_dt: bfloat16 [3584, 16], P(None, 'tensor'), may hold values from -0.09375 to 0.09375
- dt_bias: float32 [16], P('tensor'), may hold values from -2 to 0.5
- a_rate: float32 [16], P('tensor'), may hold values from 0.00024414062 to 0.05
- d_skip: float32 [16], P('tensor'), may hold values from 0.3 to 1.5
- conv_x: float32 [4, 1024], P(None, 'tensor'), may hold values from -3 to 3
- conv_bc: float32 [4, 128], replicated, may hold values from -3 to 3
- norm_gain: float32 [1024], P('tensor'), may hold values from 0.25 to 1.75
- w_out: bfloat16 [1024, 3584], P('tensor'), may hold values from -0.1875 to 0.1875
- segments: int32 [2048], P('seq'), may hold values from 0 to 5, never falling along the last dimension, each value on 1 to 1024 neighbouring positions
Outputs:
- mixed: bfloat16 [2048, 3584], P(('seq', 'tensor'))
Inputs may be any that keep to these rules, and one draw needn't show every extreme that they name: `segments`: prompt ids never fall along the tokens, so each prompt's tokens are contiguous.
All inputs are finite; a program needn't handle non-finite values.
Results may differ from a plain program's by a relative error of at most 0.02.
Values may be sent and summed in bfloat16 or wider, within the bound.
No kernel may reach another device: no remote copies, remote signals or barrier semaphores. Data moves between devices by JAX's collectives and lax.ppermute only.
A program may use at most 64 MiB of HBM per device.

v0:
```python
import jax
import jax.numpy as jnp
from jax import lax
from jax.sharding import PartitionSpec as P

BLOCK = 256


HIGHEST_PREC = lax.Precision.HIGHEST
NORM_EPS = 1e-05


def from_behind(block, axis, distance):
    devices = range(lax.axis_size(axis))
    route = [(i - distance, i) for i in devices if i - distance in devices]
    return lax.ppermute(block, axis, route)


def entering(array, axis, join, neutral):
    place = lax.axis_index(axis)
    gathered = jax.tree.map(
        lambda a, kind: lax.all_gather(a.astype(kind), axis),
        array,
        jax.tree.map(lambda a: jnp.bfloat16 if a.dtype == jnp.float32 else a.dtype, array),
    )
    state = jax.tree.map(lambda a, e: jnp.zeros_like(a) + jnp.asarray(e, a.dtype), array, neutral)

    def one(turn, state):
        return join(
            state,
            jax.tree.map(
                lambda a, own: lax.dynamic_index_in_dim(a, turn, 0, False).astype(own.dtype),
                gathered,
                array,
            ),
        )

    return lax.fori_loop(0, place, one, state)


def conv_tail(extended, seg_ext, taps, tok_rows):
    conv_len = taps.shape[0]
    seg_now = seg_ext[conv_len - 1 :]
    conv_sum = taps[conv_len - 1] * extended[conv_len - 1 :]
    for offset in range(1, conv_len):
        earlier = extended[conv_len - 1 - offset : conv_len - 1 - offset + tok_rows]
        seg_then = seg_ext[conv_len - 1 - offset : conv_len - 1 - offset + tok_rows]
        conv_sum = conv_sum + taps[conv_len - 1 - offset] * jnp.where(
            (seg_then == seg_now)[:, None], earlier, 0.0
        )
    return jax.nn.silu(conv_sum)


def ssd_block(carry, block):
    state, last_seg = carry
    inner_x, step_size, logdec, bmat, cmat, seg_ids = block
    cum_decay = jnp.cumsum(logdec, axis=0)
    position = jnp.arange(seg_ids.shape[0])
    visible = (seg_ids[:, None] == seg_ids[None, :]) & (position[:, None] >= position[None, :])
    gap_decay = jnp.where(
        visible[:, :, None], cum_decay[:, None, :] - cum_decay[None, :, :], -jnp.inf
    )
    scores = jnp.dot(cmat, bmat.T, precision=HIGHEST_PREC)
    weights = jnp.exp(gap_decay) * scores[:, :, None] * step_size[None, :, :]
    block_out = jnp.einsum("tsh,shp->thp", weights, inner_x, precision=HIGHEST_PREC)
    enter = jnp.where((seg_ids == last_seg)[:, None], jnp.exp(cum_decay), 0.0)
    block_out = block_out + enter[:, :, None] * jnp.einsum(
        "tn,hpn->thp", cmat, state, precision=HIGHEST_PREC
    )
    tail_weight = (
        jnp.where(
            (seg_ids == seg_ids[-1])[:, None], jnp.exp(cum_decay[-1][None, :] - cum_decay), 0.0
        )
        * step_size
    )
    carry_keep = jnp.where(seg_ids[-1] == last_seg, jnp.exp(cum_decay[-1]), 0.0)
    new_state = carry_keep[:, None, None] * state + jnp.einsum(
        "sh,shp,sn->hpn", tail_weight, inner_x, bmat, precision=HIGHEST_PREC
    )
    return ((new_state, seg_ids[-1]), block_out)


def link_states(earlier, later):
    gain_a, state_a, first_a, last_a = earlier
    gain_b, state_b, first_b, last_b = later
    joined = (first_b == last_a) | (last_a < 0.0) | (first_b < 0.0)
    passing = jnp.where(joined, gain_b, 0.0)
    merged_gain = gain_a * passing
    merged_state = passing[:, None, None] * state_a + state_b
    merged_first = jnp.where(first_a < 0.0, first_b, first_a)
    merged_last = jnp.where(last_b < 0.0, last_a, last_b)
    return (merged_gain, merged_state, merged_first, merged_last)


def local(
    tokens, w_zx, w_bc, w_dt, dt_bias, a_rate, d_skip, conv_x, conv_bc, norm_gain, w_out, segments
):
    tok_rows = tokens.shape[0]
    inner_w = w_zx.shape[2]
    heads = dt_bias.shape[0]
    head_size = inner_w // heads
    state_w = w_bc.shape[1] // 2
    rim_len = conv_x.shape[0] - 1
    piece = lax.all_gather(tokens, "tensor", axis=1, tiled=True)
    gate_rows = w_zx[0]
    inner_rows = w_zx[1]
    gate_sum = jnp.dot(piece, gate_rows, preferred_element_type=jnp.float32)
    inner_sum = jnp.dot(piece, inner_rows, preferred_element_type=jnp.float32)
    bc_sum = jnp.dot(piece, w_bc, preferred_element_type=jnp.float32)
    dt_raw = jnp.dot(piece, w_dt, preferred_element_type=jnp.float32)
    gate_proj = gate_sum.astype(jnp.bfloat16)
    inner_proj = inner_sum.astype(jnp.bfloat16)
    bc_proj = bc_sum.astype(jnp.bfloat16)
    rim_inner, rim_bc, rim_seg = from_behind(
        (
            inner_proj[tok_rows - rim_len :],
            bc_proj[tok_rows - rim_len :],
            segments[tok_rows - rim_len :].astype(jnp.bfloat16),
        ),
        "seq",
        1,
    )
    seg_ext = jnp.concatenate([rim_seg.astype(jnp.int32), segments], 0)
    conv_inner = conv_tail(
        jnp.concatenate([rim_inner.astype(jnp.float32), inner_proj.astype(jnp.float32)], 0),
        seg_ext,
        conv_x,
        tok_rows,
    )
    conv_state = conv_tail(
        jnp.concatenate([rim_bc.astype(jnp.float32), bc_proj.astype(jnp.float32)], 0),
        seg_ext,
        conv_bc,
        tok_rows,
    )
    bmat = conv_state[:, :state_w]
    cmat = conv_state[:, state_w:]
    step_size = jax.nn.softplus(dt_raw + dt_bias)
    logdec = -a_rate * step_size
    inner_heads = conv_inner.reshape(tok_rows, heads, head_size)
    nblocks = tok_rows // BLOCK
    blocks = (
        inner_heads.reshape(nblocks, BLOCK, heads, head_size),
        step_size.reshape(nblocks, BLOCK, heads),
        logdec.reshape(nblocks, BLOCK, heads),
        bmat.reshape(nblocks, BLOCK, state_w),
        cmat.reshape(nblocks, BLOCK, state_w),
        segments.reshape(nblocks, BLOCK),
    )
    start_carry = (jnp.zeros((heads, head_size, state_w), jnp.float32), jnp.array(-1, jnp.int32))
    (local_state, _), block_outs = lax.scan(ssd_block, start_carry, blocks)
    cum_device = jnp.cumsum(logdec, axis=0)
    device_gain = jnp.where(segments[0] == segments[-1], jnp.exp(cum_device[-1]), 0.0)
    seg_float = segments.astype(jnp.float32)
    element = (device_gain, local_state, seg_float[:1], seg_float[-1:])
    identity = (
        jnp.ones((heads,), jnp.float32),
        jnp.zeros_like(local_state),
        jnp.full((1,), -1.0, jnp.float32),
        jnp.full((1,), -1.0, jnp.float32),
    )
    incoming = entering(element, "seq", link_states, identity)
    state_in = incoming[1]
    last_in = incoming[3]
    enter = jnp.where((seg_float == last_in[0])[:, None], jnp.exp(cum_device), 0.0)
    ssd_out = block_outs.reshape(tok_rows, heads, head_size)
    ssd_out = ssd_out + enter[:, :, None] * jnp.einsum(
        "tn,hpn->thp", cmat, state_in, precision=HIGHEST_PREC
    )
    ssd_out = ssd_out + d_skip[None, :, None] * inner_heads
    gated = ssd_out.reshape(tok_rows, inner_w) * jax.nn.silu(gate_proj.astype(jnp.float32))
    local_squares = jnp.sum(gated * gated, axis=1)
    total_squares = lax.psum(local_squares, "tensor")
    scale = lax.rsqrt(total_squares / (inner_w * lax.axis_size("tensor")) + NORM_EPS)
    normed = (gated * scale[:, None] * norm_gain).astype(jnp.bfloat16)
    return lax.psum_scatter(
        jnp.dot(normed, w_out, preferred_element_type=jnp.float32).astype(jnp.bfloat16),
        "tensor",
        scatter_dimension=0,
        tiled=True,
    )


def solution(mesh):
    in_specs = (
        P("seq", "tensor"),
        P(None, None, "tensor"),
        P(),
        P(None, "tensor"),
        P("tensor"),
        P("tensor"),
        P("tensor"),
        P(None, "tensor"),
        P(),
        P("tensor"),
        P("tensor", None),
        P("seq"),
    )
    out_specs = P(("seq", "tensor"), None)
    return jax.shard_map(local, mesh=mesh, in_specs=in_specs, out_specs=out_specs, check_vma=False)
```

profile of v0, /device:TPU:0, one launch (start us, length us, event | category | flops | bytes accessed | tf_op | source)
XLA Modules:
  0.0 239.0 jit_solution(7363890159231566819)
XLA Ops:
  6.5 0.7 all-gather.6.cloned.1.call-update
  7.3 0.8 convert_convert_fusion
  8.2 1.2 dynamic-slice
  9.4 0.6 fusion.82
  10.0 1.4 dynamic-update-slice
  11.3 1.3 dynamic-update-slice.1
  12.7 2.3 collective-permute-start
  15.0 8.3 %all-reduce.2 = (bf16[4]{0:T(256)(128)(2,1)S(1)}, bf16[4]{0:T(256)(128)(2,1)S(1)}) all-reduce(bf16[4]{0:T(256)(128)(2,1)S(1)} %dynamic-update-slice, bf16[4]{0:T(256)(128)(2,1)S(1)} %dynamic-update-slice.1), channel_id=2, replica_groups=mesh['seq'=4,'tensor'=8] {'seq'}, use_global_device_ids=true, to_apply=%add | all-reduce | flops 8 | bytes 32
  23.3 0.7 reshape.139
  24.0 0.7 neg.20
  24.7 1.4 fusion.81
  27.4 0.8 slice_bitcast_fusion.8
  28.2 0.8 slice_bitcast_fusion.4
  29.1 0.8 pad_add_fusion
  29.8 0.8 slice_compare_fusion.2
  30.6 48.5 %all-gather.6.cloned.1.call-done = bf16[512,3584]{0,1:T(8,128)(2,1)} async-done(((bf16[512,448]{0,1:T(8,128)(2,1)}), bf16[512,3584]{0,1:T(8,128)(2,1)}) %all-gather.6.cloned.1.call-update) | async-done | bytes 3670032 | tf_op jit(solution)/shard_map/all_gather | solution.py:104
  79.1 2.7 %broadcast_multiply_fusion = (f32[512,2]{0,1:T(2,128)S(1)}, f32[512,2]{0,1:T(2,128)S(1)}, f32[512,2]{0,1:T(2,128)S(1)}) fusion(f32[2]{0:T(128)S(1)} %neg.20, f32[2]{0:T(128)} %param.20, bf16[512,3584]{0,1:T(8,128)(2,1)} %all-gather.6.cloned.1.call-done, bf16[3584,2]{0,1:T(2,128)(2,1)} %param.19), kind=kOutput, calls=%fused_computation.121 | convolution fusion | flops 7348224 | bytes 3696656 | tf_op jit(solution)/shard_map/dot_general | solution.py:110
  81.8 0.1 copy.71
  81.9 3.6 %fusion.83 = (f32[512,128]{1,0:T(8,128)S(1)}, bf16[512,128]{1,0:T(8,128)(2,1)S(1)}) fusion(bf16[512,3584]{0,1:T(8,128)(2,1)} %all-gather.6.cloned.1.call-done, bf16[2,3584,128]{2,1,0:T(8,128)(2,1)} %param.17), kind=kOutput, calls=%fused_computation.144 | convolution fusion | flops 469893120 | bytes 4980736 | tf_op jit(solution)/shard_map/dot_general | solution.py:108
  85.5 1.3 collective-permute-start.1
  86.8 1.1 fusion.84
  88.0 4.1 %collective-permute-start.2 = (bf16[3,128]{1,0:T(4,128)(2,1)S(1)}, bf16[3,128]{1,0:T(4,128)(2,1)S(1)}, u32[]{:S(2)}, u32[]{:S(2)}) collective-permute-start(bf16[3,128]{1,0:T(4,128)(2,1)S(1)} %slice.157), channel_id=1, source_target_pairs={{0,8},{8,16},{16,24},{1,9},{9,17},{17,25},{2,10},{10,18},{18,26},{... | collective-permute-start | bytes 2312 | tf_op jit(solution)/shard_map/ppermute | solution.py:16
  92.2 0.6 reduce-window.16
  92.8 0.2 slice_reduce_fusion.1
  93.0 0.2 reduce-window.17
  93.2 0.2 fusion.78
  93.4 5.0 %all-gather.3 = bf16[4,1,2]{2,1,0:T(2,128)(2,1)S(1)} all-gather(bf16[1,1,2]{2,1,0:T(2,128)(2,1)S(1)} %bitcast.197), channel_id=1, replica_groups=mesh['seq'=4,'tensor'=8] {'seq'}, dimensions={0}, use_global_device_ids=true | all-gather | bytes 20 | tf_op jit(solution)/shard_map/all_gather | solution.py:22
  98.6 0.3 divide_multiply_fusion.1
  98.9 0.3 reshape.172
  99.4 0.2 copy.59
  99.6 0.3 divide_multiply_fusion
  100.3 16.2 %while.31 = (s32[]{:T(128)}, f32[2,64,64]{2,1,0:T(8,128)S(1)}, s32[]{:T(128)}, f32[2,256,2,64]{1,0,3,2:T(2,128)S(1)}, s32[2,256]{1,0:T(2,128)S(1)}, /*index=5*/f...) while((s32[]{:T(128)}, f32[2,64,64]{2,1,0:T(8,128)S(1)}, ...), condition=%wide.region_3.4_spmd.clone, body=%wide.region_0.3_spmd.clone.sunk | while | flops 202246672 | bytes 2326889 | solution.py:151
  100.3 0.6 reduce-window.26
  100.9 0.2 slice_reduce_fusion.3
  101.1 0.2 reduce-window.27
  101.4 0.1 copy.95
  101.5 0.6 dynamic-slice.4
  102.1 0.6 broadcast_compare_fusion.3
  102.8 0.1 select_multiply_fusion.2
  103.0 0.3 convolution_multiply_fusion.3
  104.0 0.3 convolution_add_fusion.3
  104.3 0.4 fusion.112
  105.0 0.8 fusion.114
  105.7 0.1 copy.100
  105.9 1.9 dynamic_update_slice.6
  108.4 0.6 reduce-window.26
  109.0 0.2 slice_reduce_fusion.3
  109.2 0.2 reduce-window.27
  109.4 0.1 copy.95
  109.6 0.6 dynamic-slice.4
  110.2 0.6 broadcast_compare_fusion.3
  110.8 0.1 select_multiply_fusion.2
  111.1 0.3 convolution_multiply_fusion.3
  112.1 0.3 convolution_add_fusion.3
  112.4 0.4 fusion.112
  113.1 0.8 fusion.114
  114.0 1.9 dynamic_update_slice.6
  116.5 0.2 reshape.144
  116.7 5.4 %all-gather.1 = bf16[8,64,64]{2,1,0:T(8,128)(2,1)S(1)} all-gather(bf16[2,64,64]{2,1,0:T(8,128)(2,1)S(1)} %convert_element_type.85), channel_id=3, replica_groups=mesh['seq'=4,'tensor'=8] {'seq'}, dimensions={0}, use_global_device_ids=true | all-gather | bytes 81920 | tf_op jit(solution)/shard_map/all_gather | solution.py:22
  122.2 0.5 fusion.38
  122.8 3.5 %multiply_reduce_fusion = (f32[512]{0:T(512)S(1)}, f32[512,128]{1,0:T(8,128)S(1)}) fusion(f32[512,128]{1,0:T(8,128)S(1)} %copy.68, bf16[512,3584]{0,1:T(8,128)(2,1)} %all-gather.6.cloned.1.call-done, bf16[2,3584,128]{2,1,0:T(8,128)(2,1)} %param.17), kind=kOutput, calls=%fused_computation.101 | convolution fusion | flops 470351360 | bytes 5113856 | tf_op jit(solution)/shard_map/dot_general | solution.py:107
  126.4 18.9 %psum.7 = f32[512]{0:T(512)S(1)} all-reduce(f32[512]{0:T(512)S(1)} %get-tuple-element.290), channel_id=1, replica_groups=mesh['seq'=4,'tensor'=8] {'tensor'}, use_global_device_ids=true, to_apply=%region_9.10 | all-reduce | flops 512 | bytes 4096 | tf_op jit(solution)/shard_map/psum | solution.py:173
  145.2 3.0 %convolution_convert_fusion = bf16[512,3584]{1,0:T(8,128)(2,1)} fusion(bf16[128,3584]{1,0:T(8,128)(2,1)S(1)} %copy-done, f32[512,128]{1,0:T(8,128)S(1)} %get-tuple-element.291, f32[128]{0:T(128)S(1)} %copy-done.4, f32[512]{0:T(512)S(1)} %add_rsqrt_fusion), kind=kOutput, calls=%fused_computation.58 | convolution fusion | flops 471793664 | bytes 4852224 | tf_op jit(solution)/shard_map/dot_general | solution.py:177
  148.2 83.9 %reduce-scatter.2.cloned.1.call-done = bf16[64,3584]{1,0:T(8,128)(2,1)} async-done(((bf16[512,3584]{1,0:T(8,128)(2,1)}), bf16[64,3584]{1,0:T(8,128)(2,1)}) %reduce-scatter.2.cloned.1.call-update) | async-done | bytes 458768 | tf_op jit(solution)/shard_map/reduce_scatter | solution.py:176
  (67 shorter events, 2.3 us)
Async XLA Ops:
  6.5 138.7 %copy-start = (bf16[128,3584]{1,0:T(8,128)(2,1)S(1)}, bf16[128,3584]{1,0:T(8,128)(2,1)}, u32[]{:S(2)}) copy-start(bf16[128,3584]{1,0:T(8,128)(2,1)} %param.26) | copy-start | bytes 2752516
  6.5 72.5 %all-gather.6.cloned.1.call-start = ((), (), s32[]{:S(2)}) async-start(), calls=%async_computation.1 | async-start | bytes 4128768 | tf_op jit(solution)/shard_map/all_gather | solution.py:104
  7.3 224.9 %reduce-scatter.2.cloned.1.call-start = ((), (), s32[]{:S(2)}) async-start(), calls=%async_computation.2 | async-start | bytes 4128768 | tf_op jit(solution)/shard_map/reduce_scatter | solution.py:176
  12.7 16.4 %collective-permute-start = (bf16[3]{0:T(256)(128)(2,1)S(1)}, bf16[3]{0:T(256)(128)(2,1)S(1)}, u32[]{:S(2)}, u32[]{:S(2)}) collective-permute-start(bf16[3]{0:T(256)(128)(2,1)S(1)} %slice.118), channel_id=1, source_target_pairs={{0,8},{8,16},{16,24},{1,9},{9,17},{17,25},{2,10},{10,18},{18,26},{... | collective-permute-start | bytes 26 | tf_op jit(solution)/shard_map/ppermute | solution.py:16
  81.8 5.1 %copy-start.2 = (bf16[3584,128]{1,0:T(8,128)(2,1)S(1)}, bf16[3584,128]{1,0:T(8,128)(2,1)}, u32[]{:S(2)}) copy-start(bf16[3584,128]{1,0:T(8,128)(2,1)} %param.18) | copy-start | bytes 2752516
  81.9 4.9 %copy-start.1 = (bf16[512,3584]{0,1:T(8,128)(2,1)S(1)}, bf16[512,3584]{0,1:T(8,128)(2,1)}, u32[]{:S(2)}) copy-start(bf16[512,3584]{0,1:T(8,128)(2,1)} %all-gather.6.cloned.1.call-done) | copy-start | bytes 11010052
  85.5 13.1 %collective-permute-start.1 = (bf16[3,128]{1,0:T(4,128)(2,1)S(1)}, bf16[3,128]{1,0:T(4,128)(2,1)S(1)}, u32[]{:S(2)}, u32[]{:S(2)}) collective-permute-start(bf16[3,128]{1,0:T(4,128)(2,1)S(1)} %slice.152), channel_id=1, source_target_pairs={{0,8},{8,16},{16,24},{1,9},{9,17},{17,25},{2,10},{10,18},{18,26},{... | collective-permute-start | bytes 2312 | tf_op jit(solution)/shard_map/ppermute | solution.py:16
  88.0 11.6 %collective-permute-start.2 = (bf16[3,128]{1,0:T(4,128)(2,1)S(1)}, bf16[3,128]{1,0:T(4,128)(2,1)S(1)}, u32[]{:S(2)}, u32[]{:S(2)}) collective-permute-start(bf16[3,128]{1,0:T(4,128)(2,1)S(1)} %slice.157), channel_id=1, source_target_pairs={{0,8},{8,16},{16,24},{1,9},{9,17},{17,25},{2,10},{10,18},{18,26},{... | collective-permute-start | bytes 2312 | tf_op jit(solution)/shard_map/ppermute | solution.py:16
  100.3 21.9 %copy-start.3 = (s32[512]{0:T(512)S(1)}, s32[512]{0:T(512)}, u32[]{:S(2)}) copy-start(s32[512]{0:T(512)} %param.27) | copy-start | bytes 6148
  100.3 21.9 %copy-start.5 = (f32[2]{0:T(128)S(1)}, f32[2]{0:T(128)}, u32[]{:S(2)}) copy-start(f32[2]{0:T(128)} %param.22) | copy-start | bytes 28
  122.7 22.6 %copy-start.4 = (f32[128]{0:T(128)S(1)}, f32[128]{0:T(128)}, u32[]{:S(2)}) copy-start(f32[128]{0:T(128)} %param.25) | copy-start | bytes 1540
Sparse Core Ops, SparseCore 0:
  9.5 69.4 all-gather.5
  148.4 83.7 reduce-scatter.1
where the time goes:
time: 240 us; the launch traced here: 239 us
  waiting for transfers between devices  133 us (55%)
  blocking collectives  37.6 us (16%)
  matrix products  17.9 us (7%)
  local copies, waits for them, and re-layouts  16.6 us (7%)
  between operations  15 us (6%)
  other arithmetic  8.18 us (3%)
  starting transfers between devices  7.79 us (3%)
  loops' own time  2.73 us (1%)
    reduce_scatter x1, waiting for transfers between devices, local(): lax.psum_scatter(jnp.dot(normed, w_out, preferred_element_type=jnp.float3...  83.9 us
    all_gather x1, waiting for transfers between devices, local(): piece = lax.all_gather(tokens, 'tensor', axis=1, tiled=True)  48.5 us
    psum x1, blocking collectives, local(): total_squares = lax.psum(local_squares, 'tensor')  18.9 us
    all_gather x2, blocking collectives, entering(): lax.all_gather(a.astype(kind), axis)  10.5 us
    unnamed x1, blocking collectives  8.3 us
    ppermute x3, starting transfers between devices, from_behind(): return lax.ppermute(block, axis, route)  7.75 us
  transfers between devices with their start and end apart: 5, of which 2 were waited for; matrix products, arithmetic and copies ran while one was open for 6% of the time, Pallas kernels for 0%

commit v1 on v0

v1 whole, which is shorter than its diff:
```python
import functools

import jax
import jax.numpy as jnp
import numpy as np
from jax import lax
from jax.experimental import pallas as pl
from jax.experimental.pallas import tpu as pltpu
from jax.sharding import PartitionSpec as P

NORM_EPS = 1e-05
F32 = jnp.float32
BF16 = jnp.bfloat16
VMEM = pl.BlockSpec(memory_space=pltpu.VMEM)
SMEM = pl.BlockSpec(memory_space=pltpu.SMEM)
ANY = pl.BlockSpec(memory_space=pl.ANY)
HALO = 8


def ring_order(n):
    width = 1
    while 2 * width * (2 * width) * 2 <= 2 * n and width * width * 2 < n:
        width *= 2
    depth = n // width
    if width == 1:
        return list(range(n))
    order = [z * width for z in range(depth)]
    for back, z in enumerate(reversed(range(depth))):
        row = [z * width + x for x in range(1, width)]
        order += row if back % 2 == 0 else row[::-1]
    return order


def ring_shift(block, order, step):
    n = len(order)
    return lax.ppermute(block, "tensor", [(order[i], order[(i + step) % n]) for i in range(n)])


def ring_gather(block, order):
    n = len(order)
    forth = back = block
    for step in range(1, n // 2):
        forth, back = ring_shift(forth, order, 1), ring_shift(back, order, -1)
        yield [(-step, forth), (step, back)]
    half = block.shape[0] // 2
    yield [(n // 2, (ring_shift(forth[:half], order, 1), ring_shift(back[half:], order, -1)))]


def pack(rows):
    count, width = rows.shape
    groups = 1
    while (groups * width) % 128:
        groups *= 2
    return jnp.concatenate(jnp.split(rows, groups, 0), 1)


def unpack(packed, width):
    return jnp.concatenate(jnp.split(packed, packed.shape[1] // width, 1), 0)


def silu(v):
    return v / (1.0 + jnp.exp(-v))


def dot(a, b, dims=((1,), (0,))):
    return lax.dot_general(a.astype(BF16), b.astype(BF16), (dims, ((), ())), preferred_element_type=F32)


def conv(ext, seg_ext, taps, rows):
    size = taps.shape[0]
    seg_now = seg_ext[HALO : HALO + rows]
    total = taps[size - 1 : size] * ext[HALO : HALO + rows]
    for offset in range(1, size):
        same = seg_ext[HALO - offset : HALO - offset + rows] == seg_now
        total = total + taps[size - 1 - offset : size - offset] * jnp.where(
            same, ext[HALO - offset : HALO - offset + rows], 0.0
        )
    return silu(total)


def prefix_sum(values):
    rows = values.shape[0]
    lower = lax.broadcasted_iota(jnp.int32, (rows, rows), 0) >= lax.broadcasted_iota(jnp.int32, (rows, rows), 1)
    lower = jnp.where(lower, 1.0, 0.0).astype(BF16)
    total = jnp.zeros(values.shape, F32)
    rest = values
    parts = []
    for _ in range(3):
        part = rest.astype(BF16)
        parts.append(part)
        rest = rest - part.astype(F32)
    for part in reversed(parts):
        total = total + jnp.dot(lower, part, preferred_element_type=F32)
    return total


def block_front(ext_x, ext_bc, seg_ext, dt_raw, taps_x, taps_bc, bias, rate, rows, seg_enter, seg_leave):
    conv_x = conv(ext_x, seg_ext, taps_x, rows)
    conv_bc = conv(ext_bc, seg_ext, taps_bc, rows)
    seg = seg_ext[HALO : HALO + rows]
    shifted = dt_raw + bias
    step_size = jnp.maximum(shifted, 0.0) + jnp.log1p(jnp.exp(-jnp.abs(shifted)))
    cum = prefix_sum(-rate * step_size)
    scaled = conv_x * step_size
    last = cum[rows - 1 : rows]
    tail = jnp.where(seg == seg_leave, jnp.exp(last - cum), 0.0)
    state_w = conv_bc.shape[1] // 2
    state = dot(conv_bc, tail * scaled, ((0,), (0,)))[:state_w]
    enter = jnp.where(seg == seg_enter, jnp.exp(cum), 0.0)
    return conv_x, conv_bc, cum, scaled, state, enter, last


def block_inner(conv_bc, cum, scaled, seg_col, seg_row, heads):
    rows, width = scaled.shape
    state_w = conv_bc.shape[1] // 2
    head_w = width // heads
    scores = dot(conv_bc[:, state_w:], conv_bc[:, :state_w], ((1,), (1,)))
    later = lax.broadcasted_iota(jnp.int32, (rows, rows), 0) >= lax.broadcasted_iota(jnp.int32, (rows, rows), 1)
    visible = (seg_col == seg_row) & later
    cum_rows = cum.T
    lane = lax.broadcasted_iota(jnp.int32, (rows, width), 1)
    result = jnp.zeros((rows, width), F32)
    scaled = scaled.astype(BF16)
    for head in range(heads):
        at = head * head_w
        gap = jnp.where(visible, cum[:, at : at + 1] - cum_rows[at : at + 1, :], -jnp.inf)
        part = dot(jnp.exp(gap) * scores, scaled)
        result = jnp.where((lane >= at) & (lane < at + head_w), part, result)
    return result


def later_block(heads, width, rows, lead, proj, seg_ext, seg_row, taps_x, taps_bc, bias, rate, skip,
                out, bc_out, enter_out, state_out, gate_out, ext_x, ext_bc):
    start = lead - HALO
    rounded = proj[start:, : 3 * width].astype(BF16).astype(F32)
    gate_out[...] = silu(rounded[HALO:, :width])
    ext_x[...] = rounded[:, width : 2 * width]
    ext_bc[...] = rounded[:, 2 * width : 3 * width]
    seg_enter = seg_ext[HALO - 1 : HALO]
    seg_leave = seg_ext[HALO + rows - 1 : HALO + rows]
    conv_x, conv_bc, cum, scaled, state, enter, last = block_front(
        ext_x, ext_bc, seg_ext, proj[lead:, 3 * width :], taps_x, taps_bc[...], bias[...], rate[...], rows, seg_enter, seg_leave
    )
    out[...] = block_inner(conv_bc, cum, scaled, seg_ext[HALO:], seg_row[...], heads) + skip[...] * conv_x
    bc_out[...] = conv_bc
    enter_out[...] = enter
    keep = jnp.where(seg_enter == seg_leave, jnp.exp(last), 0.0)
    state_w = state.shape[0]
    state_out[:state_w] = state
    state_out[state_w : state_w + 1] = keep
    state_out[state_w + 1 : state_w + 2] = last
    state_out[state_w + 2 :] = jnp.zeros((state_out.shape[0] - state_w - 2, width), F32)


def first_front(width, rows, proj_a, proj_b, halo, seg_ext, seg_last, state_b, taps_x, taps_bc, bias, rate,
                conv_out, bc_out, cum_out, scaled_out, enter_out, state_out, message, ext_x, ext_bc, dt):
    own = proj_a.shape[0]
    ext_x[:HALO] = halo[:, :width].astype(F32)
    ext_bc[:HALO] = halo[:, width:].astype(F32)
    ext_x[HALO : HALO + own] = proj_a[:, width : 2 * width].astype(BF16).astype(F32)
    ext_bc[HALO : HALO + own] = proj_a[:, 2 * width : 3 * width].astype(BF16).astype(F32)
    ext_x[HALO + own :] = proj_b[: rows - own, width : 2 * width].astype(BF16).astype(F32)
    ext_bc[HALO + own :] = proj_b[: rows - own, 2 * width : 3 * width].astype(BF16).astype(F32)
    dt[:own] = proj_a[:, 3 * width :]
    dt[own:] = proj_b[: rows - own, 3 * width :]
    seg_enter = seg_ext[HALO : HALO + 1]
    seg_leave = seg_ext[HALO + rows - 1 : HALO + rows]
    conv_x, conv_bc, cum, scaled, state, enter, last = block_front(
        ext_x, ext_bc, seg_ext, dt[...], taps_x, taps_bc[...], bias[...], rate[...], rows, seg_enter, seg_leave
    )
    conv_out[...] = conv_x
    bc_out[...] = conv_bc
    cum_out[...] = cum
    scaled_out[...] = scaled
    enter_out[...] = enter
    keep = jnp.where(seg_enter == seg_leave, jnp.exp(last), 0.0)
    state_w = state.shape[0]
    state_out[:state_w] = state
    state_out[state_w : state_w + 1] = keep
    state_out[state_w + 1 :] = jnp.zeros((state_out.shape[0] - state_w - 1, width), F32)
    message[:state_w] = state_b[state_w : state_w + 1] * state + state_b[:state_w]
    message[state_w : state_w + 1] = last + state_b[state_w + 1 : state_w + 2]
    message[state_w + 1 : state_w + 2] = jnp.broadcast_to(seg_last[...].astype(F32), (1, width))
    message[state_w + 2 :] = jnp.zeros((message.shape[0] - state_w - 2, width), F32)


def first_inner(heads, width, rows, conv_x, conv_bc, cum, scaled, proj_a, proj_b, seg_col, seg_row, skip, out, gate_out):
    own = proj_a.shape[0]
    gate_out[:own] = silu(proj_a[:, :width].astype(BF16).astype(F32))
    gate_out[own:] = silu(proj_b[: rows - own, :width].astype(BF16).astype(F32))
    out[...] = (
        block_inner(conv_bc[...], cum[...], scaled[...], seg_col[HALO:], seg_row[...], heads) + skip[...] * conv_x[...]
    )


def finish(count, rows, seg_first, out_a, gate_a, bc_a, enter_a, state_a, out_b, gate_b, bc_b, enter_b, *rest):
    messages, gated = rest[:count], rest[count]
    state_w = bc_a.shape[1] // 2
    entering = jnp.zeros((state_w, out_a.shape[1]), F32)
    decay = jnp.zeros((1, out_a.shape[1]), F32)
    first = seg_first[...].astype(F32)
    for message in messages:
        passes = jnp.where(message[state_w + 1 : state_w + 2] == first, jnp.exp(decay), 0.0)
        entering = entering + passes * message[:state_w]
        decay = decay + message[state_w : state_w + 1]
    second = state_a[state_w : state_w + 1] * entering + state_a[:state_w]
    gated[:rows] = ((out_a[...] + enter_a[...] * dot(bc_a[:, state_w:], entering)) * gate_a[...]).astype(BF16)
    gated[rows:] = ((out_b[...] + enter_b[...] * dot(bc_b[:, state_w:], second)) * gate_b[...]).astype(BF16)


def project_out(parts, where, place, core, gated, *rest):
    pieces, (out, held, sems) = rest[:parts], rest[parts:]
    copies = []
    for k, (side, block, row) in enumerate(where):
        size = pieces[k].shape[0]
        copies.append(pltpu.make_async_copy(pieces[k], held.at[side, block, pl.ds(row, size)], sems.at[k]))
        copies[-1].start()
    blocks, rows, width = gated.shape
    squares = jnp.zeros((rows, width), F32)
    for block in range(blocks):
        value = gated[block].astype(F32)
        squares = squares + value * value
    scale = lax.rsqrt(jnp.sum(squares, axis=1, keepdims=True) / (blocks * width) + NORM_EPS)
    columns = held.shape[3]
    sums = [jnp.zeros((rows, columns), F32)] * 2
    for block in range(blocks):
        for k, (side, at, _) in enumerate(where):
            if at == block:
                copies[k].wait()
        value = gated[place[block]]
        for side in range(2):
            sums[side] = sums[side] + jnp.dot(value, held[side, block], preferred_element_type=F32)
    sums = [(s * scale).astype(BF16) for s in sums]
    is_first = core[0] == 0
    out[:, :columns] = jnp.where(is_first, sums[0], sums[1])
    out[:, columns:] = jnp.where(is_first, sums[1], sums[0])


def call(body, outs, scratch=(), vmem=48, flops=10**7, **kw):
    return pl.pallas_call(
        body,
        out_shape=outs,
        scratch_shapes=list(scratch),
        compiler_params=pltpu.CompilerParams(vmem_limit_bytes=vmem << 20),
        cost_estimate=pl.CostEstimate(flops=flops, bytes_accessed=1 << 21, transcendentals=1 << 17),
        **kw,
    )


def local(
    tokens, w_zx, w_bc, w_dt, dt_bias, a_rate, d_skip, conv_x, conv_bc, norm_gain, w_out, segments
):
    tok_rows, feat = tokens.shape
    width = w_zx.shape[2]
    heads = dt_bias.shape[0]
    head_w = width // heads
    state_w = w_bc.shape[1] // 2
    model = w_zx.shape[1]
    n_seq, n_tensor = lax.axis_size("seq"), lax.axis_size("tensor")
    seq_at, tensor_at = lax.axis_index("seq"), lax.axis_index("tensor")
    rows = tok_rows // 2
    lead = 32
    shape = lambda *s, kind=F32: jax.ShapeDtypeStruct(s, kind)

    order = ring_order(n_tensor)
    sources = np.zeros((n_tensor, n_tensor), np.int32)
    for i, device in enumerate(order):
        for distance in range(n_tensor):
            sources[device, distance] = order[(i + distance) % n_tensor]
    source = lax.dynamic_index_in_dim(jnp.asarray(sources), tensor_at, 0, False)

    spread = lambda v: jnp.repeat(v, head_w, axis=-1)
    weights = jnp.concatenate([w_zx[0], w_zx[1], w_bc, spread(w_dt)], 1).reshape(n_tensor, feat, 4 * width)

    def weight_of(distance):
        return lax.dynamic_index_in_dim(weights, source[distance % n_tensor], 0, False)

    def project(chunk):
        packed = pack(chunk)
        total = jnp.dot(chunk, weight_of(0), preferred_element_type=F32)
        rests = []
        for arrived in ring_gather(packed, order):
            for distance, part in arrived:
                if isinstance(part, tuple):
                    part = jnp.concatenate(part, 0)
                total = total + jnp.dot(unpack(part, feat), weight_of(distance), preferred_element_type=F32)
            rests.append(arrived)
        return total, rests

    split = rows - lead
    proj_b, steps_b = project(tokens[split:])
    first_chunk, _ = lax.optimization_barrier((tokens[:split], steps_b[-2][0][1]))
    proj_a, steps_a = project(first_chunk)

    ahead = [(i, i + 1) for i in range(n_seq - 1)]
    seg_halo = lax.ppermute(segments[tok_rows - HALO :], "seq", ahead)
    seg_all = jnp.concatenate([seg_halo, segments])[:, None]
    seg_ext_a, seg_ext_b = seg_all[: HALO + rows], seg_all[rows:]
    seg_row_a, seg_row_b = segments[None, :rows], segments[None, rows:]
    seg_first, seg_last = segments[None, :1], segments[None, tok_rows - 1 :]
    halo = lax.ppermute(proj_b[lead + rows - HALO :, width : 3 * width].astype(BF16), "seq", ahead)
    bias, rate, skip = spread(dt_bias)[None], spread(a_rate)[None], spread(d_skip)[None]

    msg_rows = state_w + 8
    block = shape(rows, width)
    ext = pltpu.VMEM((HALO + rows, width), F32)
    out_b, bc_b, enter_b, state_b, gate_b = call(
        functools.partial(later_block, heads, width, rows, lead),
        [block, block, block, shape(msg_rows, width), block],
        [ext, ext],
    )(proj_b, seg_ext_b, seg_row_b, conv_x, conv_bc, bias, rate, skip)
    cx_a, bc_a, cum_a, scaled_a, enter_a, state_a, message = call(
        functools.partial(first_front, width, rows),
        [block] * 5 + [shape(msg_rows, width)] * 2,
        [ext, ext, pltpu.VMEM((rows, width), F32)],
    )(proj_a, proj_b, halo, seg_ext_a, seg_last, state_b, conv_x, conv_bc, bias, rate)
    messages = [
        lax.ppermute(message, "seq", [(i, i + far) for i in range(n_seq - far)]) for far in range(1, n_seq)
    ]
    out_a, gate_a = call(functools.partial(first_inner, heads, width, rows), [block, block])(
        cx_a, bc_a, cum_a, scaled_a, proj_a, proj_b, seg_ext_a, seg_row_a, skip
    )
    gated = call(
        functools.partial(finish, len(messages), rows), shape(tok_rows, width, kind=BF16)
    )(seg_first, out_a, gate_a, bc_a, enter_a, state_a, out_b, gate_b, bc_b, enter_b, *messages)

    core = seq_at % 2
    scaled_out = (w_out.astype(F32) * norm_gain[:, None]).astype(BF16)
    columns = model // 2
    own_half = lax.dynamic_slice_in_dim(scaled_out, core * columns, columns, 1)
    other_half = lax.dynamic_slice_in_dim(scaled_out, (1 - core) * columns, columns, 1)
    own_first, _ = lax.optimization_barrier((own_half, steps_a[-2][0][1]))
    swap = [(i, i ^ 1) for i in range(n_seq)]
    pieces, where = [own_half, other_half], [(0, 0, 0), (1, 0, 0)]
    for arrived in ring_gather(own_first, order):
        for distance, part in arrived:
            row = 0
            for part in part if isinstance(part, tuple) else (part,):
                pieces += [part, lax.ppermute(part, "seq", swap)]
                where += [(side, distance % n_tensor, row) for side in range(2)]
                row += part.shape[0]

    mine = lax.all_to_all(gated.reshape(n_tensor, tok_rows // n_tensor, width), "tensor", 0, 0)
    return call(
        functools.partial(project_out, len(pieces), tuple(where)),
        shape(tok_rows // n_tensor, model, kind=BF16),
        [pltpu.VMEM((2, n_tensor, width, columns), BF16), pltpu.SemaphoreType.DMA((len(pieces),))],
        in_specs=[SMEM, SMEM, VMEM] + [ANY] * len(pieces),
        flops=10**9,
    )(source, core[None], mine, *pieces)


def solution(mesh):
    in_specs = (
        P("seq", "tensor"),
        P(None, None, "tensor"),
        P(),
        P(None, "tensor"),
        P("tensor"),
        P("tensor"),
        P("tensor"),
        P(None, "tensor"),
        P(),
        P("tensor"),
        P("tensor", None),
        P("seq"),
    )
    out_specs = P(("seq", "tensor"), None)
    return jax.shard_map(local, mesh=mesh, in_specs=in_specs, out_specs=out_specs, check_vma=False)
```

time: 240 us -> 171 us (0.71)
  waiting for transfers between devices: 133 us -> 65.9 us
  blocking collectives: 37.6 us -> 0 us
  starting transfers between devices: 7.79 us -> 39.3 us
  Pallas kernels: 0 us -> 11 us
  matrix products: 17.9 us -> 9.42 us
  local copies, waits for them, and re-layouts: 16.6 us -> 23.8 us
  other arithmetic: 8.18 us -> 4.33 us
  loops' own time: 2.73 us -> 0 us
    reduce_scatter x1 -> x0, waiting for transfers between devices: 83.9 us -> none  [local(): lax.psum_scatter(jnp.dot(normed, w_out, preferred_element_type=jnp.float3...]
    ppermute x3 -> x37, waiting for transfers between devices: 0.01 us -> 59.2 us  [the longest x24 58.9 us: ring_shift(): lax.ppermute(block, 'tensor', [(order[i], order[(i + step) % n]) for i in...]
    all_gather x1 -> x0, waiting for transfers between devices: 48.5 us -> none  [local(): piece = lax.all_gather(tokens, 'tensor', axis=1, tiled=True)]
    ppermute x3 -> x37, starting transfers between devices: 7.75 us -> 34.3 us  [the longest x24 25.9 us: ring_shift(): lax.ppermute(block, 'tensor', [(order[i], order[(i + step) % n]) for i in...]
    psum x1 -> x0, blocking collectives: 18.9 us -> none  [local(): total_squares = lax.psum(local_squares, 'tensor')]
    pallas_call x0 -> x5, Pallas kernels: none -> 11 us  [the longest x1 6.72 us: local(): call(functools.partial(project_out, len(pieces), tuple(where)), shape(tok...]
    all_gather x2 -> x0, blocking collectives: 10.5 us -> none  [entering(): lax.all_gather(a.astype(kind), axis)]
    dot_general x14 -> x16, matrix products: 17.9 us -> 9.42 us  [the longest x14 8.46 us: project(): jnp.dot(unpack(part, feat), weight_of(distance), preferred_element_type=F32)]
  transfers between devices with their start and end apart: 5 -> 38, of which waited for: 2 -> 16; matrix products, arithmetic and copies ran while one was open for 6% -> 17% of each run, Pallas kernels for 0% -> 2%
where the time goes in v1:
time: 171 us; the launch traced here: 170 us
  waiting for transfers between devices  65.9 us (39%)
  starting transfers between devices  39.3 us (23%)
  local copies, waits for them, and re-layouts  23.8 us (14%)
  between operations  15.9 us (9%)
  Pallas kernels  11 us (6%)
  matrix products  9.42 us (6%)
  other arithmetic  4.33 us (3%)
    ppermute x24, waiting for transfers between devices, ring_shift(): lax.ppermute(block, 'tensor', [(order[i], order[(i + step) % n]) for i in...  58.9 us
    ppermute x24, starting transfers between devices, ring_shift(): lax.ppermute(block, 'tensor', [(order[i], order[(i + step) % n]) for i in...  25.9 us
    dot_general x14, matrix products, project(): jnp.dot(unpack(part, feat), weight_of(distance), preferred_element_type=F32)  8.46 us
    unnamed x34, local copies, waits for them, and re-layouts  7.2 us
    all_to_all x1, waiting for transfers between devices, local(): lax.all_to_all(gated.reshape(n_tensor, tok_rows // n_tensor, width), 'ten...  6.76 us
    pallas_call x1, Pallas kernels, local(): call(functools.partial(project_out, len(pieces), tuple(where)), shape(tok...  6.72 us
    all_to_all x1, starting transfers between devices, local(): lax.all_to_all(gated.reshape(n_tensor, tok_rows // n_tensor, width), 'ten...  4.99 us
    concatenate x2, local copies, waits for them, and re-layouts, local(): jnp.concatenate([w_zx[0], w_zx[1], w_bc, spread(w_dt)], 1)  4.02 us
  transfers between devices with their start and end apart: 38, of which 16 were waited for; matrix products, arithmetic and copies ran while one was open for 17% of the time, Pallas kernels for 2%

profile of v1, /device:TPU:0, one launch (start us, length us, event | category | flops | bytes accessed | tf_op | source)
XLA Modules:
  0.0 169.6 jit_solution(1068472200292294414)
XLA Ops:
  0.0 1.2 fusion.134
  1.3 0.8 pad_maximum_fusion.1
  2.1 2.9 %collective-permute-start.11 = (bf16[144,896]{0,1:T(8,128)(2,1)}, bf16[144,896]{0,1:T(8,128)(2,1)}, u32[]{:S(2)}, u32[]{:S(2)}) collective-permute-start(bf16[144,896]{0,1:T(8,128)(2,1)} %pad_maximum_fusion.1), channel_id=1, source_target_pairs={{0,1},{2,0},{4,2},{6,4},{7,6},{5,7},{3,5},{1,3},{8,9},{10,8},{12,1... | collective-permute-start | bytes 774152 | tf_op jit(solution)/shard_map/ppermute | solution.py:36
  5.1 0.8 slice.122
  5.9 1.4 collective-permute-start.17
  7.3 0.7 constant_dynamic-slice_fusion.2
  8.0 0.7 fusion.144
  10.1 1.6 fusion.127
  11.7 1.0 broadcast_in_dim.31
  12.8 2.3 %concatenate.73 = bf16[8,448,128]{1,0,2:T(8,128)(2,1)S(1)} reshape(bf16[3584,2,64]{0,2,1:T(8,128)(2,1)} %broadcast_in_dim.31) | data formatting | bytes 1835008 | tf_op jit(solution)/shard_map/concatenate | solution.py:273
  15.1 1.7 %copy.21 = bf16[8,448,128]{2,1,0:T(8,128)(2,1)} copy(bf16[8,448,128]{1,0,2:T(8,128)(2,1)S(1)} %concatenate.73) | data formatting | bytes 1835008 | tf_op jit(solution)/shard_map/concatenate | solution.py:273
  17.5 1.7 %pad_maximum_fusion = bf16[8,448,512]{2,1,0:T(8,128)(2,1)S(1)} fusion(bf16[8,448,128]{2,1,0:T(8,128)(2,1)} %copy.21, bf16[8,448,128]{2,1,0:T(8,128)(2,1)} %bitcast.69, bf16[8,448,128]{2,1,0:T(8,128)(2,1)S(1)} %bitcast.68, bf16[8,448,128]{2,1,0:T(8,128)(2,1)S(1)} %bitcast.67), kind=kLoop, calls=%fused_computation | loop fusion | flops 14680064 | bytes 7340032 | tf_op jit(solution)/shard_map/concatenate | solution.py:273
  19.2 1.8 %copy-done.8 = bf16[8,448,512]{2,1,0:T(8,128)(2,1)} copy-done((bf16[8,448,512]{2,1,0:T(8,128)(2,1)}, bf16[8,448,512]{2,1,0:T(8,128)(2,1)S(1)}, u32[]{:S(2)}) %copy-start.8) | copy-done | bytes 3670040
  21.7 1.4 multiply_convert_fusion
  37.8 1.8 %collective-permute-start.12 = (bf16[144,896]{0,1:T(8,128)(2,1)}, bf16[144,896]{0,1:T(8,128)(2,1)S(1)}, u32[]{:S(2)}, u32[]{:S(2)}) collective-permute-start(bf16[144,896]{0,1:T(8,128)(2,1)} %collective-permute-done.11), channel_id=1, source_target_pairs={{0,1},{2,0},{4,2},{6,4},{7,6},{5,7},{3,5},{1,3},{8,9},{10,8},{12,1... | collective-permute-start | bytes 774152 | tf_op jit(solution)/shard_map/ppermute | solution.py:36
  39.6 1.1 fusion.131
  40.7 1.5 fusion.24
  42.2 1.1 fusion.130
  43.7 1.5 fusion.3
  45.2 4.6 %collective-permute-done.12 = bf16[144,896]{0,1:T(8,128)(2,1)S(1)} collective-permute-done((bf16[144,896]{0,1:T(8,128)(2,1)}, bf16[144,896]{0,1:T(8,128)(2,1)S(1)}, u32[]{:S(2)}, u32[]{:S(2)}) %collective-permute-start.12) | collective-permute-done | bytes 258080 | tf_op jit(solution)/shard_map/ppermute | solution.py:36
  50.3 5.6 %collective-permute-done.1 = bf16[144,896]{0,1:T(8,128)(2,1)S(1)} collective-permute-done((bf16[144,896]{0,1:T(8,128)(2,1)}, bf16[144,896]{0,1:T(8,128)(2,1)S(1)}, u32[]{:S(2)}, u32[]{:S(2)}) %collective-permute-start.1) | collective-permute-done | bytes 258080 | tf_op jit(solution)/shard_map/ppermute | solution.py:36
  56.0 2.0 %collective-permute-start.13 = (bf16[144,896]{0,1:T(8,128)(2,1)S(1)}, bf16[144,896]{0,1:T(8,128)(2,1)S(1)}, u32[]{:S(2)}, u32[]{:S(2)}) collective-permute-start(bf16[144,896]{0,1:T(8,128)(2,1)S(1)} %collective-permute-done.12), channel_id=1, source_target_pairs={{0,1},{2,0},{4,2},{6,4},{7,6},{5,7},{3,5},{1,3},{8,9},{10,8},{12,1... | collective-permute-start | bytes 774152 | tf_op jit(solution)/shard_map/ppermute | solution.py:36
  58.5 10.8 %collective-permute-done.2 = bf16[144,896]{0,1:T(8,128)(2,1)S(1)} collective-permute-done((bf16[144,896]{0,1:T(8,128)(2,1)S(1)}, bf16[144,896]{0,1:T(8,128)(2,1)S(1)}, u32[]{:S(2)}, u32[]{:S(2)}) %collective-permute-start.2) | collective-permute-done | bytes 258080 | tf_op jit(solution)/shard_map/ppermute | solution.py:36
  69.5 2.0 %collective-permute-start.4 = (bf16[112,896]{0,1:T(8,128)(2,1)S(1)}, bf16[112,896]{0,1:T(8,128)(2,1)S(1)}, u32[]{:S(2)}, u32[]{:S(2)}) collective-permute-start(bf16[112,896]{0,1:T(8,128)(2,1)S(1)} %pad_maximum_fusion.4), channel_id=1, source_target_pairs={{0,1},{2,0},{4,2},{6,4},{7,6},{5,7},{3,5},{1,3},{8,9},{10,8},{12,1... | collective-permute-start | bytes 602120 | tf_op jit(solution)/shard_map/ppermute | solution.py:36
  71.8 2.0 %collective-permute-start.15 = (bf16[72,896]{0,1:T(8,128)(2,1)S(1)}, bf16[72,896]{0,1:T(8,128)(2,1)S(1)}, u32[]{:S(2)}, u32[]{:S(2)}) collective-permute-start(bf16[72,896]{0,1:T(8,128)(2,1)S(1)} %slice.137), channel_id=1, source_target_pairs={{0,1},{2,0},{4,2},{6,4},{7,6},{5,7},{3,5},{1,3},{8,9},{10,8},{12,1... | collective-permute-start | bytes 387080 | tf_op jit(solution)/shard_map/ppermute | solution.py:36
  74.4 7.5 %collective-permute-done.14 = bf16[72,896]{0,1:T(8,128)(2,1)S(1)} collective-permute-done((bf16[72,896]{0,1:T(8,128)(2,1)S(1)}, bf16[72,896]{0,1:T(8,128)(2,1)S(1)}, u32[]{:S(2)}, u32[]{:S(2)}) %collective-permute-start.14) | collective-permute-done | bytes 129056 | tf_op jit(solution)/shard_map/ppermute | solution.py:36
  83.2 1.3 collective-permute-start.16
  84.5 1.0 shard_map.127
  86.5 1.6 collective-permute-start.6
  88.8 5.0 %collective-permute-done.6 = bf16[112,896]{0,1:T(8,128)(2,1)S(1)} collective-permute-done((bf16[112,896]{0,1:T(8,128)(2,1)S(1)}, bf16[112,896]{0,1:T(8,128)(2,1)S(1)}, u32[]{:S(2)}, u32[]{:S(2)}) %collective-permute-start.6) | collective-permute-done | bytes 200736 | tf_op jit(solution)/shard_map/ppermute | solution.py:36
  94.9 1.0 collective-permute-start.7
  95.8 1.1 collective-permute-start.8
  97.4 3.6 %collective-permute-done.7 = bf16[112,896]{0,1:T(8,128)(2,1)S(1)} collective-permute-done((bf16[112,896]{0,1:T(8,128)(2,1)S(1)}, bf16[112,896]{0,1:T(8,128)(2,1)S(1)}, u32[]{:S(2)}, u32[]{:S(2)}) %collective-permute-start.7) | collective-permute-done | bytes 200736 | tf_op jit(solution)/shard_map/ppermute | solution.py:36
  101.0 1.0 collective-permute-start.21
  102.0 1.0 collective-permute-start.23
  103.0 1.0 collective-permute-start.9
  104.1 1.1 collective-permute-start.10
  105.7 8.7 %collective-permute-done.21.rest_2_ = bf16[128,1792]{1,0:T(8,128)(2,1)S(1)} collective-permute-done((bf16[128,1792]{1,0:T(8,128)(2,1)S(1)}, bf16[128,1792]{1,0:T(8,128)(2,1)S(1)}, u32[]{:S(2)}, u32[]{:S(2)}) %collective-permute-start.21) | collective-permute-done | bytes 458784 | tf_op jit(solution)/shard_map/ppermute | solution.py:36
  114.4 1.0 collective-permute-start.25
  115.4 1.0 collective-permute-start.27
  116.5 2.9 %collective-permute-done.9 = bf16[56,896]{0,1:T(8,128)(2,1)S(1)} collective-permute-done((bf16[56,896]{0,1:T(8,128)(2,1)S(1)}, bf16[56,896]{0,1:T(8,128)(2,1)S(1)}, u32[]{:S(2)}, u32[]{:S(2)}) %collective-permute-start.9) | collective-permute-done | bytes 100384 | tf_op jit(solution)/shard_map/ppermute | solution.py:36
  119.3 1.0 collective-permute-done.10
  121.3 5.1 %collective-permute-done.25.rest_6_ = bf16[128,1792]{1,0:T(8,128)(2,1)S(1)} collective-permute-done((bf16[128,1792]{1,0:T(8,128)(2,1)S(1)}, bf16[128,1792]{1,0:T(8,128)(2,1)S(1)}, u32[]{:S(2)}, u32[]{:S(2)}) %collective-permute-start.25) | collective-permute-done | bytes 458784 | tf_op jit(solution)/shard_map/ppermute | solution.py:36
  126.4 1.0 collective-permute-start.29
  127.4 1.0 collective-permute-start.31
  128.4 1.2 shard_map.128
  129.6 1.3 collective-permute-start.18
  132.1 3.2 %collective-permute-done.29.rest_10_ = bf16[128,1792]{1,0:T(8,128)(2,1)S(1)} collective-permute-done((bf16[128,1792]{1,0:T(8,128)(2,1)S(1)}, bf16[128,1792]{1,0:T(8,128)(2,1)S(1)}, u32[]{:S(2)}, u32[]{:S(2)}) %collective-permute-start.29) | collective-permute-done | bytes 458784 | tf_op jit(solution)/shard_map/ppermute | solution.py:36
  135.4 1.3 collective-permute-start.19
  136.7 1.3 collective-permute-start.20
  138.0 0.7 slice.139
  138.7 1.7 slice.140
  140.3 1.4 collective-permute-start.33
  141.7 0.8 copy-done
  142.7 0.8 copy-done.2
  143.8 0.8 copy-done.4
  144.6 0.7 collective-permute-start.35
  145.7 1.6 shard_map.130
  147.3 5.0 %all-to-all-start = ((bf16[8,64,128]{2,1,0:T(8,128)(2,1)}), bf16[8,64,128]{2,1,0:T(8,128)(2,1)S(1)}, u32[]{:S(2)}, u32[]{:S(2)}) async-start(bf16[8,64,128]{2,1,0:T(8,128)(2,1)} %bitcast.26), calls=%async_computation | async-start | bytes 262144 | tf_op jit(solution)/shard_map/all_to_all | solution.py:343
  152.9 6.8 %all-to-all-done.gated = bf16[8,64,128]{2,1,0:T(8,128)(2,1)S(1)} async-done(((bf16[8,64,128]{2,1,0:T(8,128)(2,1)}), bf16[8,64,128]{2,1,0:T(8,128)(2,1)S(1)}, u32[]{:S(2)}, u32[]{:S(2)}) %all-to-all-start) | async-done | bytes 131104 | tf_op jit(solution)/shard_map/all_to_all | solution.py:343
  159.7 1.0 copy-done.1
  160.7 1.0 copy-done.3
  161.7 1.0 copy-done.5
  162.7 6.7 %shard_map.131 = bf16[64,3584]{1,0:T(8,128)(2,1)} custom-call(s32[8]{0:T(128)S(1)} %get-tuple-element.70.place, s32[1]{0:T(128)} %bitcast.1.core, bf16[8,64,128]{2,1,0:T(8,128)(2,1)S(1)} %all-to-all-done.gated, bf16[128,1792]{1,0:T(8,128)(2,1)S(1)} %get-tuple-element.36.rest_0_, bf16[128,1792]{1,0:T(8,128)(2,1)S(1)} %get-tuple-element.39.rest_1_, ...), custom_call_target="tpu_custom_call" | custom-call | flops 1000000000 | bytes 2097152 | tf_op jit(solution)/shard_map/pallas_call | solution.py:344
  (115 shorter events, 13.6 us)
Async XLA Ops:
  0.0 11.7 %copy-start.12 = (bf16[3584,2]{0,1:T(2,128)(2,1)S(1)}, bf16[3584,2]{0,1:T(2,128)(2,1)}, u32[]{:S(2)}) copy-start(bf16[3584,2]{0,1:T(2,128)(2,1)} %param.16) | copy-start | bytes 43012
  2.1 35.7 %collective-permute-start.11 = (bf16[144,896]{0,1:T(8,128)(2,1)}, bf16[144,896]{0,1:T(8,128)(2,1)}, u32[]{:S(2)}, u32[]{:S(2)}) collective-permute-start(bf16[144,896]{0,1:T(8,128)(2,1)} %pad_maximum_fusion.1), channel_id=1, source_target_pairs={{0,1},{2,0},{4,2},{6,4},{7,6},{5,7},{3,5},{1,3},{8,9},{10,8},{12,1... | collective-permute-start | bytes 774152 | tf_op jit(solution)/shard_map/ppermute | solution.py:36
  5.0 37.1 %collective-permute-start = (bf16[144,896]{0,1:T(8,128)(2,1)}, bf16[144,896]{0,1:T(8,128)(2,1)}, u32[]{:S(2)}, u32[]{:S(2)}) collective-permute-start(bf16[144,896]{0,1:T(8,128)(2,1)} %pad_maximum_fusion.1), channel_id=1, source_target_pairs={{0,2},{2,4},{4,6},{6,7},{7,5},{5,3},{3,1},{1,0},{8,10},{10,12},{12... | collective-permute-start | bytes 774152 | tf_op jit(solution)/shard_map/ppermute | solution.py:36
  5.9 31.7 %collective-permute-start.17 = (s32[8]{0:T(128)S(1)}, s32[8]{0:T(128)S(1)}, u32[]{:S(2)}, u32[]{:S(2)}) collective-permute-start(s32[8]{0:T(128)S(1)} %slice.122), channel_id=1, source_target_pairs={{0,8},{8,16},{16,24},{1,9},{9,17},{17,25},{2,10},{10,18},{18,26},{... | collective-permute-start | bytes 104 | tf_op jit(solution)/shard_map/ppermute | solution.py:296
  17.5 3.6 %copy-start.10 = (bf16[512,448]{0,1:T(8,128)(2,1)S(1)}, bf16[512,448]{0,1:T(8,128)(2,1)}, u32[]{:S(2)}) copy-start(bf16[512,448]{0,1:T(8,128)(2,1)} %param.13) | copy-start | bytes 1376260
  17.5 4.2 %copy-start.13 = (f32[128]{0:T(128)S(1)}, f32[128]{0:T(128)}, u32[]{:S(2)}) copy-start(f32[128]{0:T(128)} %param.22) | copy-start | bytes 1540
  19.2 1.8 %copy-start.8 = (bf16[8,448,512]{2,1,0:T(8,128)(2,1)}, bf16[8,448,512]{2,1,0:T(8,128)(2,1)S(1)}, u32[]{:S(2)}) copy-start(bf16[8,448,512]{2,1,0:T(8,128)(2,1)S(1)} %pad_maximum_fusion) | copy-start | bytes 11010052
  21.0 2.2 %copy-start.11 = (s32[512]{0:T(512)S(1)}, s32[512]{0:T(512)}, u32[]{:S(2)}) copy-start(s32[512]{0:T(512)} %param.24) | copy-start | bytes 6148
  21.0 11.0 %copy-start.14 = (f32[2]{0:T(128)S(1)}, f32[2]{0:T(128)}, u32[]{:S(2)}) copy-start(f32[2]{0:T(128)} %param.18) | copy-start | bytes 28
  21.0 11.2 %copy-start.15 = (f32[2]{0:T(128)S(1)}, f32[2]{0:T(128)}, u32[]{:S(2)}) copy-start(f32[2]{0:T(128)} %param.19) | copy-start | bytes 28
  21.0 11.3 %copy-start.16 = (f32[2]{0:T(128)S(1)}, f32[2]{0:T(128)}, u32[]{:S(2)}) copy-start(f32[2]{0:T(128)} %param.17) | copy-start | bytes 28
  37.0 12.9 %copy-start.9 = (bf16[8,448,512]{2,1,0:T(8,128)(2,1)S(1)}, bf16[8,448,512]{2,1,0:T(8,128)(2,1)}, u32[]{:S(2)}) copy-start(bf16[8,448,512]{2,1,0:T(8,128)(2,1)} %copy-done.8) | copy-start | bytes 11010052
  37.8 12.0 %collective-permute-start.12 = (bf16[144,896]{0,1:T(8,128)(2,1)}, bf16[144,896]{0,1:T(8,128)(2,1)S(1)}, u32[]{:S(2)}, u32[]{:S(2)}) collective-permute-start(bf16[144,896]{0,1:T(8,128)(2,1)} %collective-permute-done.11), channel_id=1, source_target_pairs={{0,1},{2,0},{4,2},{6,4},{7,6},{5,7},{3,5},{1,3},{8,9},{10,8},{12,1... | collective-permute-start | bytes 774152 | tf_op jit(solution)/shard_map/ppermute | solution.py:36
  43.3 12.6 %collective-permute-start.1 = (bf16[144,896]{0,1:T(8,128)(2,1)}, bf16[144,896]{0,1:T(8,128)(2,1)S(1)}, u32[]{:S(2)}, u32[]{:S(2)}) collective-permute-start(bf16[144,896]{0,1:T(8,128)(2,1)} %collective-permute-done), channel_id=1, source_target_pairs={{0,2},{2,4},{4,6},{6,7},{7,5},{5,3},{3,1},{1,0},{8,10},{10,12},{12... | collective-permute-start | bytes 774152 | tf_op jit(solution)/shard_map/ppermute | solution.py:36
  55.9 13.3 %collective-permute-start.2 = (bf16[144,896]{0,1:T(8,128)(2,1)S(1)}, bf16[144,896]{0,1:T(8,128)(2,1)S(1)}, u32[]{:S(2)}, u32[]{:S(2)}) collective-permute-start(bf16[144,896]{0,1:T(8,128)(2,1)S(1)} %collective-permute-done.1), channel_id=1, source_target_pairs={{0,2},{2,4},{4,6},{6,7},{7,5},{5,3},{3,1},{1,0},{8,10},{10,12},{12... | collective-permute-start | bytes 774152 | tf_op jit(solution)/shard_map/ppermute | solution.py:36
  56.0 15.6 %collective-permute-start.13 = (bf16[144,896]{0,1:T(8,128)(2,1)S(1)}, bf16[144,896]{0,1:T(8,128)(2,1)S(1)}, u32[]{:S(2)}, u32[]{:S(2)}) collective-permute-start(bf16[144,896]{0,1:T(8,128)(2,1)S(1)} %collective-permute-done.12), channel_id=1, source_target_pairs={{0,1},{2,0},{4,2},{6,4},{7,6},{5,7},{3,5},{1,3},{8,9},{10,8},{12,1... | collective-permute-start | bytes 774152 | tf_op jit(solution)/shard_map/ppermute | solution.py:36
  69.4 16.1 %collective-permute-start.3 = (bf16[112,896]{0,1:T(8,128)(2,1)S(1)}, bf16[112,896]{0,1:T(8,128)(2,1)S(1)}, u32[]{:S(2)}, u32[]{:S(2)}) collective-permute-start(bf16[112,896]{0,1:T(8,128)(2,1)S(1)} %pad_maximum_fusion.4), channel_id=1, source_target_pairs={{0,2},{2,4},{4,6},{6,7},{7,5},{5,3},{3,1},{1,0},{8,10},{10,12},{12... | collective-permute-start | bytes 602120 | tf_op jit(solution)/shard_map/ppermute | solution.py:36
  69.5 16.5 %collective-permute-start.4 = (bf16[112,896]{0,1:T(8,128)(2,1)S(1)}, bf16[112,896]{0,1:T(8,128)(2,1)S(1)}, u32[]{:S(2)}, u32[]{:S(2)}) collective-permute-start(bf16[112,896]{0,1:T(8,128)(2,1)S(1)} %pad_maximum_fusion.4), channel_id=1, source_target_pairs={{0,1},{2,0},{4,2},{6,4},{7,6},{5,7},{3,5},{1,3},{8,9},{10,8},{12,1... | collective-permute-start | bytes 602120 | tf_op jit(solution)/shard_map/ppermute | solution.py:36
  71.5 10.4 %collective-permute-start.14 = (bf16[72,896]{0,1:T(8,128)(2,1)S(1)}, bf16[72,896]{0,1:T(8,128)(2,1)S(1)}, u32[]{:S(2)}, u32[]{:S(2)}) collective-permute-start(bf16[72,896]{0,1:T(8,128)(2,1)S(1)} %slice.136), channel_id=1, source_target_pairs={{0,2},{2,4},{4,6},{6,7},{7,5},{5,3},{3,1},{1,0},{8,10},{10,12},{12... | collective-permute-start | bytes 387080 | tf_op jit(solution)/shard_map/ppermute | solution.py:36
  71.8 10.3 %collective-permute-start.15 = (bf16[72,896]{0,1:T(8,128)(2,1)S(1)}, bf16[72,896]{0,1:T(8,128)(2,1)S(1)}, u32[]{:S(2)}, u32[]{:S(2)}) collective-permute-start(bf16[72,896]{0,1:T(8,128)(2,1)S(1)} %slice.137), channel_id=1, source_target_pairs={{0,1},{2,0},{4,2},{6,4},{7,6},{5,7},{3,5},{1,3},{8,9},{10,8},{12,1... | collective-permute-start | bytes 387080 | tf_op jit(solution)/shard_map/ppermute | solution.py:36
  73.9 10.6 %copy-start.6 = (f32[4,128]{1,0:T(4,128)S(1)}, f32[4,128]{1,0:T(4,128)}, u32[]{:S(2)}) copy-start(f32[4,128]{1,0:T(4,128)} %taps_x.3) | copy-start | bytes 6148
  73.9 10.6 %copy-start.7 = (f32[4,128]{1,0:T(4,128)S(1)}, f32[4,128]{1,0:T(4,128)}, u32[]{:S(2)}) copy-start(f32[4,128]{1,0:T(4,128)} %taps_bc.3) | copy-start | bytes 6148
  83.2 45.2 %collective-permute-start.16 = (bf16[8,256]{1,0:T(8,128)(2,1)S(1)}, bf16[8,256]{1,0:T(8,128)(2,1)S(1)}, u32[]{:S(2)}, u32[]{:S(2)}) collective-permute-start(bf16[8,256]{1,0:T(8,128)(2,1)S(1)} %slice.144), channel_id=1, source_target_pairs={{0,8},{8,16},{16,24},{1,9},{9,17},{17,25},{2,10},{10,18},{18,26},{... | collective-permute-start | bytes 12296 | tf_op jit(solution)/shard_map/ppermute | solution.py:301
  86.5 7.4 %collective-permute-start.6 = (bf16[112,896]{0,1:T(8,128)(2,1)S(1)}, bf16[112,896]{0,1:T(8,128)(2,1)S(1)}, u32[]{:S(2)}, u32[]{:S(2)}) collective-permute-start(bf16[112,896]{0,1:T(8,128)(2,1)S(1)} %collective-permute-done.4), channel_id=1, source_target_pairs={{0,1},{2,0},{4,2},{6,4},{7,6},{5,7},{3,5},{1,3},{8,9},{10,8},{12,1... | collective-permute-start | bytes 602120 | tf_op jit(solution)/shard_map/ppermute | solution.py:36
  88.1 6.8 %collective-permute-start.5 = (bf16[112,896]{0,1:T(8,128)(2,1)S(1)}, bf16[112,896]{0,1:T(8,128)(2,1)S(1)}, u32[]{:S(2)}, u32[]{:S(2)}) collective-permute-start(bf16[112,896]{0,1:T(8,128)(2,1)S(1)} %collective-permute-done.3), channel_id=1, source_target_pairs={{0,2},{2,4},{4,6},{6,7},{7,5},{5,3},{3,1},{1,0},{8,10},{10,12},{12... | collective-permute-start | bytes 602120 | tf_op jit(solution)/shard_map/ppermute | solution.py:36
  94.9 6.1 %collective-permute-start.7 = (bf16[112,896]{0,1:T(8,128)(2,1)S(1)}, bf16[112,896]{0,1:T(8,128)(2,1)S(1)}, u32[]{:S(2)}, u32[]{:S(2)}) collective-permute-start(bf16[112,896]{0,1:T(8,128)(2,1)S(1)} %collective-permute-done.5), channel_id=1, source_target_pairs={{0,2},{2,4},{4,6},{6,7},{7,5},{5,3},{3,1},{1,0},{8,10},{10,12},{12... | collective-permute-start | bytes 602120 | tf_op jit(solution)/shard_map/ppermute | solution.py:36
  95.8 8.1 %collective-permute-start.8 = (bf16[112,896]{0,1:T(8,128)(2,1)S(1)}, bf16[112,896]{0,1:T(8,128)(2,1)S(1)}, u32[]{:S(2)}, u32[]{:S(2)}) collective-permute-start(bf16[112,896]{0,1:T(8,128)(2,1)S(1)} %collective-permute-done.6), channel_id=1, source_target_pairs={{0,1},{2,0},{4,2},{6,4},{7,6},{5,7},{3,5},{1,3},{8,9},{10,8},{12,1... | collective-permute-start | bytes 602120 | tf_op jit(solution)/shard_map/ppermute | solution.py:36
  101.0 13.5 %collective-permute-start.21 = (bf16[128,1792]{1,0:T(8,128)(2,1)S(1)}, bf16[128,1792]{1,0:T(8,128)(2,1)S(1)}, u32[]{:S(2)}, u32[]{:S(2)}) collective-permute-start(bf16[128,1792]{1,0:T(8,128)(2,1)S(1)} %get-tuple-element.36.rest_0_), channel_id=1, source_target_pairs={{0,2},{2,4},{4,6},{6,7},{7,5},{5,3},{3,1},{1,0},{8,10},{10,12},{12... | collective-permute-start | bytes 1376264 | tf_op jit(solution)/shard_map/ppermute | solution.py:36
  102.0 13.5 %collective-permute-start.23 = (bf16[128,1792]{1,0:T(8,128)(2,1)S(1)}, bf16[128,1792]{1,0:T(8,128)(2,1)S(1)}, u32[]{:S(2)}, u32[]{:S(2)}) collective-permute-start(bf16[128,1792]{1,0:T(8,128)(2,1)S(1)} %get-tuple-element.36.rest_0_), channel_id=1, source_target_pairs={{0,1},{2,0},{4,2},{6,4},{7,6},{5,7},{3,5},{1,3},{8,9},{10,8},{12,1... | collective-permute-start | bytes 1376264 | tf_op jit(solution)/shard_map/ppermute | solution.py:36
  103.0 16.3 %collective-permute-start.9 = (bf16[56,896]{0,1:T(8,128)(2,1)S(1)}, bf16[56,896]{0,1:T(8,128)(2,1)S(1)}, u32[]{:S(2)}, u32[]{:S(2)}) collective-permute-start(bf16[56,896]{0,1:T(8,128)(2,1)S(1)} %bitcast.70), channel_id=1, source_target_pairs={{0,2},{2,4},{4,6},{6,7},{7,5},{5,3},{3,1},{1,0},{8,10},{10,12},{12... | collective-permute-start | bytes 301064 | tf_op jit(solution)/shard_map/ppermute | solution.py:36
  104.1 16.2 %collective-permute-start.10 = (bf16[56,896]{0,1:T(8,128)(2,1)S(1)}, bf16[56,896]{0,1:T(8,128)(2,1)S(1)}, u32[]{:S(2)}, u32[]{:S(2)}) collective-permute-start(bf16[56,896]{0,1:T(8,128)(2,1)S(1)} %slice.135), channel_id=1, source_target_pairs={{0,1},{2,0},{4,2},{6,4},{7,6},{5,7},{3,5},{1,3},{8,9},{10,8},{12,1... | collective-permute-start | bytes 301064 | tf_op jit(solution)/shard_map/ppermute | solution.py:36
  114.4 12.0 %collective-permute-start.25 = (bf16[128,1792]{1,0:T(8,128)(2,1)S(1)}, bf16[128,1792]{1,0:T(8,128)(2,1)S(1)}, u32[]{:S(2)}, u32[]{:S(2)}) collective-permute-start(bf16[128,1792]{1,0:T(8,128)(2,1)S(1)} %collective-permute-done.21.rest_2_), channel_id=1, source_target_pairs={{0,2},{2,4},{4,6},{6,7},{7,5},{5,3},{3,1},{1,0},{8,10},{10,12},{12... | collective-permute-start | bytes 1376264 | tf_op jit(solution)/shard_map/ppermute | solution.py:36
  115.4 12.0 %collective-permute-start.27 = (bf16[128,1792]{1,0:T(8,128)(2,1)S(1)}, bf16[128,1792]{1,0:T(8,128)(2,1)S(1)}, u32[]{:S(2)}, u32[]{:S(2)}) collective-permute-start(bf16[128,1792]{1,0:T(8,128)(2,1)S(1)} %collective-permute-done.23.rest_4_), channel_id=1, source_target_pairs={{0,1},{2,0},{4,2},{6,4},{7,6},{5,7},{3,5},{1,3},{8,9},{10,8},{12,1... | collective-permute-start | bytes 1376264 | tf_op jit(solution)/shard_map/ppermute | solution.py:36
  126.4 9.0 %collective-permute-start.29 = (bf16[128,1792]{1,0:T(8,128)(2,1)S(1)}, bf16[128,1792]{1,0:T(8,128)(2,1)S(1)}, u32[]{:S(2)}, u32[]{:S(2)}) collective-permute-start(bf16[128,1792]{1,0:T(8,128)(2,1)S(1)} %collective-permute-done.25.rest_6_), channel_id=1, source_target_pairs={{0,2},{2,4},{4,6},{6,7},{7,5},{5,3},{3,1},{1,0},{8,10},{10,12},{12... | collective-permute-start | bytes 1376264 | tf_op jit(solution)/shard_map/ppermute | solution.py:36
  127.4 9.3 %collective-permute-start.31 = (bf16[128,1792]{1,0:T(8,128)(2,1)S(1)}, bf16[128,1792]{1,0:T(8,128)(2,1)}, u32[]{:S(2)}, u32[]{:S(2)}) collective-permute-start(bf16[128,1792]{1,0:T(8,128)(2,1)S(1)} %collective-permute-done.27.rest_8_), channel_id=1, source_target_pairs={{0,1},{2,0},{4,2},{6,4},{7,6},{5,7},{3,5},{1,3},{8,9},{10,8},{12,1... | collective-permute-start | bytes 1376264 | tf_op jit(solution)/shard_map/ppermute | solution.py:36
  129.6 2.1 %collective-permute-start.18 = (f32[72,128]{1,0:T(8,128)S(1)}, f32[72,128]{1,0:T(8,128)S(1)}, u32[]{:S(2)}, u32[]{:S(2)}) collective-permute-start(f32[72,128]{1,0:T(8,128)S(1)} %get-tuple-element.35), channel_id=1, source_target_pairs={{0,8},{8,16},{16,24},{1,9},{9,17},{17,25},{2,10},{10,18},{18,26},{... | collective-permute-start | bytes 110600 | tf_op jit(solution)/shard_map/ppermute | solution.py:318
  130.9 10.8 %collective-permute-start.22 = (bf16[128,1792]{1,0:T(8,128)(2,1)S(1)}, bf16[128,1792]{1,0:T(8,128)(2,1)S(1)}, u32[]{:S(2)}, u32[]{:S(2)}) collective-permute-start(bf16[128,1792]{1,0:T(8,128)(2,1)S(1)} %collective-permute-done.21.rest_2_), channel_id=1, source_target_pairs={{0,8},{8,0},{16,24},{24,16},{1,9},{9,1},{17,25},{25,17},{2,10},{10... | collective-permute-start | bytes 1376264 | tf_op jit(solution)/shard_map/ppermute | solution.py:339
  131.0 11.7 %collective-permute-start.24 = (bf16[128,1792]{1,0:T(8,128)(2,1)S(1)}, bf16[128,1792]{1,0:T(8,128)(2,1)S(1)}, u32[]{:S(2)}, u32[]{:S(2)}) collective-permute-start(bf16[128,1792]{1,0:T(8,128)(2,1)S(1)} %collective-permute-done.23.rest_4_), channel_id=1, source_target_pairs={{0,8},{8,0},{16,24},{24,16},{1,9},{9,1},{17,25},{25,17},{2,10},{10... | collective-permute-start | bytes 1376264 | tf_op jit(solution)/shard_map/ppermute | solution.py:339
  131.8 12.0 %collective-permute-start.26 = (bf16[128,1792]{1,0:T(8,128)(2,1)S(1)}, bf16[128,1792]{1,0:T(8,128)(2,1)S(1)}, u32[]{:S(2)}, u32[]{:S(2)}) collective-permute-start(bf16[128,1792]{1,0:T(8,128)(2,1)S(1)} %collective-permute-done.25.rest_6_), channel_id=1, source_target_pairs={{0,8},{8,0},{16,24},{24,16},{1,9},{9,1},{17,25},{25,17},{2,10},{10... | collective-permute-start | bytes 1376264 | tf_op jit(solution)/shard_map/ppermute | solution.py:339
  135.4 5.0 %collective-permute-start.19 = (f32[72,128]{1,0:T(8,128)S(1)}, f32[72,128]{1,0:T(8,128)S(1)}, u32[]{:S(2)}, u32[]{:S(2)}) collective-permute-start(f32[72,128]{1,0:T(8,128)S(1)} %get-tuple-element.35), channel_id=1, source_target_pairs={{0,16},{8,24},{1,17},{9,25},{2,18},{10,26},{3,19},{11,27},{4,20},{... | collective-permute-start | bytes 110600 | tf_op jit(solution)/shard_map/ppermute | solution.py:318
  136.7 3.7 %collective-permute-start.20 = (f32[72,128]{1,0:T(8,128)S(1)}, f32[72,128]{1,0:T(8,128)S(1)}, u32[]{:S(2)}, u32[]{:S(2)}) collective-permute-start(f32[72,128]{1,0:T(8,128)S(1)} %get-tuple-element.35), channel_id=1, source_target_pairs={{0,24},{1,25},{2,26},{3,27},{4,28},{5,29},{6,30},{7,31}} | collective-permute-start | bytes 110600 | tf_op jit(solution)/shard_map/ppermute | solution.py:318
  140.3 19.3 %collective-permute-start.28 = (bf16[128,1792]{1,0:T(8,128)(2,1)S(1)}, bf16[128,1792]{1,0:T(8,128)(2,1)}, u32[]{:S(2)}, u32[]{:S(2)}) collective-permute-start(bf16[128,1792]{1,0:T(8,128)(2,1)S(1)} %collective-permute-done.27.rest_8_), channel_id=1, source_target_pairs={{0,8},{8,0},{16,24},{24,16},{1,9},{9,1},{17,25},{25,17},{2,10},{10... | collective-permute-start | bytes 1376264 | tf_op jit(solution)/shard_map/ppermute | solution.py:339
  140.3 12.0 %collective-permute-start.33 = (bf16[64,1792]{1,0:T(8,128)(2,1)}, bf16[64,1792]{1,0:T(8,128)(2,1)}, u32[]{:S(2)}, u32[]{:S(2)}) collective-permute-start(bf16[64,1792]{1,0:T(8,128)(2,1)} %slice.139), channel_id=1, source_target_pairs={{0,2},{2,4},{4,6},{6,7},{7,5},{5,3},{3,1},{1,0},{8,10},{10,12},{12... | collective-permute-start | bytes 688136 | tf_op jit(solution)/shard_map/ppermute | solution.py:36
  141.7 0.8 copy-start
  142.5 17.2 %collective-permute-start.30 = (bf16[128,1792]{1,0:T(8,128)(2,1)S(1)}, bf16[128,1792]{1,0:T(8,128)(2,1)}, u32[]{:S(2)}, u32[]{:S(2)}) collective-permute-start(bf16[128,1792]{1,0:T(8,128)(2,1)S(1)} %collective-permute-done.29.rest_10_), channel_id=1, source_target_pairs={{0,8},{8,0},{16,24},{24,16},{1,9},{9,1},{17,25},{25,17},{2,10},{10... | collective-permute-start | bytes 1376264 | tf_op jit(solution)/shard_map/ppermute | solution.py:339
  142.7 0.8 copy-start.2
  143.5 16.2 %collective-permute-start.32 = (bf16[128,1792]{1,0:T(8,128)(2,1)}, bf16[128,1792]{1,0:T(8,128)(2,1)}, u32[]{:S(2)}, u32[]{:S(2)}) collective-permute-start(bf16[128,1792]{1,0:T(8,128)(2,1)} %collective-permute-done.31.rest_12_), channel_id=1, source_target_pairs={{0,8},{8,0},{16,24},{24,16},{1,9},{9,1},{17,25},{25,17},{2,10},{10... | collective-permute-start | bytes 1376264 | tf_op jit(solution)/shard_map/ppermute | solution.py:339
  143.8 0.8 copy-start.4
  144.6 8.0 %collective-permute-start.35 = (bf16[64,1792]{1,0:T(8,128)(2,1)}, bf16[64,1792]{1,0:T(8,128)(2,1)}, u32[]{:S(2)}, u32[]{:S(2)}) collective-permute-start(bf16[64,1792]{1,0:T(8,128)(2,1)} %slice.140), channel_id=1, source_target_pairs={{0,1},{2,0},{4,2},{6,4},{7,6},{5,7},{3,5},{1,3},{8,9},{10,8},{12,1... | collective-permute-start | bytes 688136 | tf_op jit(solution)/shard_map/ppermute | solution.py:36
  147.3 12.3 %all-to-all-start = ((bf16[8,64,128]{2,1,0:T(8,128)(2,1)}), bf16[8,64,128]{2,1,0:T(8,128)(2,1)S(1)}, u32[]{:S(2)}, u32[]{:S(2)}) async-start(bf16[8,64,128]{2,1,0:T(8,128)(2,1)} %bitcast.26), calls=%async_computation | async-start | bytes 262144 | tf_op jit(solution)/shard_map/all_to_all | solution.py:343
  152.3 7.4 %collective-permute-start.34 = (bf16[64,1792]{1,0:T(8,128)(2,1)}, bf16[64,1792]{1,0:T(8,128)(2,1)}, u32[]{:S(2)}, u32[]{:S(2)}) collective-permute-start(bf16[64,1792]{1,0:T(8,128)(2,1)} %collective-permute-done.33.rest_14_), channel_id=1, source_target_pairs={{0,8},{8,0},{16,24},{24,16},{1,9},{9,1},{17,25},{25,17},{2,10},{10... | collective-permute-start | bytes 688136 | tf_op jit(solution)/shard_map/ppermute | solution.py:339
  152.6 7.1 %collective-permute-start.36 = (bf16[64,1792]{1,0:T(8,128)(2,1)}, bf16[64,1792]{1,0:T(8,128)(2,1)}, u32[]{:S(2)}, u32[]{:S(2)}) collective-permute-start(bf16[64,1792]{1,0:T(8,128)(2,1)} %collective-permute-done.35.rest_16_), channel_id=1, source_target_pairs={{0,8},{8,0},{16,24},{24,16},{1,9},{9,1},{17,25},{25,17},{2,10},{10... | collective-permute-start | bytes 688136 | tf_op jit(solution)/shard_map/ppermute | solution.py:339
  159.7 1.0 copy-start.1
  160.7 1.0 copy-start.3
  161.7 1.0 copy-start.5

commit v2 on v1

v2 whole, which is shorter than its diff:
```python
import functools

import jax
import jax.numpy as jnp
import numpy as np
from jax import lax
from jax.experimental import pallas as pl
from jax.experimental.pallas import tpu as pltpu
from jax.sharding import PartitionSpec as P

NORM_EPS = 1e-05
F32 = jnp.float32
BF16 = jnp.bfloat16
VMEM = pl.BlockSpec(memory_space=pltpu.VMEM)
ANY = pl.BlockSpec(memory_space=pl.ANY)
HALO = 8


def ring_place(index, n):
    return jnp.where(index % 2 == 0, index // 2, (2 * n - 1 - index) // 2)


def ring_index(place, n):
    return jnp.where(place < n // 2, 2 * place, 2 * n - 1 - 2 * place)


def ring_shift(block, step):
    n = lax.axis_size("tensor")
    order = [2 * i if i < n // 2 else 2 * n - 1 - 2 * i for i in range(n)]
    return lax.ppermute(block, "tensor", [(order[i], order[(i + step) % n]) for i in range(n)])


def ring_gather(block):
    n = lax.axis_size("tensor")
    forth = back = block
    steps = []
    for _ in range(1, n // 2):
        forth, back = ring_shift(forth, 1), ring_shift(back, -1)
        steps.append((forth, back))
    half = block.shape[0] // 32 * 16
    steps.append((ring_shift(forth[:half], 1), ring_shift(back[half:], -1)))
    return steps


def silu(v):
    return v / (1.0 + jnp.exp(-v))


def dot(a, b, dims=((1,), (0,))):
    return lax.dot_general(a.astype(BF16), b.astype(BF16), (dims, ((), ())), preferred_element_type=F32)


def source_of(distance):
    n = lax.axis_size("tensor")
    return ring_index((ring_place(lax.axis_index("tensor"), n) + distance + n) % n, n)


def project(distances, first, *refs):
    count = len(distances)
    blocks, (w_zx, w_bc, w_dt), refs = refs[:count], refs[count : count + 3], refs[count + 3 :]
    total, (out, held, sems) = (None, refs) if first else (refs[0], refs[1:])
    feat = w_bc.shape[0] // lax.axis_size("tensor")
    width = w_bc.shape[1]
    sources = [w_zx.at[0], w_zx.at[1], w_bc, w_dt]
    copies = []
    for k, (distance, size, skip) in enumerate(distances):
        rows = pl.ds(pl.multiple_of(source_of(distance) * feat + skip, 16), size)
        for j, source in enumerate(sources):
            copies.append(
                pltpu.make_async_copy(
                    source.at[rows], held.at[k, pl.ds(0, size), pl.ds(j * width, width)], sems.at[k, j]
                )
            )
            copies[-1].start()
    result = 0.0 if first else total[...]
    for k, (_, size, _) in enumerate(distances):
        for j in range(len(sources)):
            copies[k * len(sources) + j].wait()
        result = result + dot(blocks[k][...], held[k, :size], ((0,), (0,)))
    out[...] = result


def conv(ext, seg_ext, taps, rows):
    size = taps.shape[0]
    seg_now = seg_ext[HALO : HALO + rows]
    total = taps[size - 1 : size] * ext[HALO : HALO + rows]
    for offset in range(1, size):
        same = seg_ext[HALO - offset : HALO - offset + rows] == seg_now
        total = total + taps[size - 1 - offset : size - offset] * jnp.where(
            same, ext[HALO - offset : HALO - offset + rows], 0.0
        )
    return silu(total)


def prefix_sum(values):
    rows = values.shape[0]
    lower = lax.broadcasted_iota(jnp.int32, (rows, rows), 0) >= lax.broadcasted_iota(jnp.int32, (rows, rows), 1)
    lower = jnp.where(lower, 1.0, 0.0).astype(BF16)
    total = jnp.zeros(values.shape, F32)
    rest = values
    parts = []
    for _ in range(3):
        part = rest.astype(BF16)
        parts.append(part)
        rest = rest - part.astype(F32)
    for part in reversed(parts):
        total = total + jnp.dot(lower, part, preferred_element_type=F32)
    return total


def block_front(ext_x, ext_bc, seg_ext, dt_raw, taps_x, taps_bc, bias, rate, rows, seg_enter, seg_leave):
    conv_x = conv(ext_x, seg_ext, taps_x, rows)
    conv_bc = conv(ext_bc, seg_ext, taps_bc, rows)
    seg = seg_ext[HALO : HALO + rows]
    shifted = dt_raw + bias
    step_size = jnp.maximum(shifted, 0.0) + jnp.log1p(jnp.exp(-jnp.abs(shifted)))
    cum = prefix_sum(-rate * step_size)
    scaled = conv_x * step_size
    last = cum[rows - 1 : rows]
    tail = jnp.where(seg == seg_leave, jnp.exp(last - cum), 0.0)
    state_w = conv_bc.shape[1] // 2
    state = dot(conv_bc, tail * scaled, ((0,), (0,)))[:state_w]
    enter = jnp.where(seg == seg_enter, jnp.exp(cum), 0.0)
    return conv_x, conv_bc, cum, scaled, state, enter, last


def block_inner(conv_bc, cum, scaled, seg_col, seg_row, heads):
    rows, width = scaled.shape
    state_w = conv_bc.shape[1] // 2
    head_w = width // heads
    scores = dot(conv_bc[:, state_w:], conv_bc[:, :state_w], ((1,), (1,)))
    later = lax.broadcasted_iota(jnp.int32, (rows, rows), 0) >= lax.broadcasted_iota(jnp.int32, (rows, rows), 1)
    visible = (seg_col == seg_row) & later
    cum_rows = cum.T
    lane = lax.broadcasted_iota(jnp.int32, (rows, width), 1)
    result = jnp.zeros((rows, width), F32)
    scaled = scaled.astype(BF16)
    for head in range(heads):
        at = head * head_w
        gap = jnp.where(visible, cum[:, at : at + 1] - cum_rows[at : at + 1, :], -jnp.inf)
        part = dot(jnp.exp(gap) * scores, scaled)
        result = jnp.where((lane >= at) & (lane < at + head_w), part, result)
    return result


def later_block(heads, width, rows, proj, seg_ext, seg_row, taps_x, taps_bc, bias, rate, skip,
                out, bc_out, enter_out, state_out, gate_out, ext_x, ext_bc):
    rounded = proj[rows - HALO :, : 3 * width].astype(BF16).astype(F32)
    gate_out[...] = silu(rounded[HALO:, :width])
    ext_x[...] = rounded[:, width : 2 * width]
    ext_bc[...] = rounded[:, 2 * width : 3 * width]
    seg_enter = seg_ext[HALO - 1 : HALO]
    seg_leave = seg_ext[HALO + rows - 1 : HALO + rows]
    conv_x, conv_bc, cum, scaled, state, enter, last = block_front(
        ext_x, ext_bc, seg_ext, proj[rows:, 3 * width :], taps_x, taps_bc[...], bias[...], rate[...], rows, seg_enter, seg_leave
    )
    out[...] = block_inner(conv_bc, cum, scaled, seg_ext[HALO:], seg_row[...], heads) + skip[...] * conv_x
    bc_out[...] = conv_bc
    enter_out[...] = enter
    keep = jnp.where(seg_enter == seg_leave, jnp.exp(last), 0.0)
    state_w = state.shape[0]
    state_out[:state_w] = state
    state_out[state_w : state_w + 1] = keep
    state_out[state_w + 1 : state_w + 2] = last
    state_out[state_w + 2 :] = jnp.zeros((state_out.shape[0] - state_w - 2, width), F32)


def first_front(width, rows, proj, halo, seg_ext, seg_last, state_b, taps_x, taps_bc, bias, rate,
                conv_out, bc_out, cum_out, scaled_out, enter_out, state_out, message, ext_x, ext_bc):
    ext_x[:HALO] = halo[:, :width].astype(F32)
    ext_bc[:HALO] = halo[:, width:].astype(F32)
    ext_x[HALO:] = proj[:rows, width : 2 * width].astype(BF16).astype(F32)
    ext_bc[HALO:] = proj[:rows, 2 * width : 3 * width].astype(BF16).astype(F32)
    seg_enter = seg_ext[HALO : HALO + 1]
    seg_leave = seg_ext[HALO + rows - 1 : HALO + rows]
    conv_x, conv_bc, cum, scaled, state, enter, last = block_front(
        ext_x, ext_bc, seg_ext, proj[:rows, 3 * width :], taps_x, taps_bc[...], bias[...], rate[...], rows, seg_enter, seg_leave
    )
    conv_out[...] = conv_x
    bc_out[...] = conv_bc
    cum_out[...] = cum
    scaled_out[...] = scaled
    enter_out[...] = enter
    keep = jnp.where(seg_enter == seg_leave, jnp.exp(last), 0.0)
    state_w = state.shape[0]
    state_out[:state_w] = state
    state_out[state_w : state_w + 1] = keep
    state_out[state_w + 1 :] = jnp.zeros((state_out.shape[0] - state_w - 1, width), F32)
    message[:state_w] = state_b[state_w : state_w + 1] * state + state_b[:state_w]
    message[state_w : state_w + 1] = last + state_b[state_w + 1 : state_w + 2]
    message[state_w + 1 : state_w + 2] = jnp.broadcast_to(seg_last[...].astype(F32), (1, width))
    message[state_w + 2 :] = jnp.zeros((message.shape[0] - state_w - 2, width), F32)


def first_inner(heads, width, rows, conv_x, conv_bc, cum, scaled, proj, seg_col, seg_row, skip, out, gate_out):
    gate_out[...] = silu(proj[:rows, :width].astype(BF16).astype(F32))
    out[...] = (
        block_inner(conv_bc[...], cum[...], scaled[...], seg_col[HALO:], seg_row[...], heads) + skip[...] * conv_x[...]
    )


def finish(count, rows, seg_first, out_a, gate_a, bc_a, enter_a, state_a, out_b, gate_b, bc_b, enter_b, *rest):
    messages, gated = rest[:count], rest[count]
    state_w = bc_a.shape[1] // 2
    entering = jnp.zeros((state_w, out_a.shape[1]), F32)
    decay = jnp.zeros((1, out_a.shape[1]), F32)
    first = seg_first[...].astype(F32)
    for message in messages:
        passes = jnp.where(message[state_w + 1 : state_w + 2] == first, jnp.exp(decay), 0.0)
        entering = entering + passes * message[:state_w]
        decay = decay + message[state_w : state_w + 1]
    second = state_a[state_w : state_w + 1] * entering + state_a[:state_w]
    gated[:rows] = ((out_a[...] + enter_a[...] * dot(bc_a[:, state_w:], entering)) * gate_a[...]).astype(BF16)
    gated[rows:] = ((out_b[...] + enter_b[...] * dot(bc_b[:, state_w:], second)) * gate_b[...]).astype(BF16)


def product(gated, where, pieces, held, sems):
    copies = []
    for k, (slot, _, row) in enumerate(where):
        copies.append(
            pltpu.make_async_copy(pieces[k], held.at[slot, pl.ds(row, pieces[k].shape[0])], sems.at[k])
        )
        copies[-1].start()
    sums = [0.0] * len(gated)
    waited = set()
    for k, (slot, distance, _) in enumerate(where):
        if slot in waited:
            continue
        waited.add(slot)
        for j, (other, _, _) in enumerate(where):
            if other == slot:
                copies[j].wait()
        source = source_of(distance)
        for i, rows in enumerate(gated):
            sums[i] = sums[i] + jnp.dot(rows[source], held[slot], preferred_element_type=F32)
    return sums


def product_early(where, mine, other, *rest):
    pieces, (out, held, sems) = rest[: len(where)], rest[len(where) :]
    sums = product((mine, other), where, pieces, held, sems)
    rows = mine.shape[1]
    out[:rows] = sums[0]
    out[rows:] = sums[1]


def product_last(where, mine, other, total, *rest):
    pieces, (mine_out, other_out, held, sems) = rest[: len(where)], rest[len(where) :]
    sums = product((mine, other), where, pieces, held, sems)
    blocks, rows, width = mine.shape
    for i, (gated, out) in enumerate(((mine, mine_out), (other, other_out))):
        squares = jnp.zeros((rows, width), F32)
        for block in range(blocks):
            value = gated[block].astype(F32)
            squares = squares + value * value
        scale = lax.rsqrt(jnp.sum(squares, axis=1, keepdims=True) / (blocks * width) + NORM_EPS)
        out[...] = ((sums[i] + total[i * rows : (i + 1) * rows]) * scale).astype(BF16)


def call(body, outs, scratch=(), vmem=48, flops=10**7, **kw):
    return pl.pallas_call(
        body,
        out_shape=outs,
        scratch_shapes=list(scratch),
        compiler_params=pltpu.CompilerParams(vmem_limit_bytes=vmem << 20),
        cost_estimate=pl.CostEstimate(flops=flops, bytes_accessed=1 << 21, transcendentals=1 << 17),
        **kw,
    )


def local(
    tokens, w_zx, w_bc, w_dt, dt_bias, a_rate, d_skip, conv_x, conv_bc, norm_gain, w_out, segments
):
    tok_rows, feat = tokens.shape
    width = w_zx.shape[2]
    heads = dt_bias.shape[0]
    head_w = width // heads
    state_w = w_bc.shape[1] // 2
    model = w_zx.shape[1]
    n_seq, n_tensor = lax.axis_size("seq"), lax.axis_size("tensor")
    seq_at = lax.axis_index("seq")
    rows = tok_rows // 2
    shape = lambda *s, kind=F32: jax.ShapeDtypeStruct(s, kind)

    spread = lambda v: jnp.repeat(v, head_w, axis=-1)
    expand = np.repeat(np.eye(heads, dtype=np.float32), head_w, axis=1)
    w_step = jnp.dot(w_dt, expand.astype(BF16))
    block = tokens.T
    steps = ring_gather(block)
    last = n_tensor // 2
    arrivals = [[(0, block, 0)]]
    arrivals += [[(-i - 1, forth, 0), (i + 1, back, 0)] for i, (forth, back) in enumerate(steps[:-1])]
    arrivals += [[(last, steps[-1][0], 0), (last, steps[-1][1], steps[-1][0].shape[0])]]
    proj = ()
    for arrived in arrivals:
        proj = (
            call(
                functools.partial(project, [(d, part.shape[0], skip) for d, part, skip in arrived], not proj),
                shape(tok_rows, 4 * width),
                [
                    pltpu.VMEM((len(arrived), max(part.shape[0] for _, part, _ in arrived), 4 * width), BF16),
                    pltpu.SemaphoreType.DMA((len(arrived), 4)),
                ],
                in_specs=[VMEM] * len(arrived) + [ANY] * 3 + [VMEM] * len(proj),
                flops=10**9,
            )(*[part for _, part, _ in arrived], w_zx, w_bc, w_step, *proj),
        )
    (proj,) = proj

    ahead = [(i, i + 1) for i in range(n_seq - 1)]
    seg_halo = lax.ppermute(segments[tok_rows - HALO :], "seq", ahead)
    seg_all = jnp.concatenate([seg_halo, segments])[:, None]
    seg_ext_a, seg_ext_b = seg_all[: HALO + rows], seg_all[rows:]
    seg_row_a, seg_row_b = segments[None, :rows], segments[None, rows:]
    seg_first, seg_last = segments[None, :1], segments[None, tok_rows - 1 :]
    halo = lax.ppermute(proj[tok_rows - HALO :, width : 3 * width].astype(BF16), "seq", ahead)
    bias, rate, skip = spread(dt_bias)[None], spread(a_rate)[None], spread(d_skip)[None]

    msg_rows = state_w + 8
    plane = shape(rows, width)
    ext = pltpu.VMEM((HALO + rows, width), F32)
    out_b, bc_b, enter_b, state_b, gate_b = call(
        functools.partial(later_block, heads, width, rows),
        [plane, plane, plane, shape(msg_rows, width), plane],
        [ext, ext],
    )(proj, seg_ext_b, seg_row_b, conv_x, conv_bc, bias, rate, skip)
    cx_a, bc_a, cum_a, scaled_a, enter_a, state_a, message = call(
        functools.partial(first_front, width, rows),
        [plane] * 5 + [shape(msg_rows, width)] * 2,
        [ext, ext],
    )(proj, halo, seg_ext_a, seg_last, state_b, conv_x, conv_bc, bias, rate)
    messages = [
        lax.ppermute(message, "seq", [(i, i + far) for i in range(n_seq - far)]) for far in range(1, n_seq)
    ]
    out_a, gate_a = call(functools.partial(first_inner, heads, width, rows), [plane, plane])(
        cx_a, bc_a, cum_a, scaled_a, proj, seg_ext_a, seg_row_a, skip
    )
    gated = call(
        functools.partial(finish, len(messages), rows), shape(tok_rows, width, kind=BF16)
    )(seg_first, out_a, gate_a, bc_a, enter_a, state_a, out_b, gate_b, bc_b, enter_b, *messages)

    core = seq_at % 2
    columns = model // 2
    own = (lax.dynamic_slice_in_dim(w_out, core * columns, columns, 1).astype(F32) * norm_gain[:, None]).astype(BF16)
    own_first, _ = lax.optimization_barrier((own, steps[-1]))
    w_steps = ring_gather(own_first)
    swap = [(i, i ^ 1) for i in range(n_seq)]
    tok_own = tok_rows // n_tensor
    mine = lax.all_to_all(gated.reshape(n_tensor, tok_own, width), "tensor", 0, 0)
    other = lax.ppermute(mine, "seq", swap)
    pieces, where = [own], [(0, 0, 0)]
    for i, pair in enumerate(w_steps[:-1]):
        pieces += pair
        where += [(2 * i + 1, -i - 1, 0), (2 * i + 2, i + 1, 0)]
    total = call(
        functools.partial(product_early, where),
        shape(2 * tok_own, columns),
        [pltpu.VMEM((len(where), width, columns), BF16), pltpu.SemaphoreType.DMA((len(where),))],
        in_specs=[VMEM, VMEM] + [ANY] * len(pieces),
        flops=10**9,
    )(mine, other, *pieces)
    where = [(0, last, 0), (0, last, w_steps[-1][0].shape[0])]
    half = shape(tok_own, columns, kind=BF16)
    out_own, out_other = call(
        functools.partial(product_last, where),
        [half, half],
        [pltpu.VMEM((1, width, columns), BF16), pltpu.SemaphoreType.DMA((2,))],
        in_specs=[VMEM, VMEM, VMEM] + [ANY] * 2,
        flops=10**8,
    )(mine, other, total, *w_steps[-1])
    arrived = lax.ppermute(out_other, "seq", swap)
    is_first = core == 0
    return jnp.concatenate([jnp.where(is_first, out_own, arrived), jnp.where(is_first, arrived, out_own)], 1)


def solution(mesh):
    in_specs = (
        P("seq", "tensor"),
        P(None, None, "tensor"),
        P(),
        P(None, "tensor"),
        P("tensor"),
        P("tensor"),
        P("tensor"),
        P(None, "tensor"),
        P(),
        P("tensor"),
        P("tensor", None),
        P("seq"),
    )
    out_specs = P(("seq", "tensor"), None)
    return jax.shard_map(local, mesh=mesh, in_specs=in_specs, out_specs=out_specs, check_vma=False)
```

time: 171 us -> 109 us (0.64)
  waiting for transfers between devices: 65.9 us -> 45 us
  local copies, waits for them, and re-layouts: 23.8 us -> 6.71 us
  between operations: 15.9 us -> 0.4 us
  matrix products: 9.42 us -> 0.46 us
  Pallas kernels: 11 us -> 16.9 us
  starting transfers between devices: 39.3 us -> 36.7 us
  other arithmetic: 4.33 us -> 2.09 us
    ppermute x24 -> x16, waiting for transfers between devices: 58.9 us -> 37 us  [ring_shift(): lax.ppermute(block, 'tensor', [(order[i], order[(i + step) % n]) for i in...]
    dot_general x16 -> x1, matrix products: 9.42 us -> 0.46 us  [local(): w_step = jnp.dot(w_dt, expand.astype(BF16))]
    ppermute x24 -> x16, starting transfers between devices: 25.9 us -> 17.5 us  [ring_shift(): lax.ppermute(block, 'tensor', [(order[i], order[(i + step) % n]) for i in...]
    ppermute x3, starting transfers between devices: 3.86 us -> 10.1 us  [local(): lax.ppermute(message, 'seq', [(i, i + far) for i in range(n_seq - far)])]
    pallas_call x4 -> x10, Pallas kernels: 9.34 us -> 15.4 us  [the longest x5 9.32 us: local(): call(functools.partial(project, [(d, part.shape[0], skip) for d, part, sk...]
    concatenate x2 -> x0, local copies, waits for them, and re-layouts: 4.02 us -> none  [local(): jnp.concatenate([w_zx[0], w_zx[1], w_bc, spread(w_dt)], 1)]
    unnamed x34 -> x40, local copies, waits for them, and re-layouts: 7.2 us -> 3.33 us
    split x14 -> x0, local copies, waits for them, and re-layouts: 3.73 us -> none  [the longest x12 2.38 us: unpack(): return jnp.concatenate(jnp.split(packed, packed.shape[1] // width, 1), 0)]
  transfers between devices with their start and end apart: 38 -> 24, of which waited for: 16 -> 13; matrix products, arithmetic and copies ran while one was open for 17% -> 5% of each run, Pallas kernels for 2% -> 15%
where the time goes in v2:
time: 109 us; the launch traced here: 108 us
  waiting for transfers between devices  45 us (41%)
  starting transfers between devices  36.7 us (34%)
  Pallas kernels  16.9 us (16%)
  local copies, waits for them, and re-layouts  6.71 us (6%)
  other arithmetic  2.09 us (2%)
    ppermute x16, waiting for transfers between devices, ring_shift(): lax.ppermute(block, 'tensor', [(order[i], order[(i + step) % n]) for i in...  37 us
    ppermute x16, starting transfers between devices, ring_shift(): lax.ppermute(block, 'tensor', [(order[i], order[(i + step) % n]) for i in...  17.5 us
    ppermute x3, starting transfers between devices, local(): lax.ppermute(message, 'seq', [(i, i + far) for i in range(n_seq - far)])  10.1 us
    pallas_call x5, Pallas kernels, local(): call(functools.partial(project, [(d, part.shape[0], skip) for d, part, sk...  9.32 us
    all_to_all x1, starting transfers between devices, local(): lax.all_to_all(gated.reshape(n_tensor, tok_own, width), 'tensor', 0, 0)  6.29 us
    all_to_all x1, waiting for transfers between devices, local(): lax.all_to_all(gated.reshape(n_tensor, tok_own, width), 'tensor', 0, 0)  4.24 us
    unnamed x40, local copies, waits for them, and re-layouts  3.33 us
    pallas_call x1, Pallas kernels, local(): call(functools.partial(product_early, where), shape(2 * tok_own, columns)...  2.55 us
  transfers between devices with their start and end apart: 24, of which 13 were waited for; matrix products, arithmetic and copies ran while one was open for 5% of the time, Pallas kernels for 15%

profile of v2, /device:TPU:0, one launch (start us, length us, event | category | flops | bytes accessed | tf_op | source)
XLA Modules:
  0.0 108.3 jit_solution(5100121613940767812)
XLA Ops:
  0.1 3.1 %collective-permute-start = (bf16[448,512]{1,0:T(8,128)(2,1)}, bf16[448,512]{1,0:T(8,128)(2,1)S(1)}, u32[]{:S(2)}, u32[]{:S(2)}) collective-permute-start(bf16[448,512]{1,0:T(8,128)(2,1)} %bitcast.10), channel_id=1, source_target_pairs={{0,2},{2,4},{4,6},{6,7},{7,5},{5,3},{3,1},{1,0},{8,10},{10,12},{12... | collective-permute-start | bytes 1376264 | tf_op jit(solution)/shard_map/ppermute | solution.py:30
  3.1 10.6 %collective-permute-done.refs_0_ = bf16[448,512]{1,0:T(8,128)(2,1)S(1)} collective-permute-done((bf16[448,512]{1,0:T(8,128)(2,1)}, bf16[448,512]{1,0:T(8,128)(2,1)S(1)}, u32[]{:S(2)}, u32[]{:S(2)}) %collective-permute-start) | collective-permute-done | bytes 458784 | tf_op jit(solution)/shard_map/ppermute | solution.py:30
  13.8 1.8 %collective-permute-start.1 = (bf16[448,512]{1,0:T(8,128)(2,1)S(1)}, bf16[448,512]{1,0:T(8,128)(2,1)}, u32[]{:S(2)}, u32[]{:S(2)}) collective-permute-start(bf16[448,512]{1,0:T(8,128)(2,1)S(1)} %collective-permute-done.refs_0_), channel_id=1, source_target_pairs={{0,2},{2,4},{4,6},{6,7},{7,5},{5,3},{3,1},{1,0},{8,10},{10,12},{12... | collective-permute-start | bytes 1376264 | tf_op jit(solution)/shard_map/ppermute | solution.py:30
  15.6 0.8 copy-done.7
  16.4 0.2 collective-permute-start.5
  16.6 0.8 copy-done.9
  17.4 8.2 %collective-permute-done.1.refs_0_ = bf16[448,512]{1,0:T(8,128)(2,1)} collective-permute-done((bf16[448,512]{1,0:T(8,128)(2,1)S(1)}, bf16[448,512]{1,0:T(8,128)(2,1)}, u32[]{:S(2)}, u32[]{:S(2)}) %collective-permute-start.1) | collective-permute-done | bytes 458784 | tf_op jit(solution)/shard_map/ppermute | solution.py:30
  25.6 1.5 %collective-permute-start.2 = (bf16[448,512]{1,0:T(8,128)(2,1)}, bf16[448,512]{1,0:T(8,128)(2,1)S(1)}, u32[]{:S(2)}, u32[]{:S(2)}) collective-permute-start(bf16[448,512]{1,0:T(8,128)(2,1)} %collective-permute-done.1.refs_0_), channel_id=1, source_target_pairs={{0,2},{2,4},{4,6},{6,7},{7,5},{5,3},{3,1},{1,0},{8,10},{10,12},{12... | collective-permute-start | bytes 1376264 | tf_op jit(solution)/shard_map/ppermute | solution.py:30
  27.1 0.5 collective-permute-done.5.refs_1_
  27.6 0.5 collective-permute-start.6
  28.1 8.5 %collective-permute-done.2.refs_0_ = bf16[448,512]{1,0:T(8,128)(2,1)S(1)} collective-permute-done((bf16[448,512]{1,0:T(8,128)(2,1)}, bf16[448,512]{1,0:T(8,128)(2,1)S(1)}, u32[]{:S(2)}, u32[]{:S(2)}) %collective-permute-start.2) | collective-permute-done | bytes 458784 | tf_op jit(solution)/shard_map/ppermute | solution.py:30
  36.6 1.3 %collective-permute-start.3 = (bf16[224,512]{1,0:T(8,128)(2,1)S(1)}, bf16[224,512]{1,0:T(8,128)(2,1)S(1)}, u32[]{:S(2)}, u32[]{:S(2)}) collective-permute-start(bf16[224,512]{1,0:T(8,128)(2,1)S(1)} %slice.60), channel_id=1, source_target_pairs={{0,2},{2,4},{4,6},{6,7},{7,5},{5,3},{3,1},{1,0},{8,10},{10,12},{12... | collective-permute-start | bytes 688136 | tf_op jit(solution)/shard_map/ppermute | solution.py:30
  37.9 0.2 collective-permute-done.6.refs_1_
  38.1 1.0 slice.61
  39.1 0.9 collective-permute-start.7
  40.0 1.2 %multiply_convert_fusion.rest_0_ = bf16[128,1792]{1,0:T(8,128)(2,1)S(1)} fusion(f32[128]{0:T(128)} %param.22, bf16[128,3584]{1,0:T(8,128)(2,1)} %param.23, s32[]{:T(128)S(6)} %select_n.24), kind=kLoop, calls=%fused_computation.1 | loop fusion | flops 688128 | bytes 918020 | tf_op jit(solution)/shard_map/convert_element_type | solution.py:344
  41.1 1.6 %collective-permute-done.3.refs_0_ = bf16[224,512]{1,0:T(8,128)(2,1)S(1)} collective-permute-done((bf16[224,512]{1,0:T(8,128)(2,1)S(1)}, bf16[224,512]{1,0:T(8,128)(2,1)S(1)}, u32[]{:S(2)}, u32[]{:S(2)}) %collective-permute-start.3) | collective-permute-done | bytes 229408 | tf_op jit(solution)/shard_map/ppermute | solution.py:30
  42.7 2.4 %collective-permute-done.7.refs_1_ = bf16[224,512]{1,0:T(8,128)(2,1)S(1)} collective-permute-done((bf16[224,512]{1,0:T(8,128)(2,1)S(1)}, bf16[224,512]{1,0:T(8,128)(2,1)S(1)}, u32[]{:S(2)}, u32[]{:S(2)}) %collective-permute-start.7) | collective-permute-done | bytes 229408 | tf_op jit(solution)/shard_map/ppermute | solution.py:30
  45.1 0.7 copy-done.11
  45.8 1.6 %collective-permute-start.14 = (bf16[128,1792]{1,0:T(8,128)(2,1)S(1)}, bf16[128,1792]{1,0:T(8,128)(2,1)}, u32[]{:S(2)}, u32[]{:S(2)}) collective-permute-start(bf16[128,1792]{1,0:T(8,128)(2,1)S(1)} %multiply_convert_fusion.rest_0_), channel_id=1, source_target_pairs={{0,2},{2,4},{4,6},{6,7},{7,5},{5,3},{3,1},{1,0},{8,10},{10,12},{12... | collective-permute-start | bytes 1376264 | tf_op jit(solution)/shard_map/ppermute | solution.py:30
  47.4 0.4 collective-permute-start.15
  47.9 0.1 slice.48
  47.9 1.3 %collective-permute-start.9 = (s32[8]{0:T(128)S(1)}, s32[8]{0:T(128)S(1)}, u32[]{:S(2)}, u32[]{:S(2)}) collective-permute-start(s32[8]{0:T(128)S(1)} %slice.48), channel_id=1, source_target_pairs={{0,8},{8,16},{16,24},{1,9},{9,17},{17,25},{2,10},{10,18},{18,26},{... | collective-permute-start | bytes 104 | tf_op jit(solution)/shard_map/ppermute | solution.py:311
  49.2 0.1 slice.52
  49.4 0.1 broadcast_in_dim_reshape.10.rate
  49.5 0.1 broadcast_in_dim_reshape.11.skip
  49.7 0.1 broadcast_in_dim_reshape.9.bias
  49.8 0.1 slice.58.seg_ext
  49.9 0.5 convolution_bitcast_fusion.refs_3_.refs_4_
  50.4 1.0 copy-done.6
  51.4 0.6 shard_map.127.refs_5_
  52.0 0.6 fusion.1
  52.7 1.8 %collective-permute-done.14.rest_1_ = bf16[128,1792]{1,0:T(8,128)(2,1)} collective-permute-done((bf16[128,1792]{1,0:T(8,128)(2,1)S(1)}, bf16[128,1792]{1,0:T(8,128)(2,1)}, u32[]{:S(2)}, u32[]{:S(2)}) %collective-permute-start.14) | collective-permute-done | bytes 458784 | tf_op jit(solution)/shard_map/ppermute | solution.py:30
  54.4 1.6 %collective-permute-start.16 = (bf16[128,1792]{1,0:T(8,128)(2,1)}, bf16[128,1792]{1,0:T(8,128)(2,1)}, u32[]{:S(2)}, u32[]{:S(2)}) collective-permute-start(bf16[128,1792]{1,0:T(8,128)(2,1)} %collective-permute-done.14.rest_1_), channel_id=1, source_target_pairs={{0,2},{2,4},{4,6},{6,7},{7,5},{5,3},{3,1},{1,0},{8,10},{10,12},{12... | collective-permute-start | bytes 1376264 | tf_op jit(solution)/shard_map/ppermute | solution.py:30
  56.0 0.4 collective-permute-start.17
  56.5 1.9 %shard_map.128.refs_5_ = f32[512,512]{1,0:T(8,128)S(1)} custom-call(bf16[448,512]{1,0:T(8,128)(2,1)S(1)} %copy-done.8, bf16[448,512]{1,0:T(8,128)(2,1)S(1)} %copy-done.10, bf16[2,3584,128]{2,1,0:T(8,128)(2,1)} %refs_2_.9, bf16[3584,128]{1,0:T(8,128)(2,1)S(1)} %copy-done.3, bf16[3584,128]{1,0:T(8,128)(2,1)S(1)} %convolution_bitcast_fusion.refs_3_.refs_4_, ...), custom_call_target="tpu_custom_call" | custom-call | flops 1000000000 | bytes 2097152 | tf_op jit(solution)/shard_map/pallas_call | solution.py:297
  58.4 3.1 %shard_map.129.refs_5_ = f32[512,512]{1,0:T(8,128)S(1)} custom-call(bf16[448,512]{1,0:T(8,128)(2,1)} %collective-permute-done.1.refs_0_, bf16[448,512]{1,0:T(8,128)(2,1)} %collective-permute-done.5.refs_1_, bf16[2,3584,128]{2,1,0:T(8,128)(2,1)} %refs_2_.9, bf16[3584,128]{1,0:T(8,128)(2,1)S(1)} %copy-done.3, ...), custom_call_target="tpu_custom_call" | custom-call | flops 1000000000 | bytes 2097152 | tf_op jit(solution)/shard_map/pallas_call | solution.py:297
  61.5 3.0 %shard_map.130.refs_5_ = f32[512,512]{1,0:T(8,128)S(1)} custom-call(bf16[448,512]{1,0:T(8,128)(2,1)S(1)} %copy-done.5, bf16[448,512]{1,0:T(8,128)(2,1)} %collective-permute-done.6.refs_1_, bf16[2,3584,128]{2,1,0:T(8,128)(2,1)} %refs_2_.9, bf16[3584,128]{1,0:T(8,128)(2,1)S(1)} %copy-done.3, bf16[3584,128]{1,0:T(8,128)(2,1)S(1)} %convolution_bitcast_fusion.refs_3_.refs_4_, ...), custom_call_target="tpu_custom_call" | custom-call | flops 1000000000 | bytes 2097152 | tf_op jit(solution)/shard_map/pallas_call | solution.py:297
  64.5 3.1 %collective-permute-done.16.rest_3_ = bf16[128,1792]{1,0:T(8,128)(2,1)} collective-permute-done((bf16[128,1792]{1,0:T(8,128)(2,1)}, bf16[128,1792]{1,0:T(8,128)(2,1)}, u32[]{:S(2)}, u32[]{:S(2)}) %collective-permute-start.16) | collective-permute-done | bytes 458784 | tf_op jit(solution)/shard_map/ppermute | solution.py:30
  67.6 1.6 %collective-permute-start.18 = (bf16[128,1792]{1,0:T(8,128)(2,1)}, bf16[128,1792]{1,0:T(8,128)(2,1)S(1)}, u32[]{:S(2)}, u32[]{:S(2)}) collective-permute-start(bf16[128,1792]{1,0:T(8,128)(2,1)} %collective-permute-done.16.rest_3_), channel_id=1, source_target_pairs={{0,2},{2,4},{4,6},{6,7},{7,5},{5,3},{3,1},{1,0},{8,10},{10,12},{12... | collective-permute-start | bytes 1376264 | tf_op jit(solution)/shard_map/ppermute | solution.py:30
  69.2 0.5 collective-permute-start.19
  69.7 0.8 shard_map.131.proj
  70.5 1.3 %collective-permute-start.8 = (bf16[8,256]{1,0:T(8,128)(2,1)S(1)}, bf16[8,256]{1,0:T(8,128)(2,1)S(1)}, u32[]{:S(2)}, u32[]{:S(2)}) collective-permute-start(bf16[8,256]{1,0:T(8,128)(2,1)S(1)} %slice.66), channel_id=1, source_target_pairs={{0,8},{8,16},{16,24},{1,9},{9,17},{17,25},{2,10},{10,18},{18,26},{... | collective-permute-start | bytes 12296 | tf_op jit(solution)/shard_map/ppermute | solution.py:316
  71.8 0.1 pad_add_fusion
  71.9 0.1 slice.59.seg_ext.seg_col
  72.0 1.0 shard_map.132
  73.0 1.2 %shard_map.133 = (f32[256,128]{1,0:T(8,128)S(1)}, f32[256,128]{1,0:T(8,128)S(1)}, f32[256,128]{1,0:T(8,128)S(1)}, f32[256,128]{1,0:T(8,128)S(1)}, f32[256,128]{1...) custom-call(f32[512,512]{1,0:T(8,128)S(1)} %shard_map.131.proj, ...), custom_call_target="tpu_custom_call" | custom-call | flops 10000000 | bytes 2097152 | tf_op jit(solution)/shard_map/pallas_call | solution.py:327
  74.2 5.2 %collective-permute-start.10 = (f32[72,128]{1,0:T(8,128)S(1)}, f32[72,128]{1,0:T(8,128)S(1)}, u32[]{:S(2)}, u32[]{:S(2)}) collective-permute-start(f32[72,128]{1,0:T(8,128)S(1)} %get-tuple-element.35), channel_id=1, source_target_pairs={{0,8},{8,16},{16,24},{1,9},{9,17},{17,25},{2,10},{10,18},{18,26},{... | collective-permute-start | bytes 110600 | tf_op jit(solution)/shard_map/ppermute | solution.py:333
  79.4 3.6 %collective-permute-start.11 = (f32[72,128]{1,0:T(8,128)S(1)}, f32[72,128]{1,0:T(8,128)S(1)}, u32[]{:S(2)}, u32[]{:S(2)}) collective-permute-start(f32[72,128]{1,0:T(8,128)S(1)} %get-tuple-element.35), channel_id=1, source_target_pairs={{0,16},{8,24},{1,17},{9,25},{2,18},{10,26},{3,19},{11,27},{4,20},{... | collective-permute-start | bytes 110600 | tf_op jit(solution)/shard_map/ppermute | solution.py:333
  83.0 1.3 %collective-permute-start.12 = (f32[72,128]{1,0:T(8,128)S(1)}, f32[72,128]{1,0:T(8,128)S(1)}, u32[]{:S(2)}, u32[]{:S(2)}) collective-permute-start(f32[72,128]{1,0:T(8,128)S(1)} %get-tuple-element.35), channel_id=1, source_target_pairs={{0,24},{1,25},{2,26},{3,27},{4,28},{5,29},{6,30},{7,31}} | collective-permute-start | bytes 110600 | tf_op jit(solution)/shard_map/ppermute | solution.py:333
  84.3 0.5 shard_map.134
  84.8 1.1 %collective-permute-done.12.rest_2_ = f32[72,128]{1,0:T(8,128)S(1)} collective-permute-done((f32[72,128]{1,0:T(8,128)S(1)}, f32[72,128]{1,0:T(8,128)S(1)}, u32[]{:S(2)}, u32[]{:S(2)}) %collective-permute-start.12) | collective-permute-done | bytes 36896 | tf_op jit(solution)/shard_map/ppermute | solution.py:333
  85.9 1.5 %shard_map.135 = bf16[512,128]{1,0:T(8,128)(2,1)} custom-call(s32[1,1]{1,0:T(1,128)} %bitcast.seg_first, f32[256,128]{1,0:T(8,128)S(1)} %get-tuple-element.27.out_a, f32[256,128]{1,0:T(8,128)S(1)} %get-tuple-element.28.gate_a, f32[256,128]{1,0:T(8,128)S(1)} %get-tuple-element.24.conv_bc.bc_a, f32[256,128]{1,0:T(8,128)S(1)} %get-tuple-element.29.enter_a, ...), custom_call_target="tpu_custom_call" | custom-call | flops 10000000 | bytes 2097152 | tf_op jit(solution)/shard_map/pallas_call | solution.py:338
  87.5 6.3 %all-to-all-start = ((bf16[8,64,128]{2,1,0:T(8,128)(2,1)}), bf16[8,64,128]{2,1,0:T(8,128)(2,1)S(1)}, u32[]{:S(2)}, u32[]{:S(2)}) async-start(bf16[8,64,128]{2,1,0:T(8,128)(2,1)} %bitcast.6), calls=%async_computation | async-start | bytes 262144 | tf_op jit(solution)/shard_map/all_to_all | solution.py:349
  93.8 2.1 %collective-permute-start.20 = (bf16[64,1792]{1,0:T(8,128)(2,1)S(1)}, bf16[64,1792]{1,0:T(8,128)(2,1)S(1)}, u32[]{:S(2)}, u32[]{:S(2)}) collective-permute-start(bf16[64,1792]{1,0:T(8,128)(2,1)S(1)} %slice.63), channel_id=1, source_target_pairs={{0,2},{2,4},{4,6},{6,7},{7,5},{5,3},{3,1},{1,0},{8,10},{10,12},{12... | collective-permute-start | bytes 688136 | tf_op jit(solution)/shard_map/ppermute | solution.py:30
  95.8 1.0 slice.64
  96.8 0.1 collective-permute-start.21
  96.9 4.2 %all-to-all-done.mine = bf16[8,64,128]{2,1,0:T(8,128)(2,1)S(1)} async-done(((bf16[8,64,128]{2,1,0:T(8,128)(2,1)}), bf16[8,64,128]{2,1,0:T(8,128)(2,1)S(1)}, u32[]{:S(2)}, u32[]{:S(2)}) %all-to-all-start) | async-done | bytes 131104 | tf_op jit(solution)/shard_map/all_to_all | solution.py:349
  101.1 1.3 %collective-permute-done.13.other = bf16[8,64,128]{2,1,0:T(8,128)(2,1)S(1)} collective-permute-done((bf16[8,64,128]{2,1,0:T(8,128)(2,1)S(1)}, bf16[8,64,128]{2,1,0:T(8,128)(2,1)S(1)}, u32[]{:S(2)}, u32[]{:S(2)}) %collective-permute-start.13) | collective-permute-done | bytes 131104 | tf_op jit(solution)/shard_map/ppermute | solution.py:350
  102.5 2.5 %shard_map.136.total = f32[128,1792]{1,0:T(8,128)S(1)} custom-call(bf16[8,64,128]{2,1,0:T(8,128)(2,1)S(1)} %all-to-all-done.mine, bf16[8,64,128]{2,1,0:T(8,128)(2,1)S(1)} %collective-permute-done.13.other, bf16[128,1792]{1,0:T(8,128)(2,1)S(1)} %multiply_convert_fusion.rest_0_, bf16[128,1792]{1,0:T(8,128)(2,1)} %collective-permute-done.14.rest_1_, ...), custom_call_target="tpu_custom_call" | custom-call | flops 1000000000 | bytes 2097152 | tf_op jit(solution)/shard_map/pallas_call | solution.py:355
  105.0 0.9 shard_map.137
  105.9 0.2 collective-permute-start.22
  106.2 1.3 %collective-permute-done.22 = bf16[64,1792]{1,0:T(8,128)(2,1)S(1)} collective-permute-done((bf16[64,1792]{1,0:T(8,128)(2,1)S(1)}, bf16[64,1792]{1,0:T(8,128)(2,1)S(1)}, u32[]{:S(2)}, u32[]{:S(2)}) %collective-permute-start.22) | collective-permute-done | bytes 229408 | tf_op jit(solution)/shard_map/ppermute | solution.py:371
  107.5 0.8 pad_maximum_fusion
  (58 shorter events, 0.4 us)
Async XLA Ops:
  0.0 49.9 %copy-start = (bf16[3584,2]{0,1:T(2,128)(2,1)S(1)}, bf16[3584,2]{0,1:T(2,128)(2,1)}, u32[]{:S(2)}) copy-start(bf16[3584,2]{0,1:T(2,128)(2,1)} %param.16) | copy-start | bytes 43012
  0.0 49.9 %copy-start.16 = (bf16[2,128]{1,0:T(2,128)(2,1)S(1)}, bf16[2,128]{1,0:T(2,128)(2,1)}, u32[]{:S(2)}) copy-start(bf16[2,128]{1,0:T(2,128)(2,1)} %constant.25.clone) | copy-start | bytes 1540
  0.0 47.9 %copy-start.15 = (s32[512]{0:T(512)S(1)}, s32[512]{0:T(512)}, u32[]{:S(2)}) copy-start(s32[512]{0:T(512)} %param.24) | copy-start | bytes 6148
  0.0 49.3 %copy-start.17 = (f32[2]{0:T(128)S(1)}, f32[2]{0:T(128)}, u32[]{:S(2)}) copy-start(f32[2]{0:T(128)} %param.18) | copy-start | bytes 28
  0.0 49.4 %copy-start.18 = (f32[2]{0:T(128)S(1)}, f32[2]{0:T(128)}, u32[]{:S(2)}) copy-start(f32[2]{0:T(128)} %param.19) | copy-start | bytes 28
  0.0 49.6 %copy-start.19 = (f32[2]{0:T(128)S(1)}, f32[2]{0:T(128)}, u32[]{:S(2)}) copy-start(f32[2]{0:T(128)} %param.17) | copy-start | bytes 28
  0.0 50.3 %copy-start.1 = (bf16[2,3584,128]{2,1,0:T(8,128)(2,1)S(1)}, bf16[2,3584,128]{2,1,0:T(8,128)(2,1)}, u32[]{:S(2)}) copy-start(bf16[2,3584,128]{2,1,0:T(8,128)(2,1)} %refs_2_.9) | copy-start | bytes 5505028
  0.0 50.3 %copy-start.3 = (bf16[3584,128]{1,0:T(8,128)(2,1)S(1)}, bf16[3584,128]{1,0:T(8,128)(2,1)}, u32[]{:S(2)}) copy-start(bf16[3584,128]{1,0:T(8,128)(2,1)} %refs_3_.7) | copy-start | bytes 2752516
  0.1 13.7 %collective-permute-start = (bf16[448,512]{1,0:T(8,128)(2,1)}, bf16[448,512]{1,0:T(8,128)(2,1)S(1)}, u32[]{:S(2)}, u32[]{:S(2)}) collective-permute-start(bf16[448,512]{1,0:T(8,128)(2,1)} %bitcast.10), channel_id=1, source_target_pairs={{0,2},{2,4},{4,6},{6,7},{7,5},{5,3},{3,1},{1,0},{8,10},{10,12},{12... | collective-permute-start | bytes 1376264 | tf_op jit(solution)/shard_map/ppermute | solution.py:30
  3.1 13.2 %collective-permute-start.4 = (bf16[448,512]{1,0:T(8,128)(2,1)}, bf16[448,512]{1,0:T(8,128)(2,1)S(1)}, u32[]{:S(2)}, u32[]{:S(2)}) collective-permute-start(bf16[448,512]{1,0:T(8,128)(2,1)} %bitcast.11), channel_id=1, source_target_pairs={{0,1},{2,0},{4,2},{6,4},{7,6},{5,7},{3,5},{1,3},{8,9},{10,8},{12,1... | collective-permute-start | bytes 1376264 | tf_op jit(solution)/shard_map/ppermute | solution.py:30
  13.8 11.8 %collective-permute-start.1 = (bf16[448,512]{1,0:T(8,128)(2,1)S(1)}, bf16[448,512]{1,0:T(8,128)(2,1)}, u32[]{:S(2)}, u32[]{:S(2)}) collective-permute-start(bf16[448,512]{1,0:T(8,128)(2,1)S(1)} %collective-permute-done.refs_0_), channel_id=1, source_target_pairs={{0,2},{2,4},{4,6},{6,7},{7,5},{5,3},{3,1},{1,0},{8,10},{10,12},{12... | collective-permute-start | bytes 1376264 | tf_op jit(solution)/shard_map/ppermute | solution.py:30
  15.6 0.8 copy-start.7
  16.4 11.2 %collective-permute-start.5 = (bf16[448,512]{1,0:T(8,128)(2,1)S(1)}, bf16[448,512]{1,0:T(8,128)(2,1)}, u32[]{:S(2)}, u32[]{:S(2)}) collective-permute-start(bf16[448,512]{1,0:T(8,128)(2,1)S(1)} %collective-permute-done.4.refs_1_), channel_id=1, source_target_pairs={{0,1},{2,0},{4,2},{6,4},{7,6},{5,7},{3,5},{1,3},{8,9},{10,8},{12,1... | collective-permute-start | bytes 1376264 | tf_op jit(solution)/shard_map/ppermute | solution.py:30
  16.6 0.8 copy-start.9
  25.6 11.0 %collective-permute-start.2 = (bf16[448,512]{1,0:T(8,128)(2,1)}, bf16[448,512]{1,0:T(8,128)(2,1)S(1)}, u32[]{:S(2)}, u32[]{:S(2)}) collective-permute-start(bf16[448,512]{1,0:T(8,128)(2,1)} %collective-permute-done.1.refs_0_), channel_id=1, source_target_pairs={{0,2},{2,4},{4,6},{6,7},{7,5},{5,3},{3,1},{1,0},{8,10},{10,12},{12... | collective-permute-start | bytes 1376264 | tf_op jit(solution)/shard_map/ppermute | solution.py:30
  27.6 10.5 %collective-permute-start.6 = (bf16[448,512]{1,0:T(8,128)(2,1)}, bf16[448,512]{1,0:T(8,128)(2,1)}, u32[]{:S(2)}, u32[]{:S(2)}) collective-permute-start(bf16[448,512]{1,0:T(8,128)(2,1)} %collective-permute-done.5.refs_1_), channel_id=1, source_target_pairs={{0,1},{2,0},{4,2},{6,4},{7,6},{5,7},{3,5},{1,3},{8,9},{10,8},{12,1... | collective-permute-start | bytes 1376264 | tf_op jit(solution)/shard_map/ppermute | solution.py:30
  36.6 2.5 %copy-start.4 = (bf16[448,512]{1,0:T(8,128)(2,1)}, bf16[448,512]{1,0:T(8,128)(2,1)S(1)}, u32[]{:S(2)}) copy-start(bf16[448,512]{1,0:T(8,128)(2,1)S(1)} %collective-permute-done.2.refs_0_) | copy-start | bytes 1376260
  36.6 6.1 %collective-permute-start.3 = (bf16[224,512]{1,0:T(8,128)(2,1)S(1)}, bf16[224,512]{1,0:T(8,128)(2,1)S(1)}, u32[]{:S(2)}, u32[]{:S(2)}) collective-permute-start(bf16[224,512]{1,0:T(8,128)(2,1)S(1)} %slice.60), channel_id=1, source_target_pairs={{0,2},{2,4},{4,6},{6,7},{7,5},{5,3},{3,1},{1,0},{8,10},{10,12},{12... | collective-permute-start | bytes 688136 | tf_op jit(solution)/shard_map/ppermute | solution.py:30
  39.1 6.1 %collective-permute-start.7 = (bf16[224,512]{1,0:T(8,128)(2,1)S(1)}, bf16[224,512]{1,0:T(8,128)(2,1)S(1)}, u32[]{:S(2)}, u32[]{:S(2)}) collective-permute-start(bf16[224,512]{1,0:T(8,128)(2,1)S(1)} %slice.61), channel_id=1, source_target_pairs={{0,1},{2,0},{4,2},{6,4},{7,6},{5,7},{3,5},{1,3},{8,9},{10,8},{12,1... | collective-permute-start | bytes 688136 | tf_op jit(solution)/shard_map/ppermute | solution.py:30
  45.1 0.7 copy-start.11
  45.8 8.6 %collective-permute-start.14 = (bf16[128,1792]{1,0:T(8,128)(2,1)S(1)}, bf16[128,1792]{1,0:T(8,128)(2,1)}, u32[]{:S(2)}, u32[]{:S(2)}) collective-permute-start(bf16[128,1792]{1,0:T(8,128)(2,1)S(1)} %multiply_convert_fusion.rest_0_), channel_id=1, source_target_pairs={{0,2},{2,4},{4,6},{6,7},{7,5},{5,3},{3,1},{1,0},{8,10},{10,12},{12... | collective-permute-start | bytes 1376264 | tf_op jit(solution)/shard_map/ppermute | solution.py:30
  47.4 8.6 %collective-permute-start.15 = (bf16[128,1792]{1,0:T(8,128)(2,1)S(1)}, bf16[128,1792]{1,0:T(8,128)(2,1)}, u32[]{:S(2)}, u32[]{:S(2)}) collective-permute-start(bf16[128,1792]{1,0:T(8,128)(2,1)S(1)} %multiply_convert_fusion.rest_0_), channel_id=1, source_target_pairs={{0,1},{2,0},{4,2},{6,4},{7,6},{5,7},{3,5},{1,3},{8,9},{10,8},{12,1... | collective-permute-start | bytes 1376264 | tf_op jit(solution)/shard_map/ppermute | solution.py:30
  47.9 23.8 %collective-permute-start.9 = (s32[8]{0:T(128)S(1)}, s32[8]{0:T(128)S(1)}, u32[]{:S(2)}, u32[]{:S(2)}) collective-permute-start(s32[8]{0:T(128)S(1)} %slice.48), channel_id=1, source_target_pairs={{0,8},{8,16},{16,24},{1,9},{9,17},{17,25},{2,10},{10,18},{18,26},{... | collective-permute-start | bytes 104 | tf_op jit(solution)/shard_map/ppermute | solution.py:311
  50.4 1.0 copy-start.6
  51.4 5.1 %copy-start.8 = (bf16[448,512]{1,0:T(8,128)(2,1)S(1)}, bf16[448,512]{1,0:T(8,128)(2,1)}, u32[]{:S(2)}) copy-start(bf16[448,512]{1,0:T(8,128)(2,1)} %copy-done.7) | copy-start | bytes 1376260
  51.4 5.1 %copy-start.10 = (bf16[448,512]{1,0:T(8,128)(2,1)S(1)}, bf16[448,512]{1,0:T(8,128)(2,1)}, u32[]{:S(2)}) copy-start(bf16[448,512]{1,0:T(8,128)(2,1)} %copy-done.9) | copy-start | bytes 1376260
  54.4 13.2 %collective-permute-start.16 = (bf16[128,1792]{1,0:T(8,128)(2,1)}, bf16[128,1792]{1,0:T(8,128)(2,1)}, u32[]{:S(2)}, u32[]{:S(2)}) collective-permute-start(bf16[128,1792]{1,0:T(8,128)(2,1)} %collective-permute-done.14.rest_1_), channel_id=1, source_target_pairs={{0,2},{2,4},{4,6},{6,7},{7,5},{5,3},{3,1},{1,0},{8,10},{10,12},{12... | collective-permute-start | bytes 1376264 | tf_op jit(solution)/shard_map/ppermute | solution.py:30
  56.0 13.2 %collective-permute-start.17 = (bf16[128,1792]{1,0:T(8,128)(2,1)}, bf16[128,1792]{1,0:T(8,128)(2,1)}, u32[]{:S(2)}, u32[]{:S(2)}) collective-permute-start(bf16[128,1792]{1,0:T(8,128)(2,1)} %collective-permute-done.15.rest_2_), channel_id=1, source_target_pairs={{0,1},{2,0},{4,2},{6,4},{7,6},{5,7},{3,5},{1,3},{8,9},{10,8},{12,1... | collective-permute-start | bytes 1376264 | tf_op jit(solution)/shard_map/ppermute | solution.py:30
  58.4 3.1 %copy-start.5 = (bf16[448,512]{1,0:T(8,128)(2,1)S(1)}, bf16[448,512]{1,0:T(8,128)(2,1)}, u32[]{:S(2)}) copy-start(bf16[448,512]{1,0:T(8,128)(2,1)} %copy-done.4) | copy-start | bytes 1376260
  61.5 8.2 %copy-start.2 = (bf16[2,3584,128]{2,1,0:T(8,128)(2,1)S(1)}, bf16[2,3584,128]{2,1,0:T(8,128)(2,1)}, u32[]{:S(2)}) copy-start(bf16[2,3584,128]{2,1,0:T(8,128)(2,1)} %refs_2_.9) | copy-start | bytes 5505028
  61.5 8.2 %copy-start.12 = (bf16[224,512]{1,0:T(8,128)(2,1)S(1)}, bf16[224,512]{1,0:T(8,128)(2,1)}, u32[]{:S(2)}) copy-start(bf16[224,512]{1,0:T(8,128)(2,1)} %copy-done.11) | copy-start | bytes 688132
  64.5 7.5 %copy-start.13 = (f32[4,128]{1,0:T(4,128)S(1)}, f32[4,128]{1,0:T(4,128)}, u32[]{:S(2)}) copy-start(f32[4,128]{1,0:T(4,128)} %taps_x.3) | copy-start | bytes 6148
  64.5 7.5 %copy-start.14 = (f32[4,128]{1,0:T(4,128)S(1)}, f32[4,128]{1,0:T(4,128)}, u32[]{:S(2)}) copy-start(f32[4,128]{1,0:T(4,128)} %taps_bc.3) | copy-start | bytes 6148
  67.6 26.1 %collective-permute-start.18 = (bf16[128,1792]{1,0:T(8,128)(2,1)}, bf16[128,1792]{1,0:T(8,128)(2,1)S(1)}, u32[]{:S(2)}, u32[]{:S(2)}) collective-permute-start(bf16[128,1792]{1,0:T(8,128)(2,1)} %collective-permute-done.16.rest_3_), channel_id=1, source_target_pairs={{0,2},{2,4},{4,6},{6,7},{7,5},{5,3},{3,1},{1,0},{8,10},{10,12},{12... | collective-permute-start | bytes 1376264 | tf_op jit(solution)/shard_map/ppermute | solution.py:30
  69.2 26.6 %collective-permute-start.19 = (bf16[128,1792]{1,0:T(8,128)(2,1)}, bf16[128,1792]{1,0:T(8,128)(2,1)}, u32[]{:S(2)}, u32[]{:S(2)}) collective-permute-start(bf16[128,1792]{1,0:T(8,128)(2,1)} %collective-permute-done.17.rest_4_), channel_id=1, source_target_pairs={{0,1},{2,0},{4,2},{6,4},{7,6},{5,7},{3,5},{1,3},{8,9},{10,8},{12,1... | collective-permute-start | bytes 1376264 | tf_op jit(solution)/shard_map/ppermute | solution.py:30
  70.5 2.5 %collective-permute-start.8 = (bf16[8,256]{1,0:T(8,128)(2,1)S(1)}, bf16[8,256]{1,0:T(8,128)(2,1)S(1)}, u32[]{:S(2)}, u32[]{:S(2)}) collective-permute-start(bf16[8,256]{1,0:T(8,128)(2,1)S(1)} %slice.66), channel_id=1, source_target_pairs={{0,8},{8,16},{16,24},{1,9},{9,17},{17,25},{2,10},{10,18},{18,26},{... | collective-permute-start | bytes 12296 | tf_op jit(solution)/shard_map/ppermute | solution.py:316
  74.2 10.6 %collective-permute-start.10 = (f32[72,128]{1,0:T(8,128)S(1)}, f32[72,128]{1,0:T(8,128)S(1)}, u32[]{:S(2)}, u32[]{:S(2)}) collective-permute-start(f32[72,128]{1,0:T(8,128)S(1)} %get-tuple-element.35), channel_id=1, source_target_pairs={{0,8},{8,16},{16,24},{1,9},{9,17},{17,25},{2,10},{10,18},{18,26},{... | collective-permute-start | bytes 110600 | tf_op jit(solution)/shard_map/ppermute | solution.py:333
  79.4 5.4 %collective-permute-start.11 = (f32[72,128]{1,0:T(8,128)S(1)}, f32[72,128]{1,0:T(8,128)S(1)}, u32[]{:S(2)}, u32[]{:S(2)}) collective-permute-start(f32[72,128]{1,0:T(8,128)S(1)} %get-tuple-element.35), channel_id=1, source_target_pairs={{0,16},{8,24},{1,17},{9,25},{2,18},{10,26},{3,19},{11,27},{4,20},{... | collective-permute-start | bytes 110600 | tf_op jit(solution)/shard_map/ppermute | solution.py:333
  83.0 2.9 %collective-permute-start.12 = (f32[72,128]{1,0:T(8,128)S(1)}, f32[72,128]{1,0:T(8,128)S(1)}, u32[]{:S(2)}, u32[]{:S(2)}) collective-permute-start(f32[72,128]{1,0:T(8,128)S(1)} %get-tuple-element.35), channel_id=1, source_target_pairs={{0,24},{1,25},{2,26},{3,27},{4,28},{5,29},{6,30},{7,31}} | collective-permute-start | bytes 110600 | tf_op jit(solution)/shard_map/ppermute | solution.py:333
  87.5 13.7 %all-to-all-start = ((bf16[8,64,128]{2,1,0:T(8,128)(2,1)}), bf16[8,64,128]{2,1,0:T(8,128)(2,1)S(1)}, u32[]{:S(2)}, u32[]{:S(2)}) async-start(bf16[8,64,128]{2,1,0:T(8,128)(2,1)} %bitcast.6), calls=%async_computation | async-start | bytes 262144 | tf_op jit(solution)/shard_map/all_to_all | solution.py:349
  93.8 11.2 %collective-permute-start.20 = (bf16[64,1792]{1,0:T(8,128)(2,1)S(1)}, bf16[64,1792]{1,0:T(8,128)(2,1)S(1)}, u32[]{:S(2)}, u32[]{:S(2)}) collective-permute-start(bf16[64,1792]{1,0:T(8,128)(2,1)S(1)} %slice.63), channel_id=1, source_target_pairs={{0,2},{2,4},{4,6},{6,7},{7,5},{5,3},{3,1},{1,0},{8,10},{10,12},{12... | collective-permute-start | bytes 688136 | tf_op jit(solution)/shard_map/ppermute | solution.py:30
  96.8 8.2 %collective-permute-start.21 = (bf16[64,1792]{1,0:T(8,128)(2,1)S(1)}, bf16[64,1792]{1,0:T(8,128)(2,1)S(1)}, u32[]{:S(2)}, u32[]{:S(2)}) collective-permute-start(bf16[64,1792]{1,0:T(8,128)(2,1)S(1)} %slice.64), channel_id=1, source_target_pairs={{0,1},{2,0},{4,2},{6,4},{7,6},{5,7},{3,5},{1,3},{8,9},{10,8},{12,1... | collective-permute-start | bytes 688136 | tf_op jit(solution)/shard_map/ppermute | solution.py:30
  101.1 1.3 %collective-permute-start.13 = (bf16[8,64,128]{2,1,0:T(8,128)(2,1)S(1)}, bf16[8,64,128]{2,1,0:T(8,128)(2,1)S(1)}, u32[]{:S(2)}, u32[]{:S(2)}) collective-permute-start(bf16[8,64,128]{2,1,0:T(8,128)(2,1)S(1)} %all-to-all-done.mine), channel_id=1, source_target_pairs={{0,8},{8,0},{16,24},{24,16},{1,9},{9,1},{17,25},{25,17},{2,10},{10... | collective-permute-start | bytes 393224 | tf_op jit(solution)/shard_map/ppermute | solution.py:350
  105.9 1.6 %collective-permute-start.22 = (bf16[64,1792]{1,0:T(8,128)(2,1)S(1)}, bf16[64,1792]{1,0:T(8,128)(2,1)S(1)}, u32[]{:S(2)}, u32[]{:S(2)}) collective-permute-start(bf16[64,1792]{1,0:T(8,128)(2,1)S(1)} %get-tuple-element.38), channel_id=1, source_target_pairs={{0,8},{8,0},{16,24},{24,16},{1,9},{9,1},{17,25},{25,17},{2,10},{10... | collective-permute-start | bytes 688136 | tf_op jit(solution)/shard_map/ppermute | solution.py:371

commit v3 on v2

--- a/solution.py
+++ b/solution.py
@@ -30,16 +30,15 @@
     return lax.ppermute(block, "tensor", [(order[i], order[(i + step) % n]) for i in range(n)])
 
 
-def ring_gather(block):
-    n = lax.axis_size("tensor")
-    forth = back = block
-    steps = []
-    for _ in range(1, n // 2):
-        forth, back = ring_shift(forth, 1), ring_shift(back, -1)
-        steps.append((forth, back))
-    half = block.shape[0] // 32 * 16
-    steps.append((ring_shift(forth[:half], 1), ring_shift(back[half:], -1)))
-    return steps
+def after(values, *earlier):
+    return lax.optimization_barrier((values, earlier))[0]
+
+
+def ring_step(forth, back, step):
+    if step < lax.axis_size("tensor") // 2:
+        return ring_shift(forth, 1), ring_shift(back, -1)
+    half = forth.shape[0] // 32 * 16
+    return ring_shift(forth[:half], 1), ring_shift(back[half:], -1)
 
 
 def silu(v):
@@ -286,26 +285,33 @@
     expand = np.repeat(np.eye(heads, dtype=np.float32), head_w, axis=1)
     w_step = jnp.dot(w_dt, expand.astype(BF16))
     block = tokens.T
-    steps = ring_gather(block)
     last = n_tensor // 2
-    arrivals = [[(0, block, 0)]]
-    arrivals += [[(-i - 1, forth, 0), (i + 1, back, 0)] for i, (forth, back) in enumerate(steps[:-1])]
-    arrivals += [[(last, steps[-1][0], 0), (last, steps[-1][1], steps[-1][0].shape[0])]]
-    proj = ()
-    for arrived in arrivals:
-        proj = (
+    forth = back = block
+    arrived, projs = [(0, block, 0)], []
+    for step in range(1, last + 2):
+        if step <= last:
+            if step > 1:
+                forth, back = after((forth, back), projs[step - 2])
+            forth, back = ring_step(forth, back, step)
+        sizes = [(distance, part.shape[0], skip) for distance, part, skip in arrived]
+        total = projs[-1:]
+        projs.append(
             call(
-                functools.partial(project, [(d, part.shape[0], skip) for d, part, skip in arrived], not proj),
+                functools.partial(project, sizes, not total),
                 shape(tok_rows, 4 * width),
                 [
-                    pltpu.VMEM((len(arrived), max(part.shape[0] for _, part, _ in arrived), 4 * width), BF16),
-                    pltpu.SemaphoreType.DMA((len(arrived), 4)),
+                    pltpu.VMEM((len(sizes), max(size for _, size, _ in sizes), 4 * width), BF16),
+                    pltpu.SemaphoreType.DMA((len(sizes), 4)),
                 ],
-                in_specs=[VMEM] * len(arrived) + [ANY] * 3 + [VMEM] * len(proj),
+                in_specs=[VMEM] * len(sizes) + [ANY] * 3 + [VMEM] * len(total),
                 flops=10**9,
-            )(*[part for _, part, _ in arrived], w_zx, w_bc, w_step, *proj),
+            )(*[part for _, part, _ in arrived], w_zx, w_bc, w_step, *total)
         )
-    (proj,) = proj
+        arrived = [(-step, forth, 0), (step, back, 0)]
+        if step == last:
+            arrived = [(last, forth, 0), (last, back, forth.shape[0])]
+    proj = projs[-1]
+    tokens_there = (forth, back, projs[-2])
 
     ahead = [(i, i + 1) for i in range(n_seq - 1)]
     seg_halo = lax.ppermute(segments[tok_rows - HALO :], "seq", ahead)
@@ -339,14 +345,21 @@
         functools.partial(finish, len(messages), rows), shape(tok_rows, width, kind=BF16)
     )(seg_first, out_a, gate_a, bc_a, enter_a, state_a, out_b, gate_b, bc_b, enter_b, *messages)
 
+    tok_own = tok_rows // n_tensor
+    mine = lax.all_to_all(gated.reshape(n_tensor, tok_own, width), "tensor", 0, 0)
+
     core = seq_at % 2
     columns = model // 2
     own = (lax.dynamic_slice_in_dim(w_out, core * columns, columns, 1).astype(F32) * norm_gain[:, None]).astype(BF16)
-    own_first, _ = lax.optimization_barrier((own, steps[-1]))
-    w_steps = ring_gather(own_first)
+    orders = [tokens_there, messages, mine]
+    forth = back = own
+    w_steps = []
+    for step in range(1, last + 1):
+        if step <= len(orders):
+            forth, back = after((forth, back), orders[step - 1])
+        forth, back = ring_step(forth, back, step)
+        w_steps.append((forth, back))
     swap = [(i, i ^ 1) for i in range(n_seq)]
-    tok_own = tok_rows // n_tensor
-    mine = lax.all_to_all(gated.reshape(n_tensor, tok_own, width), "tensor", 0, 0)
     other = lax.ppermute(mine, "seq", swap)
     pieces, where = [own], [(0, 0, 0)]
     for i, pair in enumerate(w_steps[:-1]):

time: 109 us -> 106 us (0.972)
  the two profiles are of different devices: /device:TPU:0 before, /device:TPU:5 now
where the time goes in v3:
time: 106 us
  waiting for transfers between devices  42 us (40%)
  starting transfers between devices  21.1 us (20%)
  Pallas kernels  17.9 us (17%)
  blocking collectives  12.4 us (12%)
  local copies, waits for them, and re-layouts  9.55 us (9%)
  matrix products  1.11 us (1%)
    ppermute x16, waiting for transfers between devices, ring_shift(): lax.ppermute(block, 'tensor', [(order[i], order[(i + step) % n]) for i in...  26.6 us
    all_to_all x1, blocking collectives, local(): lax.all_to_all(gated.reshape(n_tensor, tok_own, width), 'tensor', 0, 0)  12.4 us
    ppermute x16, starting transfers between devices, ring_shift(): lax.ppermute(block, 'tensor', [(order[i], order[(i + step) % n]) for i in...  11.9 us
    pallas_call x5, Pallas kernels, local(): call(functools.partial(project, sizes, not total), shape(tok_rows, 4 * wi...  10.4 us
    ppermute x3, waiting for transfers between devices, local(): lax.ppermute(message, 'seq', [(i, i + far) for i in range(n_seq - far)])  6.86 us
    ppermute x1, waiting for transfers between devices, local(): lax.ppermute(proj[tok_rows - HALO:, width:3 * width].astype(BF16), 'seq',...  6.42 us
    unnamed x36, local copies, waits for them, and re-layouts  5.77 us
    ppermute x3, starting transfers between devices, local(): lax.ppermute(message, 'seq', [(i, i + far) for i in range(n_seq - far)])  3.88 us
  transfers between devices with their start and end apart: 23, of which 13 were waited for; matrix products, arithmetic and copies ran while one was open for 5% of the time, Pallas kernels for 16%

profile of v3, /device:TPU:5, one launch (start us, length us, event | category | flops | bytes accessed | tf_op | source)
XLA Modules:
  0.0 105.5 jit_solution(2279391110142845641)
XLA Ops:
  0.0 1.3 %collective-permute-start = (bf16[448,512]{1,0:T(8,128)(2,1)}, bf16[448,512]{1,0:T(8,128)(2,1)S(1)}, u32[]{:S(2)}, u32[]{:S(2)}) collective-permute-start(bf16[448,512]{1,0:T(8,128)(2,1)} %bitcast.11), channel_id=1, source_target_pairs={{0,2},{2,4},{4,6},{6,7},{7,5},{5,3},{3,1},{1,0},{8,10},{10,12},{12... | collective-permute-start | bytes 1376264 | tf_op jit(solution)/shard_map/ppermute | solution.py:30
  1.3 0.2 collective-permute-start.1
  1.5 1.1 %convolution_bitcast_fusion.refs_3_.refs_4_ = bf16[3584,128]{1,0:T(8,128)(2,1)S(1)} fusion(bf16[2,128]{1,0:T(2,128)(2,1)} %constant.25.clone, bf16[3584,2]{0,1:T(2,128)(2,1)S(1)} %copy-done), kind=kOutput, calls=%fused_computation | convolution fusion | flops 1835008 | bytes 932352 | tf_op jit(solution)/shard_map/dot_general | solution.py:286
  2.6 1.5 %copy-done.1 = bf16[2,3584,128]{2,1,0:T(8,128)(2,1)S(1)} copy-done((bf16[2,3584,128]{2,1,0:T(8,128)(2,1)S(1)}, bf16[2,3584,128]{2,1,0:T(8,128)(2,1)}, u32[]{:S(2)}) %copy-start.1) | copy-done | bytes 1835032
  4.1 1.2 %copy-done.3 = bf16[3584,128]{1,0:T(8,128)(2,1)S(1)} copy-done((bf16[3584,128]{1,0:T(8,128)(2,1)S(1)}, bf16[3584,128]{1,0:T(8,128)(2,1)}, u32[]{:S(2)}) %copy-start.3) | copy-done | bytes 917528
  5.3 1.0 copy-done.9
  6.3 0.6 shard_map.127.refs_5_
  6.9 4.7 %collective-permute-done.refs_0_ = bf16[448,512]{1,0:T(8,128)(2,1)S(1)} collective-permute-done((bf16[448,512]{1,0:T(8,128)(2,1)}, bf16[448,512]{1,0:T(8,128)(2,1)S(1)}, u32[]{:S(2)}, u32[]{:S(2)}) %collective-permute-start) | collective-permute-done | bytes 458784 | tf_op jit(solution)/shard_map/ppermute | solution.py:30
  11.6 1.0 collective-permute-done.1.refs_1_
  12.6 1.3 %collective-permute-start.2 = (bf16[448,512]{1,0:T(8,128)(2,1)S(1)}, bf16[448,512]{1,0:T(8,128)(2,1)}, u32[]{:S(2)}, u32[]{:S(2)}) collective-permute-start(bf16[448,512]{1,0:T(8,128)(2,1)S(1)} %collective-permute-done.refs_0_), channel_id=1, source_target_pairs={{0,2},{2,4},{4,6},{6,7},{7,5},{5,3},{3,1},{1,0},{8,10},{10,12},{12... | collective-permute-start | bytes 1376264 | tf_op jit(solution)/shard_map/ppermute | solution.py:30
  13.9 0.2 collective-permute-start.3
  14.1 1.8 %shard_map.128.refs_5_ = f32[512,512]{1,0:T(8,128)S(1)} custom-call(bf16[448,512]{1,0:T(8,128)(2,1)S(1)} %collective-permute-done.refs_0_, bf16[448,512]{1,0:T(8,128)(2,1)S(1)} %collective-permute-done.1.refs_1_, bf16[2,3584,128]{2,1,0:T(8,128)(2,1)} %refs_2_.9, bf16[3584,128]{1,0:T(8,128)(2,1)S(1)} %copy-done.4, ...), custom_call_target="tpu_custom_call" | custom-call | flops 1000000000 | bytes 2097152 | tf_op jit(solution)/shard_map/pallas_call | solution.py:299
  15.9 6.9 %collective-permute-done.2.refs_0_ = bf16[448,512]{1,0:T(8,128)(2,1)} collective-permute-done((bf16[448,512]{1,0:T(8,128)(2,1)S(1)}, bf16[448,512]{1,0:T(8,128)(2,1)}, u32[]{:S(2)}, u32[]{:S(2)}) %collective-permute-start.2) | collective-permute-done | bytes 458784 | tf_op jit(solution)/shard_map/ppermute | solution.py:30
  22.8 1.0 collective-permute-done.3.refs_1_
  23.9 1.3 %collective-permute-start.4 = (bf16[448,512]{1,0:T(8,128)(2,1)}, bf16[448,512]{1,0:T(8,128)(2,1)S(1)}, u32[]{:S(2)}, u32[]{:S(2)}) collective-permute-start(bf16[448,512]{1,0:T(8,128)(2,1)} %collective-permute-done.2.refs_0_), channel_id=1, source_target_pairs={{0,2},{2,4},{4,6},{6,7},{7,5},{5,3},{3,1},{1,0},{8,10},{10,12},{12... | collective-permute-start | bytes 1376264 | tf_op jit(solution)/shard_map/ppermute | solution.py:30
  25.1 0.2 collective-permute-start.5
  25.4 1.3 %collective-permute-start.9 = (s32[8]{0:T(128)S(1)}, s32[8]{0:T(128)S(1)}, u32[]{:S(2)}, u32[]{:S(2)}) collective-permute-start(s32[8]{0:T(128)S(1)} %slice.48), channel_id=1, source_target_pairs={{0,8},{8,16},{16,24},{1,9},{9,17},{17,25},{2,10},{10,18},{18,26},{... | collective-permute-start | bytes 104 | tf_op jit(solution)/shard_map/ppermute | solution.py:317
  26.7 3.1 %shard_map.129.refs_5_ = f32[512,512]{1,0:T(8,128)S(1)} custom-call(bf16[448,512]{1,0:T(8,128)(2,1)} %collective-permute-done.2.refs_0_, bf16[448,512]{1,0:T(8,128)(2,1)} %collective-permute-done.3.refs_1_, bf16[2,3584,128]{2,1,0:T(8,128)(2,1)} %refs_2_.9, bf16[3584,128]{1,0:T(8,128)(2,1)S(1)} %copy-done.4, ...), custom_call_target="tpu_custom_call" | custom-call | flops 1000000000 | bytes 2097152 | tf_op jit(solution)/shard_map/pallas_call | solution.py:299
  29.8 1.0 copy-done.5
  30.8 2.3 %collective-permute-done.4.refs_0_ = bf16[448,512]{1,0:T(8,128)(2,1)S(1)} collective-permute-done((bf16[448,512]{1,0:T(8,128)(2,1)}, bf16[448,512]{1,0:T(8,128)(2,1)S(1)}, u32[]{:S(2)}, u32[]{:S(2)}) %collective-permute-start.4) | collective-permute-done | bytes 458784 | tf_op jit(solution)/shard_map/ppermute | solution.py:30
  33.1 1.0 collective-permute-done.5.refs_1_
  34.1 0.7 slice.45
  34.8 1.2 %collective-permute-start.6 = (bf16[224,512]{1,0:T(8,128)(2,1)}, bf16[224,512]{1,0:T(8,128)(2,1)}, u32[]{:S(2)}, u32[]{:S(2)}) collective-permute-start(bf16[224,512]{1,0:T(8,128)(2,1)} %slice.45), channel_id=1, source_target_pairs={{0,2},{2,4},{4,6},{6,7},{7,5},{5,3},{3,1},{1,0},{8,10},{10,12},{12... | collective-permute-start | bytes 688136 | tf_op jit(solution)/shard_map/ppermute | solution.py:30
  36.1 1.7 %slice.46 = bf16[224,512]{1,0:T(8,128)(2,1)} slice(bf16[448,512]{1,0:T(8,128)(2,1)} %collective-permute-done.5.refs_1_), slice={[224:448], [0:512]} | slice | bytes 458752 | tf_op jit(solution)/shard_map/slice | solution.py:41
  37.7 0.3 collective-permute-start.7
  38.0 0.1 multiply_convert_fusion.rest_0_
  38.1 0.1 slice.52
  38.2 0.1 slice.58.seg_ext
  38.4 0.1 broadcast_in_dim_reshape.9.bias
  38.5 0.1 broadcast_in_dim_reshape.10.rate
  38.7 0.1 broadcast_in_dim_reshape.11.skip
  38.8 0.6 fusion.1
  39.4 1.0 copy-done.8
  40.4 3.0 %shard_map.130.refs_5_ = f32[512,512]{1,0:T(8,128)S(1)} custom-call(bf16[448,512]{1,0:T(8,128)(2,1)S(1)} %copy-done.8, bf16[448,512]{1,0:T(8,128)(2,1)} %collective-permute-done.5.refs_1_, bf16[2,3584,128]{2,1,0:T(8,128)(2,1)} %refs_2_.9, bf16[3584,128]{1,0:T(8,128)(2,1)S(1)} %copy-done.4, bf16[3584,128]{1,0:T(8,128)(2,1)S(1)} %convolution_bitcast_fusion.refs_3_.refs_4_, ...), custom_call_target="tpu_custom_call" | custom-call | flops 1000000000 | bytes 2097152 | tf_op jit(solution)/shard_map/pallas_call | solution.py:299
  43.4 1.3 %collective-permute-start.14 = (bf16[128,1792]{1,0:T(8,128)(2,1)S(1)}, bf16[128,1792]{1,0:T(8,128)(2,1)S(1)}, u32[]{:S(2)}, u32[]{:S(2)}) collective-permute-start(bf16[128,1792]{1,0:T(8,128)(2,1)S(1)} %multiply_convert_fusion.rest_0_), channel_id=1, source_target_pairs={{0,2},{2,4},{4,6},{6,7},{7,5},{5,3},{3,1},{1,0},{8,10},{10,12},{12... | collective-permute-start | bytes 1376264 | tf_op jit(solution)/shard_map/ppermute | solution.py:30
  44.7 0.3 collective-permute-start.15
  45.0 1.8 %shard_map.131.proj = f32[512,512]{1,0:T(8,128)S(1)} custom-call(bf16[224,512]{1,0:T(8,128)(2,1)} %collective-permute-done.6.refs_0_, bf16[224,512]{1,0:T(8,128)(2,1)} %collective-permute-done.7.refs_1_, bf16[2,3584,128]{2,1,0:T(8,128)(2,1)S(1)} %copy-done.2, bf16[3584,128]{1,0:T(8,128)(2,1)S(1)} %copy-done.4, ...), custom_call_target="tpu_custom_call" | custom-call | flops 1000000000 | bytes 2097152 | tf_op jit(solution)/shard_map/pallas_call | solution.py:299
  46.8 1.3 %collective-permute-start.8 = (bf16[8,256]{1,0:T(8,128)(2,1)S(1)}, bf16[8,256]{1,0:T(8,128)(2,1)S(1)}, u32[]{:S(2)}, u32[]{:S(2)}) collective-permute-start(bf16[8,256]{1,0:T(8,128)(2,1)S(1)} %slice.64), channel_id=1, source_target_pairs={{0,8},{8,16},{16,24},{1,9},{9,17},{17,25},{2,10},{10,18},{18,26},{... | collective-permute-start | bytes 12296 | tf_op jit(solution)/shard_map/ppermute | solution.py:322
  48.1 0.1 pad_add_fusion
  48.2 0.1 slice.59.seg_ext.seg_col
  48.3 1.0 shard_map.132
  49.3 6.4 %collective-permute-done.8.halo = bf16[8,256]{1,0:T(8,128)(2,1)S(1)} collective-permute-done((bf16[8,256]{1,0:T(8,128)(2,1)S(1)}, bf16[8,256]{1,0:T(8,128)(2,1)S(1)}, u32[]{:S(2)}, u32[]{:S(2)}) %collective-permute-start.8) | collective-permute-done | bytes 4128 | tf_op jit(solution)/shard_map/ppermute | solution.py:322
  55.7 1.1 %shard_map.133 = (f32[256,128]{1,0:T(8,128)S(1)}, f32[256,128]{1,0:T(8,128)S(1)}, f32[256,128]{1,0:T(8,128)S(1)}, f32[256,128]{1,0:T(8,128)S(1)}, f32[256,128]{1...) custom-call(f32[512,512]{1,0:T(8,128)S(1)} %shard_map.131.proj, ...), custom_call_target="tpu_custom_call" | custom-call | flops 10000000 | bytes 2097152 | tf_op jit(solution)/shard_map/pallas_call | solution.py:333
  56.9 1.3 %collective-permute-start.10 = (f32[72,128]{1,0:T(8,128)S(1)}, f32[72,128]{1,0:T(8,128)S(1)}, u32[]{:S(2)}, u32[]{:S(2)}) collective-permute-start(f32[72,128]{1,0:T(8,128)S(1)} %get-tuple-element.52), channel_id=1, source_target_pairs={{0,8},{8,16},{16,24},{1,9},{9,17},{17,25},{2,10},{10,18},{18,26},{... | collective-permute-start | bytes 110600 | tf_op jit(solution)/shard_map/ppermute | solution.py:339
  58.2 1.3 %collective-permute-start.11 = (f32[72,128]{1,0:T(8,128)S(1)}, f32[72,128]{1,0:T(8,128)S(1)}, u32[]{:S(2)}, u32[]{:S(2)}) collective-permute-start(f32[72,128]{1,0:T(8,128)S(1)} %get-tuple-element.52), channel_id=1, source_target_pairs={{0,16},{8,24},{1,17},{9,25},{2,18},{10,26},{3,19},{11,27},{4,20},{... | collective-permute-start | bytes 110600 | tf_op jit(solution)/shard_map/ppermute | solution.py:339
  59.5 1.3 %collective-permute-start.12 = (f32[72,128]{1,0:T(8,128)S(1)}, f32[72,128]{1,0:T(8,128)S(1)}, u32[]{:S(2)}, u32[]{:S(2)}) collective-permute-start(f32[72,128]{1,0:T(8,128)S(1)} %get-tuple-element.52), channel_id=1, source_target_pairs={{0,24},{1,25},{2,26},{3,27},{4,28},{5,29},{6,30},{7,31}} | collective-permute-start | bytes 110600 | tf_op jit(solution)/shard_map/ppermute | solution.py:339
  60.8 1.1 %collective-permute-done.10.rest_0_ = f32[72,128]{1,0:T(8,128)S(1)} collective-permute-done((f32[72,128]{1,0:T(8,128)S(1)}, f32[72,128]{1,0:T(8,128)S(1)}, u32[]{:S(2)}, u32[]{:S(2)}) %collective-permute-start.10) | collective-permute-done | bytes 36896 | tf_op jit(solution)/shard_map/ppermute | solution.py:339
  61.8 3.3 %collective-permute-done.11.rest_1_ = f32[72,128]{1,0:T(8,128)S(1)} collective-permute-done((f32[72,128]{1,0:T(8,128)S(1)}, f32[72,128]{1,0:T(8,128)S(1)}, u32[]{:S(2)}, u32[]{:S(2)}) %collective-permute-start.11) | collective-permute-done | bytes 36896 | tf_op jit(solution)/shard_map/ppermute | solution.py:339
  65.1 2.5 %collective-permute-done.12.rest_2_ = f32[72,128]{1,0:T(8,128)S(1)} collective-permute-done((f32[72,128]{1,0:T(8,128)S(1)}, f32[72,128]{1,0:T(8,128)S(1)}, u32[]{:S(2)}, u32[]{:S(2)}) %collective-permute-start.12) | collective-permute-done | bytes 36896 | tf_op jit(solution)/shard_map/ppermute | solution.py:339
  67.6 0.3 collective-permute-start.16
  68.0 1.1 %collective-permute-start.17 = (bf16[128,1792]{1,0:T(8,128)(2,1)S(1)}, bf16[128,1792]{1,0:T(8,128)(2,1)S(1)}, u32[]{:S(2)}, u32[]{:S(2)}) collective-permute-start(bf16[128,1792]{1,0:T(8,128)(2,1)S(1)} %collective-permute-done.15.rest_2_), channel_id=1, source_target_pairs={{0,1},{2,0},{4,2},{6,4},{7,6},{5,7},{3,5},{1,3},{8,9},{10,8},{12,1... | collective-permute-start | bytes 1376264 | tf_op jit(solution)/shard_map/ppermute | solution.py:30
  69.1 0.5 shard_map.134
  69.6 0.9 shard_map.135
  70.5 12.4 %all_to_all.5.mine = bf16[8,64,128]{2,1,0:T(8,128)(2,1)S(1)} all-to-all(bf16[8,64,128]{2,1,0:T(8,128)(2,1)S(1)} %bitcast.10), channel_id=1, replica_groups=mesh['seq'=4,'tensor'=8] {'tensor'}, dimensions={0} | all-to-all | bytes 262144 | tf_op jit(solution)/shard_map/all_to_all | solution.py:349
  83.0 1.4 %collective-permute-start.19 = (bf16[128,1792]{1,0:T(8,128)(2,1)S(1)}, bf16[128,1792]{1,0:T(8,128)(2,1)S(1)}, u32[]{:S(2)}, u32[]{:S(2)}) collective-permute-start(bf16[128,1792]{1,0:T(8,128)(2,1)S(1)} %collective-permute-done.17.rest_4_), channel_id=1, source_target_pairs={{0,1},{2,0},{4,2},{6,4},{7,6},{5,7},{3,5},{1,3},{8,9},{10,8},{12,1... | collective-permute-start | bytes 1376264 | tf_op jit(solution)/shard_map/ppermute | solution.py:30
  84.4 9.7 %collective-permute-done.18.rest_5_ = bf16[128,1792]{1,0:T(8,128)(2,1)S(1)} collective-permute-done((bf16[128,1792]{1,0:T(8,128)(2,1)S(1)}, bf16[128,1792]{1,0:T(8,128)(2,1)S(1)}, u32[]{:S(2)}, u32[]{:S(2)}) %collective-permute-start.18) | collective-permute-done | bytes 458784 | tf_op jit(solution)/shard_map/ppermute | solution.py:30
  94.2 1.5 %collective-permute-start.21 = (bf16[64,1792]{1,0:T(8,128)(2,1)S(1)}, bf16[64,1792]{1,0:T(8,128)(2,1)S(1)}, u32[]{:S(2)}, u32[]{:S(2)}) collective-permute-start(bf16[64,1792]{1,0:T(8,128)(2,1)S(1)} %slice.62), channel_id=1, source_target_pairs={{0,1},{2,0},{4,2},{6,4},{7,6},{5,7},{3,5},{1,3},{8,9},{10,8},{12,1... | collective-permute-start | bytes 688136 | tf_op jit(solution)/shard_map/ppermute | solution.py:30
  95.7 2.3 %collective-permute-start.13 = (bf16[8,64,128]{2,1,0:T(8,128)(2,1)S(1)}, bf16[8,64,128]{2,1,0:T(8,128)(2,1)S(1)}, u32[]{:S(2)}, u32[]{:S(2)}) collective-permute-start(bf16[8,64,128]{2,1,0:T(8,128)(2,1)S(1)} %all_to_all.5.mine), channel_id=1, source_target_pairs={{0,8},{8,0},{16,24},{24,16},{1,9},{9,1},{17,25},{25,17},{2,10},{10... | collective-permute-start | bytes 393224 | tf_op jit(solution)/shard_map/ppermute | solution.py:363
  98.0 1.0 collective-permute-done.13.other
  99.0 3.2 %shard_map.136.total = f32[128,1792]{1,0:T(8,128)S(1)} custom-call(bf16[8,64,128]{2,1,0:T(8,128)(2,1)S(1)} %all_to_all.5.mine, bf16[8,64,128]{2,1,0:T(8,128)(2,1)S(1)} %collective-permute-done.13.other, bf16[128,1792]{1,0:T(8,128)(2,1)S(1)} %multiply_convert_fusion.rest_0_, bf16[128,1792]{1,0:T(8,128)(2,1)S(1)} %collective-permute-done.14.rest_1_, ...), custom_call_target="tpu_custom_call" | custom-call | flops 1000000000 | bytes 2097152 | tf_op jit(solution)/shard_map/pallas_call | solution.py:368
  102.2 0.9 shard_map.137
  103.1 0.4 collective-permute-start.22
  103.6 1.1 %collective-permute-done.22 = bf16[64,1792]{1,0:T(8,128)(2,1)S(1)} collective-permute-done((bf16[64,1792]{1,0:T(8,128)(2,1)S(1)}, bf16[64,1792]{1,0:T(8,128)(2,1)S(1)}, u32[]{:S(2)}, u32[]{:S(2)}) %collective-permute-start.22) | collective-permute-done | bytes 229408 | tf_op jit(solution)/shard_map/ppermute | solution.py:384
  104.7 0.8 pad_maximum_fusion
  (53 shorter events, 0.6 us)
Async XLA Ops:
  0.0 1.5 %copy-start = (bf16[3584,2]{0,1:T(2,128)(2,1)S(1)}, bf16[3584,2]{0,1:T(2,128)(2,1)}, u32[]{:S(2)}) copy-start(bf16[3584,2]{0,1:T(2,128)(2,1)} %param.16) | copy-start | bytes 43012
  0.0 11.6 %collective-permute-start = (bf16[448,512]{1,0:T(8,128)(2,1)}, bf16[448,512]{1,0:T(8,128)(2,1)S(1)}, u32[]{:S(2)}, u32[]{:S(2)}) collective-permute-start(bf16[448,512]{1,0:T(8,128)(2,1)} %bitcast.11), channel_id=1, source_target_pairs={{0,2},{2,4},{4,6},{6,7},{7,5},{5,3},{3,1},{1,0},{8,10},{10,12},{12... | collective-permute-start | bytes 1376264 | tf_op jit(solution)/shard_map/ppermute | solution.py:30
  1.3 11.3 %collective-permute-start.1 = (bf16[448,512]{1,0:T(8,128)(2,1)}, bf16[448,512]{1,0:T(8,128)(2,1)S(1)}, u32[]{:S(2)}, u32[]{:S(2)}) collective-permute-start(bf16[448,512]{1,0:T(8,128)(2,1)} %bitcast.12), channel_id=1, source_target_pairs={{0,1},{2,0},{4,2},{6,4},{7,6},{5,7},{3,5},{1,3},{8,9},{10,8},{12,1... | collective-permute-start | bytes 1376264 | tf_op jit(solution)/shard_map/ppermute | solution.py:30
  2.6 1.5 %copy-start.1 = (bf16[2,3584,128]{2,1,0:T(8,128)(2,1)S(1)}, bf16[2,3584,128]{2,1,0:T(8,128)(2,1)}, u32[]{:S(2)}) copy-start(bf16[2,3584,128]{2,1,0:T(8,128)(2,1)} %refs_2_.9) | copy-start | bytes 5505028
  4.1 1.2 %copy-start.3 = (bf16[3584,128]{1,0:T(8,128)(2,1)S(1)}, bf16[3584,128]{1,0:T(8,128)(2,1)}, u32[]{:S(2)}) copy-start(bf16[3584,128]{1,0:T(8,128)(2,1)} %refs_3_.7) | copy-start | bytes 2752516
  5.3 1.0 copy-start.9
  6.3 7.8 %copy-start.4 = (bf16[3584,128]{1,0:T(8,128)(2,1)S(1)}, bf16[3584,128]{1,0:T(8,128)(2,1)}, u32[]{:S(2)}) copy-start(bf16[3584,128]{1,0:T(8,128)(2,1)} %refs_3_.7) | copy-start | bytes 2752516
  6.9 18.4 %copy-start.13 = (s32[512]{0:T(512)S(1)}, s32[512]{0:T(512)}, u32[]{:S(2)}) copy-start(s32[512]{0:T(512)} %param.24) | copy-start | bytes 6148
  12.6 10.3 %collective-permute-start.2 = (bf16[448,512]{1,0:T(8,128)(2,1)S(1)}, bf16[448,512]{1,0:T(8,128)(2,1)}, u32[]{:S(2)}, u32[]{:S(2)}) collective-permute-start(bf16[448,512]{1,0:T(8,128)(2,1)S(1)} %collective-permute-done.refs_0_), channel_id=1, source_target_pairs={{0,2},{2,4},{4,6},{6,7},{7,5},{5,3},{3,1},{1,0},{8,10},{10,12},{12... | collective-permute-start | bytes 1376264 | tf_op jit(solution)/shard_map/ppermute | solution.py:30
  13.9 10.0 %collective-permute-start.3 = (bf16[448,512]{1,0:T(8,128)(2,1)S(1)}, bf16[448,512]{1,0:T(8,128)(2,1)}, u32[]{:S(2)}, u32[]{:S(2)}) collective-permute-start(bf16[448,512]{1,0:T(8,128)(2,1)S(1)} %collective-permute-done.1.refs_1_), channel_id=1, source_target_pairs={{0,1},{2,0},{4,2},{6,4},{7,6},{5,7},{3,5},{1,3},{8,9},{10,8},{12,1... | collective-permute-start | bytes 1376264 | tf_op jit(solution)/shard_map/ppermute | solution.py:30
  23.9 9.3 %collective-permute-start.4 = (bf16[448,512]{1,0:T(8,128)(2,1)}, bf16[448,512]{1,0:T(8,128)(2,1)S(1)}, u32[]{:S(2)}, u32[]{:S(2)}) collective-permute-start(bf16[448,512]{1,0:T(8,128)(2,1)} %collective-permute-done.2.refs_0_), channel_id=1, source_target_pairs={{0,2},{2,4},{4,6},{6,7},{7,5},{5,3},{3,1},{1,0},{8,10},{10,12},{12... | collective-permute-start | bytes 1376264 | tf_op jit(solution)/shard_map/ppermute | solution.py:30
  25.1 9.0 %collective-permute-start.5 = (bf16[448,512]{1,0:T(8,128)(2,1)}, bf16[448,512]{1,0:T(8,128)(2,1)}, u32[]{:S(2)}, u32[]{:S(2)}) collective-permute-start(bf16[448,512]{1,0:T(8,128)(2,1)} %collective-permute-done.3.refs_1_), channel_id=1, source_target_pairs={{0,1},{2,0},{4,2},{6,4},{7,6},{5,7},{3,5},{1,3},{8,9},{10,8},{12,1... | collective-permute-start | bytes 1376264 | tf_op jit(solution)/shard_map/ppermute | solution.py:30
  25.4 22.7 %collective-permute-start.9 = (s32[8]{0:T(128)S(1)}, s32[8]{0:T(128)S(1)}, u32[]{:S(2)}, u32[]{:S(2)}) collective-permute-start(s32[8]{0:T(128)S(1)} %slice.48), channel_id=1, source_target_pairs={{0,8},{8,16},{16,24},{1,9},{9,17},{17,25},{2,10},{10,18},{18,26},{... | collective-permute-start | bytes 104 | tf_op jit(solution)/shard_map/ppermute | solution.py:317
  26.7 11.3 %copy-start.12 = (bf16[128,3584]{1,0:T(8,128)(2,1)S(1)}, bf16[128,3584]{1,0:T(8,128)(2,1)}, u32[]{:S(2)}) copy-start(bf16[128,3584]{1,0:T(8,128)(2,1)} %param.23) | copy-start | bytes 2752516
  26.7 11.3 %copy-start.14 = (f32[128]{0:T(128)S(1)}, f32[128]{0:T(128)}, u32[]{:S(2)}) copy-start(f32[128]{0:T(128)} %param.22) | copy-start | bytes 1540
  29.8 1.0 copy-start.5
  30.8 7.5 %copy-start.15 = (f32[2]{0:T(128)S(1)}, f32[2]{0:T(128)}, u32[]{:S(2)}) copy-start(f32[2]{0:T(128)} %param.17) | copy-start | bytes 28
  30.8 7.6 %copy-start.16 = (f32[2]{0:T(128)S(1)}, f32[2]{0:T(128)}, u32[]{:S(2)}) copy-start(f32[2]{0:T(128)} %param.18) | copy-start | bytes 28
  30.8 7.8 %copy-start.17 = (f32[2]{0:T(128)S(1)}, f32[2]{0:T(128)}, u32[]{:S(2)}) copy-start(f32[2]{0:T(128)} %param.19) | copy-start | bytes 28
  33.1 4.6 %copy-start.7 = (bf16[448,512]{1,0:T(8,128)(2,1)}, bf16[448,512]{1,0:T(8,128)(2,1)S(1)}, u32[]{:S(2)}) copy-start(bf16[448,512]{1,0:T(8,128)(2,1)S(1)} %collective-permute-done.4.refs_0_) | copy-start | bytes 1376260
  33.1 6.2 %copy-start.6 = (f32[512,512]{1,0:T(8,128)S(1)}, f32[512,512]{1,0:T(8,128)}, u32[]{:S(2)}) copy-start(f32[512,512]{1,0:T(8,128)} %copy-done.5) | copy-start | bytes 3145732
  34.8 8.5 %collective-permute-start.6 = (bf16[224,512]{1,0:T(8,128)(2,1)}, bf16[224,512]{1,0:T(8,128)(2,1)}, u32[]{:S(2)}, u32[]{:S(2)}) collective-permute-start(bf16[224,512]{1,0:T(8,128)(2,1)} %slice.45), channel_id=1, source_target_pairs={{0,2},{2,4},{4,6},{6,7},{7,5},{5,3},{3,1},{1,0},{8,10},{10,12},{12... | collective-permute-start | bytes 688136 | tf_op jit(solution)/shard_map/ppermute | solution.py:30
  37.7 5.7 %collective-permute-start.7 = (bf16[224,512]{1,0:T(8,128)(2,1)}, bf16[224,512]{1,0:T(8,128)(2,1)}, u32[]{:S(2)}, u32[]{:S(2)}) collective-permute-start(bf16[224,512]{1,0:T(8,128)(2,1)} %slice.46), channel_id=1, source_target_pairs={{0,1},{2,0},{4,2},{6,4},{7,6},{5,7},{3,5},{1,3},{8,9},{10,8},{12,1... | collective-permute-start | bytes 688136 | tf_op jit(solution)/shard_map/ppermute | solution.py:30
  39.4 1.0 copy-start.8
  40.4 4.6 %copy-start.2 = (bf16[2,3584,128]{2,1,0:T(8,128)(2,1)S(1)}, bf16[2,3584,128]{2,1,0:T(8,128)(2,1)}, u32[]{:S(2)}) copy-start(bf16[2,3584,128]{2,1,0:T(8,128)(2,1)} %refs_2_.9) | copy-start | bytes 5505028
  43.4 24.2 %collective-permute-start.14 = (bf16[128,1792]{1,0:T(8,128)(2,1)S(1)}, bf16[128,1792]{1,0:T(8,128)(2,1)S(1)}, u32[]{:S(2)}, u32[]{:S(2)}) collective-permute-start(bf16[128,1792]{1,0:T(8,128)(2,1)S(1)} %multiply_convert_fusion.rest_0_), channel_id=1, source_target_pairs={{0,2},{2,4},{4,6},{6,7},{7,5},{5,3},{3,1},{1,0},{8,10},{10,12},{12... | collective-permute-start | bytes 1376264 | tf_op jit(solution)/shard_map/ppermute | solution.py:30
  44.7 23.0 %collective-permute-start.15 = (bf16[128,1792]{1,0:T(8,128)(2,1)S(1)}, bf16[128,1792]{1,0:T(8,128)(2,1)S(1)}, u32[]{:S(2)}, u32[]{:S(2)}) collective-permute-start(bf16[128,1792]{1,0:T(8,128)(2,1)S(1)} %multiply_convert_fusion.rest_0_), channel_id=1, source_target_pairs={{0,1},{2,0},{4,2},{6,4},{7,6},{5,7},{3,5},{1,3},{8,9},{10,8},{12,1... | collective-permute-start | bytes 1376264 | tf_op jit(solution)/shard_map/ppermute | solution.py:30
  44.9 3.4 %copy-start.10 = (f32[4,128]{1,0:T(4,128)S(1)}, f32[4,128]{1,0:T(4,128)}, u32[]{:S(2)}) copy-start(f32[4,128]{1,0:T(4,128)} %taps_x.3) | copy-start | bytes 6148
  44.9 3.4 %copy-start.11 = (f32[4,128]{1,0:T(4,128)S(1)}, f32[4,128]{1,0:T(4,128)}, u32[]{:S(2)}) copy-start(f32[4,128]{1,0:T(4,128)} %taps_bc.3) | copy-start | bytes 6148
  46.8 8.9 %collective-permute-start.8 = (bf16[8,256]{1,0:T(8,128)(2,1)S(1)}, bf16[8,256]{1,0:T(8,128)(2,1)S(1)}, u32[]{:S(2)}, u32[]{:S(2)}) collective-permute-start(bf16[8,256]{1,0:T(8,128)(2,1)S(1)} %slice.64), channel_id=1, source_target_pairs={{0,8},{8,16},{16,24},{1,9},{9,17},{17,25},{2,10},{10,18},{18,26},{... | collective-permute-start | bytes 12296 | tf_op jit(solution)/shard_map/ppermute | solution.py:322
  56.9 5.0 %collective-permute-start.10 = (f32[72,128]{1,0:T(8,128)S(1)}, f32[72,128]{1,0:T(8,128)S(1)}, u32[]{:S(2)}, u32[]{:S(2)}) collective-permute-start(f32[72,128]{1,0:T(8,128)S(1)} %get-tuple-element.52), channel_id=1, source_target_pairs={{0,8},{8,16},{16,24},{1,9},{9,17},{17,25},{2,10},{10,18},{18,26},{... | collective-permute-start | bytes 110600 | tf_op jit(solution)/shard_map/ppermute | solution.py:339
  58.2 7.0 %collective-permute-start.11 = (f32[72,128]{1,0:T(8,128)S(1)}, f32[72,128]{1,0:T(8,128)S(1)}, u32[]{:S(2)}, u32[]{:S(2)}) collective-permute-start(f32[72,128]{1,0:T(8,128)S(1)} %get-tuple-element.52), channel_id=1, source_target_pairs={{0,16},{8,24},{1,17},{9,25},{2,18},{10,26},{3,19},{11,27},{4,20},{... | collective-permute-start | bytes 110600 | tf_op jit(solution)/shard_map/ppermute | solution.py:339
  59.5 8.2 %collective-permute-start.12 = (f32[72,128]{1,0:T(8,128)S(1)}, f32[72,128]{1,0:T(8,128)S(1)}, u32[]{:S(2)}, u32[]{:S(2)}) collective-permute-start(f32[72,128]{1,0:T(8,128)S(1)} %get-tuple-element.52), channel_id=1, source_target_pairs={{0,24},{1,25},{2,26},{3,27},{4,28},{5,29},{6,30},{7,31}} | collective-permute-start | bytes 110600 | tf_op jit(solution)/shard_map/ppermute | solution.py:339
  67.6 15.3 %collective-permute-start.16 = (bf16[128,1792]{1,0:T(8,128)(2,1)S(1)}, bf16[128,1792]{1,0:T(8,128)(2,1)S(1)}, u32[]{:S(2)}, u32[]{:S(2)}) collective-permute-start(bf16[128,1792]{1,0:T(8,128)(2,1)S(1)} %collective-permute-done.14.rest_1_), channel_id=1, source_target_pairs={{0,2},{2,4},{4,6},{6,7},{7,5},{5,3},{3,1},{1,0},{8,10},{10,12},{12... | collective-permute-start | bytes 1376264 | tf_op jit(solution)/shard_map/ppermute | solution.py:30
  68.0 15.0 %collective-permute-start.17 = (bf16[128,1792]{1,0:T(8,128)(2,1)S(1)}, bf16[128,1792]{1,0:T(8,128)(2,1)S(1)}, u32[]{:S(2)}, u32[]{:S(2)}) collective-permute-start(bf16[128,1792]{1,0:T(8,128)(2,1)S(1)} %collective-permute-done.15.rest_2_), channel_id=1, source_target_pairs={{0,1},{2,0},{4,2},{6,4},{7,6},{5,7},{3,5},{1,3},{8,9},{10,8},{12,1... | collective-permute-start | bytes 1376264 | tf_op jit(solution)/shard_map/ppermute | solution.py:30
  82.9 11.2 %collective-permute-start.18 = (bf16[128,1792]{1,0:T(8,128)(2,1)S(1)}, bf16[128,1792]{1,0:T(8,128)(2,1)S(1)}, u32[]{:S(2)}, u32[]{:S(2)}) collective-permute-start(bf16[128,1792]{1,0:T(8,128)(2,1)S(1)} %collective-permute-done.16.rest_3_), channel_id=1, source_target_pairs={{0,2},{2,4},{4,6},{6,7},{7,5},{5,3},{3,1},{1,0},{8,10},{10,12},{12... | collective-permute-start | bytes 1376264 | tf_op jit(solution)/shard_map/ppermute | solution.py:30
  83.0 11.2 %collective-permute-start.19 = (bf16[128,1792]{1,0:T(8,128)(2,1)S(1)}, bf16[128,1792]{1,0:T(8,128)(2,1)S(1)}, u32[]{:S(2)}, u32[]{:S(2)}) collective-permute-start(bf16[128,1792]{1,0:T(8,128)(2,1)S(1)} %collective-permute-done.17.rest_4_), channel_id=1, source_target_pairs={{0,1},{2,0},{4,2},{6,4},{7,6},{5,7},{3,5},{1,3},{8,9},{10,8},{12,1... | collective-permute-start | bytes 1376264 | tf_op jit(solution)/shard_map/ppermute | solution.py:30
  94.1 8.1 %collective-permute-start.20 = (bf16[64,1792]{1,0:T(8,128)(2,1)S(1)}, bf16[64,1792]{1,0:T(8,128)(2,1)S(1)}, u32[]{:S(2)}, u32[]{:S(2)}) collective-permute-start(bf16[64,1792]{1,0:T(8,128)(2,1)S(1)} %slice.61), channel_id=1, source_target_pairs={{0,2},{2,4},{4,6},{6,7},{7,5},{5,3},{3,1},{1,0},{8,10},{10,12},{12... | collective-permute-start | bytes 688136 | tf_op jit(solution)/shard_map/ppermute | solution.py:30
  94.2 8.0 %collective-permute-start.21 = (bf16[64,1792]{1,0:T(8,128)(2,1)S(1)}, bf16[64,1792]{1,0:T(8,128)(2,1)S(1)}, u32[]{:S(2)}, u32[]{:S(2)}) collective-permute-start(bf16[64,1792]{1,0:T(8,128)(2,1)S(1)} %slice.62), channel_id=1, source_target_pairs={{0,1},{2,0},{4,2},{6,4},{7,6},{5,7},{3,5},{1,3},{8,9},{10,8},{12,1... | collective-permute-start | bytes 688136 | tf_op jit(solution)/shard_map/ppermute | solution.py:30
  95.7 3.3 %collective-permute-start.13 = (bf16[8,64,128]{2,1,0:T(8,128)(2,1)S(1)}, bf16[8,64,128]{2,1,0:T(8,128)(2,1)S(1)}, u32[]{:S(2)}, u32[]{:S(2)}) collective-permute-start(bf16[8,64,128]{2,1,0:T(8,128)(2,1)S(1)} %all_to_all.5.mine), channel_id=1, source_target_pairs={{0,8},{8,0},{16,24},{24,16},{1,9},{9,1},{17,25},{25,17},{2,10},{10... | collective-permute-start | bytes 393224 | tf_op jit(solution)/shard_map/ppermute | solution.py:363
  103.1 1.6 %collective-permute-start.22 = (bf16[64,1792]{1,0:T(8,128)(2,1)S(1)}, bf16[64,1792]{1,0:T(8,128)(2,1)S(1)}, u32[]{:S(2)}, u32[]{:S(2)}) collective-permute-start(bf16[64,1792]{1,0:T(8,128)(2,1)S(1)} %get-tuple-element.60), channel_id=1, source_target_pairs={{0,8},{8,0},{16,24},{24,16},{1,9},{9,1},{17,25},{25,17},{2,10},{10... | collective-permute-start | bytes 688136 | tf_op jit(solution)/shard_map/ppermute | solution.py:384

commit v4 on v3

--- a/solution.py
+++ b/solution.py
@@ -34,11 +34,10 @@
     return lax.optimization_barrier((values, earlier))[0]
 
 
-def ring_step(forth, back, step):
-    if step < lax.axis_size("tensor") // 2:
-        return ring_shift(forth, 1), ring_shift(back, -1)
-    half = forth.shape[0] // 32 * 16
-    return ring_shift(forth[:half], 1), ring_shift(back[half:], -1)
+def halves(forth, back, top, bottom):
+    size = top.shape[0]
+    top[...] = forth[:size]
+    bottom[...] = back[size:]
 
 
 def silu(v):
@@ -198,16 +197,18 @@
     )
 
 
-def finish(count, rows, seg_first, out_a, gate_a, bc_a, enter_a, state_a, out_b, gate_b, bc_b, enter_b, *rest):
-    messages, gated = rest[:count], rest[count]
+def finish(rows, seg_first, messages, out_a, gate_a, bc_a, enter_a, state_a, out_b, gate_b, bc_b, enter_b, gated):
     state_w = bc_a.shape[1] // 2
     entering = jnp.zeros((state_w, out_a.shape[1]), F32)
     decay = jnp.zeros((1, out_a.shape[1]), F32)
     first = seg_first[...].astype(F32)
-    for message in messages:
-        passes = jnp.where(message[state_w + 1 : state_w + 2] == first, jnp.exp(decay), 0.0)
-        entering = entering + passes * message[:state_w]
-        decay = decay + message[state_w : state_w + 1]
+    place = lax.axis_index("seq")
+    for device in reversed(range(messages.shape[0] - 1)):
+        earlier = device < place
+        passes = earlier & (messages[device, state_w + 1 : state_w + 2] == first)
+        passes = jnp.where(passes, jnp.exp(decay), 0.0)
+        entering = entering + passes * messages[device, :state_w]
+        decay = decay + jnp.where(earlier, messages[device, state_w : state_w + 1], 0.0)
     second = state_a[state_w : state_w + 1] * entering + state_a[:state_w]
     gated[:rows] = ((out_a[...] + enter_a[...] * dot(bc_a[:, state_w:], entering)) * gate_a[...]).astype(BF16)
     gated[rows:] = ((out_b[...] + enter_b[...] * dot(bc_b[:, state_w:], second)) * gate_b[...]).astype(BF16)
@@ -220,7 +221,7 @@
             pltpu.make_async_copy(pieces[k], held.at[slot, pl.ds(row, pieces[k].shape[0])], sems.at[k])
         )
         copies[-1].start()
-    sums = [0.0] * len(gated)
+    total = 0.0
     waited = set()
     for k, (slot, distance, _) in enumerate(where):
         if slot in waited:
@@ -230,22 +231,19 @@
             if other == slot:
                 copies[j].wait()
         source = source_of(distance)
-        for i, rows in enumerate(gated):
-            sums[i] = sums[i] + jnp.dot(rows[source], held[slot], preferred_element_type=F32)
-    return sums
+        rows = jnp.concatenate([part[source] for part in gated], 0)
+        total = total + jnp.dot(rows, held[slot], preferred_element_type=F32)
+    return total
 
 
 def product_early(where, mine, other, *rest):
     pieces, (out, held, sems) = rest[: len(where)], rest[len(where) :]
-    sums = product((mine, other), where, pieces, held, sems)
-    rows = mine.shape[1]
-    out[:rows] = sums[0]
-    out[rows:] = sums[1]
+    out[...] = product((mine, other), where, pieces, held, sems)
 
 
 def product_last(where, mine, other, total, *rest):
     pieces, (mine_out, other_out, held, sems) = rest[: len(where)], rest[len(where) :]
-    sums = product((mine, other), where, pieces, held, sems)
+    result = product((mine, other), where, pieces, held, sems) + total[...]
     blocks, rows, width = mine.shape
     for i, (gated, out) in enumerate(((mine, mine_out), (other, other_out))):
         squares = jnp.zeros((rows, width), F32)
@@ -253,7 +251,7 @@
             value = gated[block].astype(F32)
             squares = squares + value * value
         scale = lax.rsqrt(jnp.sum(squares, axis=1, keepdims=True) / (blocks * width) + NORM_EPS)
-        out[...] = ((sums[i] + total[i * rows : (i + 1) * rows]) * scale).astype(BF16)
+        out[...] = (result[i * rows : (i + 1) * rows] * scale).astype(BF16)
 
 
 def call(body, outs, scratch=(), vmem=48, flops=10**7, **kw):
@@ -285,33 +283,54 @@
     expand = np.repeat(np.eye(heads, dtype=np.float32), head_w, axis=1)
     w_step = jnp.dot(w_dt, expand.astype(BF16))
     block = tokens.T
+    core = seq_at % 2
+    columns = model // 2
+    own = (lax.dynamic_slice_in_dim(w_out, core * columns, columns, 1).astype(F32) * norm_gain[:, None]).astype(BF16)
     last = n_tensor // 2
+    w_half = width // 2
+    w_forth = w_back = (own[:w_half], own[w_half:])
+    w_steps = []
+
+    cut = feat // 32 * 16
+    far = source_of(last) * feat
+    w_far = jnp.concatenate(
+        [lax.dynamic_slice_in_dim(w, far, feat, 0) for w in (w_zx[0], w_zx[1], w_bc, w_step)], 1
+    )
     forth = back = block
-    arrived, projs = [(0, block, 0)], []
-    for step in range(1, last + 2):
-        if step <= last:
-            if step > 1:
-                forth, back = after((forth, back), projs[step - 2])
-            forth, back = ring_step(forth, back, step)
-        sizes = [(distance, part.shape[0], skip) for distance, part, skip in arrived]
+    arrived, projs = [(0, block), None], []
+    for step in range(1, last + 1):
+        if step > 1:
+            forth, back = after((forth, back), projs[step - 2])
+        if step == last:
+            forth, back = call(halves, [shape(cut, tok_rows, kind=BF16), shape(feat - cut, tok_rows, kind=BF16)])(
+                forth, back
+            )
+        if step == 2:
+            tops = after((w_forth[0], w_back[0]), forth, back)
+        if step == 3:
+            bottoms = after((w_forth[1], w_back[1]), forth, back)
+        forth, back = ring_shift(forth, 1), ring_shift(back, -1)
+        if step == 2:
+            tops = ring_shift(tops[0], 1), ring_shift(tops[1], -1)
+        if step == 3:
+            bottoms = ring_shift(bottoms[0], 1), ring_shift(bottoms[1], -1)
+        blocks = [item for item in arrived if item]
         total = projs[-1:]
         projs.append(
             call(
-                functools.partial(project, sizes, not total),
+                functools.partial(project, [(distance, feat, 0) for distance, _ in blocks], not total),
                 shape(tok_rows, 4 * width),
-                [
-                    pltpu.VMEM((len(sizes), max(size for _, size, _ in sizes), 4 * width), BF16),
-                    pltpu.SemaphoreType.DMA((len(sizes), 4)),
-                ],
-                in_specs=[VMEM] * len(sizes) + [ANY] * 3 + [VMEM] * len(total),
+                [pltpu.VMEM((len(blocks), feat, 4 * width), BF16), pltpu.SemaphoreType.DMA((len(blocks), 4))],
+                in_specs=[VMEM] * len(blocks) + [ANY] * 3 + [VMEM] * len(total),
                 flops=10**9,
-            )(*[part for _, part, _ in arrived], w_zx, w_bc, w_step, *total)
+            )(*[part for _, part in blocks], w_zx, w_bc, w_step, *total)
         )
-        arrived = [(-step, forth, 0), (step, back, 0)]
-        if step == last:
-            arrived = [(last, forth, 0), (last, back, forth.shape[0])]
+        arrived = [(-step, forth), (step, back)]
+    w_far = after(w_far, projs[0])
+    tokens_there = (forth, back, projs[-1], w_far)
     proj = projs[-1]
-    tokens_there = (forth, back, projs[-2])
+    for part, rows_of in ((forth, w_far[:cut]), (back, w_far[cut:])):
+        proj = proj + lax.dot_general(part, rows_of, (((0,), (0,)), ((), ())), preferred_element_type=F32)
 
     ahead = [(i, i + 1) for i in range(n_seq - 1)]
     seg_halo = lax.ppermute(segments[tok_rows - HALO :], "seq", ahead)
@@ -335,44 +354,45 @@
         [plane] * 5 + [shape(msg_rows, width)] * 2,
         [ext, ext],
     )(proj, halo, seg_ext_a, seg_last, state_b, conv_x, conv_bc, bias, rate)
-    messages = [
-        lax.ppermute(message, "seq", [(i, i + far) for i in range(n_seq - far)]) for far in range(1, n_seq)
-    ]
+    messages = lax.all_gather(message, "seq")
     out_a, gate_a = call(functools.partial(first_inner, heads, width, rows), [plane, plane])(
         cx_a, bc_a, cum_a, scaled_a, proj, seg_ext_a, seg_row_a, skip
     )
-    gated = call(
-        functools.partial(finish, len(messages), rows), shape(tok_rows, width, kind=BF16)
-    )(seg_first, out_a, gate_a, bc_a, enter_a, state_a, out_b, gate_b, bc_b, enter_b, *messages)
+    gated = call(functools.partial(finish, rows), shape(tok_rows, width, kind=BF16))(
+        seg_first, messages, out_a, gate_a, bc_a, enter_a, state_a, out_b, gate_b, bc_b, enter_b
+    )
 
     tok_own = tok_rows // n_tensor
     mine = lax.all_to_all(gated.reshape(n_tensor, tok_own, width), "tensor", 0, 0)
 
-    core = seq_at % 2
-    columns = model // 2
-    own = (lax.dynamic_slice_in_dim(w_out, core * columns, columns, 1).astype(F32) * norm_gain[:, None]).astype(BF16)
+    w_forth, w_back = (tops[0], bottoms[0]), (tops[1], bottoms[1])
+    w_steps = [(w_forth, w_back)]
     orders = [tokens_there, messages, mine]
-    forth = back = own
-    w_steps = []
-    for step in range(1, last + 1):
-        if step <= len(orders):
-            forth, back = after((forth, back), orders[step - 1])
-        forth, back = ring_step(forth, back, step)
-        w_steps.append((forth, back))
+    for step in range(2, last + 1):
+        if step - 2 < len(orders):
+            w_forth, w_back = after((w_forth, w_back), orders[step - 2])
+        if step < last:
+            w_forth = tuple(ring_shift(part, 1) for part in w_forth)
+            w_back = tuple(ring_shift(part, -1) for part in w_back)
+            w_steps.append((w_forth, w_back))
+        else:
+            w_far_parts = ring_shift(w_forth[0], 1), ring_shift(w_back[1], -1)
     swap = [(i, i ^ 1) for i in range(n_seq)]
     other = lax.ppermute(mine, "seq", swap)
     pieces, where = [own], [(0, 0, 0)]
-    for i, pair in enumerate(w_steps[:-1]):
-        pieces += pair
-        where += [(2 * i + 1, -i - 1, 0), (2 * i + 2, i + 1, 0)]
+    for i, pair in enumerate(w_steps):
+        for side, parts in enumerate(pair):
+            distance = i + 1 if side else -i - 1
+            pieces += parts
+            where += [(2 * i + 1 + side, distance, 0), (2 * i + 1 + side, distance, w_half)]
     total = call(
         functools.partial(product_early, where),
         shape(2 * tok_own, columns),
-        [pltpu.VMEM((len(where), width, columns), BF16), pltpu.SemaphoreType.DMA((len(where),))],
+        [pltpu.VMEM((n_tensor - 1, width, columns), BF16), pltpu.SemaphoreType.DMA((len(where),))],
         in_specs=[VMEM, VMEM] + [ANY] * len(pieces),
         flops=10**9,
     )(mine, other, *pieces)
-    where = [(0, last, 0), (0, last, w_steps[-1][0].shape[0])]
+    where = [(0, last, 0), (0, last, w_half)]
     half = shape(tok_own, columns, kind=BF16)
     out_own, out_other = call(
         functools.partial(product_last, where),
@@ -380,7 +400,7 @@
         [pltpu.VMEM((1, width, columns), BF16), pltpu.SemaphoreType.DMA((2,))],
         in_specs=[VMEM, VMEM, VMEM] + [ANY] * 2,
         flops=10**8,
-    )(mine, other, total, *w_steps[-1])
+    )(mine, other, total, *w_far_parts)
     arrived = lax.ppermute(out_other, "seq", swap)
     is_first = core == 0
     return jnp.concatenate([jnp.where(is_first, out_own, arrived), jnp.where(is_first, arrived, out_own)], 1)

time: 106 us -> 112 us (1.057)
  the two profiles are of different devices: /device:TPU:5 before, /device:TPU:0 now
where the time goes in v4:
time: 112 us; the launch traced here: 111 us
  starting transfers between devices  33.8 us (30%)
  waiting for transfers between devices  23.2 us (21%)
  local copies, waits for them, and re-layouts  21.4 us (19%)
  Pallas kernels  19 us (17%)
  blocking collectives  6.46 us (6%)
  matrix products  4.71 us (4%)
  other arithmetic  1.92 us (2%)
    ppermute x22, starting transfers between devices, ring_shift(): lax.ppermute(block, 'tensor', [(order[i], order[(i + step) % n]) for i in...  23.6 us
    ppermute x22, waiting for transfers between devices, ring_shift(): lax.ppermute(block, 'tensor', [(order[i], order[(i + step) % n]) for i in...  16.5 us
    unnamed x47, local copies, waits for them, and re-layouts  9.59 us
    pallas_call x4, Pallas kernels, local(): call(functools.partial(project, [(distance, feat, 0) for distance, _ in b...  8.64 us
    dynamic_slice x5, local copies, waits for them, and re-layouts, local(): lax.dynamic_slice_in_dim(w, far, feat, 0)  6.62 us
    all_gather x1, blocking collectives, local(): messages = lax.all_gather(message, 'seq')  6.46 us
    all_to_all x1, starting transfers between devices, local(): lax.all_to_all(gated.reshape(n_tensor, tok_own, width), 'tensor', 0, 0)  5.65 us
    pallas_call x1, Pallas kernels, local(): call(functools.partial(product_early, where), shape(2 * tok_own, columns)...  4.41 us
  transfers between devices with their start and end apart: 27, of which 10 were waited for; matrix products, arithmetic and copies ran while one was open for 17% of the time, Pallas kernels for 16%

profile of v4, /device:TPU:0, one launch (start us, length us, event | category | flops | bytes accessed | tf_op | source)
XLA Modules:
  0.0 110.8 jit_solution(17065801281741980939)
XLA Ops:
  0.0 2.9 %collective-permute-start.1 = (bf16[448,512]{1,0:T(8,128)(2,1)}, bf16[448,512]{1,0:T(8,128)(2,1)}, u32[]{:S(2)}, u32[]{:S(2)}) collective-permute-start(bf16[448,512]{1,0:T(8,128)(2,1)} %bitcast.21), channel_id=1, source_target_pairs={{0,1},{2,0},{4,2},{6,4},{7,6},{5,7},{3,5},{1,3},{8,9},{10,8},{12,1... | collective-permute-start | bytes 1376264 | tf_op jit(solution)/shard_map/ppermute | solution.py:30
  3.1 2.0 %fusion.8 = bf16[128,3584]{1,0:T(8,128)(2,1)} fusion(bf16[2,128]{1,0:T(2,128)(2,1)} %constant.70.clone, bf16[3584,2]{0,1:T(2,128)(2,1)S(1)} %copy-done), kind=kOutput, calls=%fused_computation.20 | convolution fusion | flops 1835008 | bytes 932352 | tf_op jit(solution)/shard_map/dot_general | solution.py:284
  5.1 1.6 %copy.18 = bf16[128,3584]{0,1:T(8,128)(2,1)S(1)} copy(bf16[128,3584]{1,0:T(8,128)(2,1)} %fusion.8) | data formatting | bytes 1835008 | tf_op jit(solution)/shard_map/dot_general | solution.py:284
  6.8 1.4 %fusion.4 = (bf16[1,3584,128]{2,1,0:T(8,128)(2,1)}, bf16[1,3584,128]{2,1,0:T(8,128)(2,1)}) fusion(bf16[2,3584,128]{2,1,0:T(8,128)(2,1)S(1)} %copy-done.1), kind=kLoop, calls=%fused_computation.16 | loop fusion | bytes 3670016 | tf_op jit(solution)/shard_map/slice | solution.py:297
  8.2 1.2 %copy-done.2 = bf16[3584,128]{1,0:T(8,128)(2,1)S(1)} copy-done((bf16[3584,128]{1,0:T(8,128)(2,1)S(1)}, bf16[3584,128]{1,0:T(8,128)(2,1)}, u32[]{:S(2)}) %copy-start.2) | copy-done | bytes 917528
  9.3 0.6 shard_map.127.refs_5_
  9.9 0.6 copy-done.17
  10.7 3.2 %collective-permute-done.1.refs_1_ = bf16[448,512]{1,0:T(8,128)(2,1)} collective-permute-done((bf16[448,512]{1,0:T(8,128)(2,1)}, bf16[448,512]{1,0:T(8,128)(2,1)}, u32[]{:S(2)}, u32[]{:S(2)}) %collective-permute-start.1) | collective-permute-done | bytes 458784 | tf_op jit(solution)/shard_map/ppermute | solution.py:30
  13.9 1.4 %collective-permute-done.refs_0_ = bf16[448,512]{1,0:T(8,128)(2,1)} collective-permute-done((bf16[448,512]{1,0:T(8,128)(2,1)}, bf16[448,512]{1,0:T(8,128)(2,1)}, u32[]{:S(2)}, u32[]{:S(2)}) %collective-permute-start) | collective-permute-done | bytes 458784 | tf_op jit(solution)/shard_map/ppermute | solution.py:30
  15.7 1.6 %collective-permute-start.3 = (bf16[448,512]{1,0:T(8,128)(2,1)}, bf16[448,512]{1,0:T(8,128)(2,1)}, u32[]{:S(2)}, u32[]{:S(2)}) collective-permute-start(bf16[448,512]{1,0:T(8,128)(2,1)} %collective-permute-done.1.refs_1_), channel_id=1, source_target_pairs={{0,1},{2,0},{4,2},{6,4},{7,6},{5,7},{3,5},{1,3},{8,9},{10,8},{12,1... | collective-permute-start | bytes 1376264 | tf_op jit(solution)/shard_map/ppermute | solution.py:30
  17.3 0.8 fusion.5
  18.1 3.1 %shard_map.128.refs_5_ = f32[512,512]{1,0:T(8,128)S(1)} custom-call(bf16[448,512]{1,0:T(8,128)(2,1)} %collective-permute-done.refs_0_, bf16[448,512]{1,0:T(8,128)(2,1)} %collective-permute-done.1.refs_1_, bf16[2,3584,128]{2,1,0:T(8,128)(2,1)} %refs_2_.7, bf16[3584,128]{1,0:T(8,128)(2,1)S(1)} %copy-done.2, bf16[3584,128]{1,0:T(8,128)(2,1)S(1)} %bitcast.17, ...), custom_call_target="tpu_custom_call" | custom-call | flops 1000000000 | bytes 2097152 | tf_op jit(solution)/shard_map/pallas_call | solution.py:320
  21.2 1.0 copy-done.4
  22.2 4.4 %collective-permute-done.2.refs_0_ = bf16[448,512]{1,0:T(8,128)(2,1)} collective-permute-done((bf16[448,512]{1,0:T(8,128)(2,1)}, bf16[448,512]{1,0:T(8,128)(2,1)}, u32[]{:S(2)}, u32[]{:S(2)}) %collective-permute-start.2) | collective-permute-done | bytes 458784 | tf_op jit(solution)/shard_map/ppermute | solution.py:30
  27.1 1.5 %collective-permute-start.4 = (bf16[448,512]{1,0:T(8,128)(2,1)}, bf16[448,512]{1,0:T(8,128)(2,1)S(1)}, u32[]{:S(2)}, u32[]{:S(2)}) collective-permute-start(bf16[448,512]{1,0:T(8,128)(2,1)} %collective-permute-done.2.refs_0_), channel_id=1, source_target_pairs={{0,2},{2,4},{4,6},{6,7},{7,5},{5,3},{3,1},{1,0},{8,10},{10,12},{12... | collective-permute-start | bytes 1376264 | tf_op jit(solution)/shard_map/ppermute | solution.py:30
  28.6 0.5 collective-permute-start.5
  29.1 1.7 %constant_dynamic-slice_fusion.1 = (bf16[1,448,128]{2,1,0:T(8,128)(2,1)}, bf16[1,448,128]{2,1,0:T(8,128)(2,1)}) fusion(bf16[1,3584,128]{2,1,0:T(8,128)(2,1)} %get-tuple-element.84, s32[]{:T(128)S(6)} %select_n.57, bf16[1,3584,128]{2,1,0:T(8,128)(2,1)} %get-tuple-element.83), kind=kLoop, calls=%fused_computation.14 | loop fusion | bytes 458756 | tf_op jit(solution)/shard_map/dynamic_slice | solution.py:297
  30.8 1.5 %collective-permute-start.11 = (bf16[64,1792]{1,0:T(8,128)(2,1)}, bf16[64,1792]{1,0:T(8,128)(2,1)S(1)}, u32[]{:S(2)}, u32[]{:S(2)}) collective-permute-start(bf16[64,1792]{1,0:T(8,128)(2,1)} %get-tuple-element.69), channel_id=1, source_target_pairs={{0,2},{2,4},{4,6},{6,7},{7,5},{5,3},{3,1},{1,0},{8,10},{10,12},{12... | collective-permute-start | bytes 688136 | tf_op jit(solution)/shard_map/ppermute | solution.py:30
  32.3 0.7 constant_dynamic-slice_fusion
  33.0 1.7 %copy.25 = bf16[448,128]{0,1:T(8,128)(2,1)} copy(bf16[448,128]{1,0:T(8,128)(2,1)} %constant_dynamic-slice_fusion) | data formatting | bytes 229376
  34.6 1.6 %copy.20 = bf16[1,448,128]{1,2,0:T(8,128)(2,1)} copy(bf16[1,448,128]{2,1,0:T(8,128)(2,1)} %get-tuple-element.93) | data formatting | bytes 229376 | tf_op jit(solution)/shard_map/dynamic_slice | solution.py:297
  36.3 1.7 %copy.19 = bf16[1,448,128]{1,2,0:T(8,128)(2,1)} copy(bf16[1,448,128]{2,1,0:T(8,128)(2,1)} %get-tuple-element.94) | data formatting | bytes 229376 | tf_op jit(solution)/shard_map/dynamic_slice | solution.py:297
  37.9 1.0 dynamic-slice_bitcast_fusion
  38.9 0.6 collective-permute-start.13
  39.5 1.5 %collective-permute-start.12 = (bf16[64,1792]{1,0:T(8,128)(2,1)}, bf16[64,1792]{1,0:T(8,128)(2,1)}, u32[]{:S(2)}, u32[]{:S(2)}) collective-permute-start(bf16[64,1792]{1,0:T(8,128)(2,1)} %get-tuple-element.70), channel_id=1, source_target_pairs={{0,2},{2,4},{4,6},{6,7},{7,5},{5,3},{3,1},{1,0},{8,10},{10,12},{12... | collective-permute-start | bytes 688136 | tf_op jit(solution)/shard_map/ppermute | solution.py:30
  41.0 1.2 %copy-done.5 = f32[512,512]{1,0:T(8,128)S(1)} copy-done((f32[512,512]{1,0:T(8,128)S(1)}, f32[512,512]{1,0:T(8,128)}, u32[]{:S(2)}) %copy-start.5) | copy-done | bytes 1048600
  42.2 3.1 %shard_map.129.refs_5_ = f32[512,512]{1,0:T(8,128)S(1)} custom-call(bf16[448,512]{1,0:T(8,128)(2,1)} %collective-permute-done.2.refs_0_, bf16[448,512]{1,0:T(8,128)(2,1)} %collective-permute-done.3.refs_1_, bf16[2,3584,128]{2,1,0:T(8,128)(2,1)} %refs_2_.7, bf16[3584,128]{1,0:T(8,128)(2,1)S(1)} %copy-done.3, bf16[3584,128]{1,0:T(8,128)(2,1)S(1)} %bitcast.18, ...), custom_call_target="tpu_custom_call" | custom-call | flops 1000000000 | bytes 2097152 | tf_op jit(solution)/shard_map/pallas_call | solution.py:320
  45.3 1.0 copy-done.6
  46.4 0.6 collective-permute-start.14
  46.9 0.8 shard_map.131
  47.7 1.5 %collective-permute-start.6 = (bf16[224,512]{1,0:T(8,128)(2,1)}, bf16[224,512]{1,0:T(8,128)(2,1)}, u32[]{:S(2)}, u32[]{:S(2)}) collective-permute-start(bf16[224,512]{1,0:T(8,128)(2,1)} %get-tuple-element.50), channel_id=1, source_target_pairs={{0,2},{2,4},{4,6},{6,7},{7,5},{5,3},{3,1},{1,0},{8,10},{10,12},{12... | collective-permute-start | bytes 688136 | tf_op jit(solution)/shard_map/ppermute | solution.py:30
  49.2 0.5 collective-permute-start.7
  49.8 0.9 pad_maximum_fusion
  51.3 0.6 fusion.7
  51.9 1.2 %copy-done.7 = f32[512,512]{1,0:T(8,128)S(1)} copy-done((f32[512,512]{1,0:T(8,128)S(1)}, f32[512,512]{1,0:T(8,128)}, u32[]{:S(2)}) %copy-start.7) | copy-done | bytes 1048600
  53.1 1.9 %shard_map.130 = f32[512,512]{1,0:T(8,128)S(1)} custom-call(bf16[448,512]{1,0:T(8,128)(2,1)S(1)} %collective-permute-done.4.refs_0_.forth, bf16[448,512]{1,0:T(8,128)(2,1)S(1)} %collective-permute-done.5.refs_1_.back, bf16[2,3584,128]{2,1,0:T(8,128)(2,1)} %refs_2_.7, bf16[3584,128]{1,0:T(8,128)(2,1)S(1)} %copy-done.3, bf16[3584,128]{1,0:T(8,128)(2,1)S(1)} %bitcast.19, ...), custom_call_target="tpu_custom_call" | custom-call | flops 1000000000 | bytes 2097152 | tf_op jit(solution)/shard_map/pallas_call | solution.py:320
  55.1 1.3 %collective-permute-start.9 = (s32[8]{0:T(128)S(1)}, s32[8]{0:T(128)S(1)}, u32[]{:S(2)}, u32[]{:S(2)}) collective-permute-start(s32[8]{0:T(128)S(1)} %slice.56), channel_id=1, source_target_pairs={{0,8},{8,16},{16,24},{1,9},{9,17},{17,25},{2,10},{10,18},{18,26},{... | collective-permute-start | bytes 104 | tf_op jit(solution)/shard_map/ppermute | solution.py:336
  56.4 1.6 %collective-permute-start.15 = (bf16[64,1792]{1,0:T(8,128)(2,1)S(1)}, bf16[64,1792]{1,0:T(8,128)(2,1)S(1)}, u32[]{:S(2)}, u32[]{:S(2)}) collective-permute-start(bf16[64,1792]{1,0:T(8,128)(2,1)S(1)} %collective-permute-done.11.rest_1_), channel_id=1, source_target_pairs={{0,2},{2,4},{4,6},{6,7},{7,5},{5,3},{3,1},{1,0},{8,10},{10,12},{12... | collective-permute-start | bytes 688136 | tf_op jit(solution)/shard_map/ppermute | solution.py:30
  58.0 1.6 %collective-permute-start.16 = (bf16[64,1792]{1,0:T(8,128)(2,1)}, bf16[64,1792]{1,0:T(8,128)(2,1)S(1)}, u32[]{:S(2)}, u32[]{:S(2)}) collective-permute-start(bf16[64,1792]{1,0:T(8,128)(2,1)} %collective-permute-done.12.rest_2_), channel_id=1, source_target_pairs={{0,2},{2,4},{4,6},{6,7},{7,5},{5,3},{3,1},{1,0},{8,10},{10,12},{12... | collective-permute-start | bytes 688136 | tf_op jit(solution)/shard_map/ppermute | solution.py:30
  60.0 0.5 collective-permute-start.18
  60.5 1.4 %fusion.1 = f32[512,512]{1,0:T(8,128)S(1)} fusion(bf16[224,512]{1,0:T(8,128)(2,1)} %collective-permute-done.7, bf16[448,512]{0,1:T(8,128)(2,1)S(1)} %copy-done.13), kind=kOutput, calls=%fused_computation.5 | convolution fusion | flops 117440512 | bytes 1540096 | tf_op jit(solution)/shard_map/dot_general | solution.py:333
  61.9 1.3 %fusion.proj = f32[512,512]{1,0:T(8,128)S(1)} fusion(f32[512,512]{1,0:T(8,128)S(1)} %fusion.1, f32[512,512]{1,0:T(8,128)S(1)} %shard_map.130, bf16[224,512]{1,0:T(8,128)(2,1)} %collective-permute-done.6, bf16[448,512]{0,1:T(8,128)(2,1)S(1)} %copy-done.13), kind=kOutput, calls=%fused_computation.1 | convolution fusion | flops 117964800 | bytes 3637248 | tf_op jit(solution)/shard_map/dot_general | solution.py:333
  63.2 3.0 %collective-permute-start.8 = (bf16[8,256]{1,0:T(8,128)(2,1)S(1)}, bf16[8,256]{1,0:T(8,128)(2,1)S(1)}, u32[]{:S(2)}, u32[]{:S(2)}) collective-permute-start(bf16[8,256]{1,0:T(8,128)(2,1)S(1)} %slice.76), channel_id=1, source_target_pairs={{0,8},{8,16},{16,24},{1,9},{9,17},{17,25},{2,10},{10,18},{18,26},{... | collective-permute-start | bytes 12296 | tf_op jit(solution)/shard_map/ppermute | solution.py:341
  66.4 1.0 shard_map.132
  67.4 1.2 %shard_map.133 = (f32[256,128]{1,0:T(8,128)S(1)}, f32[256,128]{1,0:T(8,128)S(1)}, f32[256,128]{1,0:T(8,128)S(1)}, f32[256,128]{1,0:T(8,128)S(1)}, f32[256,128]{1...) custom-call(f32[512,512]{1,0:T(8,128)S(1)} %fusion.proj, bf16[8,256]{1,0:T(8,128)(2,1)S(1)} %collective-permute-done.8.halo, ...), custom_call_target="tpu_custom_call" | custom-call | flops 10000000 | bytes 2097152 | tf_op jit(solution)/shard_map/pallas_call | solution.py:352
  69.1 6.5 %all-gather = f32[288,128]{1,0:T(8,128)S(1)} all-gather(f32[72,128]{1,0:T(8,128)S(1)} %get-tuple-element.54), channel_id=2, replica_groups=mesh['seq'=4,'tensor'=8] {'seq'}, dimensions={0}, use_global_device_ids=true | all-gather | bytes 184320 | tf_op jit(solution)/shard_map/all_gather | solution.py:357
  75.5 1.6 %shard_map.135 = bf16[512,128]{1,0:T(8,128)(2,1)} custom-call(s32[1,1]{1,0:T(1,128)} %bitcast.seg_first, f32[4,72,128]{2,1,0:T(8,128)S(1)} %bitcast.20, f32[256,128]{1,0:T(8,128)S(1)} %get-tuple-element.59.out_a, f32[256,128]{1,0:T(8,128)S(1)} %get-tuple-element.60.gate_a, f32[256,128]{1,0:T(8,128)S(1)} %get-tuple-element.56.conv_bc.bc_a, ...), custom_call_target="tpu_custom_call" | custom-call | flops 10000000 | bytes 2097152 | tf_op jit(solution)/shard_map/pallas_call | solution.py:361
  77.1 5.7 %all-to-all-start = ((bf16[8,64,128]{2,1,0:T(8,128)(2,1)}), bf16[8,64,128]{2,1,0:T(8,128)(2,1)S(1)}, u32[]{:S(2)}, u32[]{:S(2)}) async-start(bf16[8,64,128]{2,1,0:T(8,128)(2,1)} %bitcast.10), calls=%async_computation | async-start | bytes 262144 | tf_op jit(solution)/shard_map/all_to_all | solution.py:366
  82.8 2.1 %collective-permute-start.19 = (bf16[64,1792]{1,0:T(8,128)(2,1)S(1)}, bf16[64,1792]{1,0:T(8,128)(2,1)S(1)}, u32[]{:S(2)}, u32[]{:S(2)}) collective-permute-start(bf16[64,1792]{1,0:T(8,128)(2,1)S(1)} %collective-permute-done.15.rest_5_), channel_id=1, source_target_pairs={{0,2},{2,4},{4,6},{6,7},{7,5},{5,3},{3,1},{1,0},{8,10},{10,12},{12... | collective-permute-start | bytes 688136 | tf_op jit(solution)/shard_map/ppermute | solution.py:30
  84.9 1.5 %collective-permute-start.20 = (bf16[64,1792]{1,0:T(8,128)(2,1)S(1)}, bf16[64,1792]{1,0:T(8,128)(2,1)S(1)}, u32[]{:S(2)}, u32[]{:S(2)}) collective-permute-start(bf16[64,1792]{1,0:T(8,128)(2,1)S(1)} %collective-permute-done.16.rest_6_), channel_id=1, source_target_pairs={{0,2},{2,4},{4,6},{6,7},{7,5},{5,3},{3,1},{1,0},{8,10},{10,12},{12... | collective-permute-start | bytes 688136 | tf_op jit(solution)/shard_map/ppermute | solution.py:30
  86.3 0.6 collective-permute-start.21
  87.0 4.1 %all-to-all-done.mine = bf16[8,64,128]{2,1,0:T(8,128)(2,1)S(1)} async-done(((bf16[8,64,128]{2,1,0:T(8,128)(2,1)}), bf16[8,64,128]{2,1,0:T(8,128)(2,1)S(1)}, u32[]{:S(2)}, u32[]{:S(2)}) %all-to-all-start) | async-done | bytes 131104 | tf_op jit(solution)/shard_map/all_to_all | solution.py:366
  91.0 1.8 %collective-permute-done.19.rest_9_ = bf16[64,1792]{1,0:T(8,128)(2,1)S(1)} collective-permute-done((bf16[64,1792]{1,0:T(8,128)(2,1)S(1)}, bf16[64,1792]{1,0:T(8,128)(2,1)S(1)}, u32[]{:S(2)}, u32[]{:S(2)}) %collective-permute-start.19) | collective-permute-done | bytes 229408 | tf_op jit(solution)/shard_map/ppermute | solution.py:30
  92.8 4.0 %collective-permute-done.20.rest_10_ = bf16[64,1792]{1,0:T(8,128)(2,1)S(1)} collective-permute-done((bf16[64,1792]{1,0:T(8,128)(2,1)S(1)}, bf16[64,1792]{1,0:T(8,128)(2,1)S(1)}, u32[]{:S(2)}, u32[]{:S(2)}) %collective-permute-start.20) | collective-permute-done | bytes 229408 | tf_op jit(solution)/shard_map/ppermute | solution.py:30
  96.9 0.7 copy-done.9
  97.6 1.1 %collective-permute-done.22.rest_12_ = bf16[64,1792]{1,0:T(8,128)(2,1)S(1)} collective-permute-done((bf16[64,1792]{1,0:T(8,128)(2,1)S(1)}, bf16[64,1792]{1,0:T(8,128)(2,1)S(1)}, u32[]{:S(2)}, u32[]{:S(2)}) %collective-permute-start.22) | collective-permute-done | bytes 229408 | tf_op jit(solution)/shard_map/ppermute | solution.py:30
  98.7 1.2 %collective-permute-start.23 = (bf16[64,1792]{1,0:T(8,128)(2,1)S(1)}, bf16[64,1792]{1,0:T(8,128)(2,1)S(1)}, u32[]{:S(2)}, u32[]{:S(2)}) collective-permute-start(bf16[64,1792]{1,0:T(8,128)(2,1)S(1)} %collective-permute-done.19.rest_9_), channel_id=1, source_target_pairs={{0,2},{2,4},{4,6},{6,7},{7,5},{5,3},{3,1},{1,0},{8,10},{10,12},{12... | collective-permute-start | bytes 688136 | tf_op jit(solution)/shard_map/ppermute | solution.py:30
  99.9 0.8 collective-permute-start.24
  100.7 1.3 %collective-permute-done.10.other = bf16[8,64,128]{2,1,0:T(8,128)(2,1)S(1)} collective-permute-done((bf16[8,64,128]{2,1,0:T(8,128)(2,1)S(1)}, bf16[8,64,128]{2,1,0:T(8,128)(2,1)S(1)}, u32[]{:S(2)}, u32[]{:S(2)}) %collective-permute-start.10) | collective-permute-done | bytes 131104 | tf_op jit(solution)/shard_map/ppermute | solution.py:381
  102.1 0.9 copy-done.10
  103.0 4.4 %shard_map.136.total = f32[128,1792]{1,0:T(8,128)S(1)} custom-call(bf16[8,64,128]{2,1,0:T(8,128)(2,1)S(1)} %all-to-all-done.mine, bf16[8,64,128]{2,1,0:T(8,128)(2,1)S(1)} %collective-permute-done.10.other, bf16[128,1792]{1,0:T(8,128)(2,1)S(1)} %multiply_convert_fusion.rest_0_, bf16[64,1792]{1,0:T(8,128)(2,1)S(1)} %collective-permute-done.11.rest_1_, ...), custom_call_target="tpu_custom_call" | custom-call | flops 1000000000 | bytes 2097152 | tf_op jit(solution)/shard_map/pallas_call | solution.py:388
  107.4 0.9 shard_map.137
  108.6 1.3 %collective-permute-done.25 = bf16[64,1792]{1,0:T(8,128)(2,1)S(1)} collective-permute-done((bf16[64,1792]{1,0:T(8,128)(2,1)S(1)}, bf16[64,1792]{1,0:T(8,128)(2,1)S(1)}, u32[]{:S(2)}, u32[]{:S(2)}) %collective-permute-start.25) | collective-permute-done | bytes 229408 | tf_op jit(solution)/shard_map/ppermute | solution.py:404
  110.0 0.8 pad_maximum_fusion.1
  (79 shorter events, 3.4 us)
Async XLA Ops:
  0.0 3.1 %copy-start = (bf16[3584,2]{0,1:T(2,128)(2,1)S(1)}, bf16[3584,2]{0,1:T(2,128)(2,1)}, u32[]{:S(2)}) copy-start(bf16[3584,2]{0,1:T(2,128)(2,1)} %param.16) | copy-start | bytes 43012
  0.0 6.8 %copy-start.1 = (bf16[2,3584,128]{2,1,0:T(8,128)(2,1)S(1)}, bf16[2,3584,128]{2,1,0:T(8,128)(2,1)}, u32[]{:S(2)}) copy-start(bf16[2,3584,128]{2,1,0:T(8,128)(2,1)} %refs_2_.7) | copy-start | bytes 5505028
  0.0 13.9 %collective-permute-start.1 = (bf16[448,512]{1,0:T(8,128)(2,1)}, bf16[448,512]{1,0:T(8,128)(2,1)}, u32[]{:S(2)}, u32[]{:S(2)}) collective-permute-start(bf16[448,512]{1,0:T(8,128)(2,1)} %bitcast.21), channel_id=1, source_target_pairs={{0,1},{2,0},{4,2},{6,4},{7,6},{5,7},{3,5},{1,3},{8,9},{10,8},{12,1... | collective-permute-start | bytes 1376264 | tf_op jit(solution)/shard_map/ppermute | solution.py:30
  2.9 12.3 %collective-permute-start = (bf16[448,512]{1,0:T(8,128)(2,1)}, bf16[448,512]{1,0:T(8,128)(2,1)}, u32[]{:S(2)}, u32[]{:S(2)}) collective-permute-start(bf16[448,512]{1,0:T(8,128)(2,1)} %bitcast.22), channel_id=1, source_target_pairs={{0,2},{2,4},{4,6},{6,7},{7,5},{5,3},{3,1},{1,0},{8,10},{10,12},{12... | collective-permute-start | bytes 1376264 | tf_op jit(solution)/shard_map/ppermute | solution.py:30
  6.8 1.4 %copy-start.8 = (bf16[512,448]{0,1:T(8,128)(2,1)S(1)}, bf16[512,448]{0,1:T(8,128)(2,1)}, u32[]{:S(2)}) copy-start(bf16[512,448]{0,1:T(8,128)(2,1)} %param.13) | copy-start | bytes 1376260
  8.2 1.2 %copy-start.2 = (bf16[3584,128]{1,0:T(8,128)(2,1)S(1)}, bf16[3584,128]{1,0:T(8,128)(2,1)}, u32[]{:S(2)}) copy-start(bf16[3584,128]{1,0:T(8,128)(2,1)} %refs_3_.5) | copy-start | bytes 2752516
  9.3 1.2 %copy-start.17 = (bf16[128,3584]{1,0:T(8,128)(2,1)S(1)}, bf16[128,3584]{1,0:T(8,128)(2,1)}, u32[]{:S(2)}) copy-start(bf16[128,3584]{1,0:T(8,128)(2,1)} %param.23) | copy-start | bytes 2752516
  9.3 1.2 %copy-start.19 = (f32[128]{0:T(128)S(1)}, f32[128]{0:T(128)}, u32[]{:S(2)}) copy-start(f32[128]{0:T(128)} %param.22) | copy-start | bytes 1540
  15.2 11.4 %collective-permute-start.2 = (bf16[448,512]{1,0:T(8,128)(2,1)}, bf16[448,512]{1,0:T(8,128)(2,1)}, u32[]{:S(2)}, u32[]{:S(2)}) collective-permute-start(bf16[448,512]{1,0:T(8,128)(2,1)} %collective-permute-done.refs_0_), channel_id=1, source_target_pairs={{0,2},{2,4},{4,6},{6,7},{7,5},{5,3},{3,1},{1,0},{8,10},{10,12},{12... | collective-permute-start | bytes 1376264 | tf_op jit(solution)/shard_map/ppermute | solution.py:30
  15.7 11.4 %collective-permute-start.3 = (bf16[448,512]{1,0:T(8,128)(2,1)}, bf16[448,512]{1,0:T(8,128)(2,1)}, u32[]{:S(2)}, u32[]{:S(2)}) collective-permute-start(bf16[448,512]{1,0:T(8,128)(2,1)} %collective-permute-done.1.refs_1_), channel_id=1, source_target_pairs={{0,1},{2,0},{4,2},{6,4},{7,6},{5,7},{3,5},{1,3},{8,9},{10,8},{12,1... | collective-permute-start | bytes 1376264 | tf_op jit(solution)/shard_map/ppermute | solution.py:30
  18.1 11.0 %copy-start.18 = (s32[512]{0:T(512)S(1)}, s32[512]{0:T(512)}, u32[]{:S(2)}) copy-start(s32[512]{0:T(512)} %param.24) | copy-start | bytes 6148
  18.1 14.2 %copy-start.3 = (bf16[3584,128]{1,0:T(8,128)(2,1)S(1)}, bf16[3584,128]{1,0:T(8,128)(2,1)}, u32[]{:S(2)}) copy-start(bf16[3584,128]{1,0:T(8,128)(2,1)} %refs_3_.5) | copy-start | bytes 2752516
  21.2 1.0 copy-start.4
  27.1 19.3 %collective-permute-start.4 = (bf16[448,512]{1,0:T(8,128)(2,1)}, bf16[448,512]{1,0:T(8,128)(2,1)S(1)}, u32[]{:S(2)}, u32[]{:S(2)}) collective-permute-start(bf16[448,512]{1,0:T(8,128)(2,1)} %collective-permute-done.2.refs_0_), channel_id=1, source_target_pairs={{0,2},{2,4},{4,6},{6,7},{7,5},{5,3},{3,1},{1,0},{8,10},{10,12},{12... | collective-permute-start | bytes 1376264 | tf_op jit(solution)/shard_map/ppermute | solution.py:30
  28.6 18.3 %collective-permute-start.5 = (bf16[448,512]{1,0:T(8,128)(2,1)}, bf16[448,512]{1,0:T(8,128)(2,1)S(1)}, u32[]{:S(2)}, u32[]{:S(2)}) collective-permute-start(bf16[448,512]{1,0:T(8,128)(2,1)} %collective-permute-done.3.refs_1_), channel_id=1, source_target_pairs={{0,1},{2,0},{4,2},{6,4},{7,6},{5,7},{3,5},{1,3},{8,9},{10,8},{12,1... | collective-permute-start | bytes 1376264 | tf_op jit(solution)/shard_map/ppermute | solution.py:30
  30.8 18.4 %collective-permute-start.11 = (bf16[64,1792]{1,0:T(8,128)(2,1)}, bf16[64,1792]{1,0:T(8,128)(2,1)S(1)}, u32[]{:S(2)}, u32[]{:S(2)}) collective-permute-start(bf16[64,1792]{1,0:T(8,128)(2,1)} %get-tuple-element.69), channel_id=1, source_target_pairs={{0,2},{2,4},{4,6},{6,7},{7,5},{5,3},{3,1},{1,0},{8,10},{10,12},{12... | collective-permute-start | bytes 688136 | tf_op jit(solution)/shard_map/ppermute | solution.py:30
  38.9 16.1 %collective-permute-start.13 = (bf16[64,1792]{1,0:T(8,128)(2,1)}, bf16[64,1792]{1,0:T(8,128)(2,1)}, u32[]{:S(2)}, u32[]{:S(2)}) collective-permute-start(bf16[64,1792]{1,0:T(8,128)(2,1)} %get-tuple-element.69), channel_id=1, source_target_pairs={{0,1},{2,0},{4,2},{6,4},{7,6},{5,7},{3,5},{1,3},{8,9},{10,8},{12,1... | collective-permute-start | bytes 688136 | tf_op jit(solution)/shard_map/ppermute | solution.py:30
  39.5 16.9 %collective-permute-start.12 = (bf16[64,1792]{1,0:T(8,128)(2,1)}, bf16[64,1792]{1,0:T(8,128)(2,1)}, u32[]{:S(2)}, u32[]{:S(2)}) collective-permute-start(bf16[64,1792]{1,0:T(8,128)(2,1)} %get-tuple-element.70), channel_id=1, source_target_pairs={{0,2},{2,4},{4,6},{6,7},{7,5},{5,3},{3,1},{1,0},{8,10},{10,12},{12... | collective-permute-start | bytes 688136 | tf_op jit(solution)/shard_map/ppermute | solution.py:30
  41.0 1.2 %copy-start.5 = (f32[512,512]{1,0:T(8,128)S(1)}, f32[512,512]{1,0:T(8,128)}, u32[]{:S(2)}) copy-start(f32[512,512]{1,0:T(8,128)} %copy-done.4) | copy-start | bytes 3145732
  42.2 7.5 %copy-start.14 = (bf16[448,128]{0,1:T(8,128)(2,1)S(1)}, bf16[448,128]{0,1:T(8,128)(2,1)}, u32[]{:S(2)}) copy-start(bf16[448,128]{0,1:T(8,128)(2,1)} %copy.25) | copy-start | bytes 344068
  42.2 7.5 %copy-start.15 = (bf16[1,448,128]{1,2,0:T(8,128)(2,1)S(1)}, bf16[1,448,128]{1,2,0:T(8,128)(2,1)}, u32[]{:S(2)}) copy-start(bf16[1,448,128]{1,2,0:T(8,128)(2,1)} %copy.20) | copy-start | bytes 344068
  42.2 7.5 %copy-start.16 = (bf16[1,448,128]{1,2,0:T(8,128)(2,1)S(1)}, bf16[1,448,128]{1,2,0:T(8,128)(2,1)}, u32[]{:S(2)}) copy-start(bf16[1,448,128]{1,2,0:T(8,128)(2,1)} %copy.19) | copy-start | bytes 344068
  45.3 1.0 copy-start.6
  46.3 4.4 %copy-start.20 = (f32[2]{0:T(128)S(1)}, f32[2]{0:T(128)}, u32[]{:S(2)}) copy-start(f32[2]{0:T(128)} %param.17) | copy-start | bytes 28
  46.3 4.6 %copy-start.21 = (f32[2]{0:T(128)S(1)}, f32[2]{0:T(128)}, u32[]{:S(2)}) copy-start(f32[2]{0:T(128)} %param.18) | copy-start | bytes 28
  46.3 4.7 %copy-start.22 = (f32[2]{0:T(128)S(1)}, f32[2]{0:T(128)}, u32[]{:S(2)}) copy-start(f32[2]{0:T(128)} %param.19) | copy-start | bytes 28
  46.4 10.0 %collective-permute-start.14 = (bf16[64,1792]{1,0:T(8,128)(2,1)}, bf16[64,1792]{1,0:T(8,128)(2,1)}, u32[]{:S(2)}, u32[]{:S(2)}) collective-permute-start(bf16[64,1792]{1,0:T(8,128)(2,1)} %get-tuple-element.70), channel_id=1, source_target_pairs={{0,1},{2,0},{4,2},{6,4},{7,6},{5,7},{3,5},{1,3},{8,9},{10,8},{12,1... | collective-permute-start | bytes 688136 | tf_op jit(solution)/shard_map/ppermute | solution.py:30
  47.7 8.7 %collective-permute-start.6 = (bf16[224,512]{1,0:T(8,128)(2,1)}, bf16[224,512]{1,0:T(8,128)(2,1)}, u32[]{:S(2)}, u32[]{:S(2)}) collective-permute-start(bf16[224,512]{1,0:T(8,128)(2,1)} %get-tuple-element.50), channel_id=1, source_target_pairs={{0,2},{2,4},{4,6},{6,7},{7,5},{5,3},{3,1},{1,0},{8,10},{10,12},{12... | collective-permute-start | bytes 688136 | tf_op jit(solution)/shard_map/ppermute | solution.py:30
  49.2 7.2 %collective-permute-start.7 = (bf16[224,512]{1,0:T(8,128)(2,1)}, bf16[224,512]{1,0:T(8,128)(2,1)}, u32[]{:S(2)}, u32[]{:S(2)}) collective-permute-start(bf16[224,512]{1,0:T(8,128)(2,1)} %get-tuple-element.52), channel_id=1, source_target_pairs={{0,1},{2,0},{4,2},{6,4},{7,6},{5,7},{3,5},{1,3},{8,9},{10,8},{12,1... | collective-permute-start | bytes 688136 | tf_op jit(solution)/shard_map/ppermute | solution.py:30
  51.9 1.2 %copy-start.7 = (f32[512,512]{1,0:T(8,128)S(1)}, f32[512,512]{1,0:T(8,128)}, u32[]{:S(2)}) copy-start(f32[512,512]{1,0:T(8,128)} %copy-done.6) | copy-start | bytes 3145732
  53.1 7.4 %copy-start.13 = (bf16[448,512]{0,1:T(8,128)(2,1)S(1)}, bf16[448,512]{0,1:T(8,128)(2,1)}, u32[]{:S(2)}) copy-start(bf16[448,512]{0,1:T(8,128)(2,1)} %pad_maximum_fusion) | copy-start | bytes 1376260
  55.1 8.2 %collective-permute-start.9 = (s32[8]{0:T(128)S(1)}, s32[8]{0:T(128)S(1)}, u32[]{:S(2)}, u32[]{:S(2)}) collective-permute-start(s32[8]{0:T(128)S(1)} %slice.56), channel_id=1, source_target_pairs={{0,8},{8,16},{16,24},{1,9},{9,17},{17,25},{2,10},{10,18},{18,26},{... | collective-permute-start | bytes 104 | tf_op jit(solution)/shard_map/ppermute | solution.py:336
  56.4 26.4 %collective-permute-start.15 = (bf16[64,1792]{1,0:T(8,128)(2,1)S(1)}, bf16[64,1792]{1,0:T(8,128)(2,1)S(1)}, u32[]{:S(2)}, u32[]{:S(2)}) collective-permute-start(bf16[64,1792]{1,0:T(8,128)(2,1)S(1)} %collective-permute-done.11.rest_1_), channel_id=1, source_target_pairs={{0,2},{2,4},{4,6},{6,7},{7,5},{5,3},{3,1},{1,0},{8,10},{10,12},{12... | collective-permute-start | bytes 688136 | tf_op jit(solution)/shard_map/ppermute | solution.py:30
  58.0 24.8 %collective-permute-start.16 = (bf16[64,1792]{1,0:T(8,128)(2,1)}, bf16[64,1792]{1,0:T(8,128)(2,1)S(1)}, u32[]{:S(2)}, u32[]{:S(2)}) collective-permute-start(bf16[64,1792]{1,0:T(8,128)(2,1)} %collective-permute-done.12.rest_2_), channel_id=1, source_target_pairs={{0,2},{2,4},{4,6},{6,7},{7,5},{5,3},{3,1},{1,0},{8,10},{10,12},{12... | collective-permute-start | bytes 688136 | tf_op jit(solution)/shard_map/ppermute | solution.py:30
  59.6 23.2 %collective-permute-start.17 = (bf16[64,1792]{1,0:T(8,128)(2,1)}, bf16[64,1792]{1,0:T(8,128)(2,1)S(1)}, u32[]{:S(2)}, u32[]{:S(2)}) collective-permute-start(bf16[64,1792]{1,0:T(8,128)(2,1)} %collective-permute-done.13.rest_3_), channel_id=1, source_target_pairs={{0,1},{2,0},{4,2},{6,4},{7,6},{5,7},{3,5},{1,3},{8,9},{10,8},{12,1... | collective-permute-start | bytes 688136 | tf_op jit(solution)/shard_map/ppermute | solution.py:30
  60.0 22.8 %collective-permute-start.18 = (bf16[64,1792]{1,0:T(8,128)(2,1)}, bf16[64,1792]{1,0:T(8,128)(2,1)S(1)}, u32[]{:S(2)}, u32[]{:S(2)}) collective-permute-start(bf16[64,1792]{1,0:T(8,128)(2,1)} %collective-permute-done.14.rest_4_), channel_id=1, source_target_pairs={{0,1},{2,0},{4,2},{6,4},{7,6},{5,7},{3,5},{1,3},{8,9},{10,8},{12,1... | collective-permute-start | bytes 688136 | tf_op jit(solution)/shard_map/ppermute | solution.py:30
  61.9 4.5 %copy-start.11 = (f32[4,128]{1,0:T(4,128)S(1)}, f32[4,128]{1,0:T(4,128)}, u32[]{:S(2)}) copy-start(f32[4,128]{1,0:T(4,128)} %taps_x.3) | copy-start | bytes 6148
  61.9 4.5 %copy-start.12 = (f32[4,128]{1,0:T(4,128)S(1)}, f32[4,128]{1,0:T(4,128)}, u32[]{:S(2)}) copy-start(f32[4,128]{1,0:T(4,128)} %taps_bc.3) | copy-start | bytes 6148
  63.2 4.2 %collective-permute-start.8 = (bf16[8,256]{1,0:T(8,128)(2,1)S(1)}, bf16[8,256]{1,0:T(8,128)(2,1)S(1)}, u32[]{:S(2)}, u32[]{:S(2)}) collective-permute-start(bf16[8,256]{1,0:T(8,128)(2,1)S(1)} %slice.76), channel_id=1, source_target_pairs={{0,8},{8,16},{16,24},{1,9},{9,17},{17,25},{2,10},{10,18},{18,26},{... | collective-permute-start | bytes 12296 | tf_op jit(solution)/shard_map/ppermute | solution.py:341
  77.1 13.9 %all-to-all-start = ((bf16[8,64,128]{2,1,0:T(8,128)(2,1)}), bf16[8,64,128]{2,1,0:T(8,128)(2,1)S(1)}, u32[]{:S(2)}, u32[]{:S(2)}) async-start(bf16[8,64,128]{2,1,0:T(8,128)(2,1)} %bitcast.10), calls=%async_computation | async-start | bytes 262144 | tf_op jit(solution)/shard_map/all_to_all | solution.py:366
  82.8 10.0 %collective-permute-start.19 = (bf16[64,1792]{1,0:T(8,128)(2,1)S(1)}, bf16[64,1792]{1,0:T(8,128)(2,1)S(1)}, u32[]{:S(2)}, u32[]{:S(2)}) collective-permute-start(bf16[64,1792]{1,0:T(8,128)(2,1)S(1)} %collective-permute-done.15.rest_5_), channel_id=1, source_target_pairs={{0,2},{2,4},{4,6},{6,7},{7,5},{5,3},{3,1},{1,0},{8,10},{10,12},{12... | collective-permute-start | bytes 688136 | tf_op jit(solution)/shard_map/ppermute | solution.py:30
  84.9 12.0 %collective-permute-start.20 = (bf16[64,1792]{1,0:T(8,128)(2,1)S(1)}, bf16[64,1792]{1,0:T(8,128)(2,1)S(1)}, u32[]{:S(2)}, u32[]{:S(2)}) collective-permute-start(bf16[64,1792]{1,0:T(8,128)(2,1)S(1)} %collective-permute-done.16.rest_6_), channel_id=1, source_target_pairs={{0,2},{2,4},{4,6},{6,7},{7,5},{5,3},{3,1},{1,0},{8,10},{10,12},{12... | collective-permute-start | bytes 688136 | tf_op jit(solution)/shard_map/ppermute | solution.py:30
  86.3 10.5 %collective-permute-start.21 = (bf16[64,1792]{1,0:T(8,128)(2,1)S(1)}, bf16[64,1792]{1,0:T(8,128)(2,1)S(1)}, u32[]{:S(2)}, u32[]{:S(2)}) collective-permute-start(bf16[64,1792]{1,0:T(8,128)(2,1)S(1)} %collective-permute-done.17.rest_7_), channel_id=1, source_target_pairs={{0,1},{2,0},{4,2},{6,4},{7,6},{5,7},{3,5},{1,3},{8,9},{10,8},{12,1... | collective-permute-start | bytes 688136 | tf_op jit(solution)/shard_map/ppermute | solution.py:30
  86.9 11.8 %collective-permute-start.22 = (bf16[64,1792]{1,0:T(8,128)(2,1)S(1)}, bf16[64,1792]{1,0:T(8,128)(2,1)S(1)}, u32[]{:S(2)}, u32[]{:S(2)}) collective-permute-start(bf16[64,1792]{1,0:T(8,128)(2,1)S(1)} %collective-permute-done.18.rest_8_), channel_id=1, source_target_pairs={{0,1},{2,0},{4,2},{6,4},{7,6},{5,7},{3,5},{1,3},{8,9},{10,8},{12,1... | collective-permute-start | bytes 688136 | tf_op jit(solution)/shard_map/ppermute | solution.py:30
  96.9 0.7 copy-start.9
  98.7 8.7 %collective-permute-start.23 = (bf16[64,1792]{1,0:T(8,128)(2,1)S(1)}, bf16[64,1792]{1,0:T(8,128)(2,1)S(1)}, u32[]{:S(2)}, u32[]{:S(2)}) collective-permute-start(bf16[64,1792]{1,0:T(8,128)(2,1)S(1)} %collective-permute-done.19.rest_9_), channel_id=1, source_target_pairs={{0,2},{2,4},{4,6},{6,7},{7,5},{5,3},{3,1},{1,0},{8,10},{10,12},{12... | collective-permute-start | bytes 688136 | tf_op jit(solution)/shard_map/ppermute | solution.py:30
  99.9 7.5 %collective-permute-start.24 = (bf16[64,1792]{1,0:T(8,128)(2,1)S(1)}, bf16[64,1792]{1,0:T(8,128)(2,1)S(1)}, u32[]{:S(2)}, u32[]{:S(2)}) collective-permute-start(bf16[64,1792]{1,0:T(8,128)(2,1)S(1)} %collective-permute-done.22.rest_12_), channel_id=1, source_target_pairs={{0,1},{2,0},{4,2},{6,4},{7,6},{5,7},{3,5},{1,3},{8,9},{10,8},{12,1... | collective-permute-start | bytes 688136 | tf_op jit(solution)/shard_map/ppermute | solution.py:30
  100.7 1.3 %collective-permute-start.10 = (bf16[8,64,128]{2,1,0:T(8,128)(2,1)S(1)}, bf16[8,64,128]{2,1,0:T(8,128)(2,1)S(1)}, u32[]{:S(2)}, u32[]{:S(2)}) collective-permute-start(bf16[8,64,128]{2,1,0:T(8,128)(2,1)S(1)} %all-to-all-done.mine), channel_id=1, source_target_pairs={{0,8},{8,0},{16,24},{24,16},{1,9},{9,1},{17,25},{25,17},{2,10},{10... | collective-permute-start | bytes 393224 | tf_op jit(solution)/shard_map/ppermute | solution.py:381
  102.1 0.9 copy-start.10
  108.4 1.6 %collective-permute-start.25 = (bf16[64,1792]{1,0:T(8,128)(2,1)S(1)}, bf16[64,1792]{1,0:T(8,128)(2,1)S(1)}, u32[]{:S(2)}, u32[]{:S(2)}) collective-permute-start(bf16[64,1792]{1,0:T(8,128)(2,1)S(1)} %get-tuple-element.82), channel_id=1, source_target_pairs={{0,8},{8,0},{16,24},{24,16},{1,9},{9,1},{17,25},{25,17},{2,10},{10... | collective-permute-start | bytes 688136 | tf_op jit(solution)/shard_map/ppermute | solution.py:404

commit v5 on v4

--- a/solution.py
+++ b/solution.py
@@ -14,6 +14,7 @@
 VMEM = pl.BlockSpec(memory_space=pltpu.VMEM)
 ANY = pl.BlockSpec(memory_space=pl.ANY)
 HALO = 8
+W_FIRST = 3
 
 
 def ring_place(index, n):
@@ -214,36 +215,23 @@
     gated[rows:] = ((out_b[...] + enter_b[...] * dot(bc_b[:, state_w:], second)) * gate_b[...]).astype(BF16)
 
 
-def product(gated, where, pieces, held, sems):
-    copies = []
-    for k, (slot, _, row) in enumerate(where):
-        copies.append(
-            pltpu.make_async_copy(pieces[k], held.at[slot, pl.ds(row, pieces[k].shape[0])], sems.at[k])
-        )
-        copies[-1].start()
+def product(gated, distances, pieces):
     total = 0.0
-    waited = set()
-    for k, (slot, distance, _) in enumerate(where):
-        if slot in waited:
-            continue
-        waited.add(slot)
-        for j, (other, _, _) in enumerate(where):
-            if other == slot:
-                copies[j].wait()
+    for distance, piece in zip(distances, pieces):
         source = source_of(distance)
         rows = jnp.concatenate([part[source] for part in gated], 0)
-        total = total + jnp.dot(rows, held[slot], preferred_element_type=F32)
+        total = total + jnp.dot(rows, piece[...], preferred_element_type=F32)
     return total
 
 
-def product_early(where, mine, other, *rest):
-    pieces, (out, held, sems) = rest[: len(where)], rest[len(where) :]
-    out[...] = product((mine, other), where, pieces, held, sems)
-
-
-def product_last(where, mine, other, total, *rest):
-    pieces, (mine_out, other_out, held, sems) = rest[: len(where)], rest[len(where) :]
-    result = product((mine, other), where, pieces, held, sems) + total[...]
+def product_early(distances, mine, other, *rest):
+    rest[-1][...] = product((mine, other), distances, rest[:-1])
+
+
+def product_last(distance, mine, other, total, top, bottom, mine_out, other_out, held):
+    held[: top.shape[0]] = top[...]
+    held[top.shape[0] :] = bottom[...]
+    result = product((mine, other), [distance], [held]) + total[...]
     blocks, rows, width = mine.shape
     for i, (gated, out) in enumerate(((mine, mine_out), (other, other_out))):
         squares = jnp.zeros((rows, width), F32)
@@ -288,49 +276,42 @@
     own = (lax.dynamic_slice_in_dim(w_out, core * columns, columns, 1).astype(F32) * norm_gain[:, None]).astype(BF16)
     last = n_tensor // 2
     w_half = width // 2
-    w_forth = w_back = (own[:w_half], own[w_half:])
-    w_steps = []
+    w_forth = w_back = own
 
     cut = feat // 32 * 16
-    far = source_of(last) * feat
-    w_far = jnp.concatenate(
-        [lax.dynamic_slice_in_dim(w, far, feat, 0) for w in (w_zx[0], w_zx[1], w_bc, w_step)], 1
-    )
     forth = back = block
-    arrived, projs = [(0, block), None], []
-    for step in range(1, last + 1):
-        if step > 1:
-            forth, back = after((forth, back), projs[step - 2])
-        if step == last:
-            forth, back = call(halves, [shape(cut, tok_rows, kind=BF16), shape(feat - cut, tok_rows, kind=BF16)])(
-                forth, back
-            )
-        if step == 2:
-            tops = after((w_forth[0], w_back[0]), forth, back)
-        if step == 3:
-            bottoms = after((w_forth[1], w_back[1]), forth, back)
-        forth, back = ring_shift(forth, 1), ring_shift(back, -1)
-        if step == 2:
-            tops = ring_shift(tops[0], 1), ring_shift(tops[1], -1)
-        if step == 3:
-            bottoms = ring_shift(bottoms[0], 1), ring_shift(bottoms[1], -1)
-        blocks = [item for item in arrived if item]
+    arrived, projs = [(0, block, 0)], []
+    for step in range(1, last + 2):
+        if step <= last:
+            if step > 1:
+                forth, back = after(forth, projs[step - 2]), after(back, projs[step - 2])
+            if step == last:
+                forth, back = call(
+                    halves, [shape(cut, tok_rows, kind=BF16), shape(feat - cut, tok_rows, kind=BF16)]
+                )(forth, back)
+            if step == W_FIRST:
+                w_forth, w_back = after((w_forth, w_back), forth, back)
+            forth, back = ring_shift(forth, 1), ring_shift(back, -1)
+            if step == W_FIRST:
+                w_forth, w_back = ring_shift(w_forth, 1), ring_shift(w_back, -1)
+        sizes = [(distance, part.shape[0], skip) for distance, part, skip in arrived]
         total = projs[-1:]
         projs.append(
             call(
-                functools.partial(project, [(distance, feat, 0) for distance, _ in blocks], not total),
+                functools.partial(project, sizes, not total),
                 shape(tok_rows, 4 * width),
-                [pltpu.VMEM((len(blocks), feat, 4 * width), BF16), pltpu.SemaphoreType.DMA((len(blocks), 4))],
-                in_specs=[VMEM] * len(blocks) + [ANY] * 3 + [VMEM] * len(total),
+                [
+                    pltpu.VMEM((len(sizes), max(size for _, size, _ in sizes), 4 * width), BF16),
+                    pltpu.SemaphoreType.DMA((len(sizes), 4)),
+                ],
+                in_specs=[VMEM] * len(sizes) + [ANY] * 3 + [VMEM] * len(total),
                 flops=10**9,
-            )(*[part for _, part in blocks], w_zx, w_bc, w_step, *total)
+            )(*[part for _, part, _ in arrived], w_zx, w_bc, w_step, *total)
         )
-        arrived = [(-step, forth), (step, back)]
-    w_far = after(w_far, projs[0])
-    tokens_there = (forth, back, projs[-1], w_far)
+        arrived = [(-step, forth, 0), (step, back, 0)]
+        if step == last:
+            arrived = [(last, forth, 0), (last, back, cut)]
     proj = projs[-1]
-    for part, rows_of in ((forth, w_far[:cut]), (back, w_far[cut:])):
-        proj = proj + lax.dot_general(part, rows_of, (((0,), (0,)), ((), ())), preferred_element_type=F32)
 
     ahead = [(i, i + 1) for i in range(n_seq - 1)]
     seg_halo = lax.ppermute(segments[tok_rows - HALO :], "seq", ahead)
@@ -363,44 +344,35 @@
     )
 
     tok_own = tok_rows // n_tensor
-    mine = lax.all_to_all(gated.reshape(n_tensor, tok_own, width), "tensor", 0, 0)
-
-    w_forth, w_back = (tops[0], bottoms[0]), (tops[1], bottoms[1])
+
     w_steps = [(w_forth, w_back)]
-    orders = [tokens_there, messages, mine]
+    orders = [proj, messages]
     for step in range(2, last + 1):
         if step - 2 < len(orders):
             w_forth, w_back = after((w_forth, w_back), orders[step - 2])
-        if step < last:
-            w_forth = tuple(ring_shift(part, 1) for part in w_forth)
-            w_back = tuple(ring_shift(part, -1) for part in w_back)
-            w_steps.append((w_forth, w_back))
-        else:
-            w_far_parts = ring_shift(w_forth[0], 1), ring_shift(w_back[1], -1)
+        if step == 4:
+            w_forth, w_back = after((w_forth, w_back), mine)
+        if step == last:
+            half = shape(w_half, columns, kind=BF16)
+            w_forth, w_back = call(halves, [half, half])(w_forth, w_back)
+        w_forth, w_back = ring_shift(w_forth, 1), ring_shift(w_back, -1)
+        w_steps.append((w_forth, w_back))
+        if step == 2:
+            blocks = after(gated, w_forth, w_back).reshape(n_tensor, tok_own, width)
+            mine = lax.all_to_all(blocks, "tensor", 0, 0)
     swap = [(i, i ^ 1) for i in range(n_seq)]
     other = lax.ppermute(mine, "seq", swap)
-    pieces, where = [own], [(0, 0, 0)]
-    for i, pair in enumerate(w_steps):
-        for side, parts in enumerate(pair):
-            distance = i + 1 if side else -i - 1
-            pieces += parts
-            where += [(2 * i + 1 + side, distance, 0), (2 * i + 1 + side, distance, w_half)]
-    total = call(
-        functools.partial(product_early, where),
-        shape(2 * tok_own, columns),
-        [pltpu.VMEM((n_tensor - 1, width, columns), BF16), pltpu.SemaphoreType.DMA((len(where),))],
-        in_specs=[VMEM, VMEM] + [ANY] * len(pieces),
-        flops=10**9,
-    )(mine, other, *pieces)
-    where = [(0, last, 0), (0, last, w_half)]
+    pieces, distances = [own], [0]
+    for i, pair in enumerate(w_steps[:-1]):
+        pieces += pair
+        distances += [-i - 1, i + 1]
+    total = call(functools.partial(product_early, distances), shape(2 * tok_own, columns), flops=10**9)(
+        mine, other, *pieces
+    )
     half = shape(tok_own, columns, kind=BF16)
     out_own, out_other = call(
-        functools.partial(product_last, where),
-        [half, half],
-        [pltpu.VMEM((1, width, columns), BF16), pltpu.SemaphoreType.DMA((2,))],
-        in_specs=[VMEM, VMEM, VMEM] + [ANY] * 2,
-        flops=10**8,
-    )(mine, other, total, *w_far_parts)
+        functools.partial(product_last, last), [half, half], [pltpu.VMEM((width, columns), BF16)], flops=10**8
+    )(mine, other, total, *w_steps[-1])
     arrived = lax.ppermute(out_other, "seq", swap)
     is_first = core == 0
     return jnp.concatenate([jnp.where(is_first, out_own, arrived), jnp.where(is_first, arrived, out_own)], 1)

time: 112 us -> 96.5 us (0.86)
  blocking collectives: 6.46 us -> 22 us
  local copies, waits for them, and re-layouts: 21.4 us -> 6.91 us
  starting transfers between devices: 33.8 us -> 20 us
  matrix products: 4.71 us -> 1.11 us
  waiting for transfers between devices: 23.2 us -> 26.6 us
  Pallas kernels: 19 us -> 17.3 us
    all_to_all x0 -> x1, blocking collectives: none -> 14.4 us  [local(): mine = lax.all_to_all(blocks, 'tensor', 0, 0)]
    ppermute x22 -> x16, waiting for transfers between devices: 16.5 us -> 23.8 us  [ring_shift(): lax.ppermute(block, 'tensor', [(order[i], order[(i + step) % n]) for i in...]
    dynamic_slice x5 -> x0, local copies, waits for them, and re-layouts: 6.62 us -> none  [local(): lax.dynamic_slice_in_dim(w, far, feat, 0)]
    ppermute x22 -> x16, starting transfers between devices: 23.6 us -> 17.4 us  [ring_shift(): lax.ppermute(block, 'tensor', [(order[i], order[(i + step) % n]) for i in...]
    all_to_all x1 -> x0, starting transfers between devices: 5.65 us -> none  [local(): lax.all_to_all(gated.reshape(n_tensor, tok_own, width), 'tensor', 0, 0)]
    unnamed x47 -> x32, local copies, waits for them, and re-layouts: 9.59 us -> 5.52 us
    all_to_all x1 -> x0, waiting for transfers between devices: 4.06 us -> none  [local(): lax.all_to_all(gated.reshape(n_tensor, tok_own, width), 'tensor', 0, 0)]
    dot_general x2 -> x0, matrix products: 2.66 us -> none  [local(): lax.dot_general(part, rows_of, (((0,), (0,)), ((), ())), preferred_elemen...]
  transfers between devices with their start and end apart: 27 -> 20, of which waited for: 10 -> 10; matrix products, arithmetic and copies ran while one was open for 17% -> 4% of each run, Pallas kernels for 16% -> 18%
where the time goes in v5:
time: 96.5 us; the launch traced here: 96 us
  waiting for transfers between devices  26.6 us (28%)
  blocking collectives  22 us (23%)
  starting transfers between devices  20 us (21%)
  Pallas kernels  17.3 us (18%)
  local copies, waits for them, and re-layouts  6.91 us (7%)
  other arithmetic  1.82 us (2%)
  matrix products  1.11 us (1%)
    ppermute x16, waiting for transfers between devices, ring_shift(): lax.ppermute(block, 'tensor', [(order[i], order[(i + step) % n]) for i in...  23.8 us
    ppermute x16, starting transfers between devices, ring_shift(): lax.ppermute(block, 'tensor', [(order[i], order[(i + step) % n]) for i in...  17.4 us
    all_to_all x1, blocking collectives, local(): mine = lax.all_to_all(blocks, 'tensor', 0, 0)  14.4 us
    pallas_call x5, Pallas kernels, local(): call(functools.partial(project, sizes, not total), shape(tok_rows, 4 * wi...  10.3 us
    all_gather x1, blocking collectives, local(): messages = lax.all_gather(message, 'seq')  7.57 us
    unnamed x32, local copies, waits for them, and re-layouts  5.52 us
    pallas_call x1, Pallas kernels, local(): call(functools.partial(product_early, distances), shape(2 * tok_own, colu...  2.28 us
  transfers between devices with their start and end apart: 20, of which 10 were waited for; matrix products, arithmetic and copies ran while one was open for 4% of the time, Pallas kernels for 18%

profile of v5, /device:TPU:0, one launch (start us, length us, event | category | flops | bytes accessed | tf_op | source)
XLA Modules:
  0.0 96.0 jit_solution(5331098090507516938)
XLA Ops:
  0.0 3.0 %collective-permute-start = (bf16[448,512]{1,0:T(8,128)(2,1)}, bf16[448,512]{1,0:T(8,128)(2,1)S(1)}, u32[]{:S(2)}, u32[]{:S(2)}) collective-permute-start(bf16[448,512]{1,0:T(8,128)(2,1)} %bitcast.13), channel_id=1, source_target_pairs={{0,2},{2,4},{4,6},{6,7},{7,5},{5,3},{3,1},{1,0},{8,10},{10,12},{12... | collective-permute-start | bytes 1376264 | tf_op jit(solution)/shard_map/ppermute | solution.py:31
  3.0 1.1 %convolution_bitcast_fusion.refs_3_.refs_4_ = bf16[3584,128]{1,0:T(8,128)(2,1)S(1)} fusion(bf16[2,128]{1,0:T(2,128)(2,1)} %constant.25.clone, bf16[3584,2]{0,1:T(2,128)(2,1)S(1)} %copy-done), kind=kOutput, calls=%fused_computation | convolution fusion | flops 1835008 | bytes 932352 | tf_op jit(solution)/shard_map/dot_general | solution.py:272
  4.2 0.0 copy-start.1
  4.2 1.5 %copy-done.1 = bf16[2,3584,128]{2,1,0:T(8,128)(2,1)S(1)} copy-done((bf16[2,3584,128]{2,1,0:T(8,128)(2,1)S(1)}, bf16[2,3584,128]{2,1,0:T(8,128)(2,1)}, u32[]{:S(2)}) %copy-start.1) | copy-done | bytes 1835032
  5.7 1.2 %copy-done.3 = bf16[3584,128]{1,0:T(8,128)(2,1)S(1)} copy-done((bf16[3584,128]{1,0:T(8,128)(2,1)S(1)}, bf16[3584,128]{1,0:T(8,128)(2,1)}, u32[]{:S(2)}) %copy-start.3) | copy-done | bytes 917528
  6.8 1.0 %copy-done.7 = bf16[512,448]{0,1:T(8,128)(2,1)S(1)} copy-done((bf16[512,448]{0,1:T(8,128)(2,1)S(1)}, bf16[512,448]{0,1:T(8,128)(2,1)}, u32[]{:S(2)}) %copy-start.7) | copy-done | bytes 458776
  7.9 0.6 shard_map.127.refs_5_
  8.5 5.2 %collective-permute-done.refs_0_ = bf16[448,512]{1,0:T(8,128)(2,1)S(1)} collective-permute-done((bf16[448,512]{1,0:T(8,128)(2,1)}, bf16[448,512]{1,0:T(8,128)(2,1)S(1)}, u32[]{:S(2)}, u32[]{:S(2)}) %collective-permute-start) | collective-permute-done | bytes 458784 | tf_op jit(solution)/shard_map/ppermute | solution.py:31
  13.7 1.8 %collective-permute-start.1 = (bf16[448,512]{1,0:T(8,128)(2,1)S(1)}, bf16[448,512]{1,0:T(8,128)(2,1)}, u32[]{:S(2)}, u32[]{:S(2)}) collective-permute-start(bf16[448,512]{1,0:T(8,128)(2,1)S(1)} %collective-permute-done.refs_0_), channel_id=1, source_target_pairs={{0,2},{2,4},{4,6},{6,7},{7,5},{5,3},{3,1},{1,0},{8,10},{10,12},{12... | collective-permute-start | bytes 1376264 | tf_op jit(solution)/shard_map/ppermute | solution.py:31
  15.5 0.2 collective-permute-start.4
  15.7 2.9 %shard_map.128.refs_5_ = f32[512,512]{1,0:T(8,128)S(1)} custom-call(bf16[448,512]{1,0:T(8,128)(2,1)S(1)} %collective-permute-done.refs_0_, bf16[448,512]{1,0:T(8,128)(2,1)} %collective-permute-done.2.refs_1_, bf16[2,3584,128]{2,1,0:T(8,128)(2,1)} %refs_2_.9, bf16[3584,128]{1,0:T(8,128)(2,1)S(1)} %copy-done.4, ...), custom_call_target="tpu_custom_call" | custom-call | flops 1000000000 | bytes 2097152 | tf_op jit(solution)/shard_map/pallas_call | solution.py:300
  18.7 6.9 %collective-permute-done.1.refs_0_ = bf16[448,512]{1,0:T(8,128)(2,1)} collective-permute-done((bf16[448,512]{1,0:T(8,128)(2,1)S(1)}, bf16[448,512]{1,0:T(8,128)(2,1)}, u32[]{:S(2)}, u32[]{:S(2)}) %collective-permute-start.1) | collective-permute-done | bytes 458784 | tf_op jit(solution)/shard_map/ppermute | solution.py:31
  25.6 1.5 %collective-permute-start.3 = (bf16[448,512]{1,0:T(8,128)(2,1)}, bf16[448,512]{1,0:T(8,128)(2,1)S(1)}, u32[]{:S(2)}, u32[]{:S(2)}) collective-permute-start(bf16[448,512]{1,0:T(8,128)(2,1)} %collective-permute-done.1.refs_0_), channel_id=1, source_target_pairs={{0,2},{2,4},{4,6},{6,7},{7,5},{5,3},{3,1},{1,0},{8,10},{10,12},{12... | collective-permute-start | bytes 1376264 | tf_op jit(solution)/shard_map/ppermute | solution.py:31
  27.1 0.5 collective-permute-start.5
  27.6 0.9 multiply_convert_fusion.rest_0_
  28.5 1.6 %collective-permute-start.10 = (bf16[128,1792]{1,0:T(8,128)(2,1)}, bf16[128,1792]{1,0:T(8,128)(2,1)}, u32[]{:S(2)}, u32[]{:S(2)}) collective-permute-start(bf16[128,1792]{1,0:T(8,128)(2,1)} %multiply_convert_fusion.rest_0_), channel_id=1, source_target_pairs={{0,2},{2,4},{4,6},{6,7},{7,5},{5,3},{3,1},{1,0},{8,10},{10,12},{12... | collective-permute-start | bytes 1376264 | tf_op jit(solution)/shard_map/ppermute | solution.py:31
  30.1 0.5 collective-permute-start.11
  30.6 3.0 %shard_map.129.refs_5_ = f32[512,512]{1,0:T(8,128)S(1)} custom-call(bf16[448,512]{1,0:T(8,128)(2,1)} %collective-permute-done.1.refs_0_, bf16[448,512]{1,0:T(8,128)(2,1)} %collective-permute-done.4.refs_1_, bf16[2,3584,128]{2,1,0:T(8,128)(2,1)} %refs_2_.9, bf16[3584,128]{1,0:T(8,128)(2,1)S(1)} %copy-done.4, ...), custom_call_target="tpu_custom_call" | custom-call | flops 1000000000 | bytes 2097152 | tf_op jit(solution)/shard_map/pallas_call | solution.py:300
  33.6 5.6 %collective-permute-done.3.forth.refs_0_ = bf16[448,512]{1,0:T(8,128)(2,1)S(1)} collective-permute-done((bf16[448,512]{1,0:T(8,128)(2,1)}, bf16[448,512]{1,0:T(8,128)(2,1)S(1)}, u32[]{:S(2)}, u32[]{:S(2)}) %collective-permute-start.3) | collective-permute-done | bytes 458784 | tf_op jit(solution)/shard_map/ppermute | solution.py:31
  39.3 1.5 %collective-permute-done.5.back.refs_1_ = bf16[448,512]{1,0:T(8,128)(2,1)S(1)} collective-permute-done((bf16[448,512]{1,0:T(8,128)(2,1)}, bf16[448,512]{1,0:T(8,128)(2,1)S(1)}, u32[]{:S(2)}, u32[]{:S(2)}) %collective-permute-start.5) | collective-permute-done | bytes 458784 | tf_op jit(solution)/shard_map/ppermute | solution.py:31
  40.8 0.8 shard_map.130
  41.6 0.8 copy-done.5
  42.3 1.6 %collective-permute-start.6 = (bf16[224,512]{1,0:T(8,128)(2,1)}, bf16[224,512]{1,0:T(8,128)(2,1)}, u32[]{:S(2)}, u32[]{:S(2)}) collective-permute-start(bf16[224,512]{1,0:T(8,128)(2,1)} %get-tuple-element.46), channel_id=1, source_target_pairs={{0,2},{2,4},{4,6},{6,7},{7,5},{5,3},{3,1},{1,0},{8,10},{10,12},{12... | collective-permute-start | bytes 688136 | tf_op jit(solution)/shard_map/ppermute | solution.py:31
  43.9 0.4 collective-permute-start.7
  44.4 0.1 slice.34
  44.4 1.3 %collective-permute-start.9 = (s32[8]{0:T(128)S(1)}, s32[8]{0:T(128)S(1)}, u32[]{:S(2)}, u32[]{:S(2)}) collective-permute-start(s32[8]{0:T(128)S(1)} %slice.34), channel_id=1, source_target_pairs={{0,8},{8,16},{16,24},{1,9},{9,17},{17,25},{2,10},{10,18},{18,26},{... | collective-permute-start | bytes 104 | tf_op jit(solution)/shard_map/ppermute | solution.py:317
  45.7 0.1 slice.38
  45.8 0.1 slice.42.seg_ext
  45.9 0.1 broadcast_in_dim.26
  46.0 0.1 broadcast_in_dim_reshape.9.bias
  46.1 0.1 broadcast_in_dim.27
  46.1 0.1 broadcast_in_dim_reshape.10.rate
  46.2 0.1 broadcast_in_dim.28
  46.3 0.1 broadcast_in_dim_reshape.11.skip
  46.4 1.0 %copy-done.6 = bf16[448,512]{1,0:T(8,128)(2,1)S(1)} copy-done((bf16[448,512]{1,0:T(8,128)(2,1)S(1)}, bf16[448,512]{1,0:T(8,128)(2,1)}, u32[]{:S(2)}) %copy-start.6) | copy-done | bytes 458776
  47.4 2.0 %shard_map.131.refs_5_ = f32[512,512]{1,0:T(8,128)S(1)} custom-call(bf16[448,512]{1,0:T(8,128)(2,1)S(1)} %collective-permute-done.3.forth.refs_0_, bf16[448,512]{1,0:T(8,128)(2,1)S(1)} %copy-done.6, bf16[2,3584,128]{2,1,0:T(8,128)(2,1)} %refs_2_.9, bf16[3584,128]{1,0:T(8,128)(2,1)S(1)} %copy-done.4, ...), custom_call_target="tpu_custom_call" | custom-call | flops 1000000000 | bytes 2097152 | tf_op jit(solution)/shard_map/pallas_call | solution.py:300
  49.4 0.0 copy-start.8
  49.4 2.1 %collective-permute-done.6.refs_0_ = bf16[224,512]{1,0:T(8,128)(2,1)} collective-permute-done((bf16[224,512]{1,0:T(8,128)(2,1)}, bf16[224,512]{1,0:T(8,128)(2,1)}, u32[]{:S(2)}, u32[]{:S(2)}) %collective-permute-start.6) | collective-permute-done | bytes 229408 | tf_op jit(solution)/shard_map/ppermute | solution.py:31
  51.5 0.9 collective-permute-done.7.refs_1_
  52.5 1.8 %shard_map.132.proj = f32[512,512]{1,0:T(8,128)S(1)} custom-call(bf16[224,512]{1,0:T(8,128)(2,1)} %collective-permute-done.6.refs_0_, bf16[224,512]{1,0:T(8,128)(2,1)} %collective-permute-done.7.refs_1_, bf16[2,3584,128]{2,1,0:T(8,128)(2,1)S(1)} %copy-done.2, bf16[3584,128]{1,0:T(8,128)(2,1)S(1)} %copy-done.4, ...), custom_call_target="tpu_custom_call" | custom-call | flops 1000000000 | bytes 2097152 | tf_op jit(solution)/shard_map/pallas_call | solution.py:300
  54.3 1.6 %collective-permute-start.12 = (bf16[128,1792]{1,0:T(8,128)(2,1)}, bf16[128,1792]{1,0:T(8,128)(2,1)S(1)}, u32[]{:S(2)}, u32[]{:S(2)}) collective-permute-start(bf16[128,1792]{1,0:T(8,128)(2,1)} %collective-permute-done.10.rest_1_), channel_id=1, source_target_pairs={{0,2},{2,4},{4,6},{6,7},{7,5},{5,3},{3,1},{1,0},{8,10},{10,12},{12... | collective-permute-start | bytes 1376264 | tf_op jit(solution)/shard_map/ppermute | solution.py:31
  55.9 0.4 collective-permute-start.13
  56.4 0.6 fusion.1
  57.0 1.3 %collective-permute-start.8 = (bf16[8,256]{1,0:T(8,128)(2,1)S(1)}, bf16[8,256]{1,0:T(8,128)(2,1)S(1)}, u32[]{:S(2)}, u32[]{:S(2)}) collective-permute-start(bf16[8,256]{1,0:T(8,128)(2,1)S(1)} %slice.46), channel_id=1, source_target_pairs={{0,8},{8,16},{16,24},{1,9},{9,17},{17,25},{2,10},{10,18},{18,26},{... | collective-permute-start | bytes 12296 | tf_op jit(solution)/shard_map/ppermute | solution.py:322
  58.3 0.1 pad_add_fusion
  58.4 0.1 slice.43.seg_ext.seg_col
  58.5 1.0 %shard_map.133 = (f32[256,128]{1,0:T(8,128)S(1)}, f32[256,128]{1,0:T(8,128)S(1)}, f32[256,128]{1,0:T(8,128)S(1)}, f32[72,128]{1,0:T(8,128)S(1)}, f32[256,128]{1,0:T(8,128)S(1)}) custom-call(f32[512,512]{1,0:T(8,128)S(1)} %shard_map.132.proj, s32[264,1]{1,0:T(8,128)S(1)} %slice.42.seg_ext, s32[1,256]{1,0:T(1,128)S(1)} %bitcast.17, f32[4,128]{1,0:T(4,128)S(1)} %copy-done.8, ...), custom_call_target="tpu_custom_call" | custom-call | flops 10000000 | bytes 2097152 | tf_op jit(solution)/shard_map/pallas_call | solution.py:328
  59.5 1.2 %shard_map.134 = (f32[256,128]{1,0:T(8,128)S(1)}, f32[256,128]{1,0:T(8,128)S(1)}, f32[256,128]{1,0:T(8,128)S(1)}, f32[256,128]{1,0:T(8,128)S(1)}, f32[256,128]{1...) custom-call(f32[512,512]{1,0:T(8,128)S(1)} %shard_map.132.proj, ...), custom_call_target="tpu_custom_call" | custom-call | flops 10000000 | bytes 2097152 | tf_op jit(solution)/shard_map/pallas_call | solution.py:333
  60.7 7.6 %all-gather = f32[288,128]{1,0:T(8,128)S(1)} all-gather(f32[72,128]{1,0:T(8,128)S(1)} %get-tuple-element.49), channel_id=2, replica_groups=mesh['seq'=4,'tensor'=8] {'seq'}, dimensions={0}, use_global_device_ids=true | all-gather | bytes 184320 | tf_op jit(solution)/shard_map/all_gather | solution.py:338
  68.3 1.6 %collective-permute-start.15 = (bf16[128,1792]{1,0:T(8,128)(2,1)S(1)}, bf16[128,1792]{1,0:T(8,128)(2,1)S(1)}, u32[]{:S(2)}, u32[]{:S(2)}) collective-permute-start(bf16[128,1792]{1,0:T(8,128)(2,1)S(1)} %collective-permute-done.12.rest_3_), channel_id=1, source_target_pairs={{0,2},{2,4},{4,6},{6,7},{7,5},{5,3},{3,1},{1,0},{8,10},{10,12},{12... | collective-permute-start | bytes 1376264 | tf_op jit(solution)/shard_map/ppermute | solution.py:31
  69.9 0.5 collective-permute-start.16
  70.3 0.5 shard_map.135
  70.8 0.9 shard_map.136
  71.7 14.4 %all_to_all.5.mine = bf16[8,64,128]{2,1,0:T(8,128)(2,1)S(1)} all-to-all(bf16[8,64,128]{2,1,0:T(8,128)(2,1)S(1)} %bitcast.12), channel_id=1, replica_groups=mesh['seq'=4,'tensor'=8] {'tensor'}, dimensions={0} | all-to-all | bytes 262144 | tf_op jit(solution)/shard_map/all_to_all | solution.py:362
  86.1 1.0 %collective-permute-start.17 = (bf16[64,1792]{1,0:T(8,128)(2,1)S(1)}, bf16[64,1792]{1,0:T(8,128)(2,1)S(1)}, u32[]{:S(2)}, u32[]{:S(2)}) collective-permute-start(bf16[64,1792]{1,0:T(8,128)(2,1)S(1)} %get-tuple-element.71), channel_id=1, source_target_pairs={{0,2},{2,4},{4,6},{6,7},{7,5},{5,3},{3,1},{1,0},{8,10},{10,12},{12... | collective-permute-start | bytes 688136 | tf_op jit(solution)/shard_map/ppermute | solution.py:31
  87.1 1.1 %collective-permute-start.18 = (bf16[64,1792]{1,0:T(8,128)(2,1)S(1)}, bf16[64,1792]{1,0:T(8,128)(2,1)S(1)}, u32[]{:S(2)}, u32[]{:S(2)}) collective-permute-start(bf16[64,1792]{1,0:T(8,128)(2,1)S(1)} %get-tuple-element.72), channel_id=1, source_target_pairs={{0,1},{2,0},{4,2},{6,4},{7,6},{5,7},{3,5},{1,3},{8,9},{10,8},{12,1... | collective-permute-start | bytes 688136 | tf_op jit(solution)/shard_map/ppermute | solution.py:31
  88.2 1.3 %collective-permute-done.14.other = bf16[8,64,128]{2,1,0:T(8,128)(2,1)S(1)} collective-permute-done((bf16[8,64,128]{2,1,0:T(8,128)(2,1)S(1)}, bf16[8,64,128]{2,1,0:T(8,128)(2,1)S(1)}, u32[]{:S(2)}, u32[]{:S(2)}) %collective-permute-start.14) | collective-permute-done | bytes 131104 | tf_op jit(solution)/shard_map/ppermute | solution.py:364
  89.6 2.3 %shard_map.137.total = f32[128,1792]{1,0:T(8,128)S(1)} custom-call(bf16[8,64,128]{2,1,0:T(8,128)(2,1)S(1)} %all_to_all.5.mine, bf16[8,64,128]{2,1,0:T(8,128)(2,1)S(1)} %collective-permute-done.14.other, bf16[128,1792]{1,0:T(8,128)(2,1)} %multiply_convert_fusion.rest_0_, bf16[128,1792]{1,0:T(8,128)(2,1)} %collective-permute-done.10.rest_1_, ...), custom_call_target="tpu_custom_call" | custom-call | flops 1000000000 | bytes 2097152 | tf_op jit(solution)/shard_map/pallas_call | solution.py:369
  91.9 0.7 collective-permute-done.17.top
  92.6 0.7 collective-permute-done.18.bottom
  93.3 0.3 shard_map.139
  93.6 0.1 collective-permute-start.19
  93.7 1.5 %collective-permute-done.19 = bf16[64,1792]{1,0:T(8,128)(2,1)S(1)} collective-permute-done((bf16[64,1792]{1,0:T(8,128)(2,1)S(1)}, bf16[64,1792]{1,0:T(8,128)(2,1)S(1)}, u32[]{:S(2)}, u32[]{:S(2)}) %collective-permute-start.19) | collective-permute-done | bytes 229408 | tf_op jit(solution)/shard_map/ppermute | solution.py:376
  95.2 0.8 pad_maximum_fusion
  (42 shorter events, 0.2 us)
Async XLA Ops:
  0.0 3.0 %copy-start = (bf16[3584,2]{0,1:T(2,128)(2,1)S(1)}, bf16[3584,2]{0,1:T(2,128)(2,1)}, u32[]{:S(2)}) copy-start(bf16[3584,2]{0,1:T(2,128)(2,1)} %param.16) | copy-start | bytes 43012
  0.0 13.7 %collective-permute-start = (bf16[448,512]{1,0:T(8,128)(2,1)}, bf16[448,512]{1,0:T(8,128)(2,1)S(1)}, u32[]{:S(2)}, u32[]{:S(2)}) collective-permute-start(bf16[448,512]{1,0:T(8,128)(2,1)} %bitcast.13), channel_id=1, source_target_pairs={{0,2},{2,4},{4,6},{6,7},{7,5},{5,3},{3,1},{1,0},{8,10},{10,12},{12... | collective-permute-start | bytes 1376264 | tf_op jit(solution)/shard_map/ppermute | solution.py:31
  3.0 12.5 %collective-permute-start.2 = (bf16[448,512]{1,0:T(8,128)(2,1)}, bf16[448,512]{1,0:T(8,128)(2,1)}, u32[]{:S(2)}, u32[]{:S(2)}) collective-permute-start(bf16[448,512]{1,0:T(8,128)(2,1)} %bitcast.14), channel_id=1, source_target_pairs={{0,1},{2,0},{4,2},{6,4},{7,6},{5,7},{3,5},{1,3},{8,9},{10,8},{12,1... | collective-permute-start | bytes 1376264 | tf_op jit(solution)/shard_map/ppermute | solution.py:31
  4.2 1.5 %copy-start.1 = (bf16[2,3584,128]{2,1,0:T(8,128)(2,1)S(1)}, bf16[2,3584,128]{2,1,0:T(8,128)(2,1)}, u32[]{:S(2)}) copy-start(bf16[2,3584,128]{2,1,0:T(8,128)(2,1)} %refs_2_.9) | copy-start | bytes 5505028
  5.7 1.2 %copy-start.3 = (bf16[3584,128]{1,0:T(8,128)(2,1)S(1)}, bf16[3584,128]{1,0:T(8,128)(2,1)}, u32[]{:S(2)}) copy-start(bf16[3584,128]{1,0:T(8,128)(2,1)} %refs_3_.7) | copy-start | bytes 2752516
  6.8 1.0 %copy-start.7 = (bf16[512,448]{0,1:T(8,128)(2,1)S(1)}, bf16[512,448]{0,1:T(8,128)(2,1)}, u32[]{:S(2)}) copy-start(bf16[512,448]{0,1:T(8,128)(2,1)} %param.13) | copy-start | bytes 1376260
  7.9 7.8 %copy-start.4 = (bf16[3584,128]{1,0:T(8,128)(2,1)S(1)}, bf16[3584,128]{1,0:T(8,128)(2,1)}, u32[]{:S(2)}) copy-start(bf16[3584,128]{1,0:T(8,128)(2,1)} %refs_3_.7) | copy-start | bytes 2752516
  13.7 11.9 %collective-permute-start.1 = (bf16[448,512]{1,0:T(8,128)(2,1)S(1)}, bf16[448,512]{1,0:T(8,128)(2,1)}, u32[]{:S(2)}, u32[]{:S(2)}) collective-permute-start(bf16[448,512]{1,0:T(8,128)(2,1)S(1)} %collective-permute-done.refs_0_), channel_id=1, source_target_pairs={{0,2},{2,4},{4,6},{6,7},{7,5},{5,3},{3,1},{1,0},{8,10},{10,12},{12... | collective-permute-start | bytes 1376264 | tf_op jit(solution)/shard_map/ppermute | solution.py:31
  15.5 11.6 %collective-permute-start.4 = (bf16[448,512]{1,0:T(8,128)(2,1)}, bf16[448,512]{1,0:T(8,128)(2,1)}, u32[]{:S(2)}, u32[]{:S(2)}) collective-permute-start(bf16[448,512]{1,0:T(8,128)(2,1)} %collective-permute-done.2.refs_1_), channel_id=1, source_target_pairs={{0,1},{2,0},{4,2},{6,4},{7,6},{5,7},{3,5},{1,3},{8,9},{10,8},{12,1... | collective-permute-start | bytes 1376264 | tf_op jit(solution)/shard_map/ppermute | solution.py:31
  15.7 11.9 %copy-start.10 = (bf16[128,3584]{1,0:T(8,128)(2,1)S(1)}, bf16[128,3584]{1,0:T(8,128)(2,1)}, u32[]{:S(2)}) copy-start(bf16[128,3584]{1,0:T(8,128)(2,1)} %param.23) | copy-start | bytes 2752516
  15.7 11.9 %copy-start.12 = (f32[128]{0:T(128)S(1)}, f32[128]{0:T(128)}, u32[]{:S(2)}) copy-start(f32[128]{0:T(128)} %param.22) | copy-start | bytes 1540
  25.6 13.7 %collective-permute-start.3 = (bf16[448,512]{1,0:T(8,128)(2,1)}, bf16[448,512]{1,0:T(8,128)(2,1)S(1)}, u32[]{:S(2)}, u32[]{:S(2)}) collective-permute-start(bf16[448,512]{1,0:T(8,128)(2,1)} %collective-permute-done.1.refs_0_), channel_id=1, source_target_pairs={{0,2},{2,4},{4,6},{6,7},{7,5},{5,3},{3,1},{1,0},{8,10},{10,12},{12... | collective-permute-start | bytes 1376264 | tf_op jit(solution)/shard_map/ppermute | solution.py:31
  27.1 13.7 %collective-permute-start.5 = (bf16[448,512]{1,0:T(8,128)(2,1)}, bf16[448,512]{1,0:T(8,128)(2,1)S(1)}, u32[]{:S(2)}, u32[]{:S(2)}) collective-permute-start(bf16[448,512]{1,0:T(8,128)(2,1)} %collective-permute-done.4.refs_1_), channel_id=1, source_target_pairs={{0,1},{2,0},{4,2},{6,4},{7,6},{5,7},{3,5},{1,3},{8,9},{10,8},{12,1... | collective-permute-start | bytes 1376264 | tf_op jit(solution)/shard_map/ppermute | solution.py:31
  28.5 15.8 %copy-start.11 = (s32[512]{0:T(512)S(1)}, s32[512]{0:T(512)}, u32[]{:S(2)}) copy-start(s32[512]{0:T(512)} %param.24) | copy-start | bytes 6148
  28.5 17.4 %copy-start.13 = (f32[2]{0:T(128)S(1)}, f32[2]{0:T(128)}, u32[]{:S(2)}) copy-start(f32[2]{0:T(128)} %param.17) | copy-start | bytes 28
  28.5 17.5 %copy-start.14 = (f32[2]{0:T(128)S(1)}, f32[2]{0:T(128)}, u32[]{:S(2)}) copy-start(f32[2]{0:T(128)} %param.18) | copy-start | bytes 28
  28.5 17.7 %copy-start.15 = (f32[2]{0:T(128)S(1)}, f32[2]{0:T(128)}, u32[]{:S(2)}) copy-start(f32[2]{0:T(128)} %param.19) | copy-start | bytes 28
  28.5 25.7 %collective-permute-start.10 = (bf16[128,1792]{1,0:T(8,128)(2,1)}, bf16[128,1792]{1,0:T(8,128)(2,1)}, u32[]{:S(2)}, u32[]{:S(2)}) collective-permute-start(bf16[128,1792]{1,0:T(8,128)(2,1)} %multiply_convert_fusion.rest_0_), channel_id=1, source_target_pairs={{0,2},{2,4},{4,6},{6,7},{7,5},{5,3},{3,1},{1,0},{8,10},{10,12},{12... | collective-permute-start | bytes 1376264 | tf_op jit(solution)/shard_map/ppermute | solution.py:31
  30.1 24.2 %collective-permute-start.11 = (bf16[128,1792]{1,0:T(8,128)(2,1)}, bf16[128,1792]{1,0:T(8,128)(2,1)}, u32[]{:S(2)}, u32[]{:S(2)}) collective-permute-start(bf16[128,1792]{1,0:T(8,128)(2,1)} %multiply_convert_fusion.rest_0_), channel_id=1, source_target_pairs={{0,1},{2,0},{4,2},{6,4},{7,6},{5,7},{3,5},{1,3},{8,9},{10,8},{12,1... | collective-permute-start | bytes 1376264 | tf_op jit(solution)/shard_map/ppermute | solution.py:31
  41.6 0.8 copy-start.5
  42.3 9.2 %collective-permute-start.6 = (bf16[224,512]{1,0:T(8,128)(2,1)}, bf16[224,512]{1,0:T(8,128)(2,1)}, u32[]{:S(2)}, u32[]{:S(2)}) collective-permute-start(bf16[224,512]{1,0:T(8,128)(2,1)} %get-tuple-element.46), channel_id=1, source_target_pairs={{0,2},{2,4},{4,6},{6,7},{7,5},{5,3},{3,1},{1,0},{8,10},{10,12},{12... | collective-permute-start | bytes 688136 | tf_op jit(solution)/shard_map/ppermute | solution.py:31
  43.9 8.5 %collective-permute-start.7 = (bf16[224,512]{1,0:T(8,128)(2,1)}, bf16[224,512]{1,0:T(8,128)(2,1)}, u32[]{:S(2)}, u32[]{:S(2)}) collective-permute-start(bf16[224,512]{1,0:T(8,128)(2,1)} %get-tuple-element.47), channel_id=1, source_target_pairs={{0,1},{2,0},{4,2},{6,4},{7,6},{5,7},{3,5},{1,3},{8,9},{10,8},{12,1... | collective-permute-start | bytes 688136 | tf_op jit(solution)/shard_map/ppermute | solution.py:31
  44.4 13.8 %collective-permute-start.9 = (s32[8]{0:T(128)S(1)}, s32[8]{0:T(128)S(1)}, u32[]{:S(2)}, u32[]{:S(2)}) collective-permute-start(s32[8]{0:T(128)S(1)} %slice.34), channel_id=1, source_target_pairs={{0,8},{8,16},{16,24},{1,9},{9,17},{17,25},{2,10},{10,18},{18,26},{... | collective-permute-start | bytes 104 | tf_op jit(solution)/shard_map/ppermute | solution.py:317
  46.4 1.0 %copy-start.6 = (bf16[448,512]{1,0:T(8,128)(2,1)S(1)}, bf16[448,512]{1,0:T(8,128)(2,1)}, u32[]{:S(2)}) copy-start(bf16[448,512]{1,0:T(8,128)(2,1)} %copy-done.5) | copy-start | bytes 1376260
  47.4 5.1 %copy-start.2 = (bf16[2,3584,128]{2,1,0:T(8,128)(2,1)S(1)}, bf16[2,3584,128]{2,1,0:T(8,128)(2,1)}, u32[]{:S(2)}) copy-start(bf16[2,3584,128]{2,1,0:T(8,128)(2,1)} %refs_2_.9) | copy-start | bytes 5505028
  49.4 9.1 %copy-start.8 = (f32[4,128]{1,0:T(4,128)S(1)}, f32[4,128]{1,0:T(4,128)}, u32[]{:S(2)}) copy-start(f32[4,128]{1,0:T(4,128)} %taps_x.3) | copy-start | bytes 6148
  49.4 9.1 %copy-start.9 = (f32[4,128]{1,0:T(4,128)S(1)}, f32[4,128]{1,0:T(4,128)}, u32[]{:S(2)}) copy-start(f32[4,128]{1,0:T(4,128)} %taps_bc.3) | copy-start | bytes 6148
  54.3 14.0 %collective-permute-start.12 = (bf16[128,1792]{1,0:T(8,128)(2,1)}, bf16[128,1792]{1,0:T(8,128)(2,1)S(1)}, u32[]{:S(2)}, u32[]{:S(2)}) collective-permute-start(bf16[128,1792]{1,0:T(8,128)(2,1)} %collective-permute-done.10.rest_1_), channel_id=1, source_target_pairs={{0,2},{2,4},{4,6},{6,7},{7,5},{5,3},{3,1},{1,0},{8,10},{10,12},{12... | collective-permute-start | bytes 1376264 | tf_op jit(solution)/shard_map/ppermute | solution.py:31
  55.9 12.4 %collective-permute-start.13 = (bf16[128,1792]{1,0:T(8,128)(2,1)}, bf16[128,1792]{1,0:T(8,128)(2,1)S(1)}, u32[]{:S(2)}, u32[]{:S(2)}) collective-permute-start(bf16[128,1792]{1,0:T(8,128)(2,1)} %collective-permute-done.11.rest_2_), channel_id=1, source_target_pairs={{0,1},{2,0},{4,2},{6,4},{7,6},{5,7},{3,5},{1,3},{8,9},{10,8},{12,1... | collective-permute-start | bytes 1376264 | tf_op jit(solution)/shard_map/ppermute | solution.py:31
  57.0 2.5 %collective-permute-start.8 = (bf16[8,256]{1,0:T(8,128)(2,1)S(1)}, bf16[8,256]{1,0:T(8,128)(2,1)S(1)}, u32[]{:S(2)}, u32[]{:S(2)}) collective-permute-start(bf16[8,256]{1,0:T(8,128)(2,1)S(1)} %slice.46), channel_id=1, source_target_pairs={{0,8},{8,16},{16,24},{1,9},{9,17},{17,25},{2,10},{10,18},{18,26},{... | collective-permute-start | bytes 12296 | tf_op jit(solution)/shard_map/ppermute | solution.py:322
  68.3 17.8 %collective-permute-start.15 = (bf16[128,1792]{1,0:T(8,128)(2,1)S(1)}, bf16[128,1792]{1,0:T(8,128)(2,1)S(1)}, u32[]{:S(2)}, u32[]{:S(2)}) collective-permute-start(bf16[128,1792]{1,0:T(8,128)(2,1)S(1)} %collective-permute-done.12.rest_3_), channel_id=1, source_target_pairs={{0,2},{2,4},{4,6},{6,7},{7,5},{5,3},{3,1},{1,0},{8,10},{10,12},{12... | collective-permute-start | bytes 1376264 | tf_op jit(solution)/shard_map/ppermute | solution.py:31
  69.9 16.2 %collective-permute-start.16 = (bf16[128,1792]{1,0:T(8,128)(2,1)S(1)}, bf16[128,1792]{1,0:T(8,128)(2,1)S(1)}, u32[]{:S(2)}, u32[]{:S(2)}) collective-permute-start(bf16[128,1792]{1,0:T(8,128)(2,1)S(1)} %collective-permute-done.13.rest_4_), channel_id=1, source_target_pairs={{0,1},{2,0},{4,2},{6,4},{7,6},{5,7},{3,5},{1,3},{8,9},{10,8},{12,1... | collective-permute-start | bytes 1376264 | tf_op jit(solution)/shard_map/ppermute | solution.py:31
  86.1 6.4 %collective-permute-start.17 = (bf16[64,1792]{1,0:T(8,128)(2,1)S(1)}, bf16[64,1792]{1,0:T(8,128)(2,1)S(1)}, u32[]{:S(2)}, u32[]{:S(2)}) collective-permute-start(bf16[64,1792]{1,0:T(8,128)(2,1)S(1)} %get-tuple-element.71), channel_id=1, source_target_pairs={{0,2},{2,4},{4,6},{6,7},{7,5},{5,3},{3,1},{1,0},{8,10},{10,12},{12... | collective-permute-start | bytes 688136 | tf_op jit(solution)/shard_map/ppermute | solution.py:31
  87.1 6.2 %collective-permute-start.18 = (bf16[64,1792]{1,0:T(8,128)(2,1)S(1)}, bf16[64,1792]{1,0:T(8,128)(2,1)S(1)}, u32[]{:S(2)}, u32[]{:S(2)}) collective-permute-start(bf16[64,1792]{1,0:T(8,128)(2,1)S(1)} %get-tuple-element.72), channel_id=1, source_target_pairs={{0,1},{2,0},{4,2},{6,4},{7,6},{5,7},{3,5},{1,3},{8,9},{10,8},{12,1... | collective-permute-start | bytes 688136 | tf_op jit(solution)/shard_map/ppermute | solution.py:31
  88.2 1.3 %collective-permute-start.14 = (bf16[8,64,128]{2,1,0:T(8,128)(2,1)S(1)}, bf16[8,64,128]{2,1,0:T(8,128)(2,1)S(1)}, u32[]{:S(2)}, u32[]{:S(2)}) collective-permute-start(bf16[8,64,128]{2,1,0:T(8,128)(2,1)S(1)} %all_to_all.5.mine), channel_id=1, source_target_pairs={{0,8},{8,0},{16,24},{24,16},{1,9},{9,1},{17,25},{25,17},{2,10},{10... | collective-permute-start | bytes 393224 | tf_op jit(solution)/shard_map/ppermute | solution.py:364
  93.6 1.6 %collective-permute-start.19 = (bf16[64,1792]{1,0:T(8,128)(2,1)S(1)}, bf16[64,1792]{1,0:T(8,128)(2,1)S(1)}, u32[]{:S(2)}, u32[]{:S(2)}) collective-permute-start(bf16[64,1792]{1,0:T(8,128)(2,1)S(1)} %get-tuple-element.74), channel_id=1, source_target_pairs={{0,8},{8,0},{16,24},{24,16},{1,9},{9,1},{17,25},{25,17},{2,10},{10... | collective-permute-start | bytes 688136 | tf_op jit(solution)/shard_map/ppermute | solution.py:376

commit v6 on v5

--- a/solution.py
+++ b/solution.py
@@ -14,7 +14,6 @@
 VMEM = pl.BlockSpec(memory_space=pltpu.VMEM)
 ANY = pl.BlockSpec(memory_space=pl.ANY)
 HALO = 8
-W_FIRST = 3
 
 
 def ring_place(index, n):
@@ -35,10 +34,36 @@
     return lax.optimization_barrier((values, earlier))[0]
 
 
-def halves(forth, back, top, bottom):
-    size = top.shape[0]
-    top[...] = forth[:size]
-    bottom[...] = back[size:]
+def far_shift(forth, back):
+    n_seq, n = lax.axis_size("seq"), lax.axis_size("tensor")
+    order = [2 * i if i < n // 2 else 2 * n - 1 - 2 * i for i in range(n)]
+    moves = []
+    for place in range(n_seq):
+        step = 1 - 2 * (place % 2)
+        moves += [(place * n + order[i], place * n + order[(i + step) % n]) for i in range(n)]
+    chosen = call(choose, jax.ShapeDtypeStruct(forth.shape, forth.dtype))(forth, back)
+    return lax.ppermute(chosen, ("seq", "tensor"), moves)
+
+
+def choose(forth, back, out):
+    first = lax.axis_index("seq") % 2 == 0
+
+    @pl.when(first)
+    def _():
+        out[...] = forth[...]
+
+    @pl.when(jnp.logical_not(first))
+    def _():
+        out[...] = back[...]
+
+
+def join(*refs):
+    count = len(refs) // 3
+    odd = lax.axis_index("seq") // 2 % 2
+    for own, other, out in zip(refs[:count], refs[count : 2 * count], refs[2 * count :]):
+        size = own.shape[0]
+        out[pl.ds(pl.multiple_of(odd * size, size), size)] = own[...]
+        out[pl.ds(pl.multiple_of((1 - odd) * size, size), size)] = other[...]
 
 
 def silu(v):
@@ -54,29 +79,34 @@
     return ring_index((ring_place(lax.axis_index("tensor"), n) + distance + n) % n, n)
 
 
-def project(distances, first, *refs):
-    count = len(distances)
+def project(distances, ahead, first, *refs):
+    count, fetched = len(distances), len(distances) + bool(ahead)
     blocks, (w_zx, w_bc, w_dt), refs = refs[:count], refs[count : count + 3], refs[count + 3 :]
-    total, (out, held, sems) = (None, refs) if first else (refs[0], refs[1:])
-    feat = w_bc.shape[0] // lax.axis_size("tensor")
-    width = w_bc.shape[1]
+    total, refs = (None, refs) if first else (refs[0], refs[1:])
+    out, far_out, held, sems = refs if ahead else (refs[0], None, *refs[1:])
+    feat, width = held.shape[1], w_bc.shape[1]
     sources = [w_zx.at[0], w_zx.at[1], w_bc, w_dt]
     copies = []
-    for k, (distance, size, skip) in enumerate(distances):
-        rows = pl.ds(pl.multiple_of(source_of(distance) * feat + skip, 16), size)
+    for k, distance in enumerate([*distances, ahead][:fetched]):
+        rows = pl.ds(pl.multiple_of(source_of(distance) * feat, 16), feat)
         for j, source in enumerate(sources):
+            target = held.at[k] if k < count else far_out
             copies.append(
-                pltpu.make_async_copy(
-                    source.at[rows], held.at[k, pl.ds(0, size), pl.ds(j * width, width)], sems.at[k, j]
-                )
+                pltpu.make_async_copy(source.at[rows], target.at[:, pl.ds(j * width, width)], sems.at[k, j])
             )
             copies[-1].start()
     result = 0.0 if first else total[...]
-    for k, (_, size, _) in enumerate(distances):
+    for k in range(count):
         for j in range(len(sources)):
             copies[k * len(sources) + j].wait()
-        result = result + dot(blocks[k][...], held[k, :size], ((0,), (0,)))
+        result = result + dot(blocks[k][...], held[k], ((0,), (0,)))
     out[...] = result
+    for copy in copies[count * len(sources) :]:
+        copy.wait()
+
+
+def project_far(block, weights, total, out):
+    out[...] = total[...] + dot(block[...], weights[...], ((0,), (0,)))
 
 
 def conv(ext, seg_ext, taps, rows):
@@ -228,10 +258,8 @@
     rest[-1][...] = product((mine, other), distances, rest[:-1])
 
 
-def product_last(distance, mine, other, total, top, bottom, mine_out, other_out, held):
-    held[: top.shape[0]] = top[...]
-    held[top.shape[0] :] = bottom[...]
-    result = product((mine, other), [distance], [held]) + total[...]
+def product_last(distance, mine, other, total, piece, mine_out, other_out):
+    result = product((mine, other), [distance], [piece]) + total[...]
     blocks, rows, width = mine.shape
     for i, (gated, out) in enumerate(((mine, mine_out), (other, other_out))):
         squares = jnp.zeros((rows, width), F32)
@@ -276,51 +304,59 @@
     own = (lax.dynamic_slice_in_dim(w_out, core * columns, columns, 1).astype(F32) * norm_gain[:, None]).astype(BF16)
     last = n_tensor // 2
     w_half = width // 2
-    w_forth = w_back = own
-
-    cut = feat // 32 * 16
+    own_rows = lax.dynamic_slice_in_dim(own, seq_at // 2 % 2 * w_half, w_half, 0)
+    other_y = [(i, i ^ 2) for i in range(n_seq)]
+    shift_rows = [(i, i + 1) for i in range(n_seq - 1)]
+
+    seg_halo = lax.ppermute(segments[tok_rows - HALO :], "seq", shift_rows)
+    seg_all = jnp.concatenate([seg_halo, segments])[:, None]
+    small = (
+        (seg_all[: HALO + rows], seg_all[rows:]),
+        (segments[None, :rows], segments[None, rows:]),
+        (segments[None, :1], segments[None, tok_rows - 1 :]),
+        (spread(dt_bias)[None], spread(a_rate)[None], spread(d_skip)[None]),
+    )
+
     forth = back = block
-    arrived, projs = [(0, block, 0)], []
-    for step in range(1, last + 2):
-        if step <= last:
-            if step > 1:
-                forth, back = after(forth, projs[step - 2]), after(back, projs[step - 2])
-            if step == last:
-                forth, back = call(
-                    halves, [shape(cut, tok_rows, kind=BF16), shape(feat - cut, tok_rows, kind=BF16)]
-                )(forth, back)
-            if step == W_FIRST:
-                w_forth, w_back = after((w_forth, w_back), forth, back)
+    arrived, projs = [(0, block)], []
+    for step in range(1, last + 1):
+        if step == 3:
+            w_arrived, small, forth, back = after((w_arrived, small, forth, back), projs[1])
+        elif step > 1:
+            forth, back = after(forth, projs[step - 2]), after(back, projs[step - 2])
+        if step == 4:
+            w_swapped, forth, back = after((w_swapped, forth, back))
+        if step == 2:
+            w_sent = after(own_rows, forth, back)
+        if step < last:
             forth, back = ring_shift(forth, 1), ring_shift(back, -1)
-            if step == W_FIRST:
-                w_forth, w_back = ring_shift(w_forth, 1), ring_shift(w_back, -1)
-        sizes = [(distance, part.shape[0], skip) for distance, part, skip in arrived]
+        else:
+            far = far_shift(forth, back)
+        if step == 2:
+            w_arrived = ring_shift(w_sent, 1), ring_shift(w_sent, -1)
+        if step == 3:
+            w_swapped = [lax.ppermute(part, "seq", other_y) for part in w_arrived]
+        ahead = last if step == last else 0
         total = projs[-1:]
-        projs.append(
-            call(
-                functools.partial(project, sizes, not total),
-                shape(tok_rows, 4 * width),
-                [
-                    pltpu.VMEM((len(sizes), max(size for _, size, _ in sizes), 4 * width), BF16),
-                    pltpu.SemaphoreType.DMA((len(sizes), 4)),
-                ],
-                in_specs=[VMEM] * len(sizes) + [ANY] * 3 + [VMEM] * len(total),
-                flops=10**9,
-            )(*[part for _, part, _ in arrived], w_zx, w_bc, w_step, *total)
-        )
-        arrived = [(-step, forth, 0), (step, back, 0)]
-        if step == last:
-            arrived = [(last, forth, 0), (last, back, cut)]
-    proj = projs[-1]
-
-    ahead = [(i, i + 1) for i in range(n_seq - 1)]
-    seg_halo = lax.ppermute(segments[tok_rows - HALO :], "seq", ahead)
-    seg_all = jnp.concatenate([seg_halo, segments])[:, None]
-    seg_ext_a, seg_ext_b = seg_all[: HALO + rows], seg_all[rows:]
-    seg_row_a, seg_row_b = segments[None, :rows], segments[None, rows:]
-    seg_first, seg_last = segments[None, :1], segments[None, tok_rows - 1 :]
-    halo = lax.ppermute(proj[tok_rows - HALO :, width : 3 * width].astype(BF16), "seq", ahead)
-    bias, rate, skip = spread(dt_bias)[None], spread(a_rate)[None], spread(d_skip)[None]
+        fetched = len(arrived) + bool(ahead)
+        outs = [shape(tok_rows, 4 * width)] + [shape(feat, 4 * width, kind=BF16)] * bool(ahead)
+        results = call(
+            functools.partial(project, [distance for distance, _ in arrived], ahead, not total),
+            outs,
+            [pltpu.VMEM((len(arrived), feat, 4 * width), BF16), pltpu.SemaphoreType.DMA((fetched, 4))],
+            in_specs=[VMEM] * len(arrived) + [ANY] * 3 + [VMEM] * len(total),
+            flops=10**9,
+        )(*[part for _, part in arrived], w_zx, w_bc, w_step, *total)
+        projs.append(results[0])
+        arrived = [(-step, forth), (step, back)]
+    whole = shape(width, columns, kind=BF16)
+    w_forth, w_back = call(join, [whole, whole])(*w_arrived, *w_swapped)
+    proj = call(project_far, shape(tok_rows, 4 * width), flops=10**9)(
+        far, results[1], after(projs[-1], w_forth, w_back)
+    )
+
+    (seg_ext_a, seg_ext_b), (seg_row_a, seg_row_b), (seg_first, seg_last), (bias, rate, skip) = small
+    halo = lax.ppermute(proj[tok_rows - HALO :, width : 3 * width].astype(BF16), "seq", shift_rows)
 
     msg_rows = state_w + 8
     plane = shape(rows, width)
@@ -353,8 +389,8 @@
         if step == 4:
             w_forth, w_back = after((w_forth, w_back), mine)
         if step == last:
-            half = shape(w_half, columns, kind=BF16)
-            w_forth, w_back = call(halves, [half, half])(w_forth, w_back)
+            w_far = far_shift(w_forth, w_back)
+            break
         w_forth, w_back = ring_shift(w_forth, 1), ring_shift(w_back, -1)
         w_steps.append((w_forth, w_back))
         if step == 2:
@@ -363,7 +399,7 @@
     swap = [(i, i ^ 1) for i in range(n_seq)]
     other = lax.ppermute(mine, "seq", swap)
     pieces, distances = [own], [0]
-    for i, pair in enumerate(w_steps[:-1]):
+    for i, pair in enumerate(w_steps):
         pieces += pair
         distances += [-i - 1, i + 1]
     total = call(functools.partial(product_early, distances), shape(2 * tok_own, columns), flops=10**9)(
@@ -371,8 +407,8 @@
     )
     half = shape(tok_own, columns, kind=BF16)
     out_own, out_other = call(
-        functools.partial(product_last, last), [half, half], [pltpu.VMEM((width, columns), BF16)], flops=10**8
-    )(mine, other, total, *w_steps[-1])
+        functools.partial(product_last, last), [half, half], flops=10**8
+    )(mine, other, total, w_far)
     arrived = lax.ppermute(out_other, "seq", swap)
     is_first = core == 0
     return jnp.concatenate([jnp.where(is_first, out_own, arrived), jnp.where(is_first, arrived, out_own)], 1)

time: 96.5 us -> 96.8 us (level)
  Pallas kernels: 17.3 us -> 15 us
    ppermute x1 -> x5, waiting for transfers between devices: 0.01 us -> 8.08 us  [the longest x2 8.07 us: far_shift(): return lax.ppermute(chosen, ('seq', 'tensor'), moves)]
    ppermute x16 -> x12, waiting for transfers between devices: 23.8 us -> 16.2 us  [ring_shift(): lax.ppermute(block, 'tensor', [(order[i], order[(i + step) % n]) for i in...]
    ppermute x1 -> x5, starting transfers between devices: 1.28 us -> 6.04 us  [the longest x2 2.57 us: far_shift(): return lax.ppermute(chosen, ('seq', 'tensor'), moves)]
    ppermute x16 -> x12, starting transfers between devices: 17.4 us -> 13.2 us  [ring_shift(): lax.ppermute(block, 'tensor', [(order[i], order[(i + step) % n]) for i in...]
    pallas_call x8 -> x9, Pallas kernels: 11.4 us -> 9.19 us  [the longest x4 7.36 us: local(): call(functools.partial(project, [distance for distance, _ in arrived], ah...]
    all_gather x1, blocking collectives: 7.57 us -> 9.03 us  [local(): messages = lax.all_gather(message, 'seq')]
    all_to_all x1, blocking collectives: 14.4 us -> 13.1 us  [local(): mine = lax.all_to_all(blocks, 'tensor', 0, 0)]
    unnamed x32 -> x28, local copies, waits for them, and re-layouts: 5.52 us -> 5.62 us
  transfers between devices with their start and end apart: 20 -> 20, of which waited for: 10 -> 10; matrix products, arithmetic and copies ran while one was open for 4% -> 5% of each run, Pallas kernels for 18% -> 15%
where the time goes in v6:
time: 96.8 us; the launch traced here: 96.2 us
  waiting for transfers between devices  27.1 us (28%)
  blocking collectives  22.1 us (23%)
  starting transfers between devices  20.6 us (21%)
  Pallas kernels  15 us (15%)
  local copies, waits for them, and re-layouts  7.87 us (8%)
  other arithmetic  2.09 us (2%)
  matrix products  1.12 us (1%)
    ppermute x12, waiting for transfers between devices, ring_shift(): lax.ppermute(block, 'tensor', [(order[i], order[(i + step) % n]) for i in...  16.2 us
    ppermute x12, starting transfers between devices, ring_shift(): lax.ppermute(block, 'tensor', [(order[i], order[(i + step) % n]) for i in...  13.2 us
    all_to_all x1, blocking collectives, local(): mine = lax.all_to_all(blocks, 'tensor', 0, 0)  13.1 us
    all_gather x1, blocking collectives, local(): messages = lax.all_gather(message, 'seq')  9.03 us
    ppermute x2, waiting for transfers between devices, far_shift(): return lax.ppermute(chosen, ('seq', 'tensor'), moves)  8.07 us
    pallas_call x4, Pallas kernels, local(): call(functools.partial(project, [distance for distance, _ in arrived], ah...  7.36 us
    unnamed x28, local copies, waits for them, and re-layouts  5.62 us
    ppermute x2, starting transfers between devices, far_shift(): return lax.ppermute(chosen, ('seq', 'tensor'), moves)  2.57 us
  transfers between devices with their start and end apart: 20, of which 10 were waited for; matrix products, arithmetic and copies ran while one was open for 5% of the time, Pallas kernels for 15%

profile of v6, /device:TPU:0, one launch (start us, length us, event | category | flops | bytes accessed | tf_op | source)
XLA Modules:
  0.0 96.2 jit_solution(8736424425214646412)
XLA Ops:
  0.0 3.0 %collective-permute-start = (bf16[448,512]{1,0:T(8,128)(2,1)}, bf16[448,512]{1,0:T(8,128)(2,1)}, u32[]{:S(2)}, u32[]{:S(2)}) collective-permute-start(bf16[448,512]{1,0:T(8,128)(2,1)} %bitcast.13), channel_id=1, source_target_pairs={{0,2},{2,4},{4,6},{6,7},{7,5},{5,3},{3,1},{1,0},{8,10},{10,12},{12... | collective-permute-start | bytes 1376264 | tf_op jit(solution)/shard_map/ppermute | solution.py:30
  3.0 0.8 slice.32
  3.8 1.4 %collective-permute-start.4 = (s32[8]{0:T(128)S(1)}, s32[8]{0:T(128)S(1)}, u32[]{:S(2)}, u32[]{:S(2)}) collective-permute-start(s32[8]{0:T(128)S(1)} %slice.32), channel_id=1, source_target_pairs={{0,8},{8,16},{16,24},{1,9},{9,17},{17,25},{2,10},{10,18},{18,26},{... | collective-permute-start | bytes 104 | tf_op jit(solution)/shard_map/ppermute | solution.py:311
  5.3 1.2 %multiply_convert_fusion.rest_0_ = bf16[128,1792]{1,0:T(8,128)(2,1)S(1)} fusion(f32[128]{0:T(128)} %param.22, bf16[128,3584]{1,0:T(8,128)(2,1)} %param.23, s32[]{:T(128)S(6)} %select_n.35), kind=kLoop, calls=%fused_computation.1 | loop fusion | flops 688128 | bytes 918020 | tf_op jit(solution)/shard_map/convert_element_type | solution.py:304
  6.5 1.1 %convolution_bitcast_fusion.refs_3_.refs_4_ = bf16[3584,128]{1,0:T(8,128)(2,1)S(1)} fusion(bf16[2,128]{1,0:T(2,128)(2,1)} %constant.44.clone, bf16[3584,2]{0,1:T(2,128)(2,1)S(1)} %copy-done), kind=kOutput, calls=%fused_computation | convolution fusion | flops 1835008 | bytes 932352 | tf_op jit(solution)/shard_map/dot_general | solution.py:300
  7.6 0.0 copy-start.2
  7.6 1.2 %copy-done.2 = bf16[3584,128]{1,0:T(8,128)(2,1)S(1)} copy-done((bf16[3584,128]{1,0:T(8,128)(2,1)S(1)}, bf16[3584,128]{1,0:T(8,128)(2,1)}, u32[]{:S(2)}) %copy-start.2) | copy-done | bytes 917528
  8.8 1.0 %copy-done.7 = bf16[512,448]{0,1:T(8,128)(2,1)S(1)} copy-done((bf16[512,448]{0,1:T(8,128)(2,1)S(1)}, bf16[512,448]{0,1:T(8,128)(2,1)}, u32[]{:S(2)}) %copy-start.7) | copy-done | bytes 458776
  9.8 0.6 shard_map.127.refs_5_
  10.5 1.0 %copy-done.5 = f32[512,512]{1,0:T(8,128)} copy-done((f32[512,512]{1,0:T(8,128)}, f32[512,512]{1,0:T(8,128)S(1)}, u32[]{:S(2)}) %copy-start.5) | copy-done | bytes 1048600
  11.5 2.3 %collective-permute-done.refs_0_ = bf16[448,512]{1,0:T(8,128)(2,1)} collective-permute-done((bf16[448,512]{1,0:T(8,128)(2,1)}, bf16[448,512]{1,0:T(8,128)(2,1)}, u32[]{:S(2)}, u32[]{:S(2)}) %collective-permute-start) | collective-permute-done | bytes 458784 | tf_op jit(solution)/shard_map/ppermute | solution.py:30
  13.8 1.5 %collective-permute-done.1.refs_1_ = bf16[448,512]{1,0:T(8,128)(2,1)} collective-permute-done((bf16[448,512]{1,0:T(8,128)(2,1)}, bf16[448,512]{1,0:T(8,128)(2,1)}, u32[]{:S(2)}, u32[]{:S(2)}) %collective-permute-start.1) | collective-permute-done | bytes 458784 | tf_op jit(solution)/shard_map/ppermute | solution.py:30
  15.3 1.6 %collective-permute-start.5 = (bf16[448,512]{1,0:T(8,128)(2,1)}, bf16[448,512]{1,0:T(8,128)(2,1)S(1)}, u32[]{:S(2)}, u32[]{:S(2)}) collective-permute-start(bf16[448,512]{1,0:T(8,128)(2,1)} %collective-permute-done.refs_0_), channel_id=1, source_target_pairs={{0,2},{2,4},{4,6},{6,7},{7,5},{5,3},{3,1},{1,0},{8,10},{10,12},{12... | collective-permute-start | bytes 1376264 | tf_op jit(solution)/shard_map/ppermute | solution.py:30
  16.9 0.4 collective-permute-start.6
  17.4 1.6 %collective-permute-start.2 = (bf16[64,1792]{1,0:T(8,128)(2,1)S(1)}, bf16[64,1792]{1,0:T(8,128)(2,1)S(1)}, u32[]{:S(2)}, u32[]{:S(2)}) collective-permute-start(bf16[64,1792]{1,0:T(8,128)(2,1)S(1)} %constant_dynamic-slice_fusion), channel_id=1, source_target_pairs={{0,2},{2,4},{4,6},{6,7},{7,5},{5,3},{3,1},{1,0},{8,10},{10,12},{12... | collective-permute-start | bytes 688136 | tf_op jit(solution)/shard_map/ppermute | solution.py:30
  18.9 0.4 collective-permute-start.3
  19.4 0.6 fusion
  20.0 0.1 slice.35
  20.1 0.1 broadcast_in_dim.28
  20.2 0.1 broadcast_in_dim_reshape.10.rate
  20.3 0.1 broadcast_in_dim.29
  20.3 0.1 broadcast_in_dim_reshape.11.skip
  20.4 0.1 broadcast_in_dim.27
  20.5 0.1 broadcast_in_dim_reshape.9.bias
  20.6 0.1 pad_add_fusion
  20.7 1.2 %copy-done.3 = bf16[3584,128]{1,0:T(8,128)(2,1)S(1)} copy-done((bf16[3584,128]{1,0:T(8,128)(2,1)S(1)}, bf16[3584,128]{1,0:T(8,128)(2,1)}, u32[]{:S(2)}) %copy-start.3) | copy-done | bytes 917528
  21.9 1.2 %copy-done.6 = f32[512,512]{1,0:T(8,128)S(1)} copy-done((f32[512,512]{1,0:T(8,128)S(1)}, f32[512,512]{1,0:T(8,128)}, u32[]{:S(2)}) %copy-start.6) | copy-done | bytes 1048600
  23.1 3.0 %shard_map.128.refs_5_ = f32[512,512]{1,0:T(8,128)S(1)} custom-call(bf16[448,512]{1,0:T(8,128)(2,1)} %collective-permute-done.refs_0_, bf16[448,512]{1,0:T(8,128)(2,1)} %collective-permute-done.1.refs_1_, bf16[2,3584,128]{2,1,0:T(8,128)(2,1)} %refs_2_.7, bf16[3584,128]{1,0:T(8,128)(2,1)S(1)} %copy-done.3, ...), custom_call_target="tpu_custom_call" | custom-call | flops 1000000000 | bytes 2097152 | tf_op jit(solution)/shard_map/pallas_call | solution.py:343
  26.1 5.5 %collective-permute-done.2.refs_0_ = bf16[64,1792]{1,0:T(8,128)(2,1)S(1)} collective-permute-done((bf16[64,1792]{1,0:T(8,128)(2,1)S(1)}, bf16[64,1792]{1,0:T(8,128)(2,1)S(1)}, u32[]{:S(2)}, u32[]{:S(2)}) %collective-permute-start.2) | collective-permute-done | bytes 229408 | tf_op jit(solution)/shard_map/ppermute | solution.py:30
  31.6 1.3 %collective-permute-done.3.refs_1_ = bf16[64,1792]{1,0:T(8,128)(2,1)S(1)} collective-permute-done((bf16[64,1792]{1,0:T(8,128)(2,1)S(1)}, bf16[64,1792]{1,0:T(8,128)(2,1)S(1)}, u32[]{:S(2)}, u32[]{:S(2)}) %collective-permute-start.3) | collective-permute-done | bytes 229408 | tf_op jit(solution)/shard_map/ppermute | solution.py:30
  32.9 0.5 collective-permute-start.10
  33.4 1.6 %collective-permute-start.9 = (bf16[448,512]{1,0:T(8,128)(2,1)S(1)}, bf16[448,512]{1,0:T(8,128)(2,1)S(1)}, u32[]{:S(2)}, u32[]{:S(2)}) collective-permute-start(bf16[448,512]{1,0:T(8,128)(2,1)S(1)} %collective-permute-done.5.refs_0_), channel_id=1, source_target_pairs={{0,2},{2,4},{4,6},{6,7},{7,5},{5,3},{3,1},{1,0},{8,10},{10,12},{12... | collective-permute-start | bytes 1376264 | tf_op jit(solution)/shard_map/ppermute | solution.py:30
  35.0 1.4 %collective-permute-start.7 = (bf16[64,1792]{1,0:T(8,128)(2,1)S(1)}, bf16[64,1792]{1,0:T(8,128)(2,1)S(1)}, u32[]{:S(2)}, u32[]{:S(2)}) collective-permute-start(bf16[64,1792]{1,0:T(8,128)(2,1)S(1)} %collective-permute-done.2.refs_0_), channel_id=1, source_target_pairs={{0,16},{8,24},{16,0},{24,8},{1,17},{9,25},{17,1},{25,9},{2,18},{10... | collective-permute-start | bytes 688136 | tf_op jit(solution)/shard_map/ppermute | solution.py:338
  36.4 0.6 collective-permute-start.8
  37.0 1.8 %shard_map.129.refs_5_ = f32[512,512]{1,0:T(8,128)S(1)} custom-call(bf16[448,512]{1,0:T(8,128)(2,1)S(1)} %collective-permute-done.5.refs_0_, bf16[448,512]{1,0:T(8,128)(2,1)S(1)} %collective-permute-done.6.refs_1_, bf16[2,3584,128]{2,1,0:T(8,128)(2,1)} %refs_2_.7, bf16[3584,128]{1,0:T(8,128)(2,1)S(1)} %copy-done.3, ...), custom_call_target="tpu_custom_call" | custom-call | flops 1000000000 | bytes 2097152 | tf_op jit(solution)/shard_map/pallas_call | solution.py:343
  38.8 0.0 copy-start.4
  38.8 4.0 %collective-permute-done.10.back.refs_1_ = bf16[448,512]{1,0:T(8,128)(2,1)S(1)} collective-permute-done((bf16[448,512]{1,0:T(8,128)(2,1)S(1)}, bf16[448,512]{1,0:T(8,128)(2,1)S(1)}, u32[]{:S(2)}, u32[]{:S(2)}) %collective-permute-start.10) | collective-permute-done | bytes 458784 | tf_op jit(solution)/shard_map/ppermute | solution.py:30
  42.9 1.5 %collective-permute-done.9.forth.refs_0_ = bf16[448,512]{1,0:T(8,128)(2,1)S(1)} collective-permute-done((bf16[448,512]{1,0:T(8,128)(2,1)S(1)}, bf16[448,512]{1,0:T(8,128)(2,1)S(1)}, u32[]{:S(2)}, u32[]{:S(2)}) %collective-permute-start.9) | collective-permute-done | bytes 458784 | tf_op jit(solution)/shard_map/ppermute | solution.py:30
  44.4 1.6 %collective-permute-start.11 = (bf16[448,512]{1,0:T(8,128)(2,1)S(1)}, bf16[448,512]{1,0:T(8,128)(2,1)S(1)}, u32[]{:S(2)}, u32[]{:S(2)}) collective-permute-start(bf16[448,512]{1,0:T(8,128)(2,1)S(1)} %shard_map.130), channel_id=1, source_target_pairs={{0,2},{2,4},{4,6},{6,7},{7,5},{5,3},{3,1},{1,0},{8,9},{10,8},{12,1... | collective-permute-start | bytes 1376264 | tf_op jit(solution)/shard_map/ppermute | solution.py:45
  46.0 1.0 %shard_map.132 = (bf16[128,1792]{1,0:T(8,128)(2,1)}, bf16[128,1792]{1,0:T(8,128)(2,1)}) custom-call(bf16[64,1792]{1,0:T(8,128)(2,1)S(1)} %collective-permute-done.2.refs_0_, bf16[64,1792]{1,0:T(8,128)(2,1)S(1)} %collective-permute-done.3.refs_1_, bf16[64,1792]{1,0:T(8,128)(2,1)S(1)} %collective-permute-done.7.refs_2_, ...), custom_call_target="tpu_custom_call" | custom-call | flops 10000000 | bytes 2097152 | tf_op jit(solution)/shard_map/pallas_call | solution.py:353
  47.0 1.9 %shard_map.131 = (f32[512,512]{1,0:T(8,128)S(1)}, bf16[448,512]{1,0:T(8,128)(2,1)S(1)}) custom-call(bf16[448,512]{1,0:T(8,128)(2,1)S(1)} %collective-permute-done.9.forth.refs_0_, bf16[448,512]{1,0:T(8,128)(2,1)S(1)} %collective-permute-done.10.back.refs_1_, bf16[2,3584,128]{2,1,0:T(8,128)(2,1)} %refs_2_.7, bf16[3584,128]{1,0:T(8,128)(2,1)S(1)} %copy-done.4, ...), custom_call_target="tpu_custom_call" | custom-call | flops 1000000000 | bytes 2097152 | tf_op jit(solution)/shard_map/pallas_call | solution.py:343
  48.9 4.0 %collective-permute-done.11.block = bf16[448,512]{1,0:T(8,128)(2,1)S(1)} collective-permute-done((bf16[448,512]{1,0:T(8,128)(2,1)S(1)}, bf16[448,512]{1,0:T(8,128)(2,1)S(1)}, u32[]{:S(2)}, u32[]{:S(2)}) %collective-permute-start.11) | collective-permute-done | bytes 458784 | tf_op jit(solution)/shard_map/ppermute | solution.py:45
  53.0 0.5 shard_map.133.proj
  53.4 1.9 %collective-permute-start.13 = (bf16[128,1792]{1,0:T(8,128)(2,1)}, bf16[128,1792]{1,0:T(8,128)(2,1)S(1)}, u32[]{:S(2)}, u32[]{:S(2)}) collective-permute-start(bf16[128,1792]{1,0:T(8,128)(2,1)} %get-tuple-element.96.rest_1_), channel_id=1, source_target_pairs={{0,2},{2,4},{4,6},{6,7},{7,5},{5,3},{3,1},{1,0},{8,10},{10,12},{12... | collective-permute-start | bytes 1376264 | tf_op jit(solution)/shard_map/ppermute | solution.py:30
  55.4 0.1 collective-permute-start.14
  55.5 1.3 %collective-permute-start.12 = (bf16[8,256]{1,0:T(8,128)(2,1)S(1)}, bf16[8,256]{1,0:T(8,128)(2,1)S(1)}, u32[]{:S(2)}, u32[]{:S(2)}) collective-permute-start(bf16[8,256]{1,0:T(8,128)(2,1)S(1)} %slice.44), channel_id=1, source_target_pairs={{0,8},{8,16},{16,24},{1,9},{9,17},{17,25},{2,10},{10,18},{18,26},{... | collective-permute-start | bytes 12296 | tf_op jit(solution)/shard_map/ppermute | solution.py:359
  56.8 0.1 copy.16.seg_ext
  56.9 0.1 copy.17.seg_ext.seg_col
  57.1 1.0 %shard_map.134 = (f32[256,128]{1,0:T(8,128)S(1)}, f32[256,128]{1,0:T(8,128)S(1)}, f32[256,128]{1,0:T(8,128)S(1)}, f32[72,128]{1,0:T(8,128)S(1)}, f32[256,128]{1,0:T(8,128)S(1)}) custom-call(f32[512,512]{1,0:T(8,128)S(1)} %shard_map.133.proj, s32[264,1]{1,0:T(8,128)S(1)} %copy.16.seg_ext, s32[1,256]{1,0:T(1,128)S(1)} %bitcast.17, f32[4,128]{1,0:T(4,128)S(1)} %copy-done.8, ...), custom_call_target="tpu_custom_call" | custom-call | flops 10000000 | bytes 2097152 | tf_op jit(solution)/shard_map/pallas_call | solution.py:364
  58.1 1.3 %shard_map.135 = (f32[256,128]{1,0:T(8,128)S(1)}, f32[256,128]{1,0:T(8,128)S(1)}, f32[256,128]{1,0:T(8,128)S(1)}, f32[256,128]{1,0:T(8,128)S(1)}, f32[256,128]{1...) custom-call(f32[512,512]{1,0:T(8,128)S(1)} %shard_map.133.proj, ...), custom_call_target="tpu_custom_call" | custom-call | flops 10000000 | bytes 2097152 | tf_op jit(solution)/shard_map/pallas_call | solution.py:369
  59.4 9.0 %all-gather = f32[288,128]{1,0:T(8,128)S(1)} all-gather(f32[72,128]{1,0:T(8,128)S(1)} %get-tuple-element.82), channel_id=2, replica_groups=mesh['seq'=4,'tensor'=8] {'seq'}, dimensions={0}, use_global_device_ids=true | all-gather | bytes 184320 | tf_op jit(solution)/shard_map/all_gather | solution.py:374
  68.4 1.6 %collective-permute-start.16 = (bf16[128,1792]{1,0:T(8,128)(2,1)S(1)}, bf16[128,1792]{1,0:T(8,128)(2,1)S(1)}, u32[]{:S(2)}, u32[]{:S(2)}) collective-permute-start(bf16[128,1792]{1,0:T(8,128)(2,1)S(1)} %collective-permute-done.13.rest_3_), channel_id=1, source_target_pairs={{0,2},{2,4},{4,6},{6,7},{7,5},{5,3},{3,1},{1,0},{8,10},{10,12},{12... | collective-permute-start | bytes 1376264 | tf_op jit(solution)/shard_map/ppermute | solution.py:30
  70.0 0.5 collective-permute-start.17
  70.5 0.4 shard_map.136
  70.9 1.0 shard_map.137
  71.9 13.1 %all_to_all.5.mine = bf16[8,64,128]{2,1,0:T(8,128)(2,1)S(1)} all-to-all(bf16[8,64,128]{2,1,0:T(8,128)(2,1)S(1)} %bitcast.12), channel_id=1, replica_groups=mesh['seq'=4,'tensor'=8] {'tensor'}, dimensions={0} | all-to-all | bytes 262144 | tf_op jit(solution)/shard_map/all_to_all | solution.py:398
  85.0 1.0 %collective-permute-start.18 = (bf16[128,1792]{1,0:T(8,128)(2,1)S(1)}, bf16[128,1792]{1,0:T(8,128)(2,1)S(1)}, u32[]{:S(2)}, u32[]{:S(2)}) collective-permute-start(bf16[128,1792]{1,0:T(8,128)(2,1)S(1)} %shard_map.139), channel_id=1, source_target_pairs={{0,2},{2,4},{4,6},{6,7},{7,5},{5,3},{3,1},{1,0},{8,9},{10,8},{12,1... | collective-permute-start | bytes 1376264 | tf_op jit(solution)/shard_map/ppermute | solution.py:45
  86.0 1.3 %collective-permute-done.15.other = bf16[8,64,128]{2,1,0:T(8,128)(2,1)S(1)} collective-permute-done((bf16[8,64,128]{2,1,0:T(8,128)(2,1)S(1)}, bf16[8,64,128]{2,1,0:T(8,128)(2,1)S(1)}, u32[]{:S(2)}, u32[]{:S(2)}) %collective-permute-start.15) | collective-permute-done | bytes 131104 | tf_op jit(solution)/shard_map/ppermute | solution.py:400
  87.3 2.1 %shard_map.138.total = f32[128,1792]{1,0:T(8,128)S(1)} custom-call(bf16[8,64,128]{2,1,0:T(8,128)(2,1)S(1)} %all_to_all.5.mine, bf16[8,64,128]{2,1,0:T(8,128)(2,1)S(1)} %collective-permute-done.15.other, bf16[128,1792]{1,0:T(8,128)(2,1)S(1)} %multiply_convert_fusion.rest_0_, bf16[128,1792]{1,0:T(8,128)(2,1)} %get-tuple-element.96.rest_1_, ...), custom_call_target="tpu_custom_call" | custom-call | flops 1000000000 | bytes 2097152 | tf_op jit(solution)/shard_map/pallas_call | solution.py:405
  89.5 4.1 %collective-permute-done.18.piece = bf16[128,1792]{1,0:T(8,128)(2,1)S(1)} collective-permute-done((bf16[128,1792]{1,0:T(8,128)(2,1)S(1)}, bf16[128,1792]{1,0:T(8,128)(2,1)S(1)}, u32[]{:S(2)}, u32[]{:S(2)}) %collective-permute-start.18) | collective-permute-done | bytes 458784 | tf_op jit(solution)/shard_map/ppermute | solution.py:45
  93.5 0.3 shard_map.140
  93.8 0.1 collective-permute-start.19
  93.9 1.5 %collective-permute-done.19 = bf16[64,1792]{1,0:T(8,128)(2,1)S(1)} collective-permute-done((bf16[64,1792]{1,0:T(8,128)(2,1)S(1)}, bf16[64,1792]{1,0:T(8,128)(2,1)S(1)}, u32[]{:S(2)}, u32[]{:S(2)}) %collective-permute-start.19) | collective-permute-done | bytes 229408 | tf_op jit(solution)/shard_map/ppermute | solution.py:412
  95.4 0.8 pad_maximum_fusion
  (42 shorter events, 0.2 us)
Async XLA Ops:
  0.0 6.5 %copy-start = (bf16[3584,2]{0,1:T(2,128)(2,1)S(1)}, bf16[3584,2]{0,1:T(2,128)(2,1)}, u32[]{:S(2)}) copy-start(bf16[3584,2]{0,1:T(2,128)(2,1)} %param.16) | copy-start | bytes 43012
  0.0 7.6 %copy-start.1 = (bf16[2,3584,128]{2,1,0:T(8,128)(2,1)S(1)}, bf16[2,3584,128]{2,1,0:T(8,128)(2,1)}, u32[]{:S(2)}) copy-start(bf16[2,3584,128]{2,1,0:T(8,128)(2,1)} %refs_2_.7) | copy-start | bytes 5505028
  0.0 13.8 %collective-permute-start = (bf16[448,512]{1,0:T(8,128)(2,1)}, bf16[448,512]{1,0:T(8,128)(2,1)}, u32[]{:S(2)}, u32[]{:S(2)}) collective-permute-start(bf16[448,512]{1,0:T(8,128)(2,1)} %bitcast.13), channel_id=1, source_target_pairs={{0,2},{2,4},{4,6},{6,7},{7,5},{5,3},{3,1},{1,0},{8,10},{10,12},{12... | collective-permute-start | bytes 1376264 | tf_op jit(solution)/shard_map/ppermute | solution.py:30
  3.0 12.3 %collective-permute-start.1 = (bf16[448,512]{1,0:T(8,128)(2,1)}, bf16[448,512]{1,0:T(8,128)(2,1)}, u32[]{:S(2)}, u32[]{:S(2)}) collective-permute-start(bf16[448,512]{1,0:T(8,128)(2,1)} %bitcast.14), channel_id=1, source_target_pairs={{0,1},{2,0},{4,2},{6,4},{7,6},{5,7},{3,5},{1,3},{8,9},{10,8},{12,1... | collective-permute-start | bytes 1376264 | tf_op jit(solution)/shard_map/ppermute | solution.py:30
  3.8 16.8 %collective-permute-start.4 = (s32[8]{0:T(128)S(1)}, s32[8]{0:T(128)S(1)}, u32[]{:S(2)}, u32[]{:S(2)}) collective-permute-start(s32[8]{0:T(128)S(1)} %slice.32), channel_id=1, source_target_pairs={{0,8},{8,16},{16,24},{1,9},{9,17},{17,25},{2,10},{10,18},{18,26},{... | collective-permute-start | bytes 104 | tf_op jit(solution)/shard_map/ppermute | solution.py:311
  7.6 1.2 %copy-start.2 = (bf16[3584,128]{1,0:T(8,128)(2,1)S(1)}, bf16[3584,128]{1,0:T(8,128)(2,1)}, u32[]{:S(2)}) copy-start(bf16[3584,128]{1,0:T(8,128)(2,1)} %refs_3_.5) | copy-start | bytes 2752516
  8.8 1.0 %copy-start.7 = (bf16[512,448]{0,1:T(8,128)(2,1)S(1)}, bf16[512,448]{0,1:T(8,128)(2,1)}, u32[]{:S(2)}) copy-start(bf16[512,448]{0,1:T(8,128)(2,1)} %param.13) | copy-start | bytes 1376260
  9.8 7.5 %copy-start.10 = (s32[512]{0:T(512)S(1)}, s32[512]{0:T(512)}, u32[]{:S(2)}) copy-start(s32[512]{0:T(512)} %param.24) | copy-start | bytes 6148
  9.8 10.3 %copy-start.11 = (f32[2]{0:T(128)S(1)}, f32[2]{0:T(128)}, u32[]{:S(2)}) copy-start(f32[2]{0:T(128)} %param.18) | copy-start | bytes 28
  9.8 10.4 %copy-start.12 = (f32[2]{0:T(128)S(1)}, f32[2]{0:T(128)}, u32[]{:S(2)}) copy-start(f32[2]{0:T(128)} %param.19) | copy-start | bytes 28
  9.8 10.6 %copy-start.13 = (f32[2]{0:T(128)S(1)}, f32[2]{0:T(128)}, u32[]{:S(2)}) copy-start(f32[2]{0:T(128)} %param.17) | copy-start | bytes 28
  10.5 1.0 %copy-start.5 = (f32[512,512]{1,0:T(8,128)}, f32[512,512]{1,0:T(8,128)S(1)}, u32[]{:S(2)}) copy-start(f32[512,512]{1,0:T(8,128)S(1)} %shard_map.127.refs_5_) | copy-start | bytes 3145732
  15.3 17.6 %collective-permute-start.5 = (bf16[448,512]{1,0:T(8,128)(2,1)}, bf16[448,512]{1,0:T(8,128)(2,1)S(1)}, u32[]{:S(2)}, u32[]{:S(2)}) collective-permute-start(bf16[448,512]{1,0:T(8,128)(2,1)} %collective-permute-done.refs_0_), channel_id=1, source_target_pairs={{0,2},{2,4},{4,6},{6,7},{7,5},{5,3},{3,1},{1,0},{8,10},{10,12},{12... | collective-permute-start | bytes 1376264 | tf_op jit(solution)/shard_map/ppermute | solution.py:30
  16.9 16.0 %collective-permute-start.6 = (bf16[448,512]{1,0:T(8,128)(2,1)}, bf16[448,512]{1,0:T(8,128)(2,1)S(1)}, u32[]{:S(2)}, u32[]{:S(2)}) collective-permute-start(bf16[448,512]{1,0:T(8,128)(2,1)} %collective-permute-done.1.refs_1_), channel_id=1, source_target_pairs={{0,1},{2,0},{4,2},{6,4},{7,6},{5,7},{3,5},{1,3},{8,9},{10,8},{12,1... | collective-permute-start | bytes 1376264 | tf_op jit(solution)/shard_map/ppermute | solution.py:30
  17.4 14.3 %collective-permute-start.2 = (bf16[64,1792]{1,0:T(8,128)(2,1)S(1)}, bf16[64,1792]{1,0:T(8,128)(2,1)S(1)}, u32[]{:S(2)}, u32[]{:S(2)}) collective-permute-start(bf16[64,1792]{1,0:T(8,128)(2,1)S(1)} %constant_dynamic-slice_fusion), channel_id=1, source_target_pairs={{0,2},{2,4},{4,6},{6,7},{7,5},{5,3},{3,1},{1,0},{8,10},{10,12},{12... | collective-permute-start | bytes 688136 | tf_op jit(solution)/shard_map/ppermute | solution.py:30
  18.9 14.0 %collective-permute-start.3 = (bf16[64,1792]{1,0:T(8,128)(2,1)S(1)}, bf16[64,1792]{1,0:T(8,128)(2,1)S(1)}, u32[]{:S(2)}, u32[]{:S(2)}) collective-permute-start(bf16[64,1792]{1,0:T(8,128)(2,1)S(1)} %constant_dynamic-slice_fusion), channel_id=1, source_target_pairs={{0,1},{2,0},{4,2},{6,4},{7,6},{5,7},{3,5},{1,3},{8,9},{10,8},{12,1... | collective-permute-start | bytes 688136 | tf_op jit(solution)/shard_map/ppermute | solution.py:30
  20.7 1.2 %copy-start.3 = (bf16[3584,128]{1,0:T(8,128)(2,1)S(1)}, bf16[3584,128]{1,0:T(8,128)(2,1)}, u32[]{:S(2)}) copy-start(bf16[3584,128]{1,0:T(8,128)(2,1)} %refs_3_.5) | copy-start | bytes 2752516
  21.9 1.2 %copy-start.6 = (f32[512,512]{1,0:T(8,128)S(1)}, f32[512,512]{1,0:T(8,128)}, u32[]{:S(2)}) copy-start(f32[512,512]{1,0:T(8,128)} %copy-done.5) | copy-start | bytes 3145732
  32.9 10.0 %collective-permute-start.10 = (bf16[448,512]{1,0:T(8,128)(2,1)S(1)}, bf16[448,512]{1,0:T(8,128)(2,1)S(1)}, u32[]{:S(2)}, u32[]{:S(2)}) collective-permute-start(bf16[448,512]{1,0:T(8,128)(2,1)S(1)} %collective-permute-done.6.refs_1_), channel_id=1, source_target_pairs={{0,1},{2,0},{4,2},{6,4},{7,6},{5,7},{3,5},{1,3},{8,9},{10,8},{12,1... | collective-permute-start | bytes 1376264 | tf_op jit(solution)/shard_map/ppermute | solution.py:30
  33.4 11.0 %collective-permute-start.9 = (bf16[448,512]{1,0:T(8,128)(2,1)S(1)}, bf16[448,512]{1,0:T(8,128)(2,1)S(1)}, u32[]{:S(2)}, u32[]{:S(2)}) collective-permute-start(bf16[448,512]{1,0:T(8,128)(2,1)S(1)} %collective-permute-done.5.refs_0_), channel_id=1, source_target_pairs={{0,2},{2,4},{4,6},{6,7},{7,5},{5,3},{3,1},{1,0},{8,10},{10,12},{12... | collective-permute-start | bytes 1376264 | tf_op jit(solution)/shard_map/ppermute | solution.py:30
  35.0 9.4 %collective-permute-start.7 = (bf16[64,1792]{1,0:T(8,128)(2,1)S(1)}, bf16[64,1792]{1,0:T(8,128)(2,1)S(1)}, u32[]{:S(2)}, u32[]{:S(2)}) collective-permute-start(bf16[64,1792]{1,0:T(8,128)(2,1)S(1)} %collective-permute-done.2.refs_0_), channel_id=1, source_target_pairs={{0,16},{8,24},{16,0},{24,8},{1,17},{9,25},{17,1},{25,9},{2,18},{10... | collective-permute-start | bytes 688136 | tf_op jit(solution)/shard_map/ppermute | solution.py:338
  36.4 8.0 %collective-permute-start.8 = (bf16[64,1792]{1,0:T(8,128)(2,1)S(1)}, bf16[64,1792]{1,0:T(8,128)(2,1)S(1)}, u32[]{:S(2)}, u32[]{:S(2)}) collective-permute-start(bf16[64,1792]{1,0:T(8,128)(2,1)S(1)} %collective-permute-done.3.refs_1_), channel_id=1, source_target_pairs={{0,16},{8,24},{16,0},{24,8},{1,17},{9,25},{17,1},{25,9},{2,18},{10... | collective-permute-start | bytes 688136 | tf_op jit(solution)/shard_map/ppermute | solution.py:338
  38.8 8.2 %copy-start.4 = (bf16[3584,128]{1,0:T(8,128)(2,1)S(1)}, bf16[3584,128]{1,0:T(8,128)(2,1)}, u32[]{:S(2)}) copy-start(bf16[3584,128]{1,0:T(8,128)(2,1)} %refs_3_.5) | copy-start | bytes 2752516
  44.4 8.5 %collective-permute-start.11 = (bf16[448,512]{1,0:T(8,128)(2,1)S(1)}, bf16[448,512]{1,0:T(8,128)(2,1)S(1)}, u32[]{:S(2)}, u32[]{:S(2)}) collective-permute-start(bf16[448,512]{1,0:T(8,128)(2,1)S(1)} %shard_map.130), channel_id=1, source_target_pairs={{0,2},{2,4},{4,6},{6,7},{7,5},{5,3},{3,1},{1,0},{8,9},{10,8},{12,1... | collective-permute-start | bytes 1376264 | tf_op jit(solution)/shard_map/ppermute | solution.py:45
  53.0 4.1 %copy-start.8 = (f32[4,128]{1,0:T(4,128)S(1)}, f32[4,128]{1,0:T(4,128)}, u32[]{:S(2)}) copy-start(f32[4,128]{1,0:T(4,128)} %taps_x.3) | copy-start | bytes 6148
  53.0 4.1 %copy-start.9 = (f32[4,128]{1,0:T(4,128)S(1)}, f32[4,128]{1,0:T(4,128)}, u32[]{:S(2)}) copy-start(f32[4,128]{1,0:T(4,128)} %taps_bc.3) | copy-start | bytes 6148
  53.4 15.0 %collective-permute-start.13 = (bf16[128,1792]{1,0:T(8,128)(2,1)}, bf16[128,1792]{1,0:T(8,128)(2,1)S(1)}, u32[]{:S(2)}, u32[]{:S(2)}) collective-permute-start(bf16[128,1792]{1,0:T(8,128)(2,1)} %get-tuple-element.96.rest_1_), channel_id=1, source_target_pairs={{0,2},{2,4},{4,6},{6,7},{7,5},{5,3},{3,1},{1,0},{8,10},{10,12},{12... | collective-permute-start | bytes 1376264 | tf_op jit(solution)/shard_map/ppermute | solution.py:30
  55.4 13.0 %collective-permute-start.14 = (bf16[128,1792]{1,0:T(8,128)(2,1)}, bf16[128,1792]{1,0:T(8,128)(2,1)S(1)}, u32[]{:S(2)}, u32[]{:S(2)}) collective-permute-start(bf16[128,1792]{1,0:T(8,128)(2,1)} %get-tuple-element.97.rest_2_), channel_id=1, source_target_pairs={{0,1},{2,0},{4,2},{6,4},{7,6},{5,7},{3,5},{1,3},{8,9},{10,8},{12,1... | collective-permute-start | bytes 1376264 | tf_op jit(solution)/shard_map/ppermute | solution.py:30
  55.5 2.6 %collective-permute-start.12 = (bf16[8,256]{1,0:T(8,128)(2,1)S(1)}, bf16[8,256]{1,0:T(8,128)(2,1)S(1)}, u32[]{:S(2)}, u32[]{:S(2)}) collective-permute-start(bf16[8,256]{1,0:T(8,128)(2,1)S(1)} %slice.44), channel_id=1, source_target_pairs={{0,8},{8,16},{16,24},{1,9},{9,17},{17,25},{2,10},{10,18},{18,26},{... | collective-permute-start | bytes 12296 | tf_op jit(solution)/shard_map/ppermute | solution.py:359
  68.4 16.5 %collective-permute-start.16 = (bf16[128,1792]{1,0:T(8,128)(2,1)S(1)}, bf16[128,1792]{1,0:T(8,128)(2,1)S(1)}, u32[]{:S(2)}, u32[]{:S(2)}) collective-permute-start(bf16[128,1792]{1,0:T(8,128)(2,1)S(1)} %collective-permute-done.13.rest_3_), channel_id=1, source_target_pairs={{0,2},{2,4},{4,6},{6,7},{7,5},{5,3},{3,1},{1,0},{8,10},{10,12},{12... | collective-permute-start | bytes 1376264 | tf_op jit(solution)/shard_map/ppermute | solution.py:30
  70.0 15.0 %collective-permute-start.17 = (bf16[128,1792]{1,0:T(8,128)(2,1)S(1)}, bf16[128,1792]{1,0:T(8,128)(2,1)S(1)}, u32[]{:S(2)}, u32[]{:S(2)}) collective-permute-start(bf16[128,1792]{1,0:T(8,128)(2,1)S(1)} %collective-permute-done.14.rest_4_), channel_id=1, source_target_pairs={{0,1},{2,0},{4,2},{6,4},{7,6},{5,7},{3,5},{1,3},{8,9},{10,8},{12,1... | collective-permute-start | bytes 1376264 | tf_op jit(solution)/shard_map/ppermute | solution.py:30
  85.0 8.5 %collective-permute-start.18 = (bf16[128,1792]{1,0:T(8,128)(2,1)S(1)}, bf16[128,1792]{1,0:T(8,128)(2,1)S(1)}, u32[]{:S(2)}, u32[]{:S(2)}) collective-permute-start(bf16[128,1792]{1,0:T(8,128)(2,1)S(1)} %shard_map.139), channel_id=1, source_target_pairs={{0,2},{2,4},{4,6},{6,7},{7,5},{5,3},{3,1},{1,0},{8,9},{10,8},{12,1... | collective-permute-start | bytes 1376264 | tf_op jit(solution)/shard_map/ppermute | solution.py:45
  86.0 1.3 %collective-permute-start.15 = (bf16[8,64,128]{2,1,0:T(8,128)(2,1)S(1)}, bf16[8,64,128]{2,1,0:T(8,128)(2,1)S(1)}, u32[]{:S(2)}, u32[]{:S(2)}) collective-permute-start(bf16[8,64,128]{2,1,0:T(8,128)(2,1)S(1)} %all_to_all.5.mine), channel_id=1, source_target_pairs={{0,8},{8,0},{16,24},{24,16},{1,9},{9,1},{17,25},{25,17},{2,10},{10... | collective-permute-start | bytes 393224 | tf_op jit(solution)/shard_map/ppermute | solution.py:400
  93.8 1.6 %collective-permute-start.19 = (bf16[64,1792]{1,0:T(8,128)(2,1)S(1)}, bf16[64,1792]{1,0:T(8,128)(2,1)S(1)}, u32[]{:S(2)}, u32[]{:S(2)}) collective-permute-start(bf16[64,1792]{1,0:T(8,128)(2,1)S(1)} %get-tuple-element.104), channel_id=1, source_target_pairs={{0,8},{8,0},{16,24},{24,16},{1,9},{9,1},{17,25},{25,17},{2,10},{10... | collective-permute-start | bytes 688136 | tf_op jit(solution)/shard_map/ppermute | solution.py:412

commit v7 on v6

--- a/solution.py
+++ b/solution.py
@@ -35,26 +35,16 @@
 
 
 def far_shift(forth, back):
-    n_seq, n = lax.axis_size("seq"), lax.axis_size("tensor")
-    order = [2 * i if i < n // 2 else 2 * n - 1 - 2 * i for i in range(n)]
-    moves = []
-    for place in range(n_seq):
-        step = 1 - 2 * (place % 2)
-        moves += [(place * n + order[i], place * n + order[(i + step) % n]) for i in range(n)]
-    chosen = call(choose, jax.ShapeDtypeStruct(forth.shape, forth.dtype))(forth, back)
-    return lax.ppermute(chosen, ("seq", "tensor"), moves)
-
-
-def choose(forth, back, out):
-    first = lax.axis_index("seq") % 2 == 0
-
-    @pl.when(first)
-    def _():
-        out[...] = forth[...]
-
-    @pl.when(jnp.logical_not(first))
-    def _():
-        out[...] = back[...]
+    cut = forth.shape[0] // 32 * 16
+    parts = [jax.ShapeDtypeStruct((size, forth.shape[1]), forth.dtype) for size in (cut, forth.shape[0] - cut)]
+    top, bottom = call(halves, parts)(forth, back)
+    return ring_shift(top, 1), ring_shift(bottom, -1)
+
+
+def halves(forth, back, top, bottom):
+    size = top.shape[0]
+    top[...] = forth[:size]
+    bottom[...] = back[size:]
 
 
 def join(*refs):
@@ -105,8 +95,11 @@
         copy.wait()
 
 
-def project_far(block, weights, total, out):
-    out[...] = total[...] + dot(block[...], weights[...], ((0,), (0,)))
+def project_far(top, bottom, weights, total, out):
+    cut = top.shape[0]
+    out[...] = (
+        total[...] + dot(top[...], weights[:cut], ((0,), (0,))) + dot(bottom[...], weights[cut:], ((0,), (0,)))
+    )
 
 
 def conv(ext, seg_ext, taps, rows):
@@ -258,8 +251,10 @@
     rest[-1][...] = product((mine, other), distances, rest[:-1])
 
 
-def product_last(distance, mine, other, total, piece, mine_out, other_out):
-    result = product((mine, other), [distance], [piece]) + total[...]
+def product_last(distance, mine, other, total, top, bottom, mine_out, other_out, held):
+    held[: top.shape[0]] = top[...]
+    held[top.shape[0] :] = bottom[...]
+    result = product((mine, other), [distance], [held]) + total[...]
     blocks, rows, width = mine.shape
     for i, (gated, out) in enumerate(((mine, mine_out), (other, other_out))):
         squares = jnp.zeros((rows, width), F32)
@@ -321,7 +316,8 @@
     arrived, projs = [(0, block)], []
     for step in range(1, last + 1):
         if step == 3:
-            w_arrived, small, forth, back = after((w_arrived, small, forth, back), projs[1])
+            forth, back = after(forth, projs[1], small), after(back, projs[1], small)
+            w_arrived = after(w_arrived, forth, back)
         elif step > 1:
             forth, back = after(forth, projs[step - 2]), after(back, projs[step - 2])
         if step == 4:
@@ -352,7 +348,7 @@
     whole = shape(width, columns, kind=BF16)
     w_forth, w_back = call(join, [whole, whole])(*w_arrived, *w_swapped)
     proj = call(project_far, shape(tok_rows, 4 * width), flops=10**9)(
-        far, results[1], after(projs[-1], w_forth, w_back)
+        *far, results[1], after(projs[-1], w_forth, w_back)
     )
 
     (seg_ext_a, seg_ext_b), (seg_row_a, seg_row_b), (seg_first, seg_last), (bias, rate, skip) = small
@@ -382,7 +378,7 @@
     tok_own = tok_rows // n_tensor
 
     w_steps = [(w_forth, w_back)]
-    orders = [proj, messages]
+    orders = [(proj, halo), messages]
     for step in range(2, last + 1):
         if step - 2 < len(orders):
             w_forth, w_back = after((w_forth, w_back), orders[step - 2])
@@ -407,8 +403,8 @@
     )
     half = shape(tok_own, columns, kind=BF16)
     out_own, out_other = call(
-        functools.partial(product_last, last), [half, half], flops=10**8
-    )(mine, other, total, w_far)
+        functools.partial(product_last, last), [half, half], [pltpu.VMEM((width, columns), BF16)], flops=10**8
+    )(mine, other, total, *w_far)
     arrived = lax.ppermute(out_other, "seq", swap)
     is_first = core == 0
     return jnp.concatenate([jnp.where(is_first, out_own, arrived), jnp.where(is_first, arrived, out_own)], 1)

time: 96.8 us -> 97.1 us (level)
  starting transfers between devices: 20.6 us -> 22.3 us
  other arithmetic: 2.09 us -> 1.05 us
  Pallas kernels: 15 us -> 16 us
    ppermute x2 -> x0, waiting for transfers between devices: 8.07 us -> none  [far_shift(): return lax.ppermute(chosen, ('seq', 'tensor'), moves)]
    ppermute x12 -> x16, waiting for transfers between devices: 16.2 us -> 21.6 us  [ring_shift(): lax.ppermute(block, 'tensor', [(order[i], order[(i + step) % n]) for i in...]
    ppermute x12 -> x16, starting transfers between devices: 13.2 us -> 17.5 us  [ring_shift(): lax.ppermute(block, 'tensor', [(order[i], order[(i + step) % n]) for i in...]
    ppermute x2 -> x0, starting transfers between devices: 2.57 us -> none  [far_shift(): return lax.ppermute(chosen, ('seq', 'tensor'), moves)]
    all_gather x1, blocking collectives: 9.03 us -> 6.83 us  [local(): messages = lax.all_gather(message, 'seq')]
    ppermute x2, waiting for transfers between devices: 0.01 us -> 2.13 us  [local(): w_swapped = [lax.ppermute(part, 'seq', other_y) for part in w_arrived]]
    unnamed x28 -> x26, local copies, waits for them, and re-layouts: 5.62 us -> 4.25 us
    all_to_all x1, blocking collectives: 13.1 us -> 14.3 us  [local(): mine = lax.all_to_all(blocks, 'tensor', 0, 0)]
  transfers between devices with their start and end apart: 20 -> 22, of which waited for: 10 -> 16; matrix products, arithmetic and copies ran while one was open for 5% -> 4% of each run, Pallas kernels for 15% -> 16%
where the time goes in v7:
time: 97.1 us; the launch traced here: 96.5 us
  waiting for transfers between devices  27.4 us (28%)
  starting transfers between devices  22.3 us (23%)
  blocking collectives  21.2 us (22%)
  Pallas kernels  16 us (16%)
  local copies, waits for them, and re-layouts  7.19 us (7%)
  matrix products  1.11 us (1%)
  other arithmetic  1.05 us (1%)
    ppermute x16, waiting for transfers between devices, ring_shift(): lax.ppermute(block, 'tensor', [(order[i], order[(i + step) % n]) for i in...  21.6 us
    ppermute x16, starting transfers between devices, ring_shift(): lax.ppermute(block, 'tensor', [(order[i], order[(i + step) % n]) for i in...  17.5 us
    all_to_all x1, blocking collectives, local(): mine = lax.all_to_all(blocks, 'tensor', 0, 0)  14.3 us
    pallas_call x4, Pallas kernels, local(): call(functools.partial(project, [distance for distance, _ in arrived], ah...  8.53 us
    all_gather x1, blocking collectives, local(): messages = lax.all_gather(message, 'seq')  6.83 us
    unnamed x26, local copies, waits for them, and re-layouts  4.25 us
    pallas_call x1, Pallas kernels, local(): call(functools.partial(product_early, distances), shape(2 * tok_own, colu...  2.14 us
    ppermute x2, waiting for transfers between devices, local(): w_swapped = [lax.ppermute(part, 'seq', other_y) for part in w_arrived]  2.13 us
  transfers between devices with their start and end apart: 22, of which 16 were waited for; matrix products, arithmetic and copies ran while one was open for 4% of the time, Pallas kernels for 16%

profile of v7, /device:TPU:0, one launch (start us, length us, event | category | flops | bytes accessed | tf_op | source)
XLA Modules:
  0.0 96.5 jit_solution(2170640030068422888)
XLA Ops:
  0.0 3.0 %collective-permute-start = (bf16[448,512]{1,0:T(8,128)(2,1)}, bf16[448,512]{1,0:T(8,128)(2,1)}, u32[]{:S(2)}, u32[]{:S(2)}) collective-permute-start(bf16[448,512]{1,0:T(8,128)(2,1)} %bitcast.13), channel_id=1, source_target_pairs={{0,2},{2,4},{4,6},{6,7},{7,5},{5,3},{3,1},{1,0},{8,10},{10,12},{12... | collective-permute-start | bytes 1376264 | tf_op jit(solution)/shard_map/ppermute | solution.py:30
  3.0 0.8 slice.33
  3.8 1.4 %collective-permute-start.5 = (s32[8]{0:T(128)S(1)}, s32[8]{0:T(128)S(1)}, u32[]{:S(2)}, u32[]{:S(2)}) collective-permute-start(s32[8]{0:T(128)S(1)} %slice.33), channel_id=1, source_target_pairs={{0,8},{8,16},{16,24},{1,9},{9,17},{17,25},{2,10},{10,18},{18,26},{... | collective-permute-start | bytes 104 | tf_op jit(solution)/shard_map/ppermute | solution.py:306
  5.2 0.8 fusion.1
  6.0 1.1 %convolution_bitcast_fusion.refs_3_.refs_4_ = bf16[3584,128]{1,0:T(8,128)(2,1)S(1)} fusion(bf16[2,128]{1,0:T(2,128)(2,1)} %constant.44.clone, bf16[3584,2]{0,1:T(2,128)(2,1)S(1)} %copy-done), kind=kOutput, calls=%fused_computation | convolution fusion | flops 1835008 | bytes 932352 | tf_op jit(solution)/shard_map/dot_general | solution.py:295
  7.1 1.5 %copy-done.1 = bf16[2,3584,128]{2,1,0:T(8,128)(2,1)S(1)} copy-done((bf16[2,3584,128]{2,1,0:T(8,128)(2,1)S(1)}, bf16[2,3584,128]{2,1,0:T(8,128)(2,1)}, u32[]{:S(2)}) %copy-start.1) | copy-done | bytes 1835032
  8.6 1.2 %copy-done.2 = bf16[3584,128]{1,0:T(8,128)(2,1)S(1)} copy-done((bf16[3584,128]{1,0:T(8,128)(2,1)S(1)}, bf16[3584,128]{1,0:T(8,128)(2,1)}, u32[]{:S(2)}) %copy-start.2) | copy-done | bytes 917528
  9.8 1.0 %copy-done.4 = bf16[512,448]{0,1:T(8,128)(2,1)S(1)} copy-done((bf16[512,448]{0,1:T(8,128)(2,1)S(1)}, bf16[512,448]{0,1:T(8,128)(2,1)}, u32[]{:S(2)}) %copy-start.4) | copy-done | bytes 458776
  10.9 0.6 shard_map.127.refs_5_
  11.5 0.5 copy-done.7
  12.0 0.1 multiply_convert_fusion.rest_0_
  12.2 1.6 %collective-permute-done.refs_0_ = bf16[448,512]{1,0:T(8,128)(2,1)} collective-permute-done((bf16[448,512]{1,0:T(8,128)(2,1)}, bf16[448,512]{1,0:T(8,128)(2,1)}, u32[]{:S(2)}, u32[]{:S(2)}) %collective-permute-start) | collective-permute-done | bytes 458784 | tf_op jit(solution)/shard_map/ppermute | solution.py:30
  13.8 1.5 %collective-permute-done.1.refs_1_ = bf16[448,512]{1,0:T(8,128)(2,1)} collective-permute-done((bf16[448,512]{1,0:T(8,128)(2,1)}, bf16[448,512]{1,0:T(8,128)(2,1)}, u32[]{:S(2)}, u32[]{:S(2)}) %collective-permute-start.1) | collective-permute-done | bytes 458784 | tf_op jit(solution)/shard_map/ppermute | solution.py:30
  15.3 0.3 collective-permute-start.6
  15.6 1.7 %collective-permute-start.4 = (bf16[448,512]{1,0:T(8,128)(2,1)}, bf16[448,512]{1,0:T(8,128)(2,1)}, u32[]{:S(2)}, u32[]{:S(2)}) collective-permute-start(bf16[448,512]{1,0:T(8,128)(2,1)} %collective-permute-done.refs_0_), channel_id=1, source_target_pairs={{0,2},{2,4},{4,6},{6,7},{7,5},{5,3},{3,1},{1,0},{8,10},{10,12},{12... | collective-permute-start | bytes 1376264 | tf_op jit(solution)/shard_map/ppermute | solution.py:30
  17.4 0.6 fusion
  17.9 0.1 slice.36
  18.1 0.1 broadcast_in_dim_reshape.10.rate
  18.2 0.1 broadcast_in_dim_reshape.11.skip
  18.4 0.1 broadcast_in_dim_reshape.9.bias
  18.5 0.1 pad_add_fusion
  18.6 1.6 %collective-permute-start.2 = (bf16[64,1792]{1,0:T(8,128)(2,1)S(1)}, bf16[64,1792]{1,0:T(8,128)(2,1)S(1)}, u32[]{:S(2)}, u32[]{:S(2)}) collective-permute-start(bf16[64,1792]{1,0:T(8,128)(2,1)S(1)} %constant_dynamic-slice_fusion), channel_id=1, source_target_pairs={{0,2},{2,4},{4,6},{6,7},{7,5},{5,3},{3,1},{1,0},{8,10},{10,12},{12... | collective-permute-start | bytes 688136 | tf_op jit(solution)/shard_map/ppermute | solution.py:30
  20.2 0.4 collective-permute-start.3
  20.6 3.0 %shard_map.128.refs_5_ = f32[512,512]{1,0:T(8,128)S(1)} custom-call(bf16[448,512]{1,0:T(8,128)(2,1)} %collective-permute-done.refs_0_, bf16[448,512]{1,0:T(8,128)(2,1)} %collective-permute-done.1.refs_1_, bf16[2,3584,128]{2,1,0:T(8,128)(2,1)} %refs_2_.7, bf16[3584,128]{1,0:T(8,128)(2,1)S(1)} %copy-done.3, ...), custom_call_target="tpu_custom_call" | custom-call | flops 1000000000 | bytes 2097152 | tf_op jit(solution)/shard_map/pallas_call | solution.py:339
  23.7 5.4 %collective-permute-done.6.refs_1_ = bf16[448,512]{1,0:T(8,128)(2,1)} collective-permute-done((bf16[448,512]{1,0:T(8,128)(2,1)}, bf16[448,512]{1,0:T(8,128)(2,1)}, u32[]{:S(2)}, u32[]{:S(2)}) %collective-permute-start.6) | collective-permute-done | bytes 458784 | tf_op jit(solution)/shard_map/ppermute | solution.py:30
  29.1 0.2 collective-permute-start.10
  29.3 1.8 %collective-permute-start.9 = (bf16[448,512]{1,0:T(8,128)(2,1)}, bf16[448,512]{1,0:T(8,128)(2,1)S(1)}, u32[]{:S(2)}, u32[]{:S(2)}) collective-permute-start(bf16[448,512]{1,0:T(8,128)(2,1)} %collective-permute-done.4.refs_0_), channel_id=1, source_target_pairs={{0,2},{2,4},{4,6},{6,7},{7,5},{5,3},{3,1},{1,0},{8,10},{10,12},{12... | collective-permute-start | bytes 1376264 | tf_op jit(solution)/shard_map/ppermute | solution.py:30
  31.1 3.0 %collective-permute-done.2.refs_0_ = bf16[64,1792]{1,0:T(8,128)(2,1)S(1)} collective-permute-done((bf16[64,1792]{1,0:T(8,128)(2,1)S(1)}, bf16[64,1792]{1,0:T(8,128)(2,1)S(1)}, u32[]{:S(2)}, u32[]{:S(2)}) %collective-permute-start.2) | collective-permute-done | bytes 229408 | tf_op jit(solution)/shard_map/ppermute | solution.py:30
  34.1 1.8 %collective-permute-start.7 = (bf16[64,1792]{1,0:T(8,128)(2,1)S(1)}, bf16[64,1792]{1,0:T(8,128)(2,1)S(1)}, u32[]{:S(2)}, u32[]{:S(2)}) collective-permute-start(bf16[64,1792]{1,0:T(8,128)(2,1)S(1)} %collective-permute-done.2.refs_0_), channel_id=1, source_target_pairs={{0,16},{8,24},{16,0},{24,8},{1,17},{9,25},{17,1},{25,9},{2,18},{10... | collective-permute-start | bytes 688136 | tf_op jit(solution)/shard_map/ppermute | solution.py:334
  35.9 0.3 collective-permute-start.8
  36.1 3.0 %shard_map.129.refs_5_ = f32[512,512]{1,0:T(8,128)S(1)} custom-call(bf16[448,512]{1,0:T(8,128)(2,1)} %collective-permute-done.4.refs_0_, bf16[448,512]{1,0:T(8,128)(2,1)} %collective-permute-done.6.refs_1_, bf16[2,3584,128]{2,1,0:T(8,128)(2,1)} %refs_2_.7, bf16[3584,128]{1,0:T(8,128)(2,1)S(1)} %copy-done.3, ...), custom_call_target="tpu_custom_call" | custom-call | flops 1000000000 | bytes 2097152 | tf_op jit(solution)/shard_map/pallas_call | solution.py:339
  39.2 3.0 %collective-permute-done.10.back.refs_1_ = bf16[448,512]{1,0:T(8,128)(2,1)S(1)} collective-permute-done((bf16[448,512]{1,0:T(8,128)(2,1)}, bf16[448,512]{1,0:T(8,128)(2,1)S(1)}, u32[]{:S(2)}, u32[]{:S(2)}) %collective-permute-start.10) | collective-permute-done | bytes 458784 | tf_op jit(solution)/shard_map/ppermute | solution.py:30
  42.1 1.2 %collective-permute-done.9.forth.refs_0_ = bf16[448,512]{1,0:T(8,128)(2,1)S(1)} collective-permute-done((bf16[448,512]{1,0:T(8,128)(2,1)}, bf16[448,512]{1,0:T(8,128)(2,1)S(1)}, u32[]{:S(2)}, u32[]{:S(2)}) %collective-permute-start.9) | collective-permute-done | bytes 458784 | tf_op jit(solution)/shard_map/ppermute | solution.py:30
  43.4 2.1 %collective-permute-done.8.refs_3_ = bf16[64,1792]{1,0:T(8,128)(2,1)S(1)} collective-permute-done((bf16[64,1792]{1,0:T(8,128)(2,1)S(1)}, bf16[64,1792]{1,0:T(8,128)(2,1)S(1)}, u32[]{:S(2)}, u32[]{:S(2)}) %collective-permute-start.8) | collective-permute-done | bytes 229408 | tf_op jit(solution)/shard_map/ppermute | solution.py:334
  45.6 2.0 %collective-permute-start.12 = (bf16[224,512]{1,0:T(8,128)(2,1)S(1)}, bf16[224,512]{1,0:T(8,128)(2,1)S(1)}, u32[]{:S(2)}, u32[]{:S(2)}) collective-permute-start(bf16[224,512]{1,0:T(8,128)(2,1)S(1)} %get-tuple-element.62), channel_id=1, source_target_pairs={{0,1},{2,0},{4,2},{6,4},{7,6},{5,7},{3,5},{1,3},{8,9},{10,8},{12,1... | collective-permute-start | bytes 688136 | tf_op jit(solution)/shard_map/ppermute | solution.py:30
  47.6 1.0 %shard_map.132 = (bf16[128,1792]{1,0:T(8,128)(2,1)}, bf16[128,1792]{1,0:T(8,128)(2,1)}) custom-call(bf16[64,1792]{1,0:T(8,128)(2,1)S(1)} %collective-permute-done.2.refs_0_, bf16[64,1792]{1,0:T(8,128)(2,1)S(1)} %collective-permute-done.3.refs_1_, bf16[64,1792]{1,0:T(8,128)(2,1)S(1)} %collective-permute-done.7.refs_2_, ...), custom_call_target="tpu_custom_call" | custom-call | flops 10000000 | bytes 2097152 | tf_op jit(solution)/shard_map/pallas_call | solution.py:349
  48.6 1.9 %shard_map.131 = (f32[512,512]{1,0:T(8,128)S(1)}, bf16[448,512]{1,0:T(8,128)(2,1)S(1)}) custom-call(bf16[448,512]{1,0:T(8,128)(2,1)S(1)} %collective-permute-done.9.forth.refs_0_, bf16[448,512]{1,0:T(8,128)(2,1)S(1)} %collective-permute-done.10.back.refs_1_, bf16[2,3584,128]{2,1,0:T(8,128)(2,1)} %refs_2_.7, bf16[3584,128]{1,0:T(8,128)(2,1)S(1)} %copy-done.3, ...), custom_call_target="tpu_custom_call" | custom-call | flops 1000000000 | bytes 2097152 | tf_op jit(solution)/shard_map/pallas_call | solution.py:339
  50.5 1.1 %collective-permute-done.11.top = bf16[224,512]{1,0:T(8,128)(2,1)S(1)} collective-permute-done((bf16[224,512]{1,0:T(8,128)(2,1)S(1)}, bf16[224,512]{1,0:T(8,128)(2,1)S(1)}, u32[]{:S(2)}, u32[]{:S(2)}) %collective-permute-start.11) | collective-permute-done | bytes 229408 | tf_op jit(solution)/shard_map/ppermute | solution.py:30
  51.7 0.5 shard_map.133.proj
  52.2 1.3 %collective-permute-start.13 = (bf16[8,256]{1,0:T(8,128)(2,1)S(1)}, bf16[8,256]{1,0:T(8,128)(2,1)S(1)}, u32[]{:S(2)}, u32[]{:S(2)}) collective-permute-start(bf16[8,256]{1,0:T(8,128)(2,1)S(1)} %slice.44), channel_id=1, source_target_pairs={{0,8},{8,16},{16,24},{1,9},{9,17},{17,25},{2,10},{10,18},{18,26},{... | collective-permute-start | bytes 12296 | tf_op jit(solution)/shard_map/ppermute | solution.py:355
  53.5 0.8 collective-permute-done.13.halo
  54.3 0.9 collective-permute-start.14
  55.1 1.2 %collective-permute-start.15 = (bf16[128,1792]{1,0:T(8,128)(2,1)}, bf16[128,1792]{1,0:T(8,128)(2,1)S(1)}, u32[]{:S(2)}, u32[]{:S(2)}) collective-permute-start(bf16[128,1792]{1,0:T(8,128)(2,1)} %get-tuple-element.85.rest_2_), channel_id=1, source_target_pairs={{0,1},{2,0},{4,2},{6,4},{7,6},{5,7},{3,5},{1,3},{8,9},{10,8},{12,1... | collective-permute-start | bytes 1376264 | tf_op jit(solution)/shard_map/ppermute | solution.py:30
  56.3 0.1 copy.16.seg_ext
  56.4 0.1 copy.17.seg_ext.seg_col
  56.6 1.0 %shard_map.134 = (f32[256,128]{1,0:T(8,128)S(1)}, f32[256,128]{1,0:T(8,128)S(1)}, f32[256,128]{1,0:T(8,128)S(1)}, f32[72,128]{1,0:T(8,128)S(1)}, f32[256,128]{1,0:T(8,128)S(1)}) custom-call(f32[512,512]{1,0:T(8,128)S(1)} %shard_map.133.proj, s32[264,1]{1,0:T(8,128)S(1)} %copy.16.seg_ext, s32[1,256]{1,0:T(1,128)S(1)} %bitcast.17, f32[4,128]{1,0:T(4,128)S(1)} %copy-done.5, ...), custom_call_target="tpu_custom_call" | custom-call | flops 10000000 | bytes 2097152 | tf_op jit(solution)/shard_map/pallas_call | solution.py:360
  57.6 1.2 %shard_map.135 = (f32[256,128]{1,0:T(8,128)S(1)}, f32[256,128]{1,0:T(8,128)S(1)}, f32[256,128]{1,0:T(8,128)S(1)}, f32[256,128]{1,0:T(8,128)S(1)}, f32[256,128]{1...) custom-call(f32[512,512]{1,0:T(8,128)S(1)} %shard_map.133.proj, ...), custom_call_target="tpu_custom_call" | custom-call | flops 10000000 | bytes 2097152 | tf_op jit(solution)/shard_map/pallas_call | solution.py:365
  58.7 6.8 %all-gather = f32[288,128]{1,0:T(8,128)S(1)} all-gather(f32[72,128]{1,0:T(8,128)S(1)} %get-tuple-element.71), channel_id=2, replica_groups=mesh['seq'=4,'tensor'=8] {'seq'}, dimensions={0}, use_global_device_ids=true | all-gather | bytes 184320 | tf_op jit(solution)/shard_map/all_gather | solution.py:370
  65.6 2.1 %collective-permute-done.14.rest_3_ = bf16[128,1792]{1,0:T(8,128)(2,1)S(1)} collective-permute-done((bf16[128,1792]{1,0:T(8,128)(2,1)}, bf16[128,1792]{1,0:T(8,128)(2,1)S(1)}, u32[]{:S(2)}, u32[]{:S(2)}) %collective-permute-start.14) | collective-permute-done | bytes 458784 | tf_op jit(solution)/shard_map/ppermute | solution.py:30
  67.7 1.2 %collective-permute-done.15.rest_4_ = bf16[128,1792]{1,0:T(8,128)(2,1)S(1)} collective-permute-done((bf16[128,1792]{1,0:T(8,128)(2,1)}, bf16[128,1792]{1,0:T(8,128)(2,1)S(1)}, u32[]{:S(2)}, u32[]{:S(2)}) %collective-permute-start.15) | collective-permute-done | bytes 458784 | tf_op jit(solution)/shard_map/ppermute | solution.py:30
  68.8 2.2 %collective-permute-start.17 = (bf16[128,1792]{1,0:T(8,128)(2,1)S(1)}, bf16[128,1792]{1,0:T(8,128)(2,1)S(1)}, u32[]{:S(2)}, u32[]{:S(2)}) collective-permute-start(bf16[128,1792]{1,0:T(8,128)(2,1)S(1)} %collective-permute-done.14.rest_3_), channel_id=1, source_target_pairs={{0,2},{2,4},{4,6},{6,7},{7,5},{5,3},{3,1},{1,0},{8,10},{10,12},{12... | collective-permute-start | bytes 1376264 | tf_op jit(solution)/shard_map/ppermute | solution.py:30
  71.0 0.5 shard_map.136
  71.5 1.0 shard_map.137
  72.5 14.3 %all_to_all.5.mine = bf16[8,64,128]{2,1,0:T(8,128)(2,1)S(1)} all-to-all(bf16[8,64,128]{2,1,0:T(8,128)(2,1)S(1)} %bitcast.12), channel_id=1, replica_groups=mesh['seq'=4,'tensor'=8] {'tensor'}, dimensions={0} | all-to-all | bytes 262144 | tf_op jit(solution)/shard_map/all_to_all | solution.py:394
  86.8 1.0 %collective-permute-start.19 = (bf16[64,1792]{1,0:T(8,128)(2,1)S(1)}, bf16[64,1792]{1,0:T(8,128)(2,1)S(1)}, u32[]{:S(2)}, u32[]{:S(2)}) collective-permute-start(bf16[64,1792]{1,0:T(8,128)(2,1)S(1)} %get-tuple-element.91), channel_id=1, source_target_pairs={{0,2},{2,4},{4,6},{6,7},{7,5},{5,3},{3,1},{1,0},{8,10},{10,12},{12... | collective-permute-start | bytes 688136 | tf_op jit(solution)/shard_map/ppermute | solution.py:30
  87.8 1.1 %collective-permute-start.20 = (bf16[64,1792]{1,0:T(8,128)(2,1)S(1)}, bf16[64,1792]{1,0:T(8,128)(2,1)S(1)}, u32[]{:S(2)}, u32[]{:S(2)}) collective-permute-start(bf16[64,1792]{1,0:T(8,128)(2,1)S(1)} %get-tuple-element.92), channel_id=1, source_target_pairs={{0,1},{2,0},{4,2},{6,4},{7,6},{5,7},{3,5},{1,3},{8,9},{10,8},{12,1... | collective-permute-start | bytes 688136 | tf_op jit(solution)/shard_map/ppermute | solution.py:30
  88.9 1.3 %collective-permute-done.16.other = bf16[8,64,128]{2,1,0:T(8,128)(2,1)S(1)} collective-permute-done((bf16[8,64,128]{2,1,0:T(8,128)(2,1)S(1)}, bf16[8,64,128]{2,1,0:T(8,128)(2,1)S(1)}, u32[]{:S(2)}, u32[]{:S(2)}) %collective-permute-start.16) | collective-permute-done | bytes 131104 | tf_op jit(solution)/shard_map/ppermute | solution.py:396
  90.3 2.1 %shard_map.138.total = f32[128,1792]{1,0:T(8,128)S(1)} custom-call(bf16[8,64,128]{2,1,0:T(8,128)(2,1)S(1)} %all_to_all.5.mine, bf16[8,64,128]{2,1,0:T(8,128)(2,1)S(1)} %collective-permute-done.16.other, bf16[128,1792]{1,0:T(8,128)(2,1)S(1)} %multiply_convert_fusion.rest_0_, bf16[128,1792]{1,0:T(8,128)(2,1)} %get-tuple-element.84.rest_1_, ...), custom_call_target="tpu_custom_call" | custom-call | flops 1000000000 | bytes 2097152 | tf_op jit(solution)/shard_map/pallas_call | solution.py:401
  92.4 0.5 collective-permute-done.19.top
  92.9 0.9 collective-permute-done.20.bottom
  93.8 0.3 shard_map.140
  94.1 0.1 collective-permute-start.21
  94.2 1.5 %collective-permute-done.21 = bf16[64,1792]{1,0:T(8,128)(2,1)S(1)} collective-permute-done((bf16[64,1792]{1,0:T(8,128)(2,1)S(1)}, bf16[64,1792]{1,0:T(8,128)(2,1)S(1)}, u32[]{:S(2)}, u32[]{:S(2)}) %collective-permute-start.21) | collective-permute-done | bytes 229408 | tf_op jit(solution)/shard_map/ppermute | solution.py:408
  95.7 0.8 pad_maximum_fusion
  (44 shorter events, 0.6 us)
Async XLA Ops:
  0.0 6.0 %copy-start = (bf16[3584,2]{0,1:T(2,128)(2,1)S(1)}, bf16[3584,2]{0,1:T(2,128)(2,1)}, u32[]{:S(2)}) copy-start(bf16[3584,2]{0,1:T(2,128)(2,1)} %param.16) | copy-start | bytes 43012
  0.0 13.8 %collective-permute-start = (bf16[448,512]{1,0:T(8,128)(2,1)}, bf16[448,512]{1,0:T(8,128)(2,1)}, u32[]{:S(2)}, u32[]{:S(2)}) collective-permute-start(bf16[448,512]{1,0:T(8,128)(2,1)} %bitcast.13), channel_id=1, source_target_pairs={{0,2},{2,4},{4,6},{6,7},{7,5},{5,3},{3,1},{1,0},{8,10},{10,12},{12... | collective-permute-start | bytes 1376264 | tf_op jit(solution)/shard_map/ppermute | solution.py:30
  3.0 12.3 %collective-permute-start.1 = (bf16[448,512]{1,0:T(8,128)(2,1)}, bf16[448,512]{1,0:T(8,128)(2,1)}, u32[]{:S(2)}, u32[]{:S(2)}) collective-permute-start(bf16[448,512]{1,0:T(8,128)(2,1)} %bitcast.14), channel_id=1, source_target_pairs={{0,1},{2,0},{4,2},{6,4},{7,6},{5,7},{3,5},{1,3},{8,9},{10,8},{12,1... | collective-permute-start | bytes 1376264 | tf_op jit(solution)/shard_map/ppermute | solution.py:30
  3.8 14.7 %collective-permute-start.5 = (s32[8]{0:T(128)S(1)}, s32[8]{0:T(128)S(1)}, u32[]{:S(2)}, u32[]{:S(2)}) collective-permute-start(s32[8]{0:T(128)S(1)} %slice.33), channel_id=1, source_target_pairs={{0,8},{8,16},{16,24},{1,9},{9,17},{17,25},{2,10},{10,18},{18,26},{... | collective-permute-start | bytes 104 | tf_op jit(solution)/shard_map/ppermute | solution.py:306
  7.1 1.5 %copy-start.1 = (bf16[2,3584,128]{2,1,0:T(8,128)(2,1)S(1)}, bf16[2,3584,128]{2,1,0:T(8,128)(2,1)}, u32[]{:S(2)}) copy-start(bf16[2,3584,128]{2,1,0:T(8,128)(2,1)} %refs_2_.7) | copy-start | bytes 5505028
  8.6 1.2 %copy-start.2 = (bf16[3584,128]{1,0:T(8,128)(2,1)S(1)}, bf16[3584,128]{1,0:T(8,128)(2,1)}, u32[]{:S(2)}) copy-start(bf16[3584,128]{1,0:T(8,128)(2,1)} %refs_3_.5) | copy-start | bytes 2752516
  9.8 1.0 %copy-start.4 = (bf16[512,448]{0,1:T(8,128)(2,1)S(1)}, bf16[512,448]{0,1:T(8,128)(2,1)}, u32[]{:S(2)}) copy-start(bf16[512,448]{0,1:T(8,128)(2,1)} %param.13) | copy-start | bytes 1376260
  10.8 1.2 %copy-start.7 = (bf16[128,3584]{1,0:T(8,128)(2,1)S(1)}, bf16[128,3584]{1,0:T(8,128)(2,1)}, u32[]{:S(2)}) copy-start(bf16[128,3584]{1,0:T(8,128)(2,1)} %param.23) | copy-start | bytes 2752516
  10.8 1.2 %copy-start.9 = (f32[128]{0:T(128)S(1)}, f32[128]{0:T(128)}, u32[]{:S(2)}) copy-start(f32[128]{0:T(128)} %param.22) | copy-start | bytes 1540
  10.8 6.5 %copy-start.8 = (s32[512]{0:T(512)S(1)}, s32[512]{0:T(512)}, u32[]{:S(2)}) copy-start(s32[512]{0:T(512)} %param.24) | copy-start | bytes 6148
  10.8 7.2 %copy-start.10 = (f32[2]{0:T(128)S(1)}, f32[2]{0:T(128)}, u32[]{:S(2)}) copy-start(f32[2]{0:T(128)} %param.18) | copy-start | bytes 28
  10.8 7.3 %copy-start.11 = (f32[2]{0:T(128)S(1)}, f32[2]{0:T(128)}, u32[]{:S(2)}) copy-start(f32[2]{0:T(128)} %param.19) | copy-start | bytes 28
  10.9 7.5 %copy-start.12 = (f32[2]{0:T(128)S(1)}, f32[2]{0:T(128)}, u32[]{:S(2)}) copy-start(f32[2]{0:T(128)} %param.17) | copy-start | bytes 28
  12.0 8.6 %copy-start.3 = (bf16[3584,128]{1,0:T(8,128)(2,1)S(1)}, bf16[3584,128]{1,0:T(8,128)(2,1)}, u32[]{:S(2)}) copy-start(bf16[3584,128]{1,0:T(8,128)(2,1)} %refs_3_.5) | copy-start | bytes 2752516
  15.3 13.8 %collective-permute-start.6 = (bf16[448,512]{1,0:T(8,128)(2,1)}, bf16[448,512]{1,0:T(8,128)(2,1)}, u32[]{:S(2)}, u32[]{:S(2)}) collective-permute-start(bf16[448,512]{1,0:T(8,128)(2,1)} %collective-permute-done.1.refs_1_), channel_id=1, source_target_pairs={{0,1},{2,0},{4,2},{6,4},{7,6},{5,7},{3,5},{1,3},{8,9},{10,8},{12,1... | collective-permute-start | bytes 1376264 | tf_op jit(solution)/shard_map/ppermute | solution.py:30
  15.6 13.7 %collective-permute-start.4 = (bf16[448,512]{1,0:T(8,128)(2,1)}, bf16[448,512]{1,0:T(8,128)(2,1)}, u32[]{:S(2)}, u32[]{:S(2)}) collective-permute-start(bf16[448,512]{1,0:T(8,128)(2,1)} %collective-permute-done.refs_0_), channel_id=1, source_target_pairs={{0,2},{2,4},{4,6},{6,7},{7,5},{5,3},{3,1},{1,0},{8,10},{10,12},{12... | collective-permute-start | bytes 1376264 | tf_op jit(solution)/shard_map/ppermute | solution.py:30
  18.6 15.5 %collective-permute-start.2 = (bf16[64,1792]{1,0:T(8,128)(2,1)S(1)}, bf16[64,1792]{1,0:T(8,128)(2,1)S(1)}, u32[]{:S(2)}, u32[]{:S(2)}) collective-permute-start(bf16[64,1792]{1,0:T(8,128)(2,1)S(1)} %constant_dynamic-slice_fusion), channel_id=1, source_target_pairs={{0,2},{2,4},{4,6},{6,7},{7,5},{5,3},{3,1},{1,0},{8,10},{10,12},{12... | collective-permute-start | bytes 688136 | tf_op jit(solution)/shard_map/ppermute | solution.py:30
  20.2 13.9 %collective-permute-start.3 = (bf16[64,1792]{1,0:T(8,128)(2,1)S(1)}, bf16[64,1792]{1,0:T(8,128)(2,1)S(1)}, u32[]{:S(2)}, u32[]{:S(2)}) collective-permute-start(bf16[64,1792]{1,0:T(8,128)(2,1)S(1)} %constant_dynamic-slice_fusion), channel_id=1, source_target_pairs={{0,1},{2,0},{4,2},{6,4},{7,6},{5,7},{3,5},{1,3},{8,9},{10,8},{12,1... | collective-permute-start | bytes 688136 | tf_op jit(solution)/shard_map/ppermute | solution.py:30
  29.1 13.1 %collective-permute-start.10 = (bf16[448,512]{1,0:T(8,128)(2,1)}, bf16[448,512]{1,0:T(8,128)(2,1)S(1)}, u32[]{:S(2)}, u32[]{:S(2)}) collective-permute-start(bf16[448,512]{1,0:T(8,128)(2,1)} %collective-permute-done.6.refs_1_), channel_id=1, source_target_pairs={{0,1},{2,0},{4,2},{6,4},{7,6},{5,7},{3,5},{1,3},{8,9},{10,8},{12,1... | collective-permute-start | bytes 1376264 | tf_op jit(solution)/shard_map/ppermute | solution.py:30
  29.3 14.1 %collective-permute-start.9 = (bf16[448,512]{1,0:T(8,128)(2,1)}, bf16[448,512]{1,0:T(8,128)(2,1)S(1)}, u32[]{:S(2)}, u32[]{:S(2)}) collective-permute-start(bf16[448,512]{1,0:T(8,128)(2,1)} %collective-permute-done.4.refs_0_), channel_id=1, source_target_pairs={{0,2},{2,4},{4,6},{6,7},{7,5},{5,3},{3,1},{1,0},{8,10},{10,12},{12... | collective-permute-start | bytes 1376264 | tf_op jit(solution)/shard_map/ppermute | solution.py:30
  34.1 9.3 %collective-permute-start.7 = (bf16[64,1792]{1,0:T(8,128)(2,1)S(1)}, bf16[64,1792]{1,0:T(8,128)(2,1)S(1)}, u32[]{:S(2)}, u32[]{:S(2)}) collective-permute-start(bf16[64,1792]{1,0:T(8,128)(2,1)S(1)} %collective-permute-done.2.refs_0_), channel_id=1, source_target_pairs={{0,16},{8,24},{16,0},{24,8},{1,17},{9,25},{17,1},{25,9},{2,18},{10... | collective-permute-start | bytes 688136 | tf_op jit(solution)/shard_map/ppermute | solution.py:334
  35.9 9.6 %collective-permute-start.8 = (bf16[64,1792]{1,0:T(8,128)(2,1)S(1)}, bf16[64,1792]{1,0:T(8,128)(2,1)S(1)}, u32[]{:S(2)}, u32[]{:S(2)}) collective-permute-start(bf16[64,1792]{1,0:T(8,128)(2,1)S(1)} %collective-permute-done.3.refs_1_), channel_id=1, source_target_pairs={{0,16},{8,24},{16,0},{24,8},{1,17},{9,25},{17,1},{25,9},{2,18},{10... | collective-permute-start | bytes 688136 | tf_op jit(solution)/shard_map/ppermute | solution.py:334
  45.5 6.1 %collective-permute-start.11 = (bf16[224,512]{1,0:T(8,128)(2,1)S(1)}, bf16[224,512]{1,0:T(8,128)(2,1)S(1)}, u32[]{:S(2)}, u32[]{:S(2)}) collective-permute-start(bf16[224,512]{1,0:T(8,128)(2,1)S(1)} %get-tuple-element.61), channel_id=1, source_target_pairs={{0,2},{2,4},{4,6},{6,7},{7,5},{5,3},{3,1},{1,0},{8,10},{10,12},{12... | collective-permute-start | bytes 688136 | tf_op jit(solution)/shard_map/ppermute | solution.py:30
  45.6 6.1 %collective-permute-start.12 = (bf16[224,512]{1,0:T(8,128)(2,1)S(1)}, bf16[224,512]{1,0:T(8,128)(2,1)S(1)}, u32[]{:S(2)}, u32[]{:S(2)}) collective-permute-start(bf16[224,512]{1,0:T(8,128)(2,1)S(1)} %get-tuple-element.62), channel_id=1, source_target_pairs={{0,1},{2,0},{4,2},{6,4},{7,6},{5,7},{3,5},{1,3},{8,9},{10,8},{12,1... | collective-permute-start | bytes 688136 | tf_op jit(solution)/shard_map/ppermute | solution.py:30
  51.7 4.9 %copy-start.5 = (f32[4,128]{1,0:T(4,128)S(1)}, f32[4,128]{1,0:T(4,128)}, u32[]{:S(2)}) copy-start(f32[4,128]{1,0:T(4,128)} %taps_x.3) | copy-start | bytes 6148
  51.7 4.9 %copy-start.6 = (f32[4,128]{1,0:T(4,128)S(1)}, f32[4,128]{1,0:T(4,128)}, u32[]{:S(2)}) copy-start(f32[4,128]{1,0:T(4,128)} %taps_bc.3) | copy-start | bytes 6148
  52.2 2.1 %collective-permute-start.13 = (bf16[8,256]{1,0:T(8,128)(2,1)S(1)}, bf16[8,256]{1,0:T(8,128)(2,1)S(1)}, u32[]{:S(2)}, u32[]{:S(2)}) collective-permute-start(bf16[8,256]{1,0:T(8,128)(2,1)S(1)} %slice.44), channel_id=1, source_target_pairs={{0,8},{8,16},{16,24},{1,9},{9,17},{17,25},{2,10},{10,18},{18,26},{... | collective-permute-start | bytes 12296 | tf_op jit(solution)/shard_map/ppermute | solution.py:355
  54.3 13.4 %collective-permute-start.14 = (bf16[128,1792]{1,0:T(8,128)(2,1)}, bf16[128,1792]{1,0:T(8,128)(2,1)S(1)}, u32[]{:S(2)}, u32[]{:S(2)}) collective-permute-start(bf16[128,1792]{1,0:T(8,128)(2,1)} %get-tuple-element.84.rest_1_), channel_id=1, source_target_pairs={{0,2},{2,4},{4,6},{6,7},{7,5},{5,3},{3,1},{1,0},{8,10},{10,12},{12... | collective-permute-start | bytes 1376264 | tf_op jit(solution)/shard_map/ppermute | solution.py:30
  55.1 13.7 %collective-permute-start.15 = (bf16[128,1792]{1,0:T(8,128)(2,1)}, bf16[128,1792]{1,0:T(8,128)(2,1)S(1)}, u32[]{:S(2)}, u32[]{:S(2)}) collective-permute-start(bf16[128,1792]{1,0:T(8,128)(2,1)} %get-tuple-element.85.rest_2_), channel_id=1, source_target_pairs={{0,1},{2,0},{4,2},{6,4},{7,6},{5,7},{3,5},{1,3},{8,9},{10,8},{12,1... | collective-permute-start | bytes 1376264 | tf_op jit(solution)/shard_map/ppermute | solution.py:30
  68.8 18.0 %collective-permute-start.17 = (bf16[128,1792]{1,0:T(8,128)(2,1)S(1)}, bf16[128,1792]{1,0:T(8,128)(2,1)S(1)}, u32[]{:S(2)}, u32[]{:S(2)}) collective-permute-start(bf16[128,1792]{1,0:T(8,128)(2,1)S(1)} %collective-permute-done.14.rest_3_), channel_id=1, source_target_pairs={{0,2},{2,4},{4,6},{6,7},{7,5},{5,3},{3,1},{1,0},{8,10},{10,12},{12... | collective-permute-start | bytes 1376264 | tf_op jit(solution)/shard_map/ppermute | solution.py:30
  71.0 15.8 %collective-permute-start.18 = (bf16[128,1792]{1,0:T(8,128)(2,1)S(1)}, bf16[128,1792]{1,0:T(8,128)(2,1)S(1)}, u32[]{:S(2)}, u32[]{:S(2)}) collective-permute-start(bf16[128,1792]{1,0:T(8,128)(2,1)S(1)} %collective-permute-done.15.rest_4_), channel_id=1, source_target_pairs={{0,1},{2,0},{4,2},{6,4},{7,6},{5,7},{3,5},{1,3},{8,9},{10,8},{12,1... | collective-permute-start | bytes 1376264 | tf_op jit(solution)/shard_map/ppermute | solution.py:30
  86.8 6.1 %collective-permute-start.19 = (bf16[64,1792]{1,0:T(8,128)(2,1)S(1)}, bf16[64,1792]{1,0:T(8,128)(2,1)S(1)}, u32[]{:S(2)}, u32[]{:S(2)}) collective-permute-start(bf16[64,1792]{1,0:T(8,128)(2,1)S(1)} %get-tuple-element.91), channel_id=1, source_target_pairs={{0,2},{2,4},{4,6},{6,7},{7,5},{5,3},{3,1},{1,0},{8,10},{10,12},{12... | collective-permute-start | bytes 688136 | tf_op jit(solution)/shard_map/ppermute | solution.py:30
  87.8 6.0 %collective-permute-start.20 = (bf16[64,1792]{1,0:T(8,128)(2,1)S(1)}, bf16[64,1792]{1,0:T(8,128)(2,1)S(1)}, u32[]{:S(2)}, u32[]{:S(2)}) collective-permute-start(bf16[64,1792]{1,0:T(8,128)(2,1)S(1)} %get-tuple-element.92), channel_id=1, source_target_pairs={{0,1},{2,0},{4,2},{6,4},{7,6},{5,7},{3,5},{1,3},{8,9},{10,8},{12,1... | collective-permute-start | bytes 688136 | tf_op jit(solution)/shard_map/ppermute | solution.py:30
  88.9 1.3 %collective-permute-start.16 = (bf16[8,64,128]{2,1,0:T(8,128)(2,1)S(1)}, bf16[8,64,128]{2,1,0:T(8,128)(2,1)S(1)}, u32[]{:S(2)}, u32[]{:S(2)}) collective-permute-start(bf16[8,64,128]{2,1,0:T(8,128)(2,1)S(1)} %all_to_all.5.mine), channel_id=1, source_target_pairs={{0,8},{8,0},{16,24},{24,16},{1,9},{9,1},{17,25},{25,17},{2,10},{10... | collective-permute-start | bytes 393224 | tf_op jit(solution)/shard_map/ppermute | solution.py:396
  94.1 1.6 %collective-permute-start.21 = (bf16[64,1792]{1,0:T(8,128)(2,1)S(1)}, bf16[64,1792]{1,0:T(8,128)(2,1)S(1)}, u32[]{:S(2)}, u32[]{:S(2)}) collective-permute-start(bf16[64,1792]{1,0:T(8,128)(2,1)S(1)} %get-tuple-element.94), channel_id=1, source_target_pairs={{0,8},{8,0},{16,24},{24,16},{1,9},{9,1},{17,25},{25,17},{2,10},{10... | collective-permute-start | bytes 688136 | tf_op jit(solution)/shard_map/ppermute | solution.py:408

commit v8 on v7

--- a/solution.py
+++ b/solution.py
@@ -45,15 +45,6 @@
     size = top.shape[0]
     top[...] = forth[:size]
     bottom[...] = back[size:]
-
-
-def join(*refs):
-    count = len(refs) // 3
-    odd = lax.axis_index("seq") // 2 % 2
-    for own, other, out in zip(refs[:count], refs[count : 2 * count], refs[2 * count :]):
-        size = own.shape[0]
-        out[pl.ds(pl.multiple_of(odd * size, size), size)] = own[...]
-        out[pl.ds(pl.multiple_of((1 - odd) * size, size), size)] = other[...]
 
 
 def silu(v):
@@ -240,21 +231,24 @@
 
 def product(gated, distances, pieces):
     total = 0.0
-    for distance, piece in zip(distances, pieces):
+    odd = lax.axis_index("seq") // 2 % 2 == 1
+    for distance, (near, other) in zip(distances, pieces):
         source = source_of(distance)
         rows = jnp.concatenate([part[source] for part in gated], 0)
-        total = total + jnp.dot(rows, piece[...], preferred_element_type=F32)
+        half = rows.shape[1] // 2
+        swapped = jnp.concatenate([rows[:, half:], rows[:, :half]], 1)
+        rows = jnp.where(odd, swapped, rows)
+        total = total + jnp.dot(rows, jnp.concatenate([near[...], other[...]], 0), preferred_element_type=F32)
     return total
 
 
 def product_early(distances, mine, other, *rest):
-    rest[-1][...] = product((mine, other), distances, rest[:-1])
-
-
-def product_last(distance, mine, other, total, top, bottom, mine_out, other_out, held):
-    held[: top.shape[0]] = top[...]
-    held[top.shape[0] :] = bottom[...]
-    result = product((mine, other), [distance], [held]) + total[...]
+    pieces, out = rest[:-1], rest[-1]
+    out[...] = product((mine, other), distances, list(zip(pieces[::2], pieces[1::2])))
+
+
+def product_last(distance, mine, other, total, near, far, mine_out, other_out):
+    result = product((mine, other), [distance], [(near, far)]) + total[...]
     blocks, rows, width = mine.shape
     for i, (gated, out) in enumerate(((mine, mine_out), (other, other_out))):
         squares = jnp.zeros((rows, width), F32)
@@ -292,15 +286,29 @@
 
     spread = lambda v: jnp.repeat(v, head_w, axis=-1)
     expand = np.repeat(np.eye(heads, dtype=np.float32), head_w, axis=1)
-    w_step = jnp.dot(w_dt, expand.astype(BF16))
+    w_delta = jnp.dot(w_dt, expand.astype(BF16))
     block = tokens.T
     core = seq_at % 2
     columns = model // 2
     own = (lax.dynamic_slice_in_dim(w_out, core * columns, columns, 1).astype(F32) * norm_gain[:, None]).astype(BF16)
     last = n_tensor // 2
     w_half = width // 2
-    own_rows = lax.dynamic_slice_in_dim(own, seq_at // 2 % 2 * w_half, w_half, 0)
+    odd = seq_at // 2 % 2
+    own_halves = [lax.dynamic_slice_in_dim(own, place * w_half, w_half, 0) for place in (odd, 1 - odd)]
     other_y = [(i, i ^ 2) for i in range(n_seq)]
+    w_near, w_other = {0: own_halves[0]}, {0: own_halves[1]}
+
+    def w_step(k, *earlier):
+        before = after((w_near[1 - k], w_near[k - 1]), *earlier)
+        w_near[-k], w_near[k] = ring_shift(before[0], 1), ring_shift(before[1], -1)
+        return w_near[-k], w_near[k]
+
+    def w_swap(k, *earlier):
+        sides = (-k, k) if k < last else (k,)
+        for side in sides:
+            w_other[side] = lax.ppermute(after(w_near[side], *earlier), "seq", other_y)
+        return tuple(w_other[side] for side in sides)
+
     shift_rows = [(i, i + 1) for i in range(n_seq - 1)]
 
     seg_halo = lax.ppermute(segments[tok_rows - HALO :], "seq", shift_rows)
@@ -314,24 +322,21 @@
 
     forth = back = block
     arrived, projs = [(0, block)], []
+    moved = ()
     for step in range(1, last + 1):
-        if step == 3:
-            forth, back = after(forth, projs[1], small), after(back, projs[1], small)
-            w_arrived = after(w_arrived, forth, back)
-        elif step > 1:
-            forth, back = after(forth, projs[step - 2]), after(back, projs[step - 2])
-        if step == 4:
-            w_swapped, forth, back = after((w_swapped, forth, back))
-        if step == 2:
-            w_sent = after(own_rows, forth, back)
+        if step > 1:
+            ready = (projs[step - 2], moved, small) if step == 3 else (projs[step - 2], moved)
+            forth, back = after(forth, ready), after(back, ready)
+        arrivals = (forth, back)
         if step < last:
             forth, back = ring_shift(forth, 1), ring_shift(back, -1)
         else:
             far = far_shift(forth, back)
-        if step == 2:
-            w_arrived = ring_shift(w_sent, 1), ring_shift(w_sent, -1)
-        if step == 3:
-            w_swapped = [lax.ppermute(part, "seq", other_y) for part in w_arrived]
+        moved = ()
+        if step > 2:
+            moved += w_swap(step - 2, arrivals)
+        if 1 < step < last:
+            moved += w_step(step - 1, arrivals)
         ahead = last if step == last else 0
         total = projs[-1:]
         fetched = len(arrived) + bool(ahead)
@@ -342,17 +347,15 @@
             [pltpu.VMEM((len(arrived), feat, 4 * width), BF16), pltpu.SemaphoreType.DMA((fetched, 4))],
             in_specs=[VMEM] * len(arrived) + [ANY] * 3 + [VMEM] * len(total),
             flops=10**9,
-        )(*[part for _, part in arrived], w_zx, w_bc, w_step, *total)
+        )(*[part for _, part in arrived], w_zx, w_bc, w_delta, *total)
         projs.append(results[0])
         arrived = [(-step, forth), (step, back)]
-    whole = shape(width, columns, kind=BF16)
-    w_forth, w_back = call(join, [whole, whole])(*w_arrived, *w_swapped)
-    proj = call(project_far, shape(tok_rows, 4 * width), flops=10**9)(
-        *far, results[1], after(projs[-1], w_forth, w_back)
-    )
+    proj = call(project_far, shape(tok_rows, 4 * width), flops=10**9)(*far, results[1], projs[-1])
+    w_late = w_step(last - 1, far)
 
     (seg_ext_a, seg_ext_b), (seg_row_a, seg_row_b), (seg_first, seg_last), (bias, rate, skip) = small
     halo = lax.ppermute(proj[tok_rows - HALO :, width : 3 * width].astype(BF16), "seq", shift_rows)
+    halo = after(halo, moved)
 
     msg_rows = state_w + 8
     plane = shape(rows, width)
@@ -367,7 +370,7 @@
         [plane] * 5 + [shape(msg_rows, width)] * 2,
         [ext, ext],
     )(proj, halo, seg_ext_a, seg_last, state_b, conv_x, conv_bc, bias, rate)
-    messages = lax.all_gather(message, "seq")
+    messages = after(lax.all_gather(message, "seq"), w_late)
     out_a, gate_a = call(functools.partial(first_inner, heads, width, rows), [plane, plane])(
         cx_a, bc_a, cum_a, scaled_a, proj, seg_ext_a, seg_row_a, skip
     )
@@ -377,34 +380,22 @@
 
     tok_own = tok_rows // n_tensor
 
-    w_steps = [(w_forth, w_back)]
-    orders = [(proj, halo), messages]
-    for step in range(2, last + 1):
-        if step - 2 < len(orders):
-            w_forth, w_back = after((w_forth, w_back), orders[step - 2])
-        if step == 4:
-            w_forth, w_back = after((w_forth, w_back), mine)
-        if step == last:
-            w_far = far_shift(w_forth, w_back)
-            break
-        w_forth, w_back = ring_shift(w_forth, 1), ring_shift(w_back, -1)
-        w_steps.append((w_forth, w_back))
-        if step == 2:
-            blocks = after(gated, w_forth, w_back).reshape(n_tensor, tok_own, width)
-            mine = lax.all_to_all(blocks, "tensor", 0, 0)
+    w_near[last] = ring_shift(after(w_near[1 - last], messages), 1)
+    w_swap(last - 1, messages)
+    mine = lax.all_to_all(gated.reshape(n_tensor, tok_own, width), "tensor", 0, 0)
+    mine = after(mine, w_near[last], w_other[1 - last], w_other[last - 1])
+    w_swap(last, mine)
     swap = [(i, i ^ 1) for i in range(n_seq)]
     other = lax.ppermute(mine, "seq", swap)
-    pieces, distances = [own], [0]
-    for i, pair in enumerate(w_steps):
-        pieces += pair
-        distances += [-i - 1, i + 1]
+    distances = [0] + [side * k for k in range(1, last) for side in (-1, 1)]
+    pieces = [held[distance] for distance in distances for held in (w_near, w_other)]
     total = call(functools.partial(product_early, distances), shape(2 * tok_own, columns), flops=10**9)(
         mine, other, *pieces
     )
     half = shape(tok_own, columns, kind=BF16)
     out_own, out_other = call(
-        functools.partial(product_last, last), [half, half], [pltpu.VMEM((width, columns), BF16)], flops=10**8
-    )(mine, other, total, *w_far)
+        functools.partial(product_last, last), [half, half], flops=10**8
+    )(mine, other, total, w_near[last], w_other[last])
     arrived = lax.ppermute(out_other, "seq", swap)
     is_first = core == 0
     return jnp.concatenate([jnp.where(is_first, out_own, arrived), jnp.where(is_first, arrived, out_own)], 1)

time: 97.1 us -> 101 us (1.040)
  blocking collectives: 21.2 us -> 7.6 us
  waiting for transfers between devices: 27.4 us -> 35.5 us
  starting transfers between devices: 22.3 us -> 29.7 us
  other arithmetic: 1.05 us -> 2.09 us
    all_to_all x1 -> x0, blocking collectives: 14.3 us -> none  [local(): mine = lax.all_to_all(blocks, 'tensor', 0, 0)]
    all_to_all x0 -> x1, waiting for transfers between devices: none -> 7.03 us  [local(): lax.all_to_all(gated.reshape(n_tensor, tok_own, width), 'tensor', 0, 0)]
    ppermute x2 -> x7, starting transfers between devices: 2.03 us -> 6.49 us  [w_swap(): w_other[side] = lax.ppermute(after(w_near[side], *earlier), 'seq', other_y)]
    all_to_all x0 -> x1, starting transfers between devices: none -> 3.37 us  [local(): lax.all_to_all(gated.reshape(n_tensor, tok_own, width), 'tensor', 0, 0)]
    ppermute x2 -> x7, waiting for transfers between devices: 2.13 us -> 5.48 us  [w_swap(): w_other[side] = lax.ppermute(after(w_near[side], *earlier), 'seq', other_y)]
    ppermute x16 -> x15, waiting for transfers between devices: 21.6 us -> 20.2 us  [ring_shift(): lax.ppermute(block, 'tensor', [(order[i], order[(i + step) % n]) for i in...]
    unnamed x26 -> x28, local copies, waits for them, and re-layouts: 4.25 us -> 5.62 us
    convert_element_type x1, other arithmetic: 0.14 us -> 1.18 us  [local(): (lax.dynamic_slice_in_dim(w_out, core * columns, columns, 1).astype(F32)...]
  transfers between devices with their start and end apart: 22 -> 27, of which waited for: 16 -> 13; matrix products, arithmetic and copies ran while one was open for 4% -> 5% of each run, Pallas kernels for 16% -> 16%
where the time goes in v8:
time: 101 us; the launch traced here: 100 us
  waiting for transfers between devices  35.5 us (35%)
  starting transfers between devices  29.7 us (29%)
  Pallas kernels  16 us (16%)
  local copies, waits for them, and re-layouts  7.82 us (8%)
  blocking collectives  7.6 us (8%)
  other arithmetic  2.09 us (2%)
  matrix products  1.12 us (1%)
    ppermute x15, waiting for transfers between devices, ring_shift(): lax.ppermute(block, 'tensor', [(order[i], order[(i + step) % n]) for i in...  20.2 us
    ppermute x15, starting transfers between devices, ring_shift(): lax.ppermute(block, 'tensor', [(order[i], order[(i + step) % n]) for i in...  17 us
    pallas_call x4, Pallas kernels, local(): call(functools.partial(project, [distance for distance, _ in arrived], ah...  8.38 us
    all_gather x1, blocking collectives, local(): messages = after(lax.all_gather(message, 'seq'), w_late)  7.6 us
    all_to_all x1, waiting for transfers between devices, local(): lax.all_to_all(gated.reshape(n_tensor, tok_own, width), 'tensor', 0, 0)  7.03 us
    ppermute x7, starting transfers between devices, w_swap(): w_other[side] = lax.ppermute(after(w_near[side], *earlier), 'seq', other_y)  6.49 us
    unnamed x28, local copies, waits for them, and re-layouts  5.62 us
    ppermute x7, waiting for transfers between devices, w_swap(): w_other[side] = lax.ppermute(after(w_near[side], *earlier), 'seq', other_y)  5.48 us
  transfers between devices with their start and end apart: 27, of which 13 were waited for; matrix products, arithmetic and copies ran while one was open for 5% of the time, Pallas kernels for 16%

profile of v8, /device:TPU:0, one launch (start us, length us, event | category | flops | bytes accessed | tf_op | source)
XLA Modules:
  0.0 100.2 jit_solution(13409315052028307933)
XLA Ops:
  0.0 3.0 %collective-permute-start = (bf16[448,512]{1,0:T(8,128)(2,1)}, bf16[448,512]{1,0:T(8,128)(2,1)}, u32[]{:S(2)}, u32[]{:S(2)}) collective-permute-start(bf16[448,512]{1,0:T(8,128)(2,1)} %bitcast.12), channel_id=1, source_target_pairs={{0,2},{2,4},{4,6},{6,7},{7,5},{5,3},{3,1},{1,0},{8,10},{10,12},{12... | collective-permute-start | bytes 1376264 | tf_op jit(solution)/shard_map/ppermute | solution.py:30
  3.0 0.8 slice.33
  3.8 1.4 %collective-permute-start.5 = (s32[8]{0:T(128)S(1)}, s32[8]{0:T(128)S(1)}, u32[]{:S(2)}, u32[]{:S(2)}) collective-permute-start(s32[8]{0:T(128)S(1)} %slice.33), channel_id=1, source_target_pairs={{0,8},{8,16},{16,24},{1,9},{9,17},{17,25},{2,10},{10,18},{18,26},{... | collective-permute-start | bytes 104 | tf_op jit(solution)/shard_map/ppermute | solution.py:314
  5.3 1.2 %multiply_convert_fusion = bf16[128,1792]{1,0:T(8,128)(2,1)S(1)} fusion(f32[128]{0:T(128)} %param.22, bf16[128,3584]{1,0:T(8,128)(2,1)} %param.23, s32[]{:T(128)S(6)} %select_n.38), kind=kLoop, calls=%fused_computation.1 | loop fusion | flops 688128 | bytes 918020 | tf_op jit(solution)/shard_map/convert_element_type | solution.py:293
  6.5 1.1 %convolution_bitcast_fusion.refs_3_.refs_4_ = bf16[3584,128]{1,0:T(8,128)(2,1)S(1)} fusion(bf16[2,128]{1,0:T(2,128)(2,1)} %constant.45.clone, bf16[3584,2]{0,1:T(2,128)(2,1)S(1)} %copy-done), kind=kOutput, calls=%fused_computation | convolution fusion | flops 1835008 | bytes 932352 | tf_op jit(solution)/shard_map/dot_general | solution.py:289
  7.6 1.2 %copy-done.2 = bf16[3584,128]{1,0:T(8,128)(2,1)S(1)} copy-done((bf16[3584,128]{1,0:T(8,128)(2,1)S(1)}, bf16[3584,128]{1,0:T(8,128)(2,1)}, u32[]{:S(2)}) %copy-start.2) | copy-done | bytes 917528
  8.8 1.0 %copy-done.7 = bf16[512,448]{0,1:T(8,128)(2,1)S(1)} copy-done((bf16[512,448]{0,1:T(8,128)(2,1)S(1)}, bf16[512,448]{0,1:T(8,128)(2,1)}, u32[]{:S(2)}) %copy-start.7) | copy-done | bytes 458776
  9.8 0.6 shard_map.127.refs_5_
  10.5 1.0 copy-done.5
  11.5 2.3 %collective-permute-done.refs_0_ = bf16[448,512]{1,0:T(8,128)(2,1)} collective-permute-done((bf16[448,512]{1,0:T(8,128)(2,1)}, bf16[448,512]{1,0:T(8,128)(2,1)}, u32[]{:S(2)}, u32[]{:S(2)}) %collective-permute-start) | collective-permute-done | bytes 458784 | tf_op jit(solution)/shard_map/ppermute | solution.py:30
  13.8 1.8 %collective-permute-start.1 = (bf16[448,512]{1,0:T(8,128)(2,1)}, bf16[448,512]{1,0:T(8,128)(2,1)}, u32[]{:S(2)}, u32[]{:S(2)}) collective-permute-start(bf16[448,512]{1,0:T(8,128)(2,1)} %collective-permute-done.refs_0_), channel_id=1, source_target_pairs={{0,2},{2,4},{4,6},{6,7},{7,5},{5,3},{3,1},{1,0},{8,10},{10,12},{12... | collective-permute-start | bytes 1376264 | tf_op jit(solution)/shard_map/ppermute | solution.py:30
  15.6 0.2 collective-permute-start.7
  15.8 1.8 %collective-permute-start.3 = (bf16[64,1792]{1,0:T(8,128)(2,1)S(1)}, bf16[64,1792]{1,0:T(8,128)(2,1)S(1)}, u32[]{:S(2)}, u32[]{:S(2)}) collective-permute-start(bf16[64,1792]{1,0:T(8,128)(2,1)S(1)} %get-tuple-element.50.rest_0_), channel_id=1, source_target_pairs={{0,2},{2,4},{4,6},{6,7},{7,5},{5,3},{3,1},{1,0},{8,10},{10,12},{12... | collective-permute-start | bytes 688136 | tf_op jit(solution)/shard_map/ppermute | solution.py:30
  17.6 0.2 collective-permute-start.4
  17.8 0.6 fusion
  18.6 0.1 broadcast_in_dim_reshape.9.bias
  18.7 0.1 broadcast_in_dim_reshape.10.rate
  18.9 0.1 broadcast_in_dim_reshape.11.skip
  19.1 1.2 %copy-done.3 = bf16[3584,128]{1,0:T(8,128)(2,1)S(1)} copy-done((bf16[3584,128]{1,0:T(8,128)(2,1)S(1)}, bf16[3584,128]{1,0:T(8,128)(2,1)}, u32[]{:S(2)}) %copy-start.3) | copy-done | bytes 917528
  20.2 1.2 %copy-done.6 = f32[512,512]{1,0:T(8,128)S(1)} copy-done((f32[512,512]{1,0:T(8,128)S(1)}, f32[512,512]{1,0:T(8,128)}, u32[]{:S(2)}) %copy-start.6) | copy-done | bytes 1048600
  21.5 2.9 %shard_map.128.refs_5_ = f32[512,512]{1,0:T(8,128)S(1)} custom-call(bf16[448,512]{1,0:T(8,128)(2,1)} %collective-permute-done.refs_0_, bf16[448,512]{1,0:T(8,128)(2,1)S(1)} %collective-permute-done.2.refs_1_, bf16[2,3584,128]{2,1,0:T(8,128)(2,1)} %refs_2_.7, bf16[3584,128]{1,0:T(8,128)(2,1)S(1)} %copy-done.3, ...), custom_call_target="tpu_custom_call" | custom-call | flops 1000000000 | bytes 2097152 | tf_op jit(solution)/shard_map/pallas_call | solution.py:344
  24.4 7.3 %collective-permute-done.3.rest_2_ = bf16[64,1792]{1,0:T(8,128)(2,1)S(1)} collective-permute-done((bf16[64,1792]{1,0:T(8,128)(2,1)S(1)}, bf16[64,1792]{1,0:T(8,128)(2,1)S(1)}, u32[]{:S(2)}, u32[]{:S(2)}) %collective-permute-start.3) | collective-permute-done | bytes 229408 | tf_op jit(solution)/shard_map/ppermute | solution.py:30
  31.6 1.2 %collective-permute-done.4.rest_4_ = bf16[64,1792]{1,0:T(8,128)(2,1)} collective-permute-done((bf16[64,1792]{1,0:T(8,128)(2,1)S(1)}, bf16[64,1792]{1,0:T(8,128)(2,1)}, u32[]{:S(2)}, u32[]{:S(2)}) %collective-permute-start.4) | collective-permute-done | bytes 229408 | tf_op jit(solution)/shard_map/ppermute | solution.py:30
  32.8 0.5 collective-permute-start.8
  33.3 1.6 %collective-permute-start.6 = (bf16[448,512]{1,0:T(8,128)(2,1)}, bf16[448,512]{1,0:T(8,128)(2,1)S(1)}, u32[]{:S(2)}, u32[]{:S(2)}) collective-permute-start(bf16[448,512]{1,0:T(8,128)(2,1)} %collective-permute-done.1.refs_0_), channel_id=1, source_target_pairs={{0,2},{2,4},{4,6},{6,7},{7,5},{5,3},{3,1},{1,0},{8,10},{10,12},{12... | collective-permute-start | bytes 1376264 | tf_op jit(solution)/shard_map/ppermute | solution.py:30
  34.9 0.4 collective-permute-start.12
  35.4 1.6 %collective-permute-start.9 = (bf16[64,1792]{1,0:T(8,128)(2,1)}, bf16[64,1792]{1,0:T(8,128)(2,1)S(1)}, u32[]{:S(2)}, u32[]{:S(2)}) collective-permute-start(bf16[64,1792]{1,0:T(8,128)(2,1)} %collective-permute-done.4.rest_4_), channel_id=1, source_target_pairs={{0,16},{8,24},{16,0},{24,8},{1,17},{9,25},{17,1},{25,9},{2,18},{10... | collective-permute-start | bytes 688136 | tf_op jit(solution)/shard_map/ppermute | solution.py:309
  36.9 1.6 %collective-permute-start.10 = (bf16[64,1792]{1,0:T(8,128)(2,1)S(1)}, bf16[64,1792]{1,0:T(8,128)(2,1)}, u32[]{:S(2)}, u32[]{:S(2)}) collective-permute-start(bf16[64,1792]{1,0:T(8,128)(2,1)S(1)} %collective-permute-done.3.rest_2_), channel_id=1, source_target_pairs={{0,2},{2,4},{4,6},{6,7},{7,5},{5,3},{3,1},{1,0},{8,10},{10,12},{12... | collective-permute-start | bytes 688136 | tf_op jit(solution)/shard_map/ppermute | solution.py:30
  38.5 2.9 %collective-permute-done.8.rest_3_ = bf16[64,1792]{1,0:T(8,128)(2,1)S(1)} collective-permute-done((bf16[64,1792]{1,0:T(8,128)(2,1)S(1)}, bf16[64,1792]{1,0:T(8,128)(2,1)S(1)}, u32[]{:S(2)}, u32[]{:S(2)}) %collective-permute-start.8) | collective-permute-done | bytes 229408 | tf_op jit(solution)/shard_map/ppermute | solution.py:309
  41.4 0.4 collective-permute-start.11
  41.9 3.0 %shard_map.129.refs_5_ = f32[512,512]{1,0:T(8,128)S(1)} custom-call(bf16[448,512]{1,0:T(8,128)(2,1)} %collective-permute-done.1.refs_0_, bf16[448,512]{1,0:T(8,128)(2,1)} %collective-permute-done.7.refs_1_, bf16[2,3584,128]{2,1,0:T(8,128)(2,1)} %refs_2_.7, bf16[3584,128]{1,0:T(8,128)(2,1)S(1)} %copy-done.3, ...), custom_call_target="tpu_custom_call" | custom-call | flops 1000000000 | bytes 2097152 | tf_op jit(solution)/shard_map/pallas_call | solution.py:344
  44.9 4.6 %collective-permute-done.10.rest_6_ = bf16[64,1792]{1,0:T(8,128)(2,1)} collective-permute-done((bf16[64,1792]{1,0:T(8,128)(2,1)S(1)}, bf16[64,1792]{1,0:T(8,128)(2,1)}, u32[]{:S(2)}, u32[]{:S(2)}) %collective-permute-start.10) | collective-permute-done | bytes 229408 | tf_op jit(solution)/shard_map/ppermute | solution.py:30
  49.5 1.3 %collective-permute-done.11.rest_8_ = bf16[64,1792]{1,0:T(8,128)(2,1)} collective-permute-done((bf16[64,1792]{1,0:T(8,128)(2,1)}, bf16[64,1792]{1,0:T(8,128)(2,1)}, u32[]{:S(2)}, u32[]{:S(2)}) %collective-permute-start.11) | collective-permute-done | bytes 229408 | tf_op jit(solution)/shard_map/ppermute | solution.py:30
  50.8 1.6 %collective-permute-start.13 = (bf16[224,512]{1,0:T(8,128)(2,1)S(1)}, bf16[224,512]{1,0:T(8,128)(2,1)S(1)}, u32[]{:S(2)}, u32[]{:S(2)}) collective-permute-start(bf16[224,512]{1,0:T(8,128)(2,1)S(1)} %get-tuple-element.59), channel_id=1, source_target_pairs={{0,2},{2,4},{4,6},{6,7},{7,5},{5,3},{3,1},{1,0},{8,10},{10,12},{12... | collective-permute-start | bytes 688136 | tf_op jit(solution)/shard_map/ppermute | solution.py:30
  52.5 0.5 collective-permute-start.14
  52.9 1.7 %collective-permute-start.16 = (bf16[64,1792]{1,0:T(8,128)(2,1)}, bf16[64,1792]{1,0:T(8,128)(2,1)}, u32[]{:S(2)}, u32[]{:S(2)}) collective-permute-start(bf16[64,1792]{1,0:T(8,128)(2,1)} %collective-permute-done.10.rest_6_), channel_id=1, source_target_pairs={{0,16},{8,24},{16,0},{24,8},{1,17},{9,25},{17,1},{25,9},{2,18},{10... | collective-permute-start | bytes 688136 | tf_op jit(solution)/shard_map/ppermute | solution.py:309
  54.6 0.3 collective-permute-start.17
  54.9 2.0 %collective-permute-done.13.top = bf16[224,512]{1,0:T(8,128)(2,1)S(1)} collective-permute-done((bf16[224,512]{1,0:T(8,128)(2,1)S(1)}, bf16[224,512]{1,0:T(8,128)(2,1)S(1)}, u32[]{:S(2)}, u32[]{:S(2)}) %collective-permute-start.13) | collective-permute-done | bytes 229408 | tf_op jit(solution)/shard_map/ppermute | solution.py:30
  56.9 1.6 %collective-permute-done.14.bottom = bf16[224,512]{1,0:T(8,128)(2,1)S(1)} collective-permute-done((bf16[224,512]{1,0:T(8,128)(2,1)S(1)}, bf16[224,512]{1,0:T(8,128)(2,1)S(1)}, u32[]{:S(2)}, u32[]{:S(2)}) %collective-permute-start.14) | collective-permute-done | bytes 229408 | tf_op jit(solution)/shard_map/ppermute | solution.py:30
  58.5 1.8 %collective-permute-start.18 = (bf16[64,1792]{1,0:T(8,128)(2,1)}, bf16[64,1792]{1,0:T(8,128)(2,1)}, u32[]{:S(2)}, u32[]{:S(2)}) collective-permute-start(bf16[64,1792]{1,0:T(8,128)(2,1)} %collective-permute-done.10.rest_6_), channel_id=1, source_target_pairs={{0,2},{2,4},{4,6},{6,7},{7,5},{5,3},{3,1},{1,0},{8,10},{10,12},{12... | collective-permute-start | bytes 688136 | tf_op jit(solution)/shard_map/ppermute | solution.py:30
  60.3 0.2 collective-permute-start.19
  60.5 1.9 %shard_map.131 = (f32[512,512]{1,0:T(8,128)S(1)}, bf16[448,512]{1,0:T(8,128)(2,1)S(1)}) custom-call(bf16[448,512]{1,0:T(8,128)(2,1)S(1)} %collective-permute-done.6.forth.refs_0_, bf16[448,512]{1,0:T(8,128)(2,1)S(1)} %collective-permute-done.12.back.refs_1_, bf16[2,3584,128]{2,1,0:T(8,128)(2,1)} %refs_2_.7, bf16[3584,128]{1,0:T(8,128)(2,1)S(1)} %copy-done.4, ...), custom_call_target="tpu_custom_call" | custom-call | flops 1000000000 | bytes 2097152 | tf_op jit(solution)/shard_map/pallas_call | solution.py:344
  62.4 0.5 shard_map.132.proj
  62.9 1.3 %collective-permute-start.15 = (bf16[8,256]{1,0:T(8,128)(2,1)S(1)}, bf16[8,256]{1,0:T(8,128)(2,1)S(1)}, u32[]{:S(2)}, u32[]{:S(2)}) collective-permute-start(bf16[8,256]{1,0:T(8,128)(2,1)S(1)} %slice.44), channel_id=1, source_target_pairs={{0,8},{8,16},{16,24},{1,9},{9,17},{17,25},{2,10},{10,18},{18,26},{... | collective-permute-start | bytes 12296 | tf_op jit(solution)/shard_map/ppermute | solution.py:357
  64.2 0.1 copy.16.seg_ext
  64.4 0.1 copy.17.seg_ext.seg_col
  64.5 1.0 shard_map.133
  65.6 1.2 %shard_map.134 = (f32[256,128]{1,0:T(8,128)S(1)}, f32[256,128]{1,0:T(8,128)S(1)}, f32[256,128]{1,0:T(8,128)S(1)}, f32[256,128]{1,0:T(8,128)S(1)}, f32[256,128]{1...) custom-call(f32[512,512]{1,0:T(8,128)S(1)} %shard_map.132.proj, ...), custom_call_target="tpu_custom_call" | custom-call | flops 10000000 | bytes 2097152 | tf_op jit(solution)/shard_map/pallas_call | solution.py:368
  66.8 0.5 shard_map.135
  67.3 7.6 %all-gather = f32[288,128]{1,0:T(8,128)S(1)} all-gather(f32[72,128]{1,0:T(8,128)S(1)} %get-tuple-element.67), channel_id=2, replica_groups=mesh['seq'=4,'tensor'=8] {'seq'}, dimensions={0}, use_global_device_ids=true | all-gather | bytes 184320 | tf_op jit(solution)/shard_map/all_gather | solution.py:373
  74.9 1.8 %collective-permute-start.20 = (bf16[64,1792]{1,0:T(8,128)(2,1)}, bf16[64,1792]{1,0:T(8,128)(2,1)S(1)}, u32[]{:S(2)}, u32[]{:S(2)}) collective-permute-start(bf16[64,1792]{1,0:T(8,128)(2,1)} %collective-permute-done.18.rest_10_), channel_id=1, source_target_pairs={{0,2},{2,4},{4,6},{6,7},{7,5},{5,3},{3,1},{1,0},{8,10},{10,12},{12... | collective-permute-start | bytes 688136 | tf_op jit(solution)/shard_map/ppermute | solution.py:30
  76.6 1.8 %collective-permute-start.21 = (bf16[64,1792]{1,0:T(8,128)(2,1)}, bf16[64,1792]{1,0:T(8,128)(2,1)S(1)}, u32[]{:S(2)}, u32[]{:S(2)}) collective-permute-start(bf16[64,1792]{1,0:T(8,128)(2,1)} %collective-permute-done.18.rest_10_), channel_id=1, source_target_pairs={{0,16},{8,24},{16,0},{24,8},{1,17},{9,25},{17,1},{25,9},{2,18},{10... | collective-permute-start | bytes 688136 | tf_op jit(solution)/shard_map/ppermute | solution.py:309
  78.5 1.6 %shard_map.136 = bf16[512,128]{1,0:T(8,128)(2,1)} custom-call(s32[1,1]{1,0:T(1,128)} %bitcast.seg_first, f32[4,72,128]{2,1,0:T(8,128)S(1)} %bitcast.11, f32[256,128]{1,0:T(8,128)S(1)} %get-tuple-element.75.out_a, f32[256,128]{1,0:T(8,128)S(1)} %get-tuple-element.76.gate_a, f32[256,128]{1,0:T(8,128)S(1)} %get-tuple-element.72.conv_bc.bc_a, ...), custom_call_target="tpu_custom_call" | custom-call | flops 10000000 | bytes 2097152 | tf_op jit(solution)/shard_map/pallas_call | solution.py:377
  80.0 3.4 %all-to-all-start = ((bf16[8,64,128]{2,1,0:T(8,128)(2,1)}), bf16[8,64,128]{2,1,0:T(8,128)(2,1)S(1)}, u32[]{:S(2)}, u32[]{:S(2)}) async-start(bf16[8,64,128]{2,1,0:T(8,128)(2,1)} %bitcast.7), calls=%async_computation | async-start | bytes 262144 | tf_op jit(solution)/shard_map/all_to_all | solution.py:385
  83.4 0.3 collective-permute-start.22
  83.7 7.0 %all-to-all-done.mine = bf16[8,64,128]{2,1,0:T(8,128)(2,1)S(1)} async-done(((bf16[8,64,128]{2,1,0:T(8,128)(2,1)}), bf16[8,64,128]{2,1,0:T(8,128)(2,1)S(1)}, u32[]{:S(2)}, u32[]{:S(2)}) %all-to-all-start) | async-done | bytes 131104 | tf_op jit(solution)/shard_map/all_to_all | solution.py:385
  90.7 0.3 collective-permute-done.22.rest_13_
  91.0 0.3 collective-permute-start.24
  91.3 1.3 %collective-permute-done.23.other = bf16[8,64,128]{2,1,0:T(8,128)(2,1)S(1)} collective-permute-done((bf16[8,64,128]{2,1,0:T(8,128)(2,1)S(1)}, bf16[8,64,128]{2,1,0:T(8,128)(2,1)S(1)}, u32[]{:S(2)}, u32[]{:S(2)}) %collective-permute-start.23) | collective-permute-done | bytes 131104 | tf_op jit(solution)/shard_map/ppermute | solution.py:389
  92.6 2.5 %shard_map.137.total = f32[128,1792]{1,0:T(8,128)S(1)} custom-call(bf16[8,64,128]{2,1,0:T(8,128)(2,1)S(1)} %all-to-all-done.mine, bf16[8,64,128]{2,1,0:T(8,128)(2,1)S(1)} %collective-permute-done.23.other, bf16[64,1792]{1,0:T(8,128)(2,1)S(1)} %get-tuple-element.50.rest_0_, bf16[64,1792]{1,0:T(8,128)(2,1)S(1)} %get-tuple-element.91.rest_1_, ...), custom_call_target="tpu_custom_call" | custom-call | flops 1000000000 | bytes 2097152 | tf_op jit(solution)/shard_map/pallas_call | solution.py:392
  95.2 2.3 %collective-permute-done.24.far = bf16[64,1792]{1,0:T(8,128)(2,1)S(1)} collective-permute-done((bf16[64,1792]{1,0:T(8,128)(2,1)S(1)}, bf16[64,1792]{1,0:T(8,128)(2,1)S(1)}, u32[]{:S(2)}, u32[]{:S(2)}) %collective-permute-start.24) | collective-permute-done | bytes 229408 | tf_op jit(solution)/shard_map/ppermute | solution.py:309
  97.4 0.3 shard_map.138
  97.9 1.5 %collective-permute-done.25 = bf16[64,1792]{1,0:T(8,128)(2,1)S(1)} collective-permute-done((bf16[64,1792]{1,0:T(8,128)(2,1)S(1)}, bf16[64,1792]{1,0:T(8,128)(2,1)S(1)}, u32[]{:S(2)}, u32[]{:S(2)}) %collective-permute-start.25) | collective-permute-done | bytes 229408 | tf_op jit(solution)/shard_map/ppermute | solution.py:399
  99.4 0.8 pad_maximum_fusion
  (53 shorter events, 0.6 us)
Async XLA Ops:
  0.0 6.5 %copy-start = (bf16[3584,2]{0,1:T(2,128)(2,1)S(1)}, bf16[3584,2]{0,1:T(2,128)(2,1)}, u32[]{:S(2)}) copy-start(bf16[3584,2]{0,1:T(2,128)(2,1)} %param.16) | copy-start | bytes 43012
  0.0 7.6 %copy-start.1 = (bf16[2,3584,128]{2,1,0:T(8,128)(2,1)S(1)}, bf16[2,3584,128]{2,1,0:T(8,128)(2,1)}, u32[]{:S(2)}) copy-start(bf16[2,3584,128]{2,1,0:T(8,128)(2,1)} %refs_2_.7) | copy-start | bytes 5505028
  0.0 13.8 %collective-permute-start = (bf16[448,512]{1,0:T(8,128)(2,1)}, bf16[448,512]{1,0:T(8,128)(2,1)}, u32[]{:S(2)}, u32[]{:S(2)}) collective-permute-start(bf16[448,512]{1,0:T(8,128)(2,1)} %bitcast.12), channel_id=1, source_target_pairs={{0,2},{2,4},{4,6},{6,7},{7,5},{5,3},{3,1},{1,0},{8,10},{10,12},{12... | collective-permute-start | bytes 1376264 | tf_op jit(solution)/shard_map/ppermute | solution.py:30
  3.0 12.6 %collective-permute-start.2 = (bf16[448,512]{1,0:T(8,128)(2,1)}, bf16[448,512]{1,0:T(8,128)(2,1)S(1)}, u32[]{:S(2)}, u32[]{:S(2)}) collective-permute-start(bf16[448,512]{1,0:T(8,128)(2,1)} %bitcast.13), channel_id=1, source_target_pairs={{0,1},{2,0},{4,2},{6,4},{7,6},{5,7},{3,5},{1,3},{8,9},{10,8},{12,1... | collective-permute-start | bytes 1376264 | tf_op jit(solution)/shard_map/ppermute | solution.py:30
  3.8 15.2 %collective-permute-start.5 = (s32[8]{0:T(128)S(1)}, s32[8]{0:T(128)S(1)}, u32[]{:S(2)}, u32[]{:S(2)}) collective-permute-start(s32[8]{0:T(128)S(1)} %slice.33), channel_id=1, source_target_pairs={{0,8},{8,16},{16,24},{1,9},{9,17},{17,25},{2,10},{10,18},{18,26},{... | collective-permute-start | bytes 104 | tf_op jit(solution)/shard_map/ppermute | solution.py:314
  7.6 1.2 %copy-start.2 = (bf16[3584,128]{1,0:T(8,128)(2,1)S(1)}, bf16[3584,128]{1,0:T(8,128)(2,1)}, u32[]{:S(2)}) copy-start(bf16[3584,128]{1,0:T(8,128)(2,1)} %refs_3_.5) | copy-start | bytes 2752516
  8.8 1.0 %copy-start.7 = (bf16[512,448]{0,1:T(8,128)(2,1)S(1)}, bf16[512,448]{0,1:T(8,128)(2,1)}, u32[]{:S(2)}) copy-start(bf16[512,448]{0,1:T(8,128)(2,1)} %param.13) | copy-start | bytes 1376260
  9.8 6.0 %copy-start.10 = (s32[512]{0:T(512)S(1)}, s32[512]{0:T(512)}, u32[]{:S(2)}) copy-start(s32[512]{0:T(512)} %param.24) | copy-start | bytes 6148
  9.8 8.7 %copy-start.11 = (f32[2]{0:T(128)S(1)}, f32[2]{0:T(128)}, u32[]{:S(2)}) copy-start(f32[2]{0:T(128)} %param.17) | copy-start | bytes 28
  9.8 8.8 %copy-start.12 = (f32[2]{0:T(128)S(1)}, f32[2]{0:T(128)}, u32[]{:S(2)}) copy-start(f32[2]{0:T(128)} %param.18) | copy-start | bytes 28
  9.8 9.0 %copy-start.13 = (f32[2]{0:T(128)S(1)}, f32[2]{0:T(128)}, u32[]{:S(2)}) copy-start(f32[2]{0:T(128)} %param.19) | copy-start | bytes 28
  10.5 1.0 copy-start.5
  13.8 19.0 %collective-permute-start.1 = (bf16[448,512]{1,0:T(8,128)(2,1)}, bf16[448,512]{1,0:T(8,128)(2,1)}, u32[]{:S(2)}, u32[]{:S(2)}) collective-permute-start(bf16[448,512]{1,0:T(8,128)(2,1)} %collective-permute-done.refs_0_), channel_id=1, source_target_pairs={{0,2},{2,4},{4,6},{6,7},{7,5},{5,3},{3,1},{1,0},{8,10},{10,12},{12... | collective-permute-start | bytes 1376264 | tf_op jit(solution)/shard_map/ppermute | solution.py:30
  15.6 17.2 %collective-permute-start.7 = (bf16[448,512]{1,0:T(8,128)(2,1)S(1)}, bf16[448,512]{1,0:T(8,128)(2,1)}, u32[]{:S(2)}, u32[]{:S(2)}) collective-permute-start(bf16[448,512]{1,0:T(8,128)(2,1)S(1)} %collective-permute-done.2.refs_1_), channel_id=1, source_target_pairs={{0,1},{2,0},{4,2},{6,4},{7,6},{5,7},{3,5},{1,3},{8,9},{10,8},{12,1... | collective-permute-start | bytes 1376264 | tf_op jit(solution)/shard_map/ppermute | solution.py:30
  15.8 15.8 %collective-permute-start.3 = (bf16[64,1792]{1,0:T(8,128)(2,1)S(1)}, bf16[64,1792]{1,0:T(8,128)(2,1)S(1)}, u32[]{:S(2)}, u32[]{:S(2)}) collective-permute-start(bf16[64,1792]{1,0:T(8,128)(2,1)S(1)} %get-tuple-element.50.rest_0_), channel_id=1, source_target_pairs={{0,2},{2,4},{4,6},{6,7},{7,5},{5,3},{3,1},{1,0},{8,10},{10,12},{12... | collective-permute-start | bytes 688136 | tf_op jit(solution)/shard_map/ppermute | solution.py:30
  17.6 15.2 %collective-permute-start.4 = (bf16[64,1792]{1,0:T(8,128)(2,1)S(1)}, bf16[64,1792]{1,0:T(8,128)(2,1)}, u32[]{:S(2)}, u32[]{:S(2)}) collective-permute-start(bf16[64,1792]{1,0:T(8,128)(2,1)S(1)} %get-tuple-element.50.rest_0_), channel_id=1, source_target_pairs={{0,1},{2,0},{4,2},{6,4},{7,6},{5,7},{3,5},{1,3},{8,9},{10,8},{12,1... | collective-permute-start | bytes 688136 | tf_op jit(solution)/shard_map/ppermute | solution.py:30
  19.1 1.2 %copy-start.3 = (bf16[3584,128]{1,0:T(8,128)(2,1)S(1)}, bf16[3584,128]{1,0:T(8,128)(2,1)}, u32[]{:S(2)}) copy-start(bf16[3584,128]{1,0:T(8,128)(2,1)} %refs_3_.5) | copy-start | bytes 2752516
  20.2 1.2 %copy-start.6 = (f32[512,512]{1,0:T(8,128)S(1)}, f32[512,512]{1,0:T(8,128)}, u32[]{:S(2)}) copy-start(f32[512,512]{1,0:T(8,128)} %copy-done.5) | copy-start | bytes 3145732
  32.8 27.7 %copy-start.4 = (bf16[3584,128]{1,0:T(8,128)(2,1)S(1)}, bf16[3584,128]{1,0:T(8,128)(2,1)}, u32[]{:S(2)}) copy-start(bf16[3584,128]{1,0:T(8,128)(2,1)} %refs_3_.5) | copy-start | bytes 2752516
  32.8 8.6 %collective-permute-start.8 = (bf16[64,1792]{1,0:T(8,128)(2,1)S(1)}, bf16[64,1792]{1,0:T(8,128)(2,1)S(1)}, u32[]{:S(2)}, u32[]{:S(2)}) collective-permute-start(bf16[64,1792]{1,0:T(8,128)(2,1)S(1)} %collective-permute-done.3.rest_2_), channel_id=1, source_target_pairs={{0,16},{8,24},{16,0},{24,8},{1,17},{9,25},{17,1},{25,9},{2,18},{10... | collective-permute-start | bytes 688136 | tf_op jit(solution)/shard_map/ppermute | solution.py:309
  33.3 17.5 %collective-permute-start.6 = (bf16[448,512]{1,0:T(8,128)(2,1)}, bf16[448,512]{1,0:T(8,128)(2,1)S(1)}, u32[]{:S(2)}, u32[]{:S(2)}) collective-permute-start(bf16[448,512]{1,0:T(8,128)(2,1)} %collective-permute-done.1.refs_0_), channel_id=1, source_target_pairs={{0,2},{2,4},{4,6},{6,7},{7,5},{5,3},{3,1},{1,0},{8,10},{10,12},{12... | collective-permute-start | bytes 1376264 | tf_op jit(solution)/shard_map/ppermute | solution.py:30
  34.9 15.9 %collective-permute-start.12 = (bf16[448,512]{1,0:T(8,128)(2,1)}, bf16[448,512]{1,0:T(8,128)(2,1)S(1)}, u32[]{:S(2)}, u32[]{:S(2)}) collective-permute-start(bf16[448,512]{1,0:T(8,128)(2,1)} %collective-permute-done.7.refs_1_), channel_id=1, source_target_pairs={{0,1},{2,0},{4,2},{6,4},{7,6},{5,7},{3,5},{1,3},{8,9},{10,8},{12,1... | collective-permute-start | bytes 1376264 | tf_op jit(solution)/shard_map/ppermute | solution.py:30
  35.4 9.5 %collective-permute-start.9 = (bf16[64,1792]{1,0:T(8,128)(2,1)}, bf16[64,1792]{1,0:T(8,128)(2,1)S(1)}, u32[]{:S(2)}, u32[]{:S(2)}) collective-permute-start(bf16[64,1792]{1,0:T(8,128)(2,1)} %collective-permute-done.4.rest_4_), channel_id=1, source_target_pairs={{0,16},{8,24},{16,0},{24,8},{1,17},{9,25},{17,1},{25,9},{2,18},{10... | collective-permute-start | bytes 688136 | tf_op jit(solution)/shard_map/ppermute | solution.py:309
  36.9 12.5 %collective-permute-start.10 = (bf16[64,1792]{1,0:T(8,128)(2,1)S(1)}, bf16[64,1792]{1,0:T(8,128)(2,1)}, u32[]{:S(2)}, u32[]{:S(2)}) collective-permute-start(bf16[64,1792]{1,0:T(8,128)(2,1)S(1)} %collective-permute-done.3.rest_2_), channel_id=1, source_target_pairs={{0,2},{2,4},{4,6},{6,7},{7,5},{5,3},{3,1},{1,0},{8,10},{10,12},{12... | collective-permute-start | bytes 688136 | tf_op jit(solution)/shard_map/ppermute | solution.py:30
  41.4 9.4 %collective-permute-start.11 = (bf16[64,1792]{1,0:T(8,128)(2,1)}, bf16[64,1792]{1,0:T(8,128)(2,1)}, u32[]{:S(2)}, u32[]{:S(2)}) collective-permute-start(bf16[64,1792]{1,0:T(8,128)(2,1)} %collective-permute-done.4.rest_4_), channel_id=1, source_target_pairs={{0,1},{2,0},{4,2},{6,4},{7,6},{5,7},{3,5},{1,3},{8,9},{10,8},{12,1... | collective-permute-start | bytes 688136 | tf_op jit(solution)/shard_map/ppermute | solution.py:30
  50.8 6.1 %collective-permute-start.13 = (bf16[224,512]{1,0:T(8,128)(2,1)S(1)}, bf16[224,512]{1,0:T(8,128)(2,1)S(1)}, u32[]{:S(2)}, u32[]{:S(2)}) collective-permute-start(bf16[224,512]{1,0:T(8,128)(2,1)S(1)} %get-tuple-element.59), channel_id=1, source_target_pairs={{0,2},{2,4},{4,6},{6,7},{7,5},{5,3},{3,1},{1,0},{8,10},{10,12},{12... | collective-permute-start | bytes 688136 | tf_op jit(solution)/shard_map/ppermute | solution.py:30
  52.5 6.0 %collective-permute-start.14 = (bf16[224,512]{1,0:T(8,128)(2,1)S(1)}, bf16[224,512]{1,0:T(8,128)(2,1)S(1)}, u32[]{:S(2)}, u32[]{:S(2)}) collective-permute-start(bf16[224,512]{1,0:T(8,128)(2,1)S(1)} %get-tuple-element.60), channel_id=1, source_target_pairs={{0,1},{2,0},{4,2},{6,4},{7,6},{5,7},{3,5},{1,3},{8,9},{10,8},{12,1... | collective-permute-start | bytes 688136 | tf_op jit(solution)/shard_map/ppermute | solution.py:30
  52.9 12.6 %collective-permute-start.16 = (bf16[64,1792]{1,0:T(8,128)(2,1)}, bf16[64,1792]{1,0:T(8,128)(2,1)}, u32[]{:S(2)}, u32[]{:S(2)}) collective-permute-start(bf16[64,1792]{1,0:T(8,128)(2,1)} %collective-permute-done.10.rest_6_), channel_id=1, source_target_pairs={{0,16},{8,24},{16,0},{24,8},{1,17},{9,25},{17,1},{25,9},{2,18},{10... | collective-permute-start | bytes 688136 | tf_op jit(solution)/shard_map/ppermute | solution.py:309
  54.6 10.9 %collective-permute-start.17 = (bf16[64,1792]{1,0:T(8,128)(2,1)}, bf16[64,1792]{1,0:T(8,128)(2,1)}, u32[]{:S(2)}, u32[]{:S(2)}) collective-permute-start(bf16[64,1792]{1,0:T(8,128)(2,1)} %collective-permute-done.11.rest_8_), channel_id=1, source_target_pairs={{0,16},{8,24},{16,0},{24,8},{1,17},{9,25},{17,1},{25,9},{2,18},{10... | collective-permute-start | bytes 688136 | tf_op jit(solution)/shard_map/ppermute | solution.py:309
  58.5 16.4 %collective-permute-start.18 = (bf16[64,1792]{1,0:T(8,128)(2,1)}, bf16[64,1792]{1,0:T(8,128)(2,1)}, u32[]{:S(2)}, u32[]{:S(2)}) collective-permute-start(bf16[64,1792]{1,0:T(8,128)(2,1)} %collective-permute-done.10.rest_6_), channel_id=1, source_target_pairs={{0,2},{2,4},{4,6},{6,7},{7,5},{5,3},{3,1},{1,0},{8,10},{10,12},{12... | collective-permute-start | bytes 688136 | tf_op jit(solution)/shard_map/ppermute | solution.py:30
  60.3 14.5 %collective-permute-start.19 = (bf16[64,1792]{1,0:T(8,128)(2,1)}, bf16[64,1792]{1,0:T(8,128)(2,1)}, u32[]{:S(2)}, u32[]{:S(2)}) collective-permute-start(bf16[64,1792]{1,0:T(8,128)(2,1)} %collective-permute-done.11.rest_8_), channel_id=1, source_target_pairs={{0,1},{2,0},{4,2},{6,4},{7,6},{5,7},{3,5},{1,3},{8,9},{10,8},{12,1... | collective-permute-start | bytes 688136 | tf_op jit(solution)/shard_map/ppermute | solution.py:30
  62.4 2.1 %copy-start.8 = (f32[4,128]{1,0:T(4,128)S(1)}, f32[4,128]{1,0:T(4,128)}, u32[]{:S(2)}) copy-start(f32[4,128]{1,0:T(4,128)} %taps_x.3) | copy-start | bytes 6148
  62.4 2.1 %copy-start.9 = (f32[4,128]{1,0:T(4,128)S(1)}, f32[4,128]{1,0:T(4,128)}, u32[]{:S(2)}) copy-start(f32[4,128]{1,0:T(4,128)} %taps_bc.3) | copy-start | bytes 6148
  62.9 2.6 %collective-permute-start.15 = (bf16[8,256]{1,0:T(8,128)(2,1)S(1)}, bf16[8,256]{1,0:T(8,128)(2,1)S(1)}, u32[]{:S(2)}, u32[]{:S(2)}) collective-permute-start(bf16[8,256]{1,0:T(8,128)(2,1)S(1)} %slice.44), channel_id=1, source_target_pairs={{0,8},{8,16},{16,24},{1,9},{9,17},{17,25},{2,10},{10,18},{18,26},{... | collective-permute-start | bytes 12296 | tf_op jit(solution)/shard_map/ppermute | solution.py:357
  74.9 15.8 %collective-permute-start.20 = (bf16[64,1792]{1,0:T(8,128)(2,1)}, bf16[64,1792]{1,0:T(8,128)(2,1)S(1)}, u32[]{:S(2)}, u32[]{:S(2)}) collective-permute-start(bf16[64,1792]{1,0:T(8,128)(2,1)} %collective-permute-done.18.rest_10_), channel_id=1, source_target_pairs={{0,2},{2,4},{4,6},{6,7},{7,5},{5,3},{3,1},{1,0},{8,10},{10,12},{12... | collective-permute-start | bytes 688136 | tf_op jit(solution)/shard_map/ppermute | solution.py:30
  76.6 14.1 %collective-permute-start.21 = (bf16[64,1792]{1,0:T(8,128)(2,1)}, bf16[64,1792]{1,0:T(8,128)(2,1)S(1)}, u32[]{:S(2)}, u32[]{:S(2)}) collective-permute-start(bf16[64,1792]{1,0:T(8,128)(2,1)} %collective-permute-done.18.rest_10_), channel_id=1, source_target_pairs={{0,16},{8,24},{16,0},{24,8},{1,17},{9,25},{17,1},{25,9},{2,18},{10... | collective-permute-start | bytes 688136 | tf_op jit(solution)/shard_map/ppermute | solution.py:309
  80.0 10.7 %all-to-all-start = ((bf16[8,64,128]{2,1,0:T(8,128)(2,1)}), bf16[8,64,128]{2,1,0:T(8,128)(2,1)S(1)}, u32[]{:S(2)}, u32[]{:S(2)}) async-start(bf16[8,64,128]{2,1,0:T(8,128)(2,1)} %bitcast.7), calls=%async_computation | async-start | bytes 262144 | tf_op jit(solution)/shard_map/all_to_all | solution.py:385
  83.4 7.6 %collective-permute-start.22 = (bf16[64,1792]{1,0:T(8,128)(2,1)}, bf16[64,1792]{1,0:T(8,128)(2,1)S(1)}, u32[]{:S(2)}, u32[]{:S(2)}) collective-permute-start(bf16[64,1792]{1,0:T(8,128)(2,1)} %collective-permute-done.19.rest_12_), channel_id=1, source_target_pairs={{0,16},{8,24},{16,0},{24,8},{1,17},{9,25},{17,1},{25,9},{2,18},{10... | collective-permute-start | bytes 688136 | tf_op jit(solution)/shard_map/ppermute | solution.py:309
  91.0 6.4 %collective-permute-start.24 = (bf16[64,1792]{1,0:T(8,128)(2,1)S(1)}, bf16[64,1792]{1,0:T(8,128)(2,1)S(1)}, u32[]{:S(2)}, u32[]{:S(2)}) collective-permute-start(bf16[64,1792]{1,0:T(8,128)(2,1)S(1)} %collective-permute-done.20.near), channel_id=1, source_target_pairs={{0,16},{8,24},{16,0},{24,8},{1,17},{9,25},{17,1},{25,9},{2,18},{10... | collective-permute-start | bytes 688136 | tf_op jit(solution)/shard_map/ppermute | solution.py:309
  91.3 1.3 %collective-permute-start.23 = (bf16[8,64,128]{2,1,0:T(8,128)(2,1)S(1)}, bf16[8,64,128]{2,1,0:T(8,128)(2,1)S(1)}, u32[]{:S(2)}, u32[]{:S(2)}) collective-permute-start(bf16[8,64,128]{2,1,0:T(8,128)(2,1)S(1)} %all-to-all-done.mine), channel_id=1, source_target_pairs={{0,8},{8,0},{16,24},{24,16},{1,9},{9,1},{17,25},{25,17},{2,10},{10... | collective-permute-start | bytes 393224 | tf_op jit(solution)/shard_map/ppermute | solution.py:389
  97.8 1.6 %collective-permute-start.25 = (bf16[64,1792]{1,0:T(8,128)(2,1)S(1)}, bf16[64,1792]{1,0:T(8,128)(2,1)S(1)}, u32[]{:S(2)}, u32[]{:S(2)}) collective-permute-start(bf16[64,1792]{1,0:T(8,128)(2,1)S(1)} %get-tuple-element.88), channel_id=1, source_target_pairs={{0,8},{8,0},{16,24},{24,16},{1,9},{9,1},{17,25},{25,17},{2,10},{10... | collective-permute-start | bytes 688136 | tf_op jit(solution)/shard_map/ppermute | solution.py:399

commit v9 on v7

--- a/solution.py
+++ b/solution.py
@@ -45,15 +45,6 @@
     size = top.shape[0]
     top[...] = forth[:size]
     bottom[...] = back[size:]
-
-
-def join(*refs):
-    count = len(refs) // 3
-    odd = lax.axis_index("seq") // 2 % 2
-    for own, other, out in zip(refs[:count], refs[count : 2 * count], refs[2 * count :]):
-        size = own.shape[0]
-        out[pl.ds(pl.multiple_of(odd * size, size), size)] = own[...]
-        out[pl.ds(pl.multiple_of((1 - odd) * size, size), size)] = other[...]
 
 
 def silu(v):
@@ -95,13 +86,6 @@
         copy.wait()
 
 
-def project_far(top, bottom, weights, total, out):
-    cut = top.shape[0]
-    out[...] = (
-        total[...] + dot(top[...], weights[:cut], ((0,), (0,))) + dot(bottom[...], weights[cut:], ((0,), (0,)))
-    )
-
-
 def conv(ext, seg_ext, taps, rows):
     size = taps.shape[0]
     seg_now = seg_ext[HALO : HALO + rows]
@@ -214,17 +198,26 @@
     message[state_w + 2 :] = jnp.zeros((message.shape[0] - state_w - 2, width), F32)
 
 
-def first_inner(heads, width, rows, conv_x, conv_bc, cum, scaled, proj, seg_col, seg_row, skip, out, gate_out):
-    gate_out[...] = silu(proj[:rows, :width].astype(BF16).astype(F32))
-    out[...] = (
-        block_inner(conv_bc[...], cum[...], scaled[...], seg_col[HALO:], seg_row[...], heads) + skip[...] * conv_x[...]
-    )
-
-
-def finish(rows, seg_first, messages, out_a, gate_a, bc_a, enter_a, state_a, out_b, gate_b, bc_b, enter_b, gated):
+def front(heads, width, rows, top, bottom, weights, total, halo_part, halo_far, seg_ext_a, seg_ext_b, seg_row_b,
+          seg_last, taps_x, taps_bc, bias, rate, skip, out_b, bc_b, enter_b, gate_b, conv_a, bc_a, cum_a, scaled_a,
+          enter_a, gate_a, state_a, message, proj, state_b, ext_x, ext_bc):
+    cut = top.shape[0]
+    proj[...] = (
+        total[...] + dot(top[...], weights[:cut], ((0,), (0,))) + dot(bottom[...], weights[cut:], ((0,), (0,)))
+    )
+    halo = (halo_part[...] + dot(halo_far[...], weights[:, width : 3 * width])).astype(BF16)
+    later_block(heads, width, rows, proj, seg_ext_b, seg_row_b, taps_x, taps_bc, bias, rate, skip,
+                out_b, bc_b, enter_b, state_b, gate_b, ext_x, ext_bc)
+    gate_a[...] = silu(proj[:rows, :width].astype(BF16).astype(F32))
+    first_front(width, rows, proj, halo, seg_ext_a, seg_last, state_b, taps_x, taps_bc, bias, rate,
+                conv_a, bc_a, cum_a, scaled_a, enter_a, state_a, message, ext_x, ext_bc)
+
+
+def finish(heads, rows, seg_first, messages, seg_ext_a, seg_row_a, skip, conv_a, bc_a, cum_a, scaled_a, enter_a,
+           gate_a, state_a, out_b, bc_b, enter_b, gate_b, gated):
     state_w = bc_a.shape[1] // 2
-    entering = jnp.zeros((state_w, out_a.shape[1]), F32)
-    decay = jnp.zeros((1, out_a.shape[1]), F32)
+    entering = jnp.zeros((state_w, out_b.shape[1]), F32)
+    decay = jnp.zeros((1, out_b.shape[1]), F32)
     first = seg_first[...].astype(F32)
     place = lax.axis_index("seq")
     for device in reversed(range(messages.shape[0] - 1)):
@@ -234,7 +227,9 @@
         entering = entering + passes * messages[device, :state_w]
         decay = decay + jnp.where(earlier, messages[device, state_w : state_w + 1], 0.0)
     second = state_a[state_w : state_w + 1] * entering + state_a[:state_w]
-    gated[:rows] = ((out_a[...] + enter_a[...] * dot(bc_a[:, state_w:], entering)) * gate_a[...]).astype(BF16)
+    out_a = block_inner(bc_a[...], cum_a[...], scaled_a[...], seg_ext_a[HALO:], seg_row_a[...], heads)
+    out_a = out_a + skip[...] * conv_a[...]
+    gated[:rows] = ((out_a + enter_a[...] * dot(bc_a[:, state_w:], entering)) * gate_a[...]).astype(BF16)
     gated[rows:] = ((out_b[...] + enter_b[...] * dot(bc_b[:, state_w:], second)) * gate_b[...]).astype(BF16)
 
 
@@ -299,13 +294,22 @@
     own = (lax.dynamic_slice_in_dim(w_out, core * columns, columns, 1).astype(F32) * norm_gain[:, None]).astype(BF16)
     last = n_tensor // 2
     w_half = width // 2
-    own_rows = lax.dynamic_slice_in_dim(own, seq_at // 2 % 2 * w_half, w_half, 0)
-    other_y = [(i, i ^ 2) for i in range(n_seq)]
     shift_rows = [(i, i + 1) for i in range(n_seq - 1)]
 
     seg_halo = lax.ppermute(segments[tok_rows - HALO :], "seq", shift_rows)
     seg_all = jnp.concatenate([seg_halo, segments])[:, None]
+    order = [2 * i if i < last else 2 * n_tensor - 1 - 2 * i for i in range(n_tensor)]
+    halo_far = lax.ppermute(
+        tokens[tok_rows - HALO :],
+        ("seq", "tensor"),
+        [
+            (place * n_tensor + order[(i + last) % n_tensor], (place + 1) * n_tensor + order[i])
+            for place in range(n_seq - 1)
+            for i in range(n_tensor)
+        ],
+    )
     small = (
+        halo_far,
         (seg_all[: HALO + rows], seg_all[rows:]),
         (segments[None, :rows], segments[None, rows:]),
         (segments[None, :1], segments[None, tok_rows - 1 :]),
@@ -313,25 +317,20 @@
     )
 
     forth = back = block
+    w_steps = []
     arrived, projs = [(0, block)], []
     for step in range(1, last + 1):
-        if step == 3:
-            forth, back = after(forth, projs[1], small), after(back, projs[1], small)
-            w_arrived = after(w_arrived, forth, back)
-        elif step > 1:
-            forth, back = after(forth, projs[step - 2]), after(back, projs[step - 2])
-        if step == 4:
-            w_swapped, forth, back = after((w_swapped, forth, back))
-        if step == 2:
-            w_sent = after(own_rows, forth, back)
+        if step > 1:
+            ready = (projs[step - 2], small) if step == 3 else projs[step - 2]
+            forth, back = after(forth, ready), after(back, ready)
+        arrivals = (forth, back)
         if step < last:
             forth, back = ring_shift(forth, 1), ring_shift(back, -1)
         else:
             far = far_shift(forth, back)
         if step == 2:
-            w_arrived = ring_shift(w_sent, 1), ring_shift(w_sent, -1)
-        if step == 3:
-            w_swapped = [lax.ppermute(part, "seq", other_y) for part in w_arrived]
+            w_forth, w_back = after((own, own), arrivals)
+            w_steps.append((ring_shift(w_forth, 1), ring_shift(w_back, -1)))
         ahead = last if step == last else 0
         total = projs[-1:]
         fetched = len(arrived) + bool(ahead)
@@ -345,53 +344,34 @@
         )(*[part for _, part in arrived], w_zx, w_bc, w_step, *total)
         projs.append(results[0])
         arrived = [(-step, forth), (step, back)]
-    whole = shape(width, columns, kind=BF16)
-    w_forth, w_back = call(join, [whole, whole])(*w_arrived, *w_swapped)
-    proj = call(project_far, shape(tok_rows, 4 * width), flops=10**9)(
-        *far, results[1], after(projs[-1], w_forth, w_back)
-    )
-
-    (seg_ext_a, seg_ext_b), (seg_row_a, seg_row_b), (seg_first, seg_last), (bias, rate, skip) = small
-    halo = lax.ppermute(proj[tok_rows - HALO :, width : 3 * width].astype(BF16), "seq", shift_rows)
-
+    w_forth, w_back = after(w_steps[-1], projs[-1])
+    w_steps.append((ring_shift(w_forth, 1), ring_shift(w_back, -1)))
+    halo_part = lax.ppermute(projs[-1][tok_rows - HALO :, width : 3 * width], "seq", shift_rows)
+
+    halo_far, (seg_ext_a, seg_ext_b), (seg_row_a, seg_row_b), (seg_first, seg_last), (bias, rate, skip) = small
     msg_rows = state_w + 8
     plane = shape(rows, width)
+    state = shape(msg_rows, width)
     ext = pltpu.VMEM((HALO + rows, width), F32)
-    out_b, bc_b, enter_b, state_b, gate_b = call(
-        functools.partial(later_block, heads, width, rows),
-        [plane, plane, plane, shape(msg_rows, width), plane],
-        [ext, ext],
-    )(proj, seg_ext_b, seg_row_b, conv_x, conv_bc, bias, rate, skip)
-    cx_a, bc_a, cum_a, scaled_a, enter_a, state_a, message = call(
-        functools.partial(first_front, width, rows),
-        [plane] * 5 + [shape(msg_rows, width)] * 2,
-        [ext, ext],
-    )(proj, halo, seg_ext_a, seg_last, state_b, conv_x, conv_bc, bias, rate)
+    *kept, message = call(
+        functools.partial(front, heads, width, rows),
+        [plane] * 10 + [state] * 2,
+        [pltpu.VMEM((tok_rows, 4 * width), F32), pltpu.VMEM((msg_rows, width), F32), ext, ext],
+        flops=10**8,
+    )(*far, results[1], projs[-1], halo_part, halo_far, seg_ext_a, seg_ext_b, seg_row_b, seg_last,
+      conv_x, conv_bc, bias, rate, skip)
+    later, first = kept[:4], kept[4:]
     messages = lax.all_gather(message, "seq")
-    out_a, gate_a = call(functools.partial(first_inner, heads, width, rows), [plane, plane])(
-        cx_a, bc_a, cum_a, scaled_a, proj, seg_ext_a, seg_row_a, skip
-    )
-    gated = call(functools.partial(finish, rows), shape(tok_rows, width, kind=BF16))(
-        seg_first, messages, out_a, gate_a, bc_a, enter_a, state_a, out_b, gate_b, bc_b, enter_b
-    )
-
+    gated = call(functools.partial(finish, heads, rows), shape(tok_rows, width, kind=BF16))(
+        seg_first, messages, seg_ext_a, seg_row_a, skip, *first, *later
+    )
     tok_own = tok_rows // n_tensor
 
-    w_steps = [(w_forth, w_back)]
-    orders = [(proj, halo), messages]
-    for step in range(2, last + 1):
-        if step - 2 < len(orders):
-            w_forth, w_back = after((w_forth, w_back), orders[step - 2])
-        if step == 4:
-            w_forth, w_back = after((w_forth, w_back), mine)
-        if step == last:
-            w_far = far_shift(w_forth, w_back)
-            break
-        w_forth, w_back = ring_shift(w_forth, 1), ring_shift(w_back, -1)
-        w_steps.append((w_forth, w_back))
-        if step == 2:
-            blocks = after(gated, w_forth, w_back).reshape(n_tensor, tok_own, width)
-            mine = lax.all_to_all(blocks, "tensor", 0, 0)
+    mine = lax.all_to_all(gated.reshape(n_tensor, tok_own, width), "tensor", 0, 0)
+    for step in range(3, last):
+        w_forth, w_back = after(w_steps[-1], messages)
+        w_steps.append((ring_shift(w_forth, 1), ring_shift(w_back, -1)))
+    w_far = far_shift(*after(w_steps[-1], mine))
     swap = [(i, i ^ 1) for i in range(n_seq)]
     other = lax.ppermute(mine, "seq", swap)
     pieces, distances = [own], [0]

time: 97.1 us -> 109 us (1.12)
  starting transfers between devices: 22.3 us -> 28.5 us
  waiting for transfers between devices: 27.4 us -> 33.1 us
  local copies, waits for them, and re-layouts: 7.19 us -> 10.2 us
  blocking collectives: 21.2 us -> 18.4 us
    ppermute x16, waiting for transfers between devices: 21.6 us -> 29.8 us  [ring_shift(): lax.ppermute(block, 'tensor', [(order[i], order[(i + step) % n]) for i in...]
    ppermute x3 -> x2, starting transfers between devices: 3.32 us -> 7.01 us  [the longest x1 5.73 us: local(): lax.ppermute(tokens[tok_rows - HALO:], ('seq', 'tensor'), [(place * n_ten...]
    unnamed x26 -> x37, local copies, waits for them, and re-layouts: 4.25 us -> 6.91 us
    ppermute x1, starting transfers between devices: 1.45 us -> 4.09 us  [local(): seg_halo = lax.ppermute(segments[tok_rows - HALO:], 'seq', shift_rows)]
    ppermute x3 -> x2, waiting for transfers between devices: 2.94 us -> 0.52 us  [the longest x1 0.52 us: local(): lax.ppermute(projs[-1][tok_rows - HALO:, width:3 * width], 'seq', shift_r...]
    all_to_all x1, blocking collectives: 14.3 us -> 13 us  [local(): lax.all_to_all(gated.reshape(n_tensor, tok_own, width), 'tensor', 0, 0)]
    all_gather x1, blocking collectives: 6.83 us -> 5.47 us  [local(): messages = lax.all_gather(message, 'seq')]
    pallas_call x6 -> x2, Pallas kernels: 5.01 us -> 3.75 us  [the longest x1 2.65 us: local(): call(functools.partial(front, heads, width, rows), [plane] * 10 + [state]...]
  transfers between devices with their start and end apart: 22 -> 21, of which waited for: 16 -> 11; matrix products, arithmetic and copies ran while one was open for 4% -> 4% of each run, Pallas kernels for 16% -> 14%
where the time goes in v9:
time: 109 us; the launch traced here: 108 us
  waiting for transfers between devices  33.1 us (30%)
  starting transfers between devices  28.5 us (26%)
  blocking collectives  18.4 us (17%)
  Pallas kernels  15.5 us (14%)
  local copies, waits for them, and re-layouts  10.2 us (9%)
  matrix products  1.12 us (1%)
    ppermute x16, waiting for transfers between devices, ring_shift(): lax.ppermute(block, 'tensor', [(order[i], order[(i + step) % n]) for i in...  29.8 us
    ppermute x16, starting transfers between devices, ring_shift(): lax.ppermute(block, 'tensor', [(order[i], order[(i + step) % n]) for i in...  17.4 us
    all_to_all x1, blocking collectives, local(): lax.all_to_all(gated.reshape(n_tensor, tok_own, width), 'tensor', 0, 0)  13 us
    pallas_call x4, Pallas kernels, local(): call(functools.partial(project, [distance for distance, _ in arrived], ah...  8.47 us
    unnamed x37, local copies, waits for them, and re-layouts  6.91 us
    ppermute x1, starting transfers between devices, local(): lax.ppermute(tokens[tok_rows - HALO:], ('seq', 'tensor'), [(place * n_ten...  5.73 us
    all_gather x1, blocking collectives, local(): messages = lax.all_gather(message, 'seq')  5.47 us
    ppermute x1, starting transfers between devices, local(): seg_halo = lax.ppermute(segments[tok_rows - HALO:], 'seq', shift_rows)  4.09 us
  transfers between devices with their start and end apart: 21, of which 11 were waited for; matrix products, arithmetic and copies ran while one was open for 4% of the time, Pallas kernels for 14%

profile of v9, /device:TPU:0, one launch (start us, length us, event | category | flops | bytes accessed | tf_op | source)
XLA Modules:
  0.0 108.2 jit_solution(14958593073922010137)
XLA Ops:
  0.0 3.0 %collective-permute-start = (bf16[448,512]{1,0:T(8,128)(2,1)}, bf16[448,512]{1,0:T(8,128)(2,1)}, u32[]{:S(2)}, u32[]{:S(2)}) collective-permute-start(bf16[448,512]{1,0:T(8,128)(2,1)} %bitcast.11), channel_id=1, source_target_pairs={{0,2},{2,4},{4,6},{6,7},{7,5},{5,3},{3,1},{1,0},{8,10},{10,12},{12... | collective-permute-start | bytes 1376264 | tf_op jit(solution)/shard_map/ppermute | solution.py:30
  3.0 1.1 slice.35
  4.1 0.1 copy.22
  4.2 5.7 %collective-permute-start.3 = (bf16[8,448]{1,0:T(8,128)(2,1)S(1)}, bf16[8,448]{1,0:T(8,128)(2,1)S(1)}, u32[]{:S(2)}, u32[]{:S(2)}) collective-permute-start(bf16[8,448]{1,0:T(8,128)(2,1)S(1)} %copy.22), channel_id=1, source_target_pairs={{7,8},{5,10},{3,12},{1,14},{0,15},{2,13},{4,11},{6,9},{15,16},{13,... | collective-permute-start | bytes 21512 | tf_op jit(solution)/shard_map/ppermute | solution.py:302
  9.9 0.8 slice.36
  10.7 4.1 %collective-permute-start.4 = (s32[8]{0:T(128)S(1)}, s32[8]{0:T(128)S(1)}, u32[]{:S(2)}, u32[]{:S(2)}) collective-permute-start(s32[8]{0:T(128)S(1)} %slice.36), channel_id=1, source_target_pairs={{0,8},{8,16},{16,24},{1,9},{9,17},{17,25},{2,10},{10,18},{18,26},{... | collective-permute-start | bytes 104 | tf_op jit(solution)/shard_map/ppermute | solution.py:299
  14.8 1.1 %convolution_bitcast_fusion.refs_3_.refs_4_ = bf16[3584,128]{1,0:T(8,128)(2,1)S(1)} fusion(bf16[2,128]{1,0:T(2,128)(2,1)} %constant.25.clone, bf16[3584,2]{0,1:T(2,128)(2,1)S(1)} %copy-done), kind=kOutput, calls=%fused_computation | convolution fusion | flops 1835008 | bytes 932352 | tf_op jit(solution)/shard_map/dot_general | solution.py:290
  15.9 1.5 %copy-done.1 = bf16[2,3584,128]{2,1,0:T(8,128)(2,1)S(1)} copy-done((bf16[2,3584,128]{2,1,0:T(8,128)(2,1)S(1)}, bf16[2,3584,128]{2,1,0:T(8,128)(2,1)}, u32[]{:S(2)}) %copy-start.1) | copy-done | bytes 1835032
  17.4 1.0 copy-done.3
  18.4 0.6 shard_map.127.refs_5_
  19.1 2.0 %collective-permute-start.6 = (bf16[448,512]{1,0:T(8,128)(2,1)S(1)}, bf16[448,512]{1,0:T(8,128)(2,1)}, u32[]{:S(2)}, u32[]{:S(2)}) collective-permute-start(bf16[448,512]{1,0:T(8,128)(2,1)S(1)} %collective-permute-done.2.refs_1_), channel_id=1, source_target_pairs={{0,1},{2,0},{4,2},{6,4},{7,6},{5,7},{3,5},{1,3},{8,9},{10,8},{12,1... | collective-permute-start | bytes 1376264 | tf_op jit(solution)/shard_map/ppermute | solution.py:30
  21.2 0.7 fusion
  21.8 0.1 slice.39
  21.9 0.1 broadcast_in_dim.27
  22.0 0.1 broadcast_in_dim_reshape.9.bias
  22.0 0.1 broadcast_in_dim.28
  22.1 0.1 broadcast_in_dim_reshape.10.rate
  22.2 0.1 broadcast_in_dim.29
  22.3 0.1 broadcast_in_dim_reshape.11.skip
  22.4 0.1 pad_add_fusion
  22.5 3.0 %shard_map.128.refs_5_ = f32[512,512]{1,0:T(8,128)S(1)} custom-call(bf16[448,512]{1,0:T(8,128)(2,1)} %collective-permute-done.refs_0_, bf16[448,512]{1,0:T(8,128)(2,1)S(1)} %collective-permute-done.2.refs_1_, bf16[2,3584,128]{2,1,0:T(8,128)(2,1)} %refs_2_.7, bf16[3584,128]{1,0:T(8,128)(2,1)S(1)} %copy-done.2, ...), custom_call_target="tpu_custom_call" | custom-call | flops 1000000000 | bytes 2097152 | tf_op jit(solution)/shard_map/pallas_call | solution.py:338
  25.4 6.4 %collective-permute-done.1.refs_0_ = bf16[448,512]{1,0:T(8,128)(2,1)} collective-permute-done((bf16[448,512]{1,0:T(8,128)(2,1)}, bf16[448,512]{1,0:T(8,128)(2,1)}, u32[]{:S(2)}, u32[]{:S(2)}) %collective-permute-start.1) | collective-permute-done | bytes 458784 | tf_op jit(solution)/shard_map/ppermute | solution.py:30
  31.9 0.3 collective-permute-start.5
  32.2 1.7 %collective-permute-start.7 = (bf16[448,512]{1,0:T(8,128)(2,1)}, bf16[448,512]{1,0:T(8,128)(2,1)S(1)}, u32[]{:S(2)}, u32[]{:S(2)}) collective-permute-start(bf16[448,512]{1,0:T(8,128)(2,1)} %collective-permute-done.6.refs_1_), channel_id=1, source_target_pairs={{0,1},{2,0},{4,2},{6,4},{7,6},{5,7},{3,5},{1,3},{8,9},{10,8},{12,1... | collective-permute-start | bytes 1376264 | tf_op jit(solution)/shard_map/ppermute | solution.py:30
  33.9 0.1 multiply_convert_fusion.rest_0_
  34.1 0.3 collective-permute-start.12
  34.4 1.7 %collective-permute-start.13 = (bf16[128,1792]{1,0:T(8,128)(2,1)S(1)}, bf16[128,1792]{1,0:T(8,128)(2,1)}, u32[]{:S(2)}, u32[]{:S(2)}) collective-permute-start(bf16[128,1792]{1,0:T(8,128)(2,1)S(1)} %multiply_convert_fusion.rest_0_), channel_id=1, source_target_pairs={{0,1},{2,0},{4,2},{6,4},{7,6},{5,7},{3,5},{1,3},{8,9},{10,8},{12,1... | collective-permute-start | bytes 1376264 | tf_op jit(solution)/shard_map/ppermute | solution.py:30
  36.1 3.0 %shard_map.129.refs_5_ = f32[512,512]{1,0:T(8,128)S(1)} custom-call(bf16[448,512]{1,0:T(8,128)(2,1)} %collective-permute-done.1.refs_0_, bf16[448,512]{1,0:T(8,128)(2,1)} %collective-permute-done.6.refs_1_, bf16[2,3584,128]{2,1,0:T(8,128)(2,1)} %refs_2_.7, bf16[3584,128]{1,0:T(8,128)(2,1)S(1)} %copy-done.2, ...), custom_call_target="tpu_custom_call" | custom-call | flops 1000000000 | bytes 2097152 | tf_op jit(solution)/shard_map/pallas_call | solution.py:338
  39.2 6.4 %collective-permute-done.5.forth.refs_0_ = bf16[448,512]{1,0:T(8,128)(2,1)S(1)} collective-permute-done((bf16[448,512]{1,0:T(8,128)(2,1)}, bf16[448,512]{1,0:T(8,128)(2,1)S(1)}, u32[]{:S(2)}, u32[]{:S(2)}) %collective-permute-start.5) | collective-permute-done | bytes 458784 | tf_op jit(solution)/shard_map/ppermute | solution.py:30
  45.5 0.3 collective-permute-done.7.back.refs_1_
  45.8 1.9 %shard_map.131 = (f32[512,512]{1,0:T(8,128)S(1)}, bf16[448,512]{1,0:T(8,128)(2,1)S(1)}) custom-call(bf16[448,512]{1,0:T(8,128)(2,1)S(1)} %collective-permute-done.5.forth.refs_0_, bf16[448,512]{1,0:T(8,128)(2,1)S(1)} %collective-permute-done.7.back.refs_1_, bf16[2,3584,128]{2,1,0:T(8,128)(2,1)} %refs_2_.7, bf16[3584,128]{1,0:T(8,128)(2,1)S(1)} %copy-done.2, ...), custom_call_target="tpu_custom_call" | custom-call | flops 1000000000 | bytes 2097152 | tf_op jit(solution)/shard_map/pallas_call | solution.py:338
  47.7 5.9 %collective-permute-done.12.rest_1_ = bf16[128,1792]{1,0:T(8,128)(2,1)} collective-permute-done((bf16[128,1792]{1,0:T(8,128)(2,1)S(1)}, bf16[128,1792]{1,0:T(8,128)(2,1)}, u32[]{:S(2)}, u32[]{:S(2)}) %collective-permute-start.12) | collective-permute-done | bytes 458784 | tf_op jit(solution)/shard_map/ppermute | solution.py:30
  53.6 0.3 collective-permute-done.13.rest_2_
  54.0 0.3 collective-permute-start.14
  54.2 1.7 %collective-permute-start.15 = (bf16[128,1792]{1,0:T(8,128)(2,1)}, bf16[128,1792]{1,0:T(8,128)(2,1)S(1)}, u32[]{:S(2)}, u32[]{:S(2)}) collective-permute-start(bf16[128,1792]{1,0:T(8,128)(2,1)} %collective-permute-done.13.rest_2_), channel_id=1, source_target_pairs={{0,1},{2,0},{4,2},{6,4},{7,6},{5,7},{3,5},{1,3},{8,9},{10,8},{12,1... | collective-permute-start | bytes 1376264 | tf_op jit(solution)/shard_map/ppermute | solution.py:30
  56.0 0.8 shard_map.130
  56.8 0.3 collective-permute-start.8
  57.1 1.7 %collective-permute-start.9 = (bf16[224,512]{1,0:T(8,128)(2,1)}, bf16[224,512]{1,0:T(8,128)(2,1)S(1)}, u32[]{:S(2)}, u32[]{:S(2)}) collective-permute-start(bf16[224,512]{1,0:T(8,128)(2,1)} %get-tuple-element.46), channel_id=1, source_target_pairs={{0,1},{2,0},{4,2},{6,4},{7,6},{5,7},{3,5},{1,3},{8,9},{10,8},{12,1... | collective-permute-start | bytes 688136 | tf_op jit(solution)/shard_map/ppermute | solution.py:30
  58.8 1.3 %collective-permute-start.10 = (f32[8,256]{1,0:T(8,128)S(1)}, f32[8,256]{1,0:T(8,128)S(1)}, u32[]{:S(2)}, u32[]{:S(2)}) collective-permute-start(f32[8,256]{1,0:T(8,128)S(1)} %slice.44), channel_id=1, source_target_pairs={{0,8},{8,16},{16,24},{1,9},{9,17},{17,25},{2,10},{10,18},{18,26},{... | collective-permute-start | bytes 24584 | tf_op jit(solution)/shard_map/ppermute | solution.py:349
  60.1 0.1 copy.19.seg_ext_b
  60.2 0.1 copy.18.seg_ext_a
  60.4 0.5 collective-permute-done.10.halo_part
  60.9 8.9 %collective-permute-done.8.top = bf16[224,512]{1,0:T(8,128)(2,1)S(1)} collective-permute-done((bf16[224,512]{1,0:T(8,128)(2,1)}, bf16[224,512]{1,0:T(8,128)(2,1)S(1)}, u32[]{:S(2)}, u32[]{:S(2)}) %collective-permute-start.8) | collective-permute-done | bytes 229408 | tf_op jit(solution)/shard_map/ppermute | solution.py:30
  69.8 0.7 copy-done.6
  70.5 0.7 copy-done.8
  71.2 1.0 copy-done.5
  72.2 0.9 copy-done.7
  73.1 0.9 copy-done.9
  74.1 2.6 %shard_map.132 = (f32[256,128]{1,0:T(8,128)S(1)}, f32[256,128]{1,0:T(8,128)S(1)}, f32[256,128]{1,0:T(8,128)S(1)}, f32[256,128]{1,0:T(8,128)S(1)}, f32[256,128]{1...) custom-call(bf16[224,512]{1,0:T(8,128)(2,1)S(1)} %copy-done.7, ...), custom_call_target="tpu_custom_call" | custom-call | flops 100000000 | bytes 2097152 | tf_op jit(solution)/shard_map/pallas_call | solution.py:356
  76.7 5.5 %all-gather = f32[288,128]{1,0:T(8,128)S(1)} all-gather(f32[72,128]{1,0:T(8,128)S(1)} %get-tuple-element.49), channel_id=2, replica_groups=mesh['seq'=4,'tensor'=8] {'seq'}, dimensions={0}, use_global_device_ids=true | all-gather | bytes 184320 | tf_op jit(solution)/shard_map/all_gather | solution.py:364
  82.2 0.6 collective-permute-start.16
  82.8 1.5 %collective-permute-start.17 = (bf16[128,1792]{1,0:T(8,128)(2,1)S(1)}, bf16[128,1792]{1,0:T(8,128)(2,1)S(1)}, u32[]{:S(2)}, u32[]{:S(2)}) collective-permute-start(bf16[128,1792]{1,0:T(8,128)(2,1)S(1)} %collective-permute-done.15.rest_4_), channel_id=1, source_target_pairs={{0,1},{2,0},{4,2},{6,4},{7,6},{5,7},{3,5},{1,3},{8,9},{10,8},{12,1... | collective-permute-start | bytes 1376264 | tf_op jit(solution)/shard_map/ppermute | solution.py:30
  84.3 1.1 %shard_map.133 = bf16[512,128]{1,0:T(8,128)(2,1)S(1)} custom-call(s32[1,1]{1,0:T(1,128)} %bitcast.seg_first, f32[4,72,128]{2,1,0:T(8,128)S(1)} %bitcast.14, s32[264,1]{1,0:T(8,128)S(1)} %copy.18.seg_ext_a, s32[1,256]{1,0:T(1,128)S(1)} %bitcast.16, f32[1,128]{1,0:T(1,128)S(1)} %broadcast_in_dim_reshape.11.skip, f32[256,128]{1,0:T(8,128)S(1)} %get-tuple-element.50.conv_a, ...), custom_call_target="tpu_custom_call" | custom-call | flops 10000000 | bytes 2097152 | tf_op jit(solution)/shard_map/pallas_call | solution.py:365
  85.4 13.0 %all_to_all.5.mine = bf16[8,64,128]{2,1,0:T(8,128)(2,1)S(1)} all-to-all(bf16[8,64,128]{2,1,0:T(8,128)(2,1)S(1)} %bitcast.15), channel_id=1, replica_groups=mesh['seq'=4,'tensor'=8] {'tensor'}, dimensions={0} | all-to-all | bytes 262144 | tf_op jit(solution)/shard_map/all_to_all | solution.py:370
  98.4 1.1 %collective-permute-start.18 = (bf16[64,1792]{1,0:T(8,128)(2,1)S(1)}, bf16[64,1792]{1,0:T(8,128)(2,1)S(1)}, u32[]{:S(2)}, u32[]{:S(2)}) collective-permute-start(bf16[64,1792]{1,0:T(8,128)(2,1)S(1)} %get-tuple-element.69), channel_id=1, source_target_pairs={{0,2},{2,4},{4,6},{6,7},{7,5},{5,3},{3,1},{1,0},{8,10},{10,12},{12... | collective-permute-start | bytes 688136 | tf_op jit(solution)/shard_map/ppermute | solution.py:30
  99.5 1.0 collective-permute-start.19
  100.5 1.3 %collective-permute-done.11.other = bf16[8,64,128]{2,1,0:T(8,128)(2,1)S(1)} collective-permute-done((bf16[8,64,128]{2,1,0:T(8,128)(2,1)S(1)}, bf16[8,64,128]{2,1,0:T(8,128)(2,1)S(1)}, u32[]{:S(2)}, u32[]{:S(2)}) %collective-permute-start.11) | collective-permute-done | bytes 131104 | tf_op jit(solution)/shard_map/ppermute | solution.py:376
  101.8 2.1 %shard_map.134.total = f32[128,1792]{1,0:T(8,128)S(1)} custom-call(bf16[8,64,128]{2,1,0:T(8,128)(2,1)S(1)} %all_to_all.5.mine, bf16[8,64,128]{2,1,0:T(8,128)(2,1)S(1)} %collective-permute-done.11.other, bf16[128,1792]{1,0:T(8,128)(2,1)S(1)} %multiply_convert_fusion.rest_0_, bf16[128,1792]{1,0:T(8,128)(2,1)} %collective-permute-done.12.rest_1_, ...), custom_call_target="tpu_custom_call" | custom-call | flops 1000000000 | bytes 2097152 | tf_op jit(solution)/shard_map/pallas_call | solution.py:381
  104.0 0.9 collective-permute-done.18.top
  104.9 0.7 collective-permute-done.19.bottom
  105.5 0.3 shard_map.136
  105.8 0.1 collective-permute-start.20
  105.9 1.5 %collective-permute-done.20 = bf16[64,1792]{1,0:T(8,128)(2,1)S(1)} collective-permute-done((bf16[64,1792]{1,0:T(8,128)(2,1)S(1)}, bf16[64,1792]{1,0:T(8,128)(2,1)S(1)}, u32[]{:S(2)}, u32[]{:S(2)}) %collective-permute-start.20) | collective-permute-done | bytes 229408 | tf_op jit(solution)/shard_map/ppermute | solution.py:388
  107.4 0.8 pad_maximum_fusion
  (49 shorter events, 0.2 us)
Async XLA Ops:
  0.0 14.8 %copy-start = (bf16[3584,2]{0,1:T(2,128)(2,1)S(1)}, bf16[3584,2]{0,1:T(2,128)(2,1)}, u32[]{:S(2)}) copy-start(bf16[3584,2]{0,1:T(2,128)(2,1)} %param.16) | copy-start | bytes 43012
  0.0 15.9 %copy-start.2 = (bf16[3584,128]{1,0:T(8,128)(2,1)S(1)}, bf16[3584,128]{1,0:T(8,128)(2,1)}, u32[]{:S(2)}) copy-start(bf16[3584,128]{1,0:T(8,128)(2,1)} %refs_3_.5) | copy-start | bytes 2752516
  0.0 19.1 %collective-permute-start = (bf16[448,512]{1,0:T(8,128)(2,1)}, bf16[448,512]{1,0:T(8,128)(2,1)}, u32[]{:S(2)}, u32[]{:S(2)}) collective-permute-start(bf16[448,512]{1,0:T(8,128)(2,1)} %bitcast.11), channel_id=1, source_target_pairs={{0,2},{2,4},{4,6},{6,7},{7,5},{5,3},{3,1},{1,0},{8,10},{10,12},{12... | collective-permute-start | bytes 1376264 | tf_op jit(solution)/shard_map/ppermute | solution.py:30
  3.0 16.1 %collective-permute-start.2 = (bf16[448,512]{1,0:T(8,128)(2,1)}, bf16[448,512]{1,0:T(8,128)(2,1)S(1)}, u32[]{:S(2)}, u32[]{:S(2)}) collective-permute-start(bf16[448,512]{1,0:T(8,128)(2,1)} %bitcast.12), channel_id=1, source_target_pairs={{0,1},{2,0},{4,2},{6,4},{7,6},{5,7},{3,5},{1,3},{8,9},{10,8},{12,1... | collective-permute-start | bytes 1376264 | tf_op jit(solution)/shard_map/ppermute | solution.py:30
  4.2 21.3 %collective-permute-start.3 = (bf16[8,448]{1,0:T(8,128)(2,1)S(1)}, bf16[8,448]{1,0:T(8,128)(2,1)S(1)}, u32[]{:S(2)}, u32[]{:S(2)}) collective-permute-start(bf16[8,448]{1,0:T(8,128)(2,1)S(1)} %copy.22), channel_id=1, source_target_pairs={{7,8},{5,10},{3,12},{1,14},{0,15},{2,13},{4,11},{6,9},{15,16},{13,... | collective-permute-start | bytes 21512 | tf_op jit(solution)/shard_map/ppermute | solution.py:302
  10.7 11.7 %collective-permute-start.4 = (s32[8]{0:T(128)S(1)}, s32[8]{0:T(128)S(1)}, u32[]{:S(2)}, u32[]{:S(2)}) collective-permute-start(s32[8]{0:T(128)S(1)} %slice.36), channel_id=1, source_target_pairs={{0,8},{8,16},{16,24},{1,9},{9,17},{17,25},{2,10},{10,18},{18,26},{... | collective-permute-start | bytes 104 | tf_op jit(solution)/shard_map/ppermute | solution.py:299
  15.9 1.5 %copy-start.1 = (bf16[2,3584,128]{2,1,0:T(8,128)(2,1)S(1)}, bf16[2,3584,128]{2,1,0:T(8,128)(2,1)}, u32[]{:S(2)}) copy-start(bf16[2,3584,128]{2,1,0:T(8,128)(2,1)} %refs_2_.7) | copy-start | bytes 5505028
  17.4 1.0 copy-start.3
  18.4 2.7 %copy-start.13 = (s32[512]{0:T(512)S(1)}, s32[512]{0:T(512)}, u32[]{:S(2)}) copy-start(s32[512]{0:T(512)} %param.24) | copy-start | bytes 6148
  18.4 3.5 %copy-start.15 = (f32[2]{0:T(128)S(1)}, f32[2]{0:T(128)}, u32[]{:S(2)}) copy-start(f32[2]{0:T(128)} %param.17) | copy-start | bytes 28
  18.4 3.6 %copy-start.16 = (f32[2]{0:T(128)S(1)}, f32[2]{0:T(128)}, u32[]{:S(2)}) copy-start(f32[2]{0:T(128)} %param.18) | copy-start | bytes 28
  18.4 3.8 %copy-start.17 = (f32[2]{0:T(128)S(1)}, f32[2]{0:T(128)}, u32[]{:S(2)}) copy-start(f32[2]{0:T(128)} %param.19) | copy-start | bytes 28
  19.1 12.8 %collective-permute-start.1 = (bf16[448,512]{1,0:T(8,128)(2,1)}, bf16[448,512]{1,0:T(8,128)(2,1)}, u32[]{:S(2)}, u32[]{:S(2)}) collective-permute-start(bf16[448,512]{1,0:T(8,128)(2,1)} %collective-permute-done.refs_0_), channel_id=1, source_target_pairs={{0,2},{2,4},{4,6},{6,7},{7,5},{5,3},{3,1},{1,0},{8,10},{10,12},{12... | collective-permute-start | bytes 1376264 | tf_op jit(solution)/shard_map/ppermute | solution.py:30
  19.1 13.0 %collective-permute-start.6 = (bf16[448,512]{1,0:T(8,128)(2,1)S(1)}, bf16[448,512]{1,0:T(8,128)(2,1)}, u32[]{:S(2)}, u32[]{:S(2)}) collective-permute-start(bf16[448,512]{1,0:T(8,128)(2,1)S(1)} %collective-permute-done.2.refs_1_), channel_id=1, source_target_pairs={{0,1},{2,0},{4,2},{6,4},{7,6},{5,7},{3,5},{1,3},{8,9},{10,8},{12,1... | collective-permute-start | bytes 1376264 | tf_op jit(solution)/shard_map/ppermute | solution.py:30
  22.5 11.5 %copy-start.12 = (bf16[128,3584]{1,0:T(8,128)(2,1)S(1)}, bf16[128,3584]{1,0:T(8,128)(2,1)}, u32[]{:S(2)}) copy-start(bf16[128,3584]{1,0:T(8,128)(2,1)} %param.23) | copy-start | bytes 2752516
  22.5 11.5 %copy-start.14 = (f32[128]{0:T(128)S(1)}, f32[128]{0:T(128)}, u32[]{:S(2)}) copy-start(f32[128]{0:T(128)} %param.22) | copy-start | bytes 1540
  31.9 13.7 %collective-permute-start.5 = (bf16[448,512]{1,0:T(8,128)(2,1)}, bf16[448,512]{1,0:T(8,128)(2,1)S(1)}, u32[]{:S(2)}, u32[]{:S(2)}) collective-permute-start(bf16[448,512]{1,0:T(8,128)(2,1)} %collective-permute-done.1.refs_0_), channel_id=1, source_target_pairs={{0,2},{2,4},{4,6},{6,7},{7,5},{5,3},{3,1},{1,0},{8,10},{10,12},{12... | collective-permute-start | bytes 1376264 | tf_op jit(solution)/shard_map/ppermute | solution.py:30
  32.2 13.7 %collective-permute-start.7 = (bf16[448,512]{1,0:T(8,128)(2,1)}, bf16[448,512]{1,0:T(8,128)(2,1)S(1)}, u32[]{:S(2)}, u32[]{:S(2)}) collective-permute-start(bf16[448,512]{1,0:T(8,128)(2,1)} %collective-permute-done.6.refs_1_), channel_id=1, source_target_pairs={{0,1},{2,0},{4,2},{6,4},{7,6},{5,7},{3,5},{1,3},{8,9},{10,8},{12,1... | collective-permute-start | bytes 1376264 | tf_op jit(solution)/shard_map/ppermute | solution.py:30
  34.1 19.6 %collective-permute-start.12 = (bf16[128,1792]{1,0:T(8,128)(2,1)S(1)}, bf16[128,1792]{1,0:T(8,128)(2,1)}, u32[]{:S(2)}, u32[]{:S(2)}) collective-permute-start(bf16[128,1792]{1,0:T(8,128)(2,1)S(1)} %multiply_convert_fusion.rest_0_), channel_id=1, source_target_pairs={{0,2},{2,4},{4,6},{6,7},{7,5},{5,3},{3,1},{1,0},{8,10},{10,12},{12... | collective-permute-start | bytes 1376264 | tf_op jit(solution)/shard_map/ppermute | solution.py:30
  34.4 19.5 %collective-permute-start.13 = (bf16[128,1792]{1,0:T(8,128)(2,1)S(1)}, bf16[128,1792]{1,0:T(8,128)(2,1)}, u32[]{:S(2)}, u32[]{:S(2)}) collective-permute-start(bf16[128,1792]{1,0:T(8,128)(2,1)S(1)} %multiply_convert_fusion.rest_0_), channel_id=1, source_target_pairs={{0,1},{2,0},{4,2},{6,4},{7,6},{5,7},{3,5},{1,3},{8,9},{10,8},{12,1... | collective-permute-start | bytes 1376264 | tf_op jit(solution)/shard_map/ppermute | solution.py:30
  39.2 32.0 %copy-start.10 = (f32[4,128]{1,0:T(4,128)S(1)}, f32[4,128]{1,0:T(4,128)}, u32[]{:S(2)}) copy-start(f32[4,128]{1,0:T(4,128)} %taps_x.1) | copy-start | bytes 6148
  39.2 32.0 %copy-start.11 = (f32[4,128]{1,0:T(4,128)S(1)}, f32[4,128]{1,0:T(4,128)}, u32[]{:S(2)}) copy-start(f32[4,128]{1,0:T(4,128)} %taps_bc.1) | copy-start | bytes 6148
  47.7 11.1 %copy-start.4 = (bf16[448,512]{1,0:T(8,128)(2,1)}, bf16[448,512]{1,0:T(8,128)(2,1)S(1)}, u32[]{:S(2)}) copy-start(bf16[448,512]{1,0:T(8,128)(2,1)S(1)} %get-tuple-element.47.weights) | copy-start | bytes 1376260
  54.0 28.3 %collective-permute-start.14 = (bf16[128,1792]{1,0:T(8,128)(2,1)}, bf16[128,1792]{1,0:T(8,128)(2,1)S(1)}, u32[]{:S(2)}, u32[]{:S(2)}) collective-permute-start(bf16[128,1792]{1,0:T(8,128)(2,1)} %collective-permute-done.12.rest_1_), channel_id=1, source_target_pairs={{0,2},{2,4},{4,6},{6,7},{7,5},{5,3},{3,1},{1,0},{8,10},{10,12},{12... | collective-permute-start | bytes 1376264 | tf_op jit(solution)/shard_map/ppermute | solution.py:30
  54.2 28.0 %collective-permute-start.15 = (bf16[128,1792]{1,0:T(8,128)(2,1)}, bf16[128,1792]{1,0:T(8,128)(2,1)S(1)}, u32[]{:S(2)}, u32[]{:S(2)}) collective-permute-start(bf16[128,1792]{1,0:T(8,128)(2,1)} %collective-permute-done.13.rest_2_), channel_id=1, source_target_pairs={{0,1},{2,0},{4,2},{6,4},{7,6},{5,7},{3,5},{1,3},{8,9},{10,8},{12,1... | collective-permute-start | bytes 1376264 | tf_op jit(solution)/shard_map/ppermute | solution.py:30
  56.8 13.0 %collective-permute-start.8 = (bf16[224,512]{1,0:T(8,128)(2,1)}, bf16[224,512]{1,0:T(8,128)(2,1)S(1)}, u32[]{:S(2)}, u32[]{:S(2)}) collective-permute-start(bf16[224,512]{1,0:T(8,128)(2,1)} %get-tuple-element.45), channel_id=1, source_target_pairs={{0,2},{2,4},{4,6},{6,7},{7,5},{5,3},{3,1},{1,0},{8,10},{10,12},{12... | collective-permute-start | bytes 688136 | tf_op jit(solution)/shard_map/ppermute | solution.py:30
  57.1 13.4 %collective-permute-start.9 = (bf16[224,512]{1,0:T(8,128)(2,1)}, bf16[224,512]{1,0:T(8,128)(2,1)S(1)}, u32[]{:S(2)}, u32[]{:S(2)}) collective-permute-start(bf16[224,512]{1,0:T(8,128)(2,1)} %get-tuple-element.46), channel_id=1, source_target_pairs={{0,1},{2,0},{4,2},{6,4},{7,6},{5,7},{3,5},{1,3},{8,9},{10,8},{12,1... | collective-permute-start | bytes 688136 | tf_op jit(solution)/shard_map/ppermute | solution.py:30
  58.8 2.1 %collective-permute-start.10 = (f32[8,256]{1,0:T(8,128)S(1)}, f32[8,256]{1,0:T(8,128)S(1)}, u32[]{:S(2)}, u32[]{:S(2)}) collective-permute-start(f32[8,256]{1,0:T(8,128)S(1)} %slice.44), channel_id=1, source_target_pairs={{0,8},{8,16},{16,24},{1,9},{9,17},{17,25},{2,10},{10,18},{18,26},{... | collective-permute-start | bytes 24584 | tf_op jit(solution)/shard_map/ppermute | solution.py:349
  69.8 0.7 copy-start.6
  70.5 0.7 copy-start.8
  71.2 1.0 copy-start.5
  72.2 0.9 copy-start.7
  73.1 0.9 copy-start.9
  82.2 16.1 %collective-permute-start.16 = (bf16[128,1792]{1,0:T(8,128)(2,1)S(1)}, bf16[128,1792]{1,0:T(8,128)(2,1)S(1)}, u32[]{:S(2)}, u32[]{:S(2)}) collective-permute-start(bf16[128,1792]{1,0:T(8,128)(2,1)S(1)} %collective-permute-done.14.rest_3_), channel_id=1, source_target_pairs={{0,2},{2,4},{4,6},{6,7},{7,5},{5,3},{3,1},{1,0},{8,10},{10,12},{12... | collective-permute-start | bytes 1376264 | tf_op jit(solution)/shard_map/ppermute | solution.py:30
  82.8 15.5 %collective-permute-start.17 = (bf16[128,1792]{1,0:T(8,128)(2,1)S(1)}, bf16[128,1792]{1,0:T(8,128)(2,1)S(1)}, u32[]{:S(2)}, u32[]{:S(2)}) collective-permute-start(bf16[128,1792]{1,0:T(8,128)(2,1)S(1)} %collective-permute-done.15.rest_4_), channel_id=1, source_target_pairs={{0,1},{2,0},{4,2},{6,4},{7,6},{5,7},{3,5},{1,3},{8,9},{10,8},{12,1... | collective-permute-start | bytes 1376264 | tf_op jit(solution)/shard_map/ppermute | solution.py:30
  98.4 6.5 %collective-permute-start.18 = (bf16[64,1792]{1,0:T(8,128)(2,1)S(1)}, bf16[64,1792]{1,0:T(8,128)(2,1)S(1)}, u32[]{:S(2)}, u32[]{:S(2)}) collective-permute-start(bf16[64,1792]{1,0:T(8,128)(2,1)S(1)} %get-tuple-element.69), channel_id=1, source_target_pairs={{0,2},{2,4},{4,6},{6,7},{7,5},{5,3},{3,1},{1,0},{8,10},{10,12},{12... | collective-permute-start | bytes 688136 | tf_op jit(solution)/shard_map/ppermute | solution.py:30
  99.5 6.0 %collective-permute-start.19 = (bf16[64,1792]{1,0:T(8,128)(2,1)S(1)}, bf16[64,1792]{1,0:T(8,128)(2,1)S(1)}, u32[]{:S(2)}, u32[]{:S(2)}) collective-permute-start(bf16[64,1792]{1,0:T(8,128)(2,1)S(1)} %get-tuple-element.70), channel_id=1, source_target_pairs={{0,1},{2,0},{4,2},{6,4},{7,6},{5,7},{3,5},{1,3},{8,9},{10,8},{12,1... | collective-permute-start | bytes 688136 | tf_op jit(solution)/shard_map/ppermute | solution.py:30
  100.5 1.3 %collective-permute-start.11 = (bf16[8,64,128]{2,1,0:T(8,128)(2,1)S(1)}, bf16[8,64,128]{2,1,0:T(8,128)(2,1)S(1)}, u32[]{:S(2)}, u32[]{:S(2)}) collective-permute-start(bf16[8,64,128]{2,1,0:T(8,128)(2,1)S(1)} %all_to_all.5.mine), channel_id=1, source_target_pairs={{0,8},{8,0},{16,24},{24,16},{1,9},{9,1},{17,25},{25,17},{2,10},{10... | collective-permute-start | bytes 393224 | tf_op jit(solution)/shard_map/ppermute | solution.py:376
  105.8 1.6 %collective-permute-start.20 = (bf16[64,1792]{1,0:T(8,128)(2,1)S(1)}, bf16[64,1792]{1,0:T(8,128)(2,1)S(1)}, u32[]{:S(2)}, u32[]{:S(2)}) collective-permute-start(bf16[64,1792]{1,0:T(8,128)(2,1)S(1)} %get-tuple-element.72), channel_id=1, source_target_pairs={{0,8},{8,0},{16,24},{24,16},{1,9},{9,1},{17,25},{25,17},{2,10},{10... | collective-permute-start | bytes 688136 | tf_op jit(solution)/shard_map/ppermute | solution.py:388

commit v10 on v9

--- a/solution.py
+++ b/solution.py
@@ -260,7 +260,7 @@
         out[...] = (result[i * rows : (i + 1) * rows] * scale).astype(BF16)
 
 
-def call(body, outs, scratch=(), vmem=48, flops=10**7, **kw):
+def call(body, outs, scratch=(), vmem=16, flops=10**7, **kw):
     return pl.pallas_call(
         body,
         out_shape=outs,
@@ -296,25 +296,24 @@
     w_half = width // 2
     shift_rows = [(i, i + 1) for i in range(n_seq - 1)]
 
-    seg_halo = lax.ppermute(segments[tok_rows - HALO :], "seq", shift_rows)
-    seg_all = jnp.concatenate([seg_halo, segments])[:, None]
-    order = [2 * i if i < last else 2 * n_tensor - 1 - 2 * i for i in range(n_tensor)]
-    halo_far = lax.ppermute(
-        tokens[tok_rows - HALO :],
-        ("seq", "tensor"),
-        [
+
+    def early_arrays(*earlier):
+        seg_halo = lax.ppermute(after(segments[tok_rows - HALO :], *earlier), "seq", shift_rows)
+        seg_all = jnp.concatenate([seg_halo, segments])[:, None]
+        order = [2 * i if i < last else 2 * n_tensor - 1 - 2 * i for i in range(n_tensor)]
+        moves = [
             (place * n_tensor + order[(i + last) % n_tensor], (place + 1) * n_tensor + order[i])
             for place in range(n_seq - 1)
             for i in range(n_tensor)
-        ],
-    )
-    small = (
-        halo_far,
-        (seg_all[: HALO + rows], seg_all[rows:]),
-        (segments[None, :rows], segments[None, rows:]),
-        (segments[None, :1], segments[None, tok_rows - 1 :]),
-        (spread(dt_bias)[None], spread(a_rate)[None], spread(d_skip)[None]),
-    )
+        ]
+        halo_far = lax.ppermute(after(tokens[tok_rows - HALO :], *earlier), ("seq", "tensor"), moves)
+        return (
+            halo_far,
+            (seg_all[: HALO + rows], seg_all[rows:]),
+            (segments[None, :rows], segments[None, rows:]),
+            (segments[None, :1], segments[None, tok_rows - 1 :]),
+            (spread(dt_bias)[None], spread(a_rate)[None], spread(d_skip)[None]),
+        )
 
     forth = back = block
     w_steps = []
@@ -329,6 +328,7 @@
         else:
             far = far_shift(forth, back)
         if step == 2:
+            small = early_arrays(arrivals)
             w_forth, w_back = after((own, own), arrivals)
             w_steps.append((ring_shift(w_forth, 1), ring_shift(w_back, -1)))
         ahead = last if step == last else 0
@@ -344,9 +344,9 @@
         )(*[part for _, part in arrived], w_zx, w_bc, w_step, *total)
         projs.append(results[0])
         arrived = [(-step, forth), (step, back)]
-    w_forth, w_back = after(w_steps[-1], projs[-1])
+    halo_part = lax.ppermute(projs[-1][tok_rows - HALO :, width : 3 * width], "seq", shift_rows)
+    w_forth, w_back = after(w_steps[-1], far, halo_part)
     w_steps.append((ring_shift(w_forth, 1), ring_shift(w_back, -1)))
-    halo_part = lax.ppermute(projs[-1][tok_rows - HALO :, width : 3 * width], "seq", shift_rows)
 
     halo_far, (seg_ext_a, seg_ext_b), (seg_row_a, seg_row_b), (seg_first, seg_last), (bias, rate, skip) = small
     msg_rows = state_w + 8
@@ -378,7 +378,7 @@
     for i, pair in enumerate(w_steps):
         pieces += pair
         distances += [-i - 1, i + 1]
-    total = call(functools.partial(product_early, distances), shape(2 * tok_own, columns), flops=10**9)(
+    total = call(functools.partial(product_early, distances), shape(2 * tok_own, columns), vmem=16 + len(pieces), flops=10**9)(
         mine, other, *pieces
     )
     half = shape(tok_own, columns, kind=BF16)

time: 109 us -> 101 us (0.927)
  waiting for transfers between devices: 33.1 us -> 23.4 us
  local copies, waits for them, and re-layouts: 10.2 us -> 14.5 us
  Pallas kernels: 15.5 us -> 12.6 us
    ppermute x16, waiting for transfers between devices: 29.8 us -> 20.6 us  [ring_shift(): lax.ppermute(block, 'tensor', [(order[i], order[(i + step) % n]) for i in...]
    unnamed x37 -> x46, local copies, waits for them, and re-layouts: 6.91 us -> 12.7 us
    pallas_call x4, Pallas kernels: 8.47 us -> 6.4 us  [local(): call(functools.partial(project, [distance for distance, _ in arrived], ah...]
    slice x10, local copies, waits for them, and re-layouts: 2.84 us -> 1.18 us  [the longest x1 0.65 us: early_arrays(): segments[None, tok_rows - 1:]]
  transfers between devices with their start and end apart: 21 -> 21, of which waited for: 11 -> 11; matrix products, arithmetic and copies ran while one was open for 4% -> 3% of each run, Pallas kernels for 14% -> 12%
where the time goes in v10:
time: 101 us; the launch traced here: 100 us
  starting transfers between devices  28.6 us (28%)
  waiting for transfers between devices  23.4 us (23%)
  blocking collectives  18.4 us (18%)
  local copies, waits for them, and re-layouts  14.5 us (14%)
  Pallas kernels  12.6 us (12%)
  matrix products  1.11 us (1%)
  other arithmetic  1.05 us (1%)
    ppermute x16, waiting for transfers between devices, ring_shift(): lax.ppermute(block, 'tensor', [(order[i], order[(i + step) % n]) for i in...  20.6 us
    ppermute x16, starting transfers between devices, ring_shift(): lax.ppermute(block, 'tensor', [(order[i], order[(i + step) % n]) for i in...  17.5 us
    all_to_all x1, blocking collectives, local(): lax.all_to_all(gated.reshape(n_tensor, tok_own, width), 'tensor', 0, 0)  13 us
    unnamed x46, local copies, waits for them, and re-layouts  12.7 us
    pallas_call x4, Pallas kernels, local(): call(functools.partial(project, [distance for distance, _ in arrived], ah...  6.4 us
    all_gather x1, blocking collectives, local(): messages = lax.all_gather(message, 'seq')  5.47 us
    ppermute x1, starting transfers between devices, early_arrays(): lax.ppermute(after(segments[tok_rows - HALO:], *earlier), 'seq', shift_rows)  4.97 us
    ppermute x1, starting transfers between devices, early_arrays(): lax.ppermute(after(tokens[tok_rows - HALO:], *earlier), ('seq', 'tensor')...  4.82 us
  transfers between devices with their start and end apart: 21, of which 11 were waited for; matrix products, arithmetic and copies ran while one was open for 3% of the time, Pallas kernels for 12%

profile of v10, /device:TPU:0, one launch (start us, length us, event | category | flops | bytes accessed | tf_op | source)
XLA Modules:
  0.0 100.0 jit_solution(16160426226152321267)
XLA Ops:
  0.0 3.0 %collective-permute-start = (bf16[448,512]{1,0:T(8,128)(2,1)}, bf16[448,512]{1,0:T(8,128)(2,1)}, u32[]{:S(2)}, u32[]{:S(2)}) collective-permute-start(bf16[448,512]{1,0:T(8,128)(2,1)} %bitcast.11), channel_id=1, source_target_pairs={{0,2},{2,4},{4,6},{6,7},{7,5},{5,3},{3,1},{1,0},{8,10},{10,12},{12... | collective-permute-start | bytes 1376264 | tf_op jit(solution)/shard_map/ppermute | solution.py:30
  3.0 1.1 %convolution_bitcast_fusion.refs_3_.refs_4_ = bf16[3584,128]{1,0:T(8,128)(2,1)S(1)} fusion(bf16[2,128]{1,0:T(2,128)(2,1)} %constant.25.clone, bf16[3584,2]{0,1:T(2,128)(2,1)S(1)} %copy-done), kind=kOutput, calls=%fused_computation | convolution fusion | flops 1835008 | bytes 932352 | tf_op jit(solution)/shard_map/dot_general | solution.py:290
  4.2 1.5 %copy-done.1 = bf16[2,3584,128]{2,1,0:T(8,128)(2,1)S(1)} copy-done((bf16[2,3584,128]{2,1,0:T(8,128)(2,1)S(1)}, bf16[2,3584,128]{2,1,0:T(8,128)(2,1)}, u32[]{:S(2)}) %copy-start.1) | copy-done | bytes 1835032
  5.7 1.2 %copy-done.3 = bf16[3584,128]{1,0:T(8,128)(2,1)S(1)} copy-done((bf16[3584,128]{1,0:T(8,128)(2,1)S(1)}, bf16[3584,128]{1,0:T(8,128)(2,1)}, u32[]{:S(2)}) %copy-start.3) | copy-done | bytes 917528
  6.8 1.0 %copy-done.10 = bf16[512,448]{0,1:T(8,128)(2,1)S(1)} copy-done((bf16[512,448]{0,1:T(8,128)(2,1)S(1)}, bf16[512,448]{0,1:T(8,128)(2,1)}, u32[]{:S(2)}) %copy-start.10) | copy-done | bytes 458776
  7.9 0.6 shard_map.127.refs_5_
  8.5 1.0 copy-done.6
  9.5 4.3 %collective-permute-done.refs_0_ = bf16[448,512]{1,0:T(8,128)(2,1)} collective-permute-done((bf16[448,512]{1,0:T(8,128)(2,1)}, bf16[448,512]{1,0:T(8,128)(2,1)}, u32[]{:S(2)}, u32[]{:S(2)}) %collective-permute-start) | collective-permute-done | bytes 458784 | tf_op jit(solution)/shard_map/ppermute | solution.py:30
  13.8 1.8 %collective-permute-start.1 = (bf16[448,512]{1,0:T(8,128)(2,1)}, bf16[448,512]{1,0:T(8,128)(2,1)}, u32[]{:S(2)}, u32[]{:S(2)}) collective-permute-start(bf16[448,512]{1,0:T(8,128)(2,1)} %collective-permute-done.refs_0_), channel_id=1, source_target_pairs={{0,2},{2,4},{4,6},{6,7},{7,5},{5,3},{3,1},{1,0},{8,10},{10,12},{12... | collective-permute-start | bytes 1376264 | tf_op jit(solution)/shard_map/ppermute | solution.py:30
  15.6 0.2 collective-permute-start.6
  15.8 0.6 fusion
  16.5 0.1 slice.35
  16.6 0.1 slice.36
  16.6 0.1 slice.39
  16.7 0.1 copy.22
  16.8 0.1 broadcast_in_dim.27
  16.9 0.1 broadcast_in_dim_reshape.9.bias
  17.0 0.1 broadcast_in_dim_reshape.10.rate
  17.2 0.1 broadcast_in_dim_reshape.11.skip
  17.3 4.8 %collective-permute-start.3 = (bf16[8,448]{1,0:T(8,128)(2,1)S(1)}, bf16[8,448]{1,0:T(8,128)(2,1)S(1)}, u32[]{:S(2)}, u32[]{:S(2)}) collective-permute-start(bf16[8,448]{1,0:T(8,128)(2,1)S(1)} %copy.22), channel_id=1, source_target_pairs={{7,8},{5,10},{3,12},{1,14},{0,15},{2,13},{4,11},{6,9},{15,16},{13,... | collective-permute-start | bytes 21512 | tf_op jit(solution)/shard_map/ppermute | solution.py:309
  22.1 5.0 %collective-permute-start.4 = (s32[8]{0:T(128)S(1)}, s32[8]{0:T(128)S(1)}, u32[]{:S(2)}, u32[]{:S(2)}) collective-permute-start(s32[8]{0:T(128)S(1)} %slice.36), channel_id=1, source_target_pairs={{0,8},{8,16},{16,24},{1,9},{9,17},{17,25},{2,10},{10,18},{18,26},{... | collective-permute-start | bytes 104 | tf_op jit(solution)/shard_map/ppermute | solution.py:301
  27.1 1.2 %copy-done.4 = bf16[3584,128]{1,0:T(8,128)(2,1)S(1)} copy-done((bf16[3584,128]{1,0:T(8,128)(2,1)S(1)}, bf16[3584,128]{1,0:T(8,128)(2,1)}, u32[]{:S(2)}) %copy-start.4) | copy-done | bytes 917528
  28.3 1.2 %copy-done.7 = f32[512,512]{1,0:T(8,128)S(1)} copy-done((f32[512,512]{1,0:T(8,128)S(1)}, f32[512,512]{1,0:T(8,128)}, u32[]{:S(2)}) %copy-start.7) | copy-done | bytes 1048600
  29.5 2.2 %shard_map.128.refs_5_ = f32[512,512]{1,0:T(8,128)S(1)} custom-call(bf16[448,512]{1,0:T(8,128)(2,1)} %collective-permute-done.refs_0_, bf16[448,512]{1,0:T(8,128)(2,1)S(1)} %collective-permute-done.2.refs_1_, bf16[2,3584,128]{2,1,0:T(8,128)(2,1)S(1)} %copy-done.2, bf16[3584,128]{1,0:T(8,128)(2,1)S(1)} %copy-done.4, ...), custom_call_target="tpu_custom_call" | custom-call | flops 1000000000 | bytes 2097152 | tf_op jit(solution)/shard_map/pallas_call | solution.py:338
  31.7 0.1 pad_add_fusion
  31.9 2.0 %collective-permute-start.7 = (bf16[448,512]{1,0:T(8,128)(2,1)}, bf16[448,512]{1,0:T(8,128)(2,1)S(1)}, u32[]{:S(2)}, u32[]{:S(2)}) collective-permute-start(bf16[448,512]{1,0:T(8,128)(2,1)} %collective-permute-done.6.refs_1_), channel_id=1, source_target_pairs={{0,1},{2,0},{4,2},{6,4},{7,6},{5,7},{3,5},{1,3},{8,9},{10,8},{12,1... | collective-permute-start | bytes 1376264 | tf_op jit(solution)/shard_map/ppermute | solution.py:30
  33.9 0.1 multiply_convert_fusion.rest_0_
  34.1 0.1 collective-permute-start.12
  34.2 2.0 %collective-permute-start.13 = (bf16[128,1792]{1,0:T(8,128)(2,1)S(1)}, bf16[128,1792]{1,0:T(8,128)(2,1)}, u32[]{:S(2)}, u32[]{:S(2)}) collective-permute-start(bf16[128,1792]{1,0:T(8,128)(2,1)S(1)} %multiply_convert_fusion.rest_0_), channel_id=1, source_target_pairs={{0,1},{2,0},{4,2},{6,4},{7,6},{5,7},{3,5},{1,3},{8,9},{10,8},{12,1... | collective-permute-start | bytes 1376264 | tf_op jit(solution)/shard_map/ppermute | solution.py:30
  36.2 2.3 %shard_map.129.refs_5_ = f32[512,512]{1,0:T(8,128)S(1)} custom-call(bf16[448,512]{1,0:T(8,128)(2,1)} %collective-permute-done.1.refs_0_, bf16[448,512]{1,0:T(8,128)(2,1)} %collective-permute-done.6.refs_1_, bf16[2,3584,128]{2,1,0:T(8,128)(2,1)S(1)} %copy-done.2, bf16[3584,128]{1,0:T(8,128)(2,1)S(1)} %copy-done.4, ...), custom_call_target="tpu_custom_call" | custom-call | flops 1000000000 | bytes 2097152 | tf_op jit(solution)/shard_map/pallas_call | solution.py:338
  38.5 7.0 %collective-permute-done.5.forth.refs_0_ = bf16[448,512]{1,0:T(8,128)(2,1)S(1)} collective-permute-done((bf16[448,512]{1,0:T(8,128)(2,1)}, bf16[448,512]{1,0:T(8,128)(2,1)S(1)}, u32[]{:S(2)}, u32[]{:S(2)}) %collective-permute-start.5) | collective-permute-done | bytes 458784 | tf_op jit(solution)/shard_map/ppermute | solution.py:30
  45.5 0.1 collective-permute-done.7.back.refs_1_
  45.7 2.0 %collective-permute-start.9 = (bf16[224,512]{1,0:T(8,128)(2,1)S(1)}, bf16[224,512]{1,0:T(8,128)(2,1)S(1)}, u32[]{:S(2)}, u32[]{:S(2)}) collective-permute-start(bf16[224,512]{1,0:T(8,128)(2,1)S(1)} %get-tuple-element.50), channel_id=1, source_target_pairs={{0,1},{2,0},{4,2},{6,4},{7,6},{5,7},{3,5},{1,3},{8,9},{10,8},{12,1... | collective-permute-start | bytes 688136 | tf_op jit(solution)/shard_map/ppermute | solution.py:30
  47.7 1.3 %shard_map.131 = (f32[512,512]{1,0:T(8,128)S(1)}, bf16[448,512]{1,0:T(8,128)(2,1)S(1)}) custom-call(bf16[448,512]{1,0:T(8,128)(2,1)S(1)} %collective-permute-done.5.forth.refs_0_, bf16[448,512]{1,0:T(8,128)(2,1)S(1)} %collective-permute-done.7.back.refs_1_, bf16[2,3584,128]{2,1,0:T(8,128)(2,1)S(1)} %copy-done.2, bf16[3584,128]{1,0:T(8,128)(2,1)S(1)} %copy-done.5, ...), custom_call_target="tpu_custom_call" | custom-call | flops 1000000000 | bytes 2097152 | tf_op jit(solution)/shard_map/pallas_call | solution.py:338
  49.0 0.8 copy-done.11
  49.8 1.0 copy-done.8
  50.8 1.3 %collective-permute-start.10 = (f32[8,256]{1,0:T(8,128)S(1)}, f32[8,256]{1,0:T(8,128)S(1)}, u32[]{:S(2)}, u32[]{:S(2)}) collective-permute-start(f32[8,256]{1,0:T(8,128)S(1)} %slice.44), channel_id=1, source_target_pairs={{0,8},{8,16},{16,24},{1,9},{9,17},{17,25},{2,10},{10,18},{18,26},{... | collective-permute-start | bytes 24584 | tf_op jit(solution)/shard_map/ppermute | solution.py:347
  52.0 3.4 %collective-permute-done.12.rest_1_ = bf16[128,1792]{1,0:T(8,128)(2,1)} collective-permute-done((bf16[128,1792]{1,0:T(8,128)(2,1)S(1)}, bf16[128,1792]{1,0:T(8,128)(2,1)}, u32[]{:S(2)}, u32[]{:S(2)}) %collective-permute-start.12) | collective-permute-done | bytes 458784 | tf_op jit(solution)/shard_map/ppermute | solution.py:30
  55.4 0.1 collective-permute-done.13.rest_2_
  55.5 3.8 %collective-permute-done.8.top = bf16[224,512]{1,0:T(8,128)(2,1)S(1)} collective-permute-done((bf16[224,512]{1,0:T(8,128)(2,1)S(1)}, bf16[224,512]{1,0:T(8,128)(2,1)S(1)}, u32[]{:S(2)}, u32[]{:S(2)}) %collective-permute-start.8) | collective-permute-done | bytes 229408 | tf_op jit(solution)/shard_map/ppermute | solution.py:30
  59.3 0.1 collective-permute-done.9.bottom
  59.4 0.7 copy-done.13
  60.1 0.2 collective-permute-start.14
  60.3 1.8 %collective-permute-start.15 = (bf16[128,1792]{1,0:T(8,128)(2,1)}, bf16[128,1792]{1,0:T(8,128)(2,1)S(1)}, u32[]{:S(2)}, u32[]{:S(2)}) collective-permute-start(bf16[128,1792]{1,0:T(8,128)(2,1)} %collective-permute-done.13.rest_2_), channel_id=1, source_target_pairs={{0,1},{2,0},{4,2},{6,4},{7,6},{5,7},{3,5},{1,3},{8,9},{10,8},{12,1... | collective-permute-start | bytes 1376264 | tf_op jit(solution)/shard_map/ppermute | solution.py:30
  62.1 0.1 copy.19.seg_ext_b
  62.2 0.1 copy.18.seg_ext_a
  62.4 1.2 %copy-done.9 = f32[512,512]{1,0:T(8,128)S(1)} copy-done((f32[512,512]{1,0:T(8,128)S(1)}, f32[512,512]{1,0:T(8,128)}, u32[]{:S(2)}) %copy-start.9) | copy-done | bytes 1048600
  63.6 1.0 %copy-done.12 = bf16[448,512]{1,0:T(8,128)(2,1)S(1)} copy-done((bf16[448,512]{1,0:T(8,128)(2,1)S(1)}, bf16[448,512]{1,0:T(8,128)(2,1)}, u32[]{:S(2)}) %copy-start.12) | copy-done | bytes 458776
  64.6 0.9 copy-done.14
  65.6 2.6 %shard_map.132 = (f32[256,128]{1,0:T(8,128)S(1)}, f32[256,128]{1,0:T(8,128)S(1)}, f32[256,128]{1,0:T(8,128)S(1)}, f32[256,128]{1,0:T(8,128)S(1)}, f32[256,128]{1...) custom-call(bf16[224,512]{1,0:T(8,128)(2,1)S(1)} %collective-permute, ...), custom_call_target="tpu_custom_call" | custom-call | flops 100000000 | bytes 2097152 | tf_op jit(solution)/shard_map/pallas_call | solution.py:356
  68.2 5.5 %all-gather = f32[288,128]{1,0:T(8,128)S(1)} all-gather(f32[72,128]{1,0:T(8,128)S(1)} %get-tuple-element.53), channel_id=2, replica_groups=mesh['seq'=4,'tensor'=8] {'seq'}, dimensions={0}, use_global_device_ids=true | all-gather | bytes 184320 | tf_op jit(solution)/shard_map/all_gather | solution.py:364
  73.6 0.2 collective-permute-start.16
  73.9 1.8 %collective-permute-start.17 = (bf16[128,1792]{1,0:T(8,128)(2,1)S(1)}, bf16[128,1792]{1,0:T(8,128)(2,1)S(1)}, u32[]{:S(2)}, u32[]{:S(2)}) collective-permute-start(bf16[128,1792]{1,0:T(8,128)(2,1)S(1)} %collective-permute-done.15.rest_4_), channel_id=1, source_target_pairs={{0,1},{2,0},{4,2},{6,4},{7,6},{5,7},{3,5},{1,3},{8,9},{10,8},{12,1... | collective-permute-start | bytes 1376264 | tf_op jit(solution)/shard_map/ppermute | solution.py:30
  75.7 1.2 %shard_map.133 = bf16[512,128]{1,0:T(8,128)(2,1)S(1)} custom-call(s32[1,1]{1,0:T(1,128)} %bitcast.seg_first, f32[4,72,128]{2,1,0:T(8,128)S(1)} %bitcast.14, s32[264,1]{1,0:T(8,128)S(1)} %copy.18.seg_ext_a, s32[1,256]{1,0:T(1,128)S(1)} %bitcast.16, f32[1,128]{1,0:T(1,128)S(1)} %broadcast_in_dim_reshape.11.skip, f32[256,128]{1,0:T(8,128)S(1)} %get-tuple-element.54.conv_a, ...), custom_call_target="tpu_custom_call" | custom-call | flops 10000000 | bytes 2097152 | tf_op jit(solution)/shard_map/pallas_call | solution.py:365
  76.9 13.0 %all_to_all.5.mine = bf16[8,64,128]{2,1,0:T(8,128)(2,1)S(1)} all-to-all(bf16[8,64,128]{2,1,0:T(8,128)(2,1)S(1)} %bitcast.15), channel_id=1, replica_groups=mesh['seq'=4,'tensor'=8] {'tensor'}, dimensions={0} | all-to-all | bytes 262144 | tf_op jit(solution)/shard_map/all_to_all | solution.py:370
  89.9 1.5 %collective-permute-start.18 = (bf16[64,1792]{1,0:T(8,128)(2,1)S(1)}, bf16[64,1792]{1,0:T(8,128)(2,1)S(1)}, u32[]{:S(2)}, u32[]{:S(2)}) collective-permute-start(bf16[64,1792]{1,0:T(8,128)(2,1)S(1)} %get-tuple-element.73), channel_id=1, source_target_pairs={{0,2},{2,4},{4,6},{6,7},{7,5},{5,3},{3,1},{1,0},{8,10},{10,12},{12... | collective-permute-start | bytes 688136 | tf_op jit(solution)/shard_map/ppermute | solution.py:30
  91.3 0.6 collective-permute-start.19
  92.0 1.3 %collective-permute-done.11.other = bf16[8,64,128]{2,1,0:T(8,128)(2,1)S(1)} collective-permute-done((bf16[8,64,128]{2,1,0:T(8,128)(2,1)S(1)}, bf16[8,64,128]{2,1,0:T(8,128)(2,1)S(1)}, u32[]{:S(2)}, u32[]{:S(2)}) %collective-permute-start.11) | collective-permute-done | bytes 131104 | tf_op jit(solution)/shard_map/ppermute | solution.py:376
  93.3 2.2 %shard_map.134.total = f32[128,1792]{1,0:T(8,128)S(1)} custom-call(bf16[8,64,128]{2,1,0:T(8,128)(2,1)S(1)} %all_to_all.5.mine, bf16[8,64,128]{2,1,0:T(8,128)(2,1)S(1)} %collective-permute-done.11.other, bf16[128,1792]{1,0:T(8,128)(2,1)S(1)} %multiply_convert_fusion.rest_0_, bf16[128,1792]{1,0:T(8,128)(2,1)} %collective-permute-done.12.rest_1_, ...), custom_call_target="tpu_custom_call" | custom-call | flops 1000000000 | bytes 2097152 | tf_op jit(solution)/shard_map/pallas_call | solution.py:381
  95.5 0.9 collective-permute-done.18.top
  96.3 1.0 %collective-permute-done.19.bottom = bf16[64,1792]{1,0:T(8,128)(2,1)S(1)} collective-permute-done((bf16[64,1792]{1,0:T(8,128)(2,1)S(1)}, bf16[64,1792]{1,0:T(8,128)(2,1)S(1)}, u32[]{:S(2)}, u32[]{:S(2)}) %collective-permute-start.19) | collective-permute-done | bytes 229408 | tf_op jit(solution)/shard_map/ppermute | solution.py:30
  97.4 0.3 shard_map.136
  97.7 1.5 %collective-permute-done.20 = bf16[64,1792]{1,0:T(8,128)(2,1)S(1)} collective-permute-done((bf16[64,1792]{1,0:T(8,128)(2,1)S(1)}, bf16[64,1792]{1,0:T(8,128)(2,1)S(1)}, u32[]{:S(2)}, u32[]{:S(2)}) %collective-permute-start.20) | collective-permute-done | bytes 229408 | tf_op jit(solution)/shard_map/ppermute | solution.py:388
  99.2 0.8 pad_maximum_fusion
  (59 shorter events, 0.5 us)
Async XLA Ops:
  0.0 3.0 %copy-start = (bf16[3584,2]{0,1:T(2,128)(2,1)S(1)}, bf16[3584,2]{0,1:T(2,128)(2,1)}, u32[]{:S(2)}) copy-start(bf16[3584,2]{0,1:T(2,128)(2,1)} %param.16) | copy-start | bytes 43012
  0.0 13.8 %collective-permute-start = (bf16[448,512]{1,0:T(8,128)(2,1)}, bf16[448,512]{1,0:T(8,128)(2,1)}, u32[]{:S(2)}, u32[]{:S(2)}) collective-permute-start(bf16[448,512]{1,0:T(8,128)(2,1)} %bitcast.11), channel_id=1, source_target_pairs={{0,2},{2,4},{4,6},{6,7},{7,5},{5,3},{3,1},{1,0},{8,10},{10,12},{12... | collective-permute-start | bytes 1376264 | tf_op jit(solution)/shard_map/ppermute | solution.py:30
  3.0 12.6 %collective-permute-start.2 = (bf16[448,512]{1,0:T(8,128)(2,1)}, bf16[448,512]{1,0:T(8,128)(2,1)S(1)}, u32[]{:S(2)}, u32[]{:S(2)}) collective-permute-start(bf16[448,512]{1,0:T(8,128)(2,1)} %bitcast.12), channel_id=1, source_target_pairs={{0,1},{2,0},{4,2},{6,4},{7,6},{5,7},{3,5},{1,3},{8,9},{10,8},{12,1... | collective-permute-start | bytes 1376264 | tf_op jit(solution)/shard_map/ppermute | solution.py:30
  4.2 1.5 %copy-start.1 = (bf16[2,3584,128]{2,1,0:T(8,128)(2,1)S(1)}, bf16[2,3584,128]{2,1,0:T(8,128)(2,1)}, u32[]{:S(2)}) copy-start(bf16[2,3584,128]{2,1,0:T(8,128)(2,1)} %refs_2_.7) | copy-start | bytes 5505028
  5.7 1.2 %copy-start.3 = (bf16[3584,128]{1,0:T(8,128)(2,1)S(1)}, bf16[3584,128]{1,0:T(8,128)(2,1)}, u32[]{:S(2)}) copy-start(bf16[3584,128]{1,0:T(8,128)(2,1)} %refs_3_.5) | copy-start | bytes 2752516
  6.8 1.0 %copy-start.10 = (bf16[512,448]{0,1:T(8,128)(2,1)S(1)}, bf16[512,448]{0,1:T(8,128)(2,1)}, u32[]{:S(2)}) copy-start(bf16[512,448]{0,1:T(8,128)(2,1)} %param.13) | copy-start | bytes 1376260
  7.9 8.0 %copy-start.18 = (s32[512]{0:T(512)S(1)}, s32[512]{0:T(512)}, u32[]{:S(2)}) copy-start(s32[512]{0:T(512)} %param.24) | copy-start | bytes 6148
  7.9 8.9 %copy-start.20 = (f32[2]{0:T(128)S(1)}, f32[2]{0:T(128)}, u32[]{:S(2)}) copy-start(f32[2]{0:T(128)} %param.17) | copy-start | bytes 28
  7.9 9.1 %copy-start.21 = (f32[2]{0:T(128)S(1)}, f32[2]{0:T(128)}, u32[]{:S(2)}) copy-start(f32[2]{0:T(128)} %param.18) | copy-start | bytes 28
  7.9 9.2 %copy-start.22 = (f32[2]{0:T(128)S(1)}, f32[2]{0:T(128)}, u32[]{:S(2)}) copy-start(f32[2]{0:T(128)} %param.19) | copy-start | bytes 28
  7.9 19.2 %copy-start.2 = (bf16[2,3584,128]{2,1,0:T(8,128)(2,1)S(1)}, bf16[2,3584,128]{2,1,0:T(8,128)(2,1)}, u32[]{:S(2)}) copy-start(bf16[2,3584,128]{2,1,0:T(8,128)(2,1)} %refs_2_.7) | copy-start | bytes 5505028
  8.5 1.0 copy-start.6
  13.8 18.1 %collective-permute-start.1 = (bf16[448,512]{1,0:T(8,128)(2,1)}, bf16[448,512]{1,0:T(8,128)(2,1)}, u32[]{:S(2)}, u32[]{:S(2)}) collective-permute-start(bf16[448,512]{1,0:T(8,128)(2,1)} %collective-permute-done.refs_0_), channel_id=1, source_target_pairs={{0,2},{2,4},{4,6},{6,7},{7,5},{5,3},{3,1},{1,0},{8,10},{10,12},{12... | collective-permute-start | bytes 1376264 | tf_op jit(solution)/shard_map/ppermute | solution.py:30
  15.6 16.3 %collective-permute-start.6 = (bf16[448,512]{1,0:T(8,128)(2,1)S(1)}, bf16[448,512]{1,0:T(8,128)(2,1)}, u32[]{:S(2)}, u32[]{:S(2)}) collective-permute-start(bf16[448,512]{1,0:T(8,128)(2,1)S(1)} %collective-permute-done.2.refs_1_), channel_id=1, source_target_pairs={{0,1},{2,0},{4,2},{6,4},{7,6},{5,7},{3,5},{1,3},{8,9},{10,8},{12,1... | collective-permute-start | bytes 1376264 | tf_op jit(solution)/shard_map/ppermute | solution.py:30
  17.3 16.7 %copy-start.19 = (f32[128]{0:T(128)S(1)}, f32[128]{0:T(128)}, u32[]{:S(2)}) copy-start(f32[128]{0:T(128)} %param.22) | copy-start | bytes 1540
  17.3 14.6 %collective-permute-start.3 = (bf16[8,448]{1,0:T(8,128)(2,1)S(1)}, bf16[8,448]{1,0:T(8,128)(2,1)S(1)}, u32[]{:S(2)}, u32[]{:S(2)}) collective-permute-start(bf16[8,448]{1,0:T(8,128)(2,1)S(1)} %copy.22), channel_id=1, source_target_pairs={{7,8},{5,10},{3,12},{1,14},{0,15},{2,13},{4,11},{6,9},{15,16},{13,... | collective-permute-start | bytes 21512 | tf_op jit(solution)/shard_map/ppermute | solution.py:309
  22.1 9.6 %collective-permute-start.4 = (s32[8]{0:T(128)S(1)}, s32[8]{0:T(128)S(1)}, u32[]{:S(2)}, u32[]{:S(2)}) collective-permute-start(s32[8]{0:T(128)S(1)} %slice.36), channel_id=1, source_target_pairs={{0,8},{8,16},{16,24},{1,9},{9,17},{17,25},{2,10},{10,18},{18,26},{... | collective-permute-start | bytes 104 | tf_op jit(solution)/shard_map/ppermute | solution.py:301
  27.1 1.2 %copy-start.4 = (bf16[3584,128]{1,0:T(8,128)(2,1)S(1)}, bf16[3584,128]{1,0:T(8,128)(2,1)}, u32[]{:S(2)}) copy-start(bf16[3584,128]{1,0:T(8,128)(2,1)} %refs_3_.5) | copy-start | bytes 2752516
  28.3 1.2 %copy-start.7 = (f32[512,512]{1,0:T(8,128)S(1)}, f32[512,512]{1,0:T(8,128)}, u32[]{:S(2)}) copy-start(f32[512,512]{1,0:T(8,128)} %copy-done.6) | copy-start | bytes 3145732
  29.5 4.4 %copy-start.17 = (bf16[128,3584]{1,0:T(8,128)(2,1)S(1)}, bf16[128,3584]{1,0:T(8,128)(2,1)}, u32[]{:S(2)}) copy-start(bf16[128,3584]{1,0:T(8,128)(2,1)} %param.23) | copy-start | bytes 2752516
  31.8 13.6 %collective-permute-start.5 = (bf16[448,512]{1,0:T(8,128)(2,1)}, bf16[448,512]{1,0:T(8,128)(2,1)S(1)}, u32[]{:S(2)}, u32[]{:S(2)}) collective-permute-start(bf16[448,512]{1,0:T(8,128)(2,1)} %collective-permute-done.1.refs_0_), channel_id=1, source_target_pairs={{0,2},{2,4},{4,6},{6,7},{7,5},{5,3},{3,1},{1,0},{8,10},{10,12},{12... | collective-permute-start | bytes 1376264 | tf_op jit(solution)/shard_map/ppermute | solution.py:30
  31.9 13.6 %collective-permute-start.7 = (bf16[448,512]{1,0:T(8,128)(2,1)}, bf16[448,512]{1,0:T(8,128)(2,1)S(1)}, u32[]{:S(2)}, u32[]{:S(2)}) collective-permute-start(bf16[448,512]{1,0:T(8,128)(2,1)} %collective-permute-done.6.refs_1_), channel_id=1, source_target_pairs={{0,1},{2,0},{4,2},{6,4},{7,6},{5,7},{3,5},{1,3},{8,9},{10,8},{12,1... | collective-permute-start | bytes 1376264 | tf_op jit(solution)/shard_map/ppermute | solution.py:30
  34.1 13.7 %copy-start.5 = (bf16[3584,128]{1,0:T(8,128)(2,1)S(1)}, bf16[3584,128]{1,0:T(8,128)(2,1)}, u32[]{:S(2)}) copy-start(bf16[3584,128]{1,0:T(8,128)(2,1)} %refs_3_.5) | copy-start | bytes 2752516
  34.1 21.3 %collective-permute-start.12 = (bf16[128,1792]{1,0:T(8,128)(2,1)S(1)}, bf16[128,1792]{1,0:T(8,128)(2,1)}, u32[]{:S(2)}, u32[]{:S(2)}) collective-permute-start(bf16[128,1792]{1,0:T(8,128)(2,1)S(1)} %multiply_convert_fusion.rest_0_), channel_id=1, source_target_pairs={{0,2},{2,4},{4,6},{6,7},{7,5},{5,3},{3,1},{1,0},{8,10},{10,12},{12... | collective-permute-start | bytes 1376264 | tf_op jit(solution)/shard_map/ppermute | solution.py:30
  34.2 21.3 %collective-permute-start.13 = (bf16[128,1792]{1,0:T(8,128)(2,1)S(1)}, bf16[128,1792]{1,0:T(8,128)(2,1)}, u32[]{:S(2)}, u32[]{:S(2)}) collective-permute-start(bf16[128,1792]{1,0:T(8,128)(2,1)S(1)} %multiply_convert_fusion.rest_0_), channel_id=1, source_target_pairs={{0,1},{2,0},{4,2},{6,4},{7,6},{5,7},{3,5},{1,3},{8,9},{10,8},{12,1... | collective-permute-start | bytes 1376264 | tf_op jit(solution)/shard_map/ppermute | solution.py:30
  45.6 13.7 %collective-permute-start.8 = (bf16[224,512]{1,0:T(8,128)(2,1)S(1)}, bf16[224,512]{1,0:T(8,128)(2,1)S(1)}, u32[]{:S(2)}, u32[]{:S(2)}) collective-permute-start(bf16[224,512]{1,0:T(8,128)(2,1)S(1)} %get-tuple-element.49), channel_id=1, source_target_pairs={{0,2},{2,4},{4,6},{6,7},{7,5},{5,3},{3,1},{1,0},{8,10},{10,12},{12... | collective-permute-start | bytes 688136 | tf_op jit(solution)/shard_map/ppermute | solution.py:30
  45.7 16.7 %copy-start.15 = (f32[4,128]{1,0:T(4,128)S(1)}, f32[4,128]{1,0:T(4,128)}, u32[]{:S(2)}) copy-start(f32[4,128]{1,0:T(4,128)} %taps_x.1) | copy-start | bytes 6148
  45.7 16.7 %copy-start.16 = (f32[4,128]{1,0:T(4,128)S(1)}, f32[4,128]{1,0:T(4,128)}, u32[]{:S(2)}) copy-start(f32[4,128]{1,0:T(4,128)} %taps_bc.1) | copy-start | bytes 6148
  45.7 13.7 %collective-permute-start.9 = (bf16[224,512]{1,0:T(8,128)(2,1)S(1)}, bf16[224,512]{1,0:T(8,128)(2,1)S(1)}, u32[]{:S(2)}, u32[]{:S(2)}) collective-permute-start(bf16[224,512]{1,0:T(8,128)(2,1)S(1)} %get-tuple-element.50), channel_id=1, source_target_pairs={{0,1},{2,0},{4,2},{6,4},{7,6},{5,7},{3,5},{1,3},{8,9},{10,8},{12,1... | collective-permute-start | bytes 688136 | tf_op jit(solution)/shard_map/ppermute | solution.py:30
  49.0 0.8 copy-start.11
  49.8 1.0 copy-start.8
  50.8 4.7 %collective-permute-start.10 = (f32[8,256]{1,0:T(8,128)S(1)}, f32[8,256]{1,0:T(8,128)S(1)}, u32[]{:S(2)}, u32[]{:S(2)}) collective-permute-start(f32[8,256]{1,0:T(8,128)S(1)} %slice.44), channel_id=1, source_target_pairs={{0,8},{8,16},{16,24},{1,9},{9,17},{17,25},{2,10},{10,18},{18,26},{... | collective-permute-start | bytes 24584 | tf_op jit(solution)/shard_map/ppermute | solution.py:347
  59.4 0.7 copy-start.13
  60.1 13.6 %collective-permute-start.14 = (bf16[128,1792]{1,0:T(8,128)(2,1)}, bf16[128,1792]{1,0:T(8,128)(2,1)S(1)}, u32[]{:S(2)}, u32[]{:S(2)}) collective-permute-start(bf16[128,1792]{1,0:T(8,128)(2,1)} %collective-permute-done.12.rest_1_), channel_id=1, source_target_pairs={{0,2},{2,4},{4,6},{6,7},{7,5},{5,3},{3,1},{1,0},{8,10},{10,12},{12... | collective-permute-start | bytes 1376264 | tf_op jit(solution)/shard_map/ppermute | solution.py:30
  60.3 13.4 %collective-permute-start.15 = (bf16[128,1792]{1,0:T(8,128)(2,1)}, bf16[128,1792]{1,0:T(8,128)(2,1)S(1)}, u32[]{:S(2)}, u32[]{:S(2)}) collective-permute-start(bf16[128,1792]{1,0:T(8,128)(2,1)} %collective-permute-done.13.rest_2_), channel_id=1, source_target_pairs={{0,1},{2,0},{4,2},{6,4},{7,6},{5,7},{3,5},{1,3},{8,9},{10,8},{12,1... | collective-permute-start | bytes 1376264 | tf_op jit(solution)/shard_map/ppermute | solution.py:30
  62.4 1.2 %copy-start.9 = (f32[512,512]{1,0:T(8,128)S(1)}, f32[512,512]{1,0:T(8,128)}, u32[]{:S(2)}) copy-start(f32[512,512]{1,0:T(8,128)} %copy-done.8) | copy-start | bytes 3145732
  63.6 1.0 %copy-start.12 = (bf16[448,512]{1,0:T(8,128)(2,1)S(1)}, bf16[448,512]{1,0:T(8,128)(2,1)}, u32[]{:S(2)}) copy-start(bf16[448,512]{1,0:T(8,128)(2,1)} %copy-done.11) | copy-start | bytes 1376260
  64.6 0.9 copy-start.14
  73.6 16.2 %collective-permute-start.16 = (bf16[128,1792]{1,0:T(8,128)(2,1)S(1)}, bf16[128,1792]{1,0:T(8,128)(2,1)S(1)}, u32[]{:S(2)}, u32[]{:S(2)}) collective-permute-start(bf16[128,1792]{1,0:T(8,128)(2,1)S(1)} %collective-permute-done.14.rest_3_), channel_id=1, source_target_pairs={{0,2},{2,4},{4,6},{6,7},{7,5},{5,3},{3,1},{1,0},{8,10},{10,12},{12... | collective-permute-start | bytes 1376264 | tf_op jit(solution)/shard_map/ppermute | solution.py:30
  73.9 15.9 %collective-permute-start.17 = (bf16[128,1792]{1,0:T(8,128)(2,1)S(1)}, bf16[128,1792]{1,0:T(8,128)(2,1)S(1)}, u32[]{:S(2)}, u32[]{:S(2)}) collective-permute-start(bf16[128,1792]{1,0:T(8,128)(2,1)S(1)} %collective-permute-done.15.rest_4_), channel_id=1, source_target_pairs={{0,1},{2,0},{4,2},{6,4},{7,6},{5,7},{3,5},{1,3},{8,9},{10,8},{12,1... | collective-permute-start | bytes 1376264 | tf_op jit(solution)/shard_map/ppermute | solution.py:30
  89.9 6.5 %collective-permute-start.18 = (bf16[64,1792]{1,0:T(8,128)(2,1)S(1)}, bf16[64,1792]{1,0:T(8,128)(2,1)S(1)}, u32[]{:S(2)}, u32[]{:S(2)}) collective-permute-start(bf16[64,1792]{1,0:T(8,128)(2,1)S(1)} %get-tuple-element.73), channel_id=1, source_target_pairs={{0,2},{2,4},{4,6},{6,7},{7,5},{5,3},{3,1},{1,0},{8,10},{10,12},{12... | collective-permute-start | bytes 688136 | tf_op jit(solution)/shard_map/ppermute | solution.py:30
  91.3 6.0 %collective-permute-start.19 = (bf16[64,1792]{1,0:T(8,128)(2,1)S(1)}, bf16[64,1792]{1,0:T(8,128)(2,1)S(1)}, u32[]{:S(2)}, u32[]{:S(2)}) collective-permute-start(bf16[64,1792]{1,0:T(8,128)(2,1)S(1)} %get-tuple-element.74), channel_id=1, source_target_pairs={{0,1},{2,0},{4,2},{6,4},{7,6},{5,7},{3,5},{1,3},{8,9},{10,8},{12,1... | collective-permute-start | bytes 688136 | tf_op jit(solution)/shard_map/ppermute | solution.py:30
  92.0 1.3 %collective-permute-start.11 = (bf16[8,64,128]{2,1,0:T(8,128)(2,1)S(1)}, bf16[8,64,128]{2,1,0:T(8,128)(2,1)S(1)}, u32[]{:S(2)}, u32[]{:S(2)}) collective-permute-start(bf16[8,64,128]{2,1,0:T(8,128)(2,1)S(1)} %all_to_all.5.mine), channel_id=1, source_target_pairs={{0,8},{8,0},{16,24},{24,16},{1,9},{9,1},{17,25},{25,17},{2,10},{10... | collective-permute-start | bytes 393224 | tf_op jit(solution)/shard_map/ppermute | solution.py:376
  97.6 1.6 %collective-permute-start.20 = (bf16[64,1792]{1,0:T(8,128)(2,1)S(1)}, bf16[64,1792]{1,0:T(8,128)(2,1)S(1)}, u32[]{:S(2)}, u32[]{:S(2)}) collective-permute-start(bf16[64,1792]{1,0:T(8,128)(2,1)S(1)} %get-tuple-element.76), channel_id=1, source_target_pairs={{0,8},{8,0},{16,24},{24,16},{1,9},{9,1},{17,25},{25,17},{2,10},{10... | collective-permute-start | bytes 688136 | tf_op jit(solution)/shard_map/ppermute | solution.py:388

commit v11 on v7

--- a/solution.py
+++ b/solution.py
@@ -14,6 +14,7 @@
 VMEM = pl.BlockSpec(memory_space=pltpu.VMEM)
 ANY = pl.BlockSpec(memory_space=pl.ANY)
 HALO = 8
+W_FIRST = 3
 
 
 def ring_place(index, n):
@@ -45,15 +46,6 @@
     size = top.shape[0]
     top[...] = forth[:size]
     bottom[...] = back[size:]
-
-
-def join(*refs):
-    count = len(refs) // 3
-    odd = lax.axis_index("seq") // 2 % 2
-    for own, other, out in zip(refs[:count], refs[count : 2 * count], refs[2 * count :]):
-        size = own.shape[0]
-        out[pl.ds(pl.multiple_of(odd * size, size), size)] = own[...]
-        out[pl.ds(pl.multiple_of((1 - odd) * size, size), size)] = other[...]
 
 
 def silu(v):
@@ -214,17 +206,12 @@
     message[state_w + 2 :] = jnp.zeros((message.shape[0] - state_w - 2, width), F32)
 
 
-def first_inner(heads, width, rows, conv_x, conv_bc, cum, scaled, proj, seg_col, seg_row, skip, out, gate_out):
-    gate_out[...] = silu(proj[:rows, :width].astype(BF16).astype(F32))
-    out[...] = (
-        block_inner(conv_bc[...], cum[...], scaled[...], seg_col[HALO:], seg_row[...], heads) + skip[...] * conv_x[...]
-    )
-
-
-def finish(rows, seg_first, messages, out_a, gate_a, bc_a, enter_a, state_a, out_b, gate_b, bc_b, enter_b, gated):
+def finish(heads, rows, seg_first, messages, seg_ext_a, seg_row_a, skip, proj, conv_a, bc_a, cum_a, scaled_a, enter_a,
+           state_a, out_b, gate_b, bc_b, enter_b, gated):
     state_w = bc_a.shape[1] // 2
-    entering = jnp.zeros((state_w, out_a.shape[1]), F32)
-    decay = jnp.zeros((1, out_a.shape[1]), F32)
+    width = out_b.shape[1]
+    entering = jnp.zeros((state_w, width), F32)
+    decay = jnp.zeros((1, width), F32)
     first = seg_first[...].astype(F32)
     place = lax.axis_index("seq")
     for device in reversed(range(messages.shape[0] - 1)):
@@ -234,7 +221,9 @@
         entering = entering + passes * messages[device, :state_w]
         decay = decay + jnp.where(earlier, messages[device, state_w : state_w + 1], 0.0)
     second = state_a[state_w : state_w + 1] * entering + state_a[:state_w]
-    gated[:rows] = ((out_a[...] + enter_a[...] * dot(bc_a[:, state_w:], entering)) * gate_a[...]).astype(BF16)
+    out_a = block_inner(bc_a[...], cum_a[...], scaled_a[...], seg_ext_a[HALO:], seg_row_a[...], heads)
+    out_a = out_a + skip[...] * conv_a[...] + enter_a[...] * dot(bc_a[:, state_w:], entering)
+    gated[:rows] = (out_a * silu(proj[:rows, :width].astype(BF16).astype(F32))).astype(BF16)
     gated[rows:] = ((out_b[...] + enter_b[...] * dot(bc_b[:, state_w:], second)) * gate_b[...]).astype(BF16)
 
 
@@ -299,8 +288,6 @@
     own = (lax.dynamic_slice_in_dim(w_out, core * columns, columns, 1).astype(F32) * norm_gain[:, None]).astype(BF16)
     last = n_tensor // 2
     w_half = width // 2
-    own_rows = lax.dynamic_slice_in_dim(own, seq_at // 2 % 2 * w_half, w_half, 0)
-    other_y = [(i, i ^ 2) for i in range(n_seq)]
     shift_rows = [(i, i + 1) for i in range(n_seq - 1)]
 
     seg_halo = lax.ppermute(segments[tok_rows - HALO :], "seq", shift_rows)
@@ -317,21 +304,16 @@
     for step in range(1, last + 1):
         if step == 3:
             forth, back = after(forth, projs[1], small), after(back, projs[1], small)
-            w_arrived = after(w_arrived, forth, back)
         elif step > 1:
             forth, back = after(forth, projs[step - 2]), after(back, projs[step - 2])
-        if step == 4:
-            w_swapped, forth, back = after((w_swapped, forth, back))
-        if step == 2:
-            w_sent = after(own_rows, forth, back)
+        arrivals = (forth, back)
         if step < last:
             forth, back = ring_shift(forth, 1), ring_shift(back, -1)
         else:
             far = far_shift(forth, back)
-        if step == 2:
-            w_arrived = ring_shift(w_sent, 1), ring_shift(w_sent, -1)
-        if step == 3:
-            w_swapped = [lax.ppermute(part, "seq", other_y) for part in w_arrived]
+        if step == W_FIRST:
+            w_forth, w_back = after((own, own), arrivals)
+            w_forth, w_back = ring_shift(w_forth, 1), ring_shift(w_back, -1)
         ahead = last if step == last else 0
         total = projs[-1:]
         fetched = len(arrived) + bool(ahead)
@@ -345,10 +327,8 @@
         )(*[part for _, part in arrived], w_zx, w_bc, w_step, *total)
         projs.append(results[0])
         arrived = [(-step, forth), (step, back)]
-    whole = shape(width, columns, kind=BF16)
-    w_forth, w_back = call(join, [whole, whole])(*w_arrived, *w_swapped)
     proj = call(project_far, shape(tok_rows, 4 * width), flops=10**9)(
-        *far, results[1], after(projs[-1], w_forth, w_back)
+        *far, results[1], projs[-1]
     )
 
     (seg_ext_a, seg_ext_b), (seg_row_a, seg_row_b), (seg_first, seg_last), (bias, rate, skip) = small
@@ -368,17 +348,14 @@
         [ext, ext],
     )(proj, halo, seg_ext_a, seg_last, state_b, conv_x, conv_bc, bias, rate)
     messages = lax.all_gather(message, "seq")
-    out_a, gate_a = call(functools.partial(first_inner, heads, width, rows), [plane, plane])(
-        cx_a, bc_a, cum_a, scaled_a, proj, seg_ext_a, seg_row_a, skip
-    )
-    gated = call(functools.partial(finish, rows), shape(tok_rows, width, kind=BF16))(
-        seg_first, messages, out_a, gate_a, bc_a, enter_a, state_a, out_b, gate_b, bc_b, enter_b
-    )
-
+    gated = call(functools.partial(finish, heads, rows), shape(tok_rows, width, kind=BF16))(
+        seg_first, messages, seg_ext_a, seg_row_a, skip, proj, cx_a, bc_a, cum_a, scaled_a, enter_a, state_a,
+        out_b, gate_b, bc_b, enter_b
+    )
     tok_own = tok_rows // n_tensor
 
     w_steps = [(w_forth, w_back)]
-    orders = [(proj, halo), messages]
+    orders = [proj, messages]
     for step in range(2, last + 1):
         if step - 2 < len(orders):
             w_forth, w_back = after((w_forth, w_back), orders[step - 2])

time: 97.1 us -> 94.8 us (0.976)
  starting transfers between devices: 22.3 us -> 20.2 us
  waiting for transfers between devices: 27.4 us -> 29.4 us
  Pallas kernels: 16 us -> 14.7 us
  local copies, waits for them, and re-layouts: 7.19 us -> 5.91 us
    ppermute x16, waiting for transfers between devices: 21.6 us -> 26.6 us  [ring_shift(): lax.ppermute(block, 'tensor', [(order[i], order[(i + step) % n]) for i in...]
    ppermute x2 -> x0, waiting for transfers between devices: 2.13 us -> none  [local(): w_swapped = [lax.ppermute(part, 'seq', other_y) for part in w_arrived]]
    ppermute x2 -> x0, starting transfers between devices: 2.03 us -> none  [local(): w_swapped = [lax.ppermute(part, 'seq', other_y) for part in w_arrived]]
    pallas_call x3 -> x1, Pallas kernels: 2.41 us -> 1.18 us  [local(): call(functools.partial(finish, heads, rows), shape(tok_rows, width, kind=...]
  transfers between devices with their start and end apart: 22 -> 20, of which waited for: 16 -> 10; matrix products, arithmetic and copies ran while one was open for 4% -> 4% of each run, Pallas kernels for 16% -> 15%
where the time goes in v11:
time: 94.8 us; the launch traced here: 94.2 us
  waiting for transfers between devices  29.4 us (31%)
  blocking collectives  21.6 us (23%)
  starting transfers between devices  20.2 us (21%)
  Pallas kernels  14.7 us (16%)
  local copies, waits for them, and re-layouts  5.91 us (6%)
  matrix products  1.12 us (1%)
  other arithmetic  1.05 us (1%)
    ppermute x16, waiting for transfers between devices, ring_shift(): lax.ppermute(block, 'tensor', [(order[i], order[(i + step) % n]) for i in...  26.6 us
    ppermute x16, starting transfers between devices, ring_shift(): lax.ppermute(block, 'tensor', [(order[i], order[(i + step) % n]) for i in...  17.4 us
    all_to_all x1, blocking collectives, local(): mine = lax.all_to_all(blocks, 'tensor', 0, 0)  14.8 us
    pallas_call x4, Pallas kernels, local(): call(functools.partial(project, [distance for distance, _ in arrived], ah...  8.47 us
    all_gather x1, blocking collectives, local(): messages = lax.all_gather(message, 'seq')  6.82 us
    unnamed x26, local copies, waits for them, and re-layouts  3.73 us
    pallas_call x1, Pallas kernels, local(): call(functools.partial(product_early, distances), shape(2 * tok_own, colu...  2.01 us
  transfers between devices with their start and end apart: 20, of which 10 were waited for; matrix products, arithmetic and copies ran while one was open for 4% of the time, Pallas kernels for 15%

profile of v11, /device:TPU:0, one launch (start us, length us, event | category | flops | bytes accessed | tf_op | source)
XLA Modules:
  0.0 94.2 jit_solution(9863276744935303015)
XLA Ops:
  0.0 3.0 %collective-permute-start = (bf16[448,512]{1,0:T(8,128)(2,1)}, bf16[448,512]{1,0:T(8,128)(2,1)}, u32[]{:S(2)}, u32[]{:S(2)}) collective-permute-start(bf16[448,512]{1,0:T(8,128)(2,1)} %bitcast.13), channel_id=1, source_target_pairs={{0,2},{2,4},{4,6},{6,7},{7,5},{5,3},{3,1},{1,0},{8,10},{10,12},{12... | collective-permute-start | bytes 1376264 | tf_op jit(solution)/shard_map/ppermute | solution.py:31
  3.0 0.0 collective-permute-start.2
  3.0 0.8 slice.33
  3.8 1.4 %collective-permute-start.3 = (s32[8]{0:T(128)S(1)}, s32[8]{0:T(128)S(1)}, u32[]{:S(2)}, u32[]{:S(2)}) collective-permute-start(s32[8]{0:T(128)S(1)} %slice.33), channel_id=1, source_target_pairs={{0,8},{8,16},{16,24},{1,9},{9,17},{17,25},{2,10},{10,18},{18,26},{... | collective-permute-start | bytes 104 | tf_op jit(solution)/shard_map/ppermute | solution.py:293
  5.2 1.1 %convolution_bitcast_fusion.refs_3_.refs_4_ = bf16[3584,128]{1,0:T(8,128)(2,1)S(1)} fusion(bf16[2,128]{1,0:T(2,128)(2,1)} %constant.25.clone, bf16[3584,2]{0,1:T(2,128)(2,1)S(1)} %copy-done), kind=kOutput, calls=%fused_computation | convolution fusion | flops 1835008 | bytes 932352 | tf_op jit(solution)/shard_map/dot_general | solution.py:284
  6.4 0.0 copy-start.1
  6.4 1.5 %copy-done.1 = bf16[2,3584,128]{2,1,0:T(8,128)(2,1)S(1)} copy-done((bf16[2,3584,128]{2,1,0:T(8,128)(2,1)S(1)}, bf16[2,3584,128]{2,1,0:T(8,128)(2,1)}, u32[]{:S(2)}) %copy-start.1) | copy-done | bytes 1835032
  7.9 1.2 %copy-done.2 = bf16[3584,128]{1,0:T(8,128)(2,1)S(1)} copy-done((bf16[3584,128]{1,0:T(8,128)(2,1)S(1)}, bf16[3584,128]{1,0:T(8,128)(2,1)}, u32[]{:S(2)}) %copy-start.2) | copy-done | bytes 917528
  9.1 1.0 %copy-done.4 = bf16[512,448]{0,1:T(8,128)(2,1)S(1)} copy-done((bf16[512,448]{0,1:T(8,128)(2,1)S(1)}, bf16[512,448]{0,1:T(8,128)(2,1)}, u32[]{:S(2)}) %copy-start.4) | copy-done | bytes 458776
  10.1 0.6 shard_map.127.refs_5_
  10.7 3.1 %collective-permute-done.refs_0_ = bf16[448,512]{1,0:T(8,128)(2,1)} collective-permute-done((bf16[448,512]{1,0:T(8,128)(2,1)}, bf16[448,512]{1,0:T(8,128)(2,1)}, u32[]{:S(2)}, u32[]{:S(2)}) %collective-permute-start) | collective-permute-done | bytes 458784 | tf_op jit(solution)/shard_map/ppermute | solution.py:31
  13.8 1.8 %collective-permute-start.1 = (bf16[448,512]{1,0:T(8,128)(2,1)}, bf16[448,512]{1,0:T(8,128)(2,1)}, u32[]{:S(2)}, u32[]{:S(2)}) collective-permute-start(bf16[448,512]{1,0:T(8,128)(2,1)} %collective-permute-done.refs_0_), channel_id=1, source_target_pairs={{0,2},{2,4},{4,6},{6,7},{7,5},{5,3},{3,1},{1,0},{8,10},{10,12},{12... | collective-permute-start | bytes 1376264 | tf_op jit(solution)/shard_map/ppermute | solution.py:31
  15.6 0.0 collective-permute-done.2.refs_1_
  15.6 0.2 collective-permute-start.5
  15.8 0.6 fusion
  16.4 0.1 slice.36
  16.5 0.1 broadcast_in_dim.27
  16.5 0.1 broadcast_in_dim_reshape.9.bias
  16.6 0.1 broadcast_in_dim.28
  16.7 0.1 broadcast_in_dim_reshape.10.rate
  16.8 0.1 broadcast_in_dim.29
  16.9 0.1 broadcast_in_dim_reshape.11.skip
  17.0 0.1 pad_add_fusion
  17.0 0.0 copy-start.9
  17.1 3.0 %shard_map.128.refs_5_ = f32[512,512]{1,0:T(8,128)S(1)} custom-call(bf16[448,512]{1,0:T(8,128)(2,1)} %collective-permute-done.refs_0_, bf16[448,512]{1,0:T(8,128)(2,1)S(1)} %collective-permute-done.2.refs_1_, bf16[2,3584,128]{2,1,0:T(8,128)(2,1)} %refs_2_.7, bf16[3584,128]{1,0:T(8,128)(2,1)S(1)} %copy-done.3, ...), custom_call_target="tpu_custom_call" | custom-call | flops 1000000000 | bytes 2097152 | tf_op jit(solution)/shard_map/pallas_call | solution.py:321
  20.0 6.0 %collective-permute-done.1.refs_0_ = bf16[448,512]{1,0:T(8,128)(2,1)} collective-permute-done((bf16[448,512]{1,0:T(8,128)(2,1)}, bf16[448,512]{1,0:T(8,128)(2,1)}, u32[]{:S(2)}, u32[]{:S(2)}) %collective-permute-start.1) | collective-permute-done | bytes 458784 | tf_op jit(solution)/shard_map/ppermute | solution.py:31
  26.0 1.6 %collective-permute-start.4 = (bf16[448,512]{1,0:T(8,128)(2,1)}, bf16[448,512]{1,0:T(8,128)(2,1)S(1)}, u32[]{:S(2)}, u32[]{:S(2)}) collective-permute-start(bf16[448,512]{1,0:T(8,128)(2,1)} %collective-permute-done.1.refs_0_), channel_id=1, source_target_pairs={{0,2},{2,4},{4,6},{6,7},{7,5},{5,3},{3,1},{1,0},{8,10},{10,12},{12... | collective-permute-start | bytes 1376264 | tf_op jit(solution)/shard_map/ppermute | solution.py:31
  27.6 0.0 collective-permute-done.5.refs_1_
  27.6 0.4 collective-permute-start.6
  28.1 0.1 multiply_convert_fusion.rest_0_
  28.2 1.6 %collective-permute-start.10 = (bf16[128,1792]{1,0:T(8,128)(2,1)S(1)}, bf16[128,1792]{1,0:T(8,128)(2,1)S(1)}, u32[]{:S(2)}, u32[]{:S(2)}) collective-permute-start(bf16[128,1792]{1,0:T(8,128)(2,1)S(1)} %multiply_convert_fusion.rest_0_), channel_id=1, source_target_pairs={{0,2},{2,4},{4,6},{6,7},{7,5},{5,3},{3,1},{1,0},{8,10},{10,12},{12... | collective-permute-start | bytes 1376264 | tf_op jit(solution)/shard_map/ppermute | solution.py:31
  29.9 0.4 collective-permute-start.11
  30.3 3.0 %shard_map.129.refs_5_ = f32[512,512]{1,0:T(8,128)S(1)} custom-call(bf16[448,512]{1,0:T(8,128)(2,1)} %collective-permute-done.1.refs_0_, bf16[448,512]{1,0:T(8,128)(2,1)} %collective-permute-done.5.refs_1_, bf16[2,3584,128]{2,1,0:T(8,128)(2,1)} %refs_2_.7, bf16[3584,128]{1,0:T(8,128)(2,1)S(1)} %copy-done.3, ...), custom_call_target="tpu_custom_call" | custom-call | flops 1000000000 | bytes 2097152 | tf_op jit(solution)/shard_map/pallas_call | solution.py:321
  33.3 6.4 %collective-permute-done.4.forth.refs_0_ = bf16[448,512]{1,0:T(8,128)(2,1)S(1)} collective-permute-done((bf16[448,512]{1,0:T(8,128)(2,1)}, bf16[448,512]{1,0:T(8,128)(2,1)S(1)}, u32[]{:S(2)}, u32[]{:S(2)}) %collective-permute-start.4) | collective-permute-done | bytes 458784 | tf_op jit(solution)/shard_map/ppermute | solution.py:31
  39.7 1.6 %collective-permute-done.6.back.refs_1_ = bf16[448,512]{1,0:T(8,128)(2,1)S(1)} collective-permute-done((bf16[448,512]{1,0:T(8,128)(2,1)}, bf16[448,512]{1,0:T(8,128)(2,1)S(1)}, u32[]{:S(2)}, u32[]{:S(2)}) %collective-permute-start.6) | collective-permute-done | bytes 458784 | tf_op jit(solution)/shard_map/ppermute | solution.py:31
  41.3 1.6 %collective-permute-start.7 = (bf16[224,512]{1,0:T(8,128)(2,1)S(1)}, bf16[224,512]{1,0:T(8,128)(2,1)S(1)}, u32[]{:S(2)}, u32[]{:S(2)}) collective-permute-start(bf16[224,512]{1,0:T(8,128)(2,1)S(1)} %get-tuple-element.46), channel_id=1, source_target_pairs={{0,2},{2,4},{4,6},{6,7},{7,5},{5,3},{3,1},{1,0},{8,10},{10,12},{12... | collective-permute-start | bytes 688136 | tf_op jit(solution)/shard_map/ppermute | solution.py:31
  43.0 0.5 collective-permute-start.8
  43.4 1.9 %shard_map.131 = (f32[512,512]{1,0:T(8,128)S(1)}, bf16[448,512]{1,0:T(8,128)(2,1)S(1)}) custom-call(bf16[448,512]{1,0:T(8,128)(2,1)S(1)} %collective-permute-done.4.forth.refs_0_, bf16[448,512]{1,0:T(8,128)(2,1)S(1)} %collective-permute-done.6.back.refs_1_, bf16[2,3584,128]{2,1,0:T(8,128)(2,1)} %refs_2_.7, bf16[3584,128]{1,0:T(8,128)(2,1)S(1)} %copy-done.3, ...), custom_call_target="tpu_custom_call" | custom-call | flops 1000000000 | bytes 2097152 | tf_op jit(solution)/shard_map/pallas_call | solution.py:321
  45.3 6.8 %collective-permute-done.7.top = bf16[224,512]{1,0:T(8,128)(2,1)S(1)} collective-permute-done((bf16[224,512]{1,0:T(8,128)(2,1)S(1)}, bf16[224,512]{1,0:T(8,128)(2,1)S(1)}, u32[]{:S(2)}, u32[]{:S(2)}) %collective-permute-start.7) | collective-permute-done | bytes 229408 | tf_op jit(solution)/shard_map/ppermute | solution.py:31
  52.0 1.0 %collective-permute-done.8.bottom = bf16[224,512]{1,0:T(8,128)(2,1)S(1)} collective-permute-done((bf16[224,512]{1,0:T(8,128)(2,1)S(1)}, bf16[224,512]{1,0:T(8,128)(2,1)S(1)}, u32[]{:S(2)}, u32[]{:S(2)}) %collective-permute-start.8) | collective-permute-done | bytes 229408 | tf_op jit(solution)/shard_map/ppermute | solution.py:31
  53.1 0.5 shard_map.132.proj
  53.6 0.0 collective-permute-done.11.rest_2_
  53.6 1.6 %collective-permute-start.12 = (bf16[128,1792]{1,0:T(8,128)(2,1)S(1)}, bf16[128,1792]{1,0:T(8,128)(2,1)S(1)}, u32[]{:S(2)}, u32[]{:S(2)}) collective-permute-start(bf16[128,1792]{1,0:T(8,128)(2,1)S(1)} %collective-permute-done.10.rest_1_), channel_id=1, source_target_pairs={{0,2},{2,4},{4,6},{6,7},{7,5},{5,3},{3,1},{1,0},{8,10},{10,12},{12... | collective-permute-start | bytes 1376264 | tf_op jit(solution)/shard_map/ppermute | solution.py:31
  55.2 0.5 collective-permute-start.13
  55.7 1.3 %collective-permute-start.9 = (bf16[8,256]{1,0:T(8,128)(2,1)S(1)}, bf16[8,256]{1,0:T(8,128)(2,1)S(1)}, u32[]{:S(2)}, u32[]{:S(2)}) collective-permute-start(bf16[8,256]{1,0:T(8,128)(2,1)S(1)} %slice.44), channel_id=1, source_target_pairs={{0,8},{8,16},{16,24},{1,9},{9,17},{17,25},{2,10},{10,18},{18,26},{... | collective-permute-start | bytes 12296 | tf_op jit(solution)/shard_map/ppermute | solution.py:335
  57.0 0.1 copy.16.seg_ext
  57.1 0.1 copy.17.seg_ext.seg_ext_a
  57.3 1.0 %shard_map.133 = (f32[256,128]{1,0:T(8,128)S(1)}, f32[256,128]{1,0:T(8,128)S(1)}, f32[256,128]{1,0:T(8,128)S(1)}, f32[72,128]{1,0:T(8,128)S(1)}, f32[256,128]{1,0:T(8,128)S(1)}) custom-call(f32[512,512]{1,0:T(8,128)S(1)} %shard_map.132.proj, s32[264,1]{1,0:T(8,128)S(1)} %copy.16.seg_ext, s32[1,256]{1,0:T(1,128)S(1)} %bitcast.17, f32[4,128]{1,0:T(4,128)S(1)} %copy-done.5, ...), custom_call_target="tpu_custom_call" | custom-call | flops 10000000 | bytes 2097152 | tf_op jit(solution)/shard_map/pallas_call | solution.py:340
  58.3 1.2 %shard_map.134 = (f32[256,128]{1,0:T(8,128)S(1)}, f32[256,128]{1,0:T(8,128)S(1)}, f32[256,128]{1,0:T(8,128)S(1)}, f32[256,128]{1,0:T(8,128)S(1)}, f32[256,128]{1...) custom-call(f32[512,512]{1,0:T(8,128)S(1)} %shard_map.132.proj, ...), custom_call_target="tpu_custom_call" | custom-call | flops 10000000 | bytes 2097152 | tf_op jit(solution)/shard_map/pallas_call | solution.py:345
  59.5 6.8 %all-gather = f32[288,128]{1,0:T(8,128)S(1)} all-gather(f32[72,128]{1,0:T(8,128)S(1)} %get-tuple-element.51), channel_id=2, replica_groups=mesh['seq'=4,'tensor'=8] {'seq'}, dimensions={0}, use_global_device_ids=true | all-gather | bytes 184320 | tf_op jit(solution)/shard_map/all_gather | solution.py:350
  66.4 1.6 %collective-permute-start.15 = (bf16[128,1792]{1,0:T(8,128)(2,1)S(1)}, bf16[128,1792]{1,0:T(8,128)(2,1)S(1)}, u32[]{:S(2)}, u32[]{:S(2)}) collective-permute-start(bf16[128,1792]{1,0:T(8,128)(2,1)S(1)} %collective-permute-done.12.rest_3_), channel_id=1, source_target_pairs={{0,2},{2,4},{4,6},{6,7},{7,5},{5,3},{3,1},{1,0},{8,10},{10,12},{12... | collective-permute-start | bytes 1376264 | tf_op jit(solution)/shard_map/ppermute | solution.py:31
  68.0 0.4 collective-permute-start.16
  68.4 1.2 %shard_map.135 = bf16[512,128]{1,0:T(8,128)(2,1)S(1)} custom-call(s32[1,1]{1,0:T(1,128)} %bitcast.seg_first, f32[4,72,128]{2,1,0:T(8,128)S(1)} %bitcast.11, s32[264,1]{1,0:T(8,128)S(1)} %copy.17.seg_ext.seg_ext_a, s32[1,256]{1,0:T(1,128)S(1)} %bitcast.16, f32[1,128]{1,0:T(1,128)S(1)} %broadcast_in_dim_reshape.11.skip, f32[512,512]{1,0:T(8,128)S(1)} %shard_map.132.proj, ...), custom_call_target="tpu_custom_call" | custom-call | flops 10000000 | bytes 2097152 | tf_op jit(solution)/shard_map/pallas_call | solution.py:351
  69.6 14.8 %all_to_all.5.mine = bf16[8,64,128]{2,1,0:T(8,128)(2,1)S(1)} all-to-all(bf16[8,64,128]{2,1,0:T(8,128)(2,1)S(1)} %bitcast.12), channel_id=1, replica_groups=mesh['seq'=4,'tensor'=8] {'tensor'}, dimensions={0} | all-to-all | bytes 262144 | tf_op jit(solution)/shard_map/all_to_all | solution.py:371
  84.4 1.0 %collective-permute-start.17 = (bf16[64,1792]{1,0:T(8,128)(2,1)S(1)}, bf16[64,1792]{1,0:T(8,128)(2,1)S(1)}, u32[]{:S(2)}, u32[]{:S(2)}) collective-permute-start(bf16[64,1792]{1,0:T(8,128)(2,1)S(1)} %get-tuple-element.71), channel_id=1, source_target_pairs={{0,2},{2,4},{4,6},{6,7},{7,5},{5,3},{3,1},{1,0},{8,10},{10,12},{12... | collective-permute-start | bytes 688136 | tf_op jit(solution)/shard_map/ppermute | solution.py:31
  85.4 1.1 %collective-permute-start.18 = (bf16[64,1792]{1,0:T(8,128)(2,1)S(1)}, bf16[64,1792]{1,0:T(8,128)(2,1)S(1)}, u32[]{:S(2)}, u32[]{:S(2)}) collective-permute-start(bf16[64,1792]{1,0:T(8,128)(2,1)S(1)} %get-tuple-element.72), channel_id=1, source_target_pairs={{0,1},{2,0},{4,2},{6,4},{7,6},{5,7},{3,5},{1,3},{8,9},{10,8},{12,1... | collective-permute-start | bytes 688136 | tf_op jit(solution)/shard_map/ppermute | solution.py:31
  86.5 1.3 %collective-permute-done.14.other = bf16[8,64,128]{2,1,0:T(8,128)(2,1)S(1)} collective-permute-done((bf16[8,64,128]{2,1,0:T(8,128)(2,1)S(1)}, bf16[8,64,128]{2,1,0:T(8,128)(2,1)S(1)}, u32[]{:S(2)}, u32[]{:S(2)}) %collective-permute-start.14) | collective-permute-done | bytes 131104 | tf_op jit(solution)/shard_map/ppermute | solution.py:373
  87.8 2.0 %shard_map.136.total = f32[128,1792]{1,0:T(8,128)S(1)} custom-call(bf16[8,64,128]{2,1,0:T(8,128)(2,1)S(1)} %all_to_all.5.mine, bf16[8,64,128]{2,1,0:T(8,128)(2,1)S(1)} %collective-permute-done.14.other, bf16[128,1792]{1,0:T(8,128)(2,1)S(1)} %multiply_convert_fusion.rest_0_, bf16[128,1792]{1,0:T(8,128)(2,1)S(1)} %collective-permute-done.10.rest_1_, ...), custom_call_target="tpu_custom_call" | custom-call | flops 1000000000 | bytes 2097152 | tf_op jit(solution)/shard_map/pallas_call | solution.py:378
  89.9 0.8 collective-permute-done.17.top
  90.6 0.9 collective-permute-done.18.bottom
  91.6 0.3 shard_map.138
  91.8 0.1 collective-permute-start.19
  91.9 1.5 %collective-permute-done.19 = bf16[64,1792]{1,0:T(8,128)(2,1)S(1)} collective-permute-done((bf16[64,1792]{1,0:T(8,128)(2,1)S(1)}, bf16[64,1792]{1,0:T(8,128)(2,1)S(1)}, u32[]{:S(2)}, u32[]{:S(2)}) %collective-permute-start.19) | collective-permute-done | bytes 229408 | tf_op jit(solution)/shard_map/ppermute | solution.py:385
  93.4 0.8 pad_maximum_fusion
  (37 shorter events, 0.2 us)
Async XLA Ops:
  0.0 5.2 %copy-start = (bf16[3584,2]{0,1:T(2,128)(2,1)S(1)}, bf16[3584,2]{0,1:T(2,128)(2,1)}, u32[]{:S(2)}) copy-start(bf16[3584,2]{0,1:T(2,128)(2,1)} %param.16) | copy-start | bytes 43012
  0.0 13.8 %collective-permute-start = (bf16[448,512]{1,0:T(8,128)(2,1)}, bf16[448,512]{1,0:T(8,128)(2,1)}, u32[]{:S(2)}, u32[]{:S(2)}) collective-permute-start(bf16[448,512]{1,0:T(8,128)(2,1)} %bitcast.13), channel_id=1, source_target_pairs={{0,2},{2,4},{4,6},{6,7},{7,5},{5,3},{3,1},{1,0},{8,10},{10,12},{12... | collective-permute-start | bytes 1376264 | tf_op jit(solution)/shard_map/ppermute | solution.py:31
  3.0 12.6 %collective-permute-start.2 = (bf16[448,512]{1,0:T(8,128)(2,1)}, bf16[448,512]{1,0:T(8,128)(2,1)S(1)}, u32[]{:S(2)}, u32[]{:S(2)}) collective-permute-start(bf16[448,512]{1,0:T(8,128)(2,1)} %bitcast.14), channel_id=1, source_target_pairs={{0,1},{2,0},{4,2},{6,4},{7,6},{5,7},{3,5},{1,3},{8,9},{10,8},{12,1... | collective-permute-start | bytes 1376264 | tf_op jit(solution)/shard_map/ppermute | solution.py:31
  3.8 13.2 %collective-permute-start.3 = (s32[8]{0:T(128)S(1)}, s32[8]{0:T(128)S(1)}, u32[]{:S(2)}, u32[]{:S(2)}) collective-permute-start(s32[8]{0:T(128)S(1)} %slice.33), channel_id=1, source_target_pairs={{0,8},{8,16},{16,24},{1,9},{9,17},{17,25},{2,10},{10,18},{18,26},{... | collective-permute-start | bytes 104 | tf_op jit(solution)/shard_map/ppermute | solution.py:293
  6.4 1.5 %copy-start.1 = (bf16[2,3584,128]{2,1,0:T(8,128)(2,1)S(1)}, bf16[2,3584,128]{2,1,0:T(8,128)(2,1)}, u32[]{:S(2)}) copy-start(bf16[2,3584,128]{2,1,0:T(8,128)(2,1)} %refs_2_.7) | copy-start | bytes 5505028
  7.9 1.2 %copy-start.2 = (bf16[3584,128]{1,0:T(8,128)(2,1)S(1)}, bf16[3584,128]{1,0:T(8,128)(2,1)}, u32[]{:S(2)}) copy-start(bf16[3584,128]{1,0:T(8,128)(2,1)} %refs_3_.5) | copy-start | bytes 2752516
  9.1 1.0 %copy-start.4 = (bf16[512,448]{0,1:T(8,128)(2,1)S(1)}, bf16[512,448]{0,1:T(8,128)(2,1)}, u32[]{:S(2)}) copy-start(bf16[512,448]{0,1:T(8,128)(2,1)} %param.13) | copy-start | bytes 1376260
  10.1 5.7 %copy-start.8 = (s32[512]{0:T(512)S(1)}, s32[512]{0:T(512)}, u32[]{:S(2)}) copy-start(s32[512]{0:T(512)} %param.24) | copy-start | bytes 6148
  10.1 6.4 %copy-start.10 = (f32[2]{0:T(128)S(1)}, f32[2]{0:T(128)}, u32[]{:S(2)}) copy-start(f32[2]{0:T(128)} %param.17) | copy-start | bytes 28
  10.1 6.6 %copy-start.11 = (f32[2]{0:T(128)S(1)}, f32[2]{0:T(128)}, u32[]{:S(2)}) copy-start(f32[2]{0:T(128)} %param.18) | copy-start | bytes 28
  10.1 6.7 %copy-start.12 = (f32[2]{0:T(128)S(1)}, f32[2]{0:T(128)}, u32[]{:S(2)}) copy-start(f32[2]{0:T(128)} %param.19) | copy-start | bytes 28
  10.1 7.0 %copy-start.3 = (bf16[3584,128]{1,0:T(8,128)(2,1)S(1)}, bf16[3584,128]{1,0:T(8,128)(2,1)}, u32[]{:S(2)}) copy-start(bf16[3584,128]{1,0:T(8,128)(2,1)} %refs_3_.5) | copy-start | bytes 2752516
  13.8 12.3 %collective-permute-start.1 = (bf16[448,512]{1,0:T(8,128)(2,1)}, bf16[448,512]{1,0:T(8,128)(2,1)}, u32[]{:S(2)}, u32[]{:S(2)}) collective-permute-start(bf16[448,512]{1,0:T(8,128)(2,1)} %collective-permute-done.refs_0_), channel_id=1, source_target_pairs={{0,2},{2,4},{4,6},{6,7},{7,5},{5,3},{3,1},{1,0},{8,10},{10,12},{12... | collective-permute-start | bytes 1376264 | tf_op jit(solution)/shard_map/ppermute | solution.py:31
  15.6 12.0 %collective-permute-start.5 = (bf16[448,512]{1,0:T(8,128)(2,1)S(1)}, bf16[448,512]{1,0:T(8,128)(2,1)}, u32[]{:S(2)}, u32[]{:S(2)}) collective-permute-start(bf16[448,512]{1,0:T(8,128)(2,1)S(1)} %collective-permute-done.2.refs_1_), channel_id=1, source_target_pairs={{0,1},{2,0},{4,2},{6,4},{7,6},{5,7},{3,5},{1,3},{8,9},{10,8},{12,1... | collective-permute-start | bytes 1376264 | tf_op jit(solution)/shard_map/ppermute | solution.py:31
  17.0 11.0 %copy-start.7 = (bf16[128,3584]{1,0:T(8,128)(2,1)S(1)}, bf16[128,3584]{1,0:T(8,128)(2,1)}, u32[]{:S(2)}) copy-start(bf16[128,3584]{1,0:T(8,128)(2,1)} %param.23) | copy-start | bytes 2752516
  17.0 11.0 %copy-start.9 = (f32[128]{0:T(128)S(1)}, f32[128]{0:T(128)}, u32[]{:S(2)}) copy-start(f32[128]{0:T(128)} %param.22) | copy-start | bytes 1540
  26.0 13.7 %collective-permute-start.4 = (bf16[448,512]{1,0:T(8,128)(2,1)}, bf16[448,512]{1,0:T(8,128)(2,1)S(1)}, u32[]{:S(2)}, u32[]{:S(2)}) collective-permute-start(bf16[448,512]{1,0:T(8,128)(2,1)} %collective-permute-done.1.refs_0_), channel_id=1, source_target_pairs={{0,2},{2,4},{4,6},{6,7},{7,5},{5,3},{3,1},{1,0},{8,10},{10,12},{12... | collective-permute-start | bytes 1376264 | tf_op jit(solution)/shard_map/ppermute | solution.py:31
  27.6 13.7 %collective-permute-start.6 = (bf16[448,512]{1,0:T(8,128)(2,1)}, bf16[448,512]{1,0:T(8,128)(2,1)S(1)}, u32[]{:S(2)}, u32[]{:S(2)}) collective-permute-start(bf16[448,512]{1,0:T(8,128)(2,1)} %collective-permute-done.5.refs_1_), channel_id=1, source_target_pairs={{0,1},{2,0},{4,2},{6,4},{7,6},{5,7},{3,5},{1,3},{8,9},{10,8},{12,1... | collective-permute-start | bytes 1376264 | tf_op jit(solution)/shard_map/ppermute | solution.py:31
  28.2 25.3 %collective-permute-start.10 = (bf16[128,1792]{1,0:T(8,128)(2,1)S(1)}, bf16[128,1792]{1,0:T(8,128)(2,1)S(1)}, u32[]{:S(2)}, u32[]{:S(2)}) collective-permute-start(bf16[128,1792]{1,0:T(8,128)(2,1)S(1)} %multiply_convert_fusion.rest_0_), channel_id=1, source_target_pairs={{0,2},{2,4},{4,6},{6,7},{7,5},{5,3},{3,1},{1,0},{8,10},{10,12},{12... | collective-permute-start | bytes 1376264 | tf_op jit(solution)/shard_map/ppermute | solution.py:31
  29.9 23.7 %collective-permute-start.11 = (bf16[128,1792]{1,0:T(8,128)(2,1)S(1)}, bf16[128,1792]{1,0:T(8,128)(2,1)S(1)}, u32[]{:S(2)}, u32[]{:S(2)}) collective-permute-start(bf16[128,1792]{1,0:T(8,128)(2,1)S(1)} %multiply_convert_fusion.rest_0_), channel_id=1, source_target_pairs={{0,1},{2,0},{4,2},{6,4},{7,6},{5,7},{3,5},{1,3},{8,9},{10,8},{12,1... | collective-permute-start | bytes 1376264 | tf_op jit(solution)/shard_map/ppermute | solution.py:31
  41.3 10.7 %collective-permute-start.7 = (bf16[224,512]{1,0:T(8,128)(2,1)S(1)}, bf16[224,512]{1,0:T(8,128)(2,1)S(1)}, u32[]{:S(2)}, u32[]{:S(2)}) collective-permute-start(bf16[224,512]{1,0:T(8,128)(2,1)S(1)} %get-tuple-element.46), channel_id=1, source_target_pairs={{0,2},{2,4},{4,6},{6,7},{7,5},{5,3},{3,1},{1,0},{8,10},{10,12},{12... | collective-permute-start | bytes 688136 | tf_op jit(solution)/shard_map/ppermute | solution.py:31
  43.0 10.1 %collective-permute-start.8 = (bf16[224,512]{1,0:T(8,128)(2,1)S(1)}, bf16[224,512]{1,0:T(8,128)(2,1)S(1)}, u32[]{:S(2)}, u32[]{:S(2)}) collective-permute-start(bf16[224,512]{1,0:T(8,128)(2,1)S(1)} %get-tuple-element.47), channel_id=1, source_target_pairs={{0,1},{2,0},{4,2},{6,4},{7,6},{5,7},{3,5},{1,3},{8,9},{10,8},{12,1... | collective-permute-start | bytes 688136 | tf_op jit(solution)/shard_map/ppermute | solution.py:31
  53.1 4.2 %copy-start.5 = (f32[4,128]{1,0:T(4,128)S(1)}, f32[4,128]{1,0:T(4,128)}, u32[]{:S(2)}) copy-start(f32[4,128]{1,0:T(4,128)} %taps_x.3) | copy-start | bytes 6148
  53.1 4.2 %copy-start.6 = (f32[4,128]{1,0:T(4,128)S(1)}, f32[4,128]{1,0:T(4,128)}, u32[]{:S(2)}) copy-start(f32[4,128]{1,0:T(4,128)} %taps_bc.3) | copy-start | bytes 6148
  53.6 12.8 %collective-permute-start.12 = (bf16[128,1792]{1,0:T(8,128)(2,1)S(1)}, bf16[128,1792]{1,0:T(8,128)(2,1)S(1)}, u32[]{:S(2)}, u32[]{:S(2)}) collective-permute-start(bf16[128,1792]{1,0:T(8,128)(2,1)S(1)} %collective-permute-done.10.rest_1_), channel_id=1, source_target_pairs={{0,2},{2,4},{4,6},{6,7},{7,5},{5,3},{3,1},{1,0},{8,10},{10,12},{12... | collective-permute-start | bytes 1376264 | tf_op jit(solution)/shard_map/ppermute | solution.py:31
  55.2 11.1 %collective-permute-start.13 = (bf16[128,1792]{1,0:T(8,128)(2,1)S(1)}, bf16[128,1792]{1,0:T(8,128)(2,1)}, u32[]{:S(2)}, u32[]{:S(2)}) collective-permute-start(bf16[128,1792]{1,0:T(8,128)(2,1)S(1)} %collective-permute-done.11.rest_2_), channel_id=1, source_target_pairs={{0,1},{2,0},{4,2},{6,4},{7,6},{5,7},{3,5},{1,3},{8,9},{10,8},{12,1... | collective-permute-start | bytes 1376264 | tf_op jit(solution)/shard_map/ppermute | solution.py:31
  55.7 2.6 %collective-permute-start.9 = (bf16[8,256]{1,0:T(8,128)(2,1)S(1)}, bf16[8,256]{1,0:T(8,128)(2,1)S(1)}, u32[]{:S(2)}, u32[]{:S(2)}) collective-permute-start(bf16[8,256]{1,0:T(8,128)(2,1)S(1)} %slice.44), channel_id=1, source_target_pairs={{0,8},{8,16},{16,24},{1,9},{9,17},{17,25},{2,10},{10,18},{18,26},{... | collective-permute-start | bytes 12296 | tf_op jit(solution)/shard_map/ppermute | solution.py:335
  66.4 18.0 %collective-permute-start.15 = (bf16[128,1792]{1,0:T(8,128)(2,1)S(1)}, bf16[128,1792]{1,0:T(8,128)(2,1)S(1)}, u32[]{:S(2)}, u32[]{:S(2)}) collective-permute-start(bf16[128,1792]{1,0:T(8,128)(2,1)S(1)} %collective-permute-done.12.rest_3_), channel_id=1, source_target_pairs={{0,2},{2,4},{4,6},{6,7},{7,5},{5,3},{3,1},{1,0},{8,10},{10,12},{12... | collective-permute-start | bytes 1376264 | tf_op jit(solution)/shard_map/ppermute | solution.py:31
  68.0 16.4 %collective-permute-start.16 = (bf16[128,1792]{1,0:T(8,128)(2,1)}, bf16[128,1792]{1,0:T(8,128)(2,1)S(1)}, u32[]{:S(2)}, u32[]{:S(2)}) collective-permute-start(bf16[128,1792]{1,0:T(8,128)(2,1)} %collective-permute-done.13.rest_4_), channel_id=1, source_target_pairs={{0,1},{2,0},{4,2},{6,4},{7,6},{5,7},{3,5},{1,3},{8,9},{10,8},{12,1... | collective-permute-start | bytes 1376264 | tf_op jit(solution)/shard_map/ppermute | solution.py:31
  84.4 6.2 %collective-permute-start.17 = (bf16[64,1792]{1,0:T(8,128)(2,1)S(1)}, bf16[64,1792]{1,0:T(8,128)(2,1)S(1)}, u32[]{:S(2)}, u32[]{:S(2)}) collective-permute-start(bf16[64,1792]{1,0:T(8,128)(2,1)S(1)} %get-tuple-element.71), channel_id=1, source_target_pairs={{0,2},{2,4},{4,6},{6,7},{7,5},{5,3},{3,1},{1,0},{8,10},{10,12},{12... | collective-permute-start | bytes 688136 | tf_op jit(solution)/shard_map/ppermute | solution.py:31
  85.4 6.2 %collective-permute-start.18 = (bf16[64,1792]{1,0:T(8,128)(2,1)S(1)}, bf16[64,1792]{1,0:T(8,128)(2,1)S(1)}, u32[]{:S(2)}, u32[]{:S(2)}) collective-permute-start(bf16[64,1792]{1,0:T(8,128)(2,1)S(1)} %get-tuple-element.72), channel_id=1, source_target_pairs={{0,1},{2,0},{4,2},{6,4},{7,6},{5,7},{3,5},{1,3},{8,9},{10,8},{12,1... | collective-permute-start | bytes 688136 | tf_op jit(solution)/shard_map/ppermute | solution.py:31
  86.5 1.3 %collective-permute-start.14 = (bf16[8,64,128]{2,1,0:T(8,128)(2,1)S(1)}, bf16[8,64,128]{2,1,0:T(8,128)(2,1)S(1)}, u32[]{:S(2)}, u32[]{:S(2)}) collective-permute-start(bf16[8,64,128]{2,1,0:T(8,128)(2,1)S(1)} %all_to_all.5.mine), channel_id=1, source_target_pairs={{0,8},{8,0},{16,24},{24,16},{1,9},{9,1},{17,25},{25,17},{2,10},{10... | collective-permute-start | bytes 393224 | tf_op jit(solution)/shard_map/ppermute | solution.py:373
  91.8 1.6 %collective-permute-start.19 = (bf16[64,1792]{1,0:T(8,128)(2,1)S(1)}, bf16[64,1792]{1,0:T(8,128)(2,1)S(1)}, u32[]{:S(2)}, u32[]{:S(2)}) collective-permute-start(bf16[64,1792]{1,0:T(8,128)(2,1)S(1)} %get-tuple-element.74), channel_id=1, source_target_pairs={{0,8},{8,0},{16,24},{24,16},{1,9},{9,1},{17,25},{25,17},{2,10},{10... | collective-permute-start | bytes 688136 | tf_op jit(solution)/shard_map/ppermute | solution.py:385

commit v12 on v11

--- a/solution.py
+++ b/solution.py
@@ -14,7 +14,6 @@
 VMEM = pl.BlockSpec(memory_space=pltpu.VMEM)
 ANY = pl.BlockSpec(memory_space=pl.ANY)
 HALO = 8
-W_FIRST = 3
 
 
 def ring_place(index, n):
@@ -59,6 +58,15 @@
 def source_of(distance):
     n = lax.axis_size("tensor")
     return ring_index((ring_place(lax.axis_index("tensor"), n) + distance + n) % n, n)
+
+
+def join(*refs):
+    count = len(refs) // 3
+    odd = lax.axis_index("seq") // 2 % 2
+    for own, other, out in zip(refs[:count], refs[count : 2 * count], refs[2 * count :]):
+        size = own.shape[0]
+        out[pl.ds(pl.multiple_of(odd * size, size), size)] = own[...]
+        out[pl.ds(pl.multiple_of((1 - odd) * size, size), size)] = other[...]
 
 
 def project(distances, ahead, first, *refs):
@@ -288,6 +296,8 @@
     own = (lax.dynamic_slice_in_dim(w_out, core * columns, columns, 1).astype(F32) * norm_gain[:, None]).astype(BF16)
     last = n_tensor // 2
     w_half = width // 2
+    own_rows = lax.dynamic_slice_in_dim(own, seq_at // 2 % 2 * w_half, w_half, 0)
+    other_y = [(i, i ^ 2) for i in range(n_seq)]
     shift_rows = [(i, i + 1) for i in range(n_seq - 1)]
 
     seg_halo = lax.ppermute(segments[tok_rows - HALO :], "seq", shift_rows)
@@ -311,11 +321,15 @@
             forth, back = ring_shift(forth, 1), ring_shift(back, -1)
         else:
             far = far_shift(forth, back)
-        if step == W_FIRST:
-            w_forth, w_back = after((own, own), arrivals)
-            w_forth, w_back = ring_shift(w_forth, 1), ring_shift(w_back, -1)
+        if step == 2:
+            w_near = after(own_rows, arrivals)
+            w_near = ring_shift(w_near, 1), ring_shift(w_near, -1)
+        if step == 3:
+            w_other = [lax.ppermute(part, "seq", other_y) for part in after(w_near, arrivals)]
         ahead = last if step == last else 0
         total = projs[-1:]
+        if step == last:
+            total = [after(projs[-1], w_other)]
         fetched = len(arrived) + bool(ahead)
         outs = [shape(tok_rows, 4 * width)] + [shape(feat, 4 * width, kind=BF16)] * bool(ahead)
         results = call(
@@ -327,6 +341,8 @@
         )(*[part for _, part in arrived], w_zx, w_bc, w_step, *total)
         projs.append(results[0])
         arrived = [(-step, forth), (step, back)]
+    whole = shape(width, columns, kind=BF16)
+    w_forth, w_back = call(join, [whole, whole])(*after(w_near, projs[-1]), *w_other)
     proj = call(project_far, shape(tok_rows, 4 * width), flops=10**9)(
         *far, results[1], projs[-1]
     )

time: 94.8 us -> 97.7 us (1.031)
  starting transfers between devices: 20.2 us -> 22.3 us
  blocking collectives: 21.6 us -> 20.5 us
  waiting for transfers between devices: 29.4 us -> 30.5 us
    ppermute x0 -> x2, waiting for transfers between devices: none -> 2.67 us  [local(): lax.ppermute(part, 'seq', other_y)]
    ppermute x0 -> x2, starting transfers between devices: none -> 2.03 us  [local(): lax.ppermute(part, 'seq', other_y)]
    ppermute x16, waiting for transfers between devices: 26.6 us -> 25 us  [ring_shift(): lax.ppermute(block, 'tensor', [(order[i], order[(i + step) % n]) for i in...]
    unnamed x26 -> x30, local copies, waits for them, and re-layouts: 3.73 us -> 4.26 us
  transfers between devices with their start and end apart: 20 -> 22, of which waited for: 10 -> 12; matrix products, arithmetic and copies ran while one was open for 4% -> 4% of each run, Pallas kernels for 15% -> 14%
where the time goes in v12:
time: 97.7 us; the launch traced here: 97.1 us
  waiting for transfers between devices  30.5 us (31%)
  starting transfers between devices  22.3 us (23%)
  blocking collectives  20.5 us (21%)
  Pallas kernels  14.9 us (15%)
  local copies, waits for them, and re-layouts  6.51 us (7%)
  matrix products  1.12 us (1%)
  other arithmetic  1.05 us (1%)
    ppermute x16, waiting for transfers between devices, ring_shift(): lax.ppermute(block, 'tensor', [(order[i], order[(i + step) % n]) for i in...  25 us
    ppermute x16, starting transfers between devices, ring_shift(): lax.ppermute(block, 'tensor', [(order[i], order[(i + step) % n]) for i in...  17.4 us
    all_to_all x1, blocking collectives, local(): mine = lax.all_to_all(blocks, 'tensor', 0, 0)  14.3 us
    pallas_call x4, Pallas kernels, local(): call(functools.partial(project, [distance for distance, _ in arrived], ah...  8.52 us
    all_gather x1, blocking collectives, local(): messages = lax.all_gather(message, 'seq')  6.24 us
    unnamed x30, local copies, waits for them, and re-layouts  4.26 us
    ppermute x2, waiting for transfers between devices, local(): lax.ppermute(part, 'seq', other_y)  2.67 us
    ppermute x2, starting transfers between devices, local(): lax.ppermute(part, 'seq', other_y)  2.03 us
  transfers between devices with their start and end apart: 22, of which 12 were waited for; matrix products, arithmetic and copies ran while one was open for 4% of the time, Pallas kernels for 14%

profile of v12, /device:TPU:0, one launch (start us, length us, event | category | flops | bytes accessed | tf_op | source)
XLA Modules:
  0.0 97.1 jit_solution(4569446273918262435)
XLA Ops:
  0.0 3.0 %collective-permute-start = (bf16[448,512]{1,0:T(8,128)(2,1)}, bf16[448,512]{1,0:T(8,128)(2,1)}, u32[]{:S(2)}, u32[]{:S(2)}) collective-permute-start(bf16[448,512]{1,0:T(8,128)(2,1)} %bitcast.13), channel_id=1, source_target_pairs={{0,2},{2,4},{4,6},{6,7},{7,5},{5,3},{3,1},{1,0},{8,10},{10,12},{12... | collective-permute-start | bytes 1376264 | tf_op jit(solution)/shard_map/ppermute | solution.py:30
  3.0 0.8 slice.33
  3.8 1.4 %collective-permute-start.3 = (s32[8]{0:T(128)S(1)}, s32[8]{0:T(128)S(1)}, u32[]{:S(2)}, u32[]{:S(2)}) collective-permute-start(s32[8]{0:T(128)S(1)} %slice.33), channel_id=1, source_target_pairs={{0,8},{8,16},{16,24},{1,9},{9,17},{17,25},{2,10},{10,18},{18,26},{... | collective-permute-start | bytes 104 | tf_op jit(solution)/shard_map/ppermute | solution.py:303
  5.3 1.1 %convolution_bitcast_fusion.refs_3_.refs_4_ = bf16[3584,128]{1,0:T(8,128)(2,1)S(1)} fusion(bf16[2,128]{1,0:T(2,128)(2,1)} %constant.44.clone, bf16[3584,2]{0,1:T(2,128)(2,1)S(1)} %copy-done), kind=kOutput, calls=%fused_computation | convolution fusion | flops 1835008 | bytes 932352 | tf_op jit(solution)/shard_map/dot_general | solution.py:292
  6.4 1.5 %copy-done.1 = bf16[2,3584,128]{2,1,0:T(8,128)(2,1)S(1)} copy-done((bf16[2,3584,128]{2,1,0:T(8,128)(2,1)S(1)}, bf16[2,3584,128]{2,1,0:T(8,128)(2,1)}, u32[]{:S(2)}) %copy-start.1) | copy-done | bytes 1835032
  7.9 1.2 %copy-done.2 = bf16[3584,128]{1,0:T(8,128)(2,1)S(1)} copy-done((bf16[3584,128]{1,0:T(8,128)(2,1)S(1)}, bf16[3584,128]{1,0:T(8,128)(2,1)}, u32[]{:S(2)}) %copy-start.2) | copy-done | bytes 917528
  9.1 1.0 %copy-done.4 = bf16[512,448]{0,1:T(8,128)(2,1)S(1)} copy-done((bf16[512,448]{0,1:T(8,128)(2,1)S(1)}, bf16[512,448]{0,1:T(8,128)(2,1)}, u32[]{:S(2)}) %copy-start.4) | copy-done | bytes 458776
  10.1 0.0 copy-start.13
  10.1 0.6 shard_map.127.refs_5_
  10.8 0.5 copy-done.9
  11.3 0.1 multiply_convert_fusion.rest_0_
  11.4 2.4 %collective-permute-done.refs_0_ = bf16[448,512]{1,0:T(8,128)(2,1)} collective-permute-done((bf16[448,512]{1,0:T(8,128)(2,1)}, bf16[448,512]{1,0:T(8,128)(2,1)}, u32[]{:S(2)}, u32[]{:S(2)}) %collective-permute-start) | collective-permute-done | bytes 458784 | tf_op jit(solution)/shard_map/ppermute | solution.py:30
  13.8 1.5 %collective-permute-done.2.refs_1_ = bf16[448,512]{1,0:T(8,128)(2,1)} collective-permute-done((bf16[448,512]{1,0:T(8,128)(2,1)}, bf16[448,512]{1,0:T(8,128)(2,1)}, u32[]{:S(2)}, u32[]{:S(2)}) %collective-permute-start.2) | collective-permute-done | bytes 458784 | tf_op jit(solution)/shard_map/ppermute | solution.py:30
  15.3 0.3 collective-permute-start.5
  15.6 1.7 %collective-permute-start.1 = (bf16[448,512]{1,0:T(8,128)(2,1)}, bf16[448,512]{1,0:T(8,128)(2,1)}, u32[]{:S(2)}, u32[]{:S(2)}) collective-permute-start(bf16[448,512]{1,0:T(8,128)(2,1)} %collective-permute-done.refs_0_), channel_id=1, source_target_pairs={{0,2},{2,4},{4,6},{6,7},{7,5},{5,3},{3,1},{1,0},{8,10},{10,12},{12... | collective-permute-start | bytes 1376264 | tf_op jit(solution)/shard_map/ppermute | solution.py:30
  17.4 0.7 fusion
  18.0 0.1 slice.36
  18.1 0.1 broadcast_in_dim.28
  18.2 0.1 broadcast_in_dim_reshape.10.rate
  18.2 0.1 broadcast_in_dim.29
  18.3 0.1 broadcast_in_dim_reshape.11.skip
  18.4 0.1 broadcast_in_dim.27
  18.5 0.1 broadcast_in_dim_reshape.9.bias
  18.6 0.1 pad_add_fusion
  18.7 3.0 %shard_map.128.refs_5_ = f32[512,512]{1,0:T(8,128)S(1)} custom-call(bf16[448,512]{1,0:T(8,128)(2,1)} %collective-permute-done.refs_0_, bf16[448,512]{1,0:T(8,128)(2,1)} %collective-permute-done.2.refs_1_, bf16[2,3584,128]{2,1,0:T(8,128)(2,1)} %refs_2_.7, bf16[3584,128]{1,0:T(8,128)(2,1)S(1)} %copy-done.3, ...), custom_call_target="tpu_custom_call" | custom-call | flops 1000000000 | bytes 2097152 | tf_op jit(solution)/shard_map/pallas_call | solution.py:335
  21.7 5.1 %collective-permute-done.5.refs_1_ = bf16[448,512]{1,0:T(8,128)(2,1)} collective-permute-done((bf16[448,512]{1,0:T(8,128)(2,1)}, bf16[448,512]{1,0:T(8,128)(2,1)}, u32[]{:S(2)}, u32[]{:S(2)}) %collective-permute-start.5) | collective-permute-done | bytes 458784 | tf_op jit(solution)/shard_map/ppermute | solution.py:30
  26.8 1.2 %collective-permute-done.1.refs_0_ = bf16[448,512]{1,0:T(8,128)(2,1)} collective-permute-done((bf16[448,512]{1,0:T(8,128)(2,1)}, bf16[448,512]{1,0:T(8,128)(2,1)}, u32[]{:S(2)}, u32[]{:S(2)}) %collective-permute-start.1) | collective-permute-done | bytes 458784 | tf_op jit(solution)/shard_map/ppermute | solution.py:30
  28.0 1.6 %collective-permute-start.6 = (bf16[448,512]{1,0:T(8,128)(2,1)}, bf16[448,512]{1,0:T(8,128)(2,1)S(1)}, u32[]{:S(2)}, u32[]{:S(2)}) collective-permute-start(bf16[448,512]{1,0:T(8,128)(2,1)} %collective-permute-done.5.refs_1_), channel_id=1, source_target_pairs={{0,1},{2,0},{4,2},{6,4},{7,6},{5,7},{3,5},{1,3},{8,9},{10,8},{12,1... | collective-permute-start | bytes 1376264 | tf_op jit(solution)/shard_map/ppermute | solution.py:30
  29.6 0.5 collective-permute-start.4
  30.0 1.6 %collective-permute-start.10 = (bf16[64,1792]{1,0:T(8,128)(2,1)S(1)}, bf16[64,1792]{1,0:T(8,128)(2,1)S(1)}, u32[]{:S(2)}, u32[]{:S(2)}) collective-permute-start(bf16[64,1792]{1,0:T(8,128)(2,1)S(1)} %constant_dynamic-slice_fusion), channel_id=1, source_target_pairs={{0,1},{2,0},{4,2},{6,4},{7,6},{5,7},{3,5},{1,3},{8,9},{10,8},{12,1... | collective-permute-start | bytes 688136 | tf_op jit(solution)/shard_map/ppermute | solution.py:30
  31.6 0.5 collective-permute-start.9
  32.1 12.1 %collective-permute-done.10.refs_1_ = bf16[64,1792]{1,0:T(8,128)(2,1)S(1)} collective-permute-done((bf16[64,1792]{1,0:T(8,128)(2,1)S(1)}, bf16[64,1792]{1,0:T(8,128)(2,1)S(1)}, u32[]{:S(2)}, u32[]{:S(2)}) %collective-permute-start.10) | collective-permute-done | bytes 229408 | tf_op jit(solution)/shard_map/ppermute | solution.py:30
  44.2 1.2 %collective-permute-done.9.refs_0_ = bf16[64,1792]{1,0:T(8,128)(2,1)S(1)} collective-permute-done((bf16[64,1792]{1,0:T(8,128)(2,1)S(1)}, bf16[64,1792]{1,0:T(8,128)(2,1)S(1)}, u32[]{:S(2)}, u32[]{:S(2)}) %collective-permute-start.9) | collective-permute-done | bytes 229408 | tf_op jit(solution)/shard_map/ppermute | solution.py:30
  45.5 2.0 %collective-permute-start.12 = (bf16[64,1792]{1,0:T(8,128)(2,1)S(1)}, bf16[64,1792]{1,0:T(8,128)(2,1)S(1)}, u32[]{:S(2)}, u32[]{:S(2)}) collective-permute-start(bf16[64,1792]{1,0:T(8,128)(2,1)S(1)} %collective-permute-done.10.refs_1_), channel_id=1, source_target_pairs={{0,16},{8,24},{16,0},{24,8},{1,17},{9,25},{17,1},{25,9},{2,18},{10... | collective-permute-start | bytes 688136 | tf_op jit(solution)/shard_map/ppermute | solution.py:328
  47.5 3.0 %shard_map.129.refs_5_ = f32[512,512]{1,0:T(8,128)S(1)} custom-call(bf16[448,512]{1,0:T(8,128)(2,1)} %collective-permute-done.1.refs_0_, bf16[448,512]{1,0:T(8,128)(2,1)} %collective-permute-done.5.refs_1_, bf16[2,3584,128]{2,1,0:T(8,128)(2,1)} %refs_2_.7, bf16[3584,128]{1,0:T(8,128)(2,1)S(1)} %copy-done.3, ...), custom_call_target="tpu_custom_call" | custom-call | flops 1000000000 | bytes 2097152 | tf_op jit(solution)/shard_map/pallas_call | solution.py:335
  50.6 0.6 collective-permute-start.7
  51.1 1.5 %collective-permute-start.8 = (bf16[224,512]{1,0:T(8,128)(2,1)S(1)}, bf16[224,512]{1,0:T(8,128)(2,1)S(1)}, u32[]{:S(2)}, u32[]{:S(2)}) collective-permute-start(bf16[224,512]{1,0:T(8,128)(2,1)S(1)} %get-tuple-element.53), channel_id=1, source_target_pairs={{0,1},{2,0},{4,2},{6,4},{7,6},{5,7},{3,5},{1,3},{8,9},{10,8},{12,1... | collective-permute-start | bytes 688136 | tf_op jit(solution)/shard_map/ppermute | solution.py:30
  52.6 0.2 collective-permute-done.11.refs_2_
  52.9 2.5 %collective-permute-done.12.refs_3_ = bf16[64,1792]{1,0:T(8,128)(2,1)S(1)} collective-permute-done((bf16[64,1792]{1,0:T(8,128)(2,1)S(1)}, bf16[64,1792]{1,0:T(8,128)(2,1)S(1)}, u32[]{:S(2)}, u32[]{:S(2)}) %collective-permute-start.12) | collective-permute-done | bytes 229408 | tf_op jit(solution)/shard_map/ppermute | solution.py:328
  55.3 1.9 %shard_map.131 = (f32[512,512]{1,0:T(8,128)S(1)}, bf16[448,512]{1,0:T(8,128)(2,1)S(1)}) custom-call(bf16[448,512]{1,0:T(8,128)(2,1)S(1)} %collective-permute-done.4.forth.refs_0_, bf16[448,512]{1,0:T(8,128)(2,1)S(1)} %collective-permute-done.6.back.refs_1_, bf16[2,3584,128]{2,1,0:T(8,128)(2,1)} %refs_2_.7, bf16[3584,128]{1,0:T(8,128)(2,1)S(1)} %copy-done.3, ...), custom_call_target="tpu_custom_call" | custom-call | flops 1000000000 | bytes 2097152 | tf_op jit(solution)/shard_map/pallas_call | solution.py:335
  57.2 0.1 shard_map.136
  57.4 0.5 shard_map.132.proj
  57.9 0.6 collective-permute-start.14
  58.5 1.5 %collective-permute-start.15 = (bf16[128,1792]{1,0:T(8,128)(2,1)S(1)}, bf16[128,1792]{1,0:T(8,128)(2,1)S(1)}, u32[]{:S(2)}, u32[]{:S(2)}) collective-permute-start(bf16[128,1792]{1,0:T(8,128)(2,1)S(1)} %get-tuple-element.77.rest_2_), channel_id=1, source_target_pairs={{0,1},{2,0},{4,2},{6,4},{7,6},{5,7},{3,5},{1,3},{8,9},{10,8},{12,1... | collective-permute-start | bytes 1376264 | tf_op jit(solution)/shard_map/ppermute | solution.py:30
  59.9 1.3 %collective-permute-start.13 = (bf16[8,256]{1,0:T(8,128)(2,1)S(1)}, bf16[8,256]{1,0:T(8,128)(2,1)S(1)}, u32[]{:S(2)}, u32[]{:S(2)}) collective-permute-start(bf16[8,256]{1,0:T(8,128)(2,1)S(1)} %slice.44), channel_id=1, source_target_pairs={{0,8},{8,16},{16,24},{1,9},{9,17},{17,25},{2,10},{10,18},{18,26},{... | collective-permute-start | bytes 12296 | tf_op jit(solution)/shard_map/ppermute | solution.py:351
  61.2 0.1 copy.16.seg_ext
  61.4 0.1 copy.17.seg_ext.seg_ext_a
  61.5 1.0 %shard_map.133 = (f32[256,128]{1,0:T(8,128)S(1)}, f32[256,128]{1,0:T(8,128)S(1)}, f32[256,128]{1,0:T(8,128)S(1)}, f32[72,128]{1,0:T(8,128)S(1)}, f32[256,128]{1,0:T(8,128)S(1)}) custom-call(f32[512,512]{1,0:T(8,128)S(1)} %shard_map.132.proj, s32[264,1]{1,0:T(8,128)S(1)} %copy.16.seg_ext, s32[1,256]{1,0:T(1,128)S(1)} %bitcast.17, f32[4,128]{1,0:T(4,128)S(1)} %copy-done.7, ...), custom_call_target="tpu_custom_call" | custom-call | flops 10000000 | bytes 2097152 | tf_op jit(solution)/shard_map/pallas_call | solution.py:356
  62.5 1.3 %shard_map.134 = (f32[256,128]{1,0:T(8,128)S(1)}, f32[256,128]{1,0:T(8,128)S(1)}, f32[256,128]{1,0:T(8,128)S(1)}, f32[256,128]{1,0:T(8,128)S(1)}, f32[256,128]{1...) custom-call(f32[512,512]{1,0:T(8,128)S(1)} %shard_map.132.proj, ...), custom_call_target="tpu_custom_call" | custom-call | flops 10000000 | bytes 2097152 | tf_op jit(solution)/shard_map/pallas_call | solution.py:361
  63.8 6.2 %all-gather = f32[288,128]{1,0:T(8,128)S(1)} all-gather(f32[72,128]{1,0:T(8,128)S(1)} %get-tuple-element.61), channel_id=2, replica_groups=mesh['seq'=4,'tensor'=8] {'seq'}, dimensions={0}, use_global_device_ids=true | all-gather | bytes 184320 | tf_op jit(solution)/shard_map/all_gather | solution.py:366
  70.1 0.6 collective-permute-start.17
  70.6 1.5 %collective-permute-start.18 = (bf16[128,1792]{1,0:T(8,128)(2,1)S(1)}, bf16[128,1792]{1,0:T(8,128)(2,1)S(1)}, u32[]{:S(2)}, u32[]{:S(2)}) collective-permute-start(bf16[128,1792]{1,0:T(8,128)(2,1)S(1)} %collective-permute-done.15.rest_4_), channel_id=1, source_target_pairs={{0,1},{2,0},{4,2},{6,4},{7,6},{5,7},{3,5},{1,3},{8,9},{10,8},{12,1... | collective-permute-start | bytes 1376264 | tf_op jit(solution)/shard_map/ppermute | solution.py:30
  72.1 1.2 %shard_map.135 = bf16[512,128]{1,0:T(8,128)(2,1)S(1)} custom-call(s32[1,1]{1,0:T(1,128)} %bitcast.seg_first, f32[4,72,128]{2,1,0:T(8,128)S(1)} %bitcast.11, s32[264,1]{1,0:T(8,128)S(1)} %copy.17.seg_ext.seg_ext_a, s32[1,256]{1,0:T(1,128)S(1)} %bitcast.16, f32[1,128]{1,0:T(1,128)S(1)} %broadcast_in_dim_reshape.11.skip, f32[512,512]{1,0:T(8,128)S(1)} %shard_map.132.proj, ...), custom_call_target="tpu_custom_call" | custom-call | flops 10000000 | bytes 2097152 | tf_op jit(solution)/shard_map/pallas_call | solution.py:367
  73.3 14.3 %all_to_all.5.mine = bf16[8,64,128]{2,1,0:T(8,128)(2,1)S(1)} all-to-all(bf16[8,64,128]{2,1,0:T(8,128)(2,1)S(1)} %bitcast.12), channel_id=1, replica_groups=mesh['seq'=4,'tensor'=8] {'tensor'}, dimensions={0} | all-to-all | bytes 262144 | tf_op jit(solution)/shard_map/all_to_all | solution.py:387
  87.6 0.8 collective-permute-start.19
  88.4 1.3 %collective-permute-start.20 = (bf16[64,1792]{1,0:T(8,128)(2,1)S(1)}, bf16[64,1792]{1,0:T(8,128)(2,1)S(1)}, u32[]{:S(2)}, u32[]{:S(2)}) collective-permute-start(bf16[64,1792]{1,0:T(8,128)(2,1)S(1)} %get-tuple-element.84), channel_id=1, source_target_pairs={{0,1},{2,0},{4,2},{6,4},{7,6},{5,7},{3,5},{1,3},{8,9},{10,8},{12,1... | collective-permute-start | bytes 688136 | tf_op jit(solution)/shard_map/ppermute | solution.py:30
  89.7 1.3 %collective-permute-done.16.other = bf16[8,64,128]{2,1,0:T(8,128)(2,1)S(1)} collective-permute-done((bf16[8,64,128]{2,1,0:T(8,128)(2,1)S(1)}, bf16[8,64,128]{2,1,0:T(8,128)(2,1)S(1)}, u32[]{:S(2)}, u32[]{:S(2)}) %collective-permute-start.16) | collective-permute-done | bytes 131104 | tf_op jit(solution)/shard_map/ppermute | solution.py:389
  91.0 2.0 %shard_map.137.total = f32[128,1792]{1,0:T(8,128)S(1)} custom-call(bf16[8,64,128]{2,1,0:T(8,128)(2,1)S(1)} %all_to_all.5.mine, bf16[8,64,128]{2,1,0:T(8,128)(2,1)S(1)} %collective-permute-done.16.other, bf16[128,1792]{1,0:T(8,128)(2,1)S(1)} %multiply_convert_fusion.rest_0_, bf16[128,1792]{1,0:T(8,128)(2,1)S(1)} %get-tuple-element.76.rest_1_, ...), custom_call_target="tpu_custom_call" | custom-call | flops 1000000000 | bytes 2097152 | tf_op jit(solution)/shard_map/pallas_call | solution.py:394
  93.0 1.2 %collective-permute-done.19.top = bf16[64,1792]{1,0:T(8,128)(2,1)S(1)} collective-permute-done((bf16[64,1792]{1,0:T(8,128)(2,1)S(1)}, bf16[64,1792]{1,0:T(8,128)(2,1)S(1)}, u32[]{:S(2)}, u32[]{:S(2)}) %collective-permute-start.19) | collective-permute-done | bytes 229408 | tf_op jit(solution)/shard_map/ppermute | solution.py:30
  94.2 0.2 collective-permute-done.20.bottom
  94.4 0.3 shard_map.139
  94.7 0.1 collective-permute-start.21
  94.8 1.5 %collective-permute-done.21 = bf16[64,1792]{1,0:T(8,128)(2,1)S(1)} collective-permute-done((bf16[64,1792]{1,0:T(8,128)(2,1)S(1)}, bf16[64,1792]{1,0:T(8,128)(2,1)S(1)}, u32[]{:S(2)}, u32[]{:S(2)}) %collective-permute-start.21) | collective-permute-done | bytes 229408 | tf_op jit(solution)/shard_map/ppermute | solution.py:401
  96.3 0.8 pad_maximum_fusion
  (47 shorter events, 0.2 us)
Async XLA Ops:
  0.0 5.3 %copy-start = (bf16[3584,2]{0,1:T(2,128)(2,1)S(1)}, bf16[3584,2]{0,1:T(2,128)(2,1)}, u32[]{:S(2)}) copy-start(bf16[3584,2]{0,1:T(2,128)(2,1)} %param.16) | copy-start | bytes 43012
  0.0 13.8 %collective-permute-start = (bf16[448,512]{1,0:T(8,128)(2,1)}, bf16[448,512]{1,0:T(8,128)(2,1)}, u32[]{:S(2)}, u32[]{:S(2)}) collective-permute-start(bf16[448,512]{1,0:T(8,128)(2,1)} %bitcast.13), channel_id=1, source_target_pairs={{0,2},{2,4},{4,6},{6,7},{7,5},{5,3},{3,1},{1,0},{8,10},{10,12},{12... | collective-permute-start | bytes 1376264 | tf_op jit(solution)/shard_map/ppermute | solution.py:30
  3.0 12.3 %collective-permute-start.2 = (bf16[448,512]{1,0:T(8,128)(2,1)}, bf16[448,512]{1,0:T(8,128)(2,1)}, u32[]{:S(2)}, u32[]{:S(2)}) collective-permute-start(bf16[448,512]{1,0:T(8,128)(2,1)} %bitcast.14), channel_id=1, source_target_pairs={{0,1},{2,0},{4,2},{6,4},{7,6},{5,7},{3,5},{1,3},{8,9},{10,8},{12,1... | collective-permute-start | bytes 1376264 | tf_op jit(solution)/shard_map/ppermute | solution.py:30
  3.8 14.8 %collective-permute-start.3 = (s32[8]{0:T(128)S(1)}, s32[8]{0:T(128)S(1)}, u32[]{:S(2)}, u32[]{:S(2)}) collective-permute-start(s32[8]{0:T(128)S(1)} %slice.33), channel_id=1, source_target_pairs={{0,8},{8,16},{16,24},{1,9},{9,17},{17,25},{2,10},{10,18},{18,26},{... | collective-permute-start | bytes 104 | tf_op jit(solution)/shard_map/ppermute | solution.py:303
  6.4 1.5 %copy-start.1 = (bf16[2,3584,128]{2,1,0:T(8,128)(2,1)S(1)}, bf16[2,3584,128]{2,1,0:T(8,128)(2,1)}, u32[]{:S(2)}) copy-start(bf16[2,3584,128]{2,1,0:T(8,128)(2,1)} %refs_2_.7) | copy-start | bytes 5505028
  7.9 1.2 %copy-start.2 = (bf16[3584,128]{1,0:T(8,128)(2,1)S(1)}, bf16[3584,128]{1,0:T(8,128)(2,1)}, u32[]{:S(2)}) copy-start(bf16[3584,128]{1,0:T(8,128)(2,1)} %refs_3_.5) | copy-start | bytes 2752516
  9.1 1.0 %copy-start.4 = (bf16[512,448]{0,1:T(8,128)(2,1)S(1)}, bf16[512,448]{0,1:T(8,128)(2,1)}, u32[]{:S(2)}) copy-start(bf16[512,448]{0,1:T(8,128)(2,1)} %param.13) | copy-start | bytes 1376260
  10.1 1.2 %copy-start.9 = (bf16[128,3584]{1,0:T(8,128)(2,1)S(1)}, bf16[128,3584]{1,0:T(8,128)(2,1)}, u32[]{:S(2)}) copy-start(bf16[128,3584]{1,0:T(8,128)(2,1)} %param.23) | copy-start | bytes 2752516
  10.1 1.2 %copy-start.11 = (f32[128]{0:T(128)S(1)}, f32[128]{0:T(128)}, u32[]{:S(2)}) copy-start(f32[128]{0:T(128)} %param.22) | copy-start | bytes 1540
  10.1 7.3 %copy-start.10 = (s32[512]{0:T(512)S(1)}, s32[512]{0:T(512)}, u32[]{:S(2)}) copy-start(s32[512]{0:T(512)} %param.24) | copy-start | bytes 6148
  10.1 8.0 %copy-start.12 = (f32[2]{0:T(128)S(1)}, f32[2]{0:T(128)}, u32[]{:S(2)}) copy-start(f32[2]{0:T(128)} %param.18) | copy-start | bytes 28
  10.1 8.1 %copy-start.13 = (f32[2]{0:T(128)S(1)}, f32[2]{0:T(128)}, u32[]{:S(2)}) copy-start(f32[2]{0:T(128)} %param.19) | copy-start | bytes 28
  10.1 8.3 %copy-start.14 = (f32[2]{0:T(128)S(1)}, f32[2]{0:T(128)}, u32[]{:S(2)}) copy-start(f32[2]{0:T(128)} %param.17) | copy-start | bytes 28
  10.1 8.5 %copy-start.3 = (bf16[3584,128]{1,0:T(8,128)(2,1)S(1)}, bf16[3584,128]{1,0:T(8,128)(2,1)}, u32[]{:S(2)}) copy-start(bf16[3584,128]{1,0:T(8,128)(2,1)} %refs_3_.5) | copy-start | bytes 2752516
  15.3 11.4 %collective-permute-start.5 = (bf16[448,512]{1,0:T(8,128)(2,1)}, bf16[448,512]{1,0:T(8,128)(2,1)}, u32[]{:S(2)}, u32[]{:S(2)}) collective-permute-start(bf16[448,512]{1,0:T(8,128)(2,1)} %collective-permute-done.2.refs_1_), channel_id=1, source_target_pairs={{0,1},{2,0},{4,2},{6,4},{7,6},{5,7},{3,5},{1,3},{8,9},{10,8},{12,1... | collective-permute-start | bytes 1376264 | tf_op jit(solution)/shard_map/ppermute | solution.py:30
  15.6 12.3 %collective-permute-start.1 = (bf16[448,512]{1,0:T(8,128)(2,1)}, bf16[448,512]{1,0:T(8,128)(2,1)}, u32[]{:S(2)}, u32[]{:S(2)}) collective-permute-start(bf16[448,512]{1,0:T(8,128)(2,1)} %collective-permute-done.refs_0_), channel_id=1, source_target_pairs={{0,2},{2,4},{4,6},{6,7},{7,5},{5,3},{3,1},{1,0},{8,10},{10,12},{12... | collective-permute-start | bytes 1376264 | tf_op jit(solution)/shard_map/ppermute | solution.py:30
  28.0 22.5 %collective-permute-start.6 = (bf16[448,512]{1,0:T(8,128)(2,1)}, bf16[448,512]{1,0:T(8,128)(2,1)S(1)}, u32[]{:S(2)}, u32[]{:S(2)}) collective-permute-start(bf16[448,512]{1,0:T(8,128)(2,1)} %collective-permute-done.5.refs_1_), channel_id=1, source_target_pairs={{0,1},{2,0},{4,2},{6,4},{7,6},{5,7},{3,5},{1,3},{8,9},{10,8},{12,1... | collective-permute-start | bytes 1376264 | tf_op jit(solution)/shard_map/ppermute | solution.py:30
  29.6 21.0 %collective-permute-start.4 = (bf16[448,512]{1,0:T(8,128)(2,1)}, bf16[448,512]{1,0:T(8,128)(2,1)S(1)}, u32[]{:S(2)}, u32[]{:S(2)}) collective-permute-start(bf16[448,512]{1,0:T(8,128)(2,1)} %collective-permute-done.1.refs_0_), channel_id=1, source_target_pairs={{0,2},{2,4},{4,6},{6,7},{7,5},{5,3},{3,1},{1,0},{8,10},{10,12},{12... | collective-permute-start | bytes 1376264 | tf_op jit(solution)/shard_map/ppermute | solution.py:30
  30.0 14.2 %collective-permute-start.10 = (bf16[64,1792]{1,0:T(8,128)(2,1)S(1)}, bf16[64,1792]{1,0:T(8,128)(2,1)S(1)}, u32[]{:S(2)}, u32[]{:S(2)}) collective-permute-start(bf16[64,1792]{1,0:T(8,128)(2,1)S(1)} %constant_dynamic-slice_fusion), channel_id=1, source_target_pairs={{0,1},{2,0},{4,2},{6,4},{7,6},{5,7},{3,5},{1,3},{8,9},{10,8},{12,1... | collective-permute-start | bytes 688136 | tf_op jit(solution)/shard_map/ppermute | solution.py:30
  31.6 13.8 %collective-permute-start.9 = (bf16[64,1792]{1,0:T(8,128)(2,1)S(1)}, bf16[64,1792]{1,0:T(8,128)(2,1)S(1)}, u32[]{:S(2)}, u32[]{:S(2)}) collective-permute-start(bf16[64,1792]{1,0:T(8,128)(2,1)S(1)} %constant_dynamic-slice_fusion), channel_id=1, source_target_pairs={{0,2},{2,4},{4,6},{6,7},{7,5},{5,3},{3,1},{1,0},{8,10},{10,12},{12... | collective-permute-start | bytes 688136 | tf_op jit(solution)/shard_map/ppermute | solution.py:30
  45.5 7.4 %collective-permute-start.11 = (bf16[64,1792]{1,0:T(8,128)(2,1)S(1)}, bf16[64,1792]{1,0:T(8,128)(2,1)S(1)}, u32[]{:S(2)}, u32[]{:S(2)}) collective-permute-start(bf16[64,1792]{1,0:T(8,128)(2,1)S(1)} %collective-permute-done.9.refs_0_), channel_id=1, source_target_pairs={{0,16},{8,24},{16,0},{24,8},{1,17},{9,25},{17,1},{25,9},{2,18},{10... | collective-permute-start | bytes 688136 | tf_op jit(solution)/shard_map/ppermute | solution.py:328
  45.5 9.9 %collective-permute-start.12 = (bf16[64,1792]{1,0:T(8,128)(2,1)S(1)}, bf16[64,1792]{1,0:T(8,128)(2,1)S(1)}, u32[]{:S(2)}, u32[]{:S(2)}) collective-permute-start(bf16[64,1792]{1,0:T(8,128)(2,1)S(1)} %collective-permute-done.10.refs_1_), channel_id=1, source_target_pairs={{0,16},{8,24},{16,0},{24,8},{1,17},{9,25},{17,1},{25,9},{2,18},{10... | collective-permute-start | bytes 688136 | tf_op jit(solution)/shard_map/ppermute | solution.py:328
  50.6 6.8 %collective-permute-start.7 = (bf16[224,512]{1,0:T(8,128)(2,1)S(1)}, bf16[224,512]{1,0:T(8,128)(2,1)S(1)}, u32[]{:S(2)}, u32[]{:S(2)}) collective-permute-start(bf16[224,512]{1,0:T(8,128)(2,1)S(1)} %get-tuple-element.52), channel_id=1, source_target_pairs={{0,2},{2,4},{4,6},{6,7},{7,5},{5,3},{3,1},{1,0},{8,10},{10,12},{12... | collective-permute-start | bytes 688136 | tf_op jit(solution)/shard_map/ppermute | solution.py:30
  51.1 6.2 %collective-permute-start.8 = (bf16[224,512]{1,0:T(8,128)(2,1)S(1)}, bf16[224,512]{1,0:T(8,128)(2,1)S(1)}, u32[]{:S(2)}, u32[]{:S(2)}) collective-permute-start(bf16[224,512]{1,0:T(8,128)(2,1)S(1)} %get-tuple-element.53), channel_id=1, source_target_pairs={{0,1},{2,0},{4,2},{6,4},{7,6},{5,7},{3,5},{1,3},{8,9},{10,8},{12,1... | collective-permute-start | bytes 688136 | tf_op jit(solution)/shard_map/ppermute | solution.py:30
  57.3 1.2 %copy-start.5 = (bf16[128,1792]{1,0:T(8,128)(2,1)}, bf16[128,1792]{1,0:T(8,128)(2,1)S(1)}, u32[]{:S(2)}) copy-start(bf16[128,1792]{1,0:T(8,128)(2,1)S(1)} %get-tuple-element.77.rest_2_) | copy-start | bytes 1376260
  57.3 4.2 %copy-start.7 = (f32[4,128]{1,0:T(4,128)S(1)}, f32[4,128]{1,0:T(4,128)}, u32[]{:S(2)}) copy-start(f32[4,128]{1,0:T(4,128)} %taps_x.3) | copy-start | bytes 6148
  57.3 4.2 %copy-start.8 = (f32[4,128]{1,0:T(4,128)S(1)}, f32[4,128]{1,0:T(4,128)}, u32[]{:S(2)}) copy-start(f32[4,128]{1,0:T(4,128)} %taps_bc.3) | copy-start | bytes 6148
  57.9 12.2 %collective-permute-start.14 = (bf16[128,1792]{1,0:T(8,128)(2,1)S(1)}, bf16[128,1792]{1,0:T(8,128)(2,1)}, u32[]{:S(2)}, u32[]{:S(2)}) collective-permute-start(bf16[128,1792]{1,0:T(8,128)(2,1)S(1)} %get-tuple-element.76.rest_1_), channel_id=1, source_target_pairs={{0,2},{2,4},{4,6},{6,7},{7,5},{5,3},{3,1},{1,0},{8,10},{10,12},{12... | collective-permute-start | bytes 1376264 | tf_op jit(solution)/shard_map/ppermute | solution.py:30
  58.5 11.6 %collective-permute-start.15 = (bf16[128,1792]{1,0:T(8,128)(2,1)S(1)}, bf16[128,1792]{1,0:T(8,128)(2,1)S(1)}, u32[]{:S(2)}, u32[]{:S(2)}) collective-permute-start(bf16[128,1792]{1,0:T(8,128)(2,1)S(1)} %get-tuple-element.77.rest_2_), channel_id=1, source_target_pairs={{0,1},{2,0},{4,2},{6,4},{7,6},{5,7},{3,5},{1,3},{8,9},{10,8},{12,1... | collective-permute-start | bytes 1376264 | tf_op jit(solution)/shard_map/ppermute | solution.py:30
  59.9 2.6 %collective-permute-start.13 = (bf16[8,256]{1,0:T(8,128)(2,1)S(1)}, bf16[8,256]{1,0:T(8,128)(2,1)S(1)}, u32[]{:S(2)}, u32[]{:S(2)}) collective-permute-start(bf16[8,256]{1,0:T(8,128)(2,1)S(1)} %slice.44), channel_id=1, source_target_pairs={{0,8},{8,16},{16,24},{1,9},{9,17},{17,25},{2,10},{10,18},{18,26},{... | collective-permute-start | bytes 12296 | tf_op jit(solution)/shard_map/ppermute | solution.py:351
  70.1 17.5 %collective-permute-start.17 = (bf16[128,1792]{1,0:T(8,128)(2,1)}, bf16[128,1792]{1,0:T(8,128)(2,1)S(1)}, u32[]{:S(2)}, u32[]{:S(2)}) collective-permute-start(bf16[128,1792]{1,0:T(8,128)(2,1)} %collective-permute-done.14.rest_3_), channel_id=1, source_target_pairs={{0,2},{2,4},{4,6},{6,7},{7,5},{5,3},{3,1},{1,0},{8,10},{10,12},{12... | collective-permute-start | bytes 1376264 | tf_op jit(solution)/shard_map/ppermute | solution.py:30
  70.6 16.9 %collective-permute-start.18 = (bf16[128,1792]{1,0:T(8,128)(2,1)S(1)}, bf16[128,1792]{1,0:T(8,128)(2,1)S(1)}, u32[]{:S(2)}, u32[]{:S(2)}) collective-permute-start(bf16[128,1792]{1,0:T(8,128)(2,1)S(1)} %collective-permute-done.15.rest_4_), channel_id=1, source_target_pairs={{0,1},{2,0},{4,2},{6,4},{7,6},{5,7},{3,5},{1,3},{8,9},{10,8},{12,1... | collective-permute-start | bytes 1376264 | tf_op jit(solution)/shard_map/ppermute | solution.py:30
  72.1 18.9 %copy-start.6 = (bf16[128,1792]{1,0:T(8,128)(2,1)S(1)}, bf16[128,1792]{1,0:T(8,128)(2,1)}, u32[]{:S(2)}) copy-start(bf16[128,1792]{1,0:T(8,128)(2,1)} %copy-done.5) | copy-start | bytes 1376260
  87.6 6.7 %collective-permute-start.19 = (bf16[64,1792]{1,0:T(8,128)(2,1)S(1)}, bf16[64,1792]{1,0:T(8,128)(2,1)S(1)}, u32[]{:S(2)}, u32[]{:S(2)}) collective-permute-start(bf16[64,1792]{1,0:T(8,128)(2,1)S(1)} %get-tuple-element.83), channel_id=1, source_target_pairs={{0,2},{2,4},{4,6},{6,7},{7,5},{5,3},{3,1},{1,0},{8,10},{10,12},{12... | collective-permute-start | bytes 688136 | tf_op jit(solution)/shard_map/ppermute | solution.py:30
  88.4 6.0 %collective-permute-start.20 = (bf16[64,1792]{1,0:T(8,128)(2,1)S(1)}, bf16[64,1792]{1,0:T(8,128)(2,1)S(1)}, u32[]{:S(2)}, u32[]{:S(2)}) collective-permute-start(bf16[64,1792]{1,0:T(8,128)(2,1)S(1)} %get-tuple-element.84), channel_id=1, source_target_pairs={{0,1},{2,0},{4,2},{6,4},{7,6},{5,7},{3,5},{1,3},{8,9},{10,8},{12,1... | collective-permute-start | bytes 688136 | tf_op jit(solution)/shard_map/ppermute | solution.py:30
  89.7 1.3 %collective-permute-start.16 = (bf16[8,64,128]{2,1,0:T(8,128)(2,1)S(1)}, bf16[8,64,128]{2,1,0:T(8,128)(2,1)S(1)}, u32[]{:S(2)}, u32[]{:S(2)}) collective-permute-start(bf16[8,64,128]{2,1,0:T(8,128)(2,1)S(1)} %all_to_all.5.mine), channel_id=1, source_target_pairs={{0,8},{8,0},{16,24},{24,16},{1,9},{9,1},{17,25},{25,17},{2,10},{10... | collective-permute-start | bytes 393224 | tf_op jit(solution)/shard_map/ppermute | solution.py:389
  94.7 1.6 %collective-permute-start.21 = (bf16[64,1792]{1,0:T(8,128)(2,1)S(1)}, bf16[64,1792]{1,0:T(8,128)(2,1)S(1)}, u32[]{:S(2)}, u32[]{:S(2)}) collective-permute-start(bf16[64,1792]{1,0:T(8,128)(2,1)S(1)} %get-tuple-element.86), channel_id=1, source_target_pairs={{0,8},{8,0},{16,24},{24,16},{1,9},{9,1},{17,25},{25,17},{2,10},{10... | collective-permute-start | bytes 688136 | tf_op jit(solution)/shard_map/ppermute | solution.py:401

commit v13 on v11

--- a/solution.py
+++ b/solution.py
@@ -254,13 +254,13 @@
         out[...] = (result[i * rows : (i + 1) * rows] * scale).astype(BF16)
 
 
-def call(body, outs, scratch=(), vmem=48, flops=10**7, **kw):
+def call(body, outs, scratch=(), vmem=48, flops=10**7, moved=1 << 21, **kw):
     return pl.pallas_call(
         body,
         out_shape=outs,
         scratch_shapes=list(scratch),
         compiler_params=pltpu.CompilerParams(vmem_limit_bytes=vmem << 20),
-        cost_estimate=pl.CostEstimate(flops=flops, bytes_accessed=1 << 21, transcendentals=1 << 17),
+        cost_estimate=pl.CostEstimate(flops=flops, bytes_accessed=moved, transcendentals=0),
         **kw,
     )
 
@@ -359,8 +359,6 @@
     for step in range(2, last + 1):
         if step - 2 < len(orders):
             w_forth, w_back = after((w_forth, w_back), orders[step - 2])
-        if step == 4:
-            w_forth, w_back = after((w_forth, w_back), mine)
         if step == last:
             w_far = far_shift(w_forth, w_back)
             break
@@ -375,7 +373,7 @@
     for i, pair in enumerate(w_steps):
         pieces += pair
         distances += [-i - 1, i + 1]
-    total = call(functools.partial(product_early, distances), shape(2 * tok_own, columns), flops=10**9)(
+    total = call(functools.partial(product_early, distances), shape(2 * tok_own, columns), flops=1, moved=1)(
         mine, other, *pieces
     )
     half = shape(tok_own, columns, kind=BF16)

time: 94.8 us -> 92.5 us (0.976)
  blocking collectives: 21.6 us -> 6.83 us
  waiting for transfers between devices: 29.4 us -> 36.3 us
  starting transfers between devices: 20.2 us -> 25.1 us
    all_to_all x1 -> x0, blocking collectives: 14.8 us -> none  [local(): mine = lax.all_to_all(blocks, 'tensor', 0, 0)]
    ppermute x16, waiting for transfers between devices: 26.6 us -> 32.3 us  [ring_shift(): lax.ppermute(block, 'tensor', [(order[i], order[(i + step) % n]) for i in...]
    all_to_all x0 -> x1, starting transfers between devices: none -> 4.8 us  [local(): mine = lax.all_to_all(blocks, 'tensor', 0, 0)]
    all_to_all x0 -> x1, waiting for transfers between devices: none -> 1.17 us  [local(): mine = lax.all_to_all(blocks, 'tensor', 0, 0)]
  transfers between devices with their start and end apart: 20 -> 21, of which waited for: 10 -> 12; matrix products, arithmetic and copies ran while one was open for 4% -> 4% of each run, Pallas kernels for 15% -> 16%
where the time goes in v13:
time: 92.5 us; the launch traced here: 91.9 us
  waiting for transfers between devices  36.3 us (39%)
  starting transfers between devices  25.1 us (27%)
  Pallas kernels  15.4 us (17%)
  blocking collectives  6.83 us (7%)
  local copies, waits for them, and re-layouts  5.9 us (6%)
  matrix products  1.12 us (1%)
  other arithmetic  1.05 us (1%)
    ppermute x16, waiting for transfers between devices, ring_shift(): lax.ppermute(block, 'tensor', [(order[i], order[(i + step) % n]) for i in...  32.3 us
    ppermute x16, starting transfers between devices, ring_shift(): lax.ppermute(block, 'tensor', [(order[i], order[(i + step) % n]) for i in...  17.5 us
    pallas_call x4, Pallas kernels, local(): call(functools.partial(project, [distance for distance, _ in arrived], ah...  8.46 us
    all_gather x1, blocking collectives, local(): messages = lax.all_gather(message, 'seq')  6.83 us
    all_to_all x1, starting transfers between devices, local(): mine = lax.all_to_all(blocks, 'tensor', 0, 0)  4.8 us
    unnamed x26, local copies, waits for them, and re-layouts  3.73 us
    pallas_call x1, Pallas kernels, local(): call(functools.partial(product_early, distances), shape(2 * tok_own, colu...  2.14 us
  transfers between devices with their start and end apart: 21, of which 12 were waited for; matrix products, arithmetic and copies ran while one was open for 4% of the time, Pallas kernels for 16%

profile of v13, /device:TPU:0, one launch (start us, length us, event | category | flops | bytes accessed | tf_op | source)
XLA Modules:
  0.0 91.9 jit_solution(12597848002803448226)
XLA Ops:
  0.0 3.0 %collective-permute-start = (bf16[448,512]{1,0:T(8,128)(2,1)}, bf16[448,512]{1,0:T(8,128)(2,1)}, u32[]{:S(2)}, u32[]{:S(2)}) collective-permute-start(bf16[448,512]{1,0:T(8,128)(2,1)} %bitcast.12), channel_id=1, source_target_pairs={{0,2},{2,4},{4,6},{6,7},{7,5},{5,3},{3,1},{1,0},{8,10},{10,12},{12... | collective-permute-start | bytes 1376264 | tf_op jit(solution)/shard_map/ppermute | solution.py:31
  3.0 0.0 collective-permute-start.2
  3.0 0.8 slice.33
  3.8 1.4 %collective-permute-start.3 = (s32[8]{0:T(128)S(1)}, s32[8]{0:T(128)S(1)}, u32[]{:S(2)}, u32[]{:S(2)}) collective-permute-start(s32[8]{0:T(128)S(1)} %slice.33), channel_id=1, source_target_pairs={{0,8},{8,16},{16,24},{1,9},{9,17},{17,25},{2,10},{10,18},{18,26},{... | collective-permute-start | bytes 104 | tf_op jit(solution)/shard_map/ppermute | solution.py:293
  5.2 1.1 %convolution_bitcast_fusion.refs_3_.refs_4_ = bf16[3584,128]{1,0:T(8,128)(2,1)S(1)} fusion(bf16[2,128]{1,0:T(2,128)(2,1)} %constant.25.clone, bf16[3584,2]{0,1:T(2,128)(2,1)S(1)} %copy-done), kind=kOutput, calls=%fused_computation | convolution fusion | flops 1835008 | bytes 932352 | tf_op jit(solution)/shard_map/dot_general | solution.py:284
  6.4 0.0 copy-start.1
  6.4 1.5 %copy-done.1 = bf16[2,3584,128]{2,1,0:T(8,128)(2,1)S(1)} copy-done((bf16[2,3584,128]{2,1,0:T(8,128)(2,1)S(1)}, bf16[2,3584,128]{2,1,0:T(8,128)(2,1)}, u32[]{:S(2)}) %copy-start.1) | copy-done | bytes 1835032
  7.9 1.2 %copy-done.2 = bf16[3584,128]{1,0:T(8,128)(2,1)S(1)} copy-done((bf16[3584,128]{1,0:T(8,128)(2,1)S(1)}, bf16[3584,128]{1,0:T(8,128)(2,1)}, u32[]{:S(2)}) %copy-start.2) | copy-done | bytes 917528
  9.1 1.0 %copy-done.4 = bf16[512,448]{0,1:T(8,128)(2,1)S(1)} copy-done((bf16[512,448]{0,1:T(8,128)(2,1)S(1)}, bf16[512,448]{0,1:T(8,128)(2,1)}, u32[]{:S(2)}) %copy-start.4) | copy-done | bytes 458776
  10.1 0.6 shard_map.127.refs_5_
  10.7 3.1 %collective-permute-done.refs_0_ = bf16[448,512]{1,0:T(8,128)(2,1)} collective-permute-done((bf16[448,512]{1,0:T(8,128)(2,1)}, bf16[448,512]{1,0:T(8,128)(2,1)}, u32[]{:S(2)}, u32[]{:S(2)}) %collective-permute-start) | collective-permute-done | bytes 458784 | tf_op jit(solution)/shard_map/ppermute | solution.py:31
  13.8 1.8 %collective-permute-start.1 = (bf16[448,512]{1,0:T(8,128)(2,1)}, bf16[448,512]{1,0:T(8,128)(2,1)}, u32[]{:S(2)}, u32[]{:S(2)}) collective-permute-start(bf16[448,512]{1,0:T(8,128)(2,1)} %collective-permute-done.refs_0_), channel_id=1, source_target_pairs={{0,2},{2,4},{4,6},{6,7},{7,5},{5,3},{3,1},{1,0},{8,10},{10,12},{12... | collective-permute-start | bytes 1376264 | tf_op jit(solution)/shard_map/ppermute | solution.py:31
  15.6 0.2 collective-permute-start.5
  15.8 0.6 fusion
  16.4 0.1 slice.36
  16.5 0.1 broadcast_in_dim.27
  16.5 0.1 broadcast_in_dim_reshape.9.bias
  16.6 0.1 broadcast_in_dim.28
  16.7 0.1 broadcast_in_dim_reshape.10.rate
  16.8 0.1 broadcast_in_dim.29
  16.9 0.1 broadcast_in_dim_reshape.11.skip
  16.9 0.1 pad_add_fusion
  17.0 0.0 copy-start.9
  17.1 3.0 %shard_map.128.refs_5_ = f32[512,512]{1,0:T(8,128)S(1)} custom-call(bf16[448,512]{1,0:T(8,128)(2,1)} %collective-permute-done.refs_0_, bf16[448,512]{1,0:T(8,128)(2,1)S(1)} %collective-permute-done.2.refs_1_, bf16[2,3584,128]{2,1,0:T(8,128)(2,1)} %refs_2_.7, bf16[3584,128]{1,0:T(8,128)(2,1)S(1)} %copy-done.3, ...), custom_call_target="tpu_custom_call" | custom-call | flops 1000000000 | bytes 2097152 | tf_op jit(solution)/shard_map/pallas_call | solution.py:321
  20.0 6.0 %collective-permute-done.1.refs_0_ = bf16[448,512]{1,0:T(8,128)(2,1)} collective-permute-done((bf16[448,512]{1,0:T(8,128)(2,1)}, bf16[448,512]{1,0:T(8,128)(2,1)}, u32[]{:S(2)}, u32[]{:S(2)}) %collective-permute-start.1) | collective-permute-done | bytes 458784 | tf_op jit(solution)/shard_map/ppermute | solution.py:31
  26.0 1.6 %collective-permute-start.4 = (bf16[448,512]{1,0:T(8,128)(2,1)}, bf16[448,512]{1,0:T(8,128)(2,1)S(1)}, u32[]{:S(2)}, u32[]{:S(2)}) collective-permute-start(bf16[448,512]{1,0:T(8,128)(2,1)} %collective-permute-done.1.refs_0_), channel_id=1, source_target_pairs={{0,2},{2,4},{4,6},{6,7},{7,5},{5,3},{3,1},{1,0},{8,10},{10,12},{12... | collective-permute-start | bytes 1376264 | tf_op jit(solution)/shard_map/ppermute | solution.py:31
  27.6 0.0 collective-permute-done.5.refs_1_
  27.6 0.4 collective-permute-start.6
  28.1 0.1 multiply_convert_fusion.rest_0_
  28.2 1.6 %collective-permute-start.10 = (bf16[128,1792]{1,0:T(8,128)(2,1)S(1)}, bf16[128,1792]{1,0:T(8,128)(2,1)S(1)}, u32[]{:S(2)}, u32[]{:S(2)}) collective-permute-start(bf16[128,1792]{1,0:T(8,128)(2,1)S(1)} %multiply_convert_fusion.rest_0_), channel_id=1, source_target_pairs={{0,2},{2,4},{4,6},{6,7},{7,5},{5,3},{3,1},{1,0},{8,10},{10,12},{12... | collective-permute-start | bytes 1376264 | tf_op jit(solution)/shard_map/ppermute | solution.py:31
  29.9 0.4 collective-permute-start.11
  30.3 3.0 %shard_map.129.refs_5_ = f32[512,512]{1,0:T(8,128)S(1)} custom-call(bf16[448,512]{1,0:T(8,128)(2,1)} %collective-permute-done.1.refs_0_, bf16[448,512]{1,0:T(8,128)(2,1)} %collective-permute-done.5.refs_1_, bf16[2,3584,128]{2,1,0:T(8,128)(2,1)} %refs_2_.7, bf16[3584,128]{1,0:T(8,128)(2,1)S(1)} %copy-done.3, ...), custom_call_target="tpu_custom_call" | custom-call | flops 1000000000 | bytes 2097152 | tf_op jit(solution)/shard_map/pallas_call | solution.py:321
  33.3 6.4 %collective-permute-done.4.forth.refs_0_ = bf16[448,512]{1,0:T(8,128)(2,1)S(1)} collective-permute-done((bf16[448,512]{1,0:T(8,128)(2,1)}, bf16[448,512]{1,0:T(8,128)(2,1)S(1)}, u32[]{:S(2)}, u32[]{:S(2)}) %collective-permute-start.4) | collective-permute-done | bytes 458784 | tf_op jit(solution)/shard_map/ppermute | solution.py:31
  39.7 1.6 %collective-permute-done.6.back.refs_1_ = bf16[448,512]{1,0:T(8,128)(2,1)S(1)} collective-permute-done((bf16[448,512]{1,0:T(8,128)(2,1)}, bf16[448,512]{1,0:T(8,128)(2,1)S(1)}, u32[]{:S(2)}, u32[]{:S(2)}) %collective-permute-start.6) | collective-permute-done | bytes 458784 | tf_op jit(solution)/shard_map/ppermute | solution.py:31
  41.3 1.6 %collective-permute-start.7 = (bf16[224,512]{1,0:T(8,128)(2,1)S(1)}, bf16[224,512]{1,0:T(8,128)(2,1)S(1)}, u32[]{:S(2)}, u32[]{:S(2)}) collective-permute-start(bf16[224,512]{1,0:T(8,128)(2,1)S(1)} %get-tuple-element.44), channel_id=1, source_target_pairs={{0,2},{2,4},{4,6},{6,7},{7,5},{5,3},{3,1},{1,0},{8,10},{10,12},{12... | collective-permute-start | bytes 688136 | tf_op jit(solution)/shard_map/ppermute | solution.py:31
  43.0 0.5 collective-permute-start.8
  43.4 1.9 %shard_map.131 = (f32[512,512]{1,0:T(8,128)S(1)}, bf16[448,512]{1,0:T(8,128)(2,1)S(1)}) custom-call(bf16[448,512]{1,0:T(8,128)(2,1)S(1)} %collective-permute-done.4.forth.refs_0_, bf16[448,512]{1,0:T(8,128)(2,1)S(1)} %collective-permute-done.6.back.refs_1_, bf16[2,3584,128]{2,1,0:T(8,128)(2,1)} %refs_2_.7, bf16[3584,128]{1,0:T(8,128)(2,1)S(1)} %copy-done.3, ...), custom_call_target="tpu_custom_call" | custom-call | flops 1000000000 | bytes 2097152 | tf_op jit(solution)/shard_map/pallas_call | solution.py:321
  45.3 6.8 %collective-permute-done.7.top = bf16[224,512]{1,0:T(8,128)(2,1)S(1)} collective-permute-done((bf16[224,512]{1,0:T(8,128)(2,1)S(1)}, bf16[224,512]{1,0:T(8,128)(2,1)S(1)}, u32[]{:S(2)}, u32[]{:S(2)}) %collective-permute-start.7) | collective-permute-done | bytes 229408 | tf_op jit(solution)/shard_map/ppermute | solution.py:31
  52.0 1.0 %collective-permute-done.8.bottom = bf16[224,512]{1,0:T(8,128)(2,1)S(1)} collective-permute-done((bf16[224,512]{1,0:T(8,128)(2,1)S(1)}, bf16[224,512]{1,0:T(8,128)(2,1)S(1)}, u32[]{:S(2)}, u32[]{:S(2)}) %collective-permute-start.8) | collective-permute-done | bytes 229408 | tf_op jit(solution)/shard_map/ppermute | solution.py:31
  53.1 0.5 shard_map.132.proj
  53.6 0.0 collective-permute-done.10.rest_1_
  53.6 1.6 %collective-permute-start.12 = (bf16[128,1792]{1,0:T(8,128)(2,1)S(1)}, bf16[128,1792]{1,0:T(8,128)(2,1)}, u32[]{:S(2)}, u32[]{:S(2)}) collective-permute-start(bf16[128,1792]{1,0:T(8,128)(2,1)S(1)} %collective-permute-done.10.rest_1_), channel_id=1, source_target_pairs={{0,2},{2,4},{4,6},{6,7},{7,5},{5,3},{3,1},{1,0},{8,10},{10,12},{12... | collective-permute-start | bytes 1376264 | tf_op jit(solution)/shard_map/ppermute | solution.py:31
  55.2 0.5 collective-permute-start.13
  55.7 1.3 %collective-permute-start.9 = (bf16[8,256]{1,0:T(8,128)(2,1)S(1)}, bf16[8,256]{1,0:T(8,128)(2,1)S(1)}, u32[]{:S(2)}, u32[]{:S(2)}) collective-permute-start(bf16[8,256]{1,0:T(8,128)(2,1)S(1)} %slice.44), channel_id=1, source_target_pairs={{0,8},{8,16},{16,24},{1,9},{9,17},{17,25},{2,10},{10,18},{18,26},{... | collective-permute-start | bytes 12296 | tf_op jit(solution)/shard_map/ppermute | solution.py:335
  57.0 0.1 copy.16.seg_ext
  57.1 0.1 copy.17.seg_ext.seg_ext_a
  57.3 1.0 %shard_map.133 = (f32[256,128]{1,0:T(8,128)S(1)}, f32[256,128]{1,0:T(8,128)S(1)}, f32[256,128]{1,0:T(8,128)S(1)}, f32[72,128]{1,0:T(8,128)S(1)}, f32[256,128]{1,0:T(8,128)S(1)}) custom-call(f32[512,512]{1,0:T(8,128)S(1)} %shard_map.132.proj, s32[264,1]{1,0:T(8,128)S(1)} %copy.16.seg_ext, s32[1,256]{1,0:T(1,128)S(1)} %bitcast.16, f32[4,128]{1,0:T(4,128)S(1)} %copy-done.5, ...), custom_call_target="tpu_custom_call" | custom-call | flops 10000000 | bytes 2097152 | tf_op jit(solution)/shard_map/pallas_call | solution.py:340
  58.3 1.2 %shard_map.134 = (f32[256,128]{1,0:T(8,128)S(1)}, f32[256,128]{1,0:T(8,128)S(1)}, f32[256,128]{1,0:T(8,128)S(1)}, f32[256,128]{1,0:T(8,128)S(1)}, f32[256,128]{1...) custom-call(f32[512,512]{1,0:T(8,128)S(1)} %shard_map.132.proj, ...), custom_call_target="tpu_custom_call" | custom-call | flops 10000000 | bytes 2097152 | tf_op jit(solution)/shard_map/pallas_call | solution.py:345
  59.5 6.8 %all-gather = f32[288,128]{1,0:T(8,128)S(1)} all-gather(f32[72,128]{1,0:T(8,128)S(1)} %get-tuple-element.49), channel_id=2, replica_groups=mesh['seq'=4,'tensor'=8] {'seq'}, dimensions={0}, use_global_device_ids=true | all-gather | bytes 184320 | tf_op jit(solution)/shard_map/all_gather | solution.py:350
  66.3 1.6 %collective-permute-start.15 = (bf16[128,1792]{1,0:T(8,128)(2,1)}, bf16[128,1792]{1,0:T(8,128)(2,1)S(1)}, u32[]{:S(2)}, u32[]{:S(2)}) collective-permute-start(bf16[128,1792]{1,0:T(8,128)(2,1)} %collective-permute-done.12.rest_3_), channel_id=1, source_target_pairs={{0,2},{2,4},{4,6},{6,7},{7,5},{5,3},{3,1},{1,0},{8,10},{10,12},{12... | collective-permute-start | bytes 1376264 | tf_op jit(solution)/shard_map/ppermute | solution.py:31
  68.0 0.4 collective-permute-start.16
  68.4 1.8 %shard_map.135 = bf16[512,128]{1,0:T(8,128)(2,1)} custom-call(s32[1,1]{1,0:T(1,128)} %bitcast.seg_first, f32[4,72,128]{2,1,0:T(8,128)S(1)} %bitcast.11, s32[264,1]{1,0:T(8,128)S(1)} %copy.17.seg_ext.seg_ext_a, s32[1,256]{1,0:T(1,128)S(1)} %bitcast.15, f32[1,128]{1,0:T(1,128)S(1)} %broadcast_in_dim_reshape.11.skip, f32[512,512]{1,0:T(8,128)S(1)} %shard_map.132.proj, ...), custom_call_target="tpu_custom_call" | custom-call | flops 10000000 | bytes 2097152 | tf_op jit(solution)/shard_map/pallas_call | solution.py:351
  70.2 4.8 %all-to-all-start = ((bf16[8,64,128]{2,1,0:T(8,128)(2,1)}), bf16[8,64,128]{2,1,0:T(8,128)(2,1)S(1)}, u32[]{:S(2)}, u32[]{:S(2)}) async-start(bf16[8,64,128]{2,1,0:T(8,128)(2,1)} %bitcast.7), calls=%async_computation | async-start | bytes 262144 | tf_op jit(solution)/shard_map/all_to_all | solution.py:369
  75.0 4.8 %collective-permute-done.15.rest_5_.forth = bf16[128,1792]{1,0:T(8,128)(2,1)S(1)} collective-permute-done((bf16[128,1792]{1,0:T(8,128)(2,1)}, bf16[128,1792]{1,0:T(8,128)(2,1)S(1)}, u32[]{:S(2)}, u32[]{:S(2)}) %collective-permute-start.15) | collective-permute-done | bytes 458784 | tf_op jit(solution)/shard_map/ppermute | solution.py:31
  79.8 1.2 %collective-permute-done.16.rest_6_.back = bf16[128,1792]{1,0:T(8,128)(2,1)S(1)} collective-permute-done((bf16[128,1792]{1,0:T(8,128)(2,1)}, bf16[128,1792]{1,0:T(8,128)(2,1)S(1)}, u32[]{:S(2)}, u32[]{:S(2)}) %collective-permute-start.16) | collective-permute-done | bytes 458784 | tf_op jit(solution)/shard_map/ppermute | solution.py:31
  81.1 2.2 %collective-permute-start.17 = (bf16[64,1792]{1,0:T(8,128)(2,1)S(1)}, bf16[64,1792]{1,0:T(8,128)(2,1)S(1)}, u32[]{:S(2)}, u32[]{:S(2)}) collective-permute-start(bf16[64,1792]{1,0:T(8,128)(2,1)S(1)} %get-tuple-element.67), channel_id=1, source_target_pairs={{0,2},{2,4},{4,6},{6,7},{7,5},{5,3},{3,1},{1,0},{8,10},{10,12},{12... | collective-permute-start | bytes 688136 | tf_op jit(solution)/shard_map/ppermute | solution.py:31
  83.2 1.2 %all-to-all-done.mine = bf16[8,64,128]{2,1,0:T(8,128)(2,1)S(1)} async-done(((bf16[8,64,128]{2,1,0:T(8,128)(2,1)}), bf16[8,64,128]{2,1,0:T(8,128)(2,1)S(1)}, u32[]{:S(2)}, u32[]{:S(2)}) %all-to-all-start) | async-done | bytes 131104 | tf_op jit(solution)/shard_map/all_to_all | solution.py:369
  84.4 1.3 %collective-permute-done.14.other = bf16[8,64,128]{2,1,0:T(8,128)(2,1)S(1)} collective-permute-done((bf16[8,64,128]{2,1,0:T(8,128)(2,1)S(1)}, bf16[8,64,128]{2,1,0:T(8,128)(2,1)S(1)}, u32[]{:S(2)}, u32[]{:S(2)}) %collective-permute-start.14) | collective-permute-done | bytes 131104 | tf_op jit(solution)/shard_map/ppermute | solution.py:371
  85.7 2.1 %shard_map.136.total = f32[128,1792]{1,0:T(8,128)S(1)} custom-call(bf16[8,64,128]{2,1,0:T(8,128)(2,1)S(1)} %all-to-all-done.mine, bf16[8,64,128]{2,1,0:T(8,128)(2,1)S(1)} %collective-permute-done.14.other, bf16[128,1792]{1,0:T(8,128)(2,1)S(1)} %multiply_convert_fusion.rest_0_, bf16[128,1792]{1,0:T(8,128)(2,1)S(1)} %collective-permute-done.10.rest_1_, ...), custom_call_target="tpu_custom_call" | custom-call | flops 1 | bytes 1 | tf_op jit(solution)/shard_map/pallas_call | solution.py:376
  87.9 1.3 %collective-permute-done.18.bottom = bf16[64,1792]{1,0:T(8,128)(2,1)S(1)} collective-permute-done((bf16[64,1792]{1,0:T(8,128)(2,1)S(1)}, bf16[64,1792]{1,0:T(8,128)(2,1)S(1)}, u32[]{:S(2)}, u32[]{:S(2)}) %collective-permute-start.18) | collective-permute-done | bytes 229408 | tf_op jit(solution)/shard_map/ppermute | solution.py:31
  89.2 0.3 shard_map.138
  89.5 0.1 collective-permute-start.19
  89.6 1.5 %collective-permute-done.19 = bf16[64,1792]{1,0:T(8,128)(2,1)S(1)} collective-permute-done((bf16[64,1792]{1,0:T(8,128)(2,1)S(1)}, bf16[64,1792]{1,0:T(8,128)(2,1)S(1)}, u32[]{:S(2)}, u32[]{:S(2)}) %collective-permute-start.19) | collective-permute-done | bytes 229408 | tf_op jit(solution)/shard_map/ppermute | solution.py:383
  91.1 0.8 pad_maximum_fusion
  (38 shorter events, 0.2 us)
Async XLA Ops:
  0.0 5.2 %copy-start = (bf16[3584,2]{0,1:T(2,128)(2,1)S(1)}, bf16[3584,2]{0,1:T(2,128)(2,1)}, u32[]{:S(2)}) copy-start(bf16[3584,2]{0,1:T(2,128)(2,1)} %param.16) | copy-start | bytes 43012
  0.0 13.8 %collective-permute-start = (bf16[448,512]{1,0:T(8,128)(2,1)}, bf16[448,512]{1,0:T(8,128)(2,1)}, u32[]{:S(2)}, u32[]{:S(2)}) collective-permute-start(bf16[448,512]{1,0:T(8,128)(2,1)} %bitcast.12), channel_id=1, source_target_pairs={{0,2},{2,4},{4,6},{6,7},{7,5},{5,3},{3,1},{1,0},{8,10},{10,12},{12... | collective-permute-start | bytes 1376264 | tf_op jit(solution)/shard_map/ppermute | solution.py:31
  3.0 12.6 %collective-permute-start.2 = (bf16[448,512]{1,0:T(8,128)(2,1)}, bf16[448,512]{1,0:T(8,128)(2,1)S(1)}, u32[]{:S(2)}, u32[]{:S(2)}) collective-permute-start(bf16[448,512]{1,0:T(8,128)(2,1)} %bitcast.13), channel_id=1, source_target_pairs={{0,1},{2,0},{4,2},{6,4},{7,6},{5,7},{3,5},{1,3},{8,9},{10,8},{12,1... | collective-permute-start | bytes 1376264 | tf_op jit(solution)/shard_map/ppermute | solution.py:31
  3.8 13.2 %collective-permute-start.3 = (s32[8]{0:T(128)S(1)}, s32[8]{0:T(128)S(1)}, u32[]{:S(2)}, u32[]{:S(2)}) collective-permute-start(s32[8]{0:T(128)S(1)} %slice.33), channel_id=1, source_target_pairs={{0,8},{8,16},{16,24},{1,9},{9,17},{17,25},{2,10},{10,18},{18,26},{... | collective-permute-start | bytes 104 | tf_op jit(solution)/shard_map/ppermute | solution.py:293
  6.4 1.5 %copy-start.1 = (bf16[2,3584,128]{2,1,0:T(8,128)(2,1)S(1)}, bf16[2,3584,128]{2,1,0:T(8,128)(2,1)}, u32[]{:S(2)}) copy-start(bf16[2,3584,128]{2,1,0:T(8,128)(2,1)} %refs_2_.7) | copy-start | bytes 5505028
  7.9 1.2 %copy-start.2 = (bf16[3584,128]{1,0:T(8,128)(2,1)S(1)}, bf16[3584,128]{1,0:T(8,128)(2,1)}, u32[]{:S(2)}) copy-start(bf16[3584,128]{1,0:T(8,128)(2,1)} %refs_3_.5) | copy-start | bytes 2752516
  9.1 1.0 %copy-start.4 = (bf16[512,448]{0,1:T(8,128)(2,1)S(1)}, bf16[512,448]{0,1:T(8,128)(2,1)}, u32[]{:S(2)}) copy-start(bf16[512,448]{0,1:T(8,128)(2,1)} %param.13) | copy-start | bytes 1376260
  10.1 5.7 %copy-start.8 = (s32[512]{0:T(512)S(1)}, s32[512]{0:T(512)}, u32[]{:S(2)}) copy-start(s32[512]{0:T(512)} %param.24) | copy-start | bytes 6148
  10.1 6.4 %copy-start.10 = (f32[2]{0:T(128)S(1)}, f32[2]{0:T(128)}, u32[]{:S(2)}) copy-start(f32[2]{0:T(128)} %param.17) | copy-start | bytes 28
  10.1 6.6 %copy-start.11 = (f32[2]{0:T(128)S(1)}, f32[2]{0:T(128)}, u32[]{:S(2)}) copy-start(f32[2]{0:T(128)} %param.18) | copy-start | bytes 28
  10.1 6.7 %copy-start.12 = (f32[2]{0:T(128)S(1)}, f32[2]{0:T(128)}, u32[]{:S(2)}) copy-start(f32[2]{0:T(128)} %param.19) | copy-start | bytes 28
  10.1 7.0 %copy-start.3 = (bf16[3584,128]{1,0:T(8,128)(2,1)S(1)}, bf16[3584,128]{1,0:T(8,128)(2,1)}, u32[]{:S(2)}) copy-start(bf16[3584,128]{1,0:T(8,128)(2,1)} %refs_3_.5) | copy-start | bytes 2752516
  13.8 12.3 %collective-permute-start.1 = (bf16[448,512]{1,0:T(8,128)(2,1)}, bf16[448,512]{1,0:T(8,128)(2,1)}, u32[]{:S(2)}, u32[]{:S(2)}) collective-permute-start(bf16[448,512]{1,0:T(8,128)(2,1)} %collective-permute-done.refs_0_), channel_id=1, source_target_pairs={{0,2},{2,4},{4,6},{6,7},{7,5},{5,3},{3,1},{1,0},{8,10},{10,12},{12... | collective-permute-start | bytes 1376264 | tf_op jit(solution)/shard_map/ppermute | solution.py:31
  15.6 12.0 %collective-permute-start.5 = (bf16[448,512]{1,0:T(8,128)(2,1)S(1)}, bf16[448,512]{1,0:T(8,128)(2,1)}, u32[]{:S(2)}, u32[]{:S(2)}) collective-permute-start(bf16[448,512]{1,0:T(8,128)(2,1)S(1)} %collective-permute-done.2.refs_1_), channel_id=1, source_target_pairs={{0,1},{2,0},{4,2},{6,4},{7,6},{5,7},{3,5},{1,3},{8,9},{10,8},{12,1... | collective-permute-start | bytes 1376264 | tf_op jit(solution)/shard_map/ppermute | solution.py:31
  17.0 11.0 %copy-start.7 = (bf16[128,3584]{1,0:T(8,128)(2,1)S(1)}, bf16[128,3584]{1,0:T(8,128)(2,1)}, u32[]{:S(2)}) copy-start(bf16[128,3584]{1,0:T(8,128)(2,1)} %param.23) | copy-start | bytes 2752516
  17.0 11.0 %copy-start.9 = (f32[128]{0:T(128)S(1)}, f32[128]{0:T(128)}, u32[]{:S(2)}) copy-start(f32[128]{0:T(128)} %param.22) | copy-start | bytes 1540
  26.0 13.7 %collective-permute-start.4 = (bf16[448,512]{1,0:T(8,128)(2,1)}, bf16[448,512]{1,0:T(8,128)(2,1)S(1)}, u32[]{:S(2)}, u32[]{:S(2)}) collective-permute-start(bf16[448,512]{1,0:T(8,128)(2,1)} %collective-permute-done.1.refs_0_), channel_id=1, source_target_pairs={{0,2},{2,4},{4,6},{6,7},{7,5},{5,3},{3,1},{1,0},{8,10},{10,12},{12... | collective-permute-start | bytes 1376264 | tf_op jit(solution)/shard_map/ppermute | solution.py:31
  27.6 13.7 %collective-permute-start.6 = (bf16[448,512]{1,0:T(8,128)(2,1)}, bf16[448,512]{1,0:T(8,128)(2,1)S(1)}, u32[]{:S(2)}, u32[]{:S(2)}) collective-permute-start(bf16[448,512]{1,0:T(8,128)(2,1)} %collective-permute-done.5.refs_1_), channel_id=1, source_target_pairs={{0,1},{2,0},{4,2},{6,4},{7,6},{5,7},{3,5},{1,3},{8,9},{10,8},{12,1... | collective-permute-start | bytes 1376264 | tf_op jit(solution)/shard_map/ppermute | solution.py:31
  28.2 25.3 %collective-permute-start.10 = (bf16[128,1792]{1,0:T(8,128)(2,1)S(1)}, bf16[128,1792]{1,0:T(8,128)(2,1)S(1)}, u32[]{:S(2)}, u32[]{:S(2)}) collective-permute-start(bf16[128,1792]{1,0:T(8,128)(2,1)S(1)} %multiply_convert_fusion.rest_0_), channel_id=1, source_target_pairs={{0,2},{2,4},{4,6},{6,7},{7,5},{5,3},{3,1},{1,0},{8,10},{10,12},{12... | collective-permute-start | bytes 1376264 | tf_op jit(solution)/shard_map/ppermute | solution.py:31
  29.9 23.7 %collective-permute-start.11 = (bf16[128,1792]{1,0:T(8,128)(2,1)S(1)}, bf16[128,1792]{1,0:T(8,128)(2,1)S(1)}, u32[]{:S(2)}, u32[]{:S(2)}) collective-permute-start(bf16[128,1792]{1,0:T(8,128)(2,1)S(1)} %multiply_convert_fusion.rest_0_), channel_id=1, source_target_pairs={{0,1},{2,0},{4,2},{6,4},{7,6},{5,7},{3,5},{1,3},{8,9},{10,8},{12,1... | collective-permute-start | bytes 1376264 | tf_op jit(solution)/shard_map/ppermute | solution.py:31
  41.3 10.7 %collective-permute-start.7 = (bf16[224,512]{1,0:T(8,128)(2,1)S(1)}, bf16[224,512]{1,0:T(8,128)(2,1)S(1)}, u32[]{:S(2)}, u32[]{:S(2)}) collective-permute-start(bf16[224,512]{1,0:T(8,128)(2,1)S(1)} %get-tuple-element.44), channel_id=1, source_target_pairs={{0,2},{2,4},{4,6},{6,7},{7,5},{5,3},{3,1},{1,0},{8,10},{10,12},{12... | collective-permute-start | bytes 688136 | tf_op jit(solution)/shard_map/ppermute | solution.py:31
  43.0 10.1 %collective-permute-start.8 = (bf16[224,512]{1,0:T(8,128)(2,1)S(1)}, bf16[224,512]{1,0:T(8,128)(2,1)S(1)}, u32[]{:S(2)}, u32[]{:S(2)}) collective-permute-start(bf16[224,512]{1,0:T(8,128)(2,1)S(1)} %get-tuple-element.45), channel_id=1, source_target_pairs={{0,1},{2,0},{4,2},{6,4},{7,6},{5,7},{3,5},{1,3},{8,9},{10,8},{12,1... | collective-permute-start | bytes 688136 | tf_op jit(solution)/shard_map/ppermute | solution.py:31
  53.1 4.2 %copy-start.5 = (f32[4,128]{1,0:T(4,128)S(1)}, f32[4,128]{1,0:T(4,128)}, u32[]{:S(2)}) copy-start(f32[4,128]{1,0:T(4,128)} %taps_x.3) | copy-start | bytes 6148
  53.1 4.2 %copy-start.6 = (f32[4,128]{1,0:T(4,128)S(1)}, f32[4,128]{1,0:T(4,128)}, u32[]{:S(2)}) copy-start(f32[4,128]{1,0:T(4,128)} %taps_bc.3) | copy-start | bytes 6148
  53.6 12.7 %collective-permute-start.12 = (bf16[128,1792]{1,0:T(8,128)(2,1)S(1)}, bf16[128,1792]{1,0:T(8,128)(2,1)}, u32[]{:S(2)}, u32[]{:S(2)}) collective-permute-start(bf16[128,1792]{1,0:T(8,128)(2,1)S(1)} %collective-permute-done.10.rest_1_), channel_id=1, source_target_pairs={{0,2},{2,4},{4,6},{6,7},{7,5},{5,3},{3,1},{1,0},{8,10},{10,12},{12... | collective-permute-start | bytes 1376264 | tf_op jit(solution)/shard_map/ppermute | solution.py:31
  55.2 11.1 %collective-permute-start.13 = (bf16[128,1792]{1,0:T(8,128)(2,1)S(1)}, bf16[128,1792]{1,0:T(8,128)(2,1)}, u32[]{:S(2)}, u32[]{:S(2)}) collective-permute-start(bf16[128,1792]{1,0:T(8,128)(2,1)S(1)} %collective-permute-done.11.rest_2_), channel_id=1, source_target_pairs={{0,1},{2,0},{4,2},{6,4},{7,6},{5,7},{3,5},{1,3},{8,9},{10,8},{12,1... | collective-permute-start | bytes 1376264 | tf_op jit(solution)/shard_map/ppermute | solution.py:31
  55.7 2.6 %collective-permute-start.9 = (bf16[8,256]{1,0:T(8,128)(2,1)S(1)}, bf16[8,256]{1,0:T(8,128)(2,1)S(1)}, u32[]{:S(2)}, u32[]{:S(2)}) collective-permute-start(bf16[8,256]{1,0:T(8,128)(2,1)S(1)} %slice.44), channel_id=1, source_target_pairs={{0,8},{8,16},{16,24},{1,9},{9,17},{17,25},{2,10},{10,18},{18,26},{... | collective-permute-start | bytes 12296 | tf_op jit(solution)/shard_map/ppermute | solution.py:335
  66.3 13.4 %collective-permute-start.15 = (bf16[128,1792]{1,0:T(8,128)(2,1)}, bf16[128,1792]{1,0:T(8,128)(2,1)S(1)}, u32[]{:S(2)}, u32[]{:S(2)}) collective-permute-start(bf16[128,1792]{1,0:T(8,128)(2,1)} %collective-permute-done.12.rest_3_), channel_id=1, source_target_pairs={{0,2},{2,4},{4,6},{6,7},{7,5},{5,3},{3,1},{1,0},{8,10},{10,12},{12... | collective-permute-start | bytes 1376264 | tf_op jit(solution)/shard_map/ppermute | solution.py:31
  68.0 13.1 %collective-permute-start.16 = (bf16[128,1792]{1,0:T(8,128)(2,1)}, bf16[128,1792]{1,0:T(8,128)(2,1)S(1)}, u32[]{:S(2)}, u32[]{:S(2)}) collective-permute-start(bf16[128,1792]{1,0:T(8,128)(2,1)} %collective-permute-done.13.rest_4_), channel_id=1, source_target_pairs={{0,1},{2,0},{4,2},{6,4},{7,6},{5,7},{3,5},{1,3},{8,9},{10,8},{12,1... | collective-permute-start | bytes 1376264 | tf_op jit(solution)/shard_map/ppermute | solution.py:31
  70.2 14.2 %all-to-all-start = ((bf16[8,64,128]{2,1,0:T(8,128)(2,1)}), bf16[8,64,128]{2,1,0:T(8,128)(2,1)S(1)}, u32[]{:S(2)}, u32[]{:S(2)}) async-start(bf16[8,64,128]{2,1,0:T(8,128)(2,1)} %bitcast.7), calls=%async_computation | async-start | bytes 262144 | tf_op jit(solution)/shard_map/all_to_all | solution.py:369
  81.1 6.8 %collective-permute-start.17 = (bf16[64,1792]{1,0:T(8,128)(2,1)S(1)}, bf16[64,1792]{1,0:T(8,128)(2,1)S(1)}, u32[]{:S(2)}, u32[]{:S(2)}) collective-permute-start(bf16[64,1792]{1,0:T(8,128)(2,1)S(1)} %get-tuple-element.67), channel_id=1, source_target_pairs={{0,2},{2,4},{4,6},{6,7},{7,5},{5,3},{3,1},{1,0},{8,10},{10,12},{12... | collective-permute-start | bytes 688136 | tf_op jit(solution)/shard_map/ppermute | solution.py:31
  83.2 6.0 %collective-permute-start.18 = (bf16[64,1792]{1,0:T(8,128)(2,1)S(1)}, bf16[64,1792]{1,0:T(8,128)(2,1)S(1)}, u32[]{:S(2)}, u32[]{:S(2)}) collective-permute-start(bf16[64,1792]{1,0:T(8,128)(2,1)S(1)} %get-tuple-element.68), channel_id=1, source_target_pairs={{0,1},{2,0},{4,2},{6,4},{7,6},{5,7},{3,5},{1,3},{8,9},{10,8},{12,1... | collective-permute-start | bytes 688136 | tf_op jit(solution)/shard_map/ppermute | solution.py:31
  84.4 1.3 %collective-permute-start.14 = (bf16[8,64,128]{2,1,0:T(8,128)(2,1)S(1)}, bf16[8,64,128]{2,1,0:T(8,128)(2,1)S(1)}, u32[]{:S(2)}, u32[]{:S(2)}) collective-permute-start(bf16[8,64,128]{2,1,0:T(8,128)(2,1)S(1)} %all-to-all-done.mine), channel_id=1, source_target_pairs={{0,8},{8,0},{16,24},{24,16},{1,9},{9,1},{17,25},{25,17},{2,10},{10... | collective-permute-start | bytes 393224 | tf_op jit(solution)/shard_map/ppermute | solution.py:371
  89.5 1.6 %collective-permute-start.19 = (bf16[64,1792]{1,0:T(8,128)(2,1)S(1)}, bf16[64,1792]{1,0:T(8,128)(2,1)S(1)}, u32[]{:S(2)}, u32[]{:S(2)}) collective-permute-start(bf16[64,1792]{1,0:T(8,128)(2,1)S(1)} %get-tuple-element.70), channel_id=1, source_target_pairs={{0,8},{8,0},{16,24},{24,16},{1,9},{9,1},{17,25},{25,17},{2,10},{10... | collective-permute-start | bytes 688136 | tf_op jit(solution)/shard_map/ppermute | solution.py:383

commit v14 on v13

--- a/solution.py
+++ b/solution.py
@@ -59,6 +59,26 @@
 def source_of(distance):
     n = lax.axis_size("tensor")
     return ring_index((ring_place(lax.axis_index("tensor"), n) + distance + n) % n, n)
+
+
+def near_start(side, whole, near):
+    odd = lax.axis_index("seq") // 2 % 2
+    return pl.multiple_of((odd if side == 0 else 1 - odd) * (whole - near), 16)
+
+
+def take_near(*refs):
+    for side, (block, out) in enumerate(zip(refs[:2], refs[2:])):
+        near = out.shape[0]
+        out[...] = block[pl.ds(near_start(side, block.shape[0], near), near)]
+
+
+def pass_on(*refs):
+    for side, (near, lacked, half) in enumerate(zip(refs[:2], refs[2:4], refs[4:])):
+        odd = lax.axis_index("seq") // 2 % 2
+        high = odd if side == 0 else 1 - odd
+        for out in (lacked, half):
+            first = pl.multiple_of(high * (near.shape[0] - out.shape[0]), 16)
+            out[...] = near[pl.ds(first, out.shape[0])]
 
 
 def project(distances, ahead, first, *refs):
@@ -240,10 +260,16 @@
     rest[-1][...] = product((mine, other), distances, rest[:-1])
 
 
-def product_last(distance, mine, other, total, top, bottom, mine_out, other_out, held):
-    held[: top.shape[0]] = top[...]
-    held[top.shape[0] :] = bottom[...]
-    result = product((mine, other), [distance], [held]) + total[...]
+def product_last(distance, mine, other, total, *refs):
+    near, lacked, far, (mine_out, other_out, held) = refs[:2], refs[2:4], refs[4:6], refs[6:]
+    whole = held.shape[1]
+    for side in range(2):
+        for block, part in ((side, near[side]), (2, far[side])):
+            size = part.shape[0]
+            held[block, pl.ds(near_start(side, whole, size), size)] = part[...]
+        size = lacked[side].shape[0]
+        held[side, pl.ds(near_start(1 - side, whole, size), size)] = lacked[side][...]
+    result = product((mine, other), [1 - distance, distance - 1, distance], [held.at[k] for k in range(3)]) + total[...]
     blocks, rows, width = mine.shape
     for i, (gated, out) in enumerate(((mine, mine_out), (other, other_out))):
         squares = jnp.zeros((rows, width), F32)
@@ -355,18 +381,22 @@
     tok_own = tok_rows // n_tensor
 
     w_steps = [(w_forth, w_back)]
-    orders = [proj, messages]
-    for step in range(2, last + 1):
-        if step - 2 < len(orders):
-            w_forth, w_back = after((w_forth, w_back), orders[step - 2])
-        if step == last:
-            w_far = far_shift(w_forth, w_back)
-            break
+    for step in range(2, last - 1):
+        w_forth, w_back = after((w_forth, w_back), proj)
         w_forth, w_back = ring_shift(w_forth, 1), ring_shift(w_back, -1)
         w_steps.append((w_forth, w_back))
-        if step == 2:
-            blocks = after(gated, w_forth, w_back).reshape(n_tensor, tok_own, width)
-            mine = lax.all_to_all(blocks, "tensor", 0, 0)
+    gated = after(gated, w_forth, w_back)
+    near = width * 5 // 8
+    parts = lambda size: [shape(size, columns, kind=BF16)] * 2
+    w_forth, w_back = call(take_near, parts(near))(*after((w_forth, w_back), messages))
+    w_near = ring_shift(w_forth, 1), ring_shift(w_back, -1)
+    lacked_forth, lacked_back, *halves_on = call(
+        pass_on, parts(width - near) + parts(width // 2)
+    )(*w_near)
+    w_far = ring_shift(halves_on[0], 1), ring_shift(halves_on[1], -1)
+    other_y = [(i, i ^ 2) for i in range(n_seq)]
+    w_lacked = [lax.ppermute(part, "seq", other_y) for part in (lacked_forth, lacked_back)]
+    mine = lax.all_to_all(gated.reshape(n_tensor, tok_own, width), "tensor", 0, 0)
     swap = [(i, i ^ 1) for i in range(n_seq)]
     other = lax.ppermute(mine, "seq", swap)
     pieces, distances = [own], [0]
@@ -378,8 +408,8 @@
     )
     half = shape(tok_own, columns, kind=BF16)
     out_own, out_other = call(
-        functools.partial(product_last, last), [half, half], [pltpu.VMEM((width, columns), BF16)], flops=10**8
-    )(mine, other, total, *w_far)
+        functools.partial(product_last, last), [half, half], [pltpu.VMEM((3, width, columns), BF16)], flops=10**8
+    )(mine, other, total, *w_near, *w_lacked, *w_far)
     arrived = lax.ppermute(out_other, "seq", swap)
     is_first = core == 0
     return jnp.concatenate([jnp.where(is_first, out_own, arrived), jnp.where(is_first, arrived, out_own)], 1)

time: 92.5 us -> 93.2 us (level)
  waiting for transfers between devices: 36.3 us -> 33.4 us
  starting transfers between devices: 25.1 us -> 27 us
  Pallas kernels: 15.4 us -> 17.1 us
    ppermute x16, waiting for transfers between devices: 32.3 us -> 27 us  [ring_shift(): lax.ppermute(block, 'tensor', [(order[i], order[(i + step) % n]) for i in...]
    ppermute x0 -> x2, waiting for transfers between devices: none -> 2.28 us  [local(): lax.ppermute(part, 'seq', other_y)]
    ppermute x0 -> x2, starting transfers between devices: none -> 2.03 us  [local(): lax.ppermute(part, 'seq', other_y)]
    pallas_call x1 -> x3, Pallas kernels: 0.28 us -> 2.29 us  [the longest x1 0.84 us: local(): call(take_near, parts(near))(*after((w_forth, w_back), messages))]
  transfers between devices with their start and end apart: 21 -> 23, of which waited for: 12 -> 13; matrix products, arithmetic and copies ran while one was open for 4% -> 4% of each run, Pallas kernels for 16% -> 17%
where the time goes in v14:
time: 93.2 us; the launch traced here: 92.6 us
  waiting for transfers between devices  33.4 us (36%)
  starting transfers between devices  27 us (29%)
  Pallas kernels  17.1 us (18%)
  blocking collectives  6.82 us (7%)
  local copies, waits for them, and re-layouts  5.9 us (6%)
  matrix products  1.12 us (1%)
  other arithmetic  1.05 us (1%)
    ppermute x16, waiting for transfers between devices, ring_shift(): lax.ppermute(block, 'tensor', [(order[i], order[(i + step) % n]) for i in...  27 us
    ppermute x16, starting transfers between devices, ring_shift(): lax.ppermute(block, 'tensor', [(order[i], order[(i + step) % n]) for i in...  17.4 us
    pallas_call x4, Pallas kernels, local(): call(functools.partial(project, [distance for distance, _ in arrived], ah...  8.45 us
    all_gather x1, blocking collectives, local(): messages = lax.all_gather(message, 'seq')  6.82 us
    all_to_all x1, starting transfers between devices, local(): lax.all_to_all(gated.reshape(n_tensor, tok_own, width), 'tensor', 0, 0)  4.79 us
    unnamed x26, local copies, waits for them, and re-layouts  3.73 us
    ppermute x2, waiting for transfers between devices, local(): lax.ppermute(part, 'seq', other_y)  2.28 us
    ppermute x2, starting transfers between devices, local(): lax.ppermute(part, 'seq', other_y)  2.03 us
  transfers between devices with their start and end apart: 23, of which 13 were waited for; matrix products, arithmetic and copies ran while one was open for 4% of the time, Pallas kernels for 17%

profile of v14, /device:TPU:0, one launch (start us, length us, event | category | flops | bytes accessed | tf_op | source)
XLA Modules:
  0.0 92.6 jit_solution(17524234423261006627)
XLA Ops:
  0.0 3.0 %collective-permute-start = (bf16[448,512]{1,0:T(8,128)(2,1)}, bf16[448,512]{1,0:T(8,128)(2,1)}, u32[]{:S(2)}, u32[]{:S(2)}) collective-permute-start(bf16[448,512]{1,0:T(8,128)(2,1)} %bitcast.12), channel_id=1, source_target_pairs={{0,2},{2,4},{4,6},{6,7},{7,5},{5,3},{3,1},{1,0},{8,10},{10,12},{12... | collective-permute-start | bytes 1376264 | tf_op jit(solution)/shard_map/ppermute | solution.py:31
  3.0 0.8 slice.33
  3.8 1.4 %collective-permute-start.3 = (s32[8]{0:T(128)S(1)}, s32[8]{0:T(128)S(1)}, u32[]{:S(2)}, u32[]{:S(2)}) collective-permute-start(s32[8]{0:T(128)S(1)} %slice.33), channel_id=1, source_target_pairs={{0,8},{8,16},{16,24},{1,9},{9,17},{17,25},{2,10},{10,18},{18,26},{... | collective-permute-start | bytes 104 | tf_op jit(solution)/shard_map/ppermute | solution.py:319
  5.2 1.1 %convolution_bitcast_fusion.refs_3_.refs_4_ = bf16[3584,128]{1,0:T(8,128)(2,1)S(1)} fusion(bf16[2,128]{1,0:T(2,128)(2,1)} %constant.25.clone, bf16[3584,2]{0,1:T(2,128)(2,1)S(1)} %copy-done), kind=kOutput, calls=%fused_computation | convolution fusion | flops 1835008 | bytes 932352 | tf_op jit(solution)/shard_map/dot_general | solution.py:310
  6.4 1.5 %copy-done.1 = bf16[2,3584,128]{2,1,0:T(8,128)(2,1)S(1)} copy-done((bf16[2,3584,128]{2,1,0:T(8,128)(2,1)S(1)}, bf16[2,3584,128]{2,1,0:T(8,128)(2,1)}, u32[]{:S(2)}) %copy-start.1) | copy-done | bytes 1835032
  7.9 1.2 %copy-done.2 = bf16[3584,128]{1,0:T(8,128)(2,1)S(1)} copy-done((bf16[3584,128]{1,0:T(8,128)(2,1)S(1)}, bf16[3584,128]{1,0:T(8,128)(2,1)}, u32[]{:S(2)}) %copy-start.2) | copy-done | bytes 917528
  9.1 1.0 %copy-done.4 = bf16[512,448]{0,1:T(8,128)(2,1)S(1)} copy-done((bf16[512,448]{0,1:T(8,128)(2,1)S(1)}, bf16[512,448]{0,1:T(8,128)(2,1)}, u32[]{:S(2)}) %copy-start.4) | copy-done | bytes 458776
  10.1 0.6 shard_map.127.refs_5_
  10.7 3.1 %collective-permute-done.refs_0_ = bf16[448,512]{1,0:T(8,128)(2,1)} collective-permute-done((bf16[448,512]{1,0:T(8,128)(2,1)}, bf16[448,512]{1,0:T(8,128)(2,1)}, u32[]{:S(2)}, u32[]{:S(2)}) %collective-permute-start) | collective-permute-done | bytes 458784 | tf_op jit(solution)/shard_map/ppermute | solution.py:31
  13.8 1.8 %collective-permute-start.1 = (bf16[448,512]{1,0:T(8,128)(2,1)}, bf16[448,512]{1,0:T(8,128)(2,1)S(1)}, u32[]{:S(2)}, u32[]{:S(2)}) collective-permute-start(bf16[448,512]{1,0:T(8,128)(2,1)} %collective-permute-done.refs_0_), channel_id=1, source_target_pairs={{0,2},{2,4},{4,6},{6,7},{7,5},{5,3},{3,1},{1,0},{8,10},{10,12},{12... | collective-permute-start | bytes 1376264 | tf_op jit(solution)/shard_map/ppermute | solution.py:31
  15.6 0.2 collective-permute-start.5
  15.8 0.6 fusion
  16.4 0.1 slice.36
  16.5 0.1 broadcast_in_dim.27
  16.5 0.1 broadcast_in_dim_reshape.9.bias
  16.6 0.1 broadcast_in_dim.28
  16.7 0.1 broadcast_in_dim_reshape.10.rate
  16.9 0.1 broadcast_in_dim_reshape.11.skip
  16.9 0.1 pad_add_fusion
  17.1 3.1 %shard_map.128.refs_5_ = f32[512,512]{1,0:T(8,128)S(1)} custom-call(bf16[448,512]{1,0:T(8,128)(2,1)} %collective-permute-done.refs_0_, bf16[448,512]{1,0:T(8,128)(2,1)} %collective-permute-done.2.refs_1_, bf16[2,3584,128]{2,1,0:T(8,128)(2,1)} %refs_2_.7, bf16[3584,128]{1,0:T(8,128)(2,1)S(1)} %copy-done.3, ...), custom_call_target="tpu_custom_call" | custom-call | flops 1000000000 | bytes 2097152 | tf_op jit(solution)/shard_map/pallas_call | solution.py:347
  20.2 5.8 %collective-permute-done.1.refs_0_ = bf16[448,512]{1,0:T(8,128)(2,1)S(1)} collective-permute-done((bf16[448,512]{1,0:T(8,128)(2,1)}, bf16[448,512]{1,0:T(8,128)(2,1)S(1)}, u32[]{:S(2)}, u32[]{:S(2)}) %collective-permute-start.1) | collective-permute-done | bytes 458784 | tf_op jit(solution)/shard_map/ppermute | solution.py:31
  25.9 1.6 %collective-permute-start.4 = (bf16[448,512]{1,0:T(8,128)(2,1)S(1)}, bf16[448,512]{1,0:T(8,128)(2,1)S(1)}, u32[]{:S(2)}, u32[]{:S(2)}) collective-permute-start(bf16[448,512]{1,0:T(8,128)(2,1)S(1)} %collective-permute-done.1.refs_0_), channel_id=1, source_target_pairs={{0,2},{2,4},{4,6},{6,7},{7,5},{5,3},{3,1},{1,0},{8,10},{10,12},{12... | collective-permute-start | bytes 1376264 | tf_op jit(solution)/shard_map/ppermute | solution.py:31
  27.5 0.4 collective-permute-start.6
  28.0 0.1 multiply_convert_fusion.rest_0_
  28.1 1.6 %collective-permute-start.10 = (bf16[128,1792]{1,0:T(8,128)(2,1)S(1)}, bf16[128,1792]{1,0:T(8,128)(2,1)}, u32[]{:S(2)}, u32[]{:S(2)}) collective-permute-start(bf16[128,1792]{1,0:T(8,128)(2,1)S(1)} %multiply_convert_fusion.rest_0_), channel_id=1, source_target_pairs={{0,2},{2,4},{4,6},{6,7},{7,5},{5,3},{3,1},{1,0},{8,10},{10,12},{12... | collective-permute-start | bytes 1376264 | tf_op jit(solution)/shard_map/ppermute | solution.py:31
  29.8 0.4 collective-permute-start.11
  30.2 2.9 %shard_map.129.refs_5_ = f32[512,512]{1,0:T(8,128)S(1)} custom-call(bf16[448,512]{1,0:T(8,128)(2,1)S(1)} %collective-permute-done.1.refs_0_, bf16[448,512]{1,0:T(8,128)(2,1)} %collective-permute-done.5.refs_1_, bf16[2,3584,128]{2,1,0:T(8,128)(2,1)} %refs_2_.7, bf16[3584,128]{1,0:T(8,128)(2,1)S(1)} %copy-done.3, ...), custom_call_target="tpu_custom_call" | custom-call | flops 1000000000 | bytes 2097152 | tf_op jit(solution)/shard_map/pallas_call | solution.py:347
  33.1 6.3 %collective-permute-done.4.forth.refs_0_ = bf16[448,512]{1,0:T(8,128)(2,1)S(1)} collective-permute-done((bf16[448,512]{1,0:T(8,128)(2,1)S(1)}, bf16[448,512]{1,0:T(8,128)(2,1)S(1)}, u32[]{:S(2)}, u32[]{:S(2)}) %collective-permute-start.4) | collective-permute-done | bytes 458784 | tf_op jit(solution)/shard_map/ppermute | solution.py:31
  39.4 1.8 %collective-permute-done.6.back.refs_1_ = bf16[448,512]{1,0:T(8,128)(2,1)S(1)} collective-permute-done((bf16[448,512]{1,0:T(8,128)(2,1)}, bf16[448,512]{1,0:T(8,128)(2,1)S(1)}, u32[]{:S(2)}, u32[]{:S(2)}) %collective-permute-start.6) | collective-permute-done | bytes 458784 | tf_op jit(solution)/shard_map/ppermute | solution.py:31
  41.2 1.6 %collective-permute-start.7 = (bf16[224,512]{1,0:T(8,128)(2,1)S(1)}, bf16[224,512]{1,0:T(8,128)(2,1)S(1)}, u32[]{:S(2)}, u32[]{:S(2)}) collective-permute-start(bf16[224,512]{1,0:T(8,128)(2,1)S(1)} %get-tuple-element.48), channel_id=1, source_target_pairs={{0,2},{2,4},{4,6},{6,7},{7,5},{5,3},{3,1},{1,0},{8,10},{10,12},{12... | collective-permute-start | bytes 688136 | tf_op jit(solution)/shard_map/ppermute | solution.py:31
  42.9 0.5 collective-permute-start.8
  43.3 1.9 %shard_map.131 = (f32[512,512]{1,0:T(8,128)S(1)}, bf16[448,512]{1,0:T(8,128)(2,1)S(1)}) custom-call(bf16[448,512]{1,0:T(8,128)(2,1)S(1)} %collective-permute-done.4.forth.refs_0_, bf16[448,512]{1,0:T(8,128)(2,1)S(1)} %collective-permute-done.6.back.refs_1_, bf16[2,3584,128]{2,1,0:T(8,128)(2,1)} %refs_2_.7, bf16[3584,128]{1,0:T(8,128)(2,1)S(1)} %copy-done.3, ...), custom_call_target="tpu_custom_call" | custom-call | flops 1000000000 | bytes 2097152 | tf_op jit(solution)/shard_map/pallas_call | solution.py:347
  45.2 6.6 %collective-permute-done.7.top = bf16[224,512]{1,0:T(8,128)(2,1)S(1)} collective-permute-done((bf16[224,512]{1,0:T(8,128)(2,1)S(1)}, bf16[224,512]{1,0:T(8,128)(2,1)S(1)}, u32[]{:S(2)}, u32[]{:S(2)}) %collective-permute-start.7) | collective-permute-done | bytes 229408 | tf_op jit(solution)/shard_map/ppermute | solution.py:31
  51.8 1.3 %collective-permute-done.8.bottom = bf16[224,512]{1,0:T(8,128)(2,1)S(1)} collective-permute-done((bf16[224,512]{1,0:T(8,128)(2,1)S(1)}, bf16[224,512]{1,0:T(8,128)(2,1)S(1)}, u32[]{:S(2)}, u32[]{:S(2)}) %collective-permute-start.8) | collective-permute-done | bytes 229408 | tf_op jit(solution)/shard_map/ppermute | solution.py:31
  53.1 0.5 shard_map.132.proj
  53.6 1.6 %collective-permute-start.12 = (bf16[128,1792]{1,0:T(8,128)(2,1)}, bf16[128,1792]{1,0:T(8,128)(2,1)S(1)}, u32[]{:S(2)}, u32[]{:S(2)}) collective-permute-start(bf16[128,1792]{1,0:T(8,128)(2,1)} %collective-permute-done.10.rest_1_), channel_id=1, source_target_pairs={{0,2},{2,4},{4,6},{6,7},{7,5},{5,3},{3,1},{1,0},{8,10},{10,12},{12... | collective-permute-start | bytes 1376264 | tf_op jit(solution)/shard_map/ppermute | solution.py:31
  55.2 0.5 collective-permute-start.13
  55.7 1.3 %collective-permute-start.9 = (bf16[8,256]{1,0:T(8,128)(2,1)S(1)}, bf16[8,256]{1,0:T(8,128)(2,1)S(1)}, u32[]{:S(2)}, u32[]{:S(2)}) collective-permute-start(bf16[8,256]{1,0:T(8,128)(2,1)S(1)} %slice.44), channel_id=1, source_target_pairs={{0,8},{8,16},{16,24},{1,9},{9,17},{17,25},{2,10},{10,18},{18,26},{... | collective-permute-start | bytes 12296 | tf_op jit(solution)/shard_map/ppermute | solution.py:361
  57.0 0.1 copy.16.seg_ext
  57.1 0.1 copy.17.seg_ext.seg_ext_a
  57.3 1.0 %shard_map.133 = (f32[256,128]{1,0:T(8,128)S(1)}, f32[256,128]{1,0:T(8,128)S(1)}, f32[256,128]{1,0:T(8,128)S(1)}, f32[72,128]{1,0:T(8,128)S(1)}, f32[256,128]{1,0:T(8,128)S(1)}) custom-call(f32[512,512]{1,0:T(8,128)S(1)} %shard_map.132.proj, s32[264,1]{1,0:T(8,128)S(1)} %copy.16.seg_ext, s32[1,256]{1,0:T(1,128)S(1)} %bitcast.16, f32[4,128]{1,0:T(4,128)S(1)} %copy-done.5, ...), custom_call_target="tpu_custom_call" | custom-call | flops 10000000 | bytes 2097152 | tf_op jit(solution)/shard_map/pallas_call | solution.py:366
  58.3 1.2 %shard_map.134 = (f32[256,128]{1,0:T(8,128)S(1)}, f32[256,128]{1,0:T(8,128)S(1)}, f32[256,128]{1,0:T(8,128)S(1)}, f32[256,128]{1,0:T(8,128)S(1)}, f32[256,128]{1...) custom-call(f32[512,512]{1,0:T(8,128)S(1)} %shard_map.132.proj, ...), custom_call_target="tpu_custom_call" | custom-call | flops 10000000 | bytes 2097152 | tf_op jit(solution)/shard_map/pallas_call | solution.py:371
  59.5 6.8 %all-gather = f32[288,128]{1,0:T(8,128)S(1)} all-gather(f32[72,128]{1,0:T(8,128)S(1)} %get-tuple-element.53), channel_id=2, replica_groups=mesh['seq'=4,'tensor'=8] {'seq'}, dimensions={0}, use_global_device_ids=true | all-gather | bytes 184320 | tf_op jit(solution)/shard_map/all_gather | solution.py:376
  66.4 0.8 shard_map.137
  67.2 1.6 %collective-permute-start.15 = (bf16[80,1792]{1,0:T(8,128)(2,1)}, bf16[80,1792]{1,0:T(8,128)(2,1)S(1)}, u32[]{:S(2)}, u32[]{:S(2)}) collective-permute-start(bf16[80,1792]{1,0:T(8,128)(2,1)} %get-tuple-element.71), channel_id=1, source_target_pairs={{0,2},{2,4},{4,6},{6,7},{7,5},{5,3},{3,1},{1,0},{8,10},{10,12},{12... | collective-permute-start | bytes 860168 | tf_op jit(solution)/shard_map/ppermute | solution.py:31
  68.8 0.4 collective-permute-start.16
  69.2 1.7 %shard_map.135 = bf16[512,128]{1,0:T(8,128)(2,1)} custom-call(s32[1,1]{1,0:T(1,128)} %bitcast.seg_first, f32[4,72,128]{2,1,0:T(8,128)S(1)} %bitcast.11, s32[264,1]{1,0:T(8,128)S(1)} %copy.17.seg_ext.seg_ext_a, s32[1,256]{1,0:T(1,128)S(1)} %bitcast.15, f32[1,128]{1,0:T(1,128)S(1)} %broadcast_in_dim_reshape.11.skip, f32[512,512]{1,0:T(8,128)S(1)} %shard_map.132.proj, ...), custom_call_target="tpu_custom_call" | custom-call | flops 10000000 | bytes 2097152 | tf_op jit(solution)/shard_map/pallas_call | solution.py:377
  70.9 4.8 %all-to-all-start = ((bf16[8,64,128]{2,1,0:T(8,128)(2,1)}), bf16[8,64,128]{2,1,0:T(8,128)(2,1)S(1)}, u32[]{:S(2)}, u32[]{:S(2)}) async-start(bf16[8,64,128]{2,1,0:T(8,128)(2,1)} %bitcast.7), calls=%async_computation | async-start | bytes 262144 | tf_op jit(solution)/shard_map/all_to_all | solution.py:399
  75.7 0.8 collective-permute-done.15.refs_0_
  76.5 1.3 %collective-permute-done.16.refs_1_ = bf16[80,1792]{1,0:T(8,128)(2,1)S(1)} collective-permute-done((bf16[80,1792]{1,0:T(8,128)(2,1)}, bf16[80,1792]{1,0:T(8,128)(2,1)S(1)}, u32[]{:S(2)}, u32[]{:S(2)}) %collective-permute-start.16) | collective-permute-done | bytes 286752 | tf_op jit(solution)/shard_map/ppermute | solution.py:31
  77.8 0.8 shard_map.138
  78.6 1.6 %collective-permute-start.19 = (bf16[64,1792]{1,0:T(8,128)(2,1)S(1)}, bf16[64,1792]{1,0:T(8,128)(2,1)S(1)}, u32[]{:S(2)}, u32[]{:S(2)}) collective-permute-start(bf16[64,1792]{1,0:T(8,128)(2,1)S(1)} %get-tuple-element.75), channel_id=1, source_target_pairs={{0,2},{2,4},{4,6},{6,7},{7,5},{5,3},{3,1},{1,0},{8,10},{10,12},{12... | collective-permute-start | bytes 688136 | tf_op jit(solution)/shard_map/ppermute | solution.py:31
  80.2 0.4 collective-permute-start.20
  80.6 1.8 %collective-permute-start.17 = (bf16[48,1792]{1,0:T(8,128)(2,1)}, bf16[48,1792]{1,0:T(8,128)(2,1)S(1)}, u32[]{:S(2)}, u32[]{:S(2)}) collective-permute-start(bf16[48,1792]{1,0:T(8,128)(2,1)} %get-tuple-element.73), channel_id=1, source_target_pairs={{0,16},{8,24},{16,0},{24,8},{1,17},{9,25},{17,1},{25,9},{2,18},{10... | collective-permute-start | bytes 516104 | tf_op jit(solution)/shard_map/ppermute | solution.py:398
  82.4 0.2 collective-permute-start.18
  82.6 1.4 %all-to-all-done.mine = bf16[8,64,128]{2,1,0:T(8,128)(2,1)S(1)} async-done(((bf16[8,64,128]{2,1,0:T(8,128)(2,1)}), bf16[8,64,128]{2,1,0:T(8,128)(2,1)S(1)}, u32[]{:S(2)}, u32[]{:S(2)}) %all-to-all-start) | async-done | bytes 131104 | tf_op jit(solution)/shard_map/all_to_all | solution.py:399
  84.0 1.3 %collective-permute-done.14.other = bf16[8,64,128]{2,1,0:T(8,128)(2,1)S(1)} collective-permute-done((bf16[8,64,128]{2,1,0:T(8,128)(2,1)S(1)}, bf16[8,64,128]{2,1,0:T(8,128)(2,1)S(1)}, u32[]{:S(2)}, u32[]{:S(2)}) %collective-permute-start.14) | collective-permute-done | bytes 131104 | tf_op jit(solution)/shard_map/ppermute | solution.py:401
  85.3 1.9 %shard_map.136.total = f32[128,1792]{1,0:T(8,128)S(1)} custom-call(bf16[8,64,128]{2,1,0:T(8,128)(2,1)S(1)} %all-to-all-done.mine, bf16[8,64,128]{2,1,0:T(8,128)(2,1)S(1)} %collective-permute-done.14.other, bf16[128,1792]{1,0:T(8,128)(2,1)S(1)} %multiply_convert_fusion.rest_0_, bf16[128,1792]{1,0:T(8,128)(2,1)} %collective-permute-done.10.rest_1_, ...), custom_call_target="tpu_custom_call" | custom-call | flops 1 | bytes 1 | tf_op jit(solution)/shard_map/pallas_call | solution.py:406
  87.3 0.4 collective-permute-done.17.refs_2_
  87.7 1.8 %collective-permute-done.18.refs_3_ = bf16[48,1792]{1,0:T(8,128)(2,1)S(1)} collective-permute-done((bf16[48,1792]{1,0:T(8,128)(2,1)}, bf16[48,1792]{1,0:T(8,128)(2,1)S(1)}, u32[]{:S(2)}, u32[]{:S(2)}) %collective-permute-start.18) | collective-permute-done | bytes 172064 | tf_op jit(solution)/shard_map/ppermute | solution.py:398
  89.5 0.7 shard_map.139
  90.2 0.1 collective-permute-start.21
  90.3 1.5 %collective-permute-done.21 = bf16[64,1792]{1,0:T(8,128)(2,1)S(1)} collective-permute-done((bf16[64,1792]{1,0:T(8,128)(2,1)S(1)}, bf16[64,1792]{1,0:T(8,128)(2,1)S(1)}, u32[]{:S(2)}, u32[]{:S(2)}) %collective-permute-start.21) | collective-permute-done | bytes 229408 | tf_op jit(solution)/shard_map/ppermute | solution.py:413
  91.8 0.8 pad_maximum_fusion
  (43 shorter events, 0.2 us)
Async XLA Ops:
  0.0 5.2 %copy-start = (bf16[3584,2]{0,1:T(2,128)(2,1)S(1)}, bf16[3584,2]{0,1:T(2,128)(2,1)}, u32[]{:S(2)}) copy-start(bf16[3584,2]{0,1:T(2,128)(2,1)} %param.16) | copy-start | bytes 43012
  0.0 13.8 %collective-permute-start = (bf16[448,512]{1,0:T(8,128)(2,1)}, bf16[448,512]{1,0:T(8,128)(2,1)}, u32[]{:S(2)}, u32[]{:S(2)}) collective-permute-start(bf16[448,512]{1,0:T(8,128)(2,1)} %bitcast.12), channel_id=1, source_target_pairs={{0,2},{2,4},{4,6},{6,7},{7,5},{5,3},{3,1},{1,0},{8,10},{10,12},{12... | collective-permute-start | bytes 1376264 | tf_op jit(solution)/shard_map/ppermute | solution.py:31
  3.0 12.6 %collective-permute-start.2 = (bf16[448,512]{1,0:T(8,128)(2,1)}, bf16[448,512]{1,0:T(8,128)(2,1)}, u32[]{:S(2)}, u32[]{:S(2)}) collective-permute-start(bf16[448,512]{1,0:T(8,128)(2,1)} %bitcast.13), channel_id=1, source_target_pairs={{0,1},{2,0},{4,2},{6,4},{7,6},{5,7},{3,5},{1,3},{8,9},{10,8},{12,1... | collective-permute-start | bytes 1376264 | tf_op jit(solution)/shard_map/ppermute | solution.py:31
  3.8 13.2 %collective-permute-start.3 = (s32[8]{0:T(128)S(1)}, s32[8]{0:T(128)S(1)}, u32[]{:S(2)}, u32[]{:S(2)}) collective-permute-start(s32[8]{0:T(128)S(1)} %slice.33), channel_id=1, source_target_pairs={{0,8},{8,16},{16,24},{1,9},{9,17},{17,25},{2,10},{10,18},{18,26},{... | collective-permute-start | bytes 104 | tf_op jit(solution)/shard_map/ppermute | solution.py:319
  6.4 1.5 %copy-start.1 = (bf16[2,3584,128]{2,1,0:T(8,128)(2,1)S(1)}, bf16[2,3584,128]{2,1,0:T(8,128)(2,1)}, u32[]{:S(2)}) copy-start(bf16[2,3584,128]{2,1,0:T(8,128)(2,1)} %refs_2_.7) | copy-start | bytes 5505028
  7.9 1.2 %copy-start.2 = (bf16[3584,128]{1,0:T(8,128)(2,1)S(1)}, bf16[3584,128]{1,0:T(8,128)(2,1)}, u32[]{:S(2)}) copy-start(bf16[3584,128]{1,0:T(8,128)(2,1)} %refs_3_.5) | copy-start | bytes 2752516
  9.1 1.0 %copy-start.4 = (bf16[512,448]{0,1:T(8,128)(2,1)S(1)}, bf16[512,448]{0,1:T(8,128)(2,1)}, u32[]{:S(2)}) copy-start(bf16[512,448]{0,1:T(8,128)(2,1)} %param.13) | copy-start | bytes 1376260
  10.1 5.7 %copy-start.8 = (s32[512]{0:T(512)S(1)}, s32[512]{0:T(512)}, u32[]{:S(2)}) copy-start(s32[512]{0:T(512)} %param.24) | copy-start | bytes 6148
  10.1 6.4 %copy-start.10 = (f32[2]{0:T(128)S(1)}, f32[2]{0:T(128)}, u32[]{:S(2)}) copy-start(f32[2]{0:T(128)} %param.17) | copy-start | bytes 28
  10.1 6.6 %copy-start.11 = (f32[2]{0:T(128)S(1)}, f32[2]{0:T(128)}, u32[]{:S(2)}) copy-start(f32[2]{0:T(128)} %param.18) | copy-start | bytes 28
  10.1 6.7 %copy-start.12 = (f32[2]{0:T(128)S(1)}, f32[2]{0:T(128)}, u32[]{:S(2)}) copy-start(f32[2]{0:T(128)} %param.19) | copy-start | bytes 28
  10.1 7.0 %copy-start.3 = (bf16[3584,128]{1,0:T(8,128)(2,1)S(1)}, bf16[3584,128]{1,0:T(8,128)(2,1)}, u32[]{:S(2)}) copy-start(bf16[3584,128]{1,0:T(8,128)(2,1)} %refs_3_.5) | copy-start | bytes 2752516
  13.8 12.2 %collective-permute-start.1 = (bf16[448,512]{1,0:T(8,128)(2,1)}, bf16[448,512]{1,0:T(8,128)(2,1)S(1)}, u32[]{:S(2)}, u32[]{:S(2)}) collective-permute-start(bf16[448,512]{1,0:T(8,128)(2,1)} %collective-permute-done.refs_0_), channel_id=1, source_target_pairs={{0,2},{2,4},{4,6},{6,7},{7,5},{5,3},{3,1},{1,0},{8,10},{10,12},{12... | collective-permute-start | bytes 1376264 | tf_op jit(solution)/shard_map/ppermute | solution.py:31
  15.6 11.9 %collective-permute-start.5 = (bf16[448,512]{1,0:T(8,128)(2,1)}, bf16[448,512]{1,0:T(8,128)(2,1)}, u32[]{:S(2)}, u32[]{:S(2)}) collective-permute-start(bf16[448,512]{1,0:T(8,128)(2,1)} %collective-permute-done.2.refs_1_), channel_id=1, source_target_pairs={{0,1},{2,0},{4,2},{6,4},{7,6},{5,7},{3,5},{1,3},{8,9},{10,8},{12,1... | collective-permute-start | bytes 1376264 | tf_op jit(solution)/shard_map/ppermute | solution.py:31
  17.0 10.9 %copy-start.7 = (bf16[128,3584]{1,0:T(8,128)(2,1)S(1)}, bf16[128,3584]{1,0:T(8,128)(2,1)}, u32[]{:S(2)}) copy-start(bf16[128,3584]{1,0:T(8,128)(2,1)} %param.23) | copy-start | bytes 2752516
  17.0 10.9 %copy-start.9 = (f32[128]{0:T(128)S(1)}, f32[128]{0:T(128)}, u32[]{:S(2)}) copy-start(f32[128]{0:T(128)} %param.22) | copy-start | bytes 1540
  25.9 13.5 %collective-permute-start.4 = (bf16[448,512]{1,0:T(8,128)(2,1)S(1)}, bf16[448,512]{1,0:T(8,128)(2,1)S(1)}, u32[]{:S(2)}, u32[]{:S(2)}) collective-permute-start(bf16[448,512]{1,0:T(8,128)(2,1)S(1)} %collective-permute-done.1.refs_0_), channel_id=1, source_target_pairs={{0,2},{2,4},{4,6},{6,7},{7,5},{5,3},{3,1},{1,0},{8,10},{10,12},{12... | collective-permute-start | bytes 1376264 | tf_op jit(solution)/shard_map/ppermute | solution.py:31
  27.5 13.7 %collective-permute-start.6 = (bf16[448,512]{1,0:T(8,128)(2,1)}, bf16[448,512]{1,0:T(8,128)(2,1)S(1)}, u32[]{:S(2)}, u32[]{:S(2)}) collective-permute-start(bf16[448,512]{1,0:T(8,128)(2,1)} %collective-permute-done.5.refs_1_), channel_id=1, source_target_pairs={{0,1},{2,0},{4,2},{6,4},{7,6},{5,7},{3,5},{1,3},{8,9},{10,8},{12,1... | collective-permute-start | bytes 1376264 | tf_op jit(solution)/shard_map/ppermute | solution.py:31
  28.1 25.5 %collective-permute-start.10 = (bf16[128,1792]{1,0:T(8,128)(2,1)S(1)}, bf16[128,1792]{1,0:T(8,128)(2,1)}, u32[]{:S(2)}, u32[]{:S(2)}) collective-permute-start(bf16[128,1792]{1,0:T(8,128)(2,1)S(1)} %multiply_convert_fusion.rest_0_), channel_id=1, source_target_pairs={{0,2},{2,4},{4,6},{6,7},{7,5},{5,3},{3,1},{1,0},{8,10},{10,12},{12... | collective-permute-start | bytes 1376264 | tf_op jit(solution)/shard_map/ppermute | solution.py:31
  29.8 23.8 %collective-permute-start.11 = (bf16[128,1792]{1,0:T(8,128)(2,1)S(1)}, bf16[128,1792]{1,0:T(8,128)(2,1)}, u32[]{:S(2)}, u32[]{:S(2)}) collective-permute-start(bf16[128,1792]{1,0:T(8,128)(2,1)S(1)} %multiply_convert_fusion.rest_0_), channel_id=1, source_target_pairs={{0,1},{2,0},{4,2},{6,4},{7,6},{5,7},{3,5},{1,3},{8,9},{10,8},{12,1... | collective-permute-start | bytes 1376264 | tf_op jit(solution)/shard_map/ppermute | solution.py:31
  41.2 10.6 %collective-permute-start.7 = (bf16[224,512]{1,0:T(8,128)(2,1)S(1)}, bf16[224,512]{1,0:T(8,128)(2,1)S(1)}, u32[]{:S(2)}, u32[]{:S(2)}) collective-permute-start(bf16[224,512]{1,0:T(8,128)(2,1)S(1)} %get-tuple-element.48), channel_id=1, source_target_pairs={{0,2},{2,4},{4,6},{6,7},{7,5},{5,3},{3,1},{1,0},{8,10},{10,12},{12... | collective-permute-start | bytes 688136 | tf_op jit(solution)/shard_map/ppermute | solution.py:31
  42.9 10.2 %collective-permute-start.8 = (bf16[224,512]{1,0:T(8,128)(2,1)S(1)}, bf16[224,512]{1,0:T(8,128)(2,1)S(1)}, u32[]{:S(2)}, u32[]{:S(2)}) collective-permute-start(bf16[224,512]{1,0:T(8,128)(2,1)S(1)} %get-tuple-element.49), channel_id=1, source_target_pairs={{0,1},{2,0},{4,2},{6,4},{7,6},{5,7},{3,5},{1,3},{8,9},{10,8},{12,1... | collective-permute-start | bytes 688136 | tf_op jit(solution)/shard_map/ppermute | solution.py:31
  53.1 4.2 %copy-start.5 = (f32[4,128]{1,0:T(4,128)S(1)}, f32[4,128]{1,0:T(4,128)}, u32[]{:S(2)}) copy-start(f32[4,128]{1,0:T(4,128)} %taps_x.3) | copy-start | bytes 6148
  53.1 4.2 %copy-start.6 = (f32[4,128]{1,0:T(4,128)S(1)}, f32[4,128]{1,0:T(4,128)}, u32[]{:S(2)}) copy-start(f32[4,128]{1,0:T(4,128)} %taps_bc.3) | copy-start | bytes 6148
  53.6 12.7 %collective-permute-start.12 = (bf16[128,1792]{1,0:T(8,128)(2,1)}, bf16[128,1792]{1,0:T(8,128)(2,1)S(1)}, u32[]{:S(2)}, u32[]{:S(2)}) collective-permute-start(bf16[128,1792]{1,0:T(8,128)(2,1)} %collective-permute-done.10.rest_1_), channel_id=1, source_target_pairs={{0,2},{2,4},{4,6},{6,7},{7,5},{5,3},{3,1},{1,0},{8,10},{10,12},{12... | collective-permute-start | bytes 1376264 | tf_op jit(solution)/shard_map/ppermute | solution.py:31
  55.2 11.1 %collective-permute-start.13 = (bf16[128,1792]{1,0:T(8,128)(2,1)}, bf16[128,1792]{1,0:T(8,128)(2,1)S(1)}, u32[]{:S(2)}, u32[]{:S(2)}) collective-permute-start(bf16[128,1792]{1,0:T(8,128)(2,1)} %collective-permute-done.11.rest_2_), channel_id=1, source_target_pairs={{0,1},{2,0},{4,2},{6,4},{7,6},{5,7},{3,5},{1,3},{8,9},{10,8},{12,1... | collective-permute-start | bytes 1376264 | tf_op jit(solution)/shard_map/ppermute | solution.py:31
  55.7 2.6 %collective-permute-start.9 = (bf16[8,256]{1,0:T(8,128)(2,1)S(1)}, bf16[8,256]{1,0:T(8,128)(2,1)S(1)}, u32[]{:S(2)}, u32[]{:S(2)}) collective-permute-start(bf16[8,256]{1,0:T(8,128)(2,1)S(1)} %slice.44), channel_id=1, source_target_pairs={{0,8},{8,16},{16,24},{1,9},{9,17},{17,25},{2,10},{10,18},{18,26},{... | collective-permute-start | bytes 12296 | tf_op jit(solution)/shard_map/ppermute | solution.py:361
  67.2 9.3 %collective-permute-start.15 = (bf16[80,1792]{1,0:T(8,128)(2,1)}, bf16[80,1792]{1,0:T(8,128)(2,1)S(1)}, u32[]{:S(2)}, u32[]{:S(2)}) collective-permute-start(bf16[80,1792]{1,0:T(8,128)(2,1)} %get-tuple-element.71), channel_id=1, source_target_pairs={{0,2},{2,4},{4,6},{6,7},{7,5},{5,3},{3,1},{1,0},{8,10},{10,12},{12... | collective-permute-start | bytes 860168 | tf_op jit(solution)/shard_map/ppermute | solution.py:31
  68.8 9.0 %collective-permute-start.16 = (bf16[80,1792]{1,0:T(8,128)(2,1)}, bf16[80,1792]{1,0:T(8,128)(2,1)S(1)}, u32[]{:S(2)}, u32[]{:S(2)}) collective-permute-start(bf16[80,1792]{1,0:T(8,128)(2,1)} %get-tuple-element.72), channel_id=1, source_target_pairs={{0,1},{2,0},{4,2},{6,4},{7,6},{5,7},{3,5},{1,3},{8,9},{10,8},{12,1... | collective-permute-start | bytes 860168 | tf_op jit(solution)/shard_map/ppermute | solution.py:31
  70.9 13.1 %all-to-all-start = ((bf16[8,64,128]{2,1,0:T(8,128)(2,1)}), bf16[8,64,128]{2,1,0:T(8,128)(2,1)S(1)}, u32[]{:S(2)}, u32[]{:S(2)}) async-start(bf16[8,64,128]{2,1,0:T(8,128)(2,1)} %bitcast.7), calls=%async_computation | async-start | bytes 262144 | tf_op jit(solution)/shard_map/all_to_all | solution.py:399
  78.6 11.0 %collective-permute-start.19 = (bf16[64,1792]{1,0:T(8,128)(2,1)S(1)}, bf16[64,1792]{1,0:T(8,128)(2,1)S(1)}, u32[]{:S(2)}, u32[]{:S(2)}) collective-permute-start(bf16[64,1792]{1,0:T(8,128)(2,1)S(1)} %get-tuple-element.75), channel_id=1, source_target_pairs={{0,2},{2,4},{4,6},{6,7},{7,5},{5,3},{3,1},{1,0},{8,10},{10,12},{12... | collective-permute-start | bytes 688136 | tf_op jit(solution)/shard_map/ppermute | solution.py:31
  80.2 9.4 %collective-permute-start.20 = (bf16[64,1792]{1,0:T(8,128)(2,1)S(1)}, bf16[64,1792]{1,0:T(8,128)(2,1)S(1)}, u32[]{:S(2)}, u32[]{:S(2)}) collective-permute-start(bf16[64,1792]{1,0:T(8,128)(2,1)S(1)} %get-tuple-element.76), channel_id=1, source_target_pairs={{0,1},{2,0},{4,2},{6,4},{7,6},{5,7},{3,5},{1,3},{8,9},{10,8},{12,1... | collective-permute-start | bytes 688136 | tf_op jit(solution)/shard_map/ppermute | solution.py:31
  80.6 7.1 %collective-permute-start.17 = (bf16[48,1792]{1,0:T(8,128)(2,1)}, bf16[48,1792]{1,0:T(8,128)(2,1)S(1)}, u32[]{:S(2)}, u32[]{:S(2)}) collective-permute-start(bf16[48,1792]{1,0:T(8,128)(2,1)} %get-tuple-element.73), channel_id=1, source_target_pairs={{0,16},{8,24},{16,0},{24,8},{1,17},{9,25},{17,1},{25,9},{2,18},{10... | collective-permute-start | bytes 516104 | tf_op jit(solution)/shard_map/ppermute | solution.py:398
  82.4 7.1 %collective-permute-start.18 = (bf16[48,1792]{1,0:T(8,128)(2,1)}, bf16[48,1792]{1,0:T(8,128)(2,1)S(1)}, u32[]{:S(2)}, u32[]{:S(2)}) collective-permute-start(bf16[48,1792]{1,0:T(8,128)(2,1)} %get-tuple-element.74), channel_id=1, source_target_pairs={{0,16},{8,24},{16,0},{24,8},{1,17},{9,25},{17,1},{25,9},{2,18},{10... | collective-permute-start | bytes 516104 | tf_op jit(solution)/shard_map/ppermute | solution.py:398
  84.0 1.3 %collective-permute-start.14 = (bf16[8,64,128]{2,1,0:T(8,128)(2,1)S(1)}, bf16[8,64,128]{2,1,0:T(8,128)(2,1)S(1)}, u32[]{:S(2)}, u32[]{:S(2)}) collective-permute-start(bf16[8,64,128]{2,1,0:T(8,128)(2,1)S(1)} %all-to-all-done.mine), channel_id=1, source_target_pairs={{0,8},{8,0},{16,24},{24,16},{1,9},{9,1},{17,25},{25,17},{2,10},{10... | collective-permute-start | bytes 393224 | tf_op jit(solution)/shard_map/ppermute | solution.py:401
  90.2 1.6 %collective-permute-start.21 = (bf16[64,1792]{1,0:T(8,128)(2,1)S(1)}, bf16[64,1792]{1,0:T(8,128)(2,1)S(1)}, u32[]{:S(2)}, u32[]{:S(2)}) collective-permute-start(bf16[64,1792]{1,0:T(8,128)(2,1)S(1)} %get-tuple-element.78), channel_id=1, source_target_pairs={{0,8},{8,0},{16,24},{24,16},{1,9},{9,1},{17,25},{25,17},{2,10},{10... | collective-permute-start | bytes 688136 | tf_op jit(solution)/shard_map/ppermute | solution.py:413

commit v15 on v13

--- a/solution.py
+++ b/solution.py
@@ -14,7 +14,6 @@
 VMEM = pl.BlockSpec(memory_space=pltpu.VMEM)
 ANY = pl.BlockSpec(memory_space=pl.ANY)
 HALO = 8
-W_FIRST = 3
 
 
 def ring_place(index, n):
@@ -311,11 +310,12 @@
             forth, back = ring_shift(forth, 1), ring_shift(back, -1)
         else:
             far = far_shift(forth, back)
-        if step == W_FIRST:
-            w_forth, w_back = after((own, own), arrivals)
-            w_forth, w_back = ring_shift(w_forth, 1), ring_shift(w_back, -1)
+        if step == 1:
+            w_forth, w_back = ring_shift(own, 1), ring_shift(own, -1)
         ahead = last if step == last else 0
         total = projs[-1:]
+        if step == 2:
+            total = [after(projs[-1], w_forth, w_back)]
         fetched = len(arrived) + bool(ahead)
         outs = [shape(tok_rows, 4 * width)] + [shape(feat, 4 * width, kind=BF16)] * bool(ahead)
         results = call(

time: 92.5 us -> 96.9 us (1.048)
  local copies, waits for them, and re-layouts: 5.9 us -> 7.78 us
  other arithmetic: 1.05 us -> 2.09 us
    unnamed x26 -> x28, local copies, waits for them, and re-layouts: 3.73 us -> 5.61 us
    ppermute x16, waiting for transfers between devices: 32.3 us -> 33.7 us  [ring_shift(): lax.ppermute(block, 'tensor', [(order[i], order[(i + step) % n]) for i in...]
    ppermute x16, starting transfers between devices: 17.5 us -> 18.7 us  [ring_shift(): lax.ppermute(block, 'tensor', [(order[i], order[(i + step) % n]) for i in...]
    all_to_all x1, waiting for transfers between devices: 1.17 us -> 0.01 us  [local(): mine = lax.all_to_all(blocks, 'tensor', 0, 0)]
    pallas_call x4, Pallas kernels: 8.46 us -> 7.36 us  [local(): call(functools.partial(project, [distance for distance, _ in arrived], ah...]
    convert_element_type x1, other arithmetic: 0.14 us -> 1.18 us  [local(): (lax.dynamic_slice_in_dim(w_out, core * columns, columns, 1).astype(F32)...]
    all_to_all x1, starting transfers between devices: 4.8 us -> 3.78 us  [local(): mine = lax.all_to_all(blocks, 'tensor', 0, 0)]
  transfers between devices with their start and end apart: 21 -> 21, of which waited for: 12 -> 14; matrix products, arithmetic and copies ran while one was open for 4% -> 5% of each run, Pallas kernels for 16% -> 15%
where the time goes in v15:
time: 96.9 us; the launch traced here: 96.3 us
  waiting for transfers between devices  36.5 us (38%)
  starting transfers between devices  25.1 us (26%)
  Pallas kernels  16 us (17%)
  local copies, waits for them, and re-layouts  7.78 us (8%)
  blocking collectives  7.47 us (8%)
  other arithmetic  2.09 us (2%)
  matrix products  1.12 us (1%)
    ppermute x16, waiting for transfers between devices, ring_shift(): lax.ppermute(block, 'tensor', [(order[i], order[(i + step) % n]) for i in...  33.7 us
    ppermute x16, starting transfers between devices, ring_shift(): lax.ppermute(block, 'tensor', [(order[i], order[(i + step) % n]) for i in...  18.7 us
    all_gather x1, blocking collectives, local(): messages = lax.all_gather(message, 'seq')  7.47 us
    pallas_call x4, Pallas kernels, local(): call(functools.partial(project, [distance for distance, _ in arrived], ah...  7.36 us
    unnamed x28, local copies, waits for them, and re-layouts  5.61 us
    all_to_all x1, starting transfers between devices, local(): mine = lax.all_to_all(blocks, 'tensor', 0, 0)  3.78 us
    pallas_call x1, Pallas kernels, local(): call(functools.partial(product_early, distances), shape(2 * tok_own, colu...  2.15 us
  transfers between devices with their start and end apart: 21, of which 14 were waited for; matrix products, arithmetic and copies ran while one was open for 5% of the time, Pallas kernels for 15%

profile of v15, /device:TPU:0, one launch (start us, length us, event | category | flops | bytes accessed | tf_op | source)
XLA Modules:
  0.0 96.3 jit_solution(12613820672842856612)
XLA Ops:
  0.0 3.0 %collective-permute-start = (bf16[448,512]{1,0:T(8,128)(2,1)}, bf16[448,512]{1,0:T(8,128)(2,1)}, u32[]{:S(2)}, u32[]{:S(2)}) collective-permute-start(bf16[448,512]{1,0:T(8,128)(2,1)} %bitcast.12), channel_id=1, source_target_pairs={{0,2},{2,4},{4,6},{6,7},{7,5},{5,3},{3,1},{1,0},{8,10},{10,12},{12... | collective-permute-start | bytes 1376264 | tf_op jit(solution)/shard_map/ppermute | solution.py:30
  3.0 1.2 %multiply_convert_fusion.rest_0_ = bf16[128,1792]{1,0:T(8,128)(2,1)S(1)} fusion(f32[128]{0:T(128)} %param.22, bf16[128,3584]{1,0:T(8,128)(2,1)} %param.23, s32[]{:T(128)S(6)} %select_n.24), kind=kLoop, calls=%fused_computation.1 | loop fusion | flops 688128 | bytes 918020 | tf_op jit(solution)/shard_map/convert_element_type | solution.py:287
  4.2 2.1 %collective-permute-start.3 = (bf16[128,1792]{1,0:T(8,128)(2,1)S(1)}, bf16[128,1792]{1,0:T(8,128)(2,1)}, u32[]{:S(2)}, u32[]{:S(2)}) collective-permute-start(bf16[128,1792]{1,0:T(8,128)(2,1)S(1)} %multiply_convert_fusion.rest_0_), channel_id=1, source_target_pairs={{0,2},{2,4},{4,6},{6,7},{7,5},{5,3},{3,1},{1,0},{8,10},{10,12},{12... | collective-permute-start | bytes 1376264 | tf_op jit(solution)/shard_map/ppermute | solution.py:30
  6.3 0.8 slice.33
  7.0 1.3 %collective-permute-start.5 = (s32[8]{0:T(128)S(1)}, s32[8]{0:T(128)S(1)}, u32[]{:S(2)}, u32[]{:S(2)}) collective-permute-start(s32[8]{0:T(128)S(1)} %slice.33), channel_id=1, source_target_pairs={{0,8},{8,16},{16,24},{1,9},{9,17},{17,25},{2,10},{10,18},{18,26},{... | collective-permute-start | bytes 104 | tf_op jit(solution)/shard_map/ppermute | solution.py:292
  8.3 1.1 %convolution_bitcast_fusion.refs_3_.refs_4_ = bf16[3584,128]{1,0:T(8,128)(2,1)S(1)} fusion(bf16[2,128]{1,0:T(2,128)(2,1)} %constant.25.clone, bf16[3584,2]{0,1:T(2,128)(2,1)S(1)} %copy-done), kind=kOutput, calls=%fused_computation | convolution fusion | flops 1835008 | bytes 932352 | tf_op jit(solution)/shard_map/dot_general | solution.py:283
  9.5 0.0 copy-start.2
  9.5 1.2 %copy-done.2 = bf16[3584,128]{1,0:T(8,128)(2,1)S(1)} copy-done((bf16[3584,128]{1,0:T(8,128)(2,1)S(1)}, bf16[3584,128]{1,0:T(8,128)(2,1)}, u32[]{:S(2)}) %copy-start.2) | copy-done | bytes 917528
  10.7 1.0 %copy-done.7 = bf16[512,448]{0,1:T(8,128)(2,1)S(1)} copy-done((bf16[512,448]{0,1:T(8,128)(2,1)S(1)}, bf16[512,448]{0,1:T(8,128)(2,1)}, u32[]{:S(2)}) %copy-start.7) | copy-done | bytes 458776
  11.7 0.6 shard_map.127.refs_5_
  12.3 1.0 %copy-done.5 = f32[512,512]{1,0:T(8,128)} copy-done((f32[512,512]{1,0:T(8,128)}, f32[512,512]{1,0:T(8,128)S(1)}, u32[]{:S(2)}) %copy-start.5) | copy-done | bytes 1048600
  13.3 1.3 %collective-permute-done.refs_0_ = bf16[448,512]{1,0:T(8,128)(2,1)} collective-permute-done((bf16[448,512]{1,0:T(8,128)(2,1)}, bf16[448,512]{1,0:T(8,128)(2,1)}, u32[]{:S(2)}, u32[]{:S(2)}) %collective-permute-start) | collective-permute-done | bytes 458784 | tf_op jit(solution)/shard_map/ppermute | solution.py:30
  14.6 2.1 %collective-permute-start.1 = (bf16[448,512]{1,0:T(8,128)(2,1)}, bf16[448,512]{1,0:T(8,128)(2,1)S(1)}, u32[]{:S(2)}, u32[]{:S(2)}) collective-permute-start(bf16[448,512]{1,0:T(8,128)(2,1)} %collective-permute-done.refs_0_), channel_id=1, source_target_pairs={{0,2},{2,4},{4,6},{6,7},{7,5},{5,3},{3,1},{1,0},{8,10},{10,12},{12... | collective-permute-start | bytes 1376264 | tf_op jit(solution)/shard_map/ppermute | solution.py:30
  16.8 0.0 collective-permute-done.2.refs_1_
  16.8 0.6 fusion
  17.4 0.1 slice.36
  17.5 0.1 broadcast_in_dim.27
  17.5 0.1 broadcast_in_dim_reshape.9.bias
  17.6 0.1 broadcast_in_dim.28
  17.7 0.1 broadcast_in_dim_reshape.10.rate
  17.8 0.1 broadcast_in_dim.29
  17.8 0.1 broadcast_in_dim_reshape.11.skip
  17.9 0.1 pad_add_fusion
  18.0 6.4 %collective-permute-done.3.rest_1_ = bf16[128,1792]{1,0:T(8,128)(2,1)} collective-permute-done((bf16[128,1792]{1,0:T(8,128)(2,1)S(1)}, bf16[128,1792]{1,0:T(8,128)(2,1)}, u32[]{:S(2)}, u32[]{:S(2)}) %collective-permute-start.3) | collective-permute-done | bytes 458784 | tf_op jit(solution)/shard_map/ppermute | solution.py:30
  24.4 2.2 %collective-permute-done.4.rest_2_ = bf16[128,1792]{1,0:T(8,128)(2,1)} collective-permute-done((bf16[128,1792]{1,0:T(8,128)(2,1)S(1)}, bf16[128,1792]{1,0:T(8,128)(2,1)}, u32[]{:S(2)}, u32[]{:S(2)}) %collective-permute-start.4) | collective-permute-done | bytes 458784 | tf_op jit(solution)/shard_map/ppermute | solution.py:30
  26.6 1.2 %copy-done.3 = bf16[3584,128]{1,0:T(8,128)(2,1)S(1)} copy-done((bf16[3584,128]{1,0:T(8,128)(2,1)S(1)}, bf16[3584,128]{1,0:T(8,128)(2,1)}, u32[]{:S(2)}) %copy-start.3) | copy-done | bytes 917528
  27.8 1.2 %copy-done.6 = f32[512,512]{1,0:T(8,128)S(1)} copy-done((f32[512,512]{1,0:T(8,128)S(1)}, f32[512,512]{1,0:T(8,128)}, u32[]{:S(2)}) %copy-start.6) | copy-done | bytes 1048600
  29.0 3.0 %shard_map.128.refs_5_ = f32[512,512]{1,0:T(8,128)S(1)} custom-call(bf16[448,512]{1,0:T(8,128)(2,1)} %collective-permute-done.refs_0_, bf16[448,512]{1,0:T(8,128)(2,1)} %collective-permute-done.2.refs_1_, bf16[2,3584,128]{2,1,0:T(8,128)(2,1)} %refs_2_.7, bf16[3584,128]{1,0:T(8,128)(2,1)S(1)} %copy-done.3, ...), custom_call_target="tpu_custom_call" | custom-call | flops 1000000000 | bytes 2097152 | tf_op jit(solution)/shard_map/pallas_call | solution.py:321
  32.0 1.3 %collective-permute-done.1.refs_0_ = bf16[448,512]{1,0:T(8,128)(2,1)S(1)} collective-permute-done((bf16[448,512]{1,0:T(8,128)(2,1)}, bf16[448,512]{1,0:T(8,128)(2,1)S(1)}, u32[]{:S(2)}, u32[]{:S(2)}) %collective-permute-start.1) | collective-permute-done | bytes 458784 | tf_op jit(solution)/shard_map/ppermute | solution.py:30
  33.3 1.8 %collective-permute-start.6 = (bf16[448,512]{1,0:T(8,128)(2,1)S(1)}, bf16[448,512]{1,0:T(8,128)(2,1)S(1)}, u32[]{:S(2)}, u32[]{:S(2)}) collective-permute-start(bf16[448,512]{1,0:T(8,128)(2,1)S(1)} %collective-permute-done.1.refs_0_), channel_id=1, source_target_pairs={{0,2},{2,4},{4,6},{6,7},{7,5},{5,3},{3,1},{1,0},{8,10},{10,12},{12... | collective-permute-start | bytes 1376264 | tf_op jit(solution)/shard_map/ppermute | solution.py:30
  35.2 0.2 collective-permute-start.8
  35.4 1.8 %shard_map.129.refs_5_ = f32[512,512]{1,0:T(8,128)S(1)} custom-call(bf16[448,512]{1,0:T(8,128)(2,1)S(1)} %collective-permute-done.1.refs_0_, bf16[448,512]{1,0:T(8,128)(2,1)S(1)} %collective-permute-done.7.refs_1_, bf16[2,3584,128]{2,1,0:T(8,128)(2,1)} %refs_2_.7, bf16[3584,128]{1,0:T(8,128)(2,1)S(1)} %copy-done.3, ...), custom_call_target="tpu_custom_call" | custom-call | flops 1000000000 | bytes 2097152 | tf_op jit(solution)/shard_map/pallas_call | solution.py:321
  37.2 7.8 %collective-permute-done.6.forth.refs_0_ = bf16[448,512]{1,0:T(8,128)(2,1)S(1)} collective-permute-done((bf16[448,512]{1,0:T(8,128)(2,1)S(1)}, bf16[448,512]{1,0:T(8,128)(2,1)S(1)}, u32[]{:S(2)}, u32[]{:S(2)}) %collective-permute-start.6) | collective-permute-done | bytes 458784 | tf_op jit(solution)/shard_map/ppermute | solution.py:30
  45.0 1.2 %collective-permute-done.8.back.refs_1_ = bf16[448,512]{1,0:T(8,128)(2,1)S(1)} collective-permute-done((bf16[448,512]{1,0:T(8,128)(2,1)S(1)}, bf16[448,512]{1,0:T(8,128)(2,1)S(1)}, u32[]{:S(2)}, u32[]{:S(2)}) %collective-permute-start.8) | collective-permute-done | bytes 458784 | tf_op jit(solution)/shard_map/ppermute | solution.py:30
  46.3 1.6 %collective-permute-start.9 = (bf16[224,512]{1,0:T(8,128)(2,1)S(1)}, bf16[224,512]{1,0:T(8,128)(2,1)S(1)}, u32[]{:S(2)}, u32[]{:S(2)}) collective-permute-start(bf16[224,512]{1,0:T(8,128)(2,1)S(1)} %get-tuple-element.44), channel_id=1, source_target_pairs={{0,2},{2,4},{4,6},{6,7},{7,5},{5,3},{3,1},{1,0},{8,10},{10,12},{12... | collective-permute-start | bytes 688136 | tf_op jit(solution)/shard_map/ppermute | solution.py:30
  47.9 0.4 collective-permute-start.10
  48.4 1.9 %shard_map.131 = (f32[512,512]{1,0:T(8,128)S(1)}, bf16[448,512]{1,0:T(8,128)(2,1)S(1)}) custom-call(bf16[448,512]{1,0:T(8,128)(2,1)S(1)} %collective-permute-done.6.forth.refs_0_, bf16[448,512]{1,0:T(8,128)(2,1)S(1)} %collective-permute-done.8.back.refs_1_, bf16[2,3584,128]{2,1,0:T(8,128)(2,1)} %refs_2_.7, bf16[3584,128]{1,0:T(8,128)(2,1)S(1)} %copy-done.4, ...), custom_call_target="tpu_custom_call" | custom-call | flops 1000000000 | bytes 2097152 | tf_op jit(solution)/shard_map/pallas_call | solution.py:321
  50.3 2.1 %collective-permute-done.9.top = bf16[224,512]{1,0:T(8,128)(2,1)S(1)} collective-permute-done((bf16[224,512]{1,0:T(8,128)(2,1)S(1)}, bf16[224,512]{1,0:T(8,128)(2,1)S(1)}, u32[]{:S(2)}, u32[]{:S(2)}) %collective-permute-start.9) | collective-permute-done | bytes 229408 | tf_op jit(solution)/shard_map/ppermute | solution.py:30
  52.4 1.6 %collective-permute-done.10.bottom = bf16[224,512]{1,0:T(8,128)(2,1)S(1)} collective-permute-done((bf16[224,512]{1,0:T(8,128)(2,1)S(1)}, bf16[224,512]{1,0:T(8,128)(2,1)S(1)}, u32[]{:S(2)}, u32[]{:S(2)}) %collective-permute-start.10) | collective-permute-done | bytes 229408 | tf_op jit(solution)/shard_map/ppermute | solution.py:30
  54.0 0.5 shard_map.132.proj
  54.4 1.6 %collective-permute-start.12 = (bf16[128,1792]{1,0:T(8,128)(2,1)}, bf16[128,1792]{1,0:T(8,128)(2,1)S(1)}, u32[]{:S(2)}, u32[]{:S(2)}) collective-permute-start(bf16[128,1792]{1,0:T(8,128)(2,1)} %collective-permute-done.3.rest_1_), channel_id=1, source_target_pairs={{0,2},{2,4},{4,6},{6,7},{7,5},{5,3},{3,1},{1,0},{8,10},{10,12},{12... | collective-permute-start | bytes 1376264 | tf_op jit(solution)/shard_map/ppermute | solution.py:30
  56.1 0.5 collective-permute-start.13
  56.5 1.3 %collective-permute-start.11 = (bf16[8,256]{1,0:T(8,128)(2,1)S(1)}, bf16[8,256]{1,0:T(8,128)(2,1)S(1)}, u32[]{:S(2)}, u32[]{:S(2)}) collective-permute-start(bf16[8,256]{1,0:T(8,128)(2,1)S(1)} %slice.44), channel_id=1, source_target_pairs={{0,8},{8,16},{16,24},{1,9},{9,17},{17,25},{2,10},{10,18},{18,26},{... | collective-permute-start | bytes 12296 | tf_op jit(solution)/shard_map/ppermute | solution.py:335
  57.8 0.1 copy.16.seg_ext
  58.0 0.1 copy.17.seg_ext.seg_ext_a
  58.1 1.0 %shard_map.133 = (f32[256,128]{1,0:T(8,128)S(1)}, f32[256,128]{1,0:T(8,128)S(1)}, f32[256,128]{1,0:T(8,128)S(1)}, f32[72,128]{1,0:T(8,128)S(1)}, f32[256,128]{1,0:T(8,128)S(1)}) custom-call(f32[512,512]{1,0:T(8,128)S(1)} %shard_map.132.proj, s32[264,1]{1,0:T(8,128)S(1)} %copy.16.seg_ext, s32[1,256]{1,0:T(1,128)S(1)} %bitcast.16, f32[4,128]{1,0:T(4,128)S(1)} %copy-done.8, ...), custom_call_target="tpu_custom_call" | custom-call | flops 10000000 | bytes 2097152 | tf_op jit(solution)/shard_map/pallas_call | solution.py:340
  59.1 1.2 %shard_map.134 = (f32[256,128]{1,0:T(8,128)S(1)}, f32[256,128]{1,0:T(8,128)S(1)}, f32[256,128]{1,0:T(8,128)S(1)}, f32[256,128]{1,0:T(8,128)S(1)}, f32[256,128]{1...) custom-call(f32[512,512]{1,0:T(8,128)S(1)} %shard_map.132.proj, ...), custom_call_target="tpu_custom_call" | custom-call | flops 10000000 | bytes 2097152 | tf_op jit(solution)/shard_map/pallas_call | solution.py:345
  60.4 7.5 %all-gather = f32[288,128]{1,0:T(8,128)S(1)} all-gather(f32[72,128]{1,0:T(8,128)S(1)} %get-tuple-element.49), channel_id=2, replica_groups=mesh['seq'=4,'tensor'=8] {'seq'}, dimensions={0}, use_global_device_ids=true | all-gather | bytes 184320 | tf_op jit(solution)/shard_map/all_gather | solution.py:350
  67.8 1.6 %collective-permute-start.15 = (bf16[128,1792]{1,0:T(8,128)(2,1)S(1)}, bf16[128,1792]{1,0:T(8,128)(2,1)S(1)}, u32[]{:S(2)}, u32[]{:S(2)}) collective-permute-start(bf16[128,1792]{1,0:T(8,128)(2,1)S(1)} %collective-permute-done.12.rest_3_), channel_id=1, source_target_pairs={{0,2},{2,4},{4,6},{6,7},{7,5},{5,3},{3,1},{1,0},{8,10},{10,12},{12... | collective-permute-start | bytes 1376264 | tf_op jit(solution)/shard_map/ppermute | solution.py:30
  69.4 0.4 collective-permute-start.16
  69.9 1.8 %shard_map.135 = bf16[512,128]{1,0:T(8,128)(2,1)} custom-call(s32[1,1]{1,0:T(1,128)} %bitcast.seg_first, f32[4,72,128]{2,1,0:T(8,128)S(1)} %bitcast.11, s32[264,1]{1,0:T(8,128)S(1)} %copy.17.seg_ext.seg_ext_a, s32[1,256]{1,0:T(1,128)S(1)} %bitcast.15, f32[1,128]{1,0:T(1,128)S(1)} %broadcast_in_dim_reshape.11.skip, f32[512,512]{1,0:T(8,128)S(1)} %shard_map.132.proj, ...), custom_call_target="tpu_custom_call" | custom-call | flops 10000000 | bytes 2097152 | tf_op jit(solution)/shard_map/pallas_call | solution.py:351
  71.7 3.8 %all-to-all-start = ((bf16[8,64,128]{2,1,0:T(8,128)(2,1)}), bf16[8,64,128]{2,1,0:T(8,128)(2,1)S(1)}, u32[]{:S(2)}, u32[]{:S(2)}) async-start(bf16[8,64,128]{2,1,0:T(8,128)(2,1)} %bitcast.7), calls=%async_computation | async-start | bytes 262144 | tf_op jit(solution)/shard_map/all_to_all | solution.py:369
  75.4 5.7 %collective-permute-done.15.rest_5_.forth = bf16[128,1792]{1,0:T(8,128)(2,1)S(1)} collective-permute-done((bf16[128,1792]{1,0:T(8,128)(2,1)S(1)}, bf16[128,1792]{1,0:T(8,128)(2,1)S(1)}, u32[]{:S(2)}, u32[]{:S(2)}) %collective-permute-start.15) | collective-permute-done | bytes 458784 | tf_op jit(solution)/shard_map/ppermute | solution.py:30
  81.2 1.2 %collective-permute-done.16.rest_6_.back = bf16[128,1792]{1,0:T(8,128)(2,1)S(1)} collective-permute-done((bf16[128,1792]{1,0:T(8,128)(2,1)S(1)}, bf16[128,1792]{1,0:T(8,128)(2,1)S(1)}, u32[]{:S(2)}, u32[]{:S(2)}) %collective-permute-start.16) | collective-permute-done | bytes 458784 | tf_op jit(solution)/shard_map/ppermute | solution.py:30
  82.3 0.8 shard_map.137
  83.1 3.2 %collective-permute-start.17 = (bf16[64,1792]{1,0:T(8,128)(2,1)}, bf16[64,1792]{1,0:T(8,128)(2,1)S(1)}, u32[]{:S(2)}, u32[]{:S(2)}) collective-permute-start(bf16[64,1792]{1,0:T(8,128)(2,1)} %get-tuple-element.65), channel_id=1, source_target_pairs={{0,2},{2,4},{4,6},{6,7},{7,5},{5,3},{3,1},{1,0},{8,10},{10,12},{12... | collective-permute-start | bytes 688136 | tf_op jit(solution)/shard_map/ppermute | solution.py:30
  86.4 1.3 %collective-permute-done.14.other = bf16[8,64,128]{2,1,0:T(8,128)(2,1)S(1)} collective-permute-done((bf16[8,64,128]{2,1,0:T(8,128)(2,1)S(1)}, bf16[8,64,128]{2,1,0:T(8,128)(2,1)S(1)}, u32[]{:S(2)}, u32[]{:S(2)}) %collective-permute-start.14) | collective-permute-done | bytes 131104 | tf_op jit(solution)/shard_map/ppermute | solution.py:371
  87.7 2.1 %shard_map.136.total = f32[128,1792]{1,0:T(8,128)S(1)} custom-call(bf16[8,64,128]{2,1,0:T(8,128)(2,1)S(1)} %all-to-all-done.mine, bf16[8,64,128]{2,1,0:T(8,128)(2,1)S(1)} %collective-permute-done.14.other, bf16[128,1792]{1,0:T(8,128)(2,1)S(1)} %multiply_convert_fusion.rest_0_, bf16[128,1792]{1,0:T(8,128)(2,1)} %collective-permute-done.3.rest_1_, ...), custom_call_target="tpu_custom_call" | custom-call | flops 1 | bytes 1 | tf_op jit(solution)/shard_map/pallas_call | solution.py:376
  89.8 0.3 collective-permute-done.17.top
  90.2 2.5 %collective-permute-done.18.bottom = bf16[64,1792]{1,0:T(8,128)(2,1)} collective-permute-done((bf16[64,1792]{1,0:T(8,128)(2,1)}, bf16[64,1792]{1,0:T(8,128)(2,1)}, u32[]{:S(2)}, u32[]{:S(2)}) %collective-permute-start.18) | collective-permute-done | bytes 229408 | tf_op jit(solution)/shard_map/ppermute | solution.py:30
  92.7 1.2 %shard_map.138 = (bf16[64,1792]{1,0:T(8,128)(2,1)S(1)}, bf16[64,1792]{1,0:T(8,128)(2,1)S(1)}) custom-call(bf16[8,64,128]{2,1,0:T(8,128)(2,1)S(1)} %all-to-all-done.mine, bf16[8,64,128]{2,1,0:T(8,128)(2,1)S(1)} %collective-permute-done.14.other, f32[128,1792]{1,0:T(8,128)S(1)} %shard_map.136.total, bf16[64,1792]{1,0:T(8,128)(2,1)S(1)} %collective-permute-done.17.top, ...), custom_call_target="tpu_custom_call" | custom-call | flops 100000000 | bytes 2097152 | tf_op jit(solution)/shard_map/pallas_call | solution.py:380
  93.9 0.1 collective-permute-start.19
  94.0 1.5 %collective-permute-done.19 = bf16[64,1792]{1,0:T(8,128)(2,1)S(1)} collective-permute-done((bf16[64,1792]{1,0:T(8,128)(2,1)S(1)}, bf16[64,1792]{1,0:T(8,128)(2,1)S(1)}, u32[]{:S(2)}, u32[]{:S(2)}) %collective-permute-start.19) | collective-permute-done | bytes 229408 | tf_op jit(solution)/shard_map/ppermute | solution.py:383
  95.5 0.8 pad_maximum_fusion
  (40 shorter events, 0.2 us)
Async XLA Ops:
  0.0 8.3 %copy-start = (bf16[3584,2]{0,1:T(2,128)(2,1)S(1)}, bf16[3584,2]{0,1:T(2,128)(2,1)}, u32[]{:S(2)}) copy-start(bf16[3584,2]{0,1:T(2,128)(2,1)} %param.16) | copy-start | bytes 43012
  0.0 9.5 %copy-start.1 = (bf16[2,3584,128]{2,1,0:T(8,128)(2,1)S(1)}, bf16[2,3584,128]{2,1,0:T(8,128)(2,1)}, u32[]{:S(2)}) copy-start(bf16[2,3584,128]{2,1,0:T(8,128)(2,1)} %refs_2_.7) | copy-start | bytes 5505028
  0.0 14.6 %collective-permute-start = (bf16[448,512]{1,0:T(8,128)(2,1)}, bf16[448,512]{1,0:T(8,128)(2,1)}, u32[]{:S(2)}, u32[]{:S(2)}) collective-permute-start(bf16[448,512]{1,0:T(8,128)(2,1)} %bitcast.12), channel_id=1, source_target_pairs={{0,2},{2,4},{4,6},{6,7},{7,5},{5,3},{3,1},{1,0},{8,10},{10,12},{12... | collective-permute-start | bytes 1376264 | tf_op jit(solution)/shard_map/ppermute | solution.py:30
  3.0 13.8 %collective-permute-start.2 = (bf16[448,512]{1,0:T(8,128)(2,1)}, bf16[448,512]{1,0:T(8,128)(2,1)}, u32[]{:S(2)}, u32[]{:S(2)}) collective-permute-start(bf16[448,512]{1,0:T(8,128)(2,1)} %bitcast.13), channel_id=1, source_target_pairs={{0,1},{2,0},{4,2},{6,4},{7,6},{5,7},{3,5},{1,3},{8,9},{10,8},{12,1... | collective-permute-start | bytes 1376264 | tf_op jit(solution)/shard_map/ppermute | solution.py:30
  4.2 20.2 %collective-permute-start.3 = (bf16[128,1792]{1,0:T(8,128)(2,1)S(1)}, bf16[128,1792]{1,0:T(8,128)(2,1)}, u32[]{:S(2)}, u32[]{:S(2)}) collective-permute-start(bf16[128,1792]{1,0:T(8,128)(2,1)S(1)} %multiply_convert_fusion.rest_0_), channel_id=1, source_target_pairs={{0,2},{2,4},{4,6},{6,7},{7,5},{5,3},{3,1},{1,0},{8,10},{10,12},{12... | collective-permute-start | bytes 1376264 | tf_op jit(solution)/shard_map/ppermute | solution.py:30
  6.3 20.3 %collective-permute-start.4 = (bf16[128,1792]{1,0:T(8,128)(2,1)S(1)}, bf16[128,1792]{1,0:T(8,128)(2,1)}, u32[]{:S(2)}, u32[]{:S(2)}) collective-permute-start(bf16[128,1792]{1,0:T(8,128)(2,1)S(1)} %multiply_convert_fusion.rest_0_), channel_id=1, source_target_pairs={{0,1},{2,0},{4,2},{6,4},{7,6},{5,7},{3,5},{1,3},{8,9},{10,8},{12,1... | collective-permute-start | bytes 1376264 | tf_op jit(solution)/shard_map/ppermute | solution.py:30
  7.0 10.9 %collective-permute-start.5 = (s32[8]{0:T(128)S(1)}, s32[8]{0:T(128)S(1)}, u32[]{:S(2)}, u32[]{:S(2)}) collective-permute-start(s32[8]{0:T(128)S(1)} %slice.33), channel_id=1, source_target_pairs={{0,8},{8,16},{16,24},{1,9},{9,17},{17,25},{2,10},{10,18},{18,26},{... | collective-permute-start | bytes 104 | tf_op jit(solution)/shard_map/ppermute | solution.py:292
  9.5 1.2 %copy-start.2 = (bf16[3584,128]{1,0:T(8,128)(2,1)S(1)}, bf16[3584,128]{1,0:T(8,128)(2,1)}, u32[]{:S(2)}) copy-start(bf16[3584,128]{1,0:T(8,128)(2,1)} %refs_3_.5) | copy-start | bytes 2752516
  10.7 1.0 %copy-start.7 = (bf16[512,448]{0,1:T(8,128)(2,1)S(1)}, bf16[512,448]{0,1:T(8,128)(2,1)}, u32[]{:S(2)}) copy-start(bf16[512,448]{0,1:T(8,128)(2,1)} %param.13) | copy-start | bytes 1376260
  11.7 5.1 %copy-start.10 = (s32[512]{0:T(512)S(1)}, s32[512]{0:T(512)}, u32[]{:S(2)}) copy-start(s32[512]{0:T(512)} %param.24) | copy-start | bytes 6148
  11.7 5.8 %copy-start.11 = (f32[2]{0:T(128)S(1)}, f32[2]{0:T(128)}, u32[]{:S(2)}) copy-start(f32[2]{0:T(128)} %param.17) | copy-start | bytes 28
  11.7 5.9 %copy-start.12 = (f32[2]{0:T(128)S(1)}, f32[2]{0:T(128)}, u32[]{:S(2)}) copy-start(f32[2]{0:T(128)} %param.18) | copy-start | bytes 28
  11.7 6.1 %copy-start.13 = (f32[2]{0:T(128)S(1)}, f32[2]{0:T(128)}, u32[]{:S(2)}) copy-start(f32[2]{0:T(128)} %param.19) | copy-start | bytes 28
  12.3 1.0 %copy-start.5 = (f32[512,512]{1,0:T(8,128)}, f32[512,512]{1,0:T(8,128)S(1)}, u32[]{:S(2)}) copy-start(f32[512,512]{1,0:T(8,128)S(1)} %shard_map.127.refs_5_) | copy-start | bytes 3145732
  14.6 18.7 %collective-permute-start.1 = (bf16[448,512]{1,0:T(8,128)(2,1)}, bf16[448,512]{1,0:T(8,128)(2,1)S(1)}, u32[]{:S(2)}, u32[]{:S(2)}) collective-permute-start(bf16[448,512]{1,0:T(8,128)(2,1)} %collective-permute-done.refs_0_), channel_id=1, source_target_pairs={{0,2},{2,4},{4,6},{6,7},{7,5},{5,3},{3,1},{1,0},{8,10},{10,12},{12... | collective-permute-start | bytes 1376264 | tf_op jit(solution)/shard_map/ppermute | solution.py:30
  16.8 18.4 %collective-permute-start.7 = (bf16[448,512]{1,0:T(8,128)(2,1)}, bf16[448,512]{1,0:T(8,128)(2,1)S(1)}, u32[]{:S(2)}, u32[]{:S(2)}) collective-permute-start(bf16[448,512]{1,0:T(8,128)(2,1)} %collective-permute-done.2.refs_1_), channel_id=1, source_target_pairs={{0,1},{2,0},{4,2},{6,4},{7,6},{5,7},{3,5},{1,3},{8,9},{10,8},{12,1... | collective-permute-start | bytes 1376264 | tf_op jit(solution)/shard_map/ppermute | solution.py:30
  26.6 1.2 %copy-start.3 = (bf16[3584,128]{1,0:T(8,128)(2,1)S(1)}, bf16[3584,128]{1,0:T(8,128)(2,1)}, u32[]{:S(2)}) copy-start(bf16[3584,128]{1,0:T(8,128)(2,1)} %refs_3_.5) | copy-start | bytes 2752516
  27.8 1.2 %copy-start.6 = (f32[512,512]{1,0:T(8,128)S(1)}, f32[512,512]{1,0:T(8,128)}, u32[]{:S(2)}) copy-start(f32[512,512]{1,0:T(8,128)} %copy-done.5) | copy-start | bytes 3145732
  33.3 15.1 %copy-start.4 = (bf16[3584,128]{1,0:T(8,128)(2,1)S(1)}, bf16[3584,128]{1,0:T(8,128)(2,1)}, u32[]{:S(2)}) copy-start(bf16[3584,128]{1,0:T(8,128)(2,1)} %refs_3_.5) | copy-start | bytes 2752516
  33.3 11.7 %collective-permute-start.6 = (bf16[448,512]{1,0:T(8,128)(2,1)S(1)}, bf16[448,512]{1,0:T(8,128)(2,1)S(1)}, u32[]{:S(2)}, u32[]{:S(2)}) collective-permute-start(bf16[448,512]{1,0:T(8,128)(2,1)S(1)} %collective-permute-done.1.refs_0_), channel_id=1, source_target_pairs={{0,2},{2,4},{4,6},{6,7},{7,5},{5,3},{3,1},{1,0},{8,10},{10,12},{12... | collective-permute-start | bytes 1376264 | tf_op jit(solution)/shard_map/ppermute | solution.py:30
  35.2 11.1 %collective-permute-start.8 = (bf16[448,512]{1,0:T(8,128)(2,1)S(1)}, bf16[448,512]{1,0:T(8,128)(2,1)S(1)}, u32[]{:S(2)}, u32[]{:S(2)}) collective-permute-start(bf16[448,512]{1,0:T(8,128)(2,1)S(1)} %collective-permute-done.7.refs_1_), channel_id=1, source_target_pairs={{0,1},{2,0},{4,2},{6,4},{7,6},{5,7},{3,5},{1,3},{8,9},{10,8},{12,1... | collective-permute-start | bytes 1376264 | tf_op jit(solution)/shard_map/ppermute | solution.py:30
  46.3 6.1 %collective-permute-start.9 = (bf16[224,512]{1,0:T(8,128)(2,1)S(1)}, bf16[224,512]{1,0:T(8,128)(2,1)S(1)}, u32[]{:S(2)}, u32[]{:S(2)}) collective-permute-start(bf16[224,512]{1,0:T(8,128)(2,1)S(1)} %get-tuple-element.44), channel_id=1, source_target_pairs={{0,2},{2,4},{4,6},{6,7},{7,5},{5,3},{3,1},{1,0},{8,10},{10,12},{12... | collective-permute-start | bytes 688136 | tf_op jit(solution)/shard_map/ppermute | solution.py:30
  47.9 6.0 %collective-permute-start.10 = (bf16[224,512]{1,0:T(8,128)(2,1)S(1)}, bf16[224,512]{1,0:T(8,128)(2,1)S(1)}, u32[]{:S(2)}, u32[]{:S(2)}) collective-permute-start(bf16[224,512]{1,0:T(8,128)(2,1)S(1)} %get-tuple-element.45), channel_id=1, source_target_pairs={{0,1},{2,0},{4,2},{6,4},{7,6},{5,7},{3,5},{1,3},{8,9},{10,8},{12,1... | collective-permute-start | bytes 688136 | tf_op jit(solution)/shard_map/ppermute | solution.py:30
  54.0 4.1 %copy-start.8 = (f32[4,128]{1,0:T(4,128)S(1)}, f32[4,128]{1,0:T(4,128)}, u32[]{:S(2)}) copy-start(f32[4,128]{1,0:T(4,128)} %taps_x.3) | copy-start | bytes 6148
  54.0 4.2 %copy-start.9 = (f32[4,128]{1,0:T(4,128)S(1)}, f32[4,128]{1,0:T(4,128)}, u32[]{:S(2)}) copy-start(f32[4,128]{1,0:T(4,128)} %taps_bc.3) | copy-start | bytes 6148
  54.4 13.4 %collective-permute-start.12 = (bf16[128,1792]{1,0:T(8,128)(2,1)}, bf16[128,1792]{1,0:T(8,128)(2,1)S(1)}, u32[]{:S(2)}, u32[]{:S(2)}) collective-permute-start(bf16[128,1792]{1,0:T(8,128)(2,1)} %collective-permute-done.3.rest_1_), channel_id=1, source_target_pairs={{0,2},{2,4},{4,6},{6,7},{7,5},{5,3},{3,1},{1,0},{8,10},{10,12},{12... | collective-permute-start | bytes 1376264 | tf_op jit(solution)/shard_map/ppermute | solution.py:30
  56.1 11.8 %collective-permute-start.13 = (bf16[128,1792]{1,0:T(8,128)(2,1)}, bf16[128,1792]{1,0:T(8,128)(2,1)S(1)}, u32[]{:S(2)}, u32[]{:S(2)}) collective-permute-start(bf16[128,1792]{1,0:T(8,128)(2,1)} %collective-permute-done.4.rest_2_), channel_id=1, source_target_pairs={{0,1},{2,0},{4,2},{6,4},{7,6},{5,7},{3,5},{1,3},{8,9},{10,8},{12,1... | collective-permute-start | bytes 1376264 | tf_op jit(solution)/shard_map/ppermute | solution.py:30
  56.5 2.6 %collective-permute-start.11 = (bf16[8,256]{1,0:T(8,128)(2,1)S(1)}, bf16[8,256]{1,0:T(8,128)(2,1)S(1)}, u32[]{:S(2)}, u32[]{:S(2)}) collective-permute-start(bf16[8,256]{1,0:T(8,128)(2,1)S(1)} %slice.44), channel_id=1, source_target_pairs={{0,8},{8,16},{16,24},{1,9},{9,17},{17,25},{2,10},{10,18},{18,26},{... | collective-permute-start | bytes 12296 | tf_op jit(solution)/shard_map/ppermute | solution.py:335
  67.8 13.3 %collective-permute-start.15 = (bf16[128,1792]{1,0:T(8,128)(2,1)S(1)}, bf16[128,1792]{1,0:T(8,128)(2,1)S(1)}, u32[]{:S(2)}, u32[]{:S(2)}) collective-permute-start(bf16[128,1792]{1,0:T(8,128)(2,1)S(1)} %collective-permute-done.12.rest_3_), channel_id=1, source_target_pairs={{0,2},{2,4},{4,6},{6,7},{7,5},{5,3},{3,1},{1,0},{8,10},{10,12},{12... | collective-permute-start | bytes 1376264 | tf_op jit(solution)/shard_map/ppermute | solution.py:30
  69.4 12.9 %collective-permute-start.16 = (bf16[128,1792]{1,0:T(8,128)(2,1)S(1)}, bf16[128,1792]{1,0:T(8,128)(2,1)S(1)}, u32[]{:S(2)}, u32[]{:S(2)}) collective-permute-start(bf16[128,1792]{1,0:T(8,128)(2,1)S(1)} %collective-permute-done.13.rest_4_), channel_id=1, source_target_pairs={{0,1},{2,0},{4,2},{6,4},{7,6},{5,7},{3,5},{1,3},{8,9},{10,8},{12,1... | collective-permute-start | bytes 1376264 | tf_op jit(solution)/shard_map/ppermute | solution.py:30
  71.7 14.7 %all-to-all-start = ((bf16[8,64,128]{2,1,0:T(8,128)(2,1)}), bf16[8,64,128]{2,1,0:T(8,128)(2,1)S(1)}, u32[]{:S(2)}, u32[]{:S(2)}) async-start(bf16[8,64,128]{2,1,0:T(8,128)(2,1)} %bitcast.7), calls=%async_computation | async-start | bytes 262144 | tf_op jit(solution)/shard_map/all_to_all | solution.py:369
  83.1 7.1 %collective-permute-start.17 = (bf16[64,1792]{1,0:T(8,128)(2,1)}, bf16[64,1792]{1,0:T(8,128)(2,1)S(1)}, u32[]{:S(2)}, u32[]{:S(2)}) collective-permute-start(bf16[64,1792]{1,0:T(8,128)(2,1)} %get-tuple-element.65), channel_id=1, source_target_pairs={{0,2},{2,4},{4,6},{6,7},{7,5},{5,3},{3,1},{1,0},{8,10},{10,12},{12... | collective-permute-start | bytes 688136 | tf_op jit(solution)/shard_map/ppermute | solution.py:30
  86.3 6.3 %collective-permute-start.18 = (bf16[64,1792]{1,0:T(8,128)(2,1)}, bf16[64,1792]{1,0:T(8,128)(2,1)}, u32[]{:S(2)}, u32[]{:S(2)}) collective-permute-start(bf16[64,1792]{1,0:T(8,128)(2,1)} %get-tuple-element.66), channel_id=1, source_target_pairs={{0,1},{2,0},{4,2},{6,4},{7,6},{5,7},{3,5},{1,3},{8,9},{10,8},{12,1... | collective-permute-start | bytes 688136 | tf_op jit(solution)/shard_map/ppermute | solution.py:30
  86.3 1.3 %collective-permute-start.14 = (bf16[8,64,128]{2,1,0:T(8,128)(2,1)S(1)}, bf16[8,64,128]{2,1,0:T(8,128)(2,1)S(1)}, u32[]{:S(2)}, u32[]{:S(2)}) collective-permute-start(bf16[8,64,128]{2,1,0:T(8,128)(2,1)S(1)} %all-to-all-done.mine), channel_id=1, source_target_pairs={{0,8},{8,0},{16,24},{24,16},{1,9},{9,1},{17,25},{25,17},{2,10},{10... | collective-permute-start | bytes 393224 | tf_op jit(solution)/shard_map/ppermute | solution.py:371
  93.9 1.6 %collective-permute-start.19 = (bf16[64,1792]{1,0:T(8,128)(2,1)S(1)}, bf16[64,1792]{1,0:T(8,128)(2,1)S(1)}, u32[]{:S(2)}, u32[]{:S(2)}) collective-permute-start(bf16[64,1792]{1,0:T(8,128)(2,1)S(1)} %get-tuple-element.68), channel_id=1, source_target_pairs={{0,8},{8,0},{16,24},{24,16},{1,9},{9,1},{17,25},{25,17},{2,10},{10... | collective-permute-start | bytes 688136 | tf_op jit(solution)/shard_map/ppermute | solution.py:383

commit v16 on v13

--- a/solution.py
+++ b/solution.py
@@ -157,19 +157,20 @@
     return result
 
 
-def later_block(heads, width, rows, proj, seg_ext, seg_row, taps_x, taps_bc, bias, rate, skip,
-                out, bc_out, enter_out, state_out, gate_out, ext_x, ext_bc):
-    rounded = proj[rows - HALO :, : 3 * width].astype(BF16).astype(F32)
-    gate_out[...] = silu(rounded[HALO:, :width])
-    ext_x[...] = rounded[:, width : 2 * width]
-    ext_bc[...] = rounded[:, 2 * width : 3 * width]
+def later_front(width, rows, proj, seg_ext, taps_x, taps_bc, bias, rate,
+                conv_out, bc_out, cum_out, scaled_out, enter_out, state_out, ext_x, ext_bc):
+    rounded = proj[rows - HALO :, width : 3 * width].astype(BF16).astype(F32)
+    ext_x[...] = rounded[:, :width]
+    ext_bc[...] = rounded[:, width:]
     seg_enter = seg_ext[HALO - 1 : HALO]
     seg_leave = seg_ext[HALO + rows - 1 : HALO + rows]
     conv_x, conv_bc, cum, scaled, state, enter, last = block_front(
         ext_x, ext_bc, seg_ext, proj[rows:, 3 * width :], taps_x, taps_bc[...], bias[...], rate[...], rows, seg_enter, seg_leave
     )
-    out[...] = block_inner(conv_bc, cum, scaled, seg_ext[HALO:], seg_row[...], heads) + skip[...] * conv_x
+    conv_out[...] = conv_x
     bc_out[...] = conv_bc
+    cum_out[...] = cum
+    scaled_out[...] = scaled
     enter_out[...] = enter
     keep = jnp.where(seg_enter == seg_leave, jnp.exp(last), 0.0)
     state_w = state.shape[0]
@@ -206,10 +207,10 @@
     message[state_w + 2 :] = jnp.zeros((message.shape[0] - state_w - 2, width), F32)
 
 
-def finish(heads, rows, seg_first, messages, seg_ext_a, seg_row_a, skip, proj, conv_a, bc_a, cum_a, scaled_a, enter_a,
-           state_a, out_b, gate_b, bc_b, enter_b, gated):
+def finish(heads, rows, seg_first, messages, seg_ext_a, seg_row_a, seg_ext_b, seg_row_b, skip, proj,
+           conv_a, bc_a, cum_a, scaled_a, enter_a, state_a, conv_b, bc_b, cum_b, scaled_b, enter_b, gated):
     state_w = bc_a.shape[1] // 2
-    width = out_b.shape[1]
+    width = conv_a.shape[1]
     entering = jnp.zeros((state_w, width), F32)
     decay = jnp.zeros((1, width), F32)
     first = seg_first[...].astype(F32)
@@ -221,10 +222,22 @@
         entering = entering + passes * messages[device, :state_w]
         decay = decay + jnp.where(earlier, messages[device, state_w : state_w + 1], 0.0)
     second = state_a[state_w : state_w + 1] * entering + state_a[:state_w]
-    out_a = block_inner(bc_a[...], cum_a[...], scaled_a[...], seg_ext_a[HALO:], seg_row_a[...], heads)
-    out_a = out_a + skip[...] * conv_a[...] + enter_a[...] * dot(bc_a[:, state_w:], entering)
-    gated[:rows] = (out_a * silu(proj[:rows, :width].astype(BF16).astype(F32))).astype(BF16)
-    gated[rows:] = ((out_b[...] + enter_b[...] * dot(bc_b[:, state_w:], second)) * gate_b[...]).astype(BF16)
+    blocks = (
+        (0, seg_ext_a, seg_row_a, conv_a, bc_a, cum_a, scaled_a, enter_a, entering),
+        (rows, seg_ext_b, seg_row_b, conv_b, bc_b, cum_b, scaled_b, enter_b, second),
+    )
+    for first, seg_ext, seg_row, conv_x, conv_bc, cum, scaled, enter, state in blocks:
+        out = block_inner(conv_bc[...], cum[...], scaled[...], seg_ext[HALO:], seg_row[...], heads)
+        out = out + skip[...] * conv_x[...] + enter[...] * dot(conv_bc[:, state_w:], state)
+        gate = silu(proj[first : first + rows, :width].astype(BF16).astype(F32))
+        gated[first : first + rows] = (out * gate).astype(BF16)
+
+
+def lay_together(own, other, out):
+    columns = own.shape[1]
+    core = lax.axis_index("seq") % 2
+    out[:, pl.ds(pl.multiple_of(core * columns, 128), columns)] = own[...]
+    out[:, pl.ds(pl.multiple_of((1 - core) * columns, 128), columns)] = other[...]
 
 
 def product(gated, distances, pieces):
@@ -337,11 +350,9 @@
     msg_rows = state_w + 8
     plane = shape(rows, width)
     ext = pltpu.VMEM((HALO + rows, width), F32)
-    out_b, bc_b, enter_b, state_b, gate_b = call(
-        functools.partial(later_block, heads, width, rows),
-        [plane, plane, plane, shape(msg_rows, width), plane],
-        [ext, ext],
-    )(proj, seg_ext_b, seg_row_b, conv_x, conv_bc, bias, rate, skip)
+    *later, state_b = call(
+        functools.partial(later_front, width, rows), [plane] * 5 + [shape(msg_rows, width)], [ext, ext]
+    )(proj, seg_ext_b, conv_x, conv_bc, bias, rate)
     cx_a, bc_a, cum_a, scaled_a, enter_a, state_a, message = call(
         functools.partial(first_front, width, rows),
         [plane] * 5 + [shape(msg_rows, width)] * 2,
@@ -349,13 +360,13 @@
     )(proj, halo, seg_ext_a, seg_last, state_b, conv_x, conv_bc, bias, rate)
     messages = lax.all_gather(message, "seq")
     gated = call(functools.partial(finish, heads, rows), shape(tok_rows, width, kind=BF16))(
-        seg_first, messages, seg_ext_a, seg_row_a, skip, proj, cx_a, bc_a, cum_a, scaled_a, enter_a, state_a,
-        out_b, gate_b, bc_b, enter_b
+        seg_first, messages, seg_ext_a, seg_row_a, seg_ext_b, seg_row_b, skip, proj,
+        cx_a, bc_a, cum_a, scaled_a, enter_a, state_a, *later
     )
     tok_own = tok_rows // n_tensor
 
     w_steps = [(w_forth, w_back)]
-    orders = [proj, messages]
+    orders = [far, messages]
     for step in range(2, last + 1):
         if step - 2 < len(orders):
             w_forth, w_back = after((w_forth, w_back), orders[step - 2])
@@ -380,9 +391,7 @@
     out_own, out_other = call(
         functools.partial(product_last, last), [half, half], [pltpu.VMEM((width, columns), BF16)], flops=10**8
     )(mine, other, total, *w_far)
-    arrived = lax.ppermute(out_other, "seq", swap)
-    is_first = core == 0
-    return jnp.concatenate([jnp.where(is_first, out_own, arrived), jnp.where(is_first, arrived, out_own)], 1)
+    return call(lay_together, shape(tok_own, model, kind=BF16))(out_own, lax.ppermute(out_other, "seq", swap))
 
 
 def solution(mesh):

time: 92.5 us -> 94.3 us (1.019)
  waiting for transfers between devices: 36.3 us -> 37.9 us
    ppermute x16, waiting for transfers between devices: 32.3 us -> 33.9 us  [ring_shift(): lax.ppermute(block, 'tensor', [(order[i], order[(i + step) % n]) for i in...]
  transfers between devices with their start and end apart: 21 -> 21, of which waited for: 12 -> 14; matrix products, arithmetic and copies ran while one was open for 4% -> 4% of each run, Pallas kernels for 16% -> 16%
where the time goes in v16:
time: 94.3 us; the launch traced here: 93.8 us
  waiting for transfers between devices  37.9 us (40%)
  starting transfers between devices  25.1 us (27%)
  Pallas kernels  16.1 us (17%)
  blocking collectives  7.21 us (8%)
  local copies, waits for them, and re-layouts  5.91 us (6%)
  matrix products  1.12 us (1%)
    ppermute x16, waiting for transfers between devices, ring_shift(): lax.ppermute(block, 'tensor', [(order[i], order[(i + step) % n]) for i in...  33.9 us
    ppermute x16, starting transfers between devices, ring_shift(): lax.ppermute(block, 'tensor', [(order[i], order[(i + step) % n]) for i in...  17.5 us
    pallas_call x4, Pallas kernels, local(): call(functools.partial(project, [distance for distance, _ in arrived], ah...  8.47 us
    all_gather x1, blocking collectives, local(): messages = lax.all_gather(message, 'seq')  7.21 us
    all_to_all x1, starting transfers between devices, local(): mine = lax.all_to_all(blocks, 'tensor', 0, 0)  4.79 us
    unnamed x26, local copies, waits for them, and re-layouts  3.74 us
    pallas_call x1, Pallas kernels, local(): call(functools.partial(product_early, distances), shape(2 * tok_own, colu...  2.28 us
  transfers between devices with their start and end apart: 21, of which 14 were waited for; matrix products, arithmetic and copies ran while one was open for 4% of the time, Pallas kernels for 16%

profile of v16, /device:TPU:0, one launch (start us, length us, event | category | flops | bytes accessed | tf_op | source)
XLA Modules:
  0.0 93.8 jit_solution(10987796276737255167)
XLA Ops:
  0.0 3.0 %collective-permute-start = (bf16[448,512]{1,0:T(8,128)(2,1)}, bf16[448,512]{1,0:T(8,128)(2,1)}, u32[]{:S(2)}, u32[]{:S(2)}) collective-permute-start(bf16[448,512]{1,0:T(8,128)(2,1)} %bitcast.12), channel_id=1, source_target_pairs={{0,2},{2,4},{4,6},{6,7},{7,5},{5,3},{3,1},{1,0},{8,10},{10,12},{12... | collective-permute-start | bytes 1376264 | tf_op jit(solution)/shard_map/ppermute | solution.py:31
  3.0 0.8 slice.33
  3.8 1.4 %collective-permute-start.3 = (s32[8]{0:T(128)S(1)}, s32[8]{0:T(128)S(1)}, u32[]{:S(2)}, u32[]{:S(2)}) collective-permute-start(s32[8]{0:T(128)S(1)} %slice.33), channel_id=1, source_target_pairs={{0,8},{8,16},{16,24},{1,9},{9,17},{17,25},{2,10},{10,18},{18,26},{... | collective-permute-start | bytes 104 | tf_op jit(solution)/shard_map/ppermute | solution.py:306
  5.2 1.1 %convolution_bitcast_fusion.refs_3_.refs_4_ = bf16[3584,128]{1,0:T(8,128)(2,1)S(1)} fusion(bf16[2,128]{1,0:T(2,128)(2,1)} %constant.25.clone, bf16[3584,2]{0,1:T(2,128)(2,1)S(1)} %copy-done), kind=kOutput, calls=%fused_computation | convolution fusion | flops 1835008 | bytes 932352 | tf_op jit(solution)/shard_map/dot_general | solution.py:297
  6.4 0.0 copy-start.1
  6.4 1.5 %copy-done.1 = bf16[2,3584,128]{2,1,0:T(8,128)(2,1)S(1)} copy-done((bf16[2,3584,128]{2,1,0:T(8,128)(2,1)S(1)}, bf16[2,3584,128]{2,1,0:T(8,128)(2,1)}, u32[]{:S(2)}) %copy-start.1) | copy-done | bytes 1835032
  7.9 1.2 %copy-done.2 = bf16[3584,128]{1,0:T(8,128)(2,1)S(1)} copy-done((bf16[3584,128]{1,0:T(8,128)(2,1)S(1)}, bf16[3584,128]{1,0:T(8,128)(2,1)}, u32[]{:S(2)}) %copy-start.2) | copy-done | bytes 917528
  9.1 1.0 %copy-done.4 = bf16[512,448]{0,1:T(8,128)(2,1)S(1)} copy-done((bf16[512,448]{0,1:T(8,128)(2,1)S(1)}, bf16[512,448]{0,1:T(8,128)(2,1)}, u32[]{:S(2)}) %copy-start.4) | copy-done | bytes 458776
  10.1 0.6 shard_map.127.refs_5_
  10.7 3.1 %collective-permute-done.refs_0_ = bf16[448,512]{1,0:T(8,128)(2,1)} collective-permute-done((bf16[448,512]{1,0:T(8,128)(2,1)}, bf16[448,512]{1,0:T(8,128)(2,1)}, u32[]{:S(2)}, u32[]{:S(2)}) %collective-permute-start) | collective-permute-done | bytes 458784 | tf_op jit(solution)/shard_map/ppermute | solution.py:31
  13.8 1.8 %collective-permute-start.1 = (bf16[448,512]{1,0:T(8,128)(2,1)}, bf16[448,512]{1,0:T(8,128)(2,1)}, u32[]{:S(2)}, u32[]{:S(2)}) collective-permute-start(bf16[448,512]{1,0:T(8,128)(2,1)} %collective-permute-done.refs_0_), channel_id=1, source_target_pairs={{0,2},{2,4},{4,6},{6,7},{7,5},{5,3},{3,1},{1,0},{8,10},{10,12},{12... | collective-permute-start | bytes 1376264 | tf_op jit(solution)/shard_map/ppermute | solution.py:31
  15.6 0.2 collective-permute-start.5
  15.8 0.6 fusion
  16.4 0.1 slice.36
  16.5 0.1 broadcast_in_dim.27
  16.5 0.1 broadcast_in_dim_reshape.9.bias
  16.6 0.1 broadcast_in_dim.28
  16.7 0.1 broadcast_in_dim_reshape.10.rate
  16.8 0.1 broadcast_in_dim.29
  16.9 0.1 broadcast_in_dim_reshape.11.skip
  16.9 0.1 pad_add_fusion
  17.0 0.0 copy-start.9
  17.1 3.0 %shard_map.128.refs_5_ = f32[512,512]{1,0:T(8,128)S(1)} custom-call(bf16[448,512]{1,0:T(8,128)(2,1)} %collective-permute-done.refs_0_, bf16[448,512]{1,0:T(8,128)(2,1)S(1)} %collective-permute-done.2.refs_1_, bf16[2,3584,128]{2,1,0:T(8,128)(2,1)} %refs_2_.7, bf16[3584,128]{1,0:T(8,128)(2,1)S(1)} %copy-done.3, ...), custom_call_target="tpu_custom_call" | custom-call | flops 1000000000 | bytes 2097152 | tf_op jit(solution)/shard_map/pallas_call | solution.py:334
  20.0 6.0 %collective-permute-done.1.refs_0_ = bf16[448,512]{1,0:T(8,128)(2,1)} collective-permute-done((bf16[448,512]{1,0:T(8,128)(2,1)}, bf16[448,512]{1,0:T(8,128)(2,1)}, u32[]{:S(2)}, u32[]{:S(2)}) %collective-permute-start.1) | collective-permute-done | bytes 458784 | tf_op jit(solution)/shard_map/ppermute | solution.py:31
  26.0 1.6 %collective-permute-start.4 = (bf16[448,512]{1,0:T(8,128)(2,1)}, bf16[448,512]{1,0:T(8,128)(2,1)S(1)}, u32[]{:S(2)}, u32[]{:S(2)}) collective-permute-start(bf16[448,512]{1,0:T(8,128)(2,1)} %collective-permute-done.1.refs_0_), channel_id=1, source_target_pairs={{0,2},{2,4},{4,6},{6,7},{7,5},{5,3},{3,1},{1,0},{8,10},{10,12},{12... | collective-permute-start | bytes 1376264 | tf_op jit(solution)/shard_map/ppermute | solution.py:31
  27.6 0.4 collective-permute-start.6
  28.1 0.1 multiply_convert_fusion.rest_0_
  28.2 1.6 %collective-permute-start.10 = (bf16[128,1792]{1,0:T(8,128)(2,1)S(1)}, bf16[128,1792]{1,0:T(8,128)(2,1)S(1)}, u32[]{:S(2)}, u32[]{:S(2)}) collective-permute-start(bf16[128,1792]{1,0:T(8,128)(2,1)S(1)} %multiply_convert_fusion.rest_0_), channel_id=1, source_target_pairs={{0,2},{2,4},{4,6},{6,7},{7,5},{5,3},{3,1},{1,0},{8,10},{10,12},{12... | collective-permute-start | bytes 1376264 | tf_op jit(solution)/shard_map/ppermute | solution.py:31
  29.9 0.4 collective-permute-start.11
  30.3 3.0 %shard_map.129.refs_5_ = f32[512,512]{1,0:T(8,128)S(1)} custom-call(bf16[448,512]{1,0:T(8,128)(2,1)} %collective-permute-done.1.refs_0_, bf16[448,512]{1,0:T(8,128)(2,1)} %collective-permute-done.5.refs_1_, bf16[2,3584,128]{2,1,0:T(8,128)(2,1)} %refs_2_.7, bf16[3584,128]{1,0:T(8,128)(2,1)S(1)} %copy-done.3, ...), custom_call_target="tpu_custom_call" | custom-call | flops 1000000000 | bytes 2097152 | tf_op jit(solution)/shard_map/pallas_call | solution.py:334
  33.3 6.4 %collective-permute-done.4.forth.refs_0_ = bf16[448,512]{1,0:T(8,128)(2,1)S(1)} collective-permute-done((bf16[448,512]{1,0:T(8,128)(2,1)}, bf16[448,512]{1,0:T(8,128)(2,1)S(1)}, u32[]{:S(2)}, u32[]{:S(2)}) %collective-permute-start.4) | collective-permute-done | bytes 458784 | tf_op jit(solution)/shard_map/ppermute | solution.py:31
  39.7 1.6 %collective-permute-done.6.back.refs_1_ = bf16[448,512]{1,0:T(8,128)(2,1)S(1)} collective-permute-done((bf16[448,512]{1,0:T(8,128)(2,1)}, bf16[448,512]{1,0:T(8,128)(2,1)S(1)}, u32[]{:S(2)}, u32[]{:S(2)}) %collective-permute-start.6) | collective-permute-done | bytes 458784 | tf_op jit(solution)/shard_map/ppermute | solution.py:31
  41.3 1.6 %collective-permute-start.7 = (bf16[224,512]{1,0:T(8,128)(2,1)S(1)}, bf16[224,512]{1,0:T(8,128)(2,1)S(1)}, u32[]{:S(2)}, u32[]{:S(2)}) collective-permute-start(bf16[224,512]{1,0:T(8,128)(2,1)S(1)} %get-tuple-element.45), channel_id=1, source_target_pairs={{0,2},{2,4},{4,6},{6,7},{7,5},{5,3},{3,1},{1,0},{8,10},{10,12},{12... | collective-permute-start | bytes 688136 | tf_op jit(solution)/shard_map/ppermute | solution.py:31
  43.0 0.5 collective-permute-start.8
  43.4 6.1 %collective-permute-done.10.rest_1_ = bf16[128,1792]{1,0:T(8,128)(2,1)S(1)} collective-permute-done((bf16[128,1792]{1,0:T(8,128)(2,1)S(1)}, bf16[128,1792]{1,0:T(8,128)(2,1)S(1)}, u32[]{:S(2)}, u32[]{:S(2)}) %collective-permute-start.10) | collective-permute-done | bytes 458784 | tf_op jit(solution)/shard_map/ppermute | solution.py:31
  49.5 1.2 %collective-permute-done.11.rest_2_ = bf16[128,1792]{1,0:T(8,128)(2,1)} collective-permute-done((bf16[128,1792]{1,0:T(8,128)(2,1)S(1)}, bf16[128,1792]{1,0:T(8,128)(2,1)}, u32[]{:S(2)}, u32[]{:S(2)}) %collective-permute-start.11) | collective-permute-done | bytes 458784 | tf_op jit(solution)/shard_map/ppermute | solution.py:31
  50.7 1.3 %collective-permute-done.7.top = bf16[224,512]{1,0:T(8,128)(2,1)S(1)} collective-permute-done((bf16[224,512]{1,0:T(8,128)(2,1)S(1)}, bf16[224,512]{1,0:T(8,128)(2,1)S(1)}, u32[]{:S(2)}, u32[]{:S(2)}) %collective-permute-start.7) | collective-permute-done | bytes 229408 | tf_op jit(solution)/shard_map/ppermute | solution.py:31
  52.0 1.0 %collective-permute-done.8.bottom = bf16[224,512]{1,0:T(8,128)(2,1)S(1)} collective-permute-done((bf16[224,512]{1,0:T(8,128)(2,1)S(1)}, bf16[224,512]{1,0:T(8,128)(2,1)S(1)}, u32[]{:S(2)}, u32[]{:S(2)}) %collective-permute-start.8) | collective-permute-done | bytes 229408 | tf_op jit(solution)/shard_map/ppermute | solution.py:31
  53.1 1.6 %collective-permute-start.12 = (bf16[128,1792]{1,0:T(8,128)(2,1)S(1)}, bf16[128,1792]{1,0:T(8,128)(2,1)}, u32[]{:S(2)}, u32[]{:S(2)}) collective-permute-start(bf16[128,1792]{1,0:T(8,128)(2,1)S(1)} %collective-permute-done.10.rest_1_), channel_id=1, source_target_pairs={{0,2},{2,4},{4,6},{6,7},{7,5},{5,3},{3,1},{1,0},{8,10},{10,12},{12... | collective-permute-start | bytes 1376264 | tf_op jit(solution)/shard_map/ppermute | solution.py:31
  54.7 0.5 collective-permute-start.13
  55.1 1.9 %shard_map.131 = (f32[512,512]{1,0:T(8,128)S(1)}, bf16[448,512]{1,0:T(8,128)(2,1)S(1)}) custom-call(bf16[448,512]{1,0:T(8,128)(2,1)S(1)} %collective-permute-done.4.forth.refs_0_, bf16[448,512]{1,0:T(8,128)(2,1)S(1)} %collective-permute-done.6.back.refs_1_, bf16[2,3584,128]{2,1,0:T(8,128)(2,1)} %refs_2_.7, bf16[3584,128]{1,0:T(8,128)(2,1)S(1)} %copy-done.3, ...), custom_call_target="tpu_custom_call" | custom-call | flops 1000000000 | bytes 2097152 | tf_op jit(solution)/shard_map/pallas_call | solution.py:334
  57.0 0.0 copy-start.5
  57.0 0.5 shard_map.132.proj
  57.5 1.3 %collective-permute-start.9 = (bf16[8,256]{1,0:T(8,128)(2,1)S(1)}, bf16[8,256]{1,0:T(8,128)(2,1)S(1)}, u32[]{:S(2)}, u32[]{:S(2)}) collective-permute-start(bf16[8,256]{1,0:T(8,128)(2,1)S(1)} %slice.44), channel_id=1, source_target_pairs={{0,8},{8,16},{16,24},{1,9},{9,17},{17,25},{2,10},{10,18},{18,26},{... | collective-permute-start | bytes 12296 | tf_op jit(solution)/shard_map/ppermute | solution.py:348
  58.8 0.1 copy.16.seg_ext.seg_ext_b
  59.0 0.1 copy.17.seg_ext.seg_ext_a
  59.1 0.6 shard_map.133
  59.7 1.2 %shard_map.134 = (f32[256,128]{1,0:T(8,128)S(1)}, f32[256,128]{1,0:T(8,128)S(1)}, f32[256,128]{1,0:T(8,128)S(1)}, f32[256,128]{1,0:T(8,128)S(1)}, f32[256,128]{1...) custom-call(f32[512,512]{1,0:T(8,128)S(1)} %shard_map.132.proj, ...), custom_call_target="tpu_custom_call" | custom-call | flops 10000000 | bytes 2097152 | tf_op jit(solution)/shard_map/pallas_call | solution.py:356
  61.0 7.2 %all-gather = f32[288,128]{1,0:T(8,128)S(1)} all-gather(f32[72,128]{1,0:T(8,128)S(1)} %get-tuple-element.50), channel_id=2, replica_groups=mesh['seq'=4,'tensor'=8] {'seq'}, dimensions={0}, use_global_device_ids=true | all-gather | bytes 184320 | tf_op jit(solution)/shard_map/all_gather | solution.py:361
  68.2 1.6 %collective-permute-start.15 = (bf16[128,1792]{1,0:T(8,128)(2,1)}, bf16[128,1792]{1,0:T(8,128)(2,1)S(1)}, u32[]{:S(2)}, u32[]{:S(2)}) collective-permute-start(bf16[128,1792]{1,0:T(8,128)(2,1)} %collective-permute-done.12.rest_3_), channel_id=1, source_target_pairs={{0,2},{2,4},{4,6},{6,7},{7,5},{5,3},{3,1},{1,0},{8,10},{10,12},{12... | collective-permute-start | bytes 1376264 | tf_op jit(solution)/shard_map/ppermute | solution.py:31
  69.8 0.4 collective-permute-start.16
  70.3 1.9 %shard_map.135 = bf16[512,128]{1,0:T(8,128)(2,1)} custom-call(s32[1,1]{1,0:T(1,128)} %bitcast.seg_first, f32[4,72,128]{2,1,0:T(8,128)S(1)} %bitcast.11, s32[264,1]{1,0:T(8,128)S(1)} %copy.17.seg_ext.seg_ext_a, s32[1,256]{1,0:T(1,128)S(1)} %bitcast.16, s32[264,1]{1,0:T(8,128)S(1)} %copy.16.seg_ext.seg_ext_b, s32[1,256]{1,0:T(1,128)S(1)} %bitcast.15, ...), custom_call_target="tpu_custom_call" | custom-call | flops 10000000 | bytes 2097152 | tf_op jit(solution)/shard_map/pallas_call | solution.py:362
  72.1 4.8 %all-to-all-start = ((bf16[8,64,128]{2,1,0:T(8,128)(2,1)}), bf16[8,64,128]{2,1,0:T(8,128)(2,1)S(1)}, u32[]{:S(2)}, u32[]{:S(2)}) async-start(bf16[8,64,128]{2,1,0:T(8,128)(2,1)} %bitcast.7), calls=%async_computation | async-start | bytes 262144 | tf_op jit(solution)/shard_map/all_to_all | solution.py:380
  76.9 4.7 %collective-permute-done.15.rest_5_.forth = bf16[128,1792]{1,0:T(8,128)(2,1)S(1)} collective-permute-done((bf16[128,1792]{1,0:T(8,128)(2,1)}, bf16[128,1792]{1,0:T(8,128)(2,1)S(1)}, u32[]{:S(2)}, u32[]{:S(2)}) %collective-permute-start.15) | collective-permute-done | bytes 458784 | tf_op jit(solution)/shard_map/ppermute | solution.py:31
  81.7 1.2 %collective-permute-done.16.rest_6_.back = bf16[128,1792]{1,0:T(8,128)(2,1)S(1)} collective-permute-done((bf16[128,1792]{1,0:T(8,128)(2,1)}, bf16[128,1792]{1,0:T(8,128)(2,1)S(1)}, u32[]{:S(2)}, u32[]{:S(2)}) %collective-permute-start.16) | collective-permute-done | bytes 458784 | tf_op jit(solution)/shard_map/ppermute | solution.py:31
  82.9 2.2 %collective-permute-start.17 = (bf16[64,1792]{1,0:T(8,128)(2,1)S(1)}, bf16[64,1792]{1,0:T(8,128)(2,1)S(1)}, u32[]{:S(2)}, u32[]{:S(2)}) collective-permute-start(bf16[64,1792]{1,0:T(8,128)(2,1)S(1)} %get-tuple-element.69), channel_id=1, source_target_pairs={{0,2},{2,4},{4,6},{6,7},{7,5},{5,3},{3,1},{1,0},{8,10},{10,12},{12... | collective-permute-start | bytes 688136 | tf_op jit(solution)/shard_map/ppermute | solution.py:31
  85.1 1.2 %all-to-all-done.mine = bf16[8,64,128]{2,1,0:T(8,128)(2,1)S(1)} async-done(((bf16[8,64,128]{2,1,0:T(8,128)(2,1)}), bf16[8,64,128]{2,1,0:T(8,128)(2,1)S(1)}, u32[]{:S(2)}, u32[]{:S(2)}) %all-to-all-start) | async-done | bytes 131104 | tf_op jit(solution)/shard_map/all_to_all | solution.py:380
  86.3 1.3 %collective-permute-done.14.other = bf16[8,64,128]{2,1,0:T(8,128)(2,1)S(1)} collective-permute-done((bf16[8,64,128]{2,1,0:T(8,128)(2,1)S(1)}, bf16[8,64,128]{2,1,0:T(8,128)(2,1)S(1)}, u32[]{:S(2)}, u32[]{:S(2)}) %collective-permute-start.14) | collective-permute-done | bytes 131104 | tf_op jit(solution)/shard_map/ppermute | solution.py:382
  87.6 2.3 %shard_map.136.total = f32[128,1792]{1,0:T(8,128)S(1)} custom-call(bf16[8,64,128]{2,1,0:T(8,128)(2,1)S(1)} %all-to-all-done.mine, bf16[8,64,128]{2,1,0:T(8,128)(2,1)S(1)} %collective-permute-done.14.other, bf16[128,1792]{1,0:T(8,128)(2,1)S(1)} %multiply_convert_fusion.rest_0_, bf16[128,1792]{1,0:T(8,128)(2,1)S(1)} %collective-permute-done.10.rest_1_, ...), custom_call_target="tpu_custom_call" | custom-call | flops 1 | bytes 1 | tf_op jit(solution)/shard_map/pallas_call | solution.py:387
  89.9 1.2 %collective-permute-done.18.bottom = bf16[64,1792]{1,0:T(8,128)(2,1)S(1)} collective-permute-done((bf16[64,1792]{1,0:T(8,128)(2,1)S(1)}, bf16[64,1792]{1,0:T(8,128)(2,1)S(1)}, u32[]{:S(2)}, u32[]{:S(2)}) %collective-permute-start.18) | collective-permute-done | bytes 229408 | tf_op jit(solution)/shard_map/ppermute | solution.py:31
  91.1 0.3 shard_map.138
  91.4 0.1 collective-permute-start.19
  91.5 1.5 %collective-permute-done.19.other = bf16[64,1792]{1,0:T(8,128)(2,1)S(1)} collective-permute-done((bf16[64,1792]{1,0:T(8,128)(2,1)S(1)}, bf16[64,1792]{1,0:T(8,128)(2,1)S(1)}, u32[]{:S(2)}, u32[]{:S(2)}) %collective-permute-start.19) | collective-permute-done | bytes 229408 | tf_op jit(solution)/shard_map/ppermute | solution.py:394
  92.9 0.8 shard_map.139
  (37 shorter events, 0.2 us)
Async XLA Ops:
  0.0 5.2 %copy-start = (bf16[3584,2]{0,1:T(2,128)(2,1)S(1)}, bf16[3584,2]{0,1:T(2,128)(2,1)}, u32[]{:S(2)}) copy-start(bf16[3584,2]{0,1:T(2,128)(2,1)} %param.16) | copy-start | bytes 43012
  0.0 13.8 %collective-permute-start = (bf16[448,512]{1,0:T(8,128)(2,1)}, bf16[448,512]{1,0:T(8,128)(2,1)}, u32[]{:S(2)}, u32[]{:S(2)}) collective-permute-start(bf16[448,512]{1,0:T(8,128)(2,1)} %bitcast.12), channel_id=1, source_target_pairs={{0,2},{2,4},{4,6},{6,7},{7,5},{5,3},{3,1},{1,0},{8,10},{10,12},{12... | collective-permute-start | bytes 1376264 | tf_op jit(solution)/shard_map/ppermute | solution.py:31
  3.0 12.6 %collective-permute-start.2 = (bf16[448,512]{1,0:T(8,128)(2,1)}, bf16[448,512]{1,0:T(8,128)(2,1)S(1)}, u32[]{:S(2)}, u32[]{:S(2)}) collective-permute-start(bf16[448,512]{1,0:T(8,128)(2,1)} %bitcast.13), channel_id=1, source_target_pairs={{0,1},{2,0},{4,2},{6,4},{7,6},{5,7},{3,5},{1,3},{8,9},{10,8},{12,1... | collective-permute-start | bytes 1376264 | tf_op jit(solution)/shard_map/ppermute | solution.py:31
  3.8 13.2 %collective-permute-start.3 = (s32[8]{0:T(128)S(1)}, s32[8]{0:T(128)S(1)}, u32[]{:S(2)}, u32[]{:S(2)}) collective-permute-start(s32[8]{0:T(128)S(1)} %slice.33), channel_id=1, source_target_pairs={{0,8},{8,16},{16,24},{1,9},{9,17},{17,25},{2,10},{10,18},{18,26},{... | collective-permute-start | bytes 104 | tf_op jit(solution)/shard_map/ppermute | solution.py:306
  6.4 1.5 %copy-start.1 = (bf16[2,3584,128]{2,1,0:T(8,128)(2,1)S(1)}, bf16[2,3584,128]{2,1,0:T(8,128)(2,1)}, u32[]{:S(2)}) copy-start(bf16[2,3584,128]{2,1,0:T(8,128)(2,1)} %refs_2_.7) | copy-start | bytes 5505028
  7.9 1.2 %copy-start.2 = (bf16[3584,128]{1,0:T(8,128)(2,1)S(1)}, bf16[3584,128]{1,0:T(8,128)(2,1)}, u32[]{:S(2)}) copy-start(bf16[3584,128]{1,0:T(8,128)(2,1)} %refs_3_.5) | copy-start | bytes 2752516
  9.1 1.0 %copy-start.4 = (bf16[512,448]{0,1:T(8,128)(2,1)S(1)}, bf16[512,448]{0,1:T(8,128)(2,1)}, u32[]{:S(2)}) copy-start(bf16[512,448]{0,1:T(8,128)(2,1)} %param.13) | copy-start | bytes 1376260
  10.1 5.7 %copy-start.8 = (s32[512]{0:T(512)S(1)}, s32[512]{0:T(512)}, u32[]{:S(2)}) copy-start(s32[512]{0:T(512)} %param.24) | copy-start | bytes 6148
  10.1 6.4 %copy-start.10 = (f32[2]{0:T(128)S(1)}, f32[2]{0:T(128)}, u32[]{:S(2)}) copy-start(f32[2]{0:T(128)} %param.17) | copy-start | bytes 28
  10.1 6.6 %copy-start.11 = (f32[2]{0:T(128)S(1)}, f32[2]{0:T(128)}, u32[]{:S(2)}) copy-start(f32[2]{0:T(128)} %param.18) | copy-start | bytes 28
  10.1 6.7 %copy-start.12 = (f32[2]{0:T(128)S(1)}, f32[2]{0:T(128)}, u32[]{:S(2)}) copy-start(f32[2]{0:T(128)} %param.19) | copy-start | bytes 28
  10.1 7.0 %copy-start.3 = (bf16[3584,128]{1,0:T(8,128)(2,1)S(1)}, bf16[3584,128]{1,0:T(8,128)(2,1)}, u32[]{:S(2)}) copy-start(bf16[3584,128]{1,0:T(8,128)(2,1)} %refs_3_.5) | copy-start | bytes 2752516
  13.8 12.3 %collective-permute-start.1 = (bf16[448,512]{1,0:T(8,128)(2,1)}, bf16[448,512]{1,0:T(8,128)(2,1)}, u32[]{:S(2)}, u32[]{:S(2)}) collective-permute-start(bf16[448,512]{1,0:T(8,128)(2,1)} %collective-permute-done.refs_0_), channel_id=1, source_target_pairs={{0,2},{2,4},{4,6},{6,7},{7,5},{5,3},{3,1},{1,0},{8,10},{10,12},{12... | collective-permute-start | bytes 1376264 | tf_op jit(solution)/shard_map/ppermute | solution.py:31
  15.6 12.0 %collective-permute-start.5 = (bf16[448,512]{1,0:T(8,128)(2,1)S(1)}, bf16[448,512]{1,0:T(8,128)(2,1)}, u32[]{:S(2)}, u32[]{:S(2)}) collective-permute-start(bf16[448,512]{1,0:T(8,128)(2,1)S(1)} %collective-permute-done.2.refs_1_), channel_id=1, source_target_pairs={{0,1},{2,0},{4,2},{6,4},{7,6},{5,7},{3,5},{1,3},{8,9},{10,8},{12,1... | collective-permute-start | bytes 1376264 | tf_op jit(solution)/shard_map/ppermute | solution.py:31
  17.0 11.0 %copy-start.7 = (bf16[128,3584]{1,0:T(8,128)(2,1)S(1)}, bf16[128,3584]{1,0:T(8,128)(2,1)}, u32[]{:S(2)}) copy-start(bf16[128,3584]{1,0:T(8,128)(2,1)} %param.23) | copy-start | bytes 2752516
  17.0 11.0 %copy-start.9 = (f32[128]{0:T(128)S(1)}, f32[128]{0:T(128)}, u32[]{:S(2)}) copy-start(f32[128]{0:T(128)} %param.22) | copy-start | bytes 1540
  26.0 13.7 %collective-permute-start.4 = (bf16[448,512]{1,0:T(8,128)(2,1)}, bf16[448,512]{1,0:T(8,128)(2,1)S(1)}, u32[]{:S(2)}, u32[]{:S(2)}) collective-permute-start(bf16[448,512]{1,0:T(8,128)(2,1)} %collective-permute-done.1.refs_0_), channel_id=1, source_target_pairs={{0,2},{2,4},{4,6},{6,7},{7,5},{5,3},{3,1},{1,0},{8,10},{10,12},{12... | collective-permute-start | bytes 1376264 | tf_op jit(solution)/shard_map/ppermute | solution.py:31
  27.6 13.7 %collective-permute-start.6 = (bf16[448,512]{1,0:T(8,128)(2,1)}, bf16[448,512]{1,0:T(8,128)(2,1)S(1)}, u32[]{:S(2)}, u32[]{:S(2)}) collective-permute-start(bf16[448,512]{1,0:T(8,128)(2,1)} %collective-permute-done.5.refs_1_), channel_id=1, source_target_pairs={{0,1},{2,0},{4,2},{6,4},{7,6},{5,7},{3,5},{1,3},{8,9},{10,8},{12,1... | collective-permute-start | bytes 1376264 | tf_op jit(solution)/shard_map/ppermute | solution.py:31
  28.2 21.3 %collective-permute-start.10 = (bf16[128,1792]{1,0:T(8,128)(2,1)S(1)}, bf16[128,1792]{1,0:T(8,128)(2,1)S(1)}, u32[]{:S(2)}, u32[]{:S(2)}) collective-permute-start(bf16[128,1792]{1,0:T(8,128)(2,1)S(1)} %multiply_convert_fusion.rest_0_), channel_id=1, source_target_pairs={{0,2},{2,4},{4,6},{6,7},{7,5},{5,3},{3,1},{1,0},{8,10},{10,12},{12... | collective-permute-start | bytes 1376264 | tf_op jit(solution)/shard_map/ppermute | solution.py:31
  29.9 20.9 %collective-permute-start.11 = (bf16[128,1792]{1,0:T(8,128)(2,1)S(1)}, bf16[128,1792]{1,0:T(8,128)(2,1)}, u32[]{:S(2)}, u32[]{:S(2)}) collective-permute-start(bf16[128,1792]{1,0:T(8,128)(2,1)S(1)} %multiply_convert_fusion.rest_0_), channel_id=1, source_target_pairs={{0,1},{2,0},{4,2},{6,4},{7,6},{5,7},{3,5},{1,3},{8,9},{10,8},{12,1... | collective-permute-start | bytes 1376264 | tf_op jit(solution)/shard_map/ppermute | solution.py:31
  41.3 10.7 %collective-permute-start.7 = (bf16[224,512]{1,0:T(8,128)(2,1)S(1)}, bf16[224,512]{1,0:T(8,128)(2,1)S(1)}, u32[]{:S(2)}, u32[]{:S(2)}) collective-permute-start(bf16[224,512]{1,0:T(8,128)(2,1)S(1)} %get-tuple-element.45), channel_id=1, source_target_pairs={{0,2},{2,4},{4,6},{6,7},{7,5},{5,3},{3,1},{1,0},{8,10},{10,12},{12... | collective-permute-start | bytes 688136 | tf_op jit(solution)/shard_map/ppermute | solution.py:31
  43.0 10.1 %collective-permute-start.8 = (bf16[224,512]{1,0:T(8,128)(2,1)S(1)}, bf16[224,512]{1,0:T(8,128)(2,1)S(1)}, u32[]{:S(2)}, u32[]{:S(2)}) collective-permute-start(bf16[224,512]{1,0:T(8,128)(2,1)S(1)} %get-tuple-element.46), channel_id=1, source_target_pairs={{0,1},{2,0},{4,2},{6,4},{7,6},{5,7},{3,5},{1,3},{8,9},{10,8},{12,1... | collective-permute-start | bytes 688136 | tf_op jit(solution)/shard_map/ppermute | solution.py:31
  53.1 15.1 %collective-permute-start.12 = (bf16[128,1792]{1,0:T(8,128)(2,1)S(1)}, bf16[128,1792]{1,0:T(8,128)(2,1)}, u32[]{:S(2)}, u32[]{:S(2)}) collective-permute-start(bf16[128,1792]{1,0:T(8,128)(2,1)S(1)} %collective-permute-done.10.rest_1_), channel_id=1, source_target_pairs={{0,2},{2,4},{4,6},{6,7},{7,5},{5,3},{3,1},{1,0},{8,10},{10,12},{12... | collective-permute-start | bytes 1376264 | tf_op jit(solution)/shard_map/ppermute | solution.py:31
  54.7 13.6 %collective-permute-start.13 = (bf16[128,1792]{1,0:T(8,128)(2,1)}, bf16[128,1792]{1,0:T(8,128)(2,1)}, u32[]{:S(2)}, u32[]{:S(2)}) collective-permute-start(bf16[128,1792]{1,0:T(8,128)(2,1)} %collective-permute-done.11.rest_2_), channel_id=1, source_target_pairs={{0,1},{2,0},{4,2},{6,4},{7,6},{5,7},{3,5},{1,3},{8,9},{10,8},{12,1... | collective-permute-start | bytes 1376264 | tf_op jit(solution)/shard_map/ppermute | solution.py:31
  57.0 2.1 %copy-start.5 = (f32[4,128]{1,0:T(4,128)S(1)}, f32[4,128]{1,0:T(4,128)}, u32[]{:S(2)}) copy-start(f32[4,128]{1,0:T(4,128)} %taps_x.3) | copy-start | bytes 6148
  57.0 2.1 %copy-start.6 = (f32[4,128]{1,0:T(4,128)S(1)}, f32[4,128]{1,0:T(4,128)}, u32[]{:S(2)}) copy-start(f32[4,128]{1,0:T(4,128)} %taps_bc.3) | copy-start | bytes 6148
  57.5 2.2 %collective-permute-start.9 = (bf16[8,256]{1,0:T(8,128)(2,1)S(1)}, bf16[8,256]{1,0:T(8,128)(2,1)S(1)}, u32[]{:S(2)}, u32[]{:S(2)}) collective-permute-start(bf16[8,256]{1,0:T(8,128)(2,1)S(1)} %slice.44), channel_id=1, source_target_pairs={{0,8},{8,16},{16,24},{1,9},{9,17},{17,25},{2,10},{10,18},{18,26},{... | collective-permute-start | bytes 12296 | tf_op jit(solution)/shard_map/ppermute | solution.py:348
  68.2 13.4 %collective-permute-start.15 = (bf16[128,1792]{1,0:T(8,128)(2,1)}, bf16[128,1792]{1,0:T(8,128)(2,1)S(1)}, u32[]{:S(2)}, u32[]{:S(2)}) collective-permute-start(bf16[128,1792]{1,0:T(8,128)(2,1)} %collective-permute-done.12.rest_3_), channel_id=1, source_target_pairs={{0,2},{2,4},{4,6},{6,7},{7,5},{5,3},{3,1},{1,0},{8,10},{10,12},{12... | collective-permute-start | bytes 1376264 | tf_op jit(solution)/shard_map/ppermute | solution.py:31
  69.8 13.1 %collective-permute-start.16 = (bf16[128,1792]{1,0:T(8,128)(2,1)}, bf16[128,1792]{1,0:T(8,128)(2,1)S(1)}, u32[]{:S(2)}, u32[]{:S(2)}) collective-permute-start(bf16[128,1792]{1,0:T(8,128)(2,1)} %collective-permute-done.13.rest_4_), channel_id=1, source_target_pairs={{0,1},{2,0},{4,2},{6,4},{7,6},{5,7},{3,5},{1,3},{8,9},{10,8},{12,1... | collective-permute-start | bytes 1376264 | tf_op jit(solution)/shard_map/ppermute | solution.py:31
  72.1 14.1 %all-to-all-start = ((bf16[8,64,128]{2,1,0:T(8,128)(2,1)}), bf16[8,64,128]{2,1,0:T(8,128)(2,1)S(1)}, u32[]{:S(2)}, u32[]{:S(2)}) async-start(bf16[8,64,128]{2,1,0:T(8,128)(2,1)} %bitcast.7), calls=%async_computation | async-start | bytes 262144 | tf_op jit(solution)/shard_map/all_to_all | solution.py:380
  82.9 7.0 %collective-permute-start.17 = (bf16[64,1792]{1,0:T(8,128)(2,1)S(1)}, bf16[64,1792]{1,0:T(8,128)(2,1)S(1)}, u32[]{:S(2)}, u32[]{:S(2)}) collective-permute-start(bf16[64,1792]{1,0:T(8,128)(2,1)S(1)} %get-tuple-element.69), channel_id=1, source_target_pairs={{0,2},{2,4},{4,6},{6,7},{7,5},{5,3},{3,1},{1,0},{8,10},{10,12},{12... | collective-permute-start | bytes 688136 | tf_op jit(solution)/shard_map/ppermute | solution.py:31
  85.1 6.0 %collective-permute-start.18 = (bf16[64,1792]{1,0:T(8,128)(2,1)S(1)}, bf16[64,1792]{1,0:T(8,128)(2,1)S(1)}, u32[]{:S(2)}, u32[]{:S(2)}) collective-permute-start(bf16[64,1792]{1,0:T(8,128)(2,1)S(1)} %get-tuple-element.70), channel_id=1, source_target_pairs={{0,1},{2,0},{4,2},{6,4},{7,6},{5,7},{3,5},{1,3},{8,9},{10,8},{12,1... | collective-permute-start | bytes 688136 | tf_op jit(solution)/shard_map/ppermute | solution.py:31
  86.2 1.3 %collective-permute-start.14 = (bf16[8,64,128]{2,1,0:T(8,128)(2,1)S(1)}, bf16[8,64,128]{2,1,0:T(8,128)(2,1)S(1)}, u32[]{:S(2)}, u32[]{:S(2)}) collective-permute-start(bf16[8,64,128]{2,1,0:T(8,128)(2,1)S(1)} %all-to-all-done.mine), channel_id=1, source_target_pairs={{0,8},{8,0},{16,24},{24,16},{1,9},{9,1},{17,25},{25,17},{2,10},{10... | collective-permute-start | bytes 393224 | tf_op jit(solution)/shard_map/ppermute | solution.py:382
  91.4 1.6 %collective-permute-start.19 = (bf16[64,1792]{1,0:T(8,128)(2,1)S(1)}, bf16[64,1792]{1,0:T(8,128)(2,1)S(1)}, u32[]{:S(2)}, u32[]{:S(2)}) collective-permute-start(bf16[64,1792]{1,0:T(8,128)(2,1)S(1)} %get-tuple-element.72), channel_id=1, source_target_pairs={{0,8},{8,0},{16,24},{24,16},{1,9},{9,1},{17,25},{25,17},{2,10},{10... | collective-permute-start | bytes 688136 | tf_op jit(solution)/shard_map/ppermute | solution.py:394

commit v17 on v16

--- a/solution.py
+++ b/solution.py
@@ -366,7 +366,7 @@
     tok_own = tok_rows // n_tensor
 
     w_steps = [(w_forth, w_back)]
-    orders = [far, messages]
+    orders = [(far, projs[-1]), messages]
     for step in range(2, last + 1):
         if step - 2 < len(orders):
             w_forth, w_back = after((w_forth, w_back), orders[step - 2])

time: 94.3 us -> 95.2 us (level)
  waiting for transfers between devices: 37.9 us -> 35.4 us
  local copies, waits for them, and re-layouts: 5.91 us -> 7.69 us
  Pallas kernels: 16.1 us -> 17.7 us
    unnamed x26 -> x30, local copies, waits for them, and re-layouts: 3.74 us -> 5.52 us
    ppermute x16, waiting for transfers between devices: 33.9 us -> 32.1 us  [ring_shift(): lax.ppermute(block, 'tensor', [(order[i], order[(i + step) % n]) for i in...]
  transfers between devices with their start and end apart: 21 -> 21, of which waited for: 14 -> 14; matrix products, arithmetic and copies ran while one was open for 4% -> 4% of each run, Pallas kernels for 16% -> 17%
where the time goes in v17:
time: 95.2 us; the launch traced here: 94.6 us
  waiting for transfers between devices  35.4 us (37%)
  starting transfers between devices  25 us (26%)
  Pallas kernels  17.7 us (19%)
  local copies, waits for them, and re-layouts  7.69 us (8%)
  blocking collectives  7.22 us (8%)
  matrix products  1.12 us (1%)
    ppermute x16, waiting for transfers between devices, ring_shift(): lax.ppermute(block, 'tensor', [(order[i], order[(i + step) % n]) for i in...  32.1 us
    ppermute x16, starting transfers between devices, ring_shift(): lax.ppermute(block, 'tensor', [(order[i], order[(i + step) % n]) for i in...  17.4 us
    pallas_call x4, Pallas kernels, local(): call(functools.partial(project, [distance for distance, _ in arrived], ah...  8.45 us
    all_gather x1, blocking collectives, local(): messages = lax.all_gather(message, 'seq')  7.22 us
    unnamed x30, local copies, waits for them, and re-layouts  5.52 us
    all_to_all x1, starting transfers between devices, local(): mine = lax.all_to_all(blocks, 'tensor', 0, 0)  4.79 us
    pallas_call x1, Pallas kernels, local(): call(functools.partial(product_early, distances), shape(2 * tok_own, colu...  2.14 us
    pallas_call x1, Pallas kernels, local(): call(functools.partial(finish, heads, rows), shape(tok_rows, width, kind=...  1.92 us
  transfers between devices with their start and end apart: 21, of which 14 were waited for; matrix products, arithmetic and copies ran while one was open for 4% of the time, Pallas kernels for 17%

profile of v17, /device:TPU:0, one launch (start us, length us, event | category | flops | bytes accessed | tf_op | source)
XLA Modules:
  0.0 94.6 jit_solution(9451423290067213074)
XLA Ops:
  0.0 3.0 %collective-permute-start = (bf16[448,512]{1,0:T(8,128)(2,1)}, bf16[448,512]{1,0:T(8,128)(2,1)}, u32[]{:S(2)}, u32[]{:S(2)}) collective-permute-start(bf16[448,512]{1,0:T(8,128)(2,1)} %bitcast.12), channel_id=1, source_target_pairs={{0,2},{2,4},{4,6},{6,7},{7,5},{5,3},{3,1},{1,0},{8,10},{10,12},{12... | collective-permute-start | bytes 1376264 | tf_op jit(solution)/shard_map/ppermute | solution.py:31
  3.0 0.8 slice.33
  3.8 1.4 %collective-permute-start.3 = (s32[8]{0:T(128)S(1)}, s32[8]{0:T(128)S(1)}, u32[]{:S(2)}, u32[]{:S(2)}) collective-permute-start(s32[8]{0:T(128)S(1)} %slice.33), channel_id=1, source_target_pairs={{0,8},{8,16},{16,24},{1,9},{9,17},{17,25},{2,10},{10,18},{18,26},{... | collective-permute-start | bytes 104 | tf_op jit(solution)/shard_map/ppermute | solution.py:306
  5.2 1.1 %convolution_bitcast_fusion.refs_3_.refs_4_ = bf16[3584,128]{1,0:T(8,128)(2,1)S(1)} fusion(bf16[2,128]{1,0:T(2,128)(2,1)} %constant.25.clone, bf16[3584,2]{0,1:T(2,128)(2,1)S(1)} %copy-done), kind=kOutput, calls=%fused_computation | convolution fusion | flops 1835008 | bytes 932352 | tf_op jit(solution)/shard_map/dot_general | solution.py:297
  6.4 1.5 %copy-done.1 = bf16[2,3584,128]{2,1,0:T(8,128)(2,1)S(1)} copy-done((bf16[2,3584,128]{2,1,0:T(8,128)(2,1)S(1)}, bf16[2,3584,128]{2,1,0:T(8,128)(2,1)}, u32[]{:S(2)}) %copy-start.1) | copy-done | bytes 1835032
  7.9 1.2 %copy-done.2 = bf16[3584,128]{1,0:T(8,128)(2,1)S(1)} copy-done((bf16[3584,128]{1,0:T(8,128)(2,1)S(1)}, bf16[3584,128]{1,0:T(8,128)(2,1)}, u32[]{:S(2)}) %copy-start.2) | copy-done | bytes 917528
  9.1 1.0 %copy-done.4 = bf16[512,448]{0,1:T(8,128)(2,1)S(1)} copy-done((bf16[512,448]{0,1:T(8,128)(2,1)S(1)}, bf16[512,448]{0,1:T(8,128)(2,1)}, u32[]{:S(2)}) %copy-start.4) | copy-done | bytes 458776
  10.1 0.6 shard_map.127.refs_5_
  10.7 3.1 %collective-permute-done.refs_0_ = bf16[448,512]{1,0:T(8,128)(2,1)} collective-permute-done((bf16[448,512]{1,0:T(8,128)(2,1)}, bf16[448,512]{1,0:T(8,128)(2,1)}, u32[]{:S(2)}, u32[]{:S(2)}) %collective-permute-start) | collective-permute-done | bytes 458784 | tf_op jit(solution)/shard_map/ppermute | solution.py:31
  13.8 1.8 %collective-permute-start.1 = (bf16[448,512]{1,0:T(8,128)(2,1)}, bf16[448,512]{1,0:T(8,128)(2,1)S(1)}, u32[]{:S(2)}, u32[]{:S(2)}) collective-permute-start(bf16[448,512]{1,0:T(8,128)(2,1)} %collective-permute-done.refs_0_), channel_id=1, source_target_pairs={{0,2},{2,4},{4,6},{6,7},{7,5},{5,3},{3,1},{1,0},{8,10},{10,12},{12... | collective-permute-start | bytes 1376264 | tf_op jit(solution)/shard_map/ppermute | solution.py:31
  15.6 0.2 collective-permute-start.5
  15.8 0.6 fusion
  16.4 0.1 slice.36
  16.5 0.1 broadcast_in_dim.27
  16.5 0.1 broadcast_in_dim_reshape.9.bias
  16.6 0.1 broadcast_in_dim.28
  16.7 0.1 broadcast_in_dim_reshape.10.rate
  16.8 0.1 broadcast_in_dim.29
  16.9 0.1 broadcast_in_dim_reshape.11.skip
  16.9 0.1 pad_add_fusion
  17.1 3.1 %shard_map.128.refs_5_ = f32[512,512]{1,0:T(8,128)S(1)} custom-call(bf16[448,512]{1,0:T(8,128)(2,1)} %collective-permute-done.refs_0_, bf16[448,512]{1,0:T(8,128)(2,1)} %collective-permute-done.2.refs_1_, bf16[2,3584,128]{2,1,0:T(8,128)(2,1)} %refs_2_.7, bf16[3584,128]{1,0:T(8,128)(2,1)S(1)} %copy-done.3, ...), custom_call_target="tpu_custom_call" | custom-call | flops 1000000000 | bytes 2097152 | tf_op jit(solution)/shard_map/pallas_call | solution.py:334
  20.2 5.8 %collective-permute-done.1.refs_0_ = bf16[448,512]{1,0:T(8,128)(2,1)S(1)} collective-permute-done((bf16[448,512]{1,0:T(8,128)(2,1)}, bf16[448,512]{1,0:T(8,128)(2,1)S(1)}, u32[]{:S(2)}, u32[]{:S(2)}) %collective-permute-start.1) | collective-permute-done | bytes 458784 | tf_op jit(solution)/shard_map/ppermute | solution.py:31
  25.9 1.6 %collective-permute-start.4 = (bf16[448,512]{1,0:T(8,128)(2,1)S(1)}, bf16[448,512]{1,0:T(8,128)(2,1)S(1)}, u32[]{:S(2)}, u32[]{:S(2)}) collective-permute-start(bf16[448,512]{1,0:T(8,128)(2,1)S(1)} %collective-permute-done.1.refs_0_), channel_id=1, source_target_pairs={{0,2},{2,4},{4,6},{6,7},{7,5},{5,3},{3,1},{1,0},{8,10},{10,12},{12... | collective-permute-start | bytes 1376264 | tf_op jit(solution)/shard_map/ppermute | solution.py:31
  27.5 0.4 collective-permute-start.6
  28.0 0.1 multiply_convert_fusion.rest_0_
  28.1 1.6 %collective-permute-start.10 = (bf16[128,1792]{1,0:T(8,128)(2,1)S(1)}, bf16[128,1792]{1,0:T(8,128)(2,1)S(1)}, u32[]{:S(2)}, u32[]{:S(2)}) collective-permute-start(bf16[128,1792]{1,0:T(8,128)(2,1)S(1)} %multiply_convert_fusion.rest_0_), channel_id=1, source_target_pairs={{0,2},{2,4},{4,6},{6,7},{7,5},{5,3},{3,1},{1,0},{8,10},{10,12},{12... | collective-permute-start | bytes 1376264 | tf_op jit(solution)/shard_map/ppermute | solution.py:31
  29.8 0.4 collective-permute-start.11
  30.2 2.9 %shard_map.129.refs_5_ = f32[512,512]{1,0:T(8,128)S(1)} custom-call(bf16[448,512]{1,0:T(8,128)(2,1)S(1)} %collective-permute-done.1.refs_0_, bf16[448,512]{1,0:T(8,128)(2,1)} %collective-permute-done.5.refs_1_, bf16[2,3584,128]{2,1,0:T(8,128)(2,1)} %refs_2_.7, bf16[3584,128]{1,0:T(8,128)(2,1)S(1)} %copy-done.3, ...), custom_call_target="tpu_custom_call" | custom-call | flops 1000000000 | bytes 2097152 | tf_op jit(solution)/shard_map/pallas_call | solution.py:334
  33.1 6.3 %collective-permute-done.4.forth.refs_0_ = bf16[448,512]{1,0:T(8,128)(2,1)S(1)} collective-permute-done((bf16[448,512]{1,0:T(8,128)(2,1)S(1)}, bf16[448,512]{1,0:T(8,128)(2,1)S(1)}, u32[]{:S(2)}, u32[]{:S(2)}) %collective-permute-start.4) | collective-permute-done | bytes 458784 | tf_op jit(solution)/shard_map/ppermute | solution.py:31
  39.4 1.8 %collective-permute-done.6.back.refs_1_ = bf16[448,512]{1,0:T(8,128)(2,1)S(1)} collective-permute-done((bf16[448,512]{1,0:T(8,128)(2,1)}, bf16[448,512]{1,0:T(8,128)(2,1)S(1)}, u32[]{:S(2)}, u32[]{:S(2)}) %collective-permute-start.6) | collective-permute-done | bytes 458784 | tf_op jit(solution)/shard_map/ppermute | solution.py:31
  41.2 1.6 %collective-permute-start.7 = (bf16[224,512]{1,0:T(8,128)(2,1)S(1)}, bf16[224,512]{1,0:T(8,128)(2,1)S(1)}, u32[]{:S(2)}, u32[]{:S(2)}) collective-permute-start(bf16[224,512]{1,0:T(8,128)(2,1)S(1)} %get-tuple-element.45), channel_id=1, source_target_pairs={{0,2},{2,4},{4,6},{6,7},{7,5},{5,3},{3,1},{1,0},{8,10},{10,12},{12... | collective-permute-start | bytes 688136 | tf_op jit(solution)/shard_map/ppermute | solution.py:31
  42.9 0.5 collective-permute-start.8
  43.3 1.9 %shard_map.131 = (f32[512,512]{1,0:T(8,128)S(1)}, bf16[448,512]{1,0:T(8,128)(2,1)S(1)}) custom-call(bf16[448,512]{1,0:T(8,128)(2,1)S(1)} %collective-permute-done.4.forth.refs_0_, bf16[448,512]{1,0:T(8,128)(2,1)S(1)} %collective-permute-done.6.back.refs_1_, bf16[2,3584,128]{2,1,0:T(8,128)(2,1)} %refs_2_.7, bf16[3584,128]{1,0:T(8,128)(2,1)S(1)} %copy-done.3, ...), custom_call_target="tpu_custom_call" | custom-call | flops 1000000000 | bytes 2097152 | tf_op jit(solution)/shard_map/pallas_call | solution.py:334
  45.2 4.0 %collective-permute-done.10.rest_1_ = bf16[128,1792]{1,0:T(8,128)(2,1)S(1)} collective-permute-done((bf16[128,1792]{1,0:T(8,128)(2,1)S(1)}, bf16[128,1792]{1,0:T(8,128)(2,1)S(1)}, u32[]{:S(2)}, u32[]{:S(2)}) %collective-permute-start.10) | collective-permute-done | bytes 458784 | tf_op jit(solution)/shard_map/ppermute | solution.py:31
  49.2 1.5 %collective-permute-done.11.rest_2_ = bf16[128,1792]{1,0:T(8,128)(2,1)} collective-permute-done((bf16[128,1792]{1,0:T(8,128)(2,1)S(1)}, bf16[128,1792]{1,0:T(8,128)(2,1)}, u32[]{:S(2)}, u32[]{:S(2)}) %collective-permute-start.11) | collective-permute-done | bytes 458784 | tf_op jit(solution)/shard_map/ppermute | solution.py:31
  50.7 1.1 %collective-permute-done.7.top = bf16[224,512]{1,0:T(8,128)(2,1)S(1)} collective-permute-done((bf16[224,512]{1,0:T(8,128)(2,1)S(1)}, bf16[224,512]{1,0:T(8,128)(2,1)S(1)}, u32[]{:S(2)}, u32[]{:S(2)}) %collective-permute-start.7) | collective-permute-done | bytes 229408 | tf_op jit(solution)/shard_map/ppermute | solution.py:31
  51.8 1.3 %collective-permute-done.8.bottom = bf16[224,512]{1,0:T(8,128)(2,1)S(1)} collective-permute-done((bf16[224,512]{1,0:T(8,128)(2,1)S(1)}, bf16[224,512]{1,0:T(8,128)(2,1)S(1)}, u32[]{:S(2)}, u32[]{:S(2)}) %collective-permute-start.8) | collective-permute-done | bytes 229408 | tf_op jit(solution)/shard_map/ppermute | solution.py:31
  53.1 1.6 %collective-permute-start.12 = (bf16[128,1792]{1,0:T(8,128)(2,1)S(1)}, bf16[128,1792]{1,0:T(8,128)(2,1)}, u32[]{:S(2)}, u32[]{:S(2)}) collective-permute-start(bf16[128,1792]{1,0:T(8,128)(2,1)S(1)} %collective-permute-done.10.rest_1_), channel_id=1, source_target_pairs={{0,2},{2,4},{4,6},{6,7},{7,5},{5,3},{3,1},{1,0},{8,10},{10,12},{12... | collective-permute-start | bytes 1376264 | tf_op jit(solution)/shard_map/ppermute | solution.py:31
  54.7 0.5 collective-permute-start.13
  55.1 0.5 shard_map.132.proj
  55.6 1.3 %collective-permute-start.9 = (bf16[8,256]{1,0:T(8,128)(2,1)S(1)}, bf16[8,256]{1,0:T(8,128)(2,1)S(1)}, u32[]{:S(2)}, u32[]{:S(2)}) collective-permute-start(bf16[8,256]{1,0:T(8,128)(2,1)S(1)} %slice.44), channel_id=1, source_target_pairs={{0,8},{8,16},{16,24},{1,9},{9,17},{17,25},{2,10},{10,18},{18,26},{... | collective-permute-start | bytes 12296 | tf_op jit(solution)/shard_map/ppermute | solution.py:348
  56.9 0.1 copy.16.seg_ext.seg_ext_b
  57.1 0.1 copy.17.seg_ext.seg_ext_a
  57.2 0.6 shard_map.133
  57.8 1.3 %shard_map.134 = (f32[256,128]{1,0:T(8,128)S(1)}, f32[256,128]{1,0:T(8,128)S(1)}, f32[256,128]{1,0:T(8,128)S(1)}, f32[256,128]{1,0:T(8,128)S(1)}, f32[256,128]{1...) custom-call(f32[512,512]{1,0:T(8,128)S(1)} %shard_map.132.proj, ...), custom_call_target="tpu_custom_call" | custom-call | flops 10000000 | bytes 2097152 | tf_op jit(solution)/shard_map/pallas_call | solution.py:356
  59.1 7.2 %all-gather = f32[288,128]{1,0:T(8,128)S(1)} all-gather(f32[72,128]{1,0:T(8,128)S(1)} %get-tuple-element.50), channel_id=2, replica_groups=mesh['seq'=4,'tensor'=8] {'seq'}, dimensions={0}, use_global_device_ids=true | all-gather | bytes 184320 | tf_op jit(solution)/shard_map/all_gather | solution.py:361
  66.3 0.8 copy-done.5
  67.1 1.6 %collective-permute-start.15 = (bf16[128,1792]{1,0:T(8,128)(2,1)}, bf16[128,1792]{1,0:T(8,128)(2,1)S(1)}, u32[]{:S(2)}, u32[]{:S(2)}) collective-permute-start(bf16[128,1792]{1,0:T(8,128)(2,1)} %collective-permute-done.12.rest_3_), channel_id=1, source_target_pairs={{0,2},{2,4},{4,6},{6,7},{7,5},{5,3},{3,1},{1,0},{8,10},{10,12},{12... | collective-permute-start | bytes 1376264 | tf_op jit(solution)/shard_map/ppermute | solution.py:31
  68.7 0.4 collective-permute-start.16
  69.1 1.9 %shard_map.135 = bf16[512,128]{1,0:T(8,128)(2,1)} custom-call(s32[1,1]{1,0:T(1,128)} %bitcast.seg_first, f32[4,72,128]{2,1,0:T(8,128)S(1)} %bitcast.11, s32[264,1]{1,0:T(8,128)S(1)} %copy.17.seg_ext.seg_ext_a, s32[1,256]{1,0:T(1,128)S(1)} %bitcast.16, s32[264,1]{1,0:T(8,128)S(1)} %copy.16.seg_ext.seg_ext_b, s32[1,256]{1,0:T(1,128)S(1)} %bitcast.15, ...), custom_call_target="tpu_custom_call" | custom-call | flops 10000000 | bytes 2097152 | tf_op jit(solution)/shard_map/pallas_call | solution.py:362
  71.0 4.8 %all-to-all-start = ((bf16[8,64,128]{2,1,0:T(8,128)(2,1)}), bf16[8,64,128]{2,1,0:T(8,128)(2,1)S(1)}, u32[]{:S(2)}, u32[]{:S(2)}) async-start(bf16[8,64,128]{2,1,0:T(8,128)(2,1)} %bitcast.7), calls=%async_computation | async-start | bytes 262144 | tf_op jit(solution)/shard_map/all_to_all | solution.py:380
  75.8 4.7 %collective-permute-done.15.rest_5_.forth = bf16[128,1792]{1,0:T(8,128)(2,1)S(1)} collective-permute-done((bf16[128,1792]{1,0:T(8,128)(2,1)}, bf16[128,1792]{1,0:T(8,128)(2,1)S(1)}, u32[]{:S(2)}, u32[]{:S(2)}) %collective-permute-start.15) | collective-permute-done | bytes 458784 | tf_op jit(solution)/shard_map/ppermute | solution.py:31
  80.5 1.2 %collective-permute-done.16.rest_6_.back = bf16[128,1792]{1,0:T(8,128)(2,1)S(1)} collective-permute-done((bf16[128,1792]{1,0:T(8,128)(2,1)}, bf16[128,1792]{1,0:T(8,128)(2,1)S(1)}, u32[]{:S(2)}, u32[]{:S(2)}) %collective-permute-start.16) | collective-permute-done | bytes 458784 | tf_op jit(solution)/shard_map/ppermute | solution.py:31
  81.7 0.8 shard_map.137
  82.5 2.1 %collective-permute-start.17 = (bf16[64,1792]{1,0:T(8,128)(2,1)}, bf16[64,1792]{1,0:T(8,128)(2,1)S(1)}, u32[]{:S(2)}, u32[]{:S(2)}) collective-permute-start(bf16[64,1792]{1,0:T(8,128)(2,1)} %get-tuple-element.69), channel_id=1, source_target_pairs={{0,2},{2,4},{4,6},{6,7},{7,5},{5,3},{3,1},{1,0},{8,10},{10,12},{12... | collective-permute-start | bytes 688136 | tf_op jit(solution)/shard_map/ppermute | solution.py:31
  84.6 0.4 all-to-all-done.mine
  85.1 1.3 %collective-permute-done.14.other = bf16[8,64,128]{2,1,0:T(8,128)(2,1)S(1)} collective-permute-done((bf16[8,64,128]{2,1,0:T(8,128)(2,1)S(1)}, bf16[8,64,128]{2,1,0:T(8,128)(2,1)S(1)}, u32[]{:S(2)}, u32[]{:S(2)}) %collective-permute-start.14) | collective-permute-done | bytes 131104 | tf_op jit(solution)/shard_map/ppermute | solution.py:382
  86.4 1.0 %copy-done.6 = bf16[128,1792]{1,0:T(8,128)(2,1)S(1)} copy-done((bf16[128,1792]{1,0:T(8,128)(2,1)S(1)}, bf16[128,1792]{1,0:T(8,128)(2,1)}, u32[]{:S(2)}) %copy-start.6) | copy-done | bytes 458776
  87.4 2.1 %shard_map.136.total = f32[128,1792]{1,0:T(8,128)S(1)} custom-call(bf16[8,64,128]{2,1,0:T(8,128)(2,1)S(1)} %all-to-all-done.mine, bf16[8,64,128]{2,1,0:T(8,128)(2,1)S(1)} %collective-permute-done.14.other, bf16[128,1792]{1,0:T(8,128)(2,1)S(1)} %multiply_convert_fusion.rest_0_, bf16[128,1792]{1,0:T(8,128)(2,1)S(1)} %collective-permute-done.10.rest_1_, ...), custom_call_target="tpu_custom_call" | custom-call | flops 1 | bytes 1 | tf_op jit(solution)/shard_map/pallas_call | solution.py:387
  89.6 1.4 %collective-permute-done.18.bottom = bf16[64,1792]{1,0:T(8,128)(2,1)} collective-permute-done((bf16[64,1792]{1,0:T(8,128)(2,1)}, bf16[64,1792]{1,0:T(8,128)(2,1)}, u32[]{:S(2)}, u32[]{:S(2)}) %collective-permute-start.18) | collective-permute-done | bytes 229408 | tf_op jit(solution)/shard_map/ppermute | solution.py:31
  91.0 1.2 %shard_map.138 = (bf16[64,1792]{1,0:T(8,128)(2,1)S(1)}, bf16[64,1792]{1,0:T(8,128)(2,1)S(1)}) custom-call(bf16[8,64,128]{2,1,0:T(8,128)(2,1)S(1)} %all-to-all-done.mine, bf16[8,64,128]{2,1,0:T(8,128)(2,1)S(1)} %collective-permute-done.14.other, f32[128,1792]{1,0:T(8,128)S(1)} %shard_map.136.total, bf16[64,1792]{1,0:T(8,128)(2,1)S(1)} %collective-permute-done.17.top, ...), custom_call_target="tpu_custom_call" | custom-call | flops 100000000 | bytes 2097152 | tf_op jit(solution)/shard_map/pallas_call | solution.py:391
  92.2 0.1 collective-permute-start.19
  92.3 1.5 %collective-permute-done.19.other = bf16[64,1792]{1,0:T(8,128)(2,1)S(1)} collective-permute-done((bf16[64,1792]{1,0:T(8,128)(2,1)S(1)}, bf16[64,1792]{1,0:T(8,128)(2,1)S(1)}, u32[]{:S(2)}, u32[]{:S(2)}) %collective-permute-start.19) | collective-permute-done | bytes 229408 | tf_op jit(solution)/shard_map/ppermute | solution.py:394
  93.7 0.8 shard_map.139
  (41 shorter events, 0.1 us)
Async XLA Ops:
  0.0 5.2 %copy-start = (bf16[3584,2]{0,1:T(2,128)(2,1)S(1)}, bf16[3584,2]{0,1:T(2,128)(2,1)}, u32[]{:S(2)}) copy-start(bf16[3584,2]{0,1:T(2,128)(2,1)} %param.16) | copy-start | bytes 43012
  0.0 13.8 %collective-permute-start = (bf16[448,512]{1,0:T(8,128)(2,1)}, bf16[448,512]{1,0:T(8,128)(2,1)}, u32[]{:S(2)}, u32[]{:S(2)}) collective-permute-start(bf16[448,512]{1,0:T(8,128)(2,1)} %bitcast.12), channel_id=1, source_target_pairs={{0,2},{2,4},{4,6},{6,7},{7,5},{5,3},{3,1},{1,0},{8,10},{10,12},{12... | collective-permute-start | bytes 1376264 | tf_op jit(solution)/shard_map/ppermute | solution.py:31
  3.0 12.6 %collective-permute-start.2 = (bf16[448,512]{1,0:T(8,128)(2,1)}, bf16[448,512]{1,0:T(8,128)(2,1)}, u32[]{:S(2)}, u32[]{:S(2)}) collective-permute-start(bf16[448,512]{1,0:T(8,128)(2,1)} %bitcast.13), channel_id=1, source_target_pairs={{0,1},{2,0},{4,2},{6,4},{7,6},{5,7},{3,5},{1,3},{8,9},{10,8},{12,1... | collective-permute-start | bytes 1376264 | tf_op jit(solution)/shard_map/ppermute | solution.py:31
  3.8 13.2 %collective-permute-start.3 = (s32[8]{0:T(128)S(1)}, s32[8]{0:T(128)S(1)}, u32[]{:S(2)}, u32[]{:S(2)}) collective-permute-start(s32[8]{0:T(128)S(1)} %slice.33), channel_id=1, source_target_pairs={{0,8},{8,16},{16,24},{1,9},{9,17},{17,25},{2,10},{10,18},{18,26},{... | collective-permute-start | bytes 104 | tf_op jit(solution)/shard_map/ppermute | solution.py:306
  6.4 1.5 %copy-start.1 = (bf16[2,3584,128]{2,1,0:T(8,128)(2,1)S(1)}, bf16[2,3584,128]{2,1,0:T(8,128)(2,1)}, u32[]{:S(2)}) copy-start(bf16[2,3584,128]{2,1,0:T(8,128)(2,1)} %refs_2_.7) | copy-start | bytes 5505028
  7.9 1.2 %copy-start.2 = (bf16[3584,128]{1,0:T(8,128)(2,1)S(1)}, bf16[3584,128]{1,0:T(8,128)(2,1)}, u32[]{:S(2)}) copy-start(bf16[3584,128]{1,0:T(8,128)(2,1)} %refs_3_.5) | copy-start | bytes 2752516
  9.1 1.0 %copy-start.4 = (bf16[512,448]{0,1:T(8,128)(2,1)S(1)}, bf16[512,448]{0,1:T(8,128)(2,1)}, u32[]{:S(2)}) copy-start(bf16[512,448]{0,1:T(8,128)(2,1)} %param.13) | copy-start | bytes 1376260
  10.1 5.7 %copy-start.10 = (s32[512]{0:T(512)S(1)}, s32[512]{0:T(512)}, u32[]{:S(2)}) copy-start(s32[512]{0:T(512)} %param.24) | copy-start | bytes 6148
  10.1 6.4 %copy-start.12 = (f32[2]{0:T(128)S(1)}, f32[2]{0:T(128)}, u32[]{:S(2)}) copy-start(f32[2]{0:T(128)} %param.17) | copy-start | bytes 28
  10.1 6.6 %copy-start.13 = (f32[2]{0:T(128)S(1)}, f32[2]{0:T(128)}, u32[]{:S(2)}) copy-start(f32[2]{0:T(128)} %param.18) | copy-start | bytes 28
  10.1 6.7 %copy-start.14 = (f32[2]{0:T(128)S(1)}, f32[2]{0:T(128)}, u32[]{:S(2)}) copy-start(f32[2]{0:T(128)} %param.19) | copy-start | bytes 28
  10.1 7.0 %copy-start.3 = (bf16[3584,128]{1,0:T(8,128)(2,1)S(1)}, bf16[3584,128]{1,0:T(8,128)(2,1)}, u32[]{:S(2)}) copy-start(bf16[3584,128]{1,0:T(8,128)(2,1)} %refs_3_.5) | copy-start | bytes 2752516
  13.8 12.2 %collective-permute-start.1 = (bf16[448,512]{1,0:T(8,128)(2,1)}, bf16[448,512]{1,0:T(8,128)(2,1)S(1)}, u32[]{:S(2)}, u32[]{:S(2)}) collective-permute-start(bf16[448,512]{1,0:T(8,128)(2,1)} %collective-permute-done.refs_0_), channel_id=1, source_target_pairs={{0,2},{2,4},{4,6},{6,7},{7,5},{5,3},{3,1},{1,0},{8,10},{10,12},{12... | collective-permute-start | bytes 1376264 | tf_op jit(solution)/shard_map/ppermute | solution.py:31
  15.6 11.9 %collective-permute-start.5 = (bf16[448,512]{1,0:T(8,128)(2,1)}, bf16[448,512]{1,0:T(8,128)(2,1)}, u32[]{:S(2)}, u32[]{:S(2)}) collective-permute-start(bf16[448,512]{1,0:T(8,128)(2,1)} %collective-permute-done.2.refs_1_), channel_id=1, source_target_pairs={{0,1},{2,0},{4,2},{6,4},{7,6},{5,7},{3,5},{1,3},{8,9},{10,8},{12,1... | collective-permute-start | bytes 1376264 | tf_op jit(solution)/shard_map/ppermute | solution.py:31
  17.0 10.9 %copy-start.9 = (bf16[128,3584]{1,0:T(8,128)(2,1)S(1)}, bf16[128,3584]{1,0:T(8,128)(2,1)}, u32[]{:S(2)}) copy-start(bf16[128,3584]{1,0:T(8,128)(2,1)} %param.23) | copy-start | bytes 2752516
  17.0 10.9 %copy-start.11 = (f32[128]{0:T(128)S(1)}, f32[128]{0:T(128)}, u32[]{:S(2)}) copy-start(f32[128]{0:T(128)} %param.22) | copy-start | bytes 1540
  25.9 13.5 %collective-permute-start.4 = (bf16[448,512]{1,0:T(8,128)(2,1)S(1)}, bf16[448,512]{1,0:T(8,128)(2,1)S(1)}, u32[]{:S(2)}, u32[]{:S(2)}) collective-permute-start(bf16[448,512]{1,0:T(8,128)(2,1)S(1)} %collective-permute-done.1.refs_0_), channel_id=1, source_target_pairs={{0,2},{2,4},{4,6},{6,7},{7,5},{5,3},{3,1},{1,0},{8,10},{10,12},{12... | collective-permute-start | bytes 1376264 | tf_op jit(solution)/shard_map/ppermute | solution.py:31
  27.5 13.7 %collective-permute-start.6 = (bf16[448,512]{1,0:T(8,128)(2,1)}, bf16[448,512]{1,0:T(8,128)(2,1)S(1)}, u32[]{:S(2)}, u32[]{:S(2)}) collective-permute-start(bf16[448,512]{1,0:T(8,128)(2,1)} %collective-permute-done.5.refs_1_), channel_id=1, source_target_pairs={{0,1},{2,0},{4,2},{6,4},{7,6},{5,7},{3,5},{1,3},{8,9},{10,8},{12,1... | collective-permute-start | bytes 1376264 | tf_op jit(solution)/shard_map/ppermute | solution.py:31
  28.1 21.1 %collective-permute-start.10 = (bf16[128,1792]{1,0:T(8,128)(2,1)S(1)}, bf16[128,1792]{1,0:T(8,128)(2,1)S(1)}, u32[]{:S(2)}, u32[]{:S(2)}) collective-permute-start(bf16[128,1792]{1,0:T(8,128)(2,1)S(1)} %multiply_convert_fusion.rest_0_), channel_id=1, source_target_pairs={{0,2},{2,4},{4,6},{6,7},{7,5},{5,3},{3,1},{1,0},{8,10},{10,12},{12... | collective-permute-start | bytes 1376264 | tf_op jit(solution)/shard_map/ppermute | solution.py:31
  29.8 21.0 %collective-permute-start.11 = (bf16[128,1792]{1,0:T(8,128)(2,1)S(1)}, bf16[128,1792]{1,0:T(8,128)(2,1)}, u32[]{:S(2)}, u32[]{:S(2)}) collective-permute-start(bf16[128,1792]{1,0:T(8,128)(2,1)S(1)} %multiply_convert_fusion.rest_0_), channel_id=1, source_target_pairs={{0,1},{2,0},{4,2},{6,4},{7,6},{5,7},{3,5},{1,3},{8,9},{10,8},{12,1... | collective-permute-start | bytes 1376264 | tf_op jit(solution)/shard_map/ppermute | solution.py:31
  41.2 10.6 %collective-permute-start.7 = (bf16[224,512]{1,0:T(8,128)(2,1)S(1)}, bf16[224,512]{1,0:T(8,128)(2,1)S(1)}, u32[]{:S(2)}, u32[]{:S(2)}) collective-permute-start(bf16[224,512]{1,0:T(8,128)(2,1)S(1)} %get-tuple-element.45), channel_id=1, source_target_pairs={{0,2},{2,4},{4,6},{6,7},{7,5},{5,3},{3,1},{1,0},{8,10},{10,12},{12... | collective-permute-start | bytes 688136 | tf_op jit(solution)/shard_map/ppermute | solution.py:31
  42.9 10.2 %collective-permute-start.8 = (bf16[224,512]{1,0:T(8,128)(2,1)S(1)}, bf16[224,512]{1,0:T(8,128)(2,1)S(1)}, u32[]{:S(2)}, u32[]{:S(2)}) collective-permute-start(bf16[224,512]{1,0:T(8,128)(2,1)S(1)} %get-tuple-element.46), channel_id=1, source_target_pairs={{0,1},{2,0},{4,2},{6,4},{7,6},{5,7},{3,5},{1,3},{8,9},{10,8},{12,1... | collective-permute-start | bytes 688136 | tf_op jit(solution)/shard_map/ppermute | solution.py:31
  53.1 13.2 %collective-permute-start.12 = (bf16[128,1792]{1,0:T(8,128)(2,1)S(1)}, bf16[128,1792]{1,0:T(8,128)(2,1)}, u32[]{:S(2)}, u32[]{:S(2)}) collective-permute-start(bf16[128,1792]{1,0:T(8,128)(2,1)S(1)} %collective-permute-done.10.rest_1_), channel_id=1, source_target_pairs={{0,2},{2,4},{4,6},{6,7},{7,5},{5,3},{3,1},{1,0},{8,10},{10,12},{12... | collective-permute-start | bytes 1376264 | tf_op jit(solution)/shard_map/ppermute | solution.py:31
  54.7 11.7 %collective-permute-start.13 = (bf16[128,1792]{1,0:T(8,128)(2,1)}, bf16[128,1792]{1,0:T(8,128)(2,1)S(1)}, u32[]{:S(2)}, u32[]{:S(2)}) collective-permute-start(bf16[128,1792]{1,0:T(8,128)(2,1)} %collective-permute-done.11.rest_2_), channel_id=1, source_target_pairs={{0,1},{2,0},{4,2},{6,4},{7,6},{5,7},{3,5},{1,3},{8,9},{10,8},{12,1... | collective-permute-start | bytes 1376264 | tf_op jit(solution)/shard_map/ppermute | solution.py:31
  55.1 2.1 %copy-start.7 = (f32[4,128]{1,0:T(4,128)S(1)}, f32[4,128]{1,0:T(4,128)}, u32[]{:S(2)}) copy-start(f32[4,128]{1,0:T(4,128)} %taps_x.3) | copy-start | bytes 6148
  55.1 2.1 %copy-start.8 = (f32[4,128]{1,0:T(4,128)S(1)}, f32[4,128]{1,0:T(4,128)}, u32[]{:S(2)}) copy-start(f32[4,128]{1,0:T(4,128)} %taps_bc.3) | copy-start | bytes 6148
  55.6 2.2 %collective-permute-start.9 = (bf16[8,256]{1,0:T(8,128)(2,1)S(1)}, bf16[8,256]{1,0:T(8,128)(2,1)S(1)}, u32[]{:S(2)}, u32[]{:S(2)}) collective-permute-start(bf16[8,256]{1,0:T(8,128)(2,1)S(1)} %slice.44), channel_id=1, source_target_pairs={{0,8},{8,16},{16,24},{1,9},{9,17},{17,25},{2,10},{10,18},{18,26},{... | collective-permute-start | bytes 12296 | tf_op jit(solution)/shard_map/ppermute | solution.py:348
  66.3 0.8 copy-start.5
  67.1 13.4 %collective-permute-start.15 = (bf16[128,1792]{1,0:T(8,128)(2,1)}, bf16[128,1792]{1,0:T(8,128)(2,1)S(1)}, u32[]{:S(2)}, u32[]{:S(2)}) collective-permute-start(bf16[128,1792]{1,0:T(8,128)(2,1)} %collective-permute-done.12.rest_3_), channel_id=1, source_target_pairs={{0,2},{2,4},{4,6},{6,7},{7,5},{5,3},{3,1},{1,0},{8,10},{10,12},{12... | collective-permute-start | bytes 1376264 | tf_op jit(solution)/shard_map/ppermute | solution.py:31
  68.7 13.1 %collective-permute-start.16 = (bf16[128,1792]{1,0:T(8,128)(2,1)}, bf16[128,1792]{1,0:T(8,128)(2,1)S(1)}, u32[]{:S(2)}, u32[]{:S(2)}) collective-permute-start(bf16[128,1792]{1,0:T(8,128)(2,1)} %copy-done.5), channel_id=1, source_target_pairs={{0,1},{2,0},{4,2},{6,4},{7,6},{5,7},{3,5},{1,3},{8,9},{10,8},{12,1... | collective-permute-start | bytes 1376264 | tf_op jit(solution)/shard_map/ppermute | solution.py:31
  71.0 14.0 %all-to-all-start = ((bf16[8,64,128]{2,1,0:T(8,128)(2,1)}), bf16[8,64,128]{2,1,0:T(8,128)(2,1)S(1)}, u32[]{:S(2)}, u32[]{:S(2)}) async-start(bf16[8,64,128]{2,1,0:T(8,128)(2,1)} %bitcast.7), calls=%async_computation | async-start | bytes 262144 | tf_op jit(solution)/shard_map/all_to_all | solution.py:380
  82.5 7.1 %collective-permute-start.17 = (bf16[64,1792]{1,0:T(8,128)(2,1)}, bf16[64,1792]{1,0:T(8,128)(2,1)S(1)}, u32[]{:S(2)}, u32[]{:S(2)}) collective-permute-start(bf16[64,1792]{1,0:T(8,128)(2,1)} %get-tuple-element.69), channel_id=1, source_target_pairs={{0,2},{2,4},{4,6},{6,7},{7,5},{5,3},{3,1},{1,0},{8,10},{10,12},{12... | collective-permute-start | bytes 688136 | tf_op jit(solution)/shard_map/ppermute | solution.py:31
  84.6 6.3 %collective-permute-start.18 = (bf16[64,1792]{1,0:T(8,128)(2,1)}, bf16[64,1792]{1,0:T(8,128)(2,1)}, u32[]{:S(2)}, u32[]{:S(2)}) collective-permute-start(bf16[64,1792]{1,0:T(8,128)(2,1)} %get-tuple-element.70), channel_id=1, source_target_pairs={{0,1},{2,0},{4,2},{6,4},{7,6},{5,7},{3,5},{1,3},{8,9},{10,8},{12,1... | collective-permute-start | bytes 688136 | tf_op jit(solution)/shard_map/ppermute | solution.py:31
  85.1 1.3 %collective-permute-start.14 = (bf16[8,64,128]{2,1,0:T(8,128)(2,1)S(1)}, bf16[8,64,128]{2,1,0:T(8,128)(2,1)S(1)}, u32[]{:S(2)}, u32[]{:S(2)}) collective-permute-start(bf16[8,64,128]{2,1,0:T(8,128)(2,1)S(1)} %all-to-all-done.mine), channel_id=1, source_target_pairs={{0,8},{8,0},{16,24},{24,16},{1,9},{9,1},{17,25},{25,17},{2,10},{10... | collective-permute-start | bytes 393224 | tf_op jit(solution)/shard_map/ppermute | solution.py:382
  86.4 1.0 %copy-start.6 = (bf16[128,1792]{1,0:T(8,128)(2,1)S(1)}, bf16[128,1792]{1,0:T(8,128)(2,1)}, u32[]{:S(2)}) copy-start(bf16[128,1792]{1,0:T(8,128)(2,1)} %copy-done.5) | copy-start | bytes 1376260
  92.2 1.6 %collective-permute-start.19 = (bf16[64,1792]{1,0:T(8,128)(2,1)S(1)}, bf16[64,1792]{1,0:T(8,128)(2,1)S(1)}, u32[]{:S(2)}, u32[]{:S(2)}) collective-permute-start(bf16[64,1792]{1,0:T(8,128)(2,1)S(1)} %get-tuple-element.72), channel_id=1, source_target_pairs={{0,8},{8,0},{16,24},{24,16},{1,9},{9,1},{17,25},{25,17},{2,10},{10... | collective-permute-start | bytes 688136 | tf_op jit(solution)/shard_map/ppermute | solution.py:394

commit v18 on v13

--- a/solution.py
+++ b/solution.py
@@ -14,7 +14,7 @@
 VMEM = pl.BlockSpec(memory_space=pltpu.VMEM)
 ANY = pl.BlockSpec(memory_space=pl.ANY)
 HALO = 8
-W_FIRST = 3
+W_FIRST = 2
 
 
 def ring_place(index, n):
@@ -316,6 +316,8 @@
             w_forth, w_back = ring_shift(w_forth, 1), ring_shift(w_back, -1)
         ahead = last if step == last else 0
         total = projs[-1:]
+        if step == 3:
+            total = [after(projs[-1], w_forth, w_back)]
         fetched = len(arrived) + bool(ahead)
         outs = [shape(tok_rows, 4 * width)] + [shape(feat, 4 * width, kind=BF16)] * bool(ahead)
         results = call(
@@ -355,7 +357,7 @@
     tok_own = tok_rows // n_tensor
 
     w_steps = [(w_forth, w_back)]
-    orders = [proj, messages]
+    orders = [(far, projs[-1]), messages]
     for step in range(2, last + 1):
         if step - 2 < len(orders):
             w_forth, w_back = after((w_forth, w_back), orders[step - 2])

time: 92.5 us -> 97.7 us (1.056)
  waiting for transfers between devices: 36.3 us -> 38.9 us
  Pallas kernels: 15.4 us -> 17.1 us
    ppermute x16, waiting for transfers between devices: 32.3 us -> 36.1 us  [ring_shift(): lax.ppermute(block, 'tensor', [(order[i], order[(i + step) % n]) for i in...]
    ppermute x16, starting transfers between devices: 17.5 us -> 18.8 us  [ring_shift(): lax.ppermute(block, 'tensor', [(order[i], order[(i + step) % n]) for i in...]
    all_to_all x1, waiting for transfers between devices: 1.17 us -> 0.01 us  [local(): mine = lax.all_to_all(blocks, 'tensor', 0, 0)]
  transfers between devices with their start and end apart: 21 -> 21, of which waited for: 12 -> 14; matrix products, arithmetic and copies ran while one was open for 4% -> 4% of each run, Pallas kernels for 16% -> 16%
where the time goes in v18:
time: 97.7 us; the launch traced here: 97.1 us
  waiting for transfers between devices  38.9 us (40%)
  starting transfers between devices  25.9 us (27%)
  Pallas kernels  17.1 us (18%)
  blocking collectives  6.42 us (7%)
  local copies, waits for them, and re-layouts  6.41 us (7%)
  matrix products  1.12 us (1%)
  other arithmetic  1.05 us (1%)
    ppermute x16, waiting for transfers between devices, ring_shift(): lax.ppermute(block, 'tensor', [(order[i], order[(i + step) % n]) for i in...  36.1 us
    ppermute x16, starting transfers between devices, ring_shift(): lax.ppermute(block, 'tensor', [(order[i], order[(i + step) % n]) for i in...  18.8 us
    pallas_call x4, Pallas kernels, local(): call(functools.partial(project, [distance for distance, _ in arrived], ah...  8.52 us
    all_gather x1, blocking collectives, local(): messages = lax.all_gather(message, 'seq')  6.42 us
    all_to_all x1, starting transfers between devices, local(): mine = lax.all_to_all(blocks, 'tensor', 0, 0)  4.28 us
    unnamed x26, local copies, waits for them, and re-layouts  4.24 us
    pallas_call x1, Pallas kernels, local(): call(functools.partial(product_early, distances), shape(2 * tok_own, colu...  2.14 us
  transfers between devices with their start and end apart: 21, of which 14 were waited for; matrix products, arithmetic and copies ran while one was open for 4% of the time, Pallas kernels for 16%

profile of v18, /device:TPU:0, one launch (start us, length us, event | category | flops | bytes accessed | tf_op | source)
XLA Modules:
  0.0 97.1 jit_solution(14298515755171704353)
XLA Ops:
  0.0 3.0 %collective-permute-start = (bf16[448,512]{1,0:T(8,128)(2,1)}, bf16[448,512]{1,0:T(8,128)(2,1)}, u32[]{:S(2)}, u32[]{:S(2)}) collective-permute-start(bf16[448,512]{1,0:T(8,128)(2,1)} %bitcast.12), channel_id=1, source_target_pairs={{0,2},{2,4},{4,6},{6,7},{7,5},{5,3},{3,1},{1,0},{8,10},{10,12},{12... | collective-permute-start | bytes 1376264 | tf_op jit(solution)/shard_map/ppermute | solution.py:31
  3.0 0.8 slice.33
  3.8 1.4 %collective-permute-start.3 = (s32[8]{0:T(128)S(1)}, s32[8]{0:T(128)S(1)}, u32[]{:S(2)}, u32[]{:S(2)}) collective-permute-start(s32[8]{0:T(128)S(1)} %slice.33), channel_id=1, source_target_pairs={{0,8},{8,16},{16,24},{1,9},{9,17},{17,25},{2,10},{10,18},{18,26},{... | collective-permute-start | bytes 104 | tf_op jit(solution)/shard_map/ppermute | solution.py:293
  5.3 1.1 %convolution_bitcast_fusion.refs_3_.refs_4_ = bf16[3584,128]{1,0:T(8,128)(2,1)S(1)} fusion(bf16[2,128]{1,0:T(2,128)(2,1)} %constant.25.clone, bf16[3584,2]{0,1:T(2,128)(2,1)S(1)} %copy-done), kind=kOutput, calls=%fused_computation | convolution fusion | flops 1835008 | bytes 932352 | tf_op jit(solution)/shard_map/dot_general | solution.py:284
  6.4 1.5 %copy-done.1 = bf16[2,3584,128]{2,1,0:T(8,128)(2,1)S(1)} copy-done((bf16[2,3584,128]{2,1,0:T(8,128)(2,1)S(1)}, bf16[2,3584,128]{2,1,0:T(8,128)(2,1)}, u32[]{:S(2)}) %copy-start.1) | copy-done | bytes 1835032
  7.9 1.2 %copy-done.2 = bf16[3584,128]{1,0:T(8,128)(2,1)S(1)} copy-done((bf16[3584,128]{1,0:T(8,128)(2,1)S(1)}, bf16[3584,128]{1,0:T(8,128)(2,1)}, u32[]{:S(2)}) %copy-start.2) | copy-done | bytes 917528
  9.1 1.0 %copy-done.4 = bf16[512,448]{0,1:T(8,128)(2,1)S(1)} copy-done((bf16[512,448]{0,1:T(8,128)(2,1)S(1)}, bf16[512,448]{0,1:T(8,128)(2,1)}, u32[]{:S(2)}) %copy-start.4) | copy-done | bytes 458776
  10.1 0.6 shard_map.127.refs_5_
  10.8 0.5 copy-done.7
  11.3 0.1 multiply_convert_fusion.rest_0_
  11.4 2.4 %collective-permute-done.refs_0_ = bf16[448,512]{1,0:T(8,128)(2,1)} collective-permute-done((bf16[448,512]{1,0:T(8,128)(2,1)}, bf16[448,512]{1,0:T(8,128)(2,1)}, u32[]{:S(2)}, u32[]{:S(2)}) %collective-permute-start) | collective-permute-done | bytes 458784 | tf_op jit(solution)/shard_map/ppermute | solution.py:31
  13.8 1.8 %collective-permute-start.1 = (bf16[448,512]{1,0:T(8,128)(2,1)}, bf16[448,512]{1,0:T(8,128)(2,1)}, u32[]{:S(2)}, u32[]{:S(2)}) collective-permute-start(bf16[448,512]{1,0:T(8,128)(2,1)} %collective-permute-done.refs_0_), channel_id=1, source_target_pairs={{0,2},{2,4},{4,6},{6,7},{7,5},{5,3},{3,1},{1,0},{8,10},{10,12},{12... | collective-permute-start | bytes 1376264 | tf_op jit(solution)/shard_map/ppermute | solution.py:31
  15.6 0.2 collective-permute-start.5
  15.8 0.6 fusion
  16.4 0.1 slice.36
  16.5 0.1 broadcast_in_dim.27
  16.5 0.1 broadcast_in_dim_reshape.9.bias
  16.6 0.1 broadcast_in_dim.28
  16.7 0.1 broadcast_in_dim_reshape.10.rate
  16.8 0.1 broadcast_in_dim.29
  16.9 0.1 broadcast_in_dim_reshape.11.skip
  16.9 0.1 pad_add_fusion
  17.0 1.8 %collective-permute-start.6 = (bf16[128,1792]{1,0:T(8,128)(2,1)S(1)}, bf16[128,1792]{1,0:T(8,128)(2,1)}, u32[]{:S(2)}, u32[]{:S(2)}) collective-permute-start(bf16[128,1792]{1,0:T(8,128)(2,1)S(1)} %multiply_convert_fusion.rest_0_), channel_id=1, source_target_pairs={{0,2},{2,4},{4,6},{6,7},{7,5},{5,3},{3,1},{1,0},{8,10},{10,12},{12... | collective-permute-start | bytes 1376264 | tf_op jit(solution)/shard_map/ppermute | solution.py:31
  18.9 0.2 collective-permute-start.7
  19.1 3.0 %shard_map.128.refs_5_ = f32[512,512]{1,0:T(8,128)S(1)} custom-call(bf16[448,512]{1,0:T(8,128)(2,1)} %collective-permute-done.refs_0_, bf16[448,512]{1,0:T(8,128)(2,1)} %collective-permute-done.2.refs_1_, bf16[2,3584,128]{2,1,0:T(8,128)(2,1)} %refs_2_.7, bf16[3584,128]{1,0:T(8,128)(2,1)S(1)} %copy-done.3, ...), custom_call_target="tpu_custom_call" | custom-call | flops 1000000000 | bytes 2097152 | tf_op jit(solution)/shard_map/pallas_call | solution.py:323
  22.1 5.4 %collective-permute-done.1.refs_0_ = bf16[448,512]{1,0:T(8,128)(2,1)} collective-permute-done((bf16[448,512]{1,0:T(8,128)(2,1)}, bf16[448,512]{1,0:T(8,128)(2,1)}, u32[]{:S(2)}, u32[]{:S(2)}) %collective-permute-start.1) | collective-permute-done | bytes 458784 | tf_op jit(solution)/shard_map/ppermute | solution.py:31
  27.4 1.9 %collective-permute-start.4 = (bf16[448,512]{1,0:T(8,128)(2,1)}, bf16[448,512]{1,0:T(8,128)(2,1)S(1)}, u32[]{:S(2)}, u32[]{:S(2)}) collective-permute-start(bf16[448,512]{1,0:T(8,128)(2,1)} %collective-permute-done.1.refs_0_), channel_id=1, source_target_pairs={{0,2},{2,4},{4,6},{6,7},{7,5},{5,3},{3,1},{1,0},{8,10},{10,12},{12... | collective-permute-start | bytes 1376264 | tf_op jit(solution)/shard_map/ppermute | solution.py:31
  29.3 0.0 collective-permute-done.5.refs_1_
  29.3 0.2 collective-permute-start.8
  29.5 7.8 %collective-permute-done.6.rest_1_ = bf16[128,1792]{1,0:T(8,128)(2,1)} collective-permute-done((bf16[128,1792]{1,0:T(8,128)(2,1)S(1)}, bf16[128,1792]{1,0:T(8,128)(2,1)}, u32[]{:S(2)}, u32[]{:S(2)}) %collective-permute-start.6) | collective-permute-done | bytes 458784 | tf_op jit(solution)/shard_map/ppermute | solution.py:31
  37.3 1.9 %collective-permute-done.7.rest_2_ = bf16[128,1792]{1,0:T(8,128)(2,1)} collective-permute-done((bf16[128,1792]{1,0:T(8,128)(2,1)S(1)}, bf16[128,1792]{1,0:T(8,128)(2,1)}, u32[]{:S(2)}, u32[]{:S(2)}) %collective-permute-start.7) | collective-permute-done | bytes 458784 | tf_op jit(solution)/shard_map/ppermute | solution.py:31
  39.2 3.0 %shard_map.129.refs_5_ = f32[512,512]{1,0:T(8,128)S(1)} custom-call(bf16[448,512]{1,0:T(8,128)(2,1)} %collective-permute-done.1.refs_0_, bf16[448,512]{1,0:T(8,128)(2,1)} %collective-permute-done.5.refs_1_, bf16[2,3584,128]{2,1,0:T(8,128)(2,1)} %refs_2_.7, bf16[3584,128]{1,0:T(8,128)(2,1)S(1)} %copy-done.3, ...), custom_call_target="tpu_custom_call" | custom-call | flops 1000000000 | bytes 2097152 | tf_op jit(solution)/shard_map/pallas_call | solution.py:323
  42.2 4.1 %collective-permute-done.4.forth.refs_0_ = bf16[448,512]{1,0:T(8,128)(2,1)S(1)} collective-permute-done((bf16[448,512]{1,0:T(8,128)(2,1)}, bf16[448,512]{1,0:T(8,128)(2,1)S(1)}, u32[]{:S(2)}, u32[]{:S(2)}) %collective-permute-start.4) | collective-permute-done | bytes 458784 | tf_op jit(solution)/shard_map/ppermute | solution.py:31
  46.3 1.3 %collective-permute-done.8.back.refs_1_ = bf16[448,512]{1,0:T(8,128)(2,1)S(1)} collective-permute-done((bf16[448,512]{1,0:T(8,128)(2,1)}, bf16[448,512]{1,0:T(8,128)(2,1)S(1)}, u32[]{:S(2)}, u32[]{:S(2)}) %collective-permute-start.8) | collective-permute-done | bytes 458784 | tf_op jit(solution)/shard_map/ppermute | solution.py:31
  47.6 1.6 %collective-permute-start.9 = (bf16[224,512]{1,0:T(8,128)(2,1)S(1)}, bf16[224,512]{1,0:T(8,128)(2,1)S(1)}, u32[]{:S(2)}, u32[]{:S(2)}) collective-permute-start(bf16[224,512]{1,0:T(8,128)(2,1)S(1)} %get-tuple-element.48), channel_id=1, source_target_pairs={{0,2},{2,4},{4,6},{6,7},{7,5},{5,3},{3,1},{1,0},{8,10},{10,12},{12... | collective-permute-start | bytes 688136 | tf_op jit(solution)/shard_map/ppermute | solution.py:31
  49.3 0.4 collective-permute-start.10
  49.7 1.9 %shard_map.131 = (f32[512,512]{1,0:T(8,128)S(1)}, bf16[448,512]{1,0:T(8,128)(2,1)S(1)}) custom-call(bf16[448,512]{1,0:T(8,128)(2,1)S(1)} %collective-permute-done.4.forth.refs_0_, bf16[448,512]{1,0:T(8,128)(2,1)S(1)} %collective-permute-done.8.back.refs_1_, bf16[2,3584,128]{2,1,0:T(8,128)(2,1)} %refs_2_.7, bf16[3584,128]{1,0:T(8,128)(2,1)S(1)} %copy-done.3, ...), custom_call_target="tpu_custom_call" | custom-call | flops 1000000000 | bytes 2097152 | tf_op jit(solution)/shard_map/pallas_call | solution.py:323
  51.6 2.4 %collective-permute-done.9.top = bf16[224,512]{1,0:T(8,128)(2,1)S(1)} collective-permute-done((bf16[224,512]{1,0:T(8,128)(2,1)S(1)}, bf16[224,512]{1,0:T(8,128)(2,1)S(1)}, u32[]{:S(2)}, u32[]{:S(2)}) %collective-permute-start.9) | collective-permute-done | bytes 229408 | tf_op jit(solution)/shard_map/ppermute | solution.py:31
  54.0 1.3 %collective-permute-done.10.bottom = bf16[224,512]{1,0:T(8,128)(2,1)S(1)} collective-permute-done((bf16[224,512]{1,0:T(8,128)(2,1)S(1)}, bf16[224,512]{1,0:T(8,128)(2,1)S(1)}, u32[]{:S(2)}, u32[]{:S(2)}) %collective-permute-start.10) | collective-permute-done | bytes 229408 | tf_op jit(solution)/shard_map/ppermute | solution.py:31
  55.3 1.6 %collective-permute-start.12 = (bf16[128,1792]{1,0:T(8,128)(2,1)}, bf16[128,1792]{1,0:T(8,128)(2,1)S(1)}, u32[]{:S(2)}, u32[]{:S(2)}) collective-permute-start(bf16[128,1792]{1,0:T(8,128)(2,1)} %collective-permute-done.6.rest_1_), channel_id=1, source_target_pairs={{0,2},{2,4},{4,6},{6,7},{7,5},{5,3},{3,1},{1,0},{8,10},{10,12},{12... | collective-permute-start | bytes 1376264 | tf_op jit(solution)/shard_map/ppermute | solution.py:31
  56.9 0.4 collective-permute-start.13
  57.4 0.5 shard_map.132.proj
  57.8 1.3 %collective-permute-start.11 = (bf16[8,256]{1,0:T(8,128)(2,1)S(1)}, bf16[8,256]{1,0:T(8,128)(2,1)S(1)}, u32[]{:S(2)}, u32[]{:S(2)}) collective-permute-start(bf16[8,256]{1,0:T(8,128)(2,1)S(1)} %slice.44), channel_id=1, source_target_pairs={{0,8},{8,16},{16,24},{1,9},{9,17},{17,25},{2,10},{10,18},{18,26},{... | collective-permute-start | bytes 12296 | tf_op jit(solution)/shard_map/ppermute | solution.py:337
  59.1 0.1 copy.16.seg_ext
  59.3 0.1 copy.17.seg_ext.seg_ext_a
  59.5 1.0 %shard_map.133 = (f32[256,128]{1,0:T(8,128)S(1)}, f32[256,128]{1,0:T(8,128)S(1)}, f32[256,128]{1,0:T(8,128)S(1)}, f32[72,128]{1,0:T(8,128)S(1)}, f32[256,128]{1,0:T(8,128)S(1)}) custom-call(f32[512,512]{1,0:T(8,128)S(1)} %shard_map.132.proj, s32[264,1]{1,0:T(8,128)S(1)} %copy.16.seg_ext, s32[1,256]{1,0:T(1,128)S(1)} %bitcast.16, f32[4,128]{1,0:T(4,128)S(1)} %copy-done.5, ...), custom_call_target="tpu_custom_call" | custom-call | flops 10000000 | bytes 2097152 | tf_op jit(solution)/shard_map/pallas_call | solution.py:342
  60.5 1.2 %shard_map.134 = (f32[256,128]{1,0:T(8,128)S(1)}, f32[256,128]{1,0:T(8,128)S(1)}, f32[256,128]{1,0:T(8,128)S(1)}, f32[256,128]{1,0:T(8,128)S(1)}, f32[256,128]{1...) custom-call(f32[512,512]{1,0:T(8,128)S(1)} %shard_map.132.proj, ...), custom_call_target="tpu_custom_call" | custom-call | flops 10000000 | bytes 2097152 | tf_op jit(solution)/shard_map/pallas_call | solution.py:347
  61.7 6.4 %all-gather = f32[288,128]{1,0:T(8,128)S(1)} all-gather(f32[72,128]{1,0:T(8,128)S(1)} %get-tuple-element.53), channel_id=2, replica_groups=mesh['seq'=4,'tensor'=8] {'seq'}, dimensions={0}, use_global_device_ids=true | all-gather | bytes 184320 | tf_op jit(solution)/shard_map/all_gather | solution.py:352
  68.1 1.6 %collective-permute-start.15 = (bf16[128,1792]{1,0:T(8,128)(2,1)S(1)}, bf16[128,1792]{1,0:T(8,128)(2,1)S(1)}, u32[]{:S(2)}, u32[]{:S(2)}) collective-permute-start(bf16[128,1792]{1,0:T(8,128)(2,1)S(1)} %collective-permute-done.12.rest_3_), channel_id=1, source_target_pairs={{0,2},{2,4},{4,6},{6,7},{7,5},{5,3},{3,1},{1,0},{8,10},{10,12},{12... | collective-permute-start | bytes 1376264 | tf_op jit(solution)/shard_map/ppermute | solution.py:31
  69.7 0.4 collective-permute-start.16
  70.2 1.7 %shard_map.135 = bf16[512,128]{1,0:T(8,128)(2,1)} custom-call(s32[1,1]{1,0:T(1,128)} %bitcast.seg_first, f32[4,72,128]{2,1,0:T(8,128)S(1)} %bitcast.11, s32[264,1]{1,0:T(8,128)S(1)} %copy.17.seg_ext.seg_ext_a, s32[1,256]{1,0:T(1,128)S(1)} %bitcast.15, f32[1,128]{1,0:T(1,128)S(1)} %broadcast_in_dim_reshape.11.skip, f32[512,512]{1,0:T(8,128)S(1)} %shard_map.132.proj, ...), custom_call_target="tpu_custom_call" | custom-call | flops 10000000 | bytes 2097152 | tf_op jit(solution)/shard_map/pallas_call | solution.py:353
  71.9 4.3 %all-to-all-start = ((bf16[8,64,128]{2,1,0:T(8,128)(2,1)}), bf16[8,64,128]{2,1,0:T(8,128)(2,1)S(1)}, u32[]{:S(2)}, u32[]{:S(2)}) async-start(bf16[8,64,128]{2,1,0:T(8,128)(2,1)} %bitcast.7), calls=%async_computation | async-start | bytes 262144 | tf_op jit(solution)/shard_map/all_to_all | solution.py:371
  76.2 5.3 %collective-permute-done.15.rest_5_.forth = bf16[128,1792]{1,0:T(8,128)(2,1)S(1)} collective-permute-done((bf16[128,1792]{1,0:T(8,128)(2,1)S(1)}, bf16[128,1792]{1,0:T(8,128)(2,1)S(1)}, u32[]{:S(2)}, u32[]{:S(2)}) %collective-permute-start.15) | collective-permute-done | bytes 458784 | tf_op jit(solution)/shard_map/ppermute | solution.py:31
  81.5 1.4 %collective-permute-done.16.rest_6_.back = bf16[128,1792]{1,0:T(8,128)(2,1)S(1)} collective-permute-done((bf16[128,1792]{1,0:T(8,128)(2,1)S(1)}, bf16[128,1792]{1,0:T(8,128)(2,1)S(1)}, u32[]{:S(2)}, u32[]{:S(2)}) %collective-permute-start.16) | collective-permute-done | bytes 458784 | tf_op jit(solution)/shard_map/ppermute | solution.py:31
  82.8 0.8 shard_map.137
  83.6 3.5 %collective-permute-start.17 = (bf16[64,1792]{1,0:T(8,128)(2,1)}, bf16[64,1792]{1,0:T(8,128)(2,1)S(1)}, u32[]{:S(2)}, u32[]{:S(2)}) collective-permute-start(bf16[64,1792]{1,0:T(8,128)(2,1)} %get-tuple-element.69), channel_id=1, source_target_pairs={{0,2},{2,4},{4,6},{6,7},{7,5},{5,3},{3,1},{1,0},{8,10},{10,12},{12... | collective-permute-start | bytes 688136 | tf_op jit(solution)/shard_map/ppermute | solution.py:31
  87.1 1.3 %collective-permute-done.14.other = bf16[8,64,128]{2,1,0:T(8,128)(2,1)S(1)} collective-permute-done((bf16[8,64,128]{2,1,0:T(8,128)(2,1)S(1)}, bf16[8,64,128]{2,1,0:T(8,128)(2,1)S(1)}, u32[]{:S(2)}, u32[]{:S(2)}) %collective-permute-start.14) | collective-permute-done | bytes 131104 | tf_op jit(solution)/shard_map/ppermute | solution.py:373
  88.5 2.1 %shard_map.136.total = f32[128,1792]{1,0:T(8,128)S(1)} custom-call(bf16[8,64,128]{2,1,0:T(8,128)(2,1)S(1)} %all-to-all-done.mine, bf16[8,64,128]{2,1,0:T(8,128)(2,1)S(1)} %collective-permute-done.14.other, bf16[128,1792]{1,0:T(8,128)(2,1)S(1)} %multiply_convert_fusion.rest_0_, bf16[128,1792]{1,0:T(8,128)(2,1)} %collective-permute-done.6.rest_1_, ...), custom_call_target="tpu_custom_call" | custom-call | flops 1 | bytes 1 | tf_op jit(solution)/shard_map/pallas_call | solution.py:378
  90.6 0.4 collective-permute-done.17.top
  91.0 2.5 %collective-permute-done.18.bottom = bf16[64,1792]{1,0:T(8,128)(2,1)} collective-permute-done((bf16[64,1792]{1,0:T(8,128)(2,1)}, bf16[64,1792]{1,0:T(8,128)(2,1)}, u32[]{:S(2)}, u32[]{:S(2)}) %collective-permute-start.18) | collective-permute-done | bytes 229408 | tf_op jit(solution)/shard_map/ppermute | solution.py:31
  93.5 1.2 %shard_map.138 = (bf16[64,1792]{1,0:T(8,128)(2,1)S(1)}, bf16[64,1792]{1,0:T(8,128)(2,1)S(1)}) custom-call(bf16[8,64,128]{2,1,0:T(8,128)(2,1)S(1)} %all-to-all-done.mine, bf16[8,64,128]{2,1,0:T(8,128)(2,1)S(1)} %collective-permute-done.14.other, f32[128,1792]{1,0:T(8,128)S(1)} %shard_map.136.total, bf16[64,1792]{1,0:T(8,128)(2,1)S(1)} %collective-permute-done.17.top, ...), custom_call_target="tpu_custom_call" | custom-call | flops 100000000 | bytes 2097152 | tf_op jit(solution)/shard_map/pallas_call | solution.py:382
  94.7 0.1 collective-permute-start.19
  94.8 1.5 %collective-permute-done.19 = bf16[64,1792]{1,0:T(8,128)(2,1)S(1)} collective-permute-done((bf16[64,1792]{1,0:T(8,128)(2,1)S(1)}, bf16[64,1792]{1,0:T(8,128)(2,1)S(1)}, u32[]{:S(2)}, u32[]{:S(2)}) %collective-permute-start.19) | collective-permute-done | bytes 229408 | tf_op jit(solution)/shard_map/ppermute | solution.py:385
  96.3 0.8 pad_maximum_fusion
  (38 shorter events, 0.2 us)
Async XLA Ops:
  0.0 5.3 %copy-start = (bf16[3584,2]{0,1:T(2,128)(2,1)S(1)}, bf16[3584,2]{0,1:T(2,128)(2,1)}, u32[]{:S(2)}) copy-start(bf16[3584,2]{0,1:T(2,128)(2,1)} %param.16) | copy-start | bytes 43012
  0.0 13.8 %collective-permute-start = (bf16[448,512]{1,0:T(8,128)(2,1)}, bf16[448,512]{1,0:T(8,128)(2,1)}, u32[]{:S(2)}, u32[]{:S(2)}) collective-permute-start(bf16[448,512]{1,0:T(8,128)(2,1)} %bitcast.12), channel_id=1, source_target_pairs={{0,2},{2,4},{4,6},{6,7},{7,5},{5,3},{3,1},{1,0},{8,10},{10,12},{12... | collective-permute-start | bytes 1376264 | tf_op jit(solution)/shard_map/ppermute | solution.py:31
  3.0 12.6 %collective-permute-start.2 = (bf16[448,512]{1,0:T(8,128)(2,1)}, bf16[448,512]{1,0:T(8,128)(2,1)}, u32[]{:S(2)}, u32[]{:S(2)}) collective-permute-start(bf16[448,512]{1,0:T(8,128)(2,1)} %bitcast.13), channel_id=1, source_target_pairs={{0,1},{2,0},{4,2},{6,4},{7,6},{5,7},{3,5},{1,3},{8,9},{10,8},{12,1... | collective-permute-start | bytes 1376264 | tf_op jit(solution)/shard_map/ppermute | solution.py:31
  3.8 13.2 %collective-permute-start.3 = (s32[8]{0:T(128)S(1)}, s32[8]{0:T(128)S(1)}, u32[]{:S(2)}, u32[]{:S(2)}) collective-permute-start(s32[8]{0:T(128)S(1)} %slice.33), channel_id=1, source_target_pairs={{0,8},{8,16},{16,24},{1,9},{9,17},{17,25},{2,10},{10,18},{18,26},{... | collective-permute-start | bytes 104 | tf_op jit(solution)/shard_map/ppermute | solution.py:293
  6.4 1.5 %copy-start.1 = (bf16[2,3584,128]{2,1,0:T(8,128)(2,1)S(1)}, bf16[2,3584,128]{2,1,0:T(8,128)(2,1)}, u32[]{:S(2)}) copy-start(bf16[2,3584,128]{2,1,0:T(8,128)(2,1)} %refs_2_.7) | copy-start | bytes 5505028
  7.9 1.2 %copy-start.2 = (bf16[3584,128]{1,0:T(8,128)(2,1)S(1)}, bf16[3584,128]{1,0:T(8,128)(2,1)}, u32[]{:S(2)}) copy-start(bf16[3584,128]{1,0:T(8,128)(2,1)} %refs_3_.5) | copy-start | bytes 2752516
  9.1 1.0 %copy-start.4 = (bf16[512,448]{0,1:T(8,128)(2,1)S(1)}, bf16[512,448]{0,1:T(8,128)(2,1)}, u32[]{:S(2)}) copy-start(bf16[512,448]{0,1:T(8,128)(2,1)} %param.13) | copy-start | bytes 1376260
  10.1 1.2 %copy-start.7 = (bf16[128,3584]{1,0:T(8,128)(2,1)S(1)}, bf16[128,3584]{1,0:T(8,128)(2,1)}, u32[]{:S(2)}) copy-start(bf16[128,3584]{1,0:T(8,128)(2,1)} %param.23) | copy-start | bytes 2752516
  10.1 1.2 %copy-start.9 = (f32[128]{0:T(128)S(1)}, f32[128]{0:T(128)}, u32[]{:S(2)}) copy-start(f32[128]{0:T(128)} %param.22) | copy-start | bytes 1540
  10.1 5.7 %copy-start.8 = (s32[512]{0:T(512)S(1)}, s32[512]{0:T(512)}, u32[]{:S(2)}) copy-start(s32[512]{0:T(512)} %param.24) | copy-start | bytes 6148
  10.1 6.4 %copy-start.10 = (f32[2]{0:T(128)S(1)}, f32[2]{0:T(128)}, u32[]{:S(2)}) copy-start(f32[2]{0:T(128)} %param.17) | copy-start | bytes 28
  10.1 6.5 %copy-start.11 = (f32[2]{0:T(128)S(1)}, f32[2]{0:T(128)}, u32[]{:S(2)}) copy-start(f32[2]{0:T(128)} %param.18) | copy-start | bytes 28
  10.1 6.7 %copy-start.12 = (f32[2]{0:T(128)S(1)}, f32[2]{0:T(128)}, u32[]{:S(2)}) copy-start(f32[2]{0:T(128)} %param.19) | copy-start | bytes 28
  10.1 8.9 %copy-start.3 = (bf16[3584,128]{1,0:T(8,128)(2,1)S(1)}, bf16[3584,128]{1,0:T(8,128)(2,1)}, u32[]{:S(2)}) copy-start(bf16[3584,128]{1,0:T(8,128)(2,1)} %refs_3_.5) | copy-start | bytes 2752516
  13.8 13.7 %collective-permute-start.1 = (bf16[448,512]{1,0:T(8,128)(2,1)}, bf16[448,512]{1,0:T(8,128)(2,1)}, u32[]{:S(2)}, u32[]{:S(2)}) collective-permute-start(bf16[448,512]{1,0:T(8,128)(2,1)} %collective-permute-done.refs_0_), channel_id=1, source_target_pairs={{0,2},{2,4},{4,6},{6,7},{7,5},{5,3},{3,1},{1,0},{8,10},{10,12},{12... | collective-permute-start | bytes 1376264 | tf_op jit(solution)/shard_map/ppermute | solution.py:31
  15.6 13.7 %collective-permute-start.5 = (bf16[448,512]{1,0:T(8,128)(2,1)}, bf16[448,512]{1,0:T(8,128)(2,1)}, u32[]{:S(2)}, u32[]{:S(2)}) collective-permute-start(bf16[448,512]{1,0:T(8,128)(2,1)} %collective-permute-done.2.refs_1_), channel_id=1, source_target_pairs={{0,1},{2,0},{4,2},{6,4},{7,6},{5,7},{3,5},{1,3},{8,9},{10,8},{12,1... | collective-permute-start | bytes 1376264 | tf_op jit(solution)/shard_map/ppermute | solution.py:31
  17.0 20.2 %collective-permute-start.6 = (bf16[128,1792]{1,0:T(8,128)(2,1)S(1)}, bf16[128,1792]{1,0:T(8,128)(2,1)}, u32[]{:S(2)}, u32[]{:S(2)}) collective-permute-start(bf16[128,1792]{1,0:T(8,128)(2,1)S(1)} %multiply_convert_fusion.rest_0_), channel_id=1, source_target_pairs={{0,2},{2,4},{4,6},{6,7},{7,5},{5,3},{3,1},{1,0},{8,10},{10,12},{12... | collective-permute-start | bytes 1376264 | tf_op jit(solution)/shard_map/ppermute | solution.py:31
  18.9 20.3 %collective-permute-start.7 = (bf16[128,1792]{1,0:T(8,128)(2,1)S(1)}, bf16[128,1792]{1,0:T(8,128)(2,1)}, u32[]{:S(2)}, u32[]{:S(2)}) collective-permute-start(bf16[128,1792]{1,0:T(8,128)(2,1)S(1)} %multiply_convert_fusion.rest_0_), channel_id=1, source_target_pairs={{0,1},{2,0},{4,2},{6,4},{7,6},{5,7},{3,5},{1,3},{8,9},{10,8},{12,1... | collective-permute-start | bytes 1376264 | tf_op jit(solution)/shard_map/ppermute | solution.py:31
  27.4 18.9 %collective-permute-start.4 = (bf16[448,512]{1,0:T(8,128)(2,1)}, bf16[448,512]{1,0:T(8,128)(2,1)S(1)}, u32[]{:S(2)}, u32[]{:S(2)}) collective-permute-start(bf16[448,512]{1,0:T(8,128)(2,1)} %collective-permute-done.1.refs_0_), channel_id=1, source_target_pairs={{0,2},{2,4},{4,6},{6,7},{7,5},{5,3},{3,1},{1,0},{8,10},{10,12},{12... | collective-permute-start | bytes 1376264 | tf_op jit(solution)/shard_map/ppermute | solution.py:31
  29.3 18.3 %collective-permute-start.8 = (bf16[448,512]{1,0:T(8,128)(2,1)}, bf16[448,512]{1,0:T(8,128)(2,1)S(1)}, u32[]{:S(2)}, u32[]{:S(2)}) collective-permute-start(bf16[448,512]{1,0:T(8,128)(2,1)} %collective-permute-done.5.refs_1_), channel_id=1, source_target_pairs={{0,1},{2,0},{4,2},{6,4},{7,6},{5,7},{3,5},{1,3},{8,9},{10,8},{12,1... | collective-permute-start | bytes 1376264 | tf_op jit(solution)/shard_map/ppermute | solution.py:31
  47.6 6.4 %collective-permute-start.9 = (bf16[224,512]{1,0:T(8,128)(2,1)S(1)}, bf16[224,512]{1,0:T(8,128)(2,1)S(1)}, u32[]{:S(2)}, u32[]{:S(2)}) collective-permute-start(bf16[224,512]{1,0:T(8,128)(2,1)S(1)} %get-tuple-element.48), channel_id=1, source_target_pairs={{0,2},{2,4},{4,6},{6,7},{7,5},{5,3},{3,1},{1,0},{8,10},{10,12},{12... | collective-permute-start | bytes 688136 | tf_op jit(solution)/shard_map/ppermute | solution.py:31
  49.3 6.0 %collective-permute-start.10 = (bf16[224,512]{1,0:T(8,128)(2,1)S(1)}, bf16[224,512]{1,0:T(8,128)(2,1)S(1)}, u32[]{:S(2)}, u32[]{:S(2)}) collective-permute-start(bf16[224,512]{1,0:T(8,128)(2,1)S(1)} %get-tuple-element.49), channel_id=1, source_target_pairs={{0,1},{2,0},{4,2},{6,4},{7,6},{5,7},{3,5},{1,3},{8,9},{10,8},{12,1... | collective-permute-start | bytes 688136 | tf_op jit(solution)/shard_map/ppermute | solution.py:31
  55.3 12.8 %collective-permute-start.12 = (bf16[128,1792]{1,0:T(8,128)(2,1)}, bf16[128,1792]{1,0:T(8,128)(2,1)S(1)}, u32[]{:S(2)}, u32[]{:S(2)}) collective-permute-start(bf16[128,1792]{1,0:T(8,128)(2,1)} %collective-permute-done.6.rest_1_), channel_id=1, source_target_pairs={{0,2},{2,4},{4,6},{6,7},{7,5},{5,3},{3,1},{1,0},{8,10},{10,12},{12... | collective-permute-start | bytes 1376264 | tf_op jit(solution)/shard_map/ppermute | solution.py:31
  56.9 11.2 %collective-permute-start.13 = (bf16[128,1792]{1,0:T(8,128)(2,1)}, bf16[128,1792]{1,0:T(8,128)(2,1)S(1)}, u32[]{:S(2)}, u32[]{:S(2)}) collective-permute-start(bf16[128,1792]{1,0:T(8,128)(2,1)} %collective-permute-done.7.rest_2_), channel_id=1, source_target_pairs={{0,1},{2,0},{4,2},{6,4},{7,6},{5,7},{3,5},{1,3},{8,9},{10,8},{12,1... | collective-permute-start | bytes 1376264 | tf_op jit(solution)/shard_map/ppermute | solution.py:31
  57.4 2.1 %copy-start.5 = (f32[4,128]{1,0:T(4,128)S(1)}, f32[4,128]{1,0:T(4,128)}, u32[]{:S(2)}) copy-start(f32[4,128]{1,0:T(4,128)} %taps_x.3) | copy-start | bytes 6148
  57.4 2.1 %copy-start.6 = (f32[4,128]{1,0:T(4,128)S(1)}, f32[4,128]{1,0:T(4,128)}, u32[]{:S(2)}) copy-start(f32[4,128]{1,0:T(4,128)} %taps_bc.3) | copy-start | bytes 6148
  57.8 2.6 %collective-permute-start.11 = (bf16[8,256]{1,0:T(8,128)(2,1)S(1)}, bf16[8,256]{1,0:T(8,128)(2,1)S(1)}, u32[]{:S(2)}, u32[]{:S(2)}) collective-permute-start(bf16[8,256]{1,0:T(8,128)(2,1)S(1)} %slice.44), channel_id=1, source_target_pairs={{0,8},{8,16},{16,24},{1,9},{9,17},{17,25},{2,10},{10,18},{18,26},{... | collective-permute-start | bytes 12296 | tf_op jit(solution)/shard_map/ppermute | solution.py:337
  68.1 13.3 %collective-permute-start.15 = (bf16[128,1792]{1,0:T(8,128)(2,1)S(1)}, bf16[128,1792]{1,0:T(8,128)(2,1)S(1)}, u32[]{:S(2)}, u32[]{:S(2)}) collective-permute-start(bf16[128,1792]{1,0:T(8,128)(2,1)S(1)} %collective-permute-done.12.rest_3_), channel_id=1, source_target_pairs={{0,2},{2,4},{4,6},{6,7},{7,5},{5,3},{3,1},{1,0},{8,10},{10,12},{12... | collective-permute-start | bytes 1376264 | tf_op jit(solution)/shard_map/ppermute | solution.py:31
  69.7 13.1 %collective-permute-start.16 = (bf16[128,1792]{1,0:T(8,128)(2,1)S(1)}, bf16[128,1792]{1,0:T(8,128)(2,1)S(1)}, u32[]{:S(2)}, u32[]{:S(2)}) collective-permute-start(bf16[128,1792]{1,0:T(8,128)(2,1)S(1)} %collective-permute-done.13.rest_4_), channel_id=1, source_target_pairs={{0,1},{2,0},{4,2},{6,4},{7,6},{5,7},{3,5},{1,3},{8,9},{10,8},{12,1... | collective-permute-start | bytes 1376264 | tf_op jit(solution)/shard_map/ppermute | solution.py:31
  71.9 15.3 %all-to-all-start = ((bf16[8,64,128]{2,1,0:T(8,128)(2,1)}), bf16[8,64,128]{2,1,0:T(8,128)(2,1)S(1)}, u32[]{:S(2)}, u32[]{:S(2)}) async-start(bf16[8,64,128]{2,1,0:T(8,128)(2,1)} %bitcast.7), calls=%async_computation | async-start | bytes 262144 | tf_op jit(solution)/shard_map/all_to_all | solution.py:371
  83.6 7.4 %collective-permute-start.17 = (bf16[64,1792]{1,0:T(8,128)(2,1)}, bf16[64,1792]{1,0:T(8,128)(2,1)S(1)}, u32[]{:S(2)}, u32[]{:S(2)}) collective-permute-start(bf16[64,1792]{1,0:T(8,128)(2,1)} %get-tuple-element.69), channel_id=1, source_target_pairs={{0,2},{2,4},{4,6},{6,7},{7,5},{5,3},{3,1},{1,0},{8,10},{10,12},{12... | collective-permute-start | bytes 688136 | tf_op jit(solution)/shard_map/ppermute | solution.py:31
  87.1 6.3 %collective-permute-start.18 = (bf16[64,1792]{1,0:T(8,128)(2,1)}, bf16[64,1792]{1,0:T(8,128)(2,1)}, u32[]{:S(2)}, u32[]{:S(2)}) collective-permute-start(bf16[64,1792]{1,0:T(8,128)(2,1)} %get-tuple-element.70), channel_id=1, source_target_pairs={{0,1},{2,0},{4,2},{6,4},{7,6},{5,7},{3,5},{1,3},{8,9},{10,8},{12,1... | collective-permute-start | bytes 688136 | tf_op jit(solution)/shard_map/ppermute | solution.py:31
  87.1 1.3 %collective-permute-start.14 = (bf16[8,64,128]{2,1,0:T(8,128)(2,1)S(1)}, bf16[8,64,128]{2,1,0:T(8,128)(2,1)S(1)}, u32[]{:S(2)}, u32[]{:S(2)}) collective-permute-start(bf16[8,64,128]{2,1,0:T(8,128)(2,1)S(1)} %all-to-all-done.mine), channel_id=1, source_target_pairs={{0,8},{8,0},{16,24},{24,16},{1,9},{9,1},{17,25},{25,17},{2,10},{10... | collective-permute-start | bytes 393224 | tf_op jit(solution)/shard_map/ppermute | solution.py:373
  94.7 1.6 %collective-permute-start.19 = (bf16[64,1792]{1,0:T(8,128)(2,1)S(1)}, bf16[64,1792]{1,0:T(8,128)(2,1)S(1)}, u32[]{:S(2)}, u32[]{:S(2)}) collective-permute-start(bf16[64,1792]{1,0:T(8,128)(2,1)S(1)} %get-tuple-element.72), channel_id=1, source_target_pairs={{0,8},{8,0},{16,24},{24,16},{1,9},{9,1},{17,25},{25,17},{2,10},{10... | collective-permute-start | bytes 688136 | tf_op jit(solution)/shard_map/ppermute | solution.py:385

commit v19 on v13

--- a/solution.py
+++ b/solution.py
@@ -240,18 +240,36 @@
     rest[-1][...] = product((mine, other), distances, rest[:-1])
 
 
-def product_last(distance, mine, other, total, top, bottom, mine_out, other_out, held):
+def last_rows(distance, gated, total, top, bottom, held):
     held[: top.shape[0]] = top[...]
     held[top.shape[0] :] = bottom[...]
-    result = product((mine, other), [distance], [held]) + total[...]
-    blocks, rows, width = mine.shape
-    for i, (gated, out) in enumerate(((mine, mine_out), (other, other_out))):
-        squares = jnp.zeros((rows, width), F32)
-        for block in range(blocks):
-            value = gated[block].astype(F32)
-            squares = squares + value * value
-        scale = lax.rsqrt(jnp.sum(squares, axis=1, keepdims=True) / (blocks * width) + NORM_EPS)
-        out[...] = (result[i * rows : (i + 1) * rows] * scale).astype(BF16)
+    blocks, rows, width = gated.shape
+    squares = jnp.zeros((rows, width), F32)
+    for block in range(blocks):
+        value = gated[block].astype(F32)
+        squares = squares + value * value
+    scale = lax.rsqrt(jnp.sum(squares, axis=1, keepdims=True) / (blocks * width) + NORM_EPS)
+    return ((product((gated,), [distance], [held]) + total) * scale).astype(BF16)
+
+
+def last_other(distance, other, total, top, bottom, out, held):
+    rows = other.shape[1]
+    out[...] = last_rows(distance, other, total[rows:], top, bottom, held)
+
+
+def last_mine(distance, mine, total, top, bottom, out, held):
+    rows, columns = mine.shape[1], held.shape[1]
+    start = pl.multiple_of(lax.axis_index("seq") % 2 * columns, 128)
+    out[:, pl.ds(start, columns)] = last_rows(distance, mine, total[:rows], top, bottom, held)
+
+
+def put_other(whole, arrived, out, sem):
+    del whole
+    columns = arrived.shape[1]
+    start = pl.multiple_of((1 - lax.axis_index("seq") % 2) * columns, 128)
+    copy = pltpu.make_async_copy(arrived, out.at[:, pl.ds(start, columns)], sem)
+    copy.start()
+    copy.wait()
 
 
 def call(body, outs, scratch=(), vmem=48, flops=10**7, moved=1 << 21, **kw):
@@ -355,7 +373,7 @@
     tok_own = tok_rows // n_tensor
 
     w_steps = [(w_forth, w_back)]
-    orders = [proj, messages]
+    orders = [(far, projs[-1]), messages]
     for step in range(2, last + 1):
         if step - 2 < len(orders):
             w_forth, w_back = after((w_forth, w_back), orders[step - 2])
@@ -377,12 +395,18 @@
         mine, other, *pieces
     )
     half = shape(tok_own, columns, kind=BF16)
-    out_own, out_other = call(
-        functools.partial(product_last, last), [half, half], [pltpu.VMEM((width, columns), BF16)], flops=10**8
-    )(mine, other, total, *w_far)
+    held = [pltpu.VMEM((width, columns), BF16)]
+    out_other = call(functools.partial(last_other, last), half, held)(other, total, *w_far)
     arrived = lax.ppermute(out_other, "seq", swap)
-    is_first = core == 0
-    return jnp.concatenate([jnp.where(is_first, out_own, arrived), jnp.where(is_first, arrived, out_own)], 1)
+    whole = call(functools.partial(last_mine, last), shape(tok_own, model, kind=BF16), held)(mine, total, *w_far)
+    return call(
+        put_other,
+        shape(tok_own, model, kind=BF16),
+        [pltpu.SemaphoreType.DMA],
+        in_specs=[ANY, VMEM],
+        out_specs=ANY,
+        input_output_aliases={0: 0},
+    )(whole, arrived)
 
 
 def solution(mesh):

time: 92.5 us -> 92.1 us (level)
  Pallas kernels: 15.4 us -> 17.1 us
  waiting for transfers between devices: 36.3 us -> 35 us
    pallas_call x1 -> x3, Pallas kernels: 0.28 us -> 1.89 us  [the longest x1 0.98 us: local(): call(functools.partial(last_mine, last), shape(tok_own, model, kind=BF16)...]
    ppermute x1, waiting for transfers between devices: 1.47 us -> 0.49 us  [local(): arrived = lax.ppermute(out_other, 'seq', swap)]
  transfers between devices with their start and end apart: 21 -> 21, of which waited for: 12 -> 14; matrix products, arithmetic and copies ran while one was open for 4% -> 4% of each run, Pallas kernels for 16% -> 18%
where the time goes in v19:
time: 92.1 us; the launch traced here: 91.6 us
  waiting for transfers between devices  35 us (38%)
  starting transfers between devices  25.2 us (27%)
  Pallas kernels  17.1 us (19%)
  blocking collectives  6.84 us (7%)
  local copies, waits for them, and re-layouts  5.91 us (6%)
  matrix products  1.12 us (1%)
    ppermute x16, waiting for transfers between devices, ring_shift(): lax.ppermute(block, 'tensor', [(order[i], order[(i + step) % n]) for i in...  31.7 us
    ppermute x16, starting transfers between devices, ring_shift(): lax.ppermute(block, 'tensor', [(order[i], order[(i + step) % n]) for i in...  17.4 us
    pallas_call x4, Pallas kernels, local(): call(functools.partial(project, [distance for distance, _ in arrived], ah...  8.47 us
    all_gather x1, blocking collectives, local(): messages = lax.all_gather(message, 'seq')  6.84 us
    all_to_all x1, starting transfers between devices, local(): mine = lax.all_to_all(blocks, 'tensor', 0, 0)  5 us
    unnamed x26, local copies, waits for them, and re-layouts  3.73 us
    pallas_call x1, Pallas kernels, local(): call(functools.partial(product_early, distances), shape(2 * tok_own, colu...  2.14 us
  transfers between devices with their start and end apart: 21, of which 14 were waited for; matrix products, arithmetic and copies ran while one was open for 4% of the time, Pallas kernels for 18%

profile of v19, /device:TPU:0, one launch (start us, length us, event | category | flops | bytes accessed | tf_op | source)
XLA Modules:
  0.0 91.6 jit_solution(2245259233164710621)
XLA Ops:
  0.0 3.0 %collective-permute-start = (bf16[448,512]{1,0:T(8,128)(2,1)}, bf16[448,512]{1,0:T(8,128)(2,1)}, u32[]{:S(2)}, u32[]{:S(2)}) collective-permute-start(bf16[448,512]{1,0:T(8,128)(2,1)} %bitcast.12), channel_id=1, source_target_pairs={{0,2},{2,4},{4,6},{6,7},{7,5},{5,3},{3,1},{1,0},{8,10},{10,12},{12... | collective-permute-start | bytes 1376264 | tf_op jit(solution)/shard_map/ppermute | solution.py:31
  3.0 0.8 slice.33
  3.8 1.4 %collective-permute-start.3 = (s32[8]{0:T(128)S(1)}, s32[8]{0:T(128)S(1)}, u32[]{:S(2)}, u32[]{:S(2)}) collective-permute-start(s32[8]{0:T(128)S(1)} %slice.33), channel_id=1, source_target_pairs={{0,8},{8,16},{16,24},{1,9},{9,17},{17,25},{2,10},{10,18},{18,26},{... | collective-permute-start | bytes 104 | tf_op jit(solution)/shard_map/ppermute | solution.py:311
  5.2 1.1 %convolution_bitcast_fusion.refs_3_.refs_4_ = bf16[3584,128]{1,0:T(8,128)(2,1)S(1)} fusion(bf16[2,128]{1,0:T(2,128)(2,1)} %constant.25.clone, bf16[3584,2]{0,1:T(2,128)(2,1)S(1)} %copy-done), kind=kOutput, calls=%fused_computation | convolution fusion | flops 1835008 | bytes 932352 | tf_op jit(solution)/shard_map/dot_general | solution.py:302
  6.4 0.0 copy-start.1
  6.4 1.5 %copy-done.1 = bf16[2,3584,128]{2,1,0:T(8,128)(2,1)S(1)} copy-done((bf16[2,3584,128]{2,1,0:T(8,128)(2,1)S(1)}, bf16[2,3584,128]{2,1,0:T(8,128)(2,1)}, u32[]{:S(2)}) %copy-start.1) | copy-done | bytes 1835032
  7.9 1.2 %copy-done.2 = bf16[3584,128]{1,0:T(8,128)(2,1)S(1)} copy-done((bf16[3584,128]{1,0:T(8,128)(2,1)S(1)}, bf16[3584,128]{1,0:T(8,128)(2,1)}, u32[]{:S(2)}) %copy-start.2) | copy-done | bytes 917528
  9.1 1.0 %copy-done.4 = bf16[512,448]{0,1:T(8,128)(2,1)S(1)} copy-done((bf16[512,448]{0,1:T(8,128)(2,1)S(1)}, bf16[512,448]{0,1:T(8,128)(2,1)}, u32[]{:S(2)}) %copy-start.4) | copy-done | bytes 458776
  10.1 0.6 shard_map.127.refs_5_
  10.7 3.1 %collective-permute-done.refs_0_ = bf16[448,512]{1,0:T(8,128)(2,1)} collective-permute-done((bf16[448,512]{1,0:T(8,128)(2,1)}, bf16[448,512]{1,0:T(8,128)(2,1)}, u32[]{:S(2)}, u32[]{:S(2)}) %collective-permute-start) | collective-permute-done | bytes 458784 | tf_op jit(solution)/shard_map/ppermute | solution.py:31
  13.8 1.8 %collective-permute-start.1 = (bf16[448,512]{1,0:T(8,128)(2,1)}, bf16[448,512]{1,0:T(8,128)(2,1)}, u32[]{:S(2)}, u32[]{:S(2)}) collective-permute-start(bf16[448,512]{1,0:T(8,128)(2,1)} %collective-permute-done.refs_0_), channel_id=1, source_target_pairs={{0,2},{2,4},{4,6},{6,7},{7,5},{5,3},{3,1},{1,0},{8,10},{10,12},{12... | collective-permute-start | bytes 1376264 | tf_op jit(solution)/shard_map/ppermute | solution.py:31
  15.6 0.2 collective-permute-start.5
  15.8 0.6 fusion
  16.4 0.1 slice.36
  16.5 0.1 broadcast_in_dim.27
  16.5 0.1 broadcast_in_dim_reshape.9.bias
  16.6 0.1 broadcast_in_dim.28
  16.7 0.1 broadcast_in_dim_reshape.10.rate
  16.8 0.1 broadcast_in_dim.29
  16.9 0.1 broadcast_in_dim_reshape.11.skip
  17.0 0.1 pad_add_fusion
  17.1 3.0 %shard_map.128.refs_5_ = f32[512,512]{1,0:T(8,128)S(1)} custom-call(bf16[448,512]{1,0:T(8,128)(2,1)} %collective-permute-done.refs_0_, bf16[448,512]{1,0:T(8,128)(2,1)S(1)} %collective-permute-done.2.refs_1_, bf16[2,3584,128]{2,1,0:T(8,128)(2,1)} %refs_2_.7, bf16[3584,128]{1,0:T(8,128)(2,1)S(1)} %copy-done.3, ...), custom_call_target="tpu_custom_call" | custom-call | flops 1000000000 | bytes 2097152 | tf_op jit(solution)/shard_map/pallas_call | solution.py:339
  20.0 6.0 %collective-permute-done.1.refs_0_ = bf16[448,512]{1,0:T(8,128)(2,1)} collective-permute-done((bf16[448,512]{1,0:T(8,128)(2,1)}, bf16[448,512]{1,0:T(8,128)(2,1)}, u32[]{:S(2)}, u32[]{:S(2)}) %collective-permute-start.1) | collective-permute-done | bytes 458784 | tf_op jit(solution)/shard_map/ppermute | solution.py:31
  26.0 1.6 %collective-permute-start.4 = (bf16[448,512]{1,0:T(8,128)(2,1)}, bf16[448,512]{1,0:T(8,128)(2,1)S(1)}, u32[]{:S(2)}, u32[]{:S(2)}) collective-permute-start(bf16[448,512]{1,0:T(8,128)(2,1)} %collective-permute-done.1.refs_0_), channel_id=1, source_target_pairs={{0,2},{2,4},{4,6},{6,7},{7,5},{5,3},{3,1},{1,0},{8,10},{10,12},{12... | collective-permute-start | bytes 1376264 | tf_op jit(solution)/shard_map/ppermute | solution.py:31
  27.6 0.4 collective-permute-start.6
  28.1 0.1 multiply_convert_fusion.rest_0_
  28.2 1.6 %collective-permute-start.10 = (bf16[128,1792]{1,0:T(8,128)(2,1)S(1)}, bf16[128,1792]{1,0:T(8,128)(2,1)S(1)}, u32[]{:S(2)}, u32[]{:S(2)}) collective-permute-start(bf16[128,1792]{1,0:T(8,128)(2,1)S(1)} %multiply_convert_fusion.rest_0_), channel_id=1, source_target_pairs={{0,2},{2,4},{4,6},{6,7},{7,5},{5,3},{3,1},{1,0},{8,10},{10,12},{12... | collective-permute-start | bytes 1376264 | tf_op jit(solution)/shard_map/ppermute | solution.py:31
  29.9 0.4 collective-permute-start.11
  30.3 3.0 %shard_map.129.refs_5_ = f32[512,512]{1,0:T(8,128)S(1)} custom-call(bf16[448,512]{1,0:T(8,128)(2,1)} %collective-permute-done.1.refs_0_, bf16[448,512]{1,0:T(8,128)(2,1)} %collective-permute-done.5.refs_1_, bf16[2,3584,128]{2,1,0:T(8,128)(2,1)} %refs_2_.7, bf16[3584,128]{1,0:T(8,128)(2,1)S(1)} %copy-done.3, ...), custom_call_target="tpu_custom_call" | custom-call | flops 1000000000 | bytes 2097152 | tf_op jit(solution)/shard_map/pallas_call | solution.py:339
  33.3 6.4 %collective-permute-done.4.forth.refs_0_ = bf16[448,512]{1,0:T(8,128)(2,1)S(1)} collective-permute-done((bf16[448,512]{1,0:T(8,128)(2,1)}, bf16[448,512]{1,0:T(8,128)(2,1)S(1)}, u32[]{:S(2)}, u32[]{:S(2)}) %collective-permute-start.4) | collective-permute-done | bytes 458784 | tf_op jit(solution)/shard_map/ppermute | solution.py:31
  39.7 1.6 %collective-permute-done.6.back.refs_1_ = bf16[448,512]{1,0:T(8,128)(2,1)S(1)} collective-permute-done((bf16[448,512]{1,0:T(8,128)(2,1)}, bf16[448,512]{1,0:T(8,128)(2,1)S(1)}, u32[]{:S(2)}, u32[]{:S(2)}) %collective-permute-start.6) | collective-permute-done | bytes 458784 | tf_op jit(solution)/shard_map/ppermute | solution.py:31
  41.3 1.6 %collective-permute-start.7 = (bf16[224,512]{1,0:T(8,128)(2,1)S(1)}, bf16[224,512]{1,0:T(8,128)(2,1)S(1)}, u32[]{:S(2)}, u32[]{:S(2)}) collective-permute-start(bf16[224,512]{1,0:T(8,128)(2,1)S(1)} %get-tuple-element.42), channel_id=1, source_target_pairs={{0,2},{2,4},{4,6},{6,7},{7,5},{5,3},{3,1},{1,0},{8,10},{10,12},{12... | collective-permute-start | bytes 688136 | tf_op jit(solution)/shard_map/ppermute | solution.py:31
  43.0 0.5 collective-permute-start.8
  43.4 1.9 %shard_map.131 = (f32[512,512]{1,0:T(8,128)S(1)}, bf16[448,512]{1,0:T(8,128)(2,1)S(1)}) custom-call(bf16[448,512]{1,0:T(8,128)(2,1)S(1)} %collective-permute-done.4.forth.refs_0_, bf16[448,512]{1,0:T(8,128)(2,1)S(1)} %collective-permute-done.6.back.refs_1_, bf16[2,3584,128]{2,1,0:T(8,128)(2,1)} %refs_2_.7, bf16[3584,128]{1,0:T(8,128)(2,1)S(1)} %copy-done.3, ...), custom_call_target="tpu_custom_call" | custom-call | flops 1000000000 | bytes 2097152 | tf_op jit(solution)/shard_map/pallas_call | solution.py:339
  45.3 4.2 %collective-permute-done.10.rest_1_ = bf16[128,1792]{1,0:T(8,128)(2,1)S(1)} collective-permute-done((bf16[128,1792]{1,0:T(8,128)(2,1)S(1)}, bf16[128,1792]{1,0:T(8,128)(2,1)S(1)}, u32[]{:S(2)}, u32[]{:S(2)}) %collective-permute-start.10) | collective-permute-done | bytes 458784 | tf_op jit(solution)/shard_map/ppermute | solution.py:31
  49.5 1.1 %collective-permute-done.11.rest_2_ = bf16[128,1792]{1,0:T(8,128)(2,1)S(1)} collective-permute-done((bf16[128,1792]{1,0:T(8,128)(2,1)S(1)}, bf16[128,1792]{1,0:T(8,128)(2,1)S(1)}, u32[]{:S(2)}, u32[]{:S(2)}) %collective-permute-start.11) | collective-permute-done | bytes 458784 | tf_op jit(solution)/shard_map/ppermute | solution.py:31
  50.6 1.4 %collective-permute-done.7.top = bf16[224,512]{1,0:T(8,128)(2,1)S(1)} collective-permute-done((bf16[224,512]{1,0:T(8,128)(2,1)S(1)}, bf16[224,512]{1,0:T(8,128)(2,1)S(1)}, u32[]{:S(2)}, u32[]{:S(2)}) %collective-permute-start.7) | collective-permute-done | bytes 229408 | tf_op jit(solution)/shard_map/ppermute | solution.py:31
  52.0 1.0 %collective-permute-done.8.bottom = bf16[224,512]{1,0:T(8,128)(2,1)S(1)} collective-permute-done((bf16[224,512]{1,0:T(8,128)(2,1)S(1)}, bf16[224,512]{1,0:T(8,128)(2,1)S(1)}, u32[]{:S(2)}, u32[]{:S(2)}) %collective-permute-start.8) | collective-permute-done | bytes 229408 | tf_op jit(solution)/shard_map/ppermute | solution.py:31
  53.1 1.6 %collective-permute-start.12 = (bf16[128,1792]{1,0:T(8,128)(2,1)S(1)}, bf16[128,1792]{1,0:T(8,128)(2,1)}, u32[]{:S(2)}, u32[]{:S(2)}) collective-permute-start(bf16[128,1792]{1,0:T(8,128)(2,1)S(1)} %collective-permute-done.10.rest_1_), channel_id=1, source_target_pairs={{0,2},{2,4},{4,6},{6,7},{7,5},{5,3},{3,1},{1,0},{8,10},{10,12},{12... | collective-permute-start | bytes 1376264 | tf_op jit(solution)/shard_map/ppermute | solution.py:31
  54.7 0.5 collective-permute-start.13
  55.1 0.5 shard_map.132.proj
  55.6 1.3 %collective-permute-start.9 = (bf16[8,256]{1,0:T(8,128)(2,1)S(1)}, bf16[8,256]{1,0:T(8,128)(2,1)S(1)}, u32[]{:S(2)}, u32[]{:S(2)}) collective-permute-start(bf16[8,256]{1,0:T(8,128)(2,1)S(1)} %slice.44), channel_id=1, source_target_pairs={{0,8},{8,16},{16,24},{1,9},{9,17},{17,25},{2,10},{10,18},{18,26},{... | collective-permute-start | bytes 12296 | tf_op jit(solution)/shard_map/ppermute | solution.py:353
  56.9 0.1 copy.17.seg_ext
  57.1 0.1 copy.18.seg_ext.seg_ext_a
  57.2 1.0 %shard_map.133 = (f32[256,128]{1,0:T(8,128)S(1)}, f32[256,128]{1,0:T(8,128)S(1)}, f32[256,128]{1,0:T(8,128)S(1)}, f32[72,128]{1,0:T(8,128)S(1)}, f32[256,128]{1,0:T(8,128)S(1)}) custom-call(f32[512,512]{1,0:T(8,128)S(1)} %shard_map.132.proj, s32[264,1]{1,0:T(8,128)S(1)} %copy.17.seg_ext, s32[1,256]{1,0:T(1,128)S(1)} %bitcast.16, f32[4,128]{1,0:T(4,128)S(1)} %copy-done.5, ...), custom_call_target="tpu_custom_call" | custom-call | flops 10000000 | bytes 2097152 | tf_op jit(solution)/shard_map/pallas_call | solution.py:358
  58.2 1.2 %shard_map.134 = (f32[256,128]{1,0:T(8,128)S(1)}, f32[256,128]{1,0:T(8,128)S(1)}, f32[256,128]{1,0:T(8,128)S(1)}, f32[256,128]{1,0:T(8,128)S(1)}, f32[256,128]{1...) custom-call(f32[512,512]{1,0:T(8,128)S(1)} %shard_map.132.proj, ...), custom_call_target="tpu_custom_call" | custom-call | flops 10000000 | bytes 2097152 | tf_op jit(solution)/shard_map/pallas_call | solution.py:363
  59.5 6.8 %all-gather = f32[288,128]{1,0:T(8,128)S(1)} all-gather(f32[72,128]{1,0:T(8,128)S(1)} %get-tuple-element.47), channel_id=2, replica_groups=mesh['seq'=4,'tensor'=8] {'seq'}, dimensions={0}, use_global_device_ids=true | all-gather | bytes 184320 | tf_op jit(solution)/shard_map/all_gather | solution.py:368
  66.3 1.6 %collective-permute-start.15 = (bf16[128,1792]{1,0:T(8,128)(2,1)}, bf16[128,1792]{1,0:T(8,128)(2,1)S(1)}, u32[]{:S(2)}, u32[]{:S(2)}) collective-permute-start(bf16[128,1792]{1,0:T(8,128)(2,1)} %collective-permute-done.12.rest_3_), channel_id=1, source_target_pairs={{0,2},{2,4},{4,6},{6,7},{7,5},{5,3},{3,1},{1,0},{8,10},{10,12},{12... | collective-permute-start | bytes 1376264 | tf_op jit(solution)/shard_map/ppermute | solution.py:31
  67.9 0.4 collective-permute-start.16
  68.4 1.8 %shard_map.135 = bf16[512,128]{1,0:T(8,128)(2,1)} custom-call(s32[1,1]{1,0:T(1,128)} %bitcast.seg_first, f32[4,72,128]{2,1,0:T(8,128)S(1)} %bitcast.11, s32[264,1]{1,0:T(8,128)S(1)} %copy.18.seg_ext.seg_ext_a, s32[1,256]{1,0:T(1,128)S(1)} %bitcast.15, f32[1,128]{1,0:T(1,128)S(1)} %broadcast_in_dim_reshape.11.skip, f32[512,512]{1,0:T(8,128)S(1)} %shard_map.132.proj, ...), custom_call_target="tpu_custom_call" | custom-call | flops 10000000 | bytes 2097152 | tf_op jit(solution)/shard_map/pallas_call | solution.py:369
  70.2 5.0 %all-to-all-start = ((bf16[8,64,128]{2,1,0:T(8,128)(2,1)}), bf16[8,64,128]{2,1,0:T(8,128)(2,1)S(1)}, u32[]{:S(2)}, u32[]{:S(2)}) async-start(bf16[8,64,128]{2,1,0:T(8,128)(2,1)} %bitcast.7), calls=%async_computation | async-start | bytes 262144 | tf_op jit(solution)/shard_map/all_to_all | solution.py:387
  75.2 4.5 %collective-permute-done.15.rest_5_.forth = bf16[128,1792]{1,0:T(8,128)(2,1)S(1)} collective-permute-done((bf16[128,1792]{1,0:T(8,128)(2,1)}, bf16[128,1792]{1,0:T(8,128)(2,1)S(1)}, u32[]{:S(2)}, u32[]{:S(2)}) %collective-permute-start.15) | collective-permute-done | bytes 458784 | tf_op jit(solution)/shard_map/ppermute | solution.py:31
  79.7 1.3 %collective-permute-done.16.rest_6_.back = bf16[128,1792]{1,0:T(8,128)(2,1)S(1)} collective-permute-done((bf16[128,1792]{1,0:T(8,128)(2,1)}, bf16[128,1792]{1,0:T(8,128)(2,1)S(1)}, u32[]{:S(2)}, u32[]{:S(2)}) %collective-permute-start.16) | collective-permute-done | bytes 458784 | tf_op jit(solution)/shard_map/ppermute | solution.py:31
  81.0 2.1 %collective-permute-start.17 = (bf16[64,1792]{1,0:T(8,128)(2,1)S(1)}, bf16[64,1792]{1,0:T(8,128)(2,1)S(1)}, u32[]{:S(2)}, u32[]{:S(2)}) collective-permute-start(bf16[64,1792]{1,0:T(8,128)(2,1)S(1)} %get-tuple-element.65), channel_id=1, source_target_pairs={{0,2},{2,4},{4,6},{6,7},{7,5},{5,3},{3,1},{1,0},{8,10},{10,12},{12... | collective-permute-start | bytes 688136 | tf_op jit(solution)/shard_map/ppermute | solution.py:31
  83.1 0.0 collective-permute-start.18
  83.1 1.5 %all-to-all-done.mine = bf16[8,64,128]{2,1,0:T(8,128)(2,1)S(1)} async-done(((bf16[8,64,128]{2,1,0:T(8,128)(2,1)}), bf16[8,64,128]{2,1,0:T(8,128)(2,1)S(1)}, u32[]{:S(2)}, u32[]{:S(2)}) %all-to-all-start) | async-done | bytes 131104 | tf_op jit(solution)/shard_map/all_to_all | solution.py:387
  84.6 1.3 %collective-permute-done.14.other = bf16[8,64,128]{2,1,0:T(8,128)(2,1)S(1)} collective-permute-done((bf16[8,64,128]{2,1,0:T(8,128)(2,1)S(1)}, bf16[8,64,128]{2,1,0:T(8,128)(2,1)S(1)}, u32[]{:S(2)}, u32[]{:S(2)}) %collective-permute-start.14) | collective-permute-done | bytes 131104 | tf_op jit(solution)/shard_map/ppermute | solution.py:389
  85.9 2.1 %shard_map.136.total = f32[128,1792]{1,0:T(8,128)S(1)} custom-call(bf16[8,64,128]{2,1,0:T(8,128)(2,1)S(1)} %all-to-all-done.mine, bf16[8,64,128]{2,1,0:T(8,128)(2,1)S(1)} %collective-permute-done.14.other, bf16[128,1792]{1,0:T(8,128)(2,1)S(1)} %multiply_convert_fusion.rest_0_, bf16[128,1792]{1,0:T(8,128)(2,1)S(1)} %collective-permute-done.10.rest_1_, ...), custom_call_target="tpu_custom_call" | custom-call | flops 1 | bytes 1 | tf_op jit(solution)/shard_map/pallas_call | solution.py:394
  88.1 1.0 %collective-permute-done.18.bottom = bf16[64,1792]{1,0:T(8,128)(2,1)S(1)} collective-permute-done((bf16[64,1792]{1,0:T(8,128)(2,1)S(1)}, bf16[64,1792]{1,0:T(8,128)(2,1)S(1)}, u32[]{:S(2)}, u32[]{:S(2)}) %collective-permute-start.18) | collective-permute-done | bytes 229408 | tf_op jit(solution)/shard_map/ppermute | solution.py:31
  89.1 0.2 shard_map.139
  89.3 0.1 collective-permute-start.19
  89.4 1.0 %shard_map.138.whole = bf16[64,3584]{1,0:T(8,128)(2,1)} custom-call(bf16[8,64,128]{2,1,0:T(8,128)(2,1)S(1)} %all-to-all-done.mine, f32[128,1792]{1,0:T(8,128)S(1)} %shard_map.136.total, bf16[64,1792]{1,0:T(8,128)(2,1)S(1)} %collective-permute-done.17.top, bf16[64,1792]{1,0:T(8,128)(2,1)S(1)} %collective-permute-done.18.bottom), custom_call_target="tpu_custom_call" | custom-call | flops 10000000 | bytes 2097152 | tf_op jit(solution)/shard_map/pallas_call | solution.py:401
  90.4 0.5 collective-permute-done.19.arrived
  90.9 0.7 shard_map.140
  (38 shorter events, 0.2 us)
Async XLA Ops:
  0.0 5.2 %copy-start = (bf16[3584,2]{0,1:T(2,128)(2,1)S(1)}, bf16[3584,2]{0,1:T(2,128)(2,1)}, u32[]{:S(2)}) copy-start(bf16[3584,2]{0,1:T(2,128)(2,1)} %param.16) | copy-start | bytes 43012
  0.0 13.8 %collective-permute-start = (bf16[448,512]{1,0:T(8,128)(2,1)}, bf16[448,512]{1,0:T(8,128)(2,1)}, u32[]{:S(2)}, u32[]{:S(2)}) collective-permute-start(bf16[448,512]{1,0:T(8,128)(2,1)} %bitcast.12), channel_id=1, source_target_pairs={{0,2},{2,4},{4,6},{6,7},{7,5},{5,3},{3,1},{1,0},{8,10},{10,12},{12... | collective-permute-start | bytes 1376264 | tf_op jit(solution)/shard_map/ppermute | solution.py:31
  3.0 12.6 %collective-permute-start.2 = (bf16[448,512]{1,0:T(8,128)(2,1)}, bf16[448,512]{1,0:T(8,128)(2,1)S(1)}, u32[]{:S(2)}, u32[]{:S(2)}) collective-permute-start(bf16[448,512]{1,0:T(8,128)(2,1)} %bitcast.13), channel_id=1, source_target_pairs={{0,1},{2,0},{4,2},{6,4},{7,6},{5,7},{3,5},{1,3},{8,9},{10,8},{12,1... | collective-permute-start | bytes 1376264 | tf_op jit(solution)/shard_map/ppermute | solution.py:31
  3.8 13.2 %collective-permute-start.3 = (s32[8]{0:T(128)S(1)}, s32[8]{0:T(128)S(1)}, u32[]{:S(2)}, u32[]{:S(2)}) collective-permute-start(s32[8]{0:T(128)S(1)} %slice.33), channel_id=1, source_target_pairs={{0,8},{8,16},{16,24},{1,9},{9,17},{17,25},{2,10},{10,18},{18,26},{... | collective-permute-start | bytes 104 | tf_op jit(solution)/shard_map/ppermute | solution.py:311
  6.4 1.5 %copy-start.1 = (bf16[2,3584,128]{2,1,0:T(8,128)(2,1)S(1)}, bf16[2,3584,128]{2,1,0:T(8,128)(2,1)}, u32[]{:S(2)}) copy-start(bf16[2,3584,128]{2,1,0:T(8,128)(2,1)} %refs_2_.7) | copy-start | bytes 5505028
  7.9 1.2 %copy-start.2 = (bf16[3584,128]{1,0:T(8,128)(2,1)S(1)}, bf16[3584,128]{1,0:T(8,128)(2,1)}, u32[]{:S(2)}) copy-start(bf16[3584,128]{1,0:T(8,128)(2,1)} %refs_3_.5) | copy-start | bytes 2752516
  9.1 1.0 %copy-start.4 = (bf16[512,448]{0,1:T(8,128)(2,1)S(1)}, bf16[512,448]{0,1:T(8,128)(2,1)}, u32[]{:S(2)}) copy-start(bf16[512,448]{0,1:T(8,128)(2,1)} %param.13) | copy-start | bytes 1376260
  10.1 5.7 %copy-start.8 = (s32[512]{0:T(512)S(1)}, s32[512]{0:T(512)}, u32[]{:S(2)}) copy-start(s32[512]{0:T(512)} %param.24) | copy-start | bytes 6148
  10.1 6.4 %copy-start.10 = (f32[2]{0:T(128)S(1)}, f32[2]{0:T(128)}, u32[]{:S(2)}) copy-start(f32[2]{0:T(128)} %param.17) | copy-start | bytes 28
  10.1 6.6 %copy-start.11 = (f32[2]{0:T(128)S(1)}, f32[2]{0:T(128)}, u32[]{:S(2)}) copy-start(f32[2]{0:T(128)} %param.18) | copy-start | bytes 28
  10.1 6.7 %copy-start.12 = (f32[2]{0:T(128)S(1)}, f32[2]{0:T(128)}, u32[]{:S(2)}) copy-start(f32[2]{0:T(128)} %param.19) | copy-start | bytes 28
  10.1 7.0 %copy-start.3 = (bf16[3584,128]{1,0:T(8,128)(2,1)S(1)}, bf16[3584,128]{1,0:T(8,128)(2,1)}, u32[]{:S(2)}) copy-start(bf16[3584,128]{1,0:T(8,128)(2,1)} %refs_3_.5) | copy-start | bytes 2752516
  13.8 12.3 %collective-permute-start.1 = (bf16[448,512]{1,0:T(8,128)(2,1)}, bf16[448,512]{1,0:T(8,128)(2,1)}, u32[]{:S(2)}, u32[]{:S(2)}) collective-permute-start(bf16[448,512]{1,0:T(8,128)(2,1)} %collective-permute-done.refs_0_), channel_id=1, source_target_pairs={{0,2},{2,4},{4,6},{6,7},{7,5},{5,3},{3,1},{1,0},{8,10},{10,12},{12... | collective-permute-start | bytes 1376264 | tf_op jit(solution)/shard_map/ppermute | solution.py:31
  15.6 12.0 %collective-permute-start.5 = (bf16[448,512]{1,0:T(8,128)(2,1)S(1)}, bf16[448,512]{1,0:T(8,128)(2,1)}, u32[]{:S(2)}, u32[]{:S(2)}) collective-permute-start(bf16[448,512]{1,0:T(8,128)(2,1)S(1)} %collective-permute-done.2.refs_1_), channel_id=1, source_target_pairs={{0,1},{2,0},{4,2},{6,4},{7,6},{5,7},{3,5},{1,3},{8,9},{10,8},{12,1... | collective-permute-start | bytes 1376264 | tf_op jit(solution)/shard_map/ppermute | solution.py:31
  17.0 11.0 %copy-start.7 = (bf16[128,3584]{1,0:T(8,128)(2,1)S(1)}, bf16[128,3584]{1,0:T(8,128)(2,1)}, u32[]{:S(2)}) copy-start(bf16[128,3584]{1,0:T(8,128)(2,1)} %param.23) | copy-start | bytes 2752516
  17.0 11.0 %copy-start.9 = (f32[128]{0:T(128)S(1)}, f32[128]{0:T(128)}, u32[]{:S(2)}) copy-start(f32[128]{0:T(128)} %param.22) | copy-start | bytes 1540
  26.0 13.7 %collective-permute-start.4 = (bf16[448,512]{1,0:T(8,128)(2,1)}, bf16[448,512]{1,0:T(8,128)(2,1)S(1)}, u32[]{:S(2)}, u32[]{:S(2)}) collective-permute-start(bf16[448,512]{1,0:T(8,128)(2,1)} %collective-permute-done.1.refs_0_), channel_id=1, source_target_pairs={{0,2},{2,4},{4,6},{6,7},{7,5},{5,3},{3,1},{1,0},{8,10},{10,12},{12... | collective-permute-start | bytes 1376264 | tf_op jit(solution)/shard_map/ppermute | solution.py:31
  27.6 13.7 %collective-permute-start.6 = (bf16[448,512]{1,0:T(8,128)(2,1)}, bf16[448,512]{1,0:T(8,128)(2,1)S(1)}, u32[]{:S(2)}, u32[]{:S(2)}) collective-permute-start(bf16[448,512]{1,0:T(8,128)(2,1)} %collective-permute-done.5.refs_1_), channel_id=1, source_target_pairs={{0,1},{2,0},{4,2},{6,4},{7,6},{5,7},{3,5},{1,3},{8,9},{10,8},{12,1... | collective-permute-start | bytes 1376264 | tf_op jit(solution)/shard_map/ppermute | solution.py:31
  28.2 21.3 %collective-permute-start.10 = (bf16[128,1792]{1,0:T(8,128)(2,1)S(1)}, bf16[128,1792]{1,0:T(8,128)(2,1)S(1)}, u32[]{:S(2)}, u32[]{:S(2)}) collective-permute-start(bf16[128,1792]{1,0:T(8,128)(2,1)S(1)} %multiply_convert_fusion.rest_0_), channel_id=1, source_target_pairs={{0,2},{2,4},{4,6},{6,7},{7,5},{5,3},{3,1},{1,0},{8,10},{10,12},{12... | collective-permute-start | bytes 1376264 | tf_op jit(solution)/shard_map/ppermute | solution.py:31
  29.9 20.8 %collective-permute-start.11 = (bf16[128,1792]{1,0:T(8,128)(2,1)S(1)}, bf16[128,1792]{1,0:T(8,128)(2,1)S(1)}, u32[]{:S(2)}, u32[]{:S(2)}) collective-permute-start(bf16[128,1792]{1,0:T(8,128)(2,1)S(1)} %multiply_convert_fusion.rest_0_), channel_id=1, source_target_pairs={{0,1},{2,0},{4,2},{6,4},{7,6},{5,7},{3,5},{1,3},{8,9},{10,8},{12,1... | collective-permute-start | bytes 1376264 | tf_op jit(solution)/shard_map/ppermute | solution.py:31
  41.3 10.7 %collective-permute-start.7 = (bf16[224,512]{1,0:T(8,128)(2,1)S(1)}, bf16[224,512]{1,0:T(8,128)(2,1)S(1)}, u32[]{:S(2)}, u32[]{:S(2)}) collective-permute-start(bf16[224,512]{1,0:T(8,128)(2,1)S(1)} %get-tuple-element.42), channel_id=1, source_target_pairs={{0,2},{2,4},{4,6},{6,7},{7,5},{5,3},{3,1},{1,0},{8,10},{10,12},{12... | collective-permute-start | bytes 688136 | tf_op jit(solution)/shard_map/ppermute | solution.py:31
  43.0 10.1 %collective-permute-start.8 = (bf16[224,512]{1,0:T(8,128)(2,1)S(1)}, bf16[224,512]{1,0:T(8,128)(2,1)S(1)}, u32[]{:S(2)}, u32[]{:S(2)}) collective-permute-start(bf16[224,512]{1,0:T(8,128)(2,1)S(1)} %get-tuple-element.43), channel_id=1, source_target_pairs={{0,1},{2,0},{4,2},{6,4},{7,6},{5,7},{3,5},{1,3},{8,9},{10,8},{12,1... | collective-permute-start | bytes 688136 | tf_op jit(solution)/shard_map/ppermute | solution.py:31
  53.1 13.2 %collective-permute-start.12 = (bf16[128,1792]{1,0:T(8,128)(2,1)S(1)}, bf16[128,1792]{1,0:T(8,128)(2,1)}, u32[]{:S(2)}, u32[]{:S(2)}) collective-permute-start(bf16[128,1792]{1,0:T(8,128)(2,1)S(1)} %collective-permute-done.10.rest_1_), channel_id=1, source_target_pairs={{0,2},{2,4},{4,6},{6,7},{7,5},{5,3},{3,1},{1,0},{8,10},{10,12},{12... | collective-permute-start | bytes 1376264 | tf_op jit(solution)/shard_map/ppermute | solution.py:31
  54.7 11.6 %collective-permute-start.13 = (bf16[128,1792]{1,0:T(8,128)(2,1)S(1)}, bf16[128,1792]{1,0:T(8,128)(2,1)}, u32[]{:S(2)}, u32[]{:S(2)}) collective-permute-start(bf16[128,1792]{1,0:T(8,128)(2,1)S(1)} %collective-permute-done.11.rest_2_), channel_id=1, source_target_pairs={{0,1},{2,0},{4,2},{6,4},{7,6},{5,7},{3,5},{1,3},{8,9},{10,8},{12,1... | collective-permute-start | bytes 1376264 | tf_op jit(solution)/shard_map/ppermute | solution.py:31
  55.1 2.1 %copy-start.5 = (f32[4,128]{1,0:T(4,128)S(1)}, f32[4,128]{1,0:T(4,128)}, u32[]{:S(2)}) copy-start(f32[4,128]{1,0:T(4,128)} %taps_x.3) | copy-start | bytes 6148
  55.1 2.1 %copy-start.6 = (f32[4,128]{1,0:T(4,128)S(1)}, f32[4,128]{1,0:T(4,128)}, u32[]{:S(2)}) copy-start(f32[4,128]{1,0:T(4,128)} %taps_bc.3) | copy-start | bytes 6148
  55.6 2.6 %collective-permute-start.9 = (bf16[8,256]{1,0:T(8,128)(2,1)S(1)}, bf16[8,256]{1,0:T(8,128)(2,1)S(1)}, u32[]{:S(2)}, u32[]{:S(2)}) collective-permute-start(bf16[8,256]{1,0:T(8,128)(2,1)S(1)} %slice.44), channel_id=1, source_target_pairs={{0,8},{8,16},{16,24},{1,9},{9,17},{17,25},{2,10},{10,18},{18,26},{... | collective-permute-start | bytes 12296 | tf_op jit(solution)/shard_map/ppermute | solution.py:353
  66.3 13.4 %collective-permute-start.15 = (bf16[128,1792]{1,0:T(8,128)(2,1)}, bf16[128,1792]{1,0:T(8,128)(2,1)S(1)}, u32[]{:S(2)}, u32[]{:S(2)}) collective-permute-start(bf16[128,1792]{1,0:T(8,128)(2,1)} %collective-permute-done.12.rest_3_), channel_id=1, source_target_pairs={{0,2},{2,4},{4,6},{6,7},{7,5},{5,3},{3,1},{1,0},{8,10},{10,12},{12... | collective-permute-start | bytes 1376264 | tf_op jit(solution)/shard_map/ppermute | solution.py:31
  67.9 13.1 %collective-permute-start.16 = (bf16[128,1792]{1,0:T(8,128)(2,1)}, bf16[128,1792]{1,0:T(8,128)(2,1)S(1)}, u32[]{:S(2)}, u32[]{:S(2)}) collective-permute-start(bf16[128,1792]{1,0:T(8,128)(2,1)} %collective-permute-done.13.rest_4_), channel_id=1, source_target_pairs={{0,1},{2,0},{4,2},{6,4},{7,6},{5,7},{3,5},{1,3},{8,9},{10,8},{12,1... | collective-permute-start | bytes 1376264 | tf_op jit(solution)/shard_map/ppermute | solution.py:31
  70.2 14.4 %all-to-all-start = ((bf16[8,64,128]{2,1,0:T(8,128)(2,1)}), bf16[8,64,128]{2,1,0:T(8,128)(2,1)S(1)}, u32[]{:S(2)}, u32[]{:S(2)}) async-start(bf16[8,64,128]{2,1,0:T(8,128)(2,1)} %bitcast.7), calls=%async_computation | async-start | bytes 262144 | tf_op jit(solution)/shard_map/all_to_all | solution.py:387
  81.0 7.0 %collective-permute-start.17 = (bf16[64,1792]{1,0:T(8,128)(2,1)S(1)}, bf16[64,1792]{1,0:T(8,128)(2,1)S(1)}, u32[]{:S(2)}, u32[]{:S(2)}) collective-permute-start(bf16[64,1792]{1,0:T(8,128)(2,1)S(1)} %get-tuple-element.65), channel_id=1, source_target_pairs={{0,2},{2,4},{4,6},{6,7},{7,5},{5,3},{3,1},{1,0},{8,10},{10,12},{12... | collective-permute-start | bytes 688136 | tf_op jit(solution)/shard_map/ppermute | solution.py:31
  83.1 6.0 %collective-permute-start.18 = (bf16[64,1792]{1,0:T(8,128)(2,1)S(1)}, bf16[64,1792]{1,0:T(8,128)(2,1)S(1)}, u32[]{:S(2)}, u32[]{:S(2)}) collective-permute-start(bf16[64,1792]{1,0:T(8,128)(2,1)S(1)} %get-tuple-element.66), channel_id=1, source_target_pairs={{0,1},{2,0},{4,2},{6,4},{7,6},{5,7},{3,5},{1,3},{8,9},{10,8},{12,1... | collective-permute-start | bytes 688136 | tf_op jit(solution)/shard_map/ppermute | solution.py:31
  84.5 1.3 %collective-permute-start.14 = (bf16[8,64,128]{2,1,0:T(8,128)(2,1)S(1)}, bf16[8,64,128]{2,1,0:T(8,128)(2,1)S(1)}, u32[]{:S(2)}, u32[]{:S(2)}) collective-permute-start(bf16[8,64,128]{2,1,0:T(8,128)(2,1)S(1)} %all-to-all-done.mine), channel_id=1, source_target_pairs={{0,8},{8,0},{16,24},{24,16},{1,9},{9,1},{17,25},{25,17},{2,10},{10... | collective-permute-start | bytes 393224 | tf_op jit(solution)/shard_map/ppermute | solution.py:389
  89.3 1.6 %collective-permute-start.19 = (bf16[64,1792]{1,0:T(8,128)(2,1)S(1)}, bf16[64,1792]{1,0:T(8,128)(2,1)S(1)}, u32[]{:S(2)}, u32[]{:S(2)}) collective-permute-start(bf16[64,1792]{1,0:T(8,128)(2,1)S(1)} %shard_map.139), channel_id=1, source_target_pairs={{0,8},{8,0},{16,24},{24,16},{1,9},{9,1},{17,25},{25,17},{2,10},{10... | collective-permute-start | bytes 688136 | tf_op jit(solution)/shard_map/ppermute | solution.py:400

commit v20 on v19

--- a/solution.py
+++ b/solution.py
@@ -14,7 +14,6 @@
 VMEM = pl.BlockSpec(memory_space=pltpu.VMEM)
 ANY = pl.BlockSpec(memory_space=pl.ANY)
 HALO = 8
-W_FIRST = 3
 
 
 def ring_place(index, n):
@@ -59,6 +58,23 @@
 def source_of(distance):
     n = lax.axis_size("tensor")
     return ring_index((ring_place(lax.axis_index("tensor"), n) + distance + n) % n, n)
+
+
+def near_start(side, whole, size):
+    odd = lax.axis_index("seq") // 2 % 2
+    return pl.multiple_of((odd if side == 0 else 1 - odd) * (whole - size), 16)
+
+
+def lacked_rows(*refs):
+    for side, (near, out) in enumerate(zip(refs[:2], refs[2:])):
+        out[...] = near[pl.ds(near_start(side, near.shape[0], out.shape[0]), out.shape[0])]
+
+
+def join(*refs):
+    for side, (near, lacked, out) in enumerate(zip(refs[:2], refs[2:4], refs[4:])):
+        for part, place in ((near, side), (lacked, 1 - side)):
+            size = part.shape[0]
+            out[pl.ds(near_start(place, out.shape[0], size), size)] = part[...]
 
 
 def project(distances, ahead, first, *refs):
@@ -306,6 +322,11 @@
     own = (lax.dynamic_slice_in_dim(w_out, core * columns, columns, 1).astype(F32) * norm_gain[:, None]).astype(BF16)
     last = n_tensor // 2
     w_half = width // 2
+    near = width * 5 // 8
+    odd = seq_at // 2 % 2
+    own_near = [lax.dynamic_slice_in_dim(own, place * (width - near), near, 0) for place in (odd, 1 - odd)]
+    other_y = [(i, i ^ 2) for i in range(n_seq)]
+    parts = lambda size: [shape(size, columns, kind=BF16)] * 2
     shift_rows = [(i, i + 1) for i in range(n_seq - 1)]
 
     seg_halo = lax.ppermute(segments[tok_rows - HALO :], "seq", shift_rows)
@@ -324,14 +345,19 @@
             forth, back = after(forth, projs[1], small), after(back, projs[1], small)
         elif step > 1:
             forth, back = after(forth, projs[step - 2]), after(back, projs[step - 2])
+        if step == 4:
+            w_lacked, forth, back = after((w_lacked, forth, back))
         arrivals = (forth, back)
         if step < last:
             forth, back = ring_shift(forth, 1), ring_shift(back, -1)
         else:
             far = far_shift(forth, back)
-        if step == W_FIRST:
-            w_forth, w_back = after((own, own), arrivals)
-            w_forth, w_back = ring_shift(w_forth, 1), ring_shift(w_back, -1)
+        if step == 2:
+            pair = after(own_near, arrivals)
+            w_near = ring_shift(pair[0], 1), ring_shift(pair[1], -1)
+        if step == 3:
+            lacked = call(lacked_rows, parts(width - near))(*after(w_near, arrivals))
+            w_lacked = [lax.ppermute(part, "seq", other_y) for part in lacked]
         ahead = last if step == last else 0
         total = projs[-1:]
         fetched = len(arrived) + bool(ahead)
@@ -345,6 +371,7 @@
         )(*[part for _, part in arrived], w_zx, w_bc, w_step, *total)
         projs.append(results[0])
         arrived = [(-step, forth), (step, back)]
+    w_forth, w_back = call(join, parts(width))(*w_near, *w_lacked)
     proj = call(project_far, shape(tok_rows, 4 * width), flops=10**9)(
         *far, results[1], projs[-1]
     )

time: 92.1 us -> 94 us (1.021)
  waiting for transfers between devices: 35 us -> 30.2 us
  local copies, waits for them, and re-layouts: 5.91 us -> 10.1 us
    unnamed x26 -> x34, local copies, waits for them, and re-layouts: 3.73 us -> 7.09 us
    ppermute x16, waiting for transfers between devices: 31.7 us -> 28.5 us  [ring_shift(): lax.ppermute(block, 'tensor', [(order[i], order[(i + step) % n]) for i in...]
    ppermute x0 -> x2, starting transfers between devices: none -> 2.09 us  [local(): w_lacked = [lax.ppermute(part, 'seq', other_y) for part in lacked]]
    all_to_all x1, waiting for transfers between devices: 1.46 us -> 0.01 us  [local(): mine = lax.all_to_all(blocks, 'tensor', 0, 0)]
    all_to_all x1, starting transfers between devices: 5 us -> 3.71 us  [local(): mine = lax.all_to_all(blocks, 'tensor', 0, 0)]
  transfers between devices with their start and end apart: 21 -> 23, of which waited for: 14 -> 13; matrix products, arithmetic and copies ran while one was open for 4% -> 5% of each run, Pallas kernels for 18% -> 18%
where the time goes in v20:
time: 94 us; the launch traced here: 93.3 us
  waiting for transfers between devices  30.2 us (32%)
  starting transfers between devices  26 us (28%)
  Pallas kernels  18 us (19%)
  local copies, waits for them, and re-layouts  10.1 us (11%)
  blocking collectives  7.35 us (8%)
  matrix products  1.11 us (1%)
    ppermute x16, waiting for transfers between devices, ring_shift(): lax.ppermute(block, 'tensor', [(order[i], order[(i + step) % n]) for i in...  28.5 us
    ppermute x16, starting transfers between devices, ring_shift(): lax.ppermute(block, 'tensor', [(order[i], order[(i + step) % n]) for i in...  17.3 us
    pallas_call x4, Pallas kernels, local(): call(functools.partial(project, [distance for distance, _ in arrived], ah...  8.7 us
    all_gather x1, blocking collectives, local(): messages = lax.all_gather(message, 'seq')  7.35 us
    unnamed x34, local copies, waits for them, and re-layouts  7.09 us
    all_to_all x1, starting transfers between devices, local(): mine = lax.all_to_all(blocks, 'tensor', 0, 0)  3.71 us
    ppermute x2, starting transfers between devices, local(): w_lacked = [lax.ppermute(part, 'seq', other_y) for part in lacked]  2.09 us
    pallas_call x1, Pallas kernels, local(): call(functools.partial(product_early, distances), shape(2 * tok_own, colu...  2 us
  transfers between devices with their start and end apart: 23, of which 13 were waited for; matrix products, arithmetic and copies ran while one was open for 5% of the time, Pallas kernels for 18%

profile of v20, /device:TPU:0, one launch (start us, length us, event | category | flops | bytes accessed | tf_op | source)
XLA Modules:
  0.0 93.3 jit_solution(8606735307893997326)
XLA Ops:
  0.0 3.0 %collective-permute-start = (bf16[448,512]{1,0:T(8,128)(2,1)}, bf16[448,512]{1,0:T(8,128)(2,1)}, u32[]{:S(2)}, u32[]{:S(2)}) collective-permute-start(bf16[448,512]{1,0:T(8,128)(2,1)} %bitcast.12), channel_id=1, source_target_pairs={{0,2},{2,4},{4,6},{6,7},{7,5},{5,3},{3,1},{1,0},{8,10},{10,12},{12... | collective-permute-start | bytes 1376264 | tf_op jit(solution)/shard_map/ppermute | solution.py:30
  3.0 0.8 slice.33
  3.8 1.4 %collective-permute-start.5 = (s32[8]{0:T(128)S(1)}, s32[8]{0:T(128)S(1)}, u32[]{:S(2)}, u32[]{:S(2)}) collective-permute-start(s32[8]{0:T(128)S(1)} %slice.33), channel_id=1, source_target_pairs={{0,8},{8,16},{16,24},{1,9},{9,17},{17,25},{2,10},{10,18},{18,26},{... | collective-permute-start | bytes 104 | tf_op jit(solution)/shard_map/ppermute | solution.py:332
  5.2 0.8 fusion.1
  6.0 1.1 %convolution_bitcast_fusion.refs_3_.refs_4_ = bf16[3584,128]{1,0:T(8,128)(2,1)S(1)} fusion(bf16[2,128]{1,0:T(2,128)(2,1)} %constant.45.clone, bf16[3584,2]{0,1:T(2,128)(2,1)S(1)} %copy-done), kind=kOutput, calls=%fused_computation | convolution fusion | flops 1835008 | bytes 932352 | tf_op jit(solution)/shard_map/dot_general | solution.py:318
  7.1 1.5 %copy-done.1 = bf16[2,3584,128]{2,1,0:T(8,128)(2,1)S(1)} copy-done((bf16[2,3584,128]{2,1,0:T(8,128)(2,1)S(1)}, bf16[2,3584,128]{2,1,0:T(8,128)(2,1)}, u32[]{:S(2)}) %copy-start.1) | copy-done | bytes 1835032
  8.6 1.2 %copy-done.2 = bf16[3584,128]{1,0:T(8,128)(2,1)S(1)} copy-done((bf16[3584,128]{1,0:T(8,128)(2,1)S(1)}, bf16[3584,128]{1,0:T(8,128)(2,1)}, u32[]{:S(2)}) %copy-start.2) | copy-done | bytes 917528
  9.8 1.0 %copy-done.4 = bf16[512,448]{0,1:T(8,128)(2,1)S(1)} copy-done((bf16[512,448]{0,1:T(8,128)(2,1)S(1)}, bf16[512,448]{0,1:T(8,128)(2,1)}, u32[]{:S(2)}) %copy-start.4) | copy-done | bytes 458776
  10.9 0.6 shard_map.127.refs_5_
  11.5 0.5 copy-done.11
  12.0 0.1 multiply_convert_fusion.rest_0_
  12.2 1.6 %collective-permute-done.refs_0_ = bf16[448,512]{1,0:T(8,128)(2,1)} collective-permute-done((bf16[448,512]{1,0:T(8,128)(2,1)}, bf16[448,512]{1,0:T(8,128)(2,1)}, u32[]{:S(2)}, u32[]{:S(2)}) %collective-permute-start) | collective-permute-done | bytes 458784 | tf_op jit(solution)/shard_map/ppermute | solution.py:30
  13.8 1.5 %collective-permute-done.1.refs_1_ = bf16[448,512]{1,0:T(8,128)(2,1)} collective-permute-done((bf16[448,512]{1,0:T(8,128)(2,1)}, bf16[448,512]{1,0:T(8,128)(2,1)}, u32[]{:S(2)}, u32[]{:S(2)}) %collective-permute-start.1) | collective-permute-done | bytes 458784 | tf_op jit(solution)/shard_map/ppermute | solution.py:30
  15.3 1.6 %collective-permute-start.4 = (bf16[448,512]{1,0:T(8,128)(2,1)}, bf16[448,512]{1,0:T(8,128)(2,1)}, u32[]{:S(2)}, u32[]{:S(2)}) collective-permute-start(bf16[448,512]{1,0:T(8,128)(2,1)} %collective-permute-done.refs_0_), channel_id=1, source_target_pairs={{0,2},{2,4},{4,6},{6,7},{7,5},{5,3},{3,1},{1,0},{8,10},{10,12},{12... | collective-permute-start | bytes 1376264 | tf_op jit(solution)/shard_map/ppermute | solution.py:30
  16.9 0.4 collective-permute-start.6
  17.4 0.7 fusion
  18.2 0.1 broadcast_in_dim_reshape.9.bias
  18.3 0.1 broadcast_in_dim_reshape.10.rate
  18.5 0.1 broadcast_in_dim_reshape.11.skip
  18.7 1.6 %collective-permute-start.2 = (bf16[80,1792]{1,0:T(8,128)(2,1)S(1)}, bf16[80,1792]{1,0:T(8,128)(2,1)S(1)}, u32[]{:S(2)}, u32[]{:S(2)}) collective-permute-start(bf16[80,1792]{1,0:T(8,128)(2,1)S(1)} %get-tuple-element.48), channel_id=1, source_target_pairs={{0,2},{2,4},{4,6},{6,7},{7,5},{5,3},{3,1},{1,0},{8,10},{10,12},{12... | collective-permute-start | bytes 860168 | tf_op jit(solution)/shard_map/ppermute | solution.py:30
  20.3 0.4 collective-permute-start.3
  20.7 3.0 %shard_map.128.refs_5_ = f32[512,512]{1,0:T(8,128)S(1)} custom-call(bf16[448,512]{1,0:T(8,128)(2,1)} %collective-permute-done.refs_0_, bf16[448,512]{1,0:T(8,128)(2,1)} %collective-permute-done.1.refs_1_, bf16[2,3584,128]{2,1,0:T(8,128)(2,1)} %refs_2_.7, bf16[3584,128]{1,0:T(8,128)(2,1)S(1)} %copy-done.3, ...), custom_call_target="tpu_custom_call" | custom-call | flops 1000000000 | bytes 2097152 | tf_op jit(solution)/shard_map/pallas_call | solution.py:365
  23.8 5.3 %collective-permute-done.4.refs_0_ = bf16[448,512]{1,0:T(8,128)(2,1)} collective-permute-done((bf16[448,512]{1,0:T(8,128)(2,1)}, bf16[448,512]{1,0:T(8,128)(2,1)}, u32[]{:S(2)}, u32[]{:S(2)}) %collective-permute-start.4) | collective-permute-done | bytes 458784 | tf_op jit(solution)/shard_map/ppermute | solution.py:30
  29.1 1.6 %collective-permute-start.9 = (bf16[448,512]{1,0:T(8,128)(2,1)}, bf16[448,512]{1,0:T(8,128)(2,1)S(1)}, u32[]{:S(2)}, u32[]{:S(2)}) collective-permute-start(bf16[448,512]{1,0:T(8,128)(2,1)} %collective-permute-done.4.refs_0_), channel_id=1, source_target_pairs={{0,2},{2,4},{4,6},{6,7},{7,5},{5,3},{3,1},{1,0},{8,10},{10,12},{12... | collective-permute-start | bytes 1376264 | tf_op jit(solution)/shard_map/ppermute | solution.py:30
  30.7 0.5 collective-permute-start.10
  31.1 4.0 %collective-permute-done.2.refs_0_ = bf16[80,1792]{1,0:T(8,128)(2,1)S(1)} collective-permute-done((bf16[80,1792]{1,0:T(8,128)(2,1)S(1)}, bf16[80,1792]{1,0:T(8,128)(2,1)S(1)}, u32[]{:S(2)}, u32[]{:S(2)}) %collective-permute-start.2) | collective-permute-done | bytes 286752 | tf_op jit(solution)/shard_map/ppermute | solution.py:30
  35.1 1.6 %collective-permute-done.3.refs_1_ = bf16[80,1792]{1,0:T(8,128)(2,1)S(1)} collective-permute-done((bf16[80,1792]{1,0:T(8,128)(2,1)S(1)}, bf16[80,1792]{1,0:T(8,128)(2,1)S(1)}, u32[]{:S(2)}, u32[]{:S(2)}) %collective-permute-start.3) | collective-permute-done | bytes 286752 | tf_op jit(solution)/shard_map/ppermute | solution.py:30
  36.7 1.6 %collective-permute-start.7 = (bf16[48,1792]{1,0:T(8,128)(2,1)S(1)}, bf16[48,1792]{1,0:T(8,128)(2,1)S(1)}, u32[]{:S(2)}, u32[]{:S(2)}) collective-permute-start(bf16[48,1792]{1,0:T(8,128)(2,1)S(1)} %get-tuple-element.54), channel_id=1, source_target_pairs={{0,16},{8,24},{16,0},{24,8},{1,17},{9,25},{17,1},{25,9},{2,18},{10... | collective-permute-start | bytes 516104 | tf_op jit(solution)/shard_map/ppermute | solution.py:360
  38.3 0.5 collective-permute-start.8
  38.8 3.0 %shard_map.130.refs_5_ = f32[512,512]{1,0:T(8,128)S(1)} custom-call(bf16[448,512]{1,0:T(8,128)(2,1)} %collective-permute-done.4.refs_0_, bf16[448,512]{1,0:T(8,128)(2,1)} %collective-permute-done.6.refs_1_, bf16[2,3584,128]{2,1,0:T(8,128)(2,1)} %refs_2_.7, bf16[3584,128]{1,0:T(8,128)(2,1)S(1)} %copy-done.3, ...), custom_call_target="tpu_custom_call" | custom-call | flops 1000000000 | bytes 2097152 | tf_op jit(solution)/shard_map/pallas_call | solution.py:365
  41.9 1.5 %collective-permute-done.9.forth.refs_0_ = bf16[448,512]{1,0:T(8,128)(2,1)S(1)} collective-permute-done((bf16[448,512]{1,0:T(8,128)(2,1)}, bf16[448,512]{1,0:T(8,128)(2,1)S(1)}, u32[]{:S(2)}, u32[]{:S(2)}) %collective-permute-start.9) | collective-permute-done | bytes 458784 | tf_op jit(solution)/shard_map/ppermute | solution.py:30
  43.4 1.3 %collective-permute-done.10.back.refs_1_ = bf16[448,512]{1,0:T(8,128)(2,1)S(1)} collective-permute-done((bf16[448,512]{1,0:T(8,128)(2,1)}, bf16[448,512]{1,0:T(8,128)(2,1)S(1)}, u32[]{:S(2)}, u32[]{:S(2)}) %collective-permute-start.10) | collective-permute-done | bytes 458784 | tf_op jit(solution)/shard_map/ppermute | solution.py:30
  44.7 1.6 %collective-permute-start.11 = (bf16[224,512]{1,0:T(8,128)(2,1)S(1)}, bf16[224,512]{1,0:T(8,128)(2,1)S(1)}, u32[]{:S(2)}, u32[]{:S(2)}) collective-permute-start(bf16[224,512]{1,0:T(8,128)(2,1)S(1)} %get-tuple-element.60), channel_id=1, source_target_pairs={{0,2},{2,4},{4,6},{6,7},{7,5},{5,3},{3,1},{1,0},{8,10},{10,12},{12... | collective-permute-start | bytes 688136 | tf_op jit(solution)/shard_map/ppermute | solution.py:30
  46.3 0.4 collective-permute-start.12
  46.8 0.1 shard_map.137
  46.9 2.1 %shard_map.132 = (f32[512,512]{1,0:T(8,128)S(1)}, bf16[448,512]{1,0:T(8,128)(2,1)S(1)}) custom-call(bf16[448,512]{1,0:T(8,128)(2,1)S(1)} %collective-permute-done.9.forth.refs_0_, bf16[448,512]{1,0:T(8,128)(2,1)S(1)} %collective-permute-done.10.back.refs_1_, bf16[2,3584,128]{2,1,0:T(8,128)(2,1)} %refs_2_.7, bf16[3584,128]{1,0:T(8,128)(2,1)S(1)} %copy-done.3, ...), custom_call_target="tpu_custom_call" | custom-call | flops 1000000000 | bytes 2097152 | tf_op jit(solution)/shard_map/pallas_call | solution.py:365
  49.0 1.8 %collective-permute-done.11.top = bf16[224,512]{1,0:T(8,128)(2,1)S(1)} collective-permute-done((bf16[224,512]{1,0:T(8,128)(2,1)S(1)}, bf16[224,512]{1,0:T(8,128)(2,1)S(1)}, u32[]{:S(2)}, u32[]{:S(2)}) %collective-permute-start.11) | collective-permute-done | bytes 229408 | tf_op jit(solution)/shard_map/ppermute | solution.py:30
  50.8 1.6 %collective-permute-done.12.bottom = bf16[224,512]{1,0:T(8,128)(2,1)S(1)} collective-permute-done((bf16[224,512]{1,0:T(8,128)(2,1)S(1)}, bf16[224,512]{1,0:T(8,128)(2,1)S(1)}, u32[]{:S(2)}, u32[]{:S(2)}) %collective-permute-start.12) | collective-permute-done | bytes 229408 | tf_op jit(solution)/shard_map/ppermute | solution.py:30
  52.4 2.0 %collective-permute-start.14 = (bf16[128,1792]{1,0:T(8,128)(2,1)S(1)}, bf16[128,1792]{1,0:T(8,128)(2,1)S(1)}, u32[]{:S(2)}, u32[]{:S(2)}) collective-permute-start(bf16[128,1792]{1,0:T(8,128)(2,1)S(1)} %get-tuple-element.80.rest_1_), channel_id=1, source_target_pairs={{0,2},{2,4},{4,6},{6,7},{7,5},{5,3},{3,1},{1,0},{8,10},{10,12},{12... | collective-permute-start | bytes 1376264 | tf_op jit(solution)/shard_map/ppermute | solution.py:30
  54.4 0.5 shard_map.133.proj
  54.9 1.3 %collective-permute-start.13 = (bf16[8,256]{1,0:T(8,128)(2,1)S(1)}, bf16[8,256]{1,0:T(8,128)(2,1)S(1)}, u32[]{:S(2)}, u32[]{:S(2)}) collective-permute-start(bf16[8,256]{1,0:T(8,128)(2,1)S(1)} %slice.44), channel_id=1, source_target_pairs={{0,8},{8,16},{16,24},{1,9},{9,17},{17,25},{2,10},{10,18},{18,26},{... | collective-permute-start | bytes 12296 | tf_op jit(solution)/shard_map/ppermute | solution.py:380
  56.2 0.1 copy.17.seg_ext
  56.3 0.1 copy.18.seg_ext.seg_ext_a
  56.5 1.0 %shard_map.134 = (f32[256,128]{1,0:T(8,128)S(1)}, f32[256,128]{1,0:T(8,128)S(1)}, f32[256,128]{1,0:T(8,128)S(1)}, f32[72,128]{1,0:T(8,128)S(1)}, f32[256,128]{1,0:T(8,128)S(1)}) custom-call(f32[512,512]{1,0:T(8,128)S(1)} %shard_map.133.proj, s32[264,1]{1,0:T(8,128)S(1)} %copy.17.seg_ext, s32[1,256]{1,0:T(1,128)S(1)} %bitcast.16, f32[4,128]{1,0:T(4,128)S(1)} %copy-done.9, ...), custom_call_target="tpu_custom_call" | custom-call | flops 10000000 | bytes 2097152 | tf_op jit(solution)/shard_map/pallas_call | solution.py:385
  57.5 1.3 %shard_map.135 = (f32[256,128]{1,0:T(8,128)S(1)}, f32[256,128]{1,0:T(8,128)S(1)}, f32[256,128]{1,0:T(8,128)S(1)}, f32[256,128]{1,0:T(8,128)S(1)}, f32[256,128]{1...) custom-call(f32[512,512]{1,0:T(8,128)S(1)} %shard_map.133.proj, ...), custom_call_target="tpu_custom_call" | custom-call | flops 10000000 | bytes 2097152 | tf_op jit(solution)/shard_map/pallas_call | solution.py:390
  58.8 7.3 %all-gather = f32[288,128]{1,0:T(8,128)S(1)} all-gather(f32[72,128]{1,0:T(8,128)S(1)} %get-tuple-element.65), channel_id=2, replica_groups=mesh['seq'=4,'tensor'=8] {'seq'}, dimensions={0}, use_global_device_ids=true | all-gather | bytes 184320 | tf_op jit(solution)/shard_map/all_gather | solution.py:395
  66.1 0.8 copy-done.7
  66.9 2.0 %collective-permute-start.17 = (bf16[128,1792]{1,0:T(8,128)(2,1)}, bf16[128,1792]{1,0:T(8,128)(2,1)S(1)}, u32[]{:S(2)}, u32[]{:S(2)}) collective-permute-start(bf16[128,1792]{1,0:T(8,128)(2,1)} %copy-done.7), channel_id=1, source_target_pairs={{0,2},{2,4},{4,6},{6,7},{7,5},{5,3},{3,1},{1,0},{8,10},{10,12},{12... | collective-permute-start | bytes 1376264 | tf_op jit(solution)/shard_map/ppermute | solution.py:30
  69.0 1.8 %shard_map.136 = bf16[512,128]{1,0:T(8,128)(2,1)} custom-call(s32[1,1]{1,0:T(1,128)} %bitcast.seg_first, f32[4,72,128]{2,1,0:T(8,128)S(1)} %bitcast.11, s32[264,1]{1,0:T(8,128)S(1)} %copy.18.seg_ext.seg_ext_a, s32[1,256]{1,0:T(1,128)S(1)} %bitcast.15, f32[1,128]{1,0:T(1,128)S(1)} %broadcast_in_dim_reshape.11.skip, f32[512,512]{1,0:T(8,128)S(1)} %shard_map.133.proj, ...), custom_call_target="tpu_custom_call" | custom-call | flops 10000000 | bytes 2097152 | tf_op jit(solution)/shard_map/pallas_call | solution.py:396
  70.8 3.7 %all-to-all-start = ((bf16[8,64,128]{2,1,0:T(8,128)(2,1)}), bf16[8,64,128]{2,1,0:T(8,128)(2,1)S(1)}, u32[]{:S(2)}, u32[]{:S(2)}) async-start(bf16[8,64,128]{2,1,0:T(8,128)(2,1)} %bitcast.7), calls=%async_computation | async-start | bytes 262144 | tf_op jit(solution)/shard_map/all_to_all | solution.py:414
  74.5 6.3 %collective-permute-done.17.rest_5_.forth = bf16[128,1792]{1,0:T(8,128)(2,1)S(1)} collective-permute-done((bf16[128,1792]{1,0:T(8,128)(2,1)}, bf16[128,1792]{1,0:T(8,128)(2,1)S(1)}, u32[]{:S(2)}, u32[]{:S(2)}) %collective-permute-start.17) | collective-permute-done | bytes 458784 | tf_op jit(solution)/shard_map/ppermute | solution.py:30
  80.8 1.9 %collective-permute-done.18.rest_6_.back = bf16[128,1792]{1,0:T(8,128)(2,1)S(1)} collective-permute-done((bf16[128,1792]{1,0:T(8,128)(2,1)}, bf16[128,1792]{1,0:T(8,128)(2,1)S(1)}, u32[]{:S(2)}, u32[]{:S(2)}) %collective-permute-start.18) | collective-permute-done | bytes 458784 | tf_op jit(solution)/shard_map/ppermute | solution.py:30
  82.7 0.7 shard_map.139
  83.4 1.1 %collective-permute-start.19 = (bf16[64,1792]{1,0:T(8,128)(2,1)}, bf16[64,1792]{1,0:T(8,128)(2,1)S(1)}, u32[]{:S(2)}, u32[]{:S(2)}) collective-permute-start(bf16[64,1792]{1,0:T(8,128)(2,1)} %get-tuple-element.85), channel_id=1, source_target_pairs={{0,2},{2,4},{4,6},{6,7},{7,5},{5,3},{3,1},{1,0},{8,10},{10,12},{12... | collective-permute-start | bytes 688136 | tf_op jit(solution)/shard_map/ppermute | solution.py:30
  84.5 0.9 collective-permute-start.20
  85.4 1.3 %collective-permute-done.16.other = bf16[8,64,128]{2,1,0:T(8,128)(2,1)S(1)} collective-permute-done((bf16[8,64,128]{2,1,0:T(8,128)(2,1)S(1)}, bf16[8,64,128]{2,1,0:T(8,128)(2,1)S(1)}, u32[]{:S(2)}, u32[]{:S(2)}) %collective-permute-start.16) | collective-permute-done | bytes 131104 | tf_op jit(solution)/shard_map/ppermute | solution.py:416
  86.8 1.0 %copy-done.6 = bf16[128,1792]{1,0:T(8,128)(2,1)S(1)} copy-done((bf16[128,1792]{1,0:T(8,128)(2,1)S(1)}, bf16[128,1792]{1,0:T(8,128)(2,1)}, u32[]{:S(2)}) %copy-start.6) | copy-done | bytes 458776
  87.8 1.0 %copy-done.8 = bf16[128,1792]{1,0:T(8,128)(2,1)S(1)} copy-done((bf16[128,1792]{1,0:T(8,128)(2,1)S(1)}, bf16[128,1792]{1,0:T(8,128)(2,1)}, u32[]{:S(2)}) %copy-start.8) | copy-done | bytes 458776
  88.8 2.0 %shard_map.138.total = f32[128,1792]{1,0:T(8,128)S(1)} custom-call(bf16[8,64,128]{2,1,0:T(8,128)(2,1)S(1)} %all-to-all-done.mine, bf16[8,64,128]{2,1,0:T(8,128)(2,1)S(1)} %collective-permute-done.16.other, bf16[128,1792]{1,0:T(8,128)(2,1)S(1)} %multiply_convert_fusion.rest_0_, bf16[128,1792]{1,0:T(8,128)(2,1)S(1)} %get-tuple-element.80.rest_1_, ...), custom_call_target="tpu_custom_call" | custom-call | flops 1 | bytes 1 | tf_op jit(solution)/shard_map/pallas_call | solution.py:421
  90.8 0.2 shard_map.141
  91.0 0.2 collective-permute-start.21
  91.3 1.0 %shard_map.140.whole = bf16[64,3584]{1,0:T(8,128)(2,1)} custom-call(bf16[8,64,128]{2,1,0:T(8,128)(2,1)S(1)} %all-to-all-done.mine, f32[128,1792]{1,0:T(8,128)S(1)} %shard_map.138.total, bf16[64,1792]{1,0:T(8,128)(2,1)S(1)} %collective-permute-done.19.top, bf16[64,1792]{1,0:T(8,128)(2,1)S(1)} %collective-permute-done.20.bottom), custom_call_target="tpu_custom_call" | custom-call | flops 10000000 | bytes 2097152 | tf_op jit(solution)/shard_map/pallas_call | solution.py:428
  92.2 0.4 collective-permute-done.21.arrived
  92.6 0.7 shard_map.142
  (53 shorter events, 0.6 us)
Async XLA Ops:
  0.0 6.0 %copy-start = (bf16[3584,2]{0,1:T(2,128)(2,1)S(1)}, bf16[3584,2]{0,1:T(2,128)(2,1)}, u32[]{:S(2)}) copy-start(bf16[3584,2]{0,1:T(2,128)(2,1)} %param.16) | copy-start | bytes 43012
  0.0 13.8 %collective-permute-start = (bf16[448,512]{1,0:T(8,128)(2,1)}, bf16[448,512]{1,0:T(8,128)(2,1)}, u32[]{:S(2)}, u32[]{:S(2)}) collective-permute-start(bf16[448,512]{1,0:T(8,128)(2,1)} %bitcast.12), channel_id=1, source_target_pairs={{0,2},{2,4},{4,6},{6,7},{7,5},{5,3},{3,1},{1,0},{8,10},{10,12},{12... | collective-permute-start | bytes 1376264 | tf_op jit(solution)/shard_map/ppermute | solution.py:30
  3.0 12.3 %collective-permute-start.1 = (bf16[448,512]{1,0:T(8,128)(2,1)}, bf16[448,512]{1,0:T(8,128)(2,1)}, u32[]{:S(2)}, u32[]{:S(2)}) collective-permute-start(bf16[448,512]{1,0:T(8,128)(2,1)} %bitcast.13), channel_id=1, source_target_pairs={{0,1},{2,0},{4,2},{6,4},{7,6},{5,7},{3,5},{1,3},{8,9},{10,8},{12,1... | collective-permute-start | bytes 1376264 | tf_op jit(solution)/shard_map/ppermute | solution.py:30
  3.8 14.8 %collective-permute-start.5 = (s32[8]{0:T(128)S(1)}, s32[8]{0:T(128)S(1)}, u32[]{:S(2)}, u32[]{:S(2)}) collective-permute-start(s32[8]{0:T(128)S(1)} %slice.33), channel_id=1, source_target_pairs={{0,8},{8,16},{16,24},{1,9},{9,17},{17,25},{2,10},{10,18},{18,26},{... | collective-permute-start | bytes 104 | tf_op jit(solution)/shard_map/ppermute | solution.py:332
  7.1 1.5 %copy-start.1 = (bf16[2,3584,128]{2,1,0:T(8,128)(2,1)S(1)}, bf16[2,3584,128]{2,1,0:T(8,128)(2,1)}, u32[]{:S(2)}) copy-start(bf16[2,3584,128]{2,1,0:T(8,128)(2,1)} %refs_2_.7) | copy-start | bytes 5505028
  8.6 1.2 %copy-start.2 = (bf16[3584,128]{1,0:T(8,128)(2,1)S(1)}, bf16[3584,128]{1,0:T(8,128)(2,1)}, u32[]{:S(2)}) copy-start(bf16[3584,128]{1,0:T(8,128)(2,1)} %refs_3_.5) | copy-start | bytes 2752516
  9.8 1.0 %copy-start.4 = (bf16[512,448]{0,1:T(8,128)(2,1)S(1)}, bf16[512,448]{0,1:T(8,128)(2,1)}, u32[]{:S(2)}) copy-start(bf16[512,448]{0,1:T(8,128)(2,1)} %param.13) | copy-start | bytes 1376260
  10.8 1.2 %copy-start.11 = (bf16[128,3584]{1,0:T(8,128)(2,1)S(1)}, bf16[128,3584]{1,0:T(8,128)(2,1)}, u32[]{:S(2)}) copy-start(bf16[128,3584]{1,0:T(8,128)(2,1)} %param.23) | copy-start | bytes 2752516
  10.8 1.2 %copy-start.13 = (f32[128]{0:T(128)S(1)}, f32[128]{0:T(128)}, u32[]{:S(2)}) copy-start(f32[128]{0:T(128)} %param.22) | copy-start | bytes 1540
  10.8 6.5 %copy-start.12 = (s32[512]{0:T(512)S(1)}, s32[512]{0:T(512)}, u32[]{:S(2)}) copy-start(s32[512]{0:T(512)} %param.24) | copy-start | bytes 6148
  10.8 7.3 %copy-start.14 = (f32[2]{0:T(128)S(1)}, f32[2]{0:T(128)}, u32[]{:S(2)}) copy-start(f32[2]{0:T(128)} %param.17) | copy-start | bytes 28
  10.8 7.4 %copy-start.15 = (f32[2]{0:T(128)S(1)}, f32[2]{0:T(128)}, u32[]{:S(2)}) copy-start(f32[2]{0:T(128)} %param.18) | copy-start | bytes 28
  10.9 7.6 %copy-start.16 = (f32[2]{0:T(128)S(1)}, f32[2]{0:T(128)}, u32[]{:S(2)}) copy-start(f32[2]{0:T(128)} %param.19) | copy-start | bytes 28
  12.0 8.7 %copy-start.3 = (bf16[3584,128]{1,0:T(8,128)(2,1)S(1)}, bf16[3584,128]{1,0:T(8,128)(2,1)}, u32[]{:S(2)}) copy-start(bf16[3584,128]{1,0:T(8,128)(2,1)} %refs_3_.5) | copy-start | bytes 2752516
  15.3 13.8 %collective-permute-start.4 = (bf16[448,512]{1,0:T(8,128)(2,1)}, bf16[448,512]{1,0:T(8,128)(2,1)}, u32[]{:S(2)}, u32[]{:S(2)}) collective-permute-start(bf16[448,512]{1,0:T(8,128)(2,1)} %collective-permute-done.refs_0_), channel_id=1, source_target_pairs={{0,2},{2,4},{4,6},{6,7},{7,5},{5,3},{3,1},{1,0},{8,10},{10,12},{12... | collective-permute-start | bytes 1376264 | tf_op jit(solution)/shard_map/ppermute | solution.py:30
  16.9 13.8 %collective-permute-start.6 = (bf16[448,512]{1,0:T(8,128)(2,1)}, bf16[448,512]{1,0:T(8,128)(2,1)}, u32[]{:S(2)}, u32[]{:S(2)}) collective-permute-start(bf16[448,512]{1,0:T(8,128)(2,1)} %collective-permute-done.1.refs_1_), channel_id=1, source_target_pairs={{0,1},{2,0},{4,2},{6,4},{7,6},{5,7},{3,5},{1,3},{8,9},{10,8},{12,1... | collective-permute-start | bytes 1376264 | tf_op jit(solution)/shard_map/ppermute | solution.py:30
  18.7 16.4 %collective-permute-start.2 = (bf16[80,1792]{1,0:T(8,128)(2,1)S(1)}, bf16[80,1792]{1,0:T(8,128)(2,1)S(1)}, u32[]{:S(2)}, u32[]{:S(2)}) collective-permute-start(bf16[80,1792]{1,0:T(8,128)(2,1)S(1)} %get-tuple-element.48), channel_id=1, source_target_pairs={{0,2},{2,4},{4,6},{6,7},{7,5},{5,3},{3,1},{1,0},{8,10},{10,12},{12... | collective-permute-start | bytes 860168 | tf_op jit(solution)/shard_map/ppermute | solution.py:30
  20.3 16.4 %collective-permute-start.3 = (bf16[80,1792]{1,0:T(8,128)(2,1)S(1)}, bf16[80,1792]{1,0:T(8,128)(2,1)S(1)}, u32[]{:S(2)}, u32[]{:S(2)}) collective-permute-start(bf16[80,1792]{1,0:T(8,128)(2,1)S(1)} %get-tuple-element.49), channel_id=1, source_target_pairs={{0,1},{2,0},{4,2},{6,4},{7,6},{5,7},{3,5},{1,3},{8,9},{10,8},{12,1... | collective-permute-start | bytes 860168 | tf_op jit(solution)/shard_map/ppermute | solution.py:30
  29.1 14.3 %collective-permute-start.9 = (bf16[448,512]{1,0:T(8,128)(2,1)}, bf16[448,512]{1,0:T(8,128)(2,1)S(1)}, u32[]{:S(2)}, u32[]{:S(2)}) collective-permute-start(bf16[448,512]{1,0:T(8,128)(2,1)} %collective-permute-done.4.refs_0_), channel_id=1, source_target_pairs={{0,2},{2,4},{4,6},{6,7},{7,5},{5,3},{3,1},{1,0},{8,10},{10,12},{12... | collective-permute-start | bytes 1376264 | tf_op jit(solution)/shard_map/ppermute | solution.py:30
  30.7 14.0 %collective-permute-start.10 = (bf16[448,512]{1,0:T(8,128)(2,1)}, bf16[448,512]{1,0:T(8,128)(2,1)S(1)}, u32[]{:S(2)}, u32[]{:S(2)}) collective-permute-start(bf16[448,512]{1,0:T(8,128)(2,1)} %collective-permute-done.6.refs_1_), channel_id=1, source_target_pairs={{0,1},{2,0},{4,2},{6,4},{7,6},{5,7},{3,5},{1,3},{8,9},{10,8},{12,1... | collective-permute-start | bytes 1376264 | tf_op jit(solution)/shard_map/ppermute | solution.py:30
  36.7 7.9 %collective-permute-start.7 = (bf16[48,1792]{1,0:T(8,128)(2,1)S(1)}, bf16[48,1792]{1,0:T(8,128)(2,1)S(1)}, u32[]{:S(2)}, u32[]{:S(2)}) collective-permute-start(bf16[48,1792]{1,0:T(8,128)(2,1)S(1)} %get-tuple-element.54), channel_id=1, source_target_pairs={{0,16},{8,24},{16,0},{24,8},{1,17},{9,25},{17,1},{25,9},{2,18},{10... | collective-permute-start | bytes 516104 | tf_op jit(solution)/shard_map/ppermute | solution.py:360
  38.3 6.4 %collective-permute-start.8 = (bf16[48,1792]{1,0:T(8,128)(2,1)S(1)}, bf16[48,1792]{1,0:T(8,128)(2,1)S(1)}, u32[]{:S(2)}, u32[]{:S(2)}) collective-permute-start(bf16[48,1792]{1,0:T(8,128)(2,1)S(1)} %get-tuple-element.55), channel_id=1, source_target_pairs={{0,16},{8,24},{16,0},{24,8},{1,17},{9,25},{17,1},{25,9},{2,18},{10... | collective-permute-start | bytes 516104 | tf_op jit(solution)/shard_map/ppermute | solution.py:360
  44.7 6.1 %collective-permute-start.11 = (bf16[224,512]{1,0:T(8,128)(2,1)S(1)}, bf16[224,512]{1,0:T(8,128)(2,1)S(1)}, u32[]{:S(2)}, u32[]{:S(2)}) collective-permute-start(bf16[224,512]{1,0:T(8,128)(2,1)S(1)} %get-tuple-element.60), channel_id=1, source_target_pairs={{0,2},{2,4},{4,6},{6,7},{7,5},{5,3},{3,1},{1,0},{8,10},{10,12},{12... | collective-permute-start | bytes 688136 | tf_op jit(solution)/shard_map/ppermute | solution.py:30
  46.3 6.0 %collective-permute-start.12 = (bf16[224,512]{1,0:T(8,128)(2,1)S(1)}, bf16[224,512]{1,0:T(8,128)(2,1)S(1)}, u32[]{:S(2)}, u32[]{:S(2)}) collective-permute-start(bf16[224,512]{1,0:T(8,128)(2,1)S(1)} %get-tuple-element.61), channel_id=1, source_target_pairs={{0,1},{2,0},{4,2},{6,4},{7,6},{5,7},{3,5},{1,3},{8,9},{10,8},{12,1... | collective-permute-start | bytes 688136 | tf_op jit(solution)/shard_map/ppermute | solution.py:30
  46.9 7.5 %copy-start.5 = (bf16[128,1792]{1,0:T(8,128)(2,1)}, bf16[128,1792]{1,0:T(8,128)(2,1)S(1)}, u32[]{:S(2)}) copy-start(bf16[128,1792]{1,0:T(8,128)(2,1)S(1)} %get-tuple-element.81.rest_2_) | copy-start | bytes 1376260
  52.4 13.8 %collective-permute-start.14 = (bf16[128,1792]{1,0:T(8,128)(2,1)S(1)}, bf16[128,1792]{1,0:T(8,128)(2,1)S(1)}, u32[]{:S(2)}, u32[]{:S(2)}) collective-permute-start(bf16[128,1792]{1,0:T(8,128)(2,1)S(1)} %get-tuple-element.80.rest_1_), channel_id=1, source_target_pairs={{0,2},{2,4},{4,6},{6,7},{7,5},{5,3},{3,1},{1,0},{8,10},{10,12},{12... | collective-permute-start | bytes 1376264 | tf_op jit(solution)/shard_map/ppermute | solution.py:30
  54.4 11.8 %collective-permute-start.15 = (bf16[128,1792]{1,0:T(8,128)(2,1)S(1)}, bf16[128,1792]{1,0:T(8,128)(2,1)}, u32[]{:S(2)}, u32[]{:S(2)}) collective-permute-start(bf16[128,1792]{1,0:T(8,128)(2,1)S(1)} %get-tuple-element.81.rest_2_), channel_id=1, source_target_pairs={{0,1},{2,0},{4,2},{6,4},{7,6},{5,7},{3,5},{1,3},{8,9},{10,8},{12,1... | collective-permute-start | bytes 1376264 | tf_op jit(solution)/shard_map/ppermute | solution.py:30
  54.4 2.1 %copy-start.9 = (f32[4,128]{1,0:T(4,128)S(1)}, f32[4,128]{1,0:T(4,128)}, u32[]{:S(2)}) copy-start(f32[4,128]{1,0:T(4,128)} %taps_x.3) | copy-start | bytes 6148
  54.4 2.1 %copy-start.10 = (f32[4,128]{1,0:T(4,128)S(1)}, f32[4,128]{1,0:T(4,128)}, u32[]{:S(2)}) copy-start(f32[4,128]{1,0:T(4,128)} %taps_bc.3) | copy-start | bytes 6148
  54.9 2.6 %collective-permute-start.13 = (bf16[8,256]{1,0:T(8,128)(2,1)S(1)}, bf16[8,256]{1,0:T(8,128)(2,1)S(1)}, u32[]{:S(2)}, u32[]{:S(2)}) collective-permute-start(bf16[8,256]{1,0:T(8,128)(2,1)S(1)} %slice.44), channel_id=1, source_target_pairs={{0,8},{8,16},{16,24},{1,9},{9,17},{17,25},{2,10},{10,18},{18,26},{... | collective-permute-start | bytes 12296 | tf_op jit(solution)/shard_map/ppermute | solution.py:380
  66.1 0.8 copy-start.7
  66.9 13.9 %collective-permute-start.17 = (bf16[128,1792]{1,0:T(8,128)(2,1)}, bf16[128,1792]{1,0:T(8,128)(2,1)S(1)}, u32[]{:S(2)}, u32[]{:S(2)}) collective-permute-start(bf16[128,1792]{1,0:T(8,128)(2,1)} %copy-done.7), channel_id=1, source_target_pairs={{0,2},{2,4},{4,6},{6,7},{7,5},{5,3},{3,1},{1,0},{8,10},{10,12},{12... | collective-permute-start | bytes 1376264 | tf_op jit(solution)/shard_map/ppermute | solution.py:30
  69.0 13.7 %collective-permute-start.18 = (bf16[128,1792]{1,0:T(8,128)(2,1)}, bf16[128,1792]{1,0:T(8,128)(2,1)S(1)}, u32[]{:S(2)}, u32[]{:S(2)}) collective-permute-start(bf16[128,1792]{1,0:T(8,128)(2,1)} %collective-permute-done.15.rest_4_), channel_id=1, source_target_pairs={{0,1},{2,0},{4,2},{6,4},{7,6},{5,7},{3,5},{1,3},{8,9},{10,8},{12,1... | collective-permute-start | bytes 1376264 | tf_op jit(solution)/shard_map/ppermute | solution.py:30
  70.8 14.6 %all-to-all-start = ((bf16[8,64,128]{2,1,0:T(8,128)(2,1)}), bf16[8,64,128]{2,1,0:T(8,128)(2,1)S(1)}, u32[]{:S(2)}, u32[]{:S(2)}) async-start(bf16[8,64,128]{2,1,0:T(8,128)(2,1)} %bitcast.7), calls=%async_computation | async-start | bytes 262144 | tf_op jit(solution)/shard_map/all_to_all | solution.py:414
  83.4 7.4 %collective-permute-start.19 = (bf16[64,1792]{1,0:T(8,128)(2,1)}, bf16[64,1792]{1,0:T(8,128)(2,1)S(1)}, u32[]{:S(2)}, u32[]{:S(2)}) collective-permute-start(bf16[64,1792]{1,0:T(8,128)(2,1)} %get-tuple-element.85), channel_id=1, source_target_pairs={{0,2},{2,4},{4,6},{6,7},{7,5},{5,3},{3,1},{1,0},{8,10},{10,12},{12... | collective-permute-start | bytes 688136 | tf_op jit(solution)/shard_map/ppermute | solution.py:30
  84.5 6.3 %collective-permute-start.20 = (bf16[64,1792]{1,0:T(8,128)(2,1)S(1)}, bf16[64,1792]{1,0:T(8,128)(2,1)S(1)}, u32[]{:S(2)}, u32[]{:S(2)}) collective-permute-start(bf16[64,1792]{1,0:T(8,128)(2,1)S(1)} %get-tuple-element.86), channel_id=1, source_target_pairs={{0,1},{2,0},{4,2},{6,4},{7,6},{5,7},{3,5},{1,3},{8,9},{10,8},{12,1... | collective-permute-start | bytes 688136 | tf_op jit(solution)/shard_map/ppermute | solution.py:30
  85.4 1.3 %collective-permute-start.16 = (bf16[8,64,128]{2,1,0:T(8,128)(2,1)S(1)}, bf16[8,64,128]{2,1,0:T(8,128)(2,1)S(1)}, u32[]{:S(2)}, u32[]{:S(2)}) collective-permute-start(bf16[8,64,128]{2,1,0:T(8,128)(2,1)S(1)} %all-to-all-done.mine), channel_id=1, source_target_pairs={{0,8},{8,0},{16,24},{24,16},{1,9},{9,1},{17,25},{25,17},{2,10},{10... | collective-permute-start | bytes 393224 | tf_op jit(solution)/shard_map/ppermute | solution.py:416
  86.8 1.0 %copy-start.6 = (bf16[128,1792]{1,0:T(8,128)(2,1)S(1)}, bf16[128,1792]{1,0:T(8,128)(2,1)}, u32[]{:S(2)}) copy-start(bf16[128,1792]{1,0:T(8,128)(2,1)} %copy-done.5) | copy-start | bytes 1376260
  87.8 1.0 %copy-start.8 = (bf16[128,1792]{1,0:T(8,128)(2,1)S(1)}, bf16[128,1792]{1,0:T(8,128)(2,1)}, u32[]{:S(2)}) copy-start(bf16[128,1792]{1,0:T(8,128)(2,1)} %copy-done.7) | copy-start | bytes 1376260
  91.0 1.6 %collective-permute-start.21 = (bf16[64,1792]{1,0:T(8,128)(2,1)S(1)}, bf16[64,1792]{1,0:T(8,128)(2,1)S(1)}, u32[]{:S(2)}, u32[]{:S(2)}) collective-permute-start(bf16[64,1792]{1,0:T(8,128)(2,1)S(1)} %shard_map.141), channel_id=1, source_target_pairs={{0,8},{8,0},{16,24},{24,16},{1,9},{9,1},{17,25},{25,17},{2,10},{10... | collective-permute-start | bytes 688136 | tf_op jit(solution)/shard_map/ppermute | solution.py:427

commit v21 on v19

--- a/solution.py
+++ b/solution.py
@@ -206,7 +206,22 @@
     message[state_w + 2 :] = jnp.zeros((message.shape[0] - state_w - 2, width), F32)
 
 
-def finish(heads, rows, seg_first, messages, seg_ext_a, seg_row_a, skip, proj, conv_a, bc_a, cum_a, scaled_a, enter_a,
+def finish(heads, rows, count, seg_first, *refs):
+    messages, refs = refs[:count], refs[count:]
+    finish_with(heads, rows, seg_first, messages, *refs)
+
+
+def message_from(messages, device):
+    if len(messages) == 1:
+        return messages[0][device]
+    place = lax.axis_index("seq")
+    core = place % 2 == device % 2
+    plane = place // 2 == device // 2
+    own, other_core, other_plane, other_both = (m[...] for m in messages)
+    return jnp.where(plane, jnp.where(core, own, other_core), jnp.where(core, other_plane, other_both))
+
+
+def finish_with(heads, rows, seg_first, messages, seg_ext_a, seg_row_a, skip, proj, conv_a, bc_a, cum_a, scaled_a, enter_a,
            state_a, out_b, gate_b, bc_b, enter_b, gated):
     state_w = bc_a.shape[1] // 2
     width = out_b.shape[1]
@@ -214,12 +229,13 @@
     decay = jnp.zeros((1, width), F32)
     first = seg_first[...].astype(F32)
     place = lax.axis_index("seq")
-    for device in reversed(range(messages.shape[0] - 1)):
+    for device in reversed(range(lax.axis_size("seq") - 1)):
         earlier = device < place
-        passes = earlier & (messages[device, state_w + 1 : state_w + 2] == first)
+        message = message_from(messages, device)
+        passes = earlier & (message[state_w + 1 : state_w + 2] == first)
         passes = jnp.where(passes, jnp.exp(decay), 0.0)
-        entering = entering + passes * messages[device, :state_w]
-        decay = decay + jnp.where(earlier, messages[device, state_w : state_w + 1], 0.0)
+        entering = entering + passes * message[:state_w]
+        decay = decay + jnp.where(earlier, message[state_w : state_w + 1], 0.0)
     second = state_a[state_w : state_w + 1] * entering + state_a[:state_w]
     out_a = block_inner(bc_a[...], cum_a[...], scaled_a[...], seg_ext_a[HALO:], seg_row_a[...], heads)
     out_a = out_a + skip[...] * conv_a[...] + enter_a[...] * dot(bc_a[:, state_w:], entering)
@@ -365,9 +381,15 @@
         [plane] * 5 + [shape(msg_rows, width)] * 2,
         [ext, ext],
     )(proj, halo, seg_ext_a, seg_last, state_b, conv_x, conv_bc, bias, rate)
-    messages = lax.all_gather(message, "seq")
-    gated = call(functools.partial(finish, heads, rows), shape(tok_rows, width, kind=BF16))(
-        seg_first, messages, seg_ext_a, seg_row_a, skip, proj, cx_a, bc_a, cum_a, scaled_a, enter_a, state_a,
+    if n_seq == 4:
+        other_core = lax.ppermute(message, "seq", [(i, i ^ 1) for i in range(n_seq)])
+        other_plane = lax.ppermute(message, "seq", [(i, i ^ 2) for i in range(n_seq)])
+        other_both = lax.ppermute(other_core, "seq", [(i, i ^ 2) for i in range(n_seq)])
+        messages = (message, other_core, other_plane, other_both)
+    else:
+        messages = (lax.all_gather(message, "seq"),)
+    gated = call(functools.partial(finish, heads, rows, len(messages)), shape(tok_rows, width, kind=BF16))(
+        seg_first, *messages, seg_ext_a, seg_row_a, skip, proj, cx_a, bc_a, cum_a, scaled_a, enter_a, state_a,
         out_b, gate_b, bc_b, enter_b
     )
     tok_own = tok_rows // n_tensor

time: 92.1 us -> 91.8 us (level)
  blocking collectives: 6.84 us -> 0 us
  starting transfers between devices: 25.2 us -> 29.7 us
  waiting for transfers between devices: 35 us -> 37.1 us
    all_gather x1 -> x0, blocking collectives: 6.84 us -> none  [local(): messages = lax.all_gather(message, 'seq')]
    ppermute x0 -> x3, starting transfers between devices: none -> 4.48 us  [the longest x1 1.68 us: local(): lax.ppermute(message, 'seq', [(i, i ^ 1) for i in range(n_seq)])]
    ppermute x0 -> x3, waiting for transfers between devices: none -> 2.83 us  [the longest x1 1.67 us: local(): lax.ppermute(other_core, 'seq', [(i, i ^ 2) for i in range(n_seq)])]
  transfers between devices with their start and end apart: 21 -> 24, of which waited for: 14 -> 16; matrix products, arithmetic and copies ran while one was open for 4% -> 4% of each run, Pallas kernels for 18% -> 18%
where the time goes in v21:
time: 91.8 us; the launch traced here: 91.3 us
  waiting for transfers between devices  37.1 us (40%)
  starting transfers between devices  29.7 us (32%)
  Pallas kernels  17 us (19%)
  local copies, waits for them, and re-layouts  5.9 us (6%)
  matrix products  1.12 us (1%)
    ppermute x16, waiting for transfers between devices, ring_shift(): lax.ppermute(block, 'tensor', [(order[i], order[(i + step) % n]) for i in...  30.8 us
    ppermute x16, starting transfers between devices, ring_shift(): lax.ppermute(block, 'tensor', [(order[i], order[(i + step) % n]) for i in...  17.4 us
    pallas_call x4, Pallas kernels, local(): call(functools.partial(project, [distance for distance, _ in arrived], ah...  8.46 us
    all_to_all x1, starting transfers between devices, local(): mine = lax.all_to_all(blocks, 'tensor', 0, 0)  5.01 us
    unnamed x26, local copies, waits for them, and re-layouts  3.73 us
    pallas_call x1, Pallas kernels, local(): call(functools.partial(product_early, distances), shape(2 * tok_own, colu...  2.15 us
  transfers between devices with their start and end apart: 24, of which 16 were waited for; matrix products, arithmetic and copies ran while one was open for 4% of the time, Pallas kernels for 18%

profile of v21, /device:TPU:0, one launch (start us, length us, event | category | flops | bytes accessed | tf_op | source)
XLA Modules:
  0.0 91.3 jit_solution(5705744064511363758)
XLA Ops:
  0.0 3.0 %collective-permute-start = (bf16[448,512]{1,0:T(8,128)(2,1)}, bf16[448,512]{1,0:T(8,128)(2,1)}, u32[]{:S(2)}, u32[]{:S(2)}) collective-permute-start(bf16[448,512]{1,0:T(8,128)(2,1)} %bitcast.10), channel_id=1, source_target_pairs={{0,2},{2,4},{4,6},{6,7},{7,5},{5,3},{3,1},{1,0},{8,10},{10,12},{12... | collective-permute-start | bytes 1376264 | tf_op jit(solution)/shard_map/ppermute | solution.py:31
  3.0 0.8 slice.33
  3.8 1.4 %collective-permute-start.3 = (s32[8]{0:T(128)S(1)}, s32[8]{0:T(128)S(1)}, u32[]{:S(2)}, u32[]{:S(2)}) collective-permute-start(s32[8]{0:T(128)S(1)} %slice.33), channel_id=1, source_target_pairs={{0,8},{8,16},{16,24},{1,9},{9,17},{17,25},{2,10},{10,18},{18,26},{... | collective-permute-start | bytes 104 | tf_op jit(solution)/shard_map/ppermute | solution.py:327
  5.2 1.1 %convolution_bitcast_fusion.refs_3_.refs_4_ = bf16[3584,128]{1,0:T(8,128)(2,1)S(1)} fusion(bf16[2,128]{1,0:T(2,128)(2,1)} %constant.25.clone, bf16[3584,2]{0,1:T(2,128)(2,1)S(1)} %copy-done), kind=kOutput, calls=%fused_computation | convolution fusion | flops 1835008 | bytes 932352 | tf_op jit(solution)/shard_map/dot_general | solution.py:318
  6.4 1.5 %copy-done.1 = bf16[2,3584,128]{2,1,0:T(8,128)(2,1)S(1)} copy-done((bf16[2,3584,128]{2,1,0:T(8,128)(2,1)S(1)}, bf16[2,3584,128]{2,1,0:T(8,128)(2,1)}, u32[]{:S(2)}) %copy-start.1) | copy-done | bytes 1835032
  7.9 1.2 %copy-done.2 = bf16[3584,128]{1,0:T(8,128)(2,1)S(1)} copy-done((bf16[3584,128]{1,0:T(8,128)(2,1)S(1)}, bf16[3584,128]{1,0:T(8,128)(2,1)}, u32[]{:S(2)}) %copy-start.2) | copy-done | bytes 917528
  9.1 1.0 %copy-done.4 = bf16[512,448]{0,1:T(8,128)(2,1)S(1)} copy-done((bf16[512,448]{0,1:T(8,128)(2,1)S(1)}, bf16[512,448]{0,1:T(8,128)(2,1)}, u32[]{:S(2)}) %copy-start.4) | copy-done | bytes 458776
  10.1 0.6 shard_map.127.refs_5_
  10.7 3.1 %collective-permute-done.refs_0_ = bf16[448,512]{1,0:T(8,128)(2,1)} collective-permute-done((bf16[448,512]{1,0:T(8,128)(2,1)}, bf16[448,512]{1,0:T(8,128)(2,1)}, u32[]{:S(2)}, u32[]{:S(2)}) %collective-permute-start) | collective-permute-done | bytes 458784 | tf_op jit(solution)/shard_map/ppermute | solution.py:31
  13.8 1.8 %collective-permute-start.1 = (bf16[448,512]{1,0:T(8,128)(2,1)}, bf16[448,512]{1,0:T(8,128)(2,1)}, u32[]{:S(2)}, u32[]{:S(2)}) collective-permute-start(bf16[448,512]{1,0:T(8,128)(2,1)} %collective-permute-done.refs_0_), channel_id=1, source_target_pairs={{0,2},{2,4},{4,6},{6,7},{7,5},{5,3},{3,1},{1,0},{8,10},{10,12},{12... | collective-permute-start | bytes 1376264 | tf_op jit(solution)/shard_map/ppermute | solution.py:31
  15.6 0.2 collective-permute-start.5
  15.8 0.6 fusion
  16.4 0.1 slice.36
  16.5 0.1 broadcast_in_dim.27
  16.5 0.1 broadcast_in_dim_reshape.9.bias
  16.7 0.1 broadcast_in_dim_reshape.10.rate
  16.9 0.1 broadcast_in_dim_reshape.11.skip.refs_6_
  16.9 0.1 pad_add_fusion
  17.1 3.0 %shard_map.128.refs_5_ = f32[512,512]{1,0:T(8,128)S(1)} custom-call(bf16[448,512]{1,0:T(8,128)(2,1)} %collective-permute-done.refs_0_, bf16[448,512]{1,0:T(8,128)(2,1)S(1)} %collective-permute-done.2.refs_1_, bf16[2,3584,128]{2,1,0:T(8,128)(2,1)} %refs_2_.7, bf16[3584,128]{1,0:T(8,128)(2,1)S(1)} %copy-done.3, ...), custom_call_target="tpu_custom_call" | custom-call | flops 1000000000 | bytes 2097152 | tf_op jit(solution)/shard_map/pallas_call | solution.py:355
  20.0 6.0 %collective-permute-done.1.refs_0_ = bf16[448,512]{1,0:T(8,128)(2,1)} collective-permute-done((bf16[448,512]{1,0:T(8,128)(2,1)}, bf16[448,512]{1,0:T(8,128)(2,1)}, u32[]{:S(2)}, u32[]{:S(2)}) %collective-permute-start.1) | collective-permute-done | bytes 458784 | tf_op jit(solution)/shard_map/ppermute | solution.py:31
  26.0 1.6 %collective-permute-start.4 = (bf16[448,512]{1,0:T(8,128)(2,1)}, bf16[448,512]{1,0:T(8,128)(2,1)S(1)}, u32[]{:S(2)}, u32[]{:S(2)}) collective-permute-start(bf16[448,512]{1,0:T(8,128)(2,1)} %collective-permute-done.1.refs_0_), channel_id=1, source_target_pairs={{0,2},{2,4},{4,6},{6,7},{7,5},{5,3},{3,1},{1,0},{8,10},{10,12},{12... | collective-permute-start | bytes 1376264 | tf_op jit(solution)/shard_map/ppermute | solution.py:31
  27.6 0.4 collective-permute-start.6
  28.1 0.1 multiply_convert_fusion.rest_0_
  28.2 1.6 %collective-permute-start.13 = (bf16[128,1792]{1,0:T(8,128)(2,1)S(1)}, bf16[128,1792]{1,0:T(8,128)(2,1)S(1)}, u32[]{:S(2)}, u32[]{:S(2)}) collective-permute-start(bf16[128,1792]{1,0:T(8,128)(2,1)S(1)} %multiply_convert_fusion.rest_0_), channel_id=1, source_target_pairs={{0,2},{2,4},{4,6},{6,7},{7,5},{5,3},{3,1},{1,0},{8,10},{10,12},{12... | collective-permute-start | bytes 1376264 | tf_op jit(solution)/shard_map/ppermute | solution.py:31
  29.9 0.4 collective-permute-start.14
  30.3 3.0 %shard_map.129.refs_5_ = f32[512,512]{1,0:T(8,128)S(1)} custom-call(bf16[448,512]{1,0:T(8,128)(2,1)} %collective-permute-done.1.refs_0_, bf16[448,512]{1,0:T(8,128)(2,1)} %collective-permute-done.5.refs_1_, bf16[2,3584,128]{2,1,0:T(8,128)(2,1)} %refs_2_.7, bf16[3584,128]{1,0:T(8,128)(2,1)S(1)} %copy-done.3, ...), custom_call_target="tpu_custom_call" | custom-call | flops 1000000000 | bytes 2097152 | tf_op jit(solution)/shard_map/pallas_call | solution.py:355
  33.3 6.4 %collective-permute-done.4.forth.refs_0_ = bf16[448,512]{1,0:T(8,128)(2,1)S(1)} collective-permute-done((bf16[448,512]{1,0:T(8,128)(2,1)}, bf16[448,512]{1,0:T(8,128)(2,1)S(1)}, u32[]{:S(2)}, u32[]{:S(2)}) %collective-permute-start.4) | collective-permute-done | bytes 458784 | tf_op jit(solution)/shard_map/ppermute | solution.py:31
  39.7 1.6 %collective-permute-done.6.back.refs_1_ = bf16[448,512]{1,0:T(8,128)(2,1)S(1)} collective-permute-done((bf16[448,512]{1,0:T(8,128)(2,1)}, bf16[448,512]{1,0:T(8,128)(2,1)S(1)}, u32[]{:S(2)}, u32[]{:S(2)}) %collective-permute-start.6) | collective-permute-done | bytes 458784 | tf_op jit(solution)/shard_map/ppermute | solution.py:31
  41.3 1.6 %collective-permute-start.7 = (bf16[224,512]{1,0:T(8,128)(2,1)S(1)}, bf16[224,512]{1,0:T(8,128)(2,1)S(1)}, u32[]{:S(2)}, u32[]{:S(2)}) collective-permute-start(bf16[224,512]{1,0:T(8,128)(2,1)S(1)} %get-tuple-element.42), channel_id=1, source_target_pairs={{0,2},{2,4},{4,6},{6,7},{7,5},{5,3},{3,1},{1,0},{8,10},{10,12},{12... | collective-permute-start | bytes 688136 | tf_op jit(solution)/shard_map/ppermute | solution.py:31
  43.0 0.5 collective-permute-start.8
  43.4 1.9 %shard_map.131 = (f32[512,512]{1,0:T(8,128)S(1)}, bf16[448,512]{1,0:T(8,128)(2,1)S(1)}) custom-call(bf16[448,512]{1,0:T(8,128)(2,1)S(1)} %collective-permute-done.4.forth.refs_0_, bf16[448,512]{1,0:T(8,128)(2,1)S(1)} %collective-permute-done.6.back.refs_1_, bf16[2,3584,128]{2,1,0:T(8,128)(2,1)} %refs_2_.7, bf16[3584,128]{1,0:T(8,128)(2,1)S(1)} %copy-done.3, ...), custom_call_target="tpu_custom_call" | custom-call | flops 1000000000 | bytes 2097152 | tf_op jit(solution)/shard_map/pallas_call | solution.py:355
  45.3 4.2 %collective-permute-done.13.rest_1_ = bf16[128,1792]{1,0:T(8,128)(2,1)S(1)} collective-permute-done((bf16[128,1792]{1,0:T(8,128)(2,1)S(1)}, bf16[128,1792]{1,0:T(8,128)(2,1)S(1)}, u32[]{:S(2)}, u32[]{:S(2)}) %collective-permute-start.13) | collective-permute-done | bytes 458784 | tf_op jit(solution)/shard_map/ppermute | solution.py:31
  49.5 1.1 %collective-permute-done.14.rest_2_ = bf16[128,1792]{1,0:T(8,128)(2,1)S(1)} collective-permute-done((bf16[128,1792]{1,0:T(8,128)(2,1)S(1)}, bf16[128,1792]{1,0:T(8,128)(2,1)S(1)}, u32[]{:S(2)}, u32[]{:S(2)}) %collective-permute-start.14) | collective-permute-done | bytes 458784 | tf_op jit(solution)/shard_map/ppermute | solution.py:31
  50.6 1.4 %collective-permute-done.7.top = bf16[224,512]{1,0:T(8,128)(2,1)S(1)} collective-permute-done((bf16[224,512]{1,0:T(8,128)(2,1)S(1)}, bf16[224,512]{1,0:T(8,128)(2,1)S(1)}, u32[]{:S(2)}, u32[]{:S(2)}) %collective-permute-start.7) | collective-permute-done | bytes 229408 | tf_op jit(solution)/shard_map/ppermute | solution.py:31
  52.0 1.0 %collective-permute-done.8.bottom = bf16[224,512]{1,0:T(8,128)(2,1)S(1)} collective-permute-done((bf16[224,512]{1,0:T(8,128)(2,1)S(1)}, bf16[224,512]{1,0:T(8,128)(2,1)S(1)}, u32[]{:S(2)}, u32[]{:S(2)}) %collective-permute-start.8) | collective-permute-done | bytes 229408 | tf_op jit(solution)/shard_map/ppermute | solution.py:31
  53.1 1.6 %collective-permute-start.15 = (bf16[128,1792]{1,0:T(8,128)(2,1)S(1)}, bf16[128,1792]{1,0:T(8,128)(2,1)}, u32[]{:S(2)}, u32[]{:S(2)}) collective-permute-start(bf16[128,1792]{1,0:T(8,128)(2,1)S(1)} %collective-permute-done.13.rest_1_), channel_id=1, source_target_pairs={{0,2},{2,4},{4,6},{6,7},{7,5},{5,3},{3,1},{1,0},{8,10},{10,12},{12... | collective-permute-start | bytes 1376264 | tf_op jit(solution)/shard_map/ppermute | solution.py:31
  54.7 0.5 collective-permute-start.16
  55.1 0.5 shard_map.132.proj.refs_7_
  55.6 1.3 %collective-permute-start.9 = (bf16[8,256]{1,0:T(8,128)(2,1)S(1)}, bf16[8,256]{1,0:T(8,128)(2,1)S(1)}, u32[]{:S(2)}, u32[]{:S(2)}) collective-permute-start(bf16[8,256]{1,0:T(8,128)(2,1)S(1)} %slice.44), channel_id=1, source_target_pairs={{0,8},{8,16},{16,24},{1,9},{9,17},{17,25},{2,10},{10,18},{18,26},{... | collective-permute-start | bytes 12296 | tf_op jit(solution)/shard_map/ppermute | solution.py:369
  56.9 0.1 copy.17.seg_ext
  57.1 0.1 copy.18.seg_ext.refs_4_
  57.2 1.0 %shard_map.133 = (f32[256,128]{1,0:T(8,128)S(1)}, f32[256,128]{1,0:T(8,128)S(1)}, f32[256,128]{1,0:T(8,128)S(1)}, f32[72,128]{1,0:T(8,128)S(1)}, f32[256,128]{1,0:T(8,128)S(1)}) custom-call(f32[512,512]{1,0:T(8,128)S(1)} %shard_map.132.proj.refs_7_, s32[264,1]{1,0:T(8,128)S(1)} %copy.17.seg_ext, s32[1,256]{1,0:T(1,128)S(1)} %bitcast.14, ...), custom_call_target="tpu_custom_call" | custom-call | flops 10000000 | bytes 2097152 | tf_op jit(solution)/shard_map/pallas_call | solution.py:374
  58.2 1.2 %shard_map.134 = (f32[256,128]{1,0:T(8,128)S(1)}, f32[256,128]{1,0:T(8,128)S(1)}, f32[256,128]{1,0:T(8,128)S(1)}, f32[256,128]{1,0:T(8,128)S(1)}, f32[256,128]{1...) custom-call(f32[512,512]{1,0:T(8,128)S(1)} %shard_map.132.proj.refs_7_, ...), custom_call_target="tpu_custom_call" | custom-call | flops 10000000 | bytes 2097152 | tf_op jit(solution)/shard_map/pallas_call | solution.py:379
  59.5 1.7 %collective-permute-start.10 = (f32[72,128]{1,0:T(8,128)S(1)}, f32[72,128]{1,0:T(8,128)S(1)}, u32[]{:S(2)}, u32[]{:S(2)}) collective-permute-start(f32[72,128]{1,0:T(8,128)S(1)} %get-tuple-element.47.refs_0_), channel_id=1, source_target_pairs={{0,8},{8,0},{16,24},{24,16},{1,9},{9,1},{17,25},{25,17},{2,10},{10... | collective-permute-start | bytes 110600 | tf_op jit(solution)/shard_map/ppermute | solution.py:385
  61.1 1.7 %collective-permute-start.11 = (f32[72,128]{1,0:T(8,128)S(1)}, f32[72,128]{1,0:T(8,128)S(1)}, u32[]{:S(2)}, u32[]{:S(2)}) collective-permute-start(f32[72,128]{1,0:T(8,128)S(1)} %get-tuple-element.47.refs_0_), channel_id=1, source_target_pairs={{0,16},{8,24},{16,0},{24,8},{1,17},{9,25},{17,1},{25,9},{2,18},{10... | collective-permute-start | bytes 110600 | tf_op jit(solution)/shard_map/ppermute | solution.py:386
  62.8 1.1 %collective-permute-start.12 = (f32[72,128]{1,0:T(8,128)S(1)}, f32[72,128]{1,0:T(8,128)S(1)}, u32[]{:S(2)}, u32[]{:S(2)}) collective-permute-start(f32[72,128]{1,0:T(8,128)S(1)} %collective-permute-done.10.refs_1_), channel_id=1, source_target_pairs={{0,16},{8,24},{16,0},{24,8},{1,17},{9,25},{17,1},{25,9},{2,18},{10... | collective-permute-start | bytes 110600 | tf_op jit(solution)/shard_map/ppermute | solution.py:387
  63.9 1.2 %collective-permute-done.11.refs_2_ = f32[72,128]{1,0:T(8,128)S(1)} collective-permute-done((f32[72,128]{1,0:T(8,128)S(1)}, f32[72,128]{1,0:T(8,128)S(1)}, u32[]{:S(2)}, u32[]{:S(2)}) %collective-permute-start.11) | collective-permute-done | bytes 36896 | tf_op jit(solution)/shard_map/ppermute | solution.py:386
  65.1 1.7 %collective-permute-done.12.refs_3_ = f32[72,128]{1,0:T(8,128)S(1)} collective-permute-done((f32[72,128]{1,0:T(8,128)S(1)}, f32[72,128]{1,0:T(8,128)S(1)}, u32[]{:S(2)}, u32[]{:S(2)}) %collective-permute-start.12) | collective-permute-done | bytes 36896 | tf_op jit(solution)/shard_map/ppermute | solution.py:387
  66.8 1.6 %collective-permute-start.18 = (bf16[128,1792]{1,0:T(8,128)(2,1)}, bf16[128,1792]{1,0:T(8,128)(2,1)S(1)}, u32[]{:S(2)}, u32[]{:S(2)}) collective-permute-start(bf16[128,1792]{1,0:T(8,128)(2,1)} %collective-permute-done.15.rest_3_), channel_id=1, source_target_pairs={{0,2},{2,4},{4,6},{6,7},{7,5},{5,3},{3,1},{1,0},{8,10},{10,12},{12... | collective-permute-start | bytes 1376264 | tf_op jit(solution)/shard_map/ppermute | solution.py:31
  68.4 0.4 collective-permute-start.19
  68.8 1.8 %shard_map.135 = bf16[512,128]{1,0:T(8,128)(2,1)} custom-call(s32[1,1]{1,0:T(1,128)} %bitcast.seg_first, f32[72,128]{1,0:T(8,128)S(1)} %get-tuple-element.47.refs_0_, f32[72,128]{1,0:T(8,128)S(1)} %collective-permute-done.10.refs_1_, f32[72,128]{1,0:T(8,128)S(1)} %collective-permute-done.11.refs_2_, f32[72,128]{1,0:T(8,128)S(1)} %collective-permute-done.12.refs_3_, ...), custom_call_target="tpu_custom_call" | custom-call | flops 10000000 | bytes 2097152 | tf_op jit(solution)/shard_map/pallas_call | solution.py:391
  70.6 5.0 %all-to-all-start = ((bf16[8,64,128]{2,1,0:T(8,128)(2,1)}), bf16[8,64,128]{2,1,0:T(8,128)(2,1)S(1)}, u32[]{:S(2)}, u32[]{:S(2)}) async-start(bf16[8,64,128]{2,1,0:T(8,128)(2,1)} %bitcast.6), calls=%async_computation | async-start | bytes 262144 | tf_op jit(solution)/shard_map/all_to_all | solution.py:409
  75.6 3.4 %collective-permute-done.18.rest_5_.forth = bf16[128,1792]{1,0:T(8,128)(2,1)S(1)} collective-permute-done((bf16[128,1792]{1,0:T(8,128)(2,1)}, bf16[128,1792]{1,0:T(8,128)(2,1)S(1)}, u32[]{:S(2)}, u32[]{:S(2)}) %collective-permute-start.18) | collective-permute-done | bytes 458784 | tf_op jit(solution)/shard_map/ppermute | solution.py:31
  79.0 1.6 %collective-permute-done.19.rest_6_.back = bf16[128,1792]{1,0:T(8,128)(2,1)S(1)} collective-permute-done((bf16[128,1792]{1,0:T(8,128)(2,1)}, bf16[128,1792]{1,0:T(8,128)(2,1)S(1)}, u32[]{:S(2)}, u32[]{:S(2)}) %collective-permute-start.19) | collective-permute-done | bytes 458784 | tf_op jit(solution)/shard_map/ppermute | solution.py:31
  80.6 2.2 %collective-permute-start.20 = (bf16[64,1792]{1,0:T(8,128)(2,1)S(1)}, bf16[64,1792]{1,0:T(8,128)(2,1)S(1)}, u32[]{:S(2)}, u32[]{:S(2)}) collective-permute-start(bf16[64,1792]{1,0:T(8,128)(2,1)S(1)} %get-tuple-element.65), channel_id=1, source_target_pairs={{0,2},{2,4},{4,6},{6,7},{7,5},{5,3},{3,1},{1,0},{8,10},{10,12},{12... | collective-permute-start | bytes 688136 | tf_op jit(solution)/shard_map/ppermute | solution.py:31
  82.8 1.6 %all-to-all-done.mine = bf16[8,64,128]{2,1,0:T(8,128)(2,1)S(1)} async-done(((bf16[8,64,128]{2,1,0:T(8,128)(2,1)}), bf16[8,64,128]{2,1,0:T(8,128)(2,1)S(1)}, u32[]{:S(2)}, u32[]{:S(2)}) %all-to-all-start) | async-done | bytes 131104 | tf_op jit(solution)/shard_map/all_to_all | solution.py:409
  84.4 1.3 %collective-permute-done.17.other = bf16[8,64,128]{2,1,0:T(8,128)(2,1)S(1)} collective-permute-done((bf16[8,64,128]{2,1,0:T(8,128)(2,1)S(1)}, bf16[8,64,128]{2,1,0:T(8,128)(2,1)S(1)}, u32[]{:S(2)}, u32[]{:S(2)}) %collective-permute-start.17) | collective-permute-done | bytes 131104 | tf_op jit(solution)/shard_map/ppermute | solution.py:411
  85.7 2.1 %shard_map.136.total = f32[128,1792]{1,0:T(8,128)S(1)} custom-call(bf16[8,64,128]{2,1,0:T(8,128)(2,1)S(1)} %all-to-all-done.mine, bf16[8,64,128]{2,1,0:T(8,128)(2,1)S(1)} %collective-permute-done.17.other, bf16[128,1792]{1,0:T(8,128)(2,1)S(1)} %multiply_convert_fusion.rest_0_, bf16[128,1792]{1,0:T(8,128)(2,1)S(1)} %collective-permute-done.13.rest_1_, ...), custom_call_target="tpu_custom_call" | custom-call | flops 1 | bytes 1 | tf_op jit(solution)/shard_map/pallas_call | solution.py:416
  87.9 0.9 %collective-permute-done.21.bottom = bf16[64,1792]{1,0:T(8,128)(2,1)S(1)} collective-permute-done((bf16[64,1792]{1,0:T(8,128)(2,1)S(1)}, bf16[64,1792]{1,0:T(8,128)(2,1)S(1)}, u32[]{:S(2)}, u32[]{:S(2)}) %collective-permute-start.21) | collective-permute-done | bytes 229408 | tf_op jit(solution)/shard_map/ppermute | solution.py:31
  88.8 0.2 shard_map.139
  89.0 0.1 collective-permute-start.22
  89.1 1.0 %shard_map.138.whole = bf16[64,3584]{1,0:T(8,128)(2,1)} custom-call(bf16[8,64,128]{2,1,0:T(8,128)(2,1)S(1)} %all-to-all-done.mine, f32[128,1792]{1,0:T(8,128)S(1)} %shard_map.136.total, bf16[64,1792]{1,0:T(8,128)(2,1)S(1)} %collective-permute-done.20.top, bf16[64,1792]{1,0:T(8,128)(2,1)S(1)} %collective-permute-done.21.bottom), custom_call_target="tpu_custom_call" | custom-call | flops 10000000 | bytes 2097152 | tf_op jit(solution)/shard_map/pallas_call | solution.py:423
  90.1 0.5 collective-permute-done.22.arrived
  90.6 0.7 shard_map.140
  (43 shorter events, 0.3 us)
Async XLA Ops:
  0.0 5.2 %copy-start = (bf16[3584,2]{0,1:T(2,128)(2,1)S(1)}, bf16[3584,2]{0,1:T(2,128)(2,1)}, u32[]{:S(2)}) copy-start(bf16[3584,2]{0,1:T(2,128)(2,1)} %param.16) | copy-start | bytes 43012
  0.0 13.8 %collective-permute-start = (bf16[448,512]{1,0:T(8,128)(2,1)}, bf16[448,512]{1,0:T(8,128)(2,1)}, u32[]{:S(2)}, u32[]{:S(2)}) collective-permute-start(bf16[448,512]{1,0:T(8,128)(2,1)} %bitcast.10), channel_id=1, source_target_pairs={{0,2},{2,4},{4,6},{6,7},{7,5},{5,3},{3,1},{1,0},{8,10},{10,12},{12... | collective-permute-start | bytes 1376264 | tf_op jit(solution)/shard_map/ppermute | solution.py:31
  3.0 12.6 %collective-permute-start.2 = (bf16[448,512]{1,0:T(8,128)(2,1)}, bf16[448,512]{1,0:T(8,128)(2,1)S(1)}, u32[]{:S(2)}, u32[]{:S(2)}) collective-permute-start(bf16[448,512]{1,0:T(8,128)(2,1)} %bitcast.11), channel_id=1, source_target_pairs={{0,1},{2,0},{4,2},{6,4},{7,6},{5,7},{3,5},{1,3},{8,9},{10,8},{12,1... | collective-permute-start | bytes 1376264 | tf_op jit(solution)/shard_map/ppermute | solution.py:31
  3.8 13.2 %collective-permute-start.3 = (s32[8]{0:T(128)S(1)}, s32[8]{0:T(128)S(1)}, u32[]{:S(2)}, u32[]{:S(2)}) collective-permute-start(s32[8]{0:T(128)S(1)} %slice.33), channel_id=1, source_target_pairs={{0,8},{8,16},{16,24},{1,9},{9,17},{17,25},{2,10},{10,18},{18,26},{... | collective-permute-start | bytes 104 | tf_op jit(solution)/shard_map/ppermute | solution.py:327
  6.4 1.5 %copy-start.1 = (bf16[2,3584,128]{2,1,0:T(8,128)(2,1)S(1)}, bf16[2,3584,128]{2,1,0:T(8,128)(2,1)}, u32[]{:S(2)}) copy-start(bf16[2,3584,128]{2,1,0:T(8,128)(2,1)} %refs_2_.7) | copy-start | bytes 5505028
  7.9 1.2 %copy-start.2 = (bf16[3584,128]{1,0:T(8,128)(2,1)S(1)}, bf16[3584,128]{1,0:T(8,128)(2,1)}, u32[]{:S(2)}) copy-start(bf16[3584,128]{1,0:T(8,128)(2,1)} %refs_3_.5) | copy-start | bytes 2752516
  9.1 1.0 %copy-start.4 = (bf16[512,448]{0,1:T(8,128)(2,1)S(1)}, bf16[512,448]{0,1:T(8,128)(2,1)}, u32[]{:S(2)}) copy-start(bf16[512,448]{0,1:T(8,128)(2,1)} %param.13) | copy-start | bytes 1376260
  10.1 5.7 %copy-start.8 = (s32[512]{0:T(512)S(1)}, s32[512]{0:T(512)}, u32[]{:S(2)}) copy-start(s32[512]{0:T(512)} %param.24) | copy-start | bytes 6148
  10.1 6.4 %copy-start.10 = (f32[2]{0:T(128)S(1)}, f32[2]{0:T(128)}, u32[]{:S(2)}) copy-start(f32[2]{0:T(128)} %param.17) | copy-start | bytes 28
  10.1 6.6 %copy-start.11 = (f32[2]{0:T(128)S(1)}, f32[2]{0:T(128)}, u32[]{:S(2)}) copy-start(f32[2]{0:T(128)} %param.18) | copy-start | bytes 28
  10.1 6.7 %copy-start.12 = (f32[2]{0:T(128)S(1)}, f32[2]{0:T(128)}, u32[]{:S(2)}) copy-start(f32[2]{0:T(128)} %param.19) | copy-start | bytes 28
  10.1 7.0 %copy-start.3 = (bf16[3584,128]{1,0:T(8,128)(2,1)S(1)}, bf16[3584,128]{1,0:T(8,128)(2,1)}, u32[]{:S(2)}) copy-start(bf16[3584,128]{1,0:T(8,128)(2,1)} %refs_3_.5) | copy-start | bytes 2752516
  13.8 12.3 %collective-permute-start.1 = (bf16[448,512]{1,0:T(8,128)(2,1)}, bf16[448,512]{1,0:T(8,128)(2,1)}, u32[]{:S(2)}, u32[]{:S(2)}) collective-permute-start(bf16[448,512]{1,0:T(8,128)(2,1)} %collective-permute-done.refs_0_), channel_id=1, source_target_pairs={{0,2},{2,4},{4,6},{6,7},{7,5},{5,3},{3,1},{1,0},{8,10},{10,12},{12... | collective-permute-start | bytes 1376264 | tf_op jit(solution)/shard_map/ppermute | solution.py:31
  15.6 12.0 %collective-permute-start.5 = (bf16[448,512]{1,0:T(8,128)(2,1)S(1)}, bf16[448,512]{1,0:T(8,128)(2,1)}, u32[]{:S(2)}, u32[]{:S(2)}) collective-permute-start(bf16[448,512]{1,0:T(8,128)(2,1)S(1)} %collective-permute-done.2.refs_1_), channel_id=1, source_target_pairs={{0,1},{2,0},{4,2},{6,4},{7,6},{5,7},{3,5},{1,3},{8,9},{10,8},{12,1... | collective-permute-start | bytes 1376264 | tf_op jit(solution)/shard_map/ppermute | solution.py:31
  17.0 11.0 %copy-start.7 = (bf16[128,3584]{1,0:T(8,128)(2,1)S(1)}, bf16[128,3584]{1,0:T(8,128)(2,1)}, u32[]{:S(2)}) copy-start(bf16[128,3584]{1,0:T(8,128)(2,1)} %param.23) | copy-start | bytes 2752516
  17.0 11.0 %copy-start.9 = (f32[128]{0:T(128)S(1)}, f32[128]{0:T(128)}, u32[]{:S(2)}) copy-start(f32[128]{0:T(128)} %param.22) | copy-start | bytes 1540
  26.0 13.7 %collective-permute-start.4 = (bf16[448,512]{1,0:T(8,128)(2,1)}, bf16[448,512]{1,0:T(8,128)(2,1)S(1)}, u32[]{:S(2)}, u32[]{:S(2)}) collective-permute-start(bf16[448,512]{1,0:T(8,128)(2,1)} %collective-permute-done.1.refs_0_), channel_id=1, source_target_pairs={{0,2},{2,4},{4,6},{6,7},{7,5},{5,3},{3,1},{1,0},{8,10},{10,12},{12... | collective-permute-start | bytes 1376264 | tf_op jit(solution)/shard_map/ppermute | solution.py:31
  27.6 13.7 %collective-permute-start.6 = (bf16[448,512]{1,0:T(8,128)(2,1)}, bf16[448,512]{1,0:T(8,128)(2,1)S(1)}, u32[]{:S(2)}, u32[]{:S(2)}) collective-permute-start(bf16[448,512]{1,0:T(8,128)(2,1)} %collective-permute-done.5.refs_1_), channel_id=1, source_target_pairs={{0,1},{2,0},{4,2},{6,4},{7,6},{5,7},{3,5},{1,3},{8,9},{10,8},{12,1... | collective-permute-start | bytes 1376264 | tf_op jit(solution)/shard_map/ppermute | solution.py:31
  28.2 21.3 %collective-permute-start.13 = (bf16[128,1792]{1,0:T(8,128)(2,1)S(1)}, bf16[128,1792]{1,0:T(8,128)(2,1)S(1)}, u32[]{:S(2)}, u32[]{:S(2)}) collective-permute-start(bf16[128,1792]{1,0:T(8,128)(2,1)S(1)} %multiply_convert_fusion.rest_0_), channel_id=1, source_target_pairs={{0,2},{2,4},{4,6},{6,7},{7,5},{5,3},{3,1},{1,0},{8,10},{10,12},{12... | collective-permute-start | bytes 1376264 | tf_op jit(solution)/shard_map/ppermute | solution.py:31
  29.9 20.8 %collective-permute-start.14 = (bf16[128,1792]{1,0:T(8,128)(2,1)S(1)}, bf16[128,1792]{1,0:T(8,128)(2,1)S(1)}, u32[]{:S(2)}, u32[]{:S(2)}) collective-permute-start(bf16[128,1792]{1,0:T(8,128)(2,1)S(1)} %multiply_convert_fusion.rest_0_), channel_id=1, source_target_pairs={{0,1},{2,0},{4,2},{6,4},{7,6},{5,7},{3,5},{1,3},{8,9},{10,8},{12,1... | collective-permute-start | bytes 1376264 | tf_op jit(solution)/shard_map/ppermute | solution.py:31
  41.3 10.7 %collective-permute-start.7 = (bf16[224,512]{1,0:T(8,128)(2,1)S(1)}, bf16[224,512]{1,0:T(8,128)(2,1)S(1)}, u32[]{:S(2)}, u32[]{:S(2)}) collective-permute-start(bf16[224,512]{1,0:T(8,128)(2,1)S(1)} %get-tuple-element.42), channel_id=1, source_target_pairs={{0,2},{2,4},{4,6},{6,7},{7,5},{5,3},{3,1},{1,0},{8,10},{10,12},{12... | collective-permute-start | bytes 688136 | tf_op jit(solution)/shard_map/ppermute | solution.py:31
  43.0 10.1 %collective-permute-start.8 = (bf16[224,512]{1,0:T(8,128)(2,1)S(1)}, bf16[224,512]{1,0:T(8,128)(2,1)S(1)}, u32[]{:S(2)}, u32[]{:S(2)}) collective-permute-start(bf16[224,512]{1,0:T(8,128)(2,1)S(1)} %get-tuple-element.43), channel_id=1, source_target_pairs={{0,1},{2,0},{4,2},{6,4},{7,6},{5,7},{3,5},{1,3},{8,9},{10,8},{12,1... | collective-permute-start | bytes 688136 | tf_op jit(solution)/shard_map/ppermute | solution.py:31
  53.1 13.7 %collective-permute-start.15 = (bf16[128,1792]{1,0:T(8,128)(2,1)S(1)}, bf16[128,1792]{1,0:T(8,128)(2,1)}, u32[]{:S(2)}, u32[]{:S(2)}) collective-permute-start(bf16[128,1792]{1,0:T(8,128)(2,1)S(1)} %collective-permute-done.13.rest_1_), channel_id=1, source_target_pairs={{0,2},{2,4},{4,6},{6,7},{7,5},{5,3},{3,1},{1,0},{8,10},{10,12},{12... | collective-permute-start | bytes 1376264 | tf_op jit(solution)/shard_map/ppermute | solution.py:31
  54.7 12.1 %collective-permute-start.16 = (bf16[128,1792]{1,0:T(8,128)(2,1)S(1)}, bf16[128,1792]{1,0:T(8,128)(2,1)}, u32[]{:S(2)}, u32[]{:S(2)}) collective-permute-start(bf16[128,1792]{1,0:T(8,128)(2,1)S(1)} %collective-permute-done.14.rest_2_), channel_id=1, source_target_pairs={{0,1},{2,0},{4,2},{6,4},{7,6},{5,7},{3,5},{1,3},{8,9},{10,8},{12,1... | collective-permute-start | bytes 1376264 | tf_op jit(solution)/shard_map/ppermute | solution.py:31
  55.1 2.1 %copy-start.5 = (f32[4,128]{1,0:T(4,128)S(1)}, f32[4,128]{1,0:T(4,128)}, u32[]{:S(2)}) copy-start(f32[4,128]{1,0:T(4,128)} %taps_x.3) | copy-start | bytes 6148
  55.1 2.1 %copy-start.6 = (f32[4,128]{1,0:T(4,128)S(1)}, f32[4,128]{1,0:T(4,128)}, u32[]{:S(2)}) copy-start(f32[4,128]{1,0:T(4,128)} %taps_bc.3) | copy-start | bytes 6148
  55.6 2.6 %collective-permute-start.9 = (bf16[8,256]{1,0:T(8,128)(2,1)S(1)}, bf16[8,256]{1,0:T(8,128)(2,1)S(1)}, u32[]{:S(2)}, u32[]{:S(2)}) collective-permute-start(bf16[8,256]{1,0:T(8,128)(2,1)S(1)} %slice.44), channel_id=1, source_target_pairs={{0,8},{8,16},{16,24},{1,9},{9,17},{17,25},{2,10},{10,18},{18,26},{... | collective-permute-start | bytes 12296 | tf_op jit(solution)/shard_map/ppermute | solution.py:369
  59.5 3.4 %collective-permute-start.10 = (f32[72,128]{1,0:T(8,128)S(1)}, f32[72,128]{1,0:T(8,128)S(1)}, u32[]{:S(2)}, u32[]{:S(2)}) collective-permute-start(f32[72,128]{1,0:T(8,128)S(1)} %get-tuple-element.47.refs_0_), channel_id=1, source_target_pairs={{0,8},{8,0},{16,24},{24,16},{1,9},{9,1},{17,25},{25,17},{2,10},{10... | collective-permute-start | bytes 110600 | tf_op jit(solution)/shard_map/ppermute | solution.py:385
  61.1 4.0 %collective-permute-start.11 = (f32[72,128]{1,0:T(8,128)S(1)}, f32[72,128]{1,0:T(8,128)S(1)}, u32[]{:S(2)}, u32[]{:S(2)}) collective-permute-start(f32[72,128]{1,0:T(8,128)S(1)} %get-tuple-element.47.refs_0_), channel_id=1, source_target_pairs={{0,16},{8,24},{16,0},{24,8},{1,17},{9,25},{17,1},{25,9},{2,18},{10... | collective-permute-start | bytes 110600 | tf_op jit(solution)/shard_map/ppermute | solution.py:386
  62.8 4.0 %collective-permute-start.12 = (f32[72,128]{1,0:T(8,128)S(1)}, f32[72,128]{1,0:T(8,128)S(1)}, u32[]{:S(2)}, u32[]{:S(2)}) collective-permute-start(f32[72,128]{1,0:T(8,128)S(1)} %collective-permute-done.10.refs_1_), channel_id=1, source_target_pairs={{0,16},{8,24},{16,0},{24,8},{1,17},{9,25},{17,1},{25,9},{2,18},{10... | collective-permute-start | bytes 110600 | tf_op jit(solution)/shard_map/ppermute | solution.py:387
  66.8 12.2 %collective-permute-start.18 = (bf16[128,1792]{1,0:T(8,128)(2,1)}, bf16[128,1792]{1,0:T(8,128)(2,1)S(1)}, u32[]{:S(2)}, u32[]{:S(2)}) collective-permute-start(bf16[128,1792]{1,0:T(8,128)(2,1)} %collective-permute-done.15.rest_3_), channel_id=1, source_target_pairs={{0,2},{2,4},{4,6},{6,7},{7,5},{5,3},{3,1},{1,0},{8,10},{10,12},{12... | collective-permute-start | bytes 1376264 | tf_op jit(solution)/shard_map/ppermute | solution.py:31
  68.4 12.2 %collective-permute-start.19 = (bf16[128,1792]{1,0:T(8,128)(2,1)}, bf16[128,1792]{1,0:T(8,128)(2,1)S(1)}, u32[]{:S(2)}, u32[]{:S(2)}) collective-permute-start(bf16[128,1792]{1,0:T(8,128)(2,1)} %collective-permute-done.16.rest_4_), channel_id=1, source_target_pairs={{0,1},{2,0},{4,2},{6,4},{7,6},{5,7},{3,5},{1,3},{8,9},{10,8},{12,1... | collective-permute-start | bytes 1376264 | tf_op jit(solution)/shard_map/ppermute | solution.py:31
  70.6 13.8 %all-to-all-start = ((bf16[8,64,128]{2,1,0:T(8,128)(2,1)}), bf16[8,64,128]{2,1,0:T(8,128)(2,1)S(1)}, u32[]{:S(2)}, u32[]{:S(2)}) async-start(bf16[8,64,128]{2,1,0:T(8,128)(2,1)} %bitcast.6), calls=%async_computation | async-start | bytes 262144 | tf_op jit(solution)/shard_map/all_to_all | solution.py:409
  80.6 7.2 %collective-permute-start.20 = (bf16[64,1792]{1,0:T(8,128)(2,1)S(1)}, bf16[64,1792]{1,0:T(8,128)(2,1)S(1)}, u32[]{:S(2)}, u32[]{:S(2)}) collective-permute-start(bf16[64,1792]{1,0:T(8,128)(2,1)S(1)} %get-tuple-element.65), channel_id=1, source_target_pairs={{0,2},{2,4},{4,6},{6,7},{7,5},{5,3},{3,1},{1,0},{8,10},{10,12},{12... | collective-permute-start | bytes 688136 | tf_op jit(solution)/shard_map/ppermute | solution.py:31
  82.8 6.0 %collective-permute-start.21 = (bf16[64,1792]{1,0:T(8,128)(2,1)S(1)}, bf16[64,1792]{1,0:T(8,128)(2,1)S(1)}, u32[]{:S(2)}, u32[]{:S(2)}) collective-permute-start(bf16[64,1792]{1,0:T(8,128)(2,1)S(1)} %get-tuple-element.66), channel_id=1, source_target_pairs={{0,1},{2,0},{4,2},{6,4},{7,6},{5,7},{3,5},{1,3},{8,9},{10,8},{12,1... | collective-permute-start | bytes 688136 | tf_op jit(solution)/shard_map/ppermute | solution.py:31
  84.4 1.3 %collective-permute-start.17 = (bf16[8,64,128]{2,1,0:T(8,128)(2,1)S(1)}, bf16[8,64,128]{2,1,0:T(8,128)(2,1)S(1)}, u32[]{:S(2)}, u32[]{:S(2)}) collective-permute-start(bf16[8,64,128]{2,1,0:T(8,128)(2,1)S(1)} %all-to-all-done.mine), channel_id=1, source_target_pairs={{0,8},{8,0},{16,24},{24,16},{1,9},{9,1},{17,25},{25,17},{2,10},{10... | collective-permute-start | bytes 393224 | tf_op jit(solution)/shard_map/ppermute | solution.py:411
  89.0 1.6 %collective-permute-start.22 = (bf16[64,1792]{1,0:T(8,128)(2,1)S(1)}, bf16[64,1792]{1,0:T(8,128)(2,1)S(1)}, u32[]{:S(2)}, u32[]{:S(2)}) collective-permute-start(bf16[64,1792]{1,0:T(8,128)(2,1)S(1)} %shard_map.139), channel_id=1, source_target_pairs={{0,8},{8,0},{16,24},{24,16},{1,9},{9,1},{17,25},{25,17},{2,10},{10... | collective-permute-start | bytes 688136 | tf_op jit(solution)/shard_map/ppermute | solution.py:422

commit v22 on v21

--- a/solution.py
+++ b/solution.py
@@ -386,8 +386,10 @@
         other_plane = lax.ppermute(message, "seq", [(i, i ^ 2) for i in range(n_seq)])
         other_both = lax.ppermute(other_core, "seq", [(i, i ^ 2) for i in range(n_seq)])
         messages = (message, other_core, other_plane, other_both)
+        enough = other_plane
     else:
         messages = (lax.all_gather(message, "seq"),)
+        enough = messages
     gated = call(functools.partial(finish, heads, rows, len(messages)), shape(tok_rows, width, kind=BF16))(
         seg_first, *messages, seg_ext_a, seg_row_a, skip, proj, cx_a, bc_a, cum_a, scaled_a, enter_a, state_a,
         out_b, gate_b, bc_b, enter_b
@@ -395,7 +397,7 @@
     tok_own = tok_rows // n_tensor
 
     w_steps = [(w_forth, w_back)]
-    orders = [(far, projs[-1]), messages]
+    orders = [(far, projs[-1]), enough]
     for step in range(2, last + 1):
         if step - 2 < len(orders):
             w_forth, w_back = after((w_forth, w_back), orders[step - 2])

time: 91.8 us -> 93.5 us (1.019)
  starting transfers between devices: 29.7 us -> 30.7 us
    ppermute x16, waiting for transfers between devices: 30.8 us -> 24.9 us  [ring_shift(): lax.ppermute(block, 'tensor', [(order[i], order[(i + step) % n]) for i in...]
    all_to_all x1, waiting for transfers between devices: 1.58 us -> 6.1 us  [local(): mine = lax.all_to_all(blocks, 'tensor', 0, 0)]
    ppermute x1, starting transfers between devices: 1.68 us -> 0.01 us  [local(): lax.ppermute(message, 'seq', [(i, i ^ 1) for i in range(n_seq)])]
    ppermute x1, starting transfers between devices: 1.67 us -> 3.27 us  [local(): lax.ppermute(message, 'seq', [(i, i ^ 2) for i in range(n_seq)])]
    ppermute x1, waiting for transfers between devices: 0.01 us -> 1.21 us  [local(): lax.ppermute(message, 'seq', [(i, i ^ 1) for i in range(n_seq)])]
  transfers between devices with their start and end apart: 24 -> 24, of which waited for: 16 -> 14; matrix products, arithmetic and copies ran while one was open for 4% -> 4% of each run, Pallas kernels for 18% -> 17%
where the time goes in v22:
time: 93.5 us; the launch traced here: 92.9 us
  waiting for transfers between devices  37.8 us (40%)
  starting transfers between devices  30.7 us (33%)
  Pallas kernels  17 us (18%)
  local copies, waits for them, and re-layouts  5.9 us (6%)
  matrix products  1.12 us (1%)
    ppermute x16, waiting for transfers between devices, ring_shift(): lax.ppermute(block, 'tensor', [(order[i], order[(i + step) % n]) for i in...  24.9 us
    ppermute x16, starting transfers between devices, ring_shift(): lax.ppermute(block, 'tensor', [(order[i], order[(i + step) % n]) for i in...  17.4 us
    pallas_call x4, Pallas kernels, local(): call(functools.partial(project, [distance for distance, _ in arrived], ah...  8.46 us
    all_to_all x1, waiting for transfers between devices, local(): mine = lax.all_to_all(blocks, 'tensor', 0, 0)  6.1 us
    all_to_all x1, starting transfers between devices, local(): mine = lax.all_to_all(blocks, 'tensor', 0, 0)  5.01 us
    unnamed x26, local copies, waits for them, and re-layouts  3.73 us
    ppermute x1, starting transfers between devices, local(): lax.ppermute(message, 'seq', [(i, i ^ 2) for i in range(n_seq)])  3.27 us
    pallas_call x1, Pallas kernels, local(): call(functools.partial(product_early, distances), shape(2 * tok_own, colu...  2.15 us
  transfers between devices with their start and end apart: 24, of which 14 were waited for; matrix products, arithmetic and copies ran while one was open for 4% of the time, Pallas kernels for 17%

profile of v22, /device:TPU:0, one launch (start us, length us, event | category | flops | bytes accessed | tf_op | source)
XLA Modules:
  0.0 92.9 jit_solution(14815127833692731424)
XLA Ops:
  0.0 3.0 %collective-permute-start = (bf16[448,512]{1,0:T(8,128)(2,1)}, bf16[448,512]{1,0:T(8,128)(2,1)}, u32[]{:S(2)}, u32[]{:S(2)}) collective-permute-start(bf16[448,512]{1,0:T(8,128)(2,1)} %bitcast.10), channel_id=1, source_target_pairs={{0,2},{2,4},{4,6},{6,7},{7,5},{5,3},{3,1},{1,0},{8,10},{10,12},{12... | collective-permute-start | bytes 1376264 | tf_op jit(solution)/shard_map/ppermute | solution.py:31
  3.0 0.8 slice.33
  3.8 1.4 %collective-permute-start.3 = (s32[8]{0:T(128)S(1)}, s32[8]{0:T(128)S(1)}, u32[]{:S(2)}, u32[]{:S(2)}) collective-permute-start(s32[8]{0:T(128)S(1)} %slice.33), channel_id=1, source_target_pairs={{0,8},{8,16},{16,24},{1,9},{9,17},{17,25},{2,10},{10,18},{18,26},{... | collective-permute-start | bytes 104 | tf_op jit(solution)/shard_map/ppermute | solution.py:327
  5.2 1.1 %convolution_bitcast_fusion.refs_3_.refs_4_ = bf16[3584,128]{1,0:T(8,128)(2,1)S(1)} fusion(bf16[2,128]{1,0:T(2,128)(2,1)} %constant.25.clone, bf16[3584,2]{0,1:T(2,128)(2,1)S(1)} %copy-done), kind=kOutput, calls=%fused_computation | convolution fusion | flops 1835008 | bytes 932352 | tf_op jit(solution)/shard_map/dot_general | solution.py:318
  6.4 1.5 %copy-done.1 = bf16[2,3584,128]{2,1,0:T(8,128)(2,1)S(1)} copy-done((bf16[2,3584,128]{2,1,0:T(8,128)(2,1)S(1)}, bf16[2,3584,128]{2,1,0:T(8,128)(2,1)}, u32[]{:S(2)}) %copy-start.1) | copy-done | bytes 1835032
  7.9 1.2 %copy-done.2 = bf16[3584,128]{1,0:T(8,128)(2,1)S(1)} copy-done((bf16[3584,128]{1,0:T(8,128)(2,1)S(1)}, bf16[3584,128]{1,0:T(8,128)(2,1)}, u32[]{:S(2)}) %copy-start.2) | copy-done | bytes 917528
  9.1 1.0 %copy-done.4 = bf16[512,448]{0,1:T(8,128)(2,1)S(1)} copy-done((bf16[512,448]{0,1:T(8,128)(2,1)S(1)}, bf16[512,448]{0,1:T(8,128)(2,1)}, u32[]{:S(2)}) %copy-start.4) | copy-done | bytes 458776
  10.1 0.6 shard_map.127.refs_5_
  10.7 3.1 %collective-permute-done.refs_0_ = bf16[448,512]{1,0:T(8,128)(2,1)} collective-permute-done((bf16[448,512]{1,0:T(8,128)(2,1)}, bf16[448,512]{1,0:T(8,128)(2,1)}, u32[]{:S(2)}, u32[]{:S(2)}) %collective-permute-start) | collective-permute-done | bytes 458784 | tf_op jit(solution)/shard_map/ppermute | solution.py:31
  13.8 1.8 %collective-permute-start.1 = (bf16[448,512]{1,0:T(8,128)(2,1)}, bf16[448,512]{1,0:T(8,128)(2,1)}, u32[]{:S(2)}, u32[]{:S(2)}) collective-permute-start(bf16[448,512]{1,0:T(8,128)(2,1)} %collective-permute-done.refs_0_), channel_id=1, source_target_pairs={{0,2},{2,4},{4,6},{6,7},{7,5},{5,3},{3,1},{1,0},{8,10},{10,12},{12... | collective-permute-start | bytes 1376264 | tf_op jit(solution)/shard_map/ppermute | solution.py:31
  15.6 0.2 collective-permute-start.5
  15.8 0.6 fusion
  16.4 0.1 slice.36
  16.5 0.1 broadcast_in_dim.27
  16.5 0.1 broadcast_in_dim_reshape.9.bias
  16.6 0.1 broadcast_in_dim.28
  16.7 0.1 broadcast_in_dim_reshape.10.rate
  16.8 0.1 broadcast_in_dim.29
  16.9 0.1 broadcast_in_dim_reshape.11.skip.refs_6_
  16.9 0.1 pad_add_fusion
  17.1 3.0 %shard_map.128.refs_5_ = f32[512,512]{1,0:T(8,128)S(1)} custom-call(bf16[448,512]{1,0:T(8,128)(2,1)} %collective-permute-done.refs_0_, bf16[448,512]{1,0:T(8,128)(2,1)S(1)} %collective-permute-done.2.refs_1_, bf16[2,3584,128]{2,1,0:T(8,128)(2,1)} %refs_2_.7, bf16[3584,128]{1,0:T(8,128)(2,1)S(1)} %copy-done.3, ...), custom_call_target="tpu_custom_call" | custom-call | flops 1000000000 | bytes 2097152 | tf_op jit(solution)/shard_map/pallas_call | solution.py:355
  20.0 6.0 %collective-permute-done.1.refs_0_ = bf16[448,512]{1,0:T(8,128)(2,1)} collective-permute-done((bf16[448,512]{1,0:T(8,128)(2,1)}, bf16[448,512]{1,0:T(8,128)(2,1)}, u32[]{:S(2)}, u32[]{:S(2)}) %collective-permute-start.1) | collective-permute-done | bytes 458784 | tf_op jit(solution)/shard_map/ppermute | solution.py:31
  26.0 1.6 %collective-permute-start.4 = (bf16[448,512]{1,0:T(8,128)(2,1)}, bf16[448,512]{1,0:T(8,128)(2,1)S(1)}, u32[]{:S(2)}, u32[]{:S(2)}) collective-permute-start(bf16[448,512]{1,0:T(8,128)(2,1)} %collective-permute-done.1.refs_0_), channel_id=1, source_target_pairs={{0,2},{2,4},{4,6},{6,7},{7,5},{5,3},{3,1},{1,0},{8,10},{10,12},{12... | collective-permute-start | bytes 1376264 | tf_op jit(solution)/shard_map/ppermute | solution.py:31
  27.6 0.4 collective-permute-start.6
  28.1 0.1 multiply_convert_fusion.rest_0_
  28.2 1.6 %collective-permute-start.13 = (bf16[128,1792]{1,0:T(8,128)(2,1)S(1)}, bf16[128,1792]{1,0:T(8,128)(2,1)S(1)}, u32[]{:S(2)}, u32[]{:S(2)}) collective-permute-start(bf16[128,1792]{1,0:T(8,128)(2,1)S(1)} %multiply_convert_fusion.rest_0_), channel_id=1, source_target_pairs={{0,2},{2,4},{4,6},{6,7},{7,5},{5,3},{3,1},{1,0},{8,10},{10,12},{12... | collective-permute-start | bytes 1376264 | tf_op jit(solution)/shard_map/ppermute | solution.py:31
  29.9 0.4 collective-permute-start.14
  30.3 3.0 %shard_map.129.refs_5_ = f32[512,512]{1,0:T(8,128)S(1)} custom-call(bf16[448,512]{1,0:T(8,128)(2,1)} %collective-permute-done.1.refs_0_, bf16[448,512]{1,0:T(8,128)(2,1)} %collective-permute-done.5.refs_1_, bf16[2,3584,128]{2,1,0:T(8,128)(2,1)} %refs_2_.7, bf16[3584,128]{1,0:T(8,128)(2,1)S(1)} %copy-done.3, ...), custom_call_target="tpu_custom_call" | custom-call | flops 1000000000 | bytes 2097152 | tf_op jit(solution)/shard_map/pallas_call | solution.py:355
  33.3 6.4 %collective-permute-done.4.forth.refs_0_ = bf16[448,512]{1,0:T(8,128)(2,1)S(1)} collective-permute-done((bf16[448,512]{1,0:T(8,128)(2,1)}, bf16[448,512]{1,0:T(8,128)(2,1)S(1)}, u32[]{:S(2)}, u32[]{:S(2)}) %collective-permute-start.4) | collective-permute-done | bytes 458784 | tf_op jit(solution)/shard_map/ppermute | solution.py:31
  39.7 1.6 %collective-permute-done.6.back.refs_1_ = bf16[448,512]{1,0:T(8,128)(2,1)S(1)} collective-permute-done((bf16[448,512]{1,0:T(8,128)(2,1)}, bf16[448,512]{1,0:T(8,128)(2,1)S(1)}, u32[]{:S(2)}, u32[]{:S(2)}) %collective-permute-start.6) | collective-permute-done | bytes 458784 | tf_op jit(solution)/shard_map/ppermute | solution.py:31
  41.3 1.6 %collective-permute-start.7 = (bf16[224,512]{1,0:T(8,128)(2,1)S(1)}, bf16[224,512]{1,0:T(8,128)(2,1)S(1)}, u32[]{:S(2)}, u32[]{:S(2)}) collective-permute-start(bf16[224,512]{1,0:T(8,128)(2,1)S(1)} %get-tuple-element.42), channel_id=1, source_target_pairs={{0,2},{2,4},{4,6},{6,7},{7,5},{5,3},{3,1},{1,0},{8,10},{10,12},{12... | collective-permute-start | bytes 688136 | tf_op jit(solution)/shard_map/ppermute | solution.py:31
  43.0 0.5 collective-permute-start.8
  43.4 1.9 %shard_map.131 = (f32[512,512]{1,0:T(8,128)S(1)}, bf16[448,512]{1,0:T(8,128)(2,1)S(1)}) custom-call(bf16[448,512]{1,0:T(8,128)(2,1)S(1)} %collective-permute-done.4.forth.refs_0_, bf16[448,512]{1,0:T(8,128)(2,1)S(1)} %collective-permute-done.6.back.refs_1_, bf16[2,3584,128]{2,1,0:T(8,128)(2,1)} %refs_2_.7, bf16[3584,128]{1,0:T(8,128)(2,1)S(1)} %copy-done.3, ...), custom_call_target="tpu_custom_call" | custom-call | flops 1000000000 | bytes 2097152 | tf_op jit(solution)/shard_map/pallas_call | solution.py:355
  45.3 4.2 %collective-permute-done.13.rest_1_ = bf16[128,1792]{1,0:T(8,128)(2,1)S(1)} collective-permute-done((bf16[128,1792]{1,0:T(8,128)(2,1)S(1)}, bf16[128,1792]{1,0:T(8,128)(2,1)S(1)}, u32[]{:S(2)}, u32[]{:S(2)}) %collective-permute-start.13) | collective-permute-done | bytes 458784 | tf_op jit(solution)/shard_map/ppermute | solution.py:31
  49.5 1.1 %collective-permute-done.14.rest_2_ = bf16[128,1792]{1,0:T(8,128)(2,1)S(1)} collective-permute-done((bf16[128,1792]{1,0:T(8,128)(2,1)S(1)}, bf16[128,1792]{1,0:T(8,128)(2,1)S(1)}, u32[]{:S(2)}, u32[]{:S(2)}) %collective-permute-start.14) | collective-permute-done | bytes 458784 | tf_op jit(solution)/shard_map/ppermute | solution.py:31
  50.6 1.4 %collective-permute-done.7.top = bf16[224,512]{1,0:T(8,128)(2,1)S(1)} collective-permute-done((bf16[224,512]{1,0:T(8,128)(2,1)S(1)}, bf16[224,512]{1,0:T(8,128)(2,1)S(1)}, u32[]{:S(2)}, u32[]{:S(2)}) %collective-permute-start.7) | collective-permute-done | bytes 229408 | tf_op jit(solution)/shard_map/ppermute | solution.py:31
  52.0 1.0 %collective-permute-done.8.bottom = bf16[224,512]{1,0:T(8,128)(2,1)S(1)} collective-permute-done((bf16[224,512]{1,0:T(8,128)(2,1)S(1)}, bf16[224,512]{1,0:T(8,128)(2,1)S(1)}, u32[]{:S(2)}, u32[]{:S(2)}) %collective-permute-start.8) | collective-permute-done | bytes 229408 | tf_op jit(solution)/shard_map/ppermute | solution.py:31
  53.1 1.6 %collective-permute-start.15 = (bf16[128,1792]{1,0:T(8,128)(2,1)S(1)}, bf16[128,1792]{1,0:T(8,128)(2,1)}, u32[]{:S(2)}, u32[]{:S(2)}) collective-permute-start(bf16[128,1792]{1,0:T(8,128)(2,1)S(1)} %collective-permute-done.13.rest_1_), channel_id=1, source_target_pairs={{0,2},{2,4},{4,6},{6,7},{7,5},{5,3},{3,1},{1,0},{8,10},{10,12},{12... | collective-permute-start | bytes 1376264 | tf_op jit(solution)/shard_map/ppermute | solution.py:31
  54.7 0.5 collective-permute-start.16
  55.1 0.5 shard_map.132.proj.refs_7_
  55.6 1.3 %collective-permute-start.9 = (bf16[8,256]{1,0:T(8,128)(2,1)S(1)}, bf16[8,256]{1,0:T(8,128)(2,1)S(1)}, u32[]{:S(2)}, u32[]{:S(2)}) collective-permute-start(bf16[8,256]{1,0:T(8,128)(2,1)S(1)} %slice.44), channel_id=1, source_target_pairs={{0,8},{8,16},{16,24},{1,9},{9,17},{17,25},{2,10},{10,18},{18,26},{... | collective-permute-start | bytes 12296 | tf_op jit(solution)/shard_map/ppermute | solution.py:369
  56.9 0.1 copy.17.seg_ext
  57.1 0.1 copy.18.seg_ext.refs_4_
  57.2 1.0 %shard_map.133 = (f32[256,128]{1,0:T(8,128)S(1)}, f32[256,128]{1,0:T(8,128)S(1)}, f32[256,128]{1,0:T(8,128)S(1)}, f32[72,128]{1,0:T(8,128)S(1)}, f32[256,128]{1,0:T(8,128)S(1)}) custom-call(f32[512,512]{1,0:T(8,128)S(1)} %shard_map.132.proj.refs_7_, s32[264,1]{1,0:T(8,128)S(1)} %copy.17.seg_ext, s32[1,256]{1,0:T(1,128)S(1)} %bitcast.14, ...), custom_call_target="tpu_custom_call" | custom-call | flops 10000000 | bytes 2097152 | tf_op jit(solution)/shard_map/pallas_call | solution.py:374
  58.2 1.2 %shard_map.134 = (f32[256,128]{1,0:T(8,128)S(1)}, f32[256,128]{1,0:T(8,128)S(1)}, f32[256,128]{1,0:T(8,128)S(1)}, f32[256,128]{1,0:T(8,128)S(1)}, f32[256,128]{1...) custom-call(f32[512,512]{1,0:T(8,128)S(1)} %shard_map.132.proj.refs_7_, ...), custom_call_target="tpu_custom_call" | custom-call | flops 10000000 | bytes 2097152 | tf_op jit(solution)/shard_map/pallas_call | solution.py:379
  59.5 3.3 %collective-permute-start.11 = (f32[72,128]{1,0:T(8,128)S(1)}, f32[72,128]{1,0:T(8,128)S(1)}, u32[]{:S(2)}, u32[]{:S(2)}) collective-permute-start(f32[72,128]{1,0:T(8,128)S(1)} %get-tuple-element.47.refs_0_), channel_id=1, source_target_pairs={{0,16},{8,24},{16,0},{24,8},{1,17},{9,25},{17,1},{25,9},{2,18},{10... | collective-permute-start | bytes 110600 | tf_op jit(solution)/shard_map/ppermute | solution.py:386
  62.7 1.9 %collective-permute-done.11.refs_2_ = f32[72,128]{1,0:T(8,128)S(1)} collective-permute-done((f32[72,128]{1,0:T(8,128)S(1)}, f32[72,128]{1,0:T(8,128)S(1)}, u32[]{:S(2)}, u32[]{:S(2)}) %collective-permute-start.11) | collective-permute-done | bytes 36896 | tf_op jit(solution)/shard_map/ppermute | solution.py:386
  64.7 1.6 %collective-permute-start.18 = (bf16[128,1792]{1,0:T(8,128)(2,1)}, bf16[128,1792]{1,0:T(8,128)(2,1)S(1)}, u32[]{:S(2)}, u32[]{:S(2)}) collective-permute-start(bf16[128,1792]{1,0:T(8,128)(2,1)} %collective-permute-done.15.rest_3_), channel_id=1, source_target_pairs={{0,2},{2,4},{4,6},{6,7},{7,5},{5,3},{3,1},{1,0},{8,10},{10,12},{12... | collective-permute-start | bytes 1376264 | tf_op jit(solution)/shard_map/ppermute | solution.py:31
  66.3 0.4 collective-permute-start.19
  66.7 1.2 %collective-permute-done.10.refs_1_ = f32[72,128]{1,0:T(8,128)S(1)} collective-permute-done((f32[72,128]{1,0:T(8,128)S(1)}, f32[72,128]{1,0:T(8,128)S(1)}, u32[]{:S(2)}, u32[]{:S(2)}) %collective-permute-start.10) | collective-permute-done | bytes 36896 | tf_op jit(solution)/shard_map/ppermute | solution.py:385
  67.9 2.0 %collective-permute-start.12 = (f32[72,128]{1,0:T(8,128)S(1)}, f32[72,128]{1,0:T(8,128)S(1)}, u32[]{:S(2)}, u32[]{:S(2)}) collective-permute-start(f32[72,128]{1,0:T(8,128)S(1)} %collective-permute-done.10.refs_1_), channel_id=1, source_target_pairs={{0,16},{8,24},{16,0},{24,8},{1,17},{9,25},{17,1},{25,9},{2,18},{10... | collective-permute-start | bytes 110600 | tf_op jit(solution)/shard_map/ppermute | solution.py:387
  69.9 1.9 %collective-permute-done.12.refs_3_ = f32[72,128]{1,0:T(8,128)S(1)} collective-permute-done((f32[72,128]{1,0:T(8,128)S(1)}, f32[72,128]{1,0:T(8,128)S(1)}, u32[]{:S(2)}, u32[]{:S(2)}) %collective-permute-start.12) | collective-permute-done | bytes 36896 | tf_op jit(solution)/shard_map/ppermute | solution.py:387
  71.9 1.8 %shard_map.135 = bf16[512,128]{1,0:T(8,128)(2,1)} custom-call(s32[1,1]{1,0:T(1,128)} %bitcast.seg_first, f32[72,128]{1,0:T(8,128)S(1)} %get-tuple-element.47.refs_0_, f32[72,128]{1,0:T(8,128)S(1)} %collective-permute-done.10.refs_1_, f32[72,128]{1,0:T(8,128)S(1)} %collective-permute-done.11.refs_2_, f32[72,128]{1,0:T(8,128)S(1)} %collective-permute-done.12.refs_3_, ...), custom_call_target="tpu_custom_call" | custom-call | flops 10000000 | bytes 2097152 | tf_op jit(solution)/shard_map/pallas_call | solution.py:393
  73.6 5.0 %all-to-all-start = ((bf16[8,64,128]{2,1,0:T(8,128)(2,1)}), bf16[8,64,128]{2,1,0:T(8,128)(2,1)S(1)}, u32[]{:S(2)}, u32[]{:S(2)}) async-start(bf16[8,64,128]{2,1,0:T(8,128)(2,1)} %bitcast.6), calls=%async_computation | async-start | bytes 262144 | tf_op jit(solution)/shard_map/all_to_all | solution.py:411
  78.7 2.1 %collective-permute-start.20 = (bf16[64,1792]{1,0:T(8,128)(2,1)S(1)}, bf16[64,1792]{1,0:T(8,128)(2,1)S(1)}, u32[]{:S(2)}, u32[]{:S(2)}) collective-permute-start(bf16[64,1792]{1,0:T(8,128)(2,1)S(1)} %get-tuple-element.65), channel_id=1, source_target_pairs={{0,2},{2,4},{4,6},{6,7},{7,5},{5,3},{3,1},{1,0},{8,10},{10,12},{12... | collective-permute-start | bytes 688136 | tf_op jit(solution)/shard_map/ppermute | solution.py:31
  80.8 0.1 collective-permute-start.21
  80.8 6.1 %all-to-all-done.mine = bf16[8,64,128]{2,1,0:T(8,128)(2,1)S(1)} async-done(((bf16[8,64,128]{2,1,0:T(8,128)(2,1)}), bf16[8,64,128]{2,1,0:T(8,128)(2,1)S(1)}, u32[]{:S(2)}, u32[]{:S(2)}) %all-to-all-start) | async-done | bytes 131104 | tf_op jit(solution)/shard_map/all_to_all | solution.py:411
  86.9 1.3 %collective-permute-done.17.other = bf16[8,64,128]{2,1,0:T(8,128)(2,1)S(1)} collective-permute-done((bf16[8,64,128]{2,1,0:T(8,128)(2,1)S(1)}, bf16[8,64,128]{2,1,0:T(8,128)(2,1)S(1)}, u32[]{:S(2)}, u32[]{:S(2)}) %collective-permute-start.17) | collective-permute-done | bytes 131104 | tf_op jit(solution)/shard_map/ppermute | solution.py:413
  88.3 2.1 %shard_map.136.total = f32[128,1792]{1,0:T(8,128)S(1)} custom-call(bf16[8,64,128]{2,1,0:T(8,128)(2,1)S(1)} %all-to-all-done.mine, bf16[8,64,128]{2,1,0:T(8,128)(2,1)S(1)} %collective-permute-done.17.other, bf16[128,1792]{1,0:T(8,128)(2,1)S(1)} %multiply_convert_fusion.rest_0_, bf16[128,1792]{1,0:T(8,128)(2,1)S(1)} %collective-permute-done.13.rest_1_, ...), custom_call_target="tpu_custom_call" | custom-call | flops 1 | bytes 1 | tf_op jit(solution)/shard_map/pallas_call | solution.py:418
  90.5 0.2 shard_map.139
  90.7 0.2 collective-permute-start.22
  90.9 1.0 %shard_map.138.whole = bf16[64,3584]{1,0:T(8,128)(2,1)} custom-call(bf16[8,64,128]{2,1,0:T(8,128)(2,1)S(1)} %all-to-all-done.mine, f32[128,1792]{1,0:T(8,128)S(1)} %shard_map.136.total, bf16[64,1792]{1,0:T(8,128)(2,1)S(1)} %collective-permute-done.20.top, bf16[64,1792]{1,0:T(8,128)(2,1)S(1)} %collective-permute-done.21.bottom), custom_call_target="tpu_custom_call" | custom-call | flops 10000000 | bytes 2097152 | tf_op jit(solution)/shard_map/pallas_call | solution.py:425
  91.9 0.4 collective-permute-done.22.arrived
  92.2 0.7 shard_map.140
  (43 shorter events, 0.2 us)
Async XLA Ops:
  0.0 5.2 %copy-start = (bf16[3584,2]{0,1:T(2,128)(2,1)S(1)}, bf16[3584,2]{0,1:T(2,128)(2,1)}, u32[]{:S(2)}) copy-start(bf16[3584,2]{0,1:T(2,128)(2,1)} %param.16) | copy-start | bytes 43012
  0.0 13.8 %collective-permute-start = (bf16[448,512]{1,0:T(8,128)(2,1)}, bf16[448,512]{1,0:T(8,128)(2,1)}, u32[]{:S(2)}, u32[]{:S(2)}) collective-permute-start(bf16[448,512]{1,0:T(8,128)(2,1)} %bitcast.10), channel_id=1, source_target_pairs={{0,2},{2,4},{4,6},{6,7},{7,5},{5,3},{3,1},{1,0},{8,10},{10,12},{12... | collective-permute-start | bytes 1376264 | tf_op jit(solution)/shard_map/ppermute | solution.py:31
  3.0 12.6 %collective-permute-start.2 = (bf16[448,512]{1,0:T(8,128)(2,1)}, bf16[448,512]{1,0:T(8,128)(2,1)S(1)}, u32[]{:S(2)}, u32[]{:S(2)}) collective-permute-start(bf16[448,512]{1,0:T(8,128)(2,1)} %bitcast.11), channel_id=1, source_target_pairs={{0,1},{2,0},{4,2},{6,4},{7,6},{5,7},{3,5},{1,3},{8,9},{10,8},{12,1... | collective-permute-start | bytes 1376264 | tf_op jit(solution)/shard_map/ppermute | solution.py:31
  3.8 13.2 %collective-permute-start.3 = (s32[8]{0:T(128)S(1)}, s32[8]{0:T(128)S(1)}, u32[]{:S(2)}, u32[]{:S(2)}) collective-permute-start(s32[8]{0:T(128)S(1)} %slice.33), channel_id=1, source_target_pairs={{0,8},{8,16},{16,24},{1,9},{9,17},{17,25},{2,10},{10,18},{18,26},{... | collective-permute-start | bytes 104 | tf_op jit(solution)/shard_map/ppermute | solution.py:327
  6.4 1.5 %copy-start.1 = (bf16[2,3584,128]{2,1,0:T(8,128)(2,1)S(1)}, bf16[2,3584,128]{2,1,0:T(8,128)(2,1)}, u32[]{:S(2)}) copy-start(bf16[2,3584,128]{2,1,0:T(8,128)(2,1)} %refs_2_.7) | copy-start | bytes 5505028
  7.9 1.2 %copy-start.2 = (bf16[3584,128]{1,0:T(8,128)(2,1)S(1)}, bf16[3584,128]{1,0:T(8,128)(2,1)}, u32[]{:S(2)}) copy-start(bf16[3584,128]{1,0:T(8,128)(2,1)} %refs_3_.5) | copy-start | bytes 2752516
  9.1 1.0 %copy-start.4 = (bf16[512,448]{0,1:T(8,128)(2,1)S(1)}, bf16[512,448]{0,1:T(8,128)(2,1)}, u32[]{:S(2)}) copy-start(bf16[512,448]{0,1:T(8,128)(2,1)} %param.13) | copy-start | bytes 1376260
  10.1 5.7 %copy-start.8 = (s32[512]{0:T(512)S(1)}, s32[512]{0:T(512)}, u32[]{:S(2)}) copy-start(s32[512]{0:T(512)} %param.24) | copy-start | bytes 6148
  10.1 6.4 %copy-start.10 = (f32[2]{0:T(128)S(1)}, f32[2]{0:T(128)}, u32[]{:S(2)}) copy-start(f32[2]{0:T(128)} %param.17) | copy-start | bytes 28
  10.1 6.6 %copy-start.11 = (f32[2]{0:T(128)S(1)}, f32[2]{0:T(128)}, u32[]{:S(2)}) copy-start(f32[2]{0:T(128)} %param.18) | copy-start | bytes 28
  10.1 6.7 %copy-start.12 = (f32[2]{0:T(128)S(1)}, f32[2]{0:T(128)}, u32[]{:S(2)}) copy-start(f32[2]{0:T(128)} %param.19) | copy-start | bytes 28
  10.1 7.0 %copy-start.3 = (bf16[3584,128]{1,0:T(8,128)(2,1)S(1)}, bf16[3584,128]{1,0:T(8,128)(2,1)}, u32[]{:S(2)}) copy-start(bf16[3584,128]{1,0:T(8,128)(2,1)} %refs_3_.5) | copy-start | bytes 2752516
  13.8 12.3 %collective-permute-start.1 = (bf16[448,512]{1,0:T(8,128)(2,1)}, bf16[448,512]{1,0:T(8,128)(2,1)}, u32[]{:S(2)}, u32[]{:S(2)}) collective-permute-start(bf16[448,512]{1,0:T(8,128)(2,1)} %collective-permute-done.refs_0_), channel_id=1, source_target_pairs={{0,2},{2,4},{4,6},{6,7},{7,5},{5,3},{3,1},{1,0},{8,10},{10,12},{12... | collective-permute-start | bytes 1376264 | tf_op jit(solution)/shard_map/ppermute | solution.py:31
  15.6 12.0 %collective-permute-start.5 = (bf16[448,512]{1,0:T(8,128)(2,1)S(1)}, bf16[448,512]{1,0:T(8,128)(2,1)}, u32[]{:S(2)}, u32[]{:S(2)}) collective-permute-start(bf16[448,512]{1,0:T(8,128)(2,1)S(1)} %collective-permute-done.2.refs_1_), channel_id=1, source_target_pairs={{0,1},{2,0},{4,2},{6,4},{7,6},{5,7},{3,5},{1,3},{8,9},{10,8},{12,1... | collective-permute-start | bytes 1376264 | tf_op jit(solution)/shard_map/ppermute | solution.py:31
  17.0 11.0 %copy-start.7 = (bf16[128,3584]{1,0:T(8,128)(2,1)S(1)}, bf16[128,3584]{1,0:T(8,128)(2,1)}, u32[]{:S(2)}) copy-start(bf16[128,3584]{1,0:T(8,128)(2,1)} %param.23) | copy-start | bytes 2752516
  17.0 11.0 %copy-start.9 = (f32[128]{0:T(128)S(1)}, f32[128]{0:T(128)}, u32[]{:S(2)}) copy-start(f32[128]{0:T(128)} %param.22) | copy-start | bytes 1540
  26.0 13.7 %collective-permute-start.4 = (bf16[448,512]{1,0:T(8,128)(2,1)}, bf16[448,512]{1,0:T(8,128)(2,1)S(1)}, u32[]{:S(2)}, u32[]{:S(2)}) collective-permute-start(bf16[448,512]{1,0:T(8,128)(2,1)} %collective-permute-done.1.refs_0_), channel_id=1, source_target_pairs={{0,2},{2,4},{4,6},{6,7},{7,5},{5,3},{3,1},{1,0},{8,10},{10,12},{12... | collective-permute-start | bytes 1376264 | tf_op jit(solution)/shard_map/ppermute | solution.py:31
  27.6 13.7 %collective-permute-start.6 = (bf16[448,512]{1,0:T(8,128)(2,1)}, bf16[448,512]{1,0:T(8,128)(2,1)S(1)}, u32[]{:S(2)}, u32[]{:S(2)}) collective-permute-start(bf16[448,512]{1,0:T(8,128)(2,1)} %collective-permute-done.5.refs_1_), channel_id=1, source_target_pairs={{0,1},{2,0},{4,2},{6,4},{7,6},{5,7},{3,5},{1,3},{8,9},{10,8},{12,1... | collective-permute-start | bytes 1376264 | tf_op jit(solution)/shard_map/ppermute | solution.py:31
  28.2 21.3 %collective-permute-start.13 = (bf16[128,1792]{1,0:T(8,128)(2,1)S(1)}, bf16[128,1792]{1,0:T(8,128)(2,1)S(1)}, u32[]{:S(2)}, u32[]{:S(2)}) collective-permute-start(bf16[128,1792]{1,0:T(8,128)(2,1)S(1)} %multiply_convert_fusion.rest_0_), channel_id=1, source_target_pairs={{0,2},{2,4},{4,6},{6,7},{7,5},{5,3},{3,1},{1,0},{8,10},{10,12},{12... | collective-permute-start | bytes 1376264 | tf_op jit(solution)/shard_map/ppermute | solution.py:31
  29.9 20.8 %collective-permute-start.14 = (bf16[128,1792]{1,0:T(8,128)(2,1)S(1)}, bf16[128,1792]{1,0:T(8,128)(2,1)S(1)}, u32[]{:S(2)}, u32[]{:S(2)}) collective-permute-start(bf16[128,1792]{1,0:T(8,128)(2,1)S(1)} %multiply_convert_fusion.rest_0_), channel_id=1, source_target_pairs={{0,1},{2,0},{4,2},{6,4},{7,6},{5,7},{3,5},{1,3},{8,9},{10,8},{12,1... | collective-permute-start | bytes 1376264 | tf_op jit(solution)/shard_map/ppermute | solution.py:31
  41.3 10.7 %collective-permute-start.7 = (bf16[224,512]{1,0:T(8,128)(2,1)S(1)}, bf16[224,512]{1,0:T(8,128)(2,1)S(1)}, u32[]{:S(2)}, u32[]{:S(2)}) collective-permute-start(bf16[224,512]{1,0:T(8,128)(2,1)S(1)} %get-tuple-element.42), channel_id=1, source_target_pairs={{0,2},{2,4},{4,6},{6,7},{7,5},{5,3},{3,1},{1,0},{8,10},{10,12},{12... | collective-permute-start | bytes 688136 | tf_op jit(solution)/shard_map/ppermute | solution.py:31
  43.0 10.1 %collective-permute-start.8 = (bf16[224,512]{1,0:T(8,128)(2,1)S(1)}, bf16[224,512]{1,0:T(8,128)(2,1)S(1)}, u32[]{:S(2)}, u32[]{:S(2)}) collective-permute-start(bf16[224,512]{1,0:T(8,128)(2,1)S(1)} %get-tuple-element.43), channel_id=1, source_target_pairs={{0,1},{2,0},{4,2},{6,4},{7,6},{5,7},{3,5},{1,3},{8,9},{10,8},{12,1... | collective-permute-start | bytes 688136 | tf_op jit(solution)/shard_map/ppermute | solution.py:31
  53.1 11.6 %collective-permute-start.15 = (bf16[128,1792]{1,0:T(8,128)(2,1)S(1)}, bf16[128,1792]{1,0:T(8,128)(2,1)}, u32[]{:S(2)}, u32[]{:S(2)}) collective-permute-start(bf16[128,1792]{1,0:T(8,128)(2,1)S(1)} %collective-permute-done.13.rest_1_), channel_id=1, source_target_pairs={{0,2},{2,4},{4,6},{6,7},{7,5},{5,3},{3,1},{1,0},{8,10},{10,12},{12... | collective-permute-start | bytes 1376264 | tf_op jit(solution)/shard_map/ppermute | solution.py:31
  54.7 10.0 %collective-permute-start.16 = (bf16[128,1792]{1,0:T(8,128)(2,1)S(1)}, bf16[128,1792]{1,0:T(8,128)(2,1)}, u32[]{:S(2)}, u32[]{:S(2)}) collective-permute-start(bf16[128,1792]{1,0:T(8,128)(2,1)S(1)} %collective-permute-done.14.rest_2_), channel_id=1, source_target_pairs={{0,1},{2,0},{4,2},{6,4},{7,6},{5,7},{3,5},{1,3},{8,9},{10,8},{12,1... | collective-permute-start | bytes 1376264 | tf_op jit(solution)/shard_map/ppermute | solution.py:31
  55.1 2.1 %copy-start.5 = (f32[4,128]{1,0:T(4,128)S(1)}, f32[4,128]{1,0:T(4,128)}, u32[]{:S(2)}) copy-start(f32[4,128]{1,0:T(4,128)} %taps_x.3) | copy-start | bytes 6148
  55.1 2.1 %copy-start.6 = (f32[4,128]{1,0:T(4,128)S(1)}, f32[4,128]{1,0:T(4,128)}, u32[]{:S(2)}) copy-start(f32[4,128]{1,0:T(4,128)} %taps_bc.3) | copy-start | bytes 6148
  55.6 2.6 %collective-permute-start.9 = (bf16[8,256]{1,0:T(8,128)(2,1)S(1)}, bf16[8,256]{1,0:T(8,128)(2,1)S(1)}, u32[]{:S(2)}, u32[]{:S(2)}) collective-permute-start(bf16[8,256]{1,0:T(8,128)(2,1)S(1)} %slice.44), channel_id=1, source_target_pairs={{0,8},{8,16},{16,24},{1,9},{9,17},{17,25},{2,10},{10,18},{18,26},{... | collective-permute-start | bytes 12296 | tf_op jit(solution)/shard_map/ppermute | solution.py:369
  59.5 5.2 %collective-permute-start.11 = (f32[72,128]{1,0:T(8,128)S(1)}, f32[72,128]{1,0:T(8,128)S(1)}, u32[]{:S(2)}, u32[]{:S(2)}) collective-permute-start(f32[72,128]{1,0:T(8,128)S(1)} %get-tuple-element.47.refs_0_), channel_id=1, source_target_pairs={{0,16},{8,24},{16,0},{24,8},{1,17},{9,25},{17,1},{25,9},{2,18},{10... | collective-permute-start | bytes 110600 | tf_op jit(solution)/shard_map/ppermute | solution.py:386
  64.7 14.0 %collective-permute-start.18 = (bf16[128,1792]{1,0:T(8,128)(2,1)}, bf16[128,1792]{1,0:T(8,128)(2,1)S(1)}, u32[]{:S(2)}, u32[]{:S(2)}) collective-permute-start(bf16[128,1792]{1,0:T(8,128)(2,1)} %collective-permute-done.15.rest_3_), channel_id=1, source_target_pairs={{0,2},{2,4},{4,6},{6,7},{7,5},{5,3},{3,1},{1,0},{8,10},{10,12},{12... | collective-permute-start | bytes 1376264 | tf_op jit(solution)/shard_map/ppermute | solution.py:31
  66.3 12.4 %collective-permute-start.19 = (bf16[128,1792]{1,0:T(8,128)(2,1)}, bf16[128,1792]{1,0:T(8,128)(2,1)S(1)}, u32[]{:S(2)}, u32[]{:S(2)}) collective-permute-start(bf16[128,1792]{1,0:T(8,128)(2,1)} %collective-permute-done.16.rest_4_), channel_id=1, source_target_pairs={{0,1},{2,0},{4,2},{6,4},{7,6},{5,7},{3,5},{1,3},{8,9},{10,8},{12,1... | collective-permute-start | bytes 1376264 | tf_op jit(solution)/shard_map/ppermute | solution.py:31
  66.7 1.2 %collective-permute-start.10 = (f32[72,128]{1,0:T(8,128)S(1)}, f32[72,128]{1,0:T(8,128)S(1)}, u32[]{:S(2)}, u32[]{:S(2)}) collective-permute-start(f32[72,128]{1,0:T(8,128)S(1)} %get-tuple-element.47.refs_0_), channel_id=1, source_target_pairs={{0,8},{8,0},{16,24},{24,16},{1,9},{9,1},{17,25},{25,17},{2,10},{10... | collective-permute-start | bytes 110600 | tf_op jit(solution)/shard_map/ppermute | solution.py:385
  67.9 4.0 %collective-permute-start.12 = (f32[72,128]{1,0:T(8,128)S(1)}, f32[72,128]{1,0:T(8,128)S(1)}, u32[]{:S(2)}, u32[]{:S(2)}) collective-permute-start(f32[72,128]{1,0:T(8,128)S(1)} %collective-permute-done.10.refs_1_), channel_id=1, source_target_pairs={{0,16},{8,24},{16,0},{24,8},{1,17},{9,25},{17,1},{25,9},{2,18},{10... | collective-permute-start | bytes 110600 | tf_op jit(solution)/shard_map/ppermute | solution.py:387
  73.6 13.3 %all-to-all-start = ((bf16[8,64,128]{2,1,0:T(8,128)(2,1)}), bf16[8,64,128]{2,1,0:T(8,128)(2,1)S(1)}, u32[]{:S(2)}, u32[]{:S(2)}) async-start(bf16[8,64,128]{2,1,0:T(8,128)(2,1)} %bitcast.6), calls=%async_computation | async-start | bytes 262144 | tf_op jit(solution)/shard_map/all_to_all | solution.py:411
  78.7 11.7 %collective-permute-start.20 = (bf16[64,1792]{1,0:T(8,128)(2,1)S(1)}, bf16[64,1792]{1,0:T(8,128)(2,1)S(1)}, u32[]{:S(2)}, u32[]{:S(2)}) collective-permute-start(bf16[64,1792]{1,0:T(8,128)(2,1)S(1)} %get-tuple-element.65), channel_id=1, source_target_pairs={{0,2},{2,4},{4,6},{6,7},{7,5},{5,3},{3,1},{1,0},{8,10},{10,12},{12... | collective-permute-start | bytes 688136 | tf_op jit(solution)/shard_map/ppermute | solution.py:31
  80.8 9.7 %collective-permute-start.21 = (bf16[64,1792]{1,0:T(8,128)(2,1)S(1)}, bf16[64,1792]{1,0:T(8,128)(2,1)S(1)}, u32[]{:S(2)}, u32[]{:S(2)}) collective-permute-start(bf16[64,1792]{1,0:T(8,128)(2,1)S(1)} %get-tuple-element.66), channel_id=1, source_target_pairs={{0,1},{2,0},{4,2},{6,4},{7,6},{5,7},{3,5},{1,3},{8,9},{10,8},{12,1... | collective-permute-start | bytes 688136 | tf_op jit(solution)/shard_map/ppermute | solution.py:31
  86.9 1.3 %collective-permute-start.17 = (bf16[8,64,128]{2,1,0:T(8,128)(2,1)S(1)}, bf16[8,64,128]{2,1,0:T(8,128)(2,1)S(1)}, u32[]{:S(2)}, u32[]{:S(2)}) collective-permute-start(bf16[8,64,128]{2,1,0:T(8,128)(2,1)S(1)} %all-to-all-done.mine), channel_id=1, source_target_pairs={{0,8},{8,0},{16,24},{24,16},{1,9},{9,1},{17,25},{25,17},{2,10},{10... | collective-permute-start | bytes 393224 | tf_op jit(solution)/shard_map/ppermute | solution.py:413
  90.7 1.6 %collective-permute-start.22 = (bf16[64,1792]{1,0:T(8,128)(2,1)S(1)}, bf16[64,1792]{1,0:T(8,128)(2,1)S(1)}, u32[]{:S(2)}, u32[]{:S(2)}) collective-permute-start(bf16[64,1792]{1,0:T(8,128)(2,1)S(1)} %shard_map.139), channel_id=1, source_target_pairs={{0,8},{8,0},{16,24},{24,16},{1,9},{9,1},{17,25},{25,17},{2,10},{10... | collective-permute-start | bytes 688136 | tf_op jit(solution)/shard_map/ppermute | solution.py:424

commit v23 on v21

--- a/solution.py
+++ b/solution.py
@@ -211,14 +211,20 @@
     finish_with(heads, rows, seg_first, messages, *refs)
 
 
+def stack(first, second, out):
+    out[0] = first[...]
+    out[1] = second[...]
+
+
 def message_from(messages, device):
     if len(messages) == 1:
         return messages[0][device]
     place = lax.axis_index("seq")
     core = place % 2 == device % 2
     plane = place // 2 == device // 2
-    own, other_core, other_plane, other_both = (m[...] for m in messages)
-    return jnp.where(plane, jnp.where(core, own, other_core), jnp.where(core, other_plane, other_both))
+    own, other_core, other_plane = messages
+    here = jnp.where(core, own[...], other_core[...])
+    return jnp.where(plane, here, jnp.where(core, other_plane[0], other_plane[1]))
 
 
 def finish_with(heads, rows, seg_first, messages, seg_ext_a, seg_row_a, skip, proj, conv_a, bc_a, cum_a, scaled_a, enter_a,
@@ -383,9 +389,8 @@
     )(proj, halo, seg_ext_a, seg_last, state_b, conv_x, conv_bc, bias, rate)
     if n_seq == 4:
         other_core = lax.ppermute(message, "seq", [(i, i ^ 1) for i in range(n_seq)])
-        other_plane = lax.ppermute(message, "seq", [(i, i ^ 2) for i in range(n_seq)])
-        other_both = lax.ppermute(other_core, "seq", [(i, i ^ 2) for i in range(n_seq)])
-        messages = (message, other_core, other_plane, other_both)
+        chip = call(stack, shape(2, msg_rows, width))(message, other_core)
+        messages = (message, other_core, lax.ppermute(chip, "seq", [(i, i ^ 2) for i in range(n_seq)]))
     else:
         messages = (lax.all_gather(message, "seq"),)
     gated = call(functools.partial(finish, heads, rows, len(messages)), shape(tok_rows, width, kind=BF16))(

time: 91.8 us -> 92.1 us (level)
    ppermute x2 -> x1, starting transfers between devices: 2.8 us -> 1.94 us  [local(): lax.ppermute(chip, 'seq', [(i, i ^ 2) for i in range(n_seq)])]
    ppermute x2 -> x1, waiting for transfers between devices: 2.83 us -> 2.59 us  [local(): lax.ppermute(chip, 'seq', [(i, i ^ 2) for i in range(n_seq)])]
  transfers between devices with their start and end apart: 24 -> 23, of which waited for: 16 -> 16; matrix products, arithmetic and copies ran while one was open for 4% -> 4% of each run, Pallas kernels for 18% -> 18%
where the time goes in v23:
time: 92.1 us; the launch traced here: 91.5 us
  waiting for transfers between devices  38 us (41%)
  starting transfers between devices  29 us (31%)
  Pallas kernels  17 us (18%)
  local copies, waits for them, and re-layouts  5.9 us (6%)
  matrix products  1.12 us (1%)
    ppermute x16, waiting for transfers between devices, ring_shift(): lax.ppermute(block, 'tensor', [(order[i], order[(i + step) % n]) for i in...  31.6 us
    ppermute x16, starting transfers between devices, ring_shift(): lax.ppermute(block, 'tensor', [(order[i], order[(i + step) % n]) for i in...  17.5 us
    pallas_call x4, Pallas kernels, local(): call(functools.partial(project, [distance for distance, _ in arrived], ah...  8.46 us
    all_to_all x1, starting transfers between devices, local(): mine = lax.all_to_all(blocks, 'tensor', 0, 0)  5.01 us
    unnamed x26, local copies, waits for them, and re-layouts  3.73 us
    ppermute x1, waiting for transfers between devices, local(): lax.ppermute(chip, 'seq', [(i, i ^ 2) for i in range(n_seq)])  2.59 us
    pallas_call x1, Pallas kernels, local(): call(functools.partial(product_early, distances), shape(2 * tok_own, colu...  2.15 us
    ppermute x1, starting transfers between devices, local(): lax.ppermute(chip, 'seq', [(i, i ^ 2) for i in range(n_seq)])  1.94 us
  transfers between devices with their start and end apart: 23, of which 16 were waited for; matrix products, arithmetic and copies ran while one was open for 4% of the time, Pallas kernels for 18%

profile of v23, /device:TPU:0, one launch (start us, length us, event | category | flops | bytes accessed | tf_op | source)
XLA Modules:
  0.0 91.5 jit_solution(1239086365953103701)
XLA Ops:
  0.0 3.0 %collective-permute-start = (bf16[448,512]{1,0:T(8,128)(2,1)}, bf16[448,512]{1,0:T(8,128)(2,1)}, u32[]{:S(2)}, u32[]{:S(2)}) collective-permute-start(bf16[448,512]{1,0:T(8,128)(2,1)} %bitcast.10), channel_id=1, source_target_pairs={{0,2},{2,4},{4,6},{6,7},{7,5},{5,3},{3,1},{1,0},{8,10},{10,12},{12... | collective-permute-start | bytes 1376264 | tf_op jit(solution)/shard_map/ppermute | solution.py:31
  3.0 0.8 slice.33
  3.8 1.4 %collective-permute-start.3 = (s32[8]{0:T(128)S(1)}, s32[8]{0:T(128)S(1)}, u32[]{:S(2)}, u32[]{:S(2)}) collective-permute-start(s32[8]{0:T(128)S(1)} %slice.33), channel_id=1, source_target_pairs={{0,8},{8,16},{16,24},{1,9},{9,17},{17,25},{2,10},{10,18},{18,26},{... | collective-permute-start | bytes 104 | tf_op jit(solution)/shard_map/ppermute | solution.py:333
  5.2 1.1 %convolution_bitcast_fusion.refs_3_.refs_4_ = bf16[3584,128]{1,0:T(8,128)(2,1)S(1)} fusion(bf16[2,128]{1,0:T(2,128)(2,1)} %constant.25.clone, bf16[3584,2]{0,1:T(2,128)(2,1)S(1)} %copy-done), kind=kOutput, calls=%fused_computation | convolution fusion | flops 1835008 | bytes 932352 | tf_op jit(solution)/shard_map/dot_general | solution.py:324
  6.4 1.5 %copy-done.1 = bf16[2,3584,128]{2,1,0:T(8,128)(2,1)S(1)} copy-done((bf16[2,3584,128]{2,1,0:T(8,128)(2,1)S(1)}, bf16[2,3584,128]{2,1,0:T(8,128)(2,1)}, u32[]{:S(2)}) %copy-start.1) | copy-done | bytes 1835032
  7.9 1.2 %copy-done.2 = bf16[3584,128]{1,0:T(8,128)(2,1)S(1)} copy-done((bf16[3584,128]{1,0:T(8,128)(2,1)S(1)}, bf16[3584,128]{1,0:T(8,128)(2,1)}, u32[]{:S(2)}) %copy-start.2) | copy-done | bytes 917528
  9.1 1.0 %copy-done.4 = bf16[512,448]{0,1:T(8,128)(2,1)S(1)} copy-done((bf16[512,448]{0,1:T(8,128)(2,1)S(1)}, bf16[512,448]{0,1:T(8,128)(2,1)}, u32[]{:S(2)}) %copy-start.4) | copy-done | bytes 458776
  10.1 0.6 shard_map.127.refs_5_
  10.7 3.1 %collective-permute-done.refs_0_ = bf16[448,512]{1,0:T(8,128)(2,1)} collective-permute-done((bf16[448,512]{1,0:T(8,128)(2,1)}, bf16[448,512]{1,0:T(8,128)(2,1)}, u32[]{:S(2)}, u32[]{:S(2)}) %collective-permute-start) | collective-permute-done | bytes 458784 | tf_op jit(solution)/shard_map/ppermute | solution.py:31
  13.8 1.8 %collective-permute-start.1 = (bf16[448,512]{1,0:T(8,128)(2,1)}, bf16[448,512]{1,0:T(8,128)(2,1)}, u32[]{:S(2)}, u32[]{:S(2)}) collective-permute-start(bf16[448,512]{1,0:T(8,128)(2,1)} %collective-permute-done.refs_0_), channel_id=1, source_target_pairs={{0,2},{2,4},{4,6},{6,7},{7,5},{5,3},{3,1},{1,0},{8,10},{10,12},{12... | collective-permute-start | bytes 1376264 | tf_op jit(solution)/shard_map/ppermute | solution.py:31
  15.6 0.2 collective-permute-start.5
  15.8 0.6 fusion
  16.4 0.1 slice.36
  16.5 0.1 broadcast_in_dim.27
  16.5 0.1 broadcast_in_dim_reshape.9.bias
  16.6 0.1 broadcast_in_dim.28
  16.7 0.1 broadcast_in_dim_reshape.10.rate
  16.9 0.1 broadcast_in_dim_reshape.11.skip.refs_5_
  16.9 0.1 pad_add_fusion
  17.1 3.0 %shard_map.128.refs_5_ = f32[512,512]{1,0:T(8,128)S(1)} custom-call(bf16[448,512]{1,0:T(8,128)(2,1)} %collective-permute-done.refs_0_, bf16[448,512]{1,0:T(8,128)(2,1)S(1)} %collective-permute-done.2.refs_1_, bf16[2,3584,128]{2,1,0:T(8,128)(2,1)} %refs_2_.7, bf16[3584,128]{1,0:T(8,128)(2,1)S(1)} %copy-done.3, ...), custom_call_target="tpu_custom_call" | custom-call | flops 1000000000 | bytes 2097152 | tf_op jit(solution)/shard_map/pallas_call | solution.py:361
  20.0 6.0 %collective-permute-done.1.refs_0_ = bf16[448,512]{1,0:T(8,128)(2,1)} collective-permute-done((bf16[448,512]{1,0:T(8,128)(2,1)}, bf16[448,512]{1,0:T(8,128)(2,1)}, u32[]{:S(2)}, u32[]{:S(2)}) %collective-permute-start.1) | collective-permute-done | bytes 458784 | tf_op jit(solution)/shard_map/ppermute | solution.py:31
  26.0 1.6 %collective-permute-start.4 = (bf16[448,512]{1,0:T(8,128)(2,1)}, bf16[448,512]{1,0:T(8,128)(2,1)S(1)}, u32[]{:S(2)}, u32[]{:S(2)}) collective-permute-start(bf16[448,512]{1,0:T(8,128)(2,1)} %collective-permute-done.1.refs_0_), channel_id=1, source_target_pairs={{0,2},{2,4},{4,6},{6,7},{7,5},{5,3},{3,1},{1,0},{8,10},{10,12},{12... | collective-permute-start | bytes 1376264 | tf_op jit(solution)/shard_map/ppermute | solution.py:31
  27.6 0.4 collective-permute-start.6
  28.1 0.1 multiply_convert_fusion.rest_0_
  28.2 1.6 %collective-permute-start.12 = (bf16[128,1792]{1,0:T(8,128)(2,1)S(1)}, bf16[128,1792]{1,0:T(8,128)(2,1)S(1)}, u32[]{:S(2)}, u32[]{:S(2)}) collective-permute-start(bf16[128,1792]{1,0:T(8,128)(2,1)S(1)} %multiply_convert_fusion.rest_0_), channel_id=1, source_target_pairs={{0,2},{2,4},{4,6},{6,7},{7,5},{5,3},{3,1},{1,0},{8,10},{10,12},{12... | collective-permute-start | bytes 1376264 | tf_op jit(solution)/shard_map/ppermute | solution.py:31
  29.9 0.4 collective-permute-start.13
  30.3 3.0 %shard_map.129.refs_5_ = f32[512,512]{1,0:T(8,128)S(1)} custom-call(bf16[448,512]{1,0:T(8,128)(2,1)} %collective-permute-done.1.refs_0_, bf16[448,512]{1,0:T(8,128)(2,1)} %collective-permute-done.5.refs_1_, bf16[2,3584,128]{2,1,0:T(8,128)(2,1)} %refs_2_.7, bf16[3584,128]{1,0:T(8,128)(2,1)S(1)} %copy-done.3, ...), custom_call_target="tpu_custom_call" | custom-call | flops 1000000000 | bytes 2097152 | tf_op jit(solution)/shard_map/pallas_call | solution.py:361
  33.3 6.4 %collective-permute-done.4.forth.refs_0_ = bf16[448,512]{1,0:T(8,128)(2,1)S(1)} collective-permute-done((bf16[448,512]{1,0:T(8,128)(2,1)}, bf16[448,512]{1,0:T(8,128)(2,1)S(1)}, u32[]{:S(2)}, u32[]{:S(2)}) %collective-permute-start.4) | collective-permute-done | bytes 458784 | tf_op jit(solution)/shard_map/ppermute | solution.py:31
  39.7 1.6 %collective-permute-done.6.back.refs_1_ = bf16[448,512]{1,0:T(8,128)(2,1)S(1)} collective-permute-done((bf16[448,512]{1,0:T(8,128)(2,1)}, bf16[448,512]{1,0:T(8,128)(2,1)S(1)}, u32[]{:S(2)}, u32[]{:S(2)}) %collective-permute-start.6) | collective-permute-done | bytes 458784 | tf_op jit(solution)/shard_map/ppermute | solution.py:31
  41.3 1.6 %collective-permute-start.7 = (bf16[224,512]{1,0:T(8,128)(2,1)S(1)}, bf16[224,512]{1,0:T(8,128)(2,1)S(1)}, u32[]{:S(2)}, u32[]{:S(2)}) collective-permute-start(bf16[224,512]{1,0:T(8,128)(2,1)S(1)} %get-tuple-element.42), channel_id=1, source_target_pairs={{0,2},{2,4},{4,6},{6,7},{7,5},{5,3},{3,1},{1,0},{8,10},{10,12},{12... | collective-permute-start | bytes 688136 | tf_op jit(solution)/shard_map/ppermute | solution.py:31
  43.0 0.5 collective-permute-start.8
  43.4 1.9 %shard_map.131 = (f32[512,512]{1,0:T(8,128)S(1)}, bf16[448,512]{1,0:T(8,128)(2,1)S(1)}) custom-call(bf16[448,512]{1,0:T(8,128)(2,1)S(1)} %collective-permute-done.4.forth.refs_0_, bf16[448,512]{1,0:T(8,128)(2,1)S(1)} %collective-permute-done.6.back.refs_1_, bf16[2,3584,128]{2,1,0:T(8,128)(2,1)} %refs_2_.7, bf16[3584,128]{1,0:T(8,128)(2,1)S(1)} %copy-done.3, ...), custom_call_target="tpu_custom_call" | custom-call | flops 1000000000 | bytes 2097152 | tf_op jit(solution)/shard_map/pallas_call | solution.py:361
  45.3 4.2 %collective-permute-done.12.rest_1_ = bf16[128,1792]{1,0:T(8,128)(2,1)S(1)} collective-permute-done((bf16[128,1792]{1,0:T(8,128)(2,1)S(1)}, bf16[128,1792]{1,0:T(8,128)(2,1)S(1)}, u32[]{:S(2)}, u32[]{:S(2)}) %collective-permute-start.12) | collective-permute-done | bytes 458784 | tf_op jit(solution)/shard_map/ppermute | solution.py:31
  49.5 1.1 %collective-permute-done.13.rest_2_ = bf16[128,1792]{1,0:T(8,128)(2,1)S(1)} collective-permute-done((bf16[128,1792]{1,0:T(8,128)(2,1)S(1)}, bf16[128,1792]{1,0:T(8,128)(2,1)S(1)}, u32[]{:S(2)}, u32[]{:S(2)}) %collective-permute-start.13) | collective-permute-done | bytes 458784 | tf_op jit(solution)/shard_map/ppermute | solution.py:31
  50.6 1.4 %collective-permute-done.7.top = bf16[224,512]{1,0:T(8,128)(2,1)S(1)} collective-permute-done((bf16[224,512]{1,0:T(8,128)(2,1)S(1)}, bf16[224,512]{1,0:T(8,128)(2,1)S(1)}, u32[]{:S(2)}, u32[]{:S(2)}) %collective-permute-start.7) | collective-permute-done | bytes 229408 | tf_op jit(solution)/shard_map/ppermute | solution.py:31
  52.0 1.0 %collective-permute-done.8.bottom = bf16[224,512]{1,0:T(8,128)(2,1)S(1)} collective-permute-done((bf16[224,512]{1,0:T(8,128)(2,1)S(1)}, bf16[224,512]{1,0:T(8,128)(2,1)S(1)}, u32[]{:S(2)}, u32[]{:S(2)}) %collective-permute-start.8) | collective-permute-done | bytes 229408 | tf_op jit(solution)/shard_map/ppermute | solution.py:31
  53.1 1.6 %collective-permute-start.14 = (bf16[128,1792]{1,0:T(8,128)(2,1)S(1)}, bf16[128,1792]{1,0:T(8,128)(2,1)}, u32[]{:S(2)}, u32[]{:S(2)}) collective-permute-start(bf16[128,1792]{1,0:T(8,128)(2,1)S(1)} %collective-permute-done.12.rest_1_), channel_id=1, source_target_pairs={{0,2},{2,4},{4,6},{6,7},{7,5},{5,3},{3,1},{1,0},{8,10},{10,12},{12... | collective-permute-start | bytes 1376264 | tf_op jit(solution)/shard_map/ppermute | solution.py:31
  54.7 0.5 collective-permute-start.15
  55.1 0.5 shard_map.132.proj.refs_6_
  55.6 1.3 %collective-permute-start.9 = (bf16[8,256]{1,0:T(8,128)(2,1)S(1)}, bf16[8,256]{1,0:T(8,128)(2,1)S(1)}, u32[]{:S(2)}, u32[]{:S(2)}) collective-permute-start(bf16[8,256]{1,0:T(8,128)(2,1)S(1)} %slice.44), channel_id=1, source_target_pairs={{0,8},{8,16},{16,24},{1,9},{9,17},{17,25},{2,10},{10,18},{18,26},{... | collective-permute-start | bytes 12296 | tf_op jit(solution)/shard_map/ppermute | solution.py:375
  56.9 0.1 copy.17.seg_ext
  57.1 0.1 copy.18.seg_ext.refs_3_
  57.2 1.0 %shard_map.133 = (f32[256,128]{1,0:T(8,128)S(1)}, f32[256,128]{1,0:T(8,128)S(1)}, f32[256,128]{1,0:T(8,128)S(1)}, f32[72,128]{1,0:T(8,128)S(1)}, f32[256,128]{1,0:T(8,128)S(1)}) custom-call(f32[512,512]{1,0:T(8,128)S(1)} %shard_map.132.proj.refs_6_, s32[264,1]{1,0:T(8,128)S(1)} %copy.17.seg_ext, s32[1,256]{1,0:T(1,128)S(1)} %bitcast.14, ...), custom_call_target="tpu_custom_call" | custom-call | flops 10000000 | bytes 2097152 | tf_op jit(solution)/shard_map/pallas_call | solution.py:380
  58.2 1.2 %shard_map.134 = (f32[256,128]{1,0:T(8,128)S(1)}, f32[256,128]{1,0:T(8,128)S(1)}, f32[256,128]{1,0:T(8,128)S(1)}, f32[256,128]{1,0:T(8,128)S(1)}, f32[256,128]{1...) custom-call(f32[512,512]{1,0:T(8,128)S(1)} %shard_map.132.proj.refs_6_, ...), custom_call_target="tpu_custom_call" | custom-call | flops 10000000 | bytes 2097152 | tf_op jit(solution)/shard_map/pallas_call | solution.py:385
  59.5 1.7 %collective-permute-start.10 = (f32[72,128]{1,0:T(8,128)S(1)}, f32[72,128]{1,0:T(8,128)S(1)}, u32[]{:S(2)}, u32[]{:S(2)}) collective-permute-start(f32[72,128]{1,0:T(8,128)S(1)} %get-tuple-element.47.first.refs_0_), channel_id=1, source_target_pairs={{0,8},{8,0},{16,24},{24,16},{1,9},{9,1},{17,25},{25,17},{2,10},{10... | collective-permute-start | bytes 110600 | tf_op jit(solution)/shard_map/ppermute | solution.py:391
  61.1 0.9 collective-permute-done.10.second.refs_1_
  62.0 1.9 %collective-permute-start.11 = (f32[2,72,128]{2,1,0:T(8,128)S(1)}, f32[2,72,128]{2,1,0:T(8,128)S(1)}, u32[]{:S(2)}, u32[]{:S(2)}) collective-permute-start(f32[2,72,128]{2,1,0:T(8,128)S(1)} %shard_map.135), channel_id=1, source_target_pairs={{0,16},{8,24},{16,0},{24,8},{1,17},{9,25},{17,1},{25,9},{2,18},{10... | collective-permute-start | bytes 221192 | tf_op jit(solution)/shard_map/ppermute | solution.py:393
  63.9 2.6 %collective-permute-done.11.refs_2_ = f32[2,72,128]{2,1,0:T(8,128)S(1)} collective-permute-done((f32[2,72,128]{2,1,0:T(8,128)S(1)}, f32[2,72,128]{2,1,0:T(8,128)S(1)}, u32[]{:S(2)}, u32[]{:S(2)}) %collective-permute-start.11) | collective-permute-done | bytes 73760 | tf_op jit(solution)/shard_map/ppermute | solution.py:393
  66.5 1.6 %collective-permute-start.17 = (bf16[128,1792]{1,0:T(8,128)(2,1)}, bf16[128,1792]{1,0:T(8,128)(2,1)S(1)}, u32[]{:S(2)}, u32[]{:S(2)}) collective-permute-start(bf16[128,1792]{1,0:T(8,128)(2,1)} %collective-permute-done.14.rest_3_), channel_id=1, source_target_pairs={{0,2},{2,4},{4,6},{6,7},{7,5},{5,3},{3,1},{1,0},{8,10},{10,12},{12... | collective-permute-start | bytes 1376264 | tf_op jit(solution)/shard_map/ppermute | solution.py:31
  68.1 0.4 collective-permute-start.18
  68.6 1.8 %shard_map.136 = bf16[512,128]{1,0:T(8,128)(2,1)} custom-call(s32[1,1]{1,0:T(1,128)} %bitcast.seg_first, f32[72,128]{1,0:T(8,128)S(1)} %get-tuple-element.47.first.refs_0_, f32[72,128]{1,0:T(8,128)S(1)} %collective-permute-done.10.second.refs_1_, f32[2,72,128]{2,1,0:T(8,128)S(1)} %collective-permute-done.11.refs_2_, s32[264,1]{1,0:T(8,128)S(1)} %copy.18.seg_ext.refs_3_, ...), custom_call_target="tpu_custom_call" | custom-call | flops 10000000 | bytes 2097152 | tf_op jit(solution)/shard_map/pallas_call | solution.py:396
  70.3 5.0 %all-to-all-start = ((bf16[8,64,128]{2,1,0:T(8,128)(2,1)}), bf16[8,64,128]{2,1,0:T(8,128)(2,1)S(1)}, u32[]{:S(2)}, u32[]{:S(2)}) async-start(bf16[8,64,128]{2,1,0:T(8,128)(2,1)} %bitcast.6), calls=%async_computation | async-start | bytes 262144 | tf_op jit(solution)/shard_map/all_to_all | solution.py:414
  75.3 3.9 %collective-permute-done.17.rest_5_.forth = bf16[128,1792]{1,0:T(8,128)(2,1)S(1)} collective-permute-done((bf16[128,1792]{1,0:T(8,128)(2,1)}, bf16[128,1792]{1,0:T(8,128)(2,1)S(1)}, u32[]{:S(2)}, u32[]{:S(2)}) %collective-permute-start.17) | collective-permute-done | bytes 458784 | tf_op jit(solution)/shard_map/ppermute | solution.py:31
  79.3 1.5 %collective-permute-done.18.rest_6_.back = bf16[128,1792]{1,0:T(8,128)(2,1)S(1)} collective-permute-done((bf16[128,1792]{1,0:T(8,128)(2,1)}, bf16[128,1792]{1,0:T(8,128)(2,1)S(1)}, u32[]{:S(2)}, u32[]{:S(2)}) %collective-permute-start.18) | collective-permute-done | bytes 458784 | tf_op jit(solution)/shard_map/ppermute | solution.py:31
  80.8 2.3 %collective-permute-start.19 = (bf16[64,1792]{1,0:T(8,128)(2,1)S(1)}, bf16[64,1792]{1,0:T(8,128)(2,1)S(1)}, u32[]{:S(2)}, u32[]{:S(2)}) collective-permute-start(bf16[64,1792]{1,0:T(8,128)(2,1)S(1)} %get-tuple-element.65), channel_id=1, source_target_pairs={{0,2},{2,4},{4,6},{6,7},{7,5},{5,3},{3,1},{1,0},{8,10},{10,12},{12... | collective-permute-start | bytes 688136 | tf_op jit(solution)/shard_map/ppermute | solution.py:31
  83.0 1.1 %all-to-all-done.mine = bf16[8,64,128]{2,1,0:T(8,128)(2,1)S(1)} async-done(((bf16[8,64,128]{2,1,0:T(8,128)(2,1)}), bf16[8,64,128]{2,1,0:T(8,128)(2,1)S(1)}, u32[]{:S(2)}, u32[]{:S(2)}) %all-to-all-start) | async-done | bytes 131104 | tf_op jit(solution)/shard_map/all_to_all | solution.py:414
  84.1 1.3 %collective-permute-done.16.other = bf16[8,64,128]{2,1,0:T(8,128)(2,1)S(1)} collective-permute-done((bf16[8,64,128]{2,1,0:T(8,128)(2,1)S(1)}, bf16[8,64,128]{2,1,0:T(8,128)(2,1)S(1)}, u32[]{:S(2)}, u32[]{:S(2)}) %collective-permute-start.16) | collective-permute-done | bytes 131104 | tf_op jit(solution)/shard_map/ppermute | solution.py:416
  85.5 2.1 %shard_map.137.total = f32[128,1792]{1,0:T(8,128)S(1)} custom-call(bf16[8,64,128]{2,1,0:T(8,128)(2,1)S(1)} %all-to-all-done.mine, bf16[8,64,128]{2,1,0:T(8,128)(2,1)S(1)} %collective-permute-done.16.other, bf16[128,1792]{1,0:T(8,128)(2,1)S(1)} %multiply_convert_fusion.rest_0_, bf16[128,1792]{1,0:T(8,128)(2,1)S(1)} %collective-permute-done.12.rest_1_, ...), custom_call_target="tpu_custom_call" | custom-call | flops 1 | bytes 1 | tf_op jit(solution)/shard_map/pallas_call | solution.py:421
  87.6 1.4 %collective-permute-done.20.bottom = bf16[64,1792]{1,0:T(8,128)(2,1)S(1)} collective-permute-done((bf16[64,1792]{1,0:T(8,128)(2,1)S(1)}, bf16[64,1792]{1,0:T(8,128)(2,1)S(1)}, u32[]{:S(2)}, u32[]{:S(2)}) %collective-permute-start.20) | collective-permute-done | bytes 229408 | tf_op jit(solution)/shard_map/ppermute | solution.py:31
  89.0 0.2 shard_map.140
  89.3 0.1 collective-permute-start.21
  89.3 1.0 %shard_map.139.whole = bf16[64,3584]{1,0:T(8,128)(2,1)} custom-call(bf16[8,64,128]{2,1,0:T(8,128)(2,1)S(1)} %all-to-all-done.mine, f32[128,1792]{1,0:T(8,128)S(1)} %shard_map.137.total, bf16[64,1792]{1,0:T(8,128)(2,1)S(1)} %collective-permute-done.19.top, bf16[64,1792]{1,0:T(8,128)(2,1)S(1)} %collective-permute-done.20.bottom), custom_call_target="tpu_custom_call" | custom-call | flops 10000000 | bytes 2097152 | tf_op jit(solution)/shard_map/pallas_call | solution.py:428
  90.3 0.5 collective-permute-done.21.arrived
  90.8 0.7 shard_map.141
  (42 shorter events, 0.2 us)
Async XLA Ops:
  0.0 5.2 %copy-start = (bf16[3584,2]{0,1:T(2,128)(2,1)S(1)}, bf16[3584,2]{0,1:T(2,128)(2,1)}, u32[]{:S(2)}) copy-start(bf16[3584,2]{0,1:T(2,128)(2,1)} %param.16) | copy-start | bytes 43012
  0.0 13.8 %collective-permute-start = (bf16[448,512]{1,0:T(8,128)(2,1)}, bf16[448,512]{1,0:T(8,128)(2,1)}, u32[]{:S(2)}, u32[]{:S(2)}) collective-permute-start(bf16[448,512]{1,0:T(8,128)(2,1)} %bitcast.10), channel_id=1, source_target_pairs={{0,2},{2,4},{4,6},{6,7},{7,5},{5,3},{3,1},{1,0},{8,10},{10,12},{12... | collective-permute-start | bytes 1376264 | tf_op jit(solution)/shard_map/ppermute | solution.py:31
  3.0 12.6 %collective-permute-start.2 = (bf16[448,512]{1,0:T(8,128)(2,1)}, bf16[448,512]{1,0:T(8,128)(2,1)S(1)}, u32[]{:S(2)}, u32[]{:S(2)}) collective-permute-start(bf16[448,512]{1,0:T(8,128)(2,1)} %bitcast.11), channel_id=1, source_target_pairs={{0,1},{2,0},{4,2},{6,4},{7,6},{5,7},{3,5},{1,3},{8,9},{10,8},{12,1... | collective-permute-start | bytes 1376264 | tf_op jit(solution)/shard_map/ppermute | solution.py:31
  3.8 13.2 %collective-permute-start.3 = (s32[8]{0:T(128)S(1)}, s32[8]{0:T(128)S(1)}, u32[]{:S(2)}, u32[]{:S(2)}) collective-permute-start(s32[8]{0:T(128)S(1)} %slice.33), channel_id=1, source_target_pairs={{0,8},{8,16},{16,24},{1,9},{9,17},{17,25},{2,10},{10,18},{18,26},{... | collective-permute-start | bytes 104 | tf_op jit(solution)/shard_map/ppermute | solution.py:333
  6.4 1.5 %copy-start.1 = (bf16[2,3584,128]{2,1,0:T(8,128)(2,1)S(1)}, bf16[2,3584,128]{2,1,0:T(8,128)(2,1)}, u32[]{:S(2)}) copy-start(bf16[2,3584,128]{2,1,0:T(8,128)(2,1)} %refs_2_.7) | copy-start | bytes 5505028
  7.9 1.2 %copy-start.2 = (bf16[3584,128]{1,0:T(8,128)(2,1)S(1)}, bf16[3584,128]{1,0:T(8,128)(2,1)}, u32[]{:S(2)}) copy-start(bf16[3584,128]{1,0:T(8,128)(2,1)} %refs_3_.5) | copy-start | bytes 2752516
  9.1 1.0 %copy-start.4 = (bf16[512,448]{0,1:T(8,128)(2,1)S(1)}, bf16[512,448]{0,1:T(8,128)(2,1)}, u32[]{:S(2)}) copy-start(bf16[512,448]{0,1:T(8,128)(2,1)} %param.13) | copy-start | bytes 1376260
  10.1 5.7 %copy-start.8 = (s32[512]{0:T(512)S(1)}, s32[512]{0:T(512)}, u32[]{:S(2)}) copy-start(s32[512]{0:T(512)} %param.24) | copy-start | bytes 6148
  10.1 6.4 %copy-start.10 = (f32[2]{0:T(128)S(1)}, f32[2]{0:T(128)}, u32[]{:S(2)}) copy-start(f32[2]{0:T(128)} %param.17) | copy-start | bytes 28
  10.1 6.6 %copy-start.11 = (f32[2]{0:T(128)S(1)}, f32[2]{0:T(128)}, u32[]{:S(2)}) copy-start(f32[2]{0:T(128)} %param.18) | copy-start | bytes 28
  10.1 6.7 %copy-start.12 = (f32[2]{0:T(128)S(1)}, f32[2]{0:T(128)}, u32[]{:S(2)}) copy-start(f32[2]{0:T(128)} %param.19) | copy-start | bytes 28
  10.1 7.0 %copy-start.3 = (bf16[3584,128]{1,0:T(8,128)(2,1)S(1)}, bf16[3584,128]{1,0:T(8,128)(2,1)}, u32[]{:S(2)}) copy-start(bf16[3584,128]{1,0:T(8,128)(2,1)} %refs_3_.5) | copy-start | bytes 2752516
  13.8 12.3 %collective-permute-start.1 = (bf16[448,512]{1,0:T(8,128)(2,1)}, bf16[448,512]{1,0:T(8,128)(2,1)}, u32[]{:S(2)}, u32[]{:S(2)}) collective-permute-start(bf16[448,512]{1,0:T(8,128)(2,1)} %collective-permute-done.refs_0_), channel_id=1, source_target_pairs={{0,2},{2,4},{4,6},{6,7},{7,5},{5,3},{3,1},{1,0},{8,10},{10,12},{12... | collective-permute-start | bytes 1376264 | tf_op jit(solution)/shard_map/ppermute | solution.py:31
  15.6 12.0 %collective-permute-start.5 = (bf16[448,512]{1,0:T(8,128)(2,1)S(1)}, bf16[448,512]{1,0:T(8,128)(2,1)}, u32[]{:S(2)}, u32[]{:S(2)}) collective-permute-start(bf16[448,512]{1,0:T(8,128)(2,1)S(1)} %collective-permute-done.2.refs_1_), channel_id=1, source_target_pairs={{0,1},{2,0},{4,2},{6,4},{7,6},{5,7},{3,5},{1,3},{8,9},{10,8},{12,1... | collective-permute-start | bytes 1376264 | tf_op jit(solution)/shard_map/ppermute | solution.py:31
  17.0 11.0 %copy-start.7 = (bf16[128,3584]{1,0:T(8,128)(2,1)S(1)}, bf16[128,3584]{1,0:T(8,128)(2,1)}, u32[]{:S(2)}) copy-start(bf16[128,3584]{1,0:T(8,128)(2,1)} %param.23) | copy-start | bytes 2752516
  17.0 11.0 %copy-start.9 = (f32[128]{0:T(128)S(1)}, f32[128]{0:T(128)}, u32[]{:S(2)}) copy-start(f32[128]{0:T(128)} %param.22) | copy-start | bytes 1540
  26.0 13.7 %collective-permute-start.4 = (bf16[448,512]{1,0:T(8,128)(2,1)}, bf16[448,512]{1,0:T(8,128)(2,1)S(1)}, u32[]{:S(2)}, u32[]{:S(2)}) collective-permute-start(bf16[448,512]{1,0:T(8,128)(2,1)} %collective-permute-done.1.refs_0_), channel_id=1, source_target_pairs={{0,2},{2,4},{4,6},{6,7},{7,5},{5,3},{3,1},{1,0},{8,10},{10,12},{12... | collective-permute-start | bytes 1376264 | tf_op jit(solution)/shard_map/ppermute | solution.py:31
  27.6 13.7 %collective-permute-start.6 = (bf16[448,512]{1,0:T(8,128)(2,1)}, bf16[448,512]{1,0:T(8,128)(2,1)S(1)}, u32[]{:S(2)}, u32[]{:S(2)}) collective-permute-start(bf16[448,512]{1,0:T(8,128)(2,1)} %collective-permute-done.5.refs_1_), channel_id=1, source_target_pairs={{0,1},{2,0},{4,2},{6,4},{7,6},{5,7},{3,5},{1,3},{8,9},{10,8},{12,1... | collective-permute-start | bytes 1376264 | tf_op jit(solution)/shard_map/ppermute | solution.py:31
  28.2 21.3 %collective-permute-start.12 = (bf16[128,1792]{1,0:T(8,128)(2,1)S(1)}, bf16[128,1792]{1,0:T(8,128)(2,1)S(1)}, u32[]{:S(2)}, u32[]{:S(2)}) collective-permute-start(bf16[128,1792]{1,0:T(8,128)(2,1)S(1)} %multiply_convert_fusion.rest_0_), channel_id=1, source_target_pairs={{0,2},{2,4},{4,6},{6,7},{7,5},{5,3},{3,1},{1,0},{8,10},{10,12},{12... | collective-permute-start | bytes 1376264 | tf_op jit(solution)/shard_map/ppermute | solution.py:31
  29.9 20.8 %collective-permute-start.13 = (bf16[128,1792]{1,0:T(8,128)(2,1)S(1)}, bf16[128,1792]{1,0:T(8,128)(2,1)S(1)}, u32[]{:S(2)}, u32[]{:S(2)}) collective-permute-start(bf16[128,1792]{1,0:T(8,128)(2,1)S(1)} %multiply_convert_fusion.rest_0_), channel_id=1, source_target_pairs={{0,1},{2,0},{4,2},{6,4},{7,6},{5,7},{3,5},{1,3},{8,9},{10,8},{12,1... | collective-permute-start | bytes 1376264 | tf_op jit(solution)/shard_map/ppermute | solution.py:31
  41.3 10.7 %collective-permute-start.7 = (bf16[224,512]{1,0:T(8,128)(2,1)S(1)}, bf16[224,512]{1,0:T(8,128)(2,1)S(1)}, u32[]{:S(2)}, u32[]{:S(2)}) collective-permute-start(bf16[224,512]{1,0:T(8,128)(2,1)S(1)} %get-tuple-element.42), channel_id=1, source_target_pairs={{0,2},{2,4},{4,6},{6,7},{7,5},{5,3},{3,1},{1,0},{8,10},{10,12},{12... | collective-permute-start | bytes 688136 | tf_op jit(solution)/shard_map/ppermute | solution.py:31
  43.0 10.1 %collective-permute-start.8 = (bf16[224,512]{1,0:T(8,128)(2,1)S(1)}, bf16[224,512]{1,0:T(8,128)(2,1)S(1)}, u32[]{:S(2)}, u32[]{:S(2)}) collective-permute-start(bf16[224,512]{1,0:T(8,128)(2,1)S(1)} %get-tuple-element.43), channel_id=1, source_target_pairs={{0,1},{2,0},{4,2},{6,4},{7,6},{5,7},{3,5},{1,3},{8,9},{10,8},{12,1... | collective-permute-start | bytes 688136 | tf_op jit(solution)/shard_map/ppermute | solution.py:31
  53.1 13.4 %collective-permute-start.14 = (bf16[128,1792]{1,0:T(8,128)(2,1)S(1)}, bf16[128,1792]{1,0:T(8,128)(2,1)}, u32[]{:S(2)}, u32[]{:S(2)}) collective-permute-start(bf16[128,1792]{1,0:T(8,128)(2,1)S(1)} %collective-permute-done.12.rest_1_), channel_id=1, source_target_pairs={{0,2},{2,4},{4,6},{6,7},{7,5},{5,3},{3,1},{1,0},{8,10},{10,12},{12... | collective-permute-start | bytes 1376264 | tf_op jit(solution)/shard_map/ppermute | solution.py:31
  54.7 11.9 %collective-permute-start.15 = (bf16[128,1792]{1,0:T(8,128)(2,1)S(1)}, bf16[128,1792]{1,0:T(8,128)(2,1)}, u32[]{:S(2)}, u32[]{:S(2)}) collective-permute-start(bf16[128,1792]{1,0:T(8,128)(2,1)S(1)} %collective-permute-done.13.rest_2_), channel_id=1, source_target_pairs={{0,1},{2,0},{4,2},{6,4},{7,6},{5,7},{3,5},{1,3},{8,9},{10,8},{12,1... | collective-permute-start | bytes 1376264 | tf_op jit(solution)/shard_map/ppermute | solution.py:31
  55.1 2.1 %copy-start.5 = (f32[4,128]{1,0:T(4,128)S(1)}, f32[4,128]{1,0:T(4,128)}, u32[]{:S(2)}) copy-start(f32[4,128]{1,0:T(4,128)} %taps_x.3) | copy-start | bytes 6148
  55.1 2.1 %copy-start.6 = (f32[4,128]{1,0:T(4,128)S(1)}, f32[4,128]{1,0:T(4,128)}, u32[]{:S(2)}) copy-start(f32[4,128]{1,0:T(4,128)} %taps_bc.3) | copy-start | bytes 6148
  55.6 2.6 %collective-permute-start.9 = (bf16[8,256]{1,0:T(8,128)(2,1)S(1)}, bf16[8,256]{1,0:T(8,128)(2,1)S(1)}, u32[]{:S(2)}, u32[]{:S(2)}) collective-permute-start(bf16[8,256]{1,0:T(8,128)(2,1)S(1)} %slice.44), channel_id=1, source_target_pairs={{0,8},{8,16},{16,24},{1,9},{9,17},{17,25},{2,10},{10,18},{18,26},{... | collective-permute-start | bytes 12296 | tf_op jit(solution)/shard_map/ppermute | solution.py:375
  59.5 2.5 %collective-permute-start.10 = (f32[72,128]{1,0:T(8,128)S(1)}, f32[72,128]{1,0:T(8,128)S(1)}, u32[]{:S(2)}, u32[]{:S(2)}) collective-permute-start(f32[72,128]{1,0:T(8,128)S(1)} %get-tuple-element.47.first.refs_0_), channel_id=1, source_target_pairs={{0,8},{8,0},{16,24},{24,16},{1,9},{9,1},{17,25},{25,17},{2,10},{10... | collective-permute-start | bytes 110600 | tf_op jit(solution)/shard_map/ppermute | solution.py:391
  62.0 4.5 %collective-permute-start.11 = (f32[2,72,128]{2,1,0:T(8,128)S(1)}, f32[2,72,128]{2,1,0:T(8,128)S(1)}, u32[]{:S(2)}, u32[]{:S(2)}) collective-permute-start(f32[2,72,128]{2,1,0:T(8,128)S(1)} %shard_map.135), channel_id=1, source_target_pairs={{0,16},{8,24},{16,0},{24,8},{1,17},{9,25},{17,1},{25,9},{2,18},{10... | collective-permute-start | bytes 221192 | tf_op jit(solution)/shard_map/ppermute | solution.py:393
  66.5 12.7 %collective-permute-start.17 = (bf16[128,1792]{1,0:T(8,128)(2,1)}, bf16[128,1792]{1,0:T(8,128)(2,1)S(1)}, u32[]{:S(2)}, u32[]{:S(2)}) collective-permute-start(bf16[128,1792]{1,0:T(8,128)(2,1)} %collective-permute-done.14.rest_3_), channel_id=1, source_target_pairs={{0,2},{2,4},{4,6},{6,7},{7,5},{5,3},{3,1},{1,0},{8,10},{10,12},{12... | collective-permute-start | bytes 1376264 | tf_op jit(solution)/shard_map/ppermute | solution.py:31
  68.1 12.6 %collective-permute-start.18 = (bf16[128,1792]{1,0:T(8,128)(2,1)}, bf16[128,1792]{1,0:T(8,128)(2,1)S(1)}, u32[]{:S(2)}, u32[]{:S(2)}) collective-permute-start(bf16[128,1792]{1,0:T(8,128)(2,1)} %collective-permute-done.15.rest_4_), channel_id=1, source_target_pairs={{0,1},{2,0},{4,2},{6,4},{7,6},{5,7},{3,5},{1,3},{8,9},{10,8},{12,1... | collective-permute-start | bytes 1376264 | tf_op jit(solution)/shard_map/ppermute | solution.py:31
  70.3 13.8 %all-to-all-start = ((bf16[8,64,128]{2,1,0:T(8,128)(2,1)}), bf16[8,64,128]{2,1,0:T(8,128)(2,1)S(1)}, u32[]{:S(2)}, u32[]{:S(2)}) async-start(bf16[8,64,128]{2,1,0:T(8,128)(2,1)} %bitcast.6), calls=%async_computation | async-start | bytes 262144 | tf_op jit(solution)/shard_map/all_to_all | solution.py:414
  80.8 6.9 %collective-permute-start.19 = (bf16[64,1792]{1,0:T(8,128)(2,1)S(1)}, bf16[64,1792]{1,0:T(8,128)(2,1)S(1)}, u32[]{:S(2)}, u32[]{:S(2)}) collective-permute-start(bf16[64,1792]{1,0:T(8,128)(2,1)S(1)} %get-tuple-element.65), channel_id=1, source_target_pairs={{0,2},{2,4},{4,6},{6,7},{7,5},{5,3},{3,1},{1,0},{8,10},{10,12},{12... | collective-permute-start | bytes 688136 | tf_op jit(solution)/shard_map/ppermute | solution.py:31
  83.0 6.0 %collective-permute-start.20 = (bf16[64,1792]{1,0:T(8,128)(2,1)S(1)}, bf16[64,1792]{1,0:T(8,128)(2,1)S(1)}, u32[]{:S(2)}, u32[]{:S(2)}) collective-permute-start(bf16[64,1792]{1,0:T(8,128)(2,1)S(1)} %get-tuple-element.66), channel_id=1, source_target_pairs={{0,1},{2,0},{4,2},{6,4},{7,6},{5,7},{3,5},{1,3},{8,9},{10,8},{12,1... | collective-permute-start | bytes 688136 | tf_op jit(solution)/shard_map/ppermute | solution.py:31
  84.1 1.3 %collective-permute-start.16 = (bf16[8,64,128]{2,1,0:T(8,128)(2,1)S(1)}, bf16[8,64,128]{2,1,0:T(8,128)(2,1)S(1)}, u32[]{:S(2)}, u32[]{:S(2)}) collective-permute-start(bf16[8,64,128]{2,1,0:T(8,128)(2,1)S(1)} %all-to-all-done.mine), channel_id=1, source_target_pairs={{0,8},{8,0},{16,24},{24,16},{1,9},{9,1},{17,25},{25,17},{2,10},{10... | collective-permute-start | bytes 393224 | tf_op jit(solution)/shard_map/ppermute | solution.py:416
  89.3 1.6 %collective-permute-start.21 = (bf16[64,1792]{1,0:T(8,128)(2,1)S(1)}, bf16[64,1792]{1,0:T(8,128)(2,1)S(1)}, u32[]{:S(2)}, u32[]{:S(2)}) collective-permute-start(bf16[64,1792]{1,0:T(8,128)(2,1)S(1)} %shard_map.140), channel_id=1, source_target_pairs={{0,8},{8,0},{16,24},{24,16},{1,9},{9,1},{17,25},{25,17},{2,10},{10... | collective-permute-start | bytes 688136 | tf_op jit(solution)/shard_map/ppermute | solution.py:427

commit v24 on v21

--- a/solution.py
+++ b/solution.py
@@ -288,7 +288,7 @@
     copy.wait()
 
 
-def call(body, outs, scratch=(), vmem=48, flops=10**7, moved=1 << 21, **kw):
+def call(body, outs, scratch=(), vmem=40, flops=10**7, moved=1 << 21, **kw):
     return pl.pallas_call(
         body,
         out_shape=outs,

time: 91.8 us -> 92.3 us (level)
  local copies, waits for them, and re-layouts: 5.9 us -> 10.3 us
  starting transfers between devices: 29.7 us -> 27.1 us
  Pallas kernels: 17 us -> 15 us
    unnamed x26 -> x38, local copies, waits for them, and re-layouts: 3.73 us -> 8.15 us
    pallas_call x4, Pallas kernels: 8.46 us -> 6.4 us  [local(): call(functools.partial(project, [distance for distance, _ in arrived], ah...]
    ppermute x1, starting transfers between devices: 1.68 us -> 0.07 us  [local(): lax.ppermute(message, 'seq', [(i, i ^ 1) for i in range(n_seq)])]
    ppermute x16, waiting for transfers between devices: 30.8 us -> 32 us  [ring_shift(): lax.ppermute(block, 'tensor', [(order[i], order[(i + step) % n]) for i in...]
  transfers between devices with their start and end apart: 24 -> 24, of which waited for: 16 -> 17; matrix products, arithmetic and copies ran while one was open for 4% -> 4% of each run, Pallas kernels for 18% -> 15%
where the time goes in v24:
time: 92.3 us; the launch traced here: 91.7 us
  waiting for transfers between devices  37.7 us (41%)
  starting transfers between devices  27.1 us (29%)
  Pallas kernels  15 us (16%)
  local copies, waits for them, and re-layouts  10.3 us (11%)
  matrix products  1.12 us (1%)
    ppermute x16, waiting for transfers between devices, ring_shift(): lax.ppermute(block, 'tensor', [(order[i], order[(i + step) % n]) for i in...  32 us
    ppermute x16, starting transfers between devices, ring_shift(): lax.ppermute(block, 'tensor', [(order[i], order[(i + step) % n]) for i in...  17.4 us
    unnamed x38, local copies, waits for them, and re-layouts  8.15 us
    pallas_call x4, Pallas kernels, local(): call(functools.partial(project, [distance for distance, _ in arrived], ah...  6.4 us
    all_to_all x1, starting transfers between devices, local(): mine = lax.all_to_all(blocks, 'tensor', 0, 0)  4.33 us
    pallas_call x1, Pallas kernels, local(): call(functools.partial(product_early, distances), shape(2 * tok_own, colu...  2.28 us
  transfers between devices with their start and end apart: 24, of which 17 were waited for; matrix products, arithmetic and copies ran while one was open for 4% of the time, Pallas kernels for 15%

profile of v24, /device:TPU:0, one launch (start us, length us, event | category | flops | bytes accessed | tf_op | source)
XLA Modules:
  0.0 91.7 jit_solution(16909544204827870524)
XLA Ops:
  0.0 3.0 %collective-permute-start = (bf16[448,512]{1,0:T(8,128)(2,1)}, bf16[448,512]{1,0:T(8,128)(2,1)}, u32[]{:S(2)}, u32[]{:S(2)}) collective-permute-start(bf16[448,512]{1,0:T(8,128)(2,1)} %bitcast.10), channel_id=1, source_target_pairs={{0,2},{2,4},{4,6},{6,7},{7,5},{5,3},{3,1},{1,0},{8,10},{10,12},{12... | collective-permute-start | bytes 1376264 | tf_op jit(solution)/shard_map/ppermute | solution.py:31
  3.0 0.8 slice.33
  3.8 1.4 %collective-permute-start.3 = (s32[8]{0:T(128)S(1)}, s32[8]{0:T(128)S(1)}, u32[]{:S(2)}, u32[]{:S(2)}) collective-permute-start(s32[8]{0:T(128)S(1)} %slice.33), channel_id=1, source_target_pairs={{0,8},{8,16},{16,24},{1,9},{9,17},{17,25},{2,10},{10,18},{18,26},{... | collective-permute-start | bytes 104 | tf_op jit(solution)/shard_map/ppermute | solution.py:327
  5.2 1.1 %convolution_bitcast_fusion.refs_3_.refs_4_ = bf16[3584,128]{1,0:T(8,128)(2,1)S(1)} fusion(bf16[2,128]{1,0:T(2,128)(2,1)} %constant.25.clone, bf16[3584,2]{0,1:T(2,128)(2,1)S(1)} %copy-done), kind=kOutput, calls=%fused_computation | convolution fusion | flops 1835008 | bytes 932352 | tf_op jit(solution)/shard_map/dot_general | solution.py:318
  6.4 1.5 %copy-done.1 = bf16[2,3584,128]{2,1,0:T(8,128)(2,1)S(1)} copy-done((bf16[2,3584,128]{2,1,0:T(8,128)(2,1)S(1)}, bf16[2,3584,128]{2,1,0:T(8,128)(2,1)}, u32[]{:S(2)}) %copy-start.1) | copy-done | bytes 1835032
  7.9 1.2 %copy-done.3 = bf16[3584,128]{1,0:T(8,128)(2,1)S(1)} copy-done((bf16[3584,128]{1,0:T(8,128)(2,1)S(1)}, bf16[3584,128]{1,0:T(8,128)(2,1)}, u32[]{:S(2)}) %copy-start.3) | copy-done | bytes 917528
  9.1 1.0 %copy-done.8 = bf16[512,448]{0,1:T(8,128)(2,1)S(1)} copy-done((bf16[512,448]{0,1:T(8,128)(2,1)S(1)}, bf16[512,448]{0,1:T(8,128)(2,1)}, u32[]{:S(2)}) %copy-start.8) | copy-done | bytes 458776
  10.1 0.6 shard_map.127.refs_5_
  10.7 1.0 %copy-done.6 = f32[512,512]{1,0:T(8,128)} copy-done((f32[512,512]{1,0:T(8,128)}, f32[512,512]{1,0:T(8,128)S(1)}, u32[]{:S(2)}) %copy-start.6) | copy-done | bytes 1048600
  11.7 2.1 %collective-permute-done.refs_0_ = bf16[448,512]{1,0:T(8,128)(2,1)} collective-permute-done((bf16[448,512]{1,0:T(8,128)(2,1)}, bf16[448,512]{1,0:T(8,128)(2,1)}, u32[]{:S(2)}, u32[]{:S(2)}) %collective-permute-start) | collective-permute-done | bytes 458784 | tf_op jit(solution)/shard_map/ppermute | solution.py:31
  13.8 1.8 %collective-permute-start.1 = (bf16[448,512]{1,0:T(8,128)(2,1)}, bf16[448,512]{1,0:T(8,128)(2,1)}, u32[]{:S(2)}, u32[]{:S(2)}) collective-permute-start(bf16[448,512]{1,0:T(8,128)(2,1)} %collective-permute-done.refs_0_), channel_id=1, source_target_pairs={{0,2},{2,4},{4,6},{6,7},{7,5},{5,3},{3,1},{1,0},{8,10},{10,12},{12... | collective-permute-start | bytes 1376264 | tf_op jit(solution)/shard_map/ppermute | solution.py:31
  15.6 0.2 collective-permute-start.5
  15.8 0.6 fusion
  16.5 0.1 broadcast_in_dim_reshape.9.bias
  16.7 0.1 broadcast_in_dim_reshape.10.rate
  16.9 0.1 broadcast_in_dim_reshape.11.skip.refs_6_
  17.0 1.2 %copy-done.4 = bf16[3584,128]{1,0:T(8,128)(2,1)S(1)} copy-done((bf16[3584,128]{1,0:T(8,128)(2,1)S(1)}, bf16[3584,128]{1,0:T(8,128)(2,1)}, u32[]{:S(2)}) %copy-start.4) | copy-done | bytes 917528
  18.2 1.2 %copy-done.7 = f32[512,512]{1,0:T(8,128)S(1)} copy-done((f32[512,512]{1,0:T(8,128)S(1)}, f32[512,512]{1,0:T(8,128)}, u32[]{:S(2)}) %copy-start.7) | copy-done | bytes 1048600
  19.4 2.2 %shard_map.128.refs_5_ = f32[512,512]{1,0:T(8,128)S(1)} custom-call(bf16[448,512]{1,0:T(8,128)(2,1)} %collective-permute-done.refs_0_, bf16[448,512]{1,0:T(8,128)(2,1)S(1)} %collective-permute-done.2.refs_1_, bf16[2,3584,128]{2,1,0:T(8,128)(2,1)S(1)} %copy-done.2, bf16[3584,128]{1,0:T(8,128)(2,1)S(1)} %copy-done.4, ...), custom_call_target="tpu_custom_call" | custom-call | flops 1000000000 | bytes 2097152 | tf_op jit(solution)/shard_map/pallas_call | solution.py:355
  21.7 5.3 %collective-permute-done.1.refs_0_ = bf16[448,512]{1,0:T(8,128)(2,1)} collective-permute-done((bf16[448,512]{1,0:T(8,128)(2,1)}, bf16[448,512]{1,0:T(8,128)(2,1)}, u32[]{:S(2)}, u32[]{:S(2)}) %collective-permute-start.1) | collective-permute-done | bytes 458784 | tf_op jit(solution)/shard_map/ppermute | solution.py:31
  27.0 1.6 %collective-permute-start.4 = (bf16[448,512]{1,0:T(8,128)(2,1)}, bf16[448,512]{1,0:T(8,128)(2,1)S(1)}, u32[]{:S(2)}, u32[]{:S(2)}) collective-permute-start(bf16[448,512]{1,0:T(8,128)(2,1)} %collective-permute-done.1.refs_0_), channel_id=1, source_target_pairs={{0,2},{2,4},{4,6},{6,7},{7,5},{5,3},{3,1},{1,0},{8,10},{10,12},{12... | collective-permute-start | bytes 1376264 | tf_op jit(solution)/shard_map/ppermute | solution.py:31
  28.6 0.4 collective-permute-start.6
  29.0 0.1 multiply_convert_fusion.rest_0_
  29.2 1.6 %collective-permute-start.13 = (bf16[128,1792]{1,0:T(8,128)(2,1)S(1)}, bf16[128,1792]{1,0:T(8,128)(2,1)}, u32[]{:S(2)}, u32[]{:S(2)}) collective-permute-start(bf16[128,1792]{1,0:T(8,128)(2,1)S(1)} %multiply_convert_fusion.rest_0_), channel_id=1, source_target_pairs={{0,2},{2,4},{4,6},{6,7},{7,5},{5,3},{3,1},{1,0},{8,10},{10,12},{12... | collective-permute-start | bytes 1376264 | tf_op jit(solution)/shard_map/ppermute | solution.py:31
  30.8 0.4 collective-permute-start.14
  31.3 2.3 %shard_map.129.refs_5_ = f32[512,512]{1,0:T(8,128)S(1)} custom-call(bf16[448,512]{1,0:T(8,128)(2,1)} %collective-permute-done.1.refs_0_, bf16[448,512]{1,0:T(8,128)(2,1)} %collective-permute-done.5.refs_1_, bf16[2,3584,128]{2,1,0:T(8,128)(2,1)S(1)} %copy-done.2, bf16[3584,128]{1,0:T(8,128)(2,1)S(1)} %copy-done.4, ...), custom_call_target="tpu_custom_call" | custom-call | flops 1000000000 | bytes 2097152 | tf_op jit(solution)/shard_map/pallas_call | solution.py:355
  33.6 7.1 %collective-permute-done.4.forth.refs_0_ = bf16[448,512]{1,0:T(8,128)(2,1)S(1)} collective-permute-done((bf16[448,512]{1,0:T(8,128)(2,1)}, bf16[448,512]{1,0:T(8,128)(2,1)S(1)}, u32[]{:S(2)}, u32[]{:S(2)}) %collective-permute-start.4) | collective-permute-done | bytes 458784 | tf_op jit(solution)/shard_map/ppermute | solution.py:31
  40.6 1.6 %collective-permute-done.6.back.refs_1_ = bf16[448,512]{1,0:T(8,128)(2,1)S(1)} collective-permute-done((bf16[448,512]{1,0:T(8,128)(2,1)}, bf16[448,512]{1,0:T(8,128)(2,1)S(1)}, u32[]{:S(2)}, u32[]{:S(2)}) %collective-permute-start.6) | collective-permute-done | bytes 458784 | tf_op jit(solution)/shard_map/ppermute | solution.py:31
  42.3 1.6 %collective-permute-start.7 = (bf16[224,512]{1,0:T(8,128)(2,1)S(1)}, bf16[224,512]{1,0:T(8,128)(2,1)S(1)}, u32[]{:S(2)}, u32[]{:S(2)}) collective-permute-start(bf16[224,512]{1,0:T(8,128)(2,1)S(1)} %get-tuple-element.42), channel_id=1, source_target_pairs={{0,2},{2,4},{4,6},{6,7},{7,5},{5,3},{3,1},{1,0},{8,10},{10,12},{12... | collective-permute-start | bytes 688136 | tf_op jit(solution)/shard_map/ppermute | solution.py:31
  43.9 0.5 collective-permute-start.8
  44.3 1.3 %shard_map.131 = (f32[512,512]{1,0:T(8,128)S(1)}, bf16[448,512]{1,0:T(8,128)(2,1)S(1)}) custom-call(bf16[448,512]{1,0:T(8,128)(2,1)S(1)} %collective-permute-done.4.forth.refs_0_, bf16[448,512]{1,0:T(8,128)(2,1)S(1)} %collective-permute-done.6.back.refs_1_, bf16[2,3584,128]{2,1,0:T(8,128)(2,1)S(1)} %copy-done.2, bf16[3584,128]{1,0:T(8,128)(2,1)S(1)} %copy-done.5, ...), custom_call_target="tpu_custom_call" | custom-call | flops 1000000000 | bytes 2097152 | tf_op jit(solution)/shard_map/pallas_call | solution.py:355
  45.6 5.0 %collective-permute-done.13.rest_1_ = bf16[128,1792]{1,0:T(8,128)(2,1)} collective-permute-done((bf16[128,1792]{1,0:T(8,128)(2,1)S(1)}, bf16[128,1792]{1,0:T(8,128)(2,1)}, u32[]{:S(2)}, u32[]{:S(2)}) %collective-permute-start.13) | collective-permute-done | bytes 458784 | tf_op jit(solution)/shard_map/ppermute | solution.py:31
  50.6 1.6 %collective-permute-done.14.rest_2_ = bf16[128,1792]{1,0:T(8,128)(2,1)} collective-permute-done((bf16[128,1792]{1,0:T(8,128)(2,1)S(1)}, bf16[128,1792]{1,0:T(8,128)(2,1)}, u32[]{:S(2)}, u32[]{:S(2)}) %collective-permute-start.14) | collective-permute-done | bytes 458784 | tf_op jit(solution)/shard_map/ppermute | solution.py:31
  52.2 1.9 %collective-permute-done.7.top = bf16[224,512]{1,0:T(8,128)(2,1)S(1)} collective-permute-done((bf16[224,512]{1,0:T(8,128)(2,1)S(1)}, bf16[224,512]{1,0:T(8,128)(2,1)S(1)}, u32[]{:S(2)}, u32[]{:S(2)}) %collective-permute-start.7) | collective-permute-done | bytes 229408 | tf_op jit(solution)/shard_map/ppermute | solution.py:31
  54.0 1.0 %collective-permute-done.8.bottom = bf16[224,512]{1,0:T(8,128)(2,1)S(1)} collective-permute-done((bf16[224,512]{1,0:T(8,128)(2,1)S(1)}, bf16[224,512]{1,0:T(8,128)(2,1)S(1)}, u32[]{:S(2)}, u32[]{:S(2)}) %collective-permute-start.8) | collective-permute-done | bytes 229408 | tf_op jit(solution)/shard_map/ppermute | solution.py:31
  55.1 1.6 %collective-permute-start.15 = (bf16[128,1792]{1,0:T(8,128)(2,1)}, bf16[128,1792]{1,0:T(8,128)(2,1)S(1)}, u32[]{:S(2)}, u32[]{:S(2)}) collective-permute-start(bf16[128,1792]{1,0:T(8,128)(2,1)} %collective-permute-done.13.rest_1_), channel_id=1, source_target_pairs={{0,2},{2,4},{4,6},{6,7},{7,5},{5,3},{3,1},{1,0},{8,10},{10,12},{12... | collective-permute-start | bytes 1376264 | tf_op jit(solution)/shard_map/ppermute | solution.py:31
  56.6 0.5 collective-permute-start.16
  57.1 0.5 shard_map.132.proj.refs_7_
  57.6 1.3 %collective-permute-start.9 = (bf16[8,256]{1,0:T(8,128)(2,1)S(1)}, bf16[8,256]{1,0:T(8,128)(2,1)S(1)}, u32[]{:S(2)}, u32[]{:S(2)}) collective-permute-start(bf16[8,256]{1,0:T(8,128)(2,1)S(1)} %slice.44), channel_id=1, source_target_pairs={{0,8},{8,16},{16,24},{1,9},{9,17},{17,25},{2,10},{10,18},{18,26},{... | collective-permute-start | bytes 12296 | tf_op jit(solution)/shard_map/ppermute | solution.py:369
  58.9 0.1 copy.17.seg_ext
  59.0 0.1 copy.18.seg_ext.refs_4_
  59.2 1.0 %shard_map.133 = (f32[256,128]{1,0:T(8,128)S(1)}, f32[256,128]{1,0:T(8,128)S(1)}, f32[256,128]{1,0:T(8,128)S(1)}, f32[72,128]{1,0:T(8,128)S(1)}, f32[256,128]{1,0:T(8,128)S(1)}) custom-call(f32[512,512]{1,0:T(8,128)S(1)} %shard_map.132.proj.refs_7_, s32[264,1]{1,0:T(8,128)S(1)} %copy.17.seg_ext, s32[1,256]{1,0:T(1,128)S(1)} %bitcast.14, ...), custom_call_target="tpu_custom_call" | custom-call | flops 10000000 | bytes 2097152 | tf_op jit(solution)/shard_map/pallas_call | solution.py:374
  60.2 1.2 %shard_map.134 = (f32[256,128]{1,0:T(8,128)S(1)}, f32[256,128]{1,0:T(8,128)S(1)}, f32[256,128]{1,0:T(8,128)S(1)}, f32[256,128]{1,0:T(8,128)S(1)}, f32[256,128]{1...) custom-call(f32[512,512]{1,0:T(8,128)S(1)} %shard_map.132.proj.refs_7_, ...), custom_call_target="tpu_custom_call" | custom-call | flops 10000000 | bytes 2097152 | tf_op jit(solution)/shard_map/pallas_call | solution.py:379
  61.5 1.3 %collective-permute-start.11 = (f32[72,128]{1,0:T(8,128)S(1)}, f32[72,128]{1,0:T(8,128)S(1)}, u32[]{:S(2)}, u32[]{:S(2)}) collective-permute-start(f32[72,128]{1,0:T(8,128)S(1)} %get-tuple-element.47.refs_0_), channel_id=1, source_target_pairs={{0,16},{8,24},{16,0},{24,8},{1,17},{9,25},{17,1},{25,9},{2,18},{10... | collective-permute-start | bytes 110600 | tf_op jit(solution)/shard_map/ppermute | solution.py:386
  62.8 1.1 %collective-permute-start.12 = (f32[72,128]{1,0:T(8,128)S(1)}, f32[72,128]{1,0:T(8,128)S(1)}, u32[]{:S(2)}, u32[]{:S(2)}) collective-permute-start(f32[72,128]{1,0:T(8,128)S(1)} %collective-permute-done.10.refs_1_), channel_id=1, source_target_pairs={{0,16},{8,24},{16,0},{24,8},{1,17},{9,25},{17,1},{25,9},{2,18},{10... | collective-permute-start | bytes 110600 | tf_op jit(solution)/shard_map/ppermute | solution.py:387
  63.9 1.6 %collective-permute-done.11.refs_2_ = f32[72,128]{1,0:T(8,128)S(1)} collective-permute-done((f32[72,128]{1,0:T(8,128)S(1)}, f32[72,128]{1,0:T(8,128)S(1)}, u32[]{:S(2)}, u32[]{:S(2)}) %collective-permute-start.11) | collective-permute-done | bytes 36896 | tf_op jit(solution)/shard_map/ppermute | solution.py:386
  65.5 1.2 %collective-permute-done.12.refs_3_ = f32[72,128]{1,0:T(8,128)S(1)} collective-permute-done((f32[72,128]{1,0:T(8,128)S(1)}, f32[72,128]{1,0:T(8,128)S(1)}, u32[]{:S(2)}, u32[]{:S(2)}) %collective-permute-start.12) | collective-permute-done | bytes 36896 | tf_op jit(solution)/shard_map/ppermute | solution.py:387
  66.8 0.5 collective-permute-done.16.rest_4_
  67.3 1.6 %collective-permute-start.18 = (bf16[128,1792]{1,0:T(8,128)(2,1)S(1)}, bf16[128,1792]{1,0:T(8,128)(2,1)S(1)}, u32[]{:S(2)}, u32[]{:S(2)}) collective-permute-start(bf16[128,1792]{1,0:T(8,128)(2,1)S(1)} %collective-permute-done.15.rest_3_), channel_id=1, source_target_pairs={{0,2},{2,4},{4,6},{6,7},{7,5},{5,3},{3,1},{1,0},{8,10},{10,12},{12... | collective-permute-start | bytes 1376264 | tf_op jit(solution)/shard_map/ppermute | solution.py:31
  68.9 0.4 collective-permute-start.19
  69.3 1.7 %shard_map.135 = bf16[512,128]{1,0:T(8,128)(2,1)} custom-call(s32[1,1]{1,0:T(1,128)} %bitcast.seg_first, f32[72,128]{1,0:T(8,128)S(1)} %get-tuple-element.47.refs_0_, f32[72,128]{1,0:T(8,128)S(1)} %collective-permute-done.10.refs_1_, f32[72,128]{1,0:T(8,128)S(1)} %collective-permute-done.11.refs_2_, f32[72,128]{1,0:T(8,128)S(1)} %collective-permute-done.12.refs_3_, ...), custom_call_target="tpu_custom_call" | custom-call | flops 10000000 | bytes 2097152 | tf_op jit(solution)/shard_map/pallas_call | solution.py:391
  71.0 4.3 %all-to-all-start = ((bf16[8,64,128]{2,1,0:T(8,128)(2,1)}), bf16[8,64,128]{2,1,0:T(8,128)(2,1)S(1)}, u32[]{:S(2)}, u32[]{:S(2)}) async-start(bf16[8,64,128]{2,1,0:T(8,128)(2,1)} %bitcast.6), calls=%async_computation | async-start | bytes 262144 | tf_op jit(solution)/shard_map/all_to_all | solution.py:409
  75.4 3.8 %collective-permute-done.18.rest_5_.forth = bf16[128,1792]{1,0:T(8,128)(2,1)S(1)} collective-permute-done((bf16[128,1792]{1,0:T(8,128)(2,1)S(1)}, bf16[128,1792]{1,0:T(8,128)(2,1)S(1)}, u32[]{:S(2)}, u32[]{:S(2)}) %collective-permute-start.18) | collective-permute-done | bytes 458784 | tf_op jit(solution)/shard_map/ppermute | solution.py:31
  79.2 1.9 %collective-permute-done.19.rest_6_.back = bf16[128,1792]{1,0:T(8,128)(2,1)S(1)} collective-permute-done((bf16[128,1792]{1,0:T(8,128)(2,1)}, bf16[128,1792]{1,0:T(8,128)(2,1)S(1)}, u32[]{:S(2)}, u32[]{:S(2)}) %collective-permute-start.19) | collective-permute-done | bytes 458784 | tf_op jit(solution)/shard_map/ppermute | solution.py:31
  81.1 2.2 %collective-permute-start.20 = (bf16[64,1792]{1,0:T(8,128)(2,1)S(1)}, bf16[64,1792]{1,0:T(8,128)(2,1)S(1)}, u32[]{:S(2)}, u32[]{:S(2)}) collective-permute-start(bf16[64,1792]{1,0:T(8,128)(2,1)S(1)} %get-tuple-element.65), channel_id=1, source_target_pairs={{0,2},{2,4},{4,6},{6,7},{7,5},{5,3},{3,1},{1,0},{8,10},{10,12},{12... | collective-permute-start | bytes 688136 | tf_op jit(solution)/shard_map/ppermute | solution.py:31
  83.3 1.1 %all-to-all-done.mine = bf16[8,64,128]{2,1,0:T(8,128)(2,1)S(1)} async-done(((bf16[8,64,128]{2,1,0:T(8,128)(2,1)}), bf16[8,64,128]{2,1,0:T(8,128)(2,1)S(1)}, u32[]{:S(2)}, u32[]{:S(2)}) %all-to-all-start) | async-done | bytes 131104 | tf_op jit(solution)/shard_map/all_to_all | solution.py:409
  84.3 1.3 %collective-permute-done.17.other = bf16[8,64,128]{2,1,0:T(8,128)(2,1)S(1)} collective-permute-done((bf16[8,64,128]{2,1,0:T(8,128)(2,1)S(1)}, bf16[8,64,128]{2,1,0:T(8,128)(2,1)S(1)}, u32[]{:S(2)}, u32[]{:S(2)}) %collective-permute-start.17) | collective-permute-done | bytes 131104 | tf_op jit(solution)/shard_map/ppermute | solution.py:411
  85.7 1.0 %copy-done.10 = bf16[128,1792]{1,0:T(8,128)(2,1)S(1)} copy-done((bf16[128,1792]{1,0:T(8,128)(2,1)S(1)}, bf16[128,1792]{1,0:T(8,128)(2,1)}, u32[]{:S(2)}) %copy-start.10) | copy-done | bytes 458776
  86.7 2.3 %shard_map.136.total = f32[128,1792]{1,0:T(8,128)S(1)} custom-call(bf16[8,64,128]{2,1,0:T(8,128)(2,1)S(1)} %all-to-all-done.mine, bf16[8,64,128]{2,1,0:T(8,128)(2,1)S(1)} %collective-permute-done.17.other, bf16[128,1792]{1,0:T(8,128)(2,1)S(1)} %multiply_convert_fusion.rest_0_, bf16[128,1792]{1,0:T(8,128)(2,1)} %collective-permute-done.13.rest_1_, ...), custom_call_target="tpu_custom_call" | custom-call | flops 1 | bytes 1 | tf_op jit(solution)/shard_map/pallas_call | solution.py:416
  89.0 0.3 collective-permute-done.21.bottom
  89.3 0.2 shard_map.139
  89.6 1.0 %shard_map.138.whole = bf16[64,3584]{1,0:T(8,128)(2,1)} custom-call(bf16[8,64,128]{2,1,0:T(8,128)(2,1)S(1)} %all-to-all-done.mine, f32[128,1792]{1,0:T(8,128)S(1)} %shard_map.136.total, bf16[64,1792]{1,0:T(8,128)(2,1)S(1)} %collective-permute-done.20.top, bf16[64,1792]{1,0:T(8,128)(2,1)S(1)} %collective-permute-done.21.bottom), custom_call_target="tpu_custom_call" | custom-call | flops 10000000 | bytes 2097152 | tf_op jit(solution)/shard_map/pallas_call | solution.py:423
  90.6 0.5 collective-permute-done.22.arrived
  91.0 0.7 shard_map.140
  (55 shorter events, 0.7 us)
Async XLA Ops:
  0.0 5.2 %copy-start = (bf16[3584,2]{0,1:T(2,128)(2,1)S(1)}, bf16[3584,2]{0,1:T(2,128)(2,1)}, u32[]{:S(2)}) copy-start(bf16[3584,2]{0,1:T(2,128)(2,1)} %param.16) | copy-start | bytes 43012
  0.0 13.8 %collective-permute-start = (bf16[448,512]{1,0:T(8,128)(2,1)}, bf16[448,512]{1,0:T(8,128)(2,1)}, u32[]{:S(2)}, u32[]{:S(2)}) collective-permute-start(bf16[448,512]{1,0:T(8,128)(2,1)} %bitcast.10), channel_id=1, source_target_pairs={{0,2},{2,4},{4,6},{6,7},{7,5},{5,3},{3,1},{1,0},{8,10},{10,12},{12... | collective-permute-start | bytes 1376264 | tf_op jit(solution)/shard_map/ppermute | solution.py:31
  3.0 12.6 %collective-permute-start.2 = (bf16[448,512]{1,0:T(8,128)(2,1)}, bf16[448,512]{1,0:T(8,128)(2,1)S(1)}, u32[]{:S(2)}, u32[]{:S(2)}) collective-permute-start(bf16[448,512]{1,0:T(8,128)(2,1)} %bitcast.11), channel_id=1, source_target_pairs={{0,1},{2,0},{4,2},{6,4},{7,6},{5,7},{3,5},{1,3},{8,9},{10,8},{12,1... | collective-permute-start | bytes 1376264 | tf_op jit(solution)/shard_map/ppermute | solution.py:31
  3.8 13.2 %collective-permute-start.3 = (s32[8]{0:T(128)S(1)}, s32[8]{0:T(128)S(1)}, u32[]{:S(2)}, u32[]{:S(2)}) collective-permute-start(s32[8]{0:T(128)S(1)} %slice.33), channel_id=1, source_target_pairs={{0,8},{8,16},{16,24},{1,9},{9,17},{17,25},{2,10},{10,18},{18,26},{... | collective-permute-start | bytes 104 | tf_op jit(solution)/shard_map/ppermute | solution.py:327
  6.4 1.5 %copy-start.1 = (bf16[2,3584,128]{2,1,0:T(8,128)(2,1)S(1)}, bf16[2,3584,128]{2,1,0:T(8,128)(2,1)}, u32[]{:S(2)}) copy-start(bf16[2,3584,128]{2,1,0:T(8,128)(2,1)} %refs_2_.7) | copy-start | bytes 5505028
  7.9 1.2 %copy-start.3 = (bf16[3584,128]{1,0:T(8,128)(2,1)S(1)}, bf16[3584,128]{1,0:T(8,128)(2,1)}, u32[]{:S(2)}) copy-start(bf16[3584,128]{1,0:T(8,128)(2,1)} %refs_3_.5) | copy-start | bytes 2752516
  9.1 1.0 %copy-start.8 = (bf16[512,448]{0,1:T(8,128)(2,1)S(1)}, bf16[512,448]{0,1:T(8,128)(2,1)}, u32[]{:S(2)}) copy-start(bf16[512,448]{0,1:T(8,128)(2,1)} %param.13) | copy-start | bytes 1376260
  10.1 5.7 %copy-start.14 = (s32[512]{0:T(512)S(1)}, s32[512]{0:T(512)}, u32[]{:S(2)}) copy-start(s32[512]{0:T(512)} %param.24) | copy-start | bytes 6148
  10.1 6.4 %copy-start.16 = (f32[2]{0:T(128)S(1)}, f32[2]{0:T(128)}, u32[]{:S(2)}) copy-start(f32[2]{0:T(128)} %param.17) | copy-start | bytes 28
  10.1 6.6 %copy-start.17 = (f32[2]{0:T(128)S(1)}, f32[2]{0:T(128)}, u32[]{:S(2)}) copy-start(f32[2]{0:T(128)} %param.18) | copy-start | bytes 28
  10.1 6.7 %copy-start.18 = (f32[2]{0:T(128)S(1)}, f32[2]{0:T(128)}, u32[]{:S(2)}) copy-start(f32[2]{0:T(128)} %param.19) | copy-start | bytes 28
  10.1 7.0 %copy-start.2 = (bf16[2,3584,128]{2,1,0:T(8,128)(2,1)S(1)}, bf16[2,3584,128]{2,1,0:T(8,128)(2,1)}, u32[]{:S(2)}) copy-start(bf16[2,3584,128]{2,1,0:T(8,128)(2,1)} %refs_2_.7) | copy-start | bytes 5505028
  10.7 1.0 %copy-start.6 = (f32[512,512]{1,0:T(8,128)}, f32[512,512]{1,0:T(8,128)S(1)}, u32[]{:S(2)}) copy-start(f32[512,512]{1,0:T(8,128)S(1)} %shard_map.127.refs_5_) | copy-start | bytes 3145732
  13.8 13.2 %collective-permute-start.1 = (bf16[448,512]{1,0:T(8,128)(2,1)}, bf16[448,512]{1,0:T(8,128)(2,1)}, u32[]{:S(2)}, u32[]{:S(2)}) collective-permute-start(bf16[448,512]{1,0:T(8,128)(2,1)} %collective-permute-done.refs_0_), channel_id=1, source_target_pairs={{0,2},{2,4},{4,6},{6,7},{7,5},{5,3},{3,1},{1,0},{8,10},{10,12},{12... | collective-permute-start | bytes 1376264 | tf_op jit(solution)/shard_map/ppermute | solution.py:31
  15.6 13.0 %collective-permute-start.5 = (bf16[448,512]{1,0:T(8,128)(2,1)S(1)}, bf16[448,512]{1,0:T(8,128)(2,1)}, u32[]{:S(2)}, u32[]{:S(2)}) collective-permute-start(bf16[448,512]{1,0:T(8,128)(2,1)S(1)} %collective-permute-done.2.refs_1_), channel_id=1, source_target_pairs={{0,1},{2,0},{4,2},{6,4},{7,6},{5,7},{3,5},{1,3},{8,9},{10,8},{12,1... | collective-permute-start | bytes 1376264 | tf_op jit(solution)/shard_map/ppermute | solution.py:31
  17.0 1.2 %copy-start.4 = (bf16[3584,128]{1,0:T(8,128)(2,1)S(1)}, bf16[3584,128]{1,0:T(8,128)(2,1)}, u32[]{:S(2)}) copy-start(bf16[3584,128]{1,0:T(8,128)(2,1)} %refs_3_.5) | copy-start | bytes 2752516
  18.2 1.2 %copy-start.7 = (f32[512,512]{1,0:T(8,128)S(1)}, f32[512,512]{1,0:T(8,128)}, u32[]{:S(2)}) copy-start(f32[512,512]{1,0:T(8,128)} %copy-done.6) | copy-start | bytes 3145732
  19.4 9.6 %copy-start.13 = (bf16[128,3584]{1,0:T(8,128)(2,1)S(1)}, bf16[128,3584]{1,0:T(8,128)(2,1)}, u32[]{:S(2)}) copy-start(bf16[128,3584]{1,0:T(8,128)(2,1)} %param.23) | copy-start | bytes 2752516
  19.4 9.6 %copy-start.15 = (f32[128]{0:T(128)S(1)}, f32[128]{0:T(128)}, u32[]{:S(2)}) copy-start(f32[128]{0:T(128)} %param.22) | copy-start | bytes 1540
  27.0 13.6 %collective-permute-start.4 = (bf16[448,512]{1,0:T(8,128)(2,1)}, bf16[448,512]{1,0:T(8,128)(2,1)S(1)}, u32[]{:S(2)}, u32[]{:S(2)}) collective-permute-start(bf16[448,512]{1,0:T(8,128)(2,1)} %collective-permute-done.1.refs_0_), channel_id=1, source_target_pairs={{0,2},{2,4},{4,6},{6,7},{7,5},{5,3},{3,1},{1,0},{8,10},{10,12},{12... | collective-permute-start | bytes 1376264 | tf_op jit(solution)/shard_map/ppermute | solution.py:31
  28.6 13.7 %collective-permute-start.6 = (bf16[448,512]{1,0:T(8,128)(2,1)}, bf16[448,512]{1,0:T(8,128)(2,1)S(1)}, u32[]{:S(2)}, u32[]{:S(2)}) collective-permute-start(bf16[448,512]{1,0:T(8,128)(2,1)} %collective-permute-done.5.refs_1_), channel_id=1, source_target_pairs={{0,1},{2,0},{4,2},{6,4},{7,6},{5,7},{3,5},{1,3},{8,9},{10,8},{12,1... | collective-permute-start | bytes 1376264 | tf_op jit(solution)/shard_map/ppermute | solution.py:31
  29.2 15.2 %copy-start.5 = (bf16[3584,128]{1,0:T(8,128)(2,1)S(1)}, bf16[3584,128]{1,0:T(8,128)(2,1)}, u32[]{:S(2)}) copy-start(bf16[3584,128]{1,0:T(8,128)(2,1)} %refs_3_.5) | copy-start | bytes 2752516
  29.2 21.4 %collective-permute-start.13 = (bf16[128,1792]{1,0:T(8,128)(2,1)S(1)}, bf16[128,1792]{1,0:T(8,128)(2,1)}, u32[]{:S(2)}, u32[]{:S(2)}) collective-permute-start(bf16[128,1792]{1,0:T(8,128)(2,1)S(1)} %multiply_convert_fusion.rest_0_), channel_id=1, source_target_pairs={{0,2},{2,4},{4,6},{6,7},{7,5},{5,3},{3,1},{1,0},{8,10},{10,12},{12... | collective-permute-start | bytes 1376264 | tf_op jit(solution)/shard_map/ppermute | solution.py:31
  30.8 21.4 %collective-permute-start.14 = (bf16[128,1792]{1,0:T(8,128)(2,1)S(1)}, bf16[128,1792]{1,0:T(8,128)(2,1)}, u32[]{:S(2)}, u32[]{:S(2)}) collective-permute-start(bf16[128,1792]{1,0:T(8,128)(2,1)S(1)} %multiply_convert_fusion.rest_0_), channel_id=1, source_target_pairs={{0,1},{2,0},{4,2},{6,4},{7,6},{5,7},{3,5},{1,3},{8,9},{10,8},{12,1... | collective-permute-start | bytes 1376264 | tf_op jit(solution)/shard_map/ppermute | solution.py:31
  42.3 11.8 %collective-permute-start.7 = (bf16[224,512]{1,0:T(8,128)(2,1)S(1)}, bf16[224,512]{1,0:T(8,128)(2,1)S(1)}, u32[]{:S(2)}, u32[]{:S(2)}) collective-permute-start(bf16[224,512]{1,0:T(8,128)(2,1)S(1)} %get-tuple-element.42), channel_id=1, source_target_pairs={{0,2},{2,4},{4,6},{6,7},{7,5},{5,3},{3,1},{1,0},{8,10},{10,12},{12... | collective-permute-start | bytes 688136 | tf_op jit(solution)/shard_map/ppermute | solution.py:31
  43.9 11.2 %collective-permute-start.8 = (bf16[224,512]{1,0:T(8,128)(2,1)S(1)}, bf16[224,512]{1,0:T(8,128)(2,1)S(1)}, u32[]{:S(2)}, u32[]{:S(2)}) collective-permute-start(bf16[224,512]{1,0:T(8,128)(2,1)S(1)} %get-tuple-element.43), channel_id=1, source_target_pairs={{0,1},{2,0},{4,2},{6,4},{7,6},{5,7},{3,5},{1,3},{8,9},{10,8},{12,1... | collective-permute-start | bytes 688136 | tf_op jit(solution)/shard_map/ppermute | solution.py:31
  55.1 11.7 %collective-permute-start.15 = (bf16[128,1792]{1,0:T(8,128)(2,1)}, bf16[128,1792]{1,0:T(8,128)(2,1)S(1)}, u32[]{:S(2)}, u32[]{:S(2)}) collective-permute-start(bf16[128,1792]{1,0:T(8,128)(2,1)} %collective-permute-done.13.rest_1_), channel_id=1, source_target_pairs={{0,2},{2,4},{4,6},{6,7},{7,5},{5,3},{3,1},{1,0},{8,10},{10,12},{12... | collective-permute-start | bytes 1376264 | tf_op jit(solution)/shard_map/ppermute | solution.py:31
  56.6 10.7 %collective-permute-start.16 = (bf16[128,1792]{1,0:T(8,128)(2,1)}, bf16[128,1792]{1,0:T(8,128)(2,1)}, u32[]{:S(2)}, u32[]{:S(2)}) collective-permute-start(bf16[128,1792]{1,0:T(8,128)(2,1)} %collective-permute-done.14.rest_2_), channel_id=1, source_target_pairs={{0,1},{2,0},{4,2},{6,4},{7,6},{5,7},{3,5},{1,3},{8,9},{10,8},{12,1... | collective-permute-start | bytes 1376264 | tf_op jit(solution)/shard_map/ppermute | solution.py:31
  57.1 2.1 %copy-start.11 = (f32[4,128]{1,0:T(4,128)S(1)}, f32[4,128]{1,0:T(4,128)}, u32[]{:S(2)}) copy-start(f32[4,128]{1,0:T(4,128)} %taps_x.3) | copy-start | bytes 6148
  57.1 2.1 %copy-start.12 = (f32[4,128]{1,0:T(4,128)S(1)}, f32[4,128]{1,0:T(4,128)}, u32[]{:S(2)}) copy-start(f32[4,128]{1,0:T(4,128)} %taps_bc.3) | copy-start | bytes 6148
  57.6 2.6 %collective-permute-start.9 = (bf16[8,256]{1,0:T(8,128)(2,1)S(1)}, bf16[8,256]{1,0:T(8,128)(2,1)S(1)}, u32[]{:S(2)}, u32[]{:S(2)}) collective-permute-start(bf16[8,256]{1,0:T(8,128)(2,1)S(1)} %slice.44), channel_id=1, source_target_pairs={{0,8},{8,16},{16,24},{1,9},{9,17},{17,25},{2,10},{10,18},{18,26},{... | collective-permute-start | bytes 12296 | tf_op jit(solution)/shard_map/ppermute | solution.py:369
  61.4 1.4 %collective-permute-start.10 = (f32[72,128]{1,0:T(8,128)S(1)}, f32[72,128]{1,0:T(8,128)S(1)}, u32[]{:S(2)}, u32[]{:S(2)}) collective-permute-start(f32[72,128]{1,0:T(8,128)S(1)} %get-tuple-element.47.refs_0_), channel_id=1, source_target_pairs={{0,8},{8,0},{16,24},{24,16},{1,9},{9,1},{17,25},{25,17},{2,10},{10... | collective-permute-start | bytes 110600 | tf_op jit(solution)/shard_map/ppermute | solution.py:385
  61.5 4.0 %collective-permute-start.11 = (f32[72,128]{1,0:T(8,128)S(1)}, f32[72,128]{1,0:T(8,128)S(1)}, u32[]{:S(2)}, u32[]{:S(2)}) collective-permute-start(f32[72,128]{1,0:T(8,128)S(1)} %get-tuple-element.47.refs_0_), channel_id=1, source_target_pairs={{0,16},{8,24},{16,0},{24,8},{1,17},{9,25},{17,1},{25,9},{2,18},{10... | collective-permute-start | bytes 110600 | tf_op jit(solution)/shard_map/ppermute | solution.py:386
  62.8 4.0 %collective-permute-start.12 = (f32[72,128]{1,0:T(8,128)S(1)}, f32[72,128]{1,0:T(8,128)S(1)}, u32[]{:S(2)}, u32[]{:S(2)}) collective-permute-start(f32[72,128]{1,0:T(8,128)S(1)} %collective-permute-done.10.refs_1_), channel_id=1, source_target_pairs={{0,16},{8,24},{16,0},{24,8},{1,17},{9,25},{17,1},{25,9},{2,18},{10... | collective-permute-start | bytes 110600 | tf_op jit(solution)/shard_map/ppermute | solution.py:387
  66.8 14.3 %copy-start.9 = (bf16[128,1792]{1,0:T(8,128)(2,1)}, bf16[128,1792]{1,0:T(8,128)(2,1)S(1)}, u32[]{:S(2)}) copy-start(bf16[128,1792]{1,0:T(8,128)(2,1)S(1)} %collective-permute-done.15.rest_3_) | copy-start | bytes 1376260
  67.3 11.9 %collective-permute-start.18 = (bf16[128,1792]{1,0:T(8,128)(2,1)S(1)}, bf16[128,1792]{1,0:T(8,128)(2,1)S(1)}, u32[]{:S(2)}, u32[]{:S(2)}) collective-permute-start(bf16[128,1792]{1,0:T(8,128)(2,1)S(1)} %collective-permute-done.15.rest_3_), channel_id=1, source_target_pairs={{0,2},{2,4},{4,6},{6,7},{7,5},{5,3},{3,1},{1,0},{8,10},{10,12},{12... | collective-permute-start | bytes 1376264 | tf_op jit(solution)/shard_map/ppermute | solution.py:31
  68.9 12.2 %collective-permute-start.19 = (bf16[128,1792]{1,0:T(8,128)(2,1)}, bf16[128,1792]{1,0:T(8,128)(2,1)S(1)}, u32[]{:S(2)}, u32[]{:S(2)}) collective-permute-start(bf16[128,1792]{1,0:T(8,128)(2,1)} %collective-permute-done.16.rest_4_), channel_id=1, source_target_pairs={{0,1},{2,0},{4,2},{6,4},{7,6},{5,7},{3,5},{1,3},{8,9},{10,8},{12,1... | collective-permute-start | bytes 1376264 | tf_op jit(solution)/shard_map/ppermute | solution.py:31
  71.0 13.3 %all-to-all-start = ((bf16[8,64,128]{2,1,0:T(8,128)(2,1)}), bf16[8,64,128]{2,1,0:T(8,128)(2,1)S(1)}, u32[]{:S(2)}, u32[]{:S(2)}) async-start(bf16[8,64,128]{2,1,0:T(8,128)(2,1)} %bitcast.6), calls=%async_computation | async-start | bytes 262144 | tf_op jit(solution)/shard_map/all_to_all | solution.py:409
  81.1 7.9 %collective-permute-start.20 = (bf16[64,1792]{1,0:T(8,128)(2,1)S(1)}, bf16[64,1792]{1,0:T(8,128)(2,1)S(1)}, u32[]{:S(2)}, u32[]{:S(2)}) collective-permute-start(bf16[64,1792]{1,0:T(8,128)(2,1)S(1)} %get-tuple-element.65), channel_id=1, source_target_pairs={{0,2},{2,4},{4,6},{6,7},{7,5},{5,3},{3,1},{1,0},{8,10},{10,12},{12... | collective-permute-start | bytes 688136 | tf_op jit(solution)/shard_map/ppermute | solution.py:31
  83.3 6.0 %collective-permute-start.21 = (bf16[64,1792]{1,0:T(8,128)(2,1)S(1)}, bf16[64,1792]{1,0:T(8,128)(2,1)S(1)}, u32[]{:S(2)}, u32[]{:S(2)}) collective-permute-start(bf16[64,1792]{1,0:T(8,128)(2,1)S(1)} %get-tuple-element.66), channel_id=1, source_target_pairs={{0,1},{2,0},{4,2},{6,4},{7,6},{5,7},{3,5},{1,3},{8,9},{10,8},{12,1... | collective-permute-start | bytes 688136 | tf_op jit(solution)/shard_map/ppermute | solution.py:31
  84.3 1.3 %collective-permute-start.17 = (bf16[8,64,128]{2,1,0:T(8,128)(2,1)S(1)}, bf16[8,64,128]{2,1,0:T(8,128)(2,1)S(1)}, u32[]{:S(2)}, u32[]{:S(2)}) collective-permute-start(bf16[8,64,128]{2,1,0:T(8,128)(2,1)S(1)} %all-to-all-done.mine), channel_id=1, source_target_pairs={{0,8},{8,0},{16,24},{24,16},{1,9},{9,1},{17,25},{25,17},{2,10},{10... | collective-permute-start | bytes 393224 | tf_op jit(solution)/shard_map/ppermute | solution.py:411
  85.7 1.0 %copy-start.10 = (bf16[128,1792]{1,0:T(8,128)(2,1)S(1)}, bf16[128,1792]{1,0:T(8,128)(2,1)}, u32[]{:S(2)}) copy-start(bf16[128,1792]{1,0:T(8,128)(2,1)} %copy-done.9) | copy-start | bytes 1376260
  89.5 1.6 %collective-permute-start.22 = (bf16[64,1792]{1,0:T(8,128)(2,1)S(1)}, bf16[64,1792]{1,0:T(8,128)(2,1)S(1)}, u32[]{:S(2)}, u32[]{:S(2)}) collective-permute-start(bf16[64,1792]{1,0:T(8,128)(2,1)S(1)} %shard_map.139), channel_id=1, source_target_pairs={{0,8},{8,0},{16,24},{24,16},{1,9},{9,1},{17,25},{25,17},{2,10},{10... | collective-permute-start | bytes 688136 | tf_op jit(solution)/shard_map/ppermute | solution.py:422

commit v25 on v21

--- a/solution.py
+++ b/solution.py
@@ -200,10 +200,15 @@
     state_out[:state_w] = state
     state_out[state_w : state_w + 1] = keep
     state_out[state_w + 1 :] = jnp.zeros((state_out.shape[0] - state_w - 1, width), F32)
-    message[:state_w] = state_b[state_w : state_w + 1] * state + state_b[:state_w]
-    message[state_w : state_w + 1] = last + state_b[state_w + 1 : state_w + 2]
-    message[state_w + 1 : state_w + 2] = jnp.broadcast_to(seg_last[...].astype(F32), (1, width))
-    message[state_w + 2 :] = jnp.zeros((message.shape[0] - state_w - 2, width), F32)
+    message[:state_w] = (state_b[state_w : state_w + 1] * state + state_b[:state_w]).astype(BF16)
+    rest = last + state_b[state_w + 1 : state_w + 2]
+    row = lax.broadcasted_iota(jnp.int32, (message.shape[0] - state_w, width), 0)
+    head = jnp.where(row == 3, seg_last[...].astype(F32), 0.0)
+    for k in range(3):
+        part = rest.astype(BF16).astype(F32)
+        head = jnp.where(row == k, part, head)
+        rest = rest - part
+    message[state_w:] = head.astype(BF16)
 
 
 def finish(heads, rows, count, seg_first, *refs):
@@ -213,11 +218,11 @@
 
 def message_from(messages, device):
     if len(messages) == 1:
-        return messages[0][device]
+        return messages[0][device].astype(F32)
     place = lax.axis_index("seq")
     core = place % 2 == device % 2
     plane = place // 2 == device // 2
-    own, other_core, other_plane, other_both = (m[...] for m in messages)
+    own, other_core, other_plane, other_both = (m[...].astype(F32) for m in messages)
     return jnp.where(plane, jnp.where(core, own, other_core), jnp.where(core, other_plane, other_both))
 
 
@@ -232,10 +237,11 @@
     for device in reversed(range(lax.axis_size("seq") - 1)):
         earlier = device < place
         message = message_from(messages, device)
-        passes = earlier & (message[state_w + 1 : state_w + 2] == first)
+        total = sum(message[state_w + k : state_w + k + 1] for k in (2, 1, 0))
+        passes = earlier & (message[state_w + 3 : state_w + 4] == first)
         passes = jnp.where(passes, jnp.exp(decay), 0.0)
         entering = entering + passes * message[:state_w]
-        decay = decay + jnp.where(earlier, message[state_w : state_w + 1], 0.0)
+        decay = decay + jnp.where(earlier, total, 0.0)
     second = state_a[state_w : state_w + 1] * entering + state_a[:state_w]
     out_a = block_inner(bc_a[...], cum_a[...], scaled_a[...], seg_ext_a[HALO:], seg_row_a[...], heads)
     out_a = out_a + skip[...] * conv_a[...] + enter_a[...] * dot(bc_a[:, state_w:], entering)
@@ -378,7 +384,7 @@
     )(proj, seg_ext_b, seg_row_b, conv_x, conv_bc, bias, rate, skip)
     cx_a, bc_a, cum_a, scaled_a, enter_a, state_a, message = call(
         functools.partial(first_front, width, rows),
-        [plane] * 5 + [shape(msg_rows, width)] * 2,
+        [plane] * 5 + [shape(msg_rows, width), shape(state_w + 16, width, kind=BF16)],
         [ext, ext],
     )(proj, halo, seg_ext_a, seg_last, state_b, conv_x, conv_bc, bias, rate)
     if n_seq == 4:

time: 91.8 us -> 91.7 us (level)
  no operation moved by 1% of the time
where the time goes in v25:
time: 91.7 us; the launch traced here: 91.1 us
  waiting for transfers between devices  36.9 us (40%)
  starting transfers between devices  29.7 us (32%)
  Pallas kernels  17 us (19%)
  local copies, waits for them, and re-layouts  5.9 us (6%)
  matrix products  1.12 us (1%)
    ppermute x16, waiting for transfers between devices, ring_shift(): lax.ppermute(block, 'tensor', [(order[i], order[(i + step) % n]) for i in...  30.8 us
    ppermute x16, starting transfers between devices, ring_shift(): lax.ppermute(block, 'tensor', [(order[i], order[(i + step) % n]) for i in...  17.4 us
    pallas_call x4, Pallas kernels, local(): call(functools.partial(project, [distance for distance, _ in arrived], ah...  8.46 us
    all_to_all x1, starting transfers between devices, local(): mine = lax.all_to_all(blocks, 'tensor', 0, 0)  5.01 us
    unnamed x26, local copies, waits for them, and re-layouts  3.73 us
    pallas_call x1, Pallas kernels, local(): call(functools.partial(product_early, distances), shape(2 * tok_own, colu...  2.14 us
  transfers between devices with their start and end apart: 24, of which 16 were waited for; matrix products, arithmetic and copies ran while one was open for 4% of the time, Pallas kernels for 18%

profile of v25, /device:TPU:0, one launch (start us, length us, event | category | flops | bytes accessed | tf_op | source)
XLA Modules:
  0.0 91.1 jit_solution(4471891679283169402)
XLA Ops:
  0.0 3.0 %collective-permute-start = (bf16[448,512]{1,0:T(8,128)(2,1)}, bf16[448,512]{1,0:T(8,128)(2,1)}, u32[]{:S(2)}, u32[]{:S(2)}) collective-permute-start(bf16[448,512]{1,0:T(8,128)(2,1)} %bitcast.10), channel_id=1, source_target_pairs={{0,2},{2,4},{4,6},{6,7},{7,5},{5,3},{3,1},{1,0},{8,10},{10,12},{12... | collective-permute-start | bytes 1376264 | tf_op jit(solution)/shard_map/ppermute | solution.py:31
  3.0 0.8 slice.33
  3.8 1.4 %collective-permute-start.3 = (s32[8]{0:T(128)S(1)}, s32[8]{0:T(128)S(1)}, u32[]{:S(2)}, u32[]{:S(2)}) collective-permute-start(s32[8]{0:T(128)S(1)} %slice.33), channel_id=1, source_target_pairs={{0,8},{8,16},{16,24},{1,9},{9,17},{17,25},{2,10},{10,18},{18,26},{... | collective-permute-start | bytes 104 | tf_op jit(solution)/shard_map/ppermute | solution.py:333
  5.2 1.1 %convolution_bitcast_fusion.refs_3_.refs_4_ = bf16[3584,128]{1,0:T(8,128)(2,1)S(1)} fusion(bf16[2,128]{1,0:T(2,128)(2,1)} %constant.25.clone, bf16[3584,2]{0,1:T(2,128)(2,1)S(1)} %copy-done), kind=kOutput, calls=%fused_computation | convolution fusion | flops 1835008 | bytes 932352 | tf_op jit(solution)/shard_map/dot_general | solution.py:324
  6.4 1.5 %copy-done.1 = bf16[2,3584,128]{2,1,0:T(8,128)(2,1)S(1)} copy-done((bf16[2,3584,128]{2,1,0:T(8,128)(2,1)S(1)}, bf16[2,3584,128]{2,1,0:T(8,128)(2,1)}, u32[]{:S(2)}) %copy-start.1) | copy-done | bytes 1835032
  7.9 1.2 %copy-done.2 = bf16[3584,128]{1,0:T(8,128)(2,1)S(1)} copy-done((bf16[3584,128]{1,0:T(8,128)(2,1)S(1)}, bf16[3584,128]{1,0:T(8,128)(2,1)}, u32[]{:S(2)}) %copy-start.2) | copy-done | bytes 917528
  9.1 1.0 %copy-done.4 = bf16[512,448]{0,1:T(8,128)(2,1)S(1)} copy-done((bf16[512,448]{0,1:T(8,128)(2,1)S(1)}, bf16[512,448]{0,1:T(8,128)(2,1)}, u32[]{:S(2)}) %copy-start.4) | copy-done | bytes 458776
  10.1 0.6 shard_map.127.refs_5_
  10.7 3.1 %collective-permute-done.refs_0_ = bf16[448,512]{1,0:T(8,128)(2,1)} collective-permute-done((bf16[448,512]{1,0:T(8,128)(2,1)}, bf16[448,512]{1,0:T(8,128)(2,1)}, u32[]{:S(2)}, u32[]{:S(2)}) %collective-permute-start) | collective-permute-done | bytes 458784 | tf_op jit(solution)/shard_map/ppermute | solution.py:31
  13.8 1.8 %collective-permute-start.1 = (bf16[448,512]{1,0:T(8,128)(2,1)}, bf16[448,512]{1,0:T(8,128)(2,1)}, u32[]{:S(2)}, u32[]{:S(2)}) collective-permute-start(bf16[448,512]{1,0:T(8,128)(2,1)} %collective-permute-done.refs_0_), channel_id=1, source_target_pairs={{0,2},{2,4},{4,6},{6,7},{7,5},{5,3},{3,1},{1,0},{8,10},{10,12},{12... | collective-permute-start | bytes 1376264 | tf_op jit(solution)/shard_map/ppermute | solution.py:31
  15.6 0.2 collective-permute-start.5
  15.8 0.6 fusion
  16.4 0.1 slice.36
  16.5 0.1 broadcast_in_dim.27
  16.5 0.1 broadcast_in_dim_reshape.9.bias
  16.7 0.1 broadcast_in_dim_reshape.10.rate
  16.9 0.1 broadcast_in_dim_reshape.11.skip.refs_6_
  16.9 0.1 pad_add_fusion
  17.1 3.0 %shard_map.128.refs_5_ = f32[512,512]{1,0:T(8,128)S(1)} custom-call(bf16[448,512]{1,0:T(8,128)(2,1)} %collective-permute-done.refs_0_, bf16[448,512]{1,0:T(8,128)(2,1)S(1)} %collective-permute-done.2.refs_1_, bf16[2,3584,128]{2,1,0:T(8,128)(2,1)} %refs_2_.7, bf16[3584,128]{1,0:T(8,128)(2,1)S(1)} %copy-done.3, ...), custom_call_target="tpu_custom_call" | custom-call | flops 1000000000 | bytes 2097152 | tf_op jit(solution)/shard_map/pallas_call | solution.py:361
  20.0 6.0 %collective-permute-done.1.refs_0_ = bf16[448,512]{1,0:T(8,128)(2,1)} collective-permute-done((bf16[448,512]{1,0:T(8,128)(2,1)}, bf16[448,512]{1,0:T(8,128)(2,1)}, u32[]{:S(2)}, u32[]{:S(2)}) %collective-permute-start.1) | collective-permute-done | bytes 458784 | tf_op jit(solution)/shard_map/ppermute | solution.py:31
  26.0 1.6 %collective-permute-start.4 = (bf16[448,512]{1,0:T(8,128)(2,1)}, bf16[448,512]{1,0:T(8,128)(2,1)S(1)}, u32[]{:S(2)}, u32[]{:S(2)}) collective-permute-start(bf16[448,512]{1,0:T(8,128)(2,1)} %collective-permute-done.1.refs_0_), channel_id=1, source_target_pairs={{0,2},{2,4},{4,6},{6,7},{7,5},{5,3},{3,1},{1,0},{8,10},{10,12},{12... | collective-permute-start | bytes 1376264 | tf_op jit(solution)/shard_map/ppermute | solution.py:31
  27.6 0.4 collective-permute-start.6
  28.1 0.1 multiply_convert_fusion.rest_0_
  28.2 1.6 %collective-permute-start.13 = (bf16[128,1792]{1,0:T(8,128)(2,1)S(1)}, bf16[128,1792]{1,0:T(8,128)(2,1)S(1)}, u32[]{:S(2)}, u32[]{:S(2)}) collective-permute-start(bf16[128,1792]{1,0:T(8,128)(2,1)S(1)} %multiply_convert_fusion.rest_0_), channel_id=1, source_target_pairs={{0,2},{2,4},{4,6},{6,7},{7,5},{5,3},{3,1},{1,0},{8,10},{10,12},{12... | collective-permute-start | bytes 1376264 | tf_op jit(solution)/shard_map/ppermute | solution.py:31
  29.9 0.4 collective-permute-start.14
  30.3 3.0 %shard_map.129.refs_5_ = f32[512,512]{1,0:T(8,128)S(1)} custom-call(bf16[448,512]{1,0:T(8,128)(2,1)} %collective-permute-done.1.refs_0_, bf16[448,512]{1,0:T(8,128)(2,1)} %collective-permute-done.5.refs_1_, bf16[2,3584,128]{2,1,0:T(8,128)(2,1)} %refs_2_.7, bf16[3584,128]{1,0:T(8,128)(2,1)S(1)} %copy-done.3, ...), custom_call_target="tpu_custom_call" | custom-call | flops 1000000000 | bytes 2097152 | tf_op jit(solution)/shard_map/pallas_call | solution.py:361
  33.3 6.4 %collective-permute-done.4.forth.refs_0_ = bf16[448,512]{1,0:T(8,128)(2,1)S(1)} collective-permute-done((bf16[448,512]{1,0:T(8,128)(2,1)}, bf16[448,512]{1,0:T(8,128)(2,1)S(1)}, u32[]{:S(2)}, u32[]{:S(2)}) %collective-permute-start.4) | collective-permute-done | bytes 458784 | tf_op jit(solution)/shard_map/ppermute | solution.py:31
  39.7 1.6 %collective-permute-done.6.back.refs_1_ = bf16[448,512]{1,0:T(8,128)(2,1)S(1)} collective-permute-done((bf16[448,512]{1,0:T(8,128)(2,1)}, bf16[448,512]{1,0:T(8,128)(2,1)S(1)}, u32[]{:S(2)}, u32[]{:S(2)}) %collective-permute-start.6) | collective-permute-done | bytes 458784 | tf_op jit(solution)/shard_map/ppermute | solution.py:31
  41.3 1.6 %collective-permute-start.7 = (bf16[224,512]{1,0:T(8,128)(2,1)S(1)}, bf16[224,512]{1,0:T(8,128)(2,1)S(1)}, u32[]{:S(2)}, u32[]{:S(2)}) collective-permute-start(bf16[224,512]{1,0:T(8,128)(2,1)S(1)} %get-tuple-element.42), channel_id=1, source_target_pairs={{0,2},{2,4},{4,6},{6,7},{7,5},{5,3},{3,1},{1,0},{8,10},{10,12},{12... | collective-permute-start | bytes 688136 | tf_op jit(solution)/shard_map/ppermute | solution.py:31
  43.0 0.5 collective-permute-start.8
  43.4 1.9 %shard_map.131 = (f32[512,512]{1,0:T(8,128)S(1)}, bf16[448,512]{1,0:T(8,128)(2,1)S(1)}) custom-call(bf16[448,512]{1,0:T(8,128)(2,1)S(1)} %collective-permute-done.4.forth.refs_0_, bf16[448,512]{1,0:T(8,128)(2,1)S(1)} %collective-permute-done.6.back.refs_1_, bf16[2,3584,128]{2,1,0:T(8,128)(2,1)} %refs_2_.7, bf16[3584,128]{1,0:T(8,128)(2,1)S(1)} %copy-done.3, ...), custom_call_target="tpu_custom_call" | custom-call | flops 1000000000 | bytes 2097152 | tf_op jit(solution)/shard_map/pallas_call | solution.py:361
  45.3 4.2 %collective-permute-done.13.rest_1_ = bf16[128,1792]{1,0:T(8,128)(2,1)S(1)} collective-permute-done((bf16[128,1792]{1,0:T(8,128)(2,1)S(1)}, bf16[128,1792]{1,0:T(8,128)(2,1)S(1)}, u32[]{:S(2)}, u32[]{:S(2)}) %collective-permute-start.13) | collective-permute-done | bytes 458784 | tf_op jit(solution)/shard_map/ppermute | solution.py:31
  49.5 1.1 %collective-permute-done.14.rest_2_ = bf16[128,1792]{1,0:T(8,128)(2,1)S(1)} collective-permute-done((bf16[128,1792]{1,0:T(8,128)(2,1)S(1)}, bf16[128,1792]{1,0:T(8,128)(2,1)S(1)}, u32[]{:S(2)}, u32[]{:S(2)}) %collective-permute-start.14) | collective-permute-done | bytes 458784 | tf_op jit(solution)/shard_map/ppermute | solution.py:31
  50.6 1.4 %collective-permute-done.7.top = bf16[224,512]{1,0:T(8,128)(2,1)S(1)} collective-permute-done((bf16[224,512]{1,0:T(8,128)(2,1)S(1)}, bf16[224,512]{1,0:T(8,128)(2,1)S(1)}, u32[]{:S(2)}, u32[]{:S(2)}) %collective-permute-start.7) | collective-permute-done | bytes 229408 | tf_op jit(solution)/shard_map/ppermute | solution.py:31
  52.0 1.0 %collective-permute-done.8.bottom = bf16[224,512]{1,0:T(8,128)(2,1)S(1)} collective-permute-done((bf16[224,512]{1,0:T(8,128)(2,1)S(1)}, bf16[224,512]{1,0:T(8,128)(2,1)S(1)}, u32[]{:S(2)}, u32[]{:S(2)}) %collective-permute-start.8) | collective-permute-done | bytes 229408 | tf_op jit(solution)/shard_map/ppermute | solution.py:31
  53.1 1.6 %collective-permute-start.15 = (bf16[128,1792]{1,0:T(8,128)(2,1)S(1)}, bf16[128,1792]{1,0:T(8,128)(2,1)}, u32[]{:S(2)}, u32[]{:S(2)}) collective-permute-start(bf16[128,1792]{1,0:T(8,128)(2,1)S(1)} %collective-permute-done.13.rest_1_), channel_id=1, source_target_pairs={{0,2},{2,4},{4,6},{6,7},{7,5},{5,3},{3,1},{1,0},{8,10},{10,12},{12... | collective-permute-start | bytes 1376264 | tf_op jit(solution)/shard_map/ppermute | solution.py:31
  54.7 0.5 collective-permute-start.16
  55.1 0.5 shard_map.132.proj.refs_7_
  55.6 1.3 %collective-permute-start.9 = (bf16[8,256]{1,0:T(8,128)(2,1)S(1)}, bf16[8,256]{1,0:T(8,128)(2,1)S(1)}, u32[]{:S(2)}, u32[]{:S(2)}) collective-permute-start(bf16[8,256]{1,0:T(8,128)(2,1)S(1)} %slice.44), channel_id=1, source_target_pairs={{0,8},{8,16},{16,24},{1,9},{9,17},{17,25},{2,10},{10,18},{18,26},{... | collective-permute-start | bytes 12296 | tf_op jit(solution)/shard_map/ppermute | solution.py:375
  56.9 0.1 copy.17.seg_ext
  57.1 0.1 copy.18.seg_ext.refs_4_
  57.2 1.0 %shard_map.133 = (f32[256,128]{1,0:T(8,128)S(1)}, f32[256,128]{1,0:T(8,128)S(1)}, f32[256,128]{1,0:T(8,128)S(1)}, f32[72,128]{1,0:T(8,128)S(1)}, f32[256,128]{1,0:T(8,128)S(1)}) custom-call(f32[512,512]{1,0:T(8,128)S(1)} %shard_map.132.proj.refs_7_, s32[264,1]{1,0:T(8,128)S(1)} %copy.17.seg_ext, s32[1,256]{1,0:T(1,128)S(1)} %bitcast.14, ...), custom_call_target="tpu_custom_call" | custom-call | flops 10000000 | bytes 2097152 | tf_op jit(solution)/shard_map/pallas_call | solution.py:380
  58.2 1.2 %shard_map.134 = (f32[256,128]{1,0:T(8,128)S(1)}, f32[256,128]{1,0:T(8,128)S(1)}, f32[256,128]{1,0:T(8,128)S(1)}, f32[256,128]{1,0:T(8,128)S(1)}, f32[256,128]{1...) custom-call(f32[512,512]{1,0:T(8,128)S(1)} %shard_map.132.proj.refs_7_, ...), custom_call_target="tpu_custom_call" | custom-call | flops 10000000 | bytes 2097152 | tf_op jit(solution)/shard_map/pallas_call | solution.py:385
  59.5 1.7 %collective-permute-start.10 = (bf16[80,128]{1,0:T(8,128)(2,1)S(1)}, bf16[80,128]{1,0:T(8,128)(2,1)S(1)}, u32[]{:S(2)}, u32[]{:S(2)}) collective-permute-start(bf16[80,128]{1,0:T(8,128)(2,1)S(1)} %get-tuple-element.47.refs_0_), channel_id=1, source_target_pairs={{0,8},{8,0},{16,24},{24,16},{1,9},{9,1},{17,25},{25,17},{2,10},{10... | collective-permute-start | bytes 61448 | tf_op jit(solution)/shard_map/ppermute | solution.py:391
  61.1 1.7 %collective-permute-start.11 = (bf16[80,128]{1,0:T(8,128)(2,1)S(1)}, bf16[80,128]{1,0:T(8,128)(2,1)S(1)}, u32[]{:S(2)}, u32[]{:S(2)}) collective-permute-start(bf16[80,128]{1,0:T(8,128)(2,1)S(1)} %get-tuple-element.47.refs_0_), channel_id=1, source_target_pairs={{0,16},{8,24},{16,0},{24,8},{1,17},{9,25},{17,1},{25,9},{2,18},{10... | collective-permute-start | bytes 61448 | tf_op jit(solution)/shard_map/ppermute | solution.py:392
  62.8 1.1 %collective-permute-start.12 = (bf16[80,128]{1,0:T(8,128)(2,1)S(1)}, bf16[80,128]{1,0:T(8,128)(2,1)S(1)}, u32[]{:S(2)}, u32[]{:S(2)}) collective-permute-start(bf16[80,128]{1,0:T(8,128)(2,1)S(1)} %collective-permute-done.10.refs_1_), channel_id=1, source_target_pairs={{0,16},{8,24},{16,0},{24,8},{1,17},{9,25},{17,1},{25,9},{2,18},{10... | collective-permute-start | bytes 61448 | tf_op jit(solution)/shard_map/ppermute | solution.py:393
  63.9 1.0 %collective-permute-done.11.refs_2_ = bf16[80,128]{1,0:T(8,128)(2,1)S(1)} collective-permute-done((bf16[80,128]{1,0:T(8,128)(2,1)S(1)}, bf16[80,128]{1,0:T(8,128)(2,1)S(1)}, u32[]{:S(2)}, u32[]{:S(2)}) %collective-permute-start.11) | collective-permute-done | bytes 20512 | tf_op jit(solution)/shard_map/ppermute | solution.py:392
  64.9 1.7 %collective-permute-done.12.refs_3_ = bf16[80,128]{1,0:T(8,128)(2,1)S(1)} collective-permute-done((bf16[80,128]{1,0:T(8,128)(2,1)S(1)}, bf16[80,128]{1,0:T(8,128)(2,1)S(1)}, u32[]{:S(2)}, u32[]{:S(2)}) %collective-permute-start.12) | collective-permute-done | bytes 20512 | tf_op jit(solution)/shard_map/ppermute | solution.py:393
  66.6 1.6 %collective-permute-start.18 = (bf16[128,1792]{1,0:T(8,128)(2,1)}, bf16[128,1792]{1,0:T(8,128)(2,1)S(1)}, u32[]{:S(2)}, u32[]{:S(2)}) collective-permute-start(bf16[128,1792]{1,0:T(8,128)(2,1)} %collective-permute-done.15.rest_3_), channel_id=1, source_target_pairs={{0,2},{2,4},{4,6},{6,7},{7,5},{5,3},{3,1},{1,0},{8,10},{10,12},{12... | collective-permute-start | bytes 1376264 | tf_op jit(solution)/shard_map/ppermute | solution.py:31
  68.2 0.4 collective-permute-start.19
  68.6 1.8 %shard_map.135 = bf16[512,128]{1,0:T(8,128)(2,1)} custom-call(s32[1,1]{1,0:T(1,128)} %bitcast.seg_first, bf16[80,128]{1,0:T(8,128)(2,1)S(1)} %get-tuple-element.47.refs_0_, bf16[80,128]{1,0:T(8,128)(2,1)S(1)} %collective-permute-done.10.refs_1_, bf16[80,128]{1,0:T(8,128)(2,1)S(1)} %collective-permute-done.11.refs_2_, ...), custom_call_target="tpu_custom_call" | custom-call | flops 10000000 | bytes 2097152 | tf_op jit(solution)/shard_map/pallas_call | solution.py:397
  70.4 5.0 %all-to-all-start = ((bf16[8,64,128]{2,1,0:T(8,128)(2,1)}), bf16[8,64,128]{2,1,0:T(8,128)(2,1)S(1)}, u32[]{:S(2)}, u32[]{:S(2)}) async-start(bf16[8,64,128]{2,1,0:T(8,128)(2,1)} %bitcast.6), calls=%async_computation | async-start | bytes 262144 | tf_op jit(solution)/shard_map/all_to_all | solution.py:415
  75.4 3.4 %collective-permute-done.18.rest_5_.forth = bf16[128,1792]{1,0:T(8,128)(2,1)S(1)} collective-permute-done((bf16[128,1792]{1,0:T(8,128)(2,1)}, bf16[128,1792]{1,0:T(8,128)(2,1)S(1)}, u32[]{:S(2)}, u32[]{:S(2)}) %collective-permute-start.18) | collective-permute-done | bytes 458784 | tf_op jit(solution)/shard_map/ppermute | solution.py:31
  78.8 1.7 %collective-permute-done.19.rest_6_.back = bf16[128,1792]{1,0:T(8,128)(2,1)S(1)} collective-permute-done((bf16[128,1792]{1,0:T(8,128)(2,1)}, bf16[128,1792]{1,0:T(8,128)(2,1)S(1)}, u32[]{:S(2)}, u32[]{:S(2)}) %collective-permute-start.19) | collective-permute-done | bytes 458784 | tf_op jit(solution)/shard_map/ppermute | solution.py:31
  80.5 2.2 %collective-permute-start.20 = (bf16[64,1792]{1,0:T(8,128)(2,1)S(1)}, bf16[64,1792]{1,0:T(8,128)(2,1)S(1)}, u32[]{:S(2)}, u32[]{:S(2)}) collective-permute-start(bf16[64,1792]{1,0:T(8,128)(2,1)S(1)} %get-tuple-element.65), channel_id=1, source_target_pairs={{0,2},{2,4},{4,6},{6,7},{7,5},{5,3},{3,1},{1,0},{8,10},{10,12},{12... | collective-permute-start | bytes 688136 | tf_op jit(solution)/shard_map/ppermute | solution.py:31
  82.6 1.6 %all-to-all-done.mine = bf16[8,64,128]{2,1,0:T(8,128)(2,1)S(1)} async-done(((bf16[8,64,128]{2,1,0:T(8,128)(2,1)}), bf16[8,64,128]{2,1,0:T(8,128)(2,1)S(1)}, u32[]{:S(2)}, u32[]{:S(2)}) %all-to-all-start) | async-done | bytes 131104 | tf_op jit(solution)/shard_map/all_to_all | solution.py:415
  84.2 1.3 %collective-permute-done.17.other = bf16[8,64,128]{2,1,0:T(8,128)(2,1)S(1)} collective-permute-done((bf16[8,64,128]{2,1,0:T(8,128)(2,1)S(1)}, bf16[8,64,128]{2,1,0:T(8,128)(2,1)S(1)}, u32[]{:S(2)}, u32[]{:S(2)}) %collective-permute-start.17) | collective-permute-done | bytes 131104 | tf_op jit(solution)/shard_map/ppermute | solution.py:417
  85.5 2.1 %shard_map.136.total = f32[128,1792]{1,0:T(8,128)S(1)} custom-call(bf16[8,64,128]{2,1,0:T(8,128)(2,1)S(1)} %all-to-all-done.mine, bf16[8,64,128]{2,1,0:T(8,128)(2,1)S(1)} %collective-permute-done.17.other, bf16[128,1792]{1,0:T(8,128)(2,1)S(1)} %multiply_convert_fusion.rest_0_, bf16[128,1792]{1,0:T(8,128)(2,1)S(1)} %collective-permute-done.13.rest_1_, ...), custom_call_target="tpu_custom_call" | custom-call | flops 1 | bytes 1 | tf_op jit(solution)/shard_map/pallas_call | solution.py:422
  87.7 0.9 %collective-permute-done.21.bottom = bf16[64,1792]{1,0:T(8,128)(2,1)S(1)} collective-permute-done((bf16[64,1792]{1,0:T(8,128)(2,1)S(1)}, bf16[64,1792]{1,0:T(8,128)(2,1)S(1)}, u32[]{:S(2)}, u32[]{:S(2)}) %collective-permute-start.21) | collective-permute-done | bytes 229408 | tf_op jit(solution)/shard_map/ppermute | solution.py:31
  88.6 0.2 shard_map.139
  88.9 0.1 collective-permute-start.22
  88.9 1.0 %shard_map.138.whole = bf16[64,3584]{1,0:T(8,128)(2,1)} custom-call(bf16[8,64,128]{2,1,0:T(8,128)(2,1)S(1)} %all-to-all-done.mine, f32[128,1792]{1,0:T(8,128)S(1)} %shard_map.136.total, bf16[64,1792]{1,0:T(8,128)(2,1)S(1)} %collective-permute-done.20.top, bf16[64,1792]{1,0:T(8,128)(2,1)S(1)} %collective-permute-done.21.bottom), custom_call_target="tpu_custom_call" | custom-call | flops 10000000 | bytes 2097152 | tf_op jit(solution)/shard_map/pallas_call | solution.py:429
  89.9 0.5 collective-permute-done.22.arrived
  90.4 0.7 shard_map.140
  (43 shorter events, 0.3 us)
Async XLA Ops:
  0.0 5.2 %copy-start = (bf16[3584,2]{0,1:T(2,128)(2,1)S(1)}, bf16[3584,2]{0,1:T(2,128)(2,1)}, u32[]{:S(2)}) copy-start(bf16[3584,2]{0,1:T(2,128)(2,1)} %param.16) | copy-start | bytes 43012
  0.0 13.8 %collective-permute-start = (bf16[448,512]{1,0:T(8,128)(2,1)}, bf16[448,512]{1,0:T(8,128)(2,1)}, u32[]{:S(2)}, u32[]{:S(2)}) collective-permute-start(bf16[448,512]{1,0:T(8,128)(2,1)} %bitcast.10), channel_id=1, source_target_pairs={{0,2},{2,4},{4,6},{6,7},{7,5},{5,3},{3,1},{1,0},{8,10},{10,12},{12... | collective-permute-start | bytes 1376264 | tf_op jit(solution)/shard_map/ppermute | solution.py:31
  3.0 12.6 %collective-permute-start.2 = (bf16[448,512]{1,0:T(8,128)(2,1)}, bf16[448,512]{1,0:T(8,128)(2,1)S(1)}, u32[]{:S(2)}, u32[]{:S(2)}) collective-permute-start(bf16[448,512]{1,0:T(8,128)(2,1)} %bitcast.11), channel_id=1, source_target_pairs={{0,1},{2,0},{4,2},{6,4},{7,6},{5,7},{3,5},{1,3},{8,9},{10,8},{12,1... | collective-permute-start | bytes 1376264 | tf_op jit(solution)/shard_map/ppermute | solution.py:31
  3.8 13.2 %collective-permute-start.3 = (s32[8]{0:T(128)S(1)}, s32[8]{0:T(128)S(1)}, u32[]{:S(2)}, u32[]{:S(2)}) collective-permute-start(s32[8]{0:T(128)S(1)} %slice.33), channel_id=1, source_target_pairs={{0,8},{8,16},{16,24},{1,9},{9,17},{17,25},{2,10},{10,18},{18,26},{... | collective-permute-start | bytes 104 | tf_op jit(solution)/shard_map/ppermute | solution.py:333
  6.4 1.5 %copy-start.1 = (bf16[2,3584,128]{2,1,0:T(8,128)(2,1)S(1)}, bf16[2,3584,128]{2,1,0:T(8,128)(2,1)}, u32[]{:S(2)}) copy-start(bf16[2,3584,128]{2,1,0:T(8,128)(2,1)} %refs_2_.7) | copy-start | bytes 5505028
  7.9 1.2 %copy-start.2 = (bf16[3584,128]{1,0:T(8,128)(2,1)S(1)}, bf16[3584,128]{1,0:T(8,128)(2,1)}, u32[]{:S(2)}) copy-start(bf16[3584,128]{1,0:T(8,128)(2,1)} %refs_3_.5) | copy-start | bytes 2752516
  9.1 1.0 %copy-start.4 = (bf16[512,448]{0,1:T(8,128)(2,1)S(1)}, bf16[512,448]{0,1:T(8,128)(2,1)}, u32[]{:S(2)}) copy-start(bf16[512,448]{0,1:T(8,128)(2,1)} %param.13) | copy-start | bytes 1376260
  10.1 5.7 %copy-start.8 = (s32[512]{0:T(512)S(1)}, s32[512]{0:T(512)}, u32[]{:S(2)}) copy-start(s32[512]{0:T(512)} %param.24) | copy-start | bytes 6148
  10.1 6.4 %copy-start.10 = (f32[2]{0:T(128)S(1)}, f32[2]{0:T(128)}, u32[]{:S(2)}) copy-start(f32[2]{0:T(128)} %param.17) | copy-start | bytes 28
  10.1 6.6 %copy-start.11 = (f32[2]{0:T(128)S(1)}, f32[2]{0:T(128)}, u32[]{:S(2)}) copy-start(f32[2]{0:T(128)} %param.18) | copy-start | bytes 28
  10.1 6.7 %copy-start.12 = (f32[2]{0:T(128)S(1)}, f32[2]{0:T(128)}, u32[]{:S(2)}) copy-start(f32[2]{0:T(128)} %param.19) | copy-start | bytes 28
  10.1 7.0 %copy-start.3 = (bf16[3584,128]{1,0:T(8,128)(2,1)S(1)}, bf16[3584,128]{1,0:T(8,128)(2,1)}, u32[]{:S(2)}) copy-start(bf16[3584,128]{1,0:T(8,128)(2,1)} %refs_3_.5) | copy-start | bytes 2752516
  13.8 12.3 %collective-permute-start.1 = (bf16[448,512]{1,0:T(8,128)(2,1)}, bf16[448,512]{1,0:T(8,128)(2,1)}, u32[]{:S(2)}, u32[]{:S(2)}) collective-permute-start(bf16[448,512]{1,0:T(8,128)(2,1)} %collective-permute-done.refs_0_), channel_id=1, source_target_pairs={{0,2},{2,4},{4,6},{6,7},{7,5},{5,3},{3,1},{1,0},{8,10},{10,12},{12... | collective-permute-start | bytes 1376264 | tf_op jit(solution)/shard_map/ppermute | solution.py:31
  15.6 12.0 %collective-permute-start.5 = (bf16[448,512]{1,0:T(8,128)(2,1)S(1)}, bf16[448,512]{1,0:T(8,128)(2,1)}, u32[]{:S(2)}, u32[]{:S(2)}) collective-permute-start(bf16[448,512]{1,0:T(8,128)(2,1)S(1)} %collective-permute-done.2.refs_1_), channel_id=1, source_target_pairs={{0,1},{2,0},{4,2},{6,4},{7,6},{5,7},{3,5},{1,3},{8,9},{10,8},{12,1... | collective-permute-start | bytes 1376264 | tf_op jit(solution)/shard_map/ppermute | solution.py:31
  17.0 11.0 %copy-start.7 = (bf16[128,3584]{1,0:T(8,128)(2,1)S(1)}, bf16[128,3584]{1,0:T(8,128)(2,1)}, u32[]{:S(2)}) copy-start(bf16[128,3584]{1,0:T(8,128)(2,1)} %param.23) | copy-start | bytes 2752516
  17.0 11.0 %copy-start.9 = (f32[128]{0:T(128)S(1)}, f32[128]{0:T(128)}, u32[]{:S(2)}) copy-start(f32[128]{0:T(128)} %param.22) | copy-start | bytes 1540
  26.0 13.7 %collective-permute-start.4 = (bf16[448,512]{1,0:T(8,128)(2,1)}, bf16[448,512]{1,0:T(8,128)(2,1)S(1)}, u32[]{:S(2)}, u32[]{:S(2)}) collective-permute-start(bf16[448,512]{1,0:T(8,128)(2,1)} %collective-permute-done.1.refs_0_), channel_id=1, source_target_pairs={{0,2},{2,4},{4,6},{6,7},{7,5},{5,3},{3,1},{1,0},{8,10},{10,12},{12... | collective-permute-start | bytes 1376264 | tf_op jit(solution)/shard_map/ppermute | solution.py:31
  27.6 13.7 %collective-permute-start.6 = (bf16[448,512]{1,0:T(8,128)(2,1)}, bf16[448,512]{1,0:T(8,128)(2,1)S(1)}, u32[]{:S(2)}, u32[]{:S(2)}) collective-permute-start(bf16[448,512]{1,0:T(8,128)(2,1)} %collective-permute-done.5.refs_1_), channel_id=1, source_target_pairs={{0,1},{2,0},{4,2},{6,4},{7,6},{5,7},{3,5},{1,3},{8,9},{10,8},{12,1... | collective-permute-start | bytes 1376264 | tf_op jit(solution)/shard_map/ppermute | solution.py:31
  28.2 21.3 %collective-permute-start.13 = (bf16[128,1792]{1,0:T(8,128)(2,1)S(1)}, bf16[128,1792]{1,0:T(8,128)(2,1)S(1)}, u32[]{:S(2)}, u32[]{:S(2)}) collective-permute-start(bf16[128,1792]{1,0:T(8,128)(2,1)S(1)} %multiply_convert_fusion.rest_0_), channel_id=1, source_target_pairs={{0,2},{2,4},{4,6},{6,7},{7,5},{5,3},{3,1},{1,0},{8,10},{10,12},{12... | collective-permute-start | bytes 1376264 | tf_op jit(solution)/shard_map/ppermute | solution.py:31
  29.9 20.8 %collective-permute-start.14 = (bf16[128,1792]{1,0:T(8,128)(2,1)S(1)}, bf16[128,1792]{1,0:T(8,128)(2,1)S(1)}, u32[]{:S(2)}, u32[]{:S(2)}) collective-permute-start(bf16[128,1792]{1,0:T(8,128)(2,1)S(1)} %multiply_convert_fusion.rest_0_), channel_id=1, source_target_pairs={{0,1},{2,0},{4,2},{6,4},{7,6},{5,7},{3,5},{1,3},{8,9},{10,8},{12,1... | collective-permute-start | bytes 1376264 | tf_op jit(solution)/shard_map/ppermute | solution.py:31
  41.3 10.7 %collective-permute-start.7 = (bf16[224,512]{1,0:T(8,128)(2,1)S(1)}, bf16[224,512]{1,0:T(8,128)(2,1)S(1)}, u32[]{:S(2)}, u32[]{:S(2)}) collective-permute-start(bf16[224,512]{1,0:T(8,128)(2,1)S(1)} %get-tuple-element.42), channel_id=1, source_target_pairs={{0,2},{2,4},{4,6},{6,7},{7,5},{5,3},{3,1},{1,0},{8,10},{10,12},{12... | collective-permute-start | bytes 688136 | tf_op jit(solution)/shard_map/ppermute | solution.py:31
  43.0 10.1 %collective-permute-start.8 = (bf16[224,512]{1,0:T(8,128)(2,1)S(1)}, bf16[224,512]{1,0:T(8,128)(2,1)S(1)}, u32[]{:S(2)}, u32[]{:S(2)}) collective-permute-start(bf16[224,512]{1,0:T(8,128)(2,1)S(1)} %get-tuple-element.43), channel_id=1, source_target_pairs={{0,1},{2,0},{4,2},{6,4},{7,6},{5,7},{3,5},{1,3},{8,9},{10,8},{12,1... | collective-permute-start | bytes 688136 | tf_op jit(solution)/shard_map/ppermute | solution.py:31
  53.1 13.5 %collective-permute-start.15 = (bf16[128,1792]{1,0:T(8,128)(2,1)S(1)}, bf16[128,1792]{1,0:T(8,128)(2,1)}, u32[]{:S(2)}, u32[]{:S(2)}) collective-permute-start(bf16[128,1792]{1,0:T(8,128)(2,1)S(1)} %collective-permute-done.13.rest_1_), channel_id=1, source_target_pairs={{0,2},{2,4},{4,6},{6,7},{7,5},{5,3},{3,1},{1,0},{8,10},{10,12},{12... | collective-permute-start | bytes 1376264 | tf_op jit(solution)/shard_map/ppermute | solution.py:31
  54.7 11.9 %collective-permute-start.16 = (bf16[128,1792]{1,0:T(8,128)(2,1)S(1)}, bf16[128,1792]{1,0:T(8,128)(2,1)}, u32[]{:S(2)}, u32[]{:S(2)}) collective-permute-start(bf16[128,1792]{1,0:T(8,128)(2,1)S(1)} %collective-permute-done.14.rest_2_), channel_id=1, source_target_pairs={{0,1},{2,0},{4,2},{6,4},{7,6},{5,7},{3,5},{1,3},{8,9},{10,8},{12,1... | collective-permute-start | bytes 1376264 | tf_op jit(solution)/shard_map/ppermute | solution.py:31
  55.1 2.1 %copy-start.5 = (f32[4,128]{1,0:T(4,128)S(1)}, f32[4,128]{1,0:T(4,128)}, u32[]{:S(2)}) copy-start(f32[4,128]{1,0:T(4,128)} %taps_x.3) | copy-start | bytes 6148
  55.1 2.1 %copy-start.6 = (f32[4,128]{1,0:T(4,128)S(1)}, f32[4,128]{1,0:T(4,128)}, u32[]{:S(2)}) copy-start(f32[4,128]{1,0:T(4,128)} %taps_bc.3) | copy-start | bytes 6148
  55.6 2.6 %collective-permute-start.9 = (bf16[8,256]{1,0:T(8,128)(2,1)S(1)}, bf16[8,256]{1,0:T(8,128)(2,1)S(1)}, u32[]{:S(2)}, u32[]{:S(2)}) collective-permute-start(bf16[8,256]{1,0:T(8,128)(2,1)S(1)} %slice.44), channel_id=1, source_target_pairs={{0,8},{8,16},{16,24},{1,9},{9,17},{17,25},{2,10},{10,18},{18,26},{... | collective-permute-start | bytes 12296 | tf_op jit(solution)/shard_map/ppermute | solution.py:375
  59.5 3.3 %collective-permute-start.10 = (bf16[80,128]{1,0:T(8,128)(2,1)S(1)}, bf16[80,128]{1,0:T(8,128)(2,1)S(1)}, u32[]{:S(2)}, u32[]{:S(2)}) collective-permute-start(bf16[80,128]{1,0:T(8,128)(2,1)S(1)} %get-tuple-element.47.refs_0_), channel_id=1, source_target_pairs={{0,8},{8,0},{16,24},{24,16},{1,9},{9,1},{17,25},{25,17},{2,10},{10... | collective-permute-start | bytes 61448 | tf_op jit(solution)/shard_map/ppermute | solution.py:391
  61.1 3.8 %collective-permute-start.11 = (bf16[80,128]{1,0:T(8,128)(2,1)S(1)}, bf16[80,128]{1,0:T(8,128)(2,1)S(1)}, u32[]{:S(2)}, u32[]{:S(2)}) collective-permute-start(bf16[80,128]{1,0:T(8,128)(2,1)S(1)} %get-tuple-element.47.refs_0_), channel_id=1, source_target_pairs={{0,16},{8,24},{16,0},{24,8},{1,17},{9,25},{17,1},{25,9},{2,18},{10... | collective-permute-start | bytes 61448 | tf_op jit(solution)/shard_map/ppermute | solution.py:392
  62.8 3.8 %collective-permute-start.12 = (bf16[80,128]{1,0:T(8,128)(2,1)S(1)}, bf16[80,128]{1,0:T(8,128)(2,1)S(1)}, u32[]{:S(2)}, u32[]{:S(2)}) collective-permute-start(bf16[80,128]{1,0:T(8,128)(2,1)S(1)} %collective-permute-done.10.refs_1_), channel_id=1, source_target_pairs={{0,16},{8,24},{16,0},{24,8},{1,17},{9,25},{17,1},{25,9},{2,18},{10... | collective-permute-start | bytes 61448 | tf_op jit(solution)/shard_map/ppermute | solution.py:393
  66.6 12.2 %collective-permute-start.18 = (bf16[128,1792]{1,0:T(8,128)(2,1)}, bf16[128,1792]{1,0:T(8,128)(2,1)S(1)}, u32[]{:S(2)}, u32[]{:S(2)}) collective-permute-start(bf16[128,1792]{1,0:T(8,128)(2,1)} %collective-permute-done.15.rest_3_), channel_id=1, source_target_pairs={{0,2},{2,4},{4,6},{6,7},{7,5},{5,3},{3,1},{1,0},{8,10},{10,12},{12... | collective-permute-start | bytes 1376264 | tf_op jit(solution)/shard_map/ppermute | solution.py:31
  68.2 12.2 %collective-permute-start.19 = (bf16[128,1792]{1,0:T(8,128)(2,1)}, bf16[128,1792]{1,0:T(8,128)(2,1)S(1)}, u32[]{:S(2)}, u32[]{:S(2)}) collective-permute-start(bf16[128,1792]{1,0:T(8,128)(2,1)} %collective-permute-done.16.rest_4_), channel_id=1, source_target_pairs={{0,1},{2,0},{4,2},{6,4},{7,6},{5,7},{3,5},{1,3},{8,9},{10,8},{12,1... | collective-permute-start | bytes 1376264 | tf_op jit(solution)/shard_map/ppermute | solution.py:31
  70.4 13.8 %all-to-all-start = ((bf16[8,64,128]{2,1,0:T(8,128)(2,1)}), bf16[8,64,128]{2,1,0:T(8,128)(2,1)S(1)}, u32[]{:S(2)}, u32[]{:S(2)}) async-start(bf16[8,64,128]{2,1,0:T(8,128)(2,1)} %bitcast.6), calls=%async_computation | async-start | bytes 262144 | tf_op jit(solution)/shard_map/all_to_all | solution.py:415
  80.5 7.2 %collective-permute-start.20 = (bf16[64,1792]{1,0:T(8,128)(2,1)S(1)}, bf16[64,1792]{1,0:T(8,128)(2,1)S(1)}, u32[]{:S(2)}, u32[]{:S(2)}) collective-permute-start(bf16[64,1792]{1,0:T(8,128)(2,1)S(1)} %get-tuple-element.65), channel_id=1, source_target_pairs={{0,2},{2,4},{4,6},{6,7},{7,5},{5,3},{3,1},{1,0},{8,10},{10,12},{12... | collective-permute-start | bytes 688136 | tf_op jit(solution)/shard_map/ppermute | solution.py:31
  82.6 6.0 %collective-permute-start.21 = (bf16[64,1792]{1,0:T(8,128)(2,1)S(1)}, bf16[64,1792]{1,0:T(8,128)(2,1)S(1)}, u32[]{:S(2)}, u32[]{:S(2)}) collective-permute-start(bf16[64,1792]{1,0:T(8,128)(2,1)S(1)} %get-tuple-element.66), channel_id=1, source_target_pairs={{0,1},{2,0},{4,2},{6,4},{7,6},{5,7},{3,5},{1,3},{8,9},{10,8},{12,1... | collective-permute-start | bytes 688136 | tf_op jit(solution)/shard_map/ppermute | solution.py:31
  84.2 1.3 %collective-permute-start.17 = (bf16[8,64,128]{2,1,0:T(8,128)(2,1)S(1)}, bf16[8,64,128]{2,1,0:T(8,128)(2,1)S(1)}, u32[]{:S(2)}, u32[]{:S(2)}) collective-permute-start(bf16[8,64,128]{2,1,0:T(8,128)(2,1)S(1)} %all-to-all-done.mine), channel_id=1, source_target_pairs={{0,8},{8,0},{16,24},{24,16},{1,9},{9,1},{17,25},{25,17},{2,10},{10... | collective-permute-start | bytes 393224 | tf_op jit(solution)/shard_map/ppermute | solution.py:417
  88.9 1.6 %collective-permute-start.22 = (bf16[64,1792]{1,0:T(8,128)(2,1)S(1)}, bf16[64,1792]{1,0:T(8,128)(2,1)S(1)}, u32[]{:S(2)}, u32[]{:S(2)}) collective-permute-start(bf16[64,1792]{1,0:T(8,128)(2,1)S(1)} %shard_map.139), channel_id=1, source_target_pairs={{0,8},{8,0},{16,24},{24,16},{1,9},{9,1},{17,25},{25,17},{2,10},{10... | collective-permute-start | bytes 688136 | tf_op jit(solution)/shard_map/ppermute | solution.py:428

commit v26 on v25

--- a/solution.py
+++ b/solution.py
@@ -216,14 +216,20 @@
     finish_with(heads, rows, seg_first, messages, *refs)
 
 
+def stack(first, second, out):
+    out[0] = first[...]
+    out[1] = second[...]
+
+
 def message_from(messages, device):
     if len(messages) == 1:
         return messages[0][device].astype(F32)
     place = lax.axis_index("seq")
     core = place % 2 == device % 2
     plane = place // 2 == device // 2
-    own, other_core, other_plane, other_both = (m[...].astype(F32) for m in messages)
-    return jnp.where(plane, jnp.where(core, own, other_core), jnp.where(core, other_plane, other_both))
+    own, other_core, other_plane = (m[...].astype(F32) for m in messages)
+    here = jnp.where(core, own, other_core)
+    return jnp.where(plane, here, jnp.where(core, other_plane[0], other_plane[1]))
 
 
 def finish_with(heads, rows, seg_first, messages, seg_ext_a, seg_row_a, skip, proj, conv_a, bc_a, cum_a, scaled_a, enter_a,
@@ -389,9 +395,8 @@
     )(proj, halo, seg_ext_a, seg_last, state_b, conv_x, conv_bc, bias, rate)
     if n_seq == 4:
         other_core = lax.ppermute(message, "seq", [(i, i ^ 1) for i in range(n_seq)])
-        other_plane = lax.ppermute(message, "seq", [(i, i ^ 2) for i in range(n_seq)])
-        other_both = lax.ppermute(other_core, "seq", [(i, i ^ 2) for i in range(n_seq)])
-        messages = (message, other_core, other_plane, other_both)
+        chip = call(stack, shape(2, *message.shape, kind=BF16))(message, other_core)
+        messages = (message, other_core, lax.ppermute(chip, "seq", [(i, i ^ 2) for i in range(n_seq)]))
     else:
         messages = (lax.all_gather(message, "seq"),)
     gated = call(functools.partial(finish, heads, rows, len(messages)), shape(tok_rows, width, kind=BF16))(

time: 91.7 us -> 91.2 us (level)
    ppermute x2 -> x1, starting transfers between devices: 2.77 us -> 1.93 us  [local(): lax.ppermute(chip, 'seq', [(i, i ^ 2) for i in range(n_seq)])]
    ppermute x2 -> x1, waiting for transfers between devices: 2.67 us -> 2.07 us  [local(): lax.ppermute(chip, 'seq', [(i, i ^ 2) for i in range(n_seq)])]
  transfers between devices with their start and end apart: 24 -> 23, of which waited for: 16 -> 16; matrix products, arithmetic and copies ran while one was open for 4% -> 4% of each run, Pallas kernels for 18% -> 18%
where the time goes in v26:
time: 91.2 us; the launch traced here: 90.7 us
  waiting for transfers between devices  37.3 us (41%)
  starting transfers between devices  28.9 us (32%)
  Pallas kernels  17 us (19%)
  local copies, waits for them, and re-layouts  5.9 us (6%)
  matrix products  1.12 us (1%)
    ppermute x16, waiting for transfers between devices, ring_shift(): lax.ppermute(block, 'tensor', [(order[i], order[(i + step) % n]) for i in...  31.2 us
    ppermute x16, starting transfers between devices, ring_shift(): lax.ppermute(block, 'tensor', [(order[i], order[(i + step) % n]) for i in...  17.4 us
    pallas_call x4, Pallas kernels, local(): call(functools.partial(project, [distance for distance, _ in arrived], ah...  8.46 us
    all_to_all x1, starting transfers between devices, local(): mine = lax.all_to_all(blocks, 'tensor', 0, 0)  5.02 us
    unnamed x26, local copies, waits for them, and re-layouts  3.73 us
    pallas_call x1, Pallas kernels, local(): call(functools.partial(product_early, distances), shape(2 * tok_own, colu...  2.15 us
    ppermute x1, waiting for transfers between devices, local(): lax.ppermute(chip, 'seq', [(i, i ^ 2) for i in range(n_seq)])  2.07 us
    ppermute x1, starting transfers between devices, local(): lax.ppermute(chip, 'seq', [(i, i ^ 2) for i in range(n_seq)])  1.93 us
  transfers between devices with their start and end apart: 23, of which 16 were waited for; matrix products, arithmetic and copies ran while one was open for 4% of the time, Pallas kernels for 18%

profile of v26, /device:TPU:0, one launch (start us, length us, event | category | flops | bytes accessed | tf_op | source)
XLA Modules:
  0.0 90.7 jit_solution(12754670295319949299)
XLA Ops:
  0.0 3.0 %collective-permute-start = (bf16[448,512]{1,0:T(8,128)(2,1)}, bf16[448,512]{1,0:T(8,128)(2,1)}, u32[]{:S(2)}, u32[]{:S(2)}) collective-permute-start(bf16[448,512]{1,0:T(8,128)(2,1)} %bitcast.10), channel_id=1, source_target_pairs={{0,2},{2,4},{4,6},{6,7},{7,5},{5,3},{3,1},{1,0},{8,10},{10,12},{12... | collective-permute-start | bytes 1376264 | tf_op jit(solution)/shard_map/ppermute | solution.py:31
  3.0 0.8 slice.33
  3.8 1.4 %collective-permute-start.3 = (s32[8]{0:T(128)S(1)}, s32[8]{0:T(128)S(1)}, u32[]{:S(2)}, u32[]{:S(2)}) collective-permute-start(s32[8]{0:T(128)S(1)} %slice.33), channel_id=1, source_target_pairs={{0,8},{8,16},{16,24},{1,9},{9,17},{17,25},{2,10},{10,18},{18,26},{... | collective-permute-start | bytes 104 | tf_op jit(solution)/shard_map/ppermute | solution.py:339
  5.2 1.1 %convolution_bitcast_fusion.refs_3_.refs_4_ = bf16[3584,128]{1,0:T(8,128)(2,1)S(1)} fusion(bf16[2,128]{1,0:T(2,128)(2,1)} %constant.25.clone, bf16[3584,2]{0,1:T(2,128)(2,1)S(1)} %copy-done), kind=kOutput, calls=%fused_computation | convolution fusion | flops 1835008 | bytes 932352 | tf_op jit(solution)/shard_map/dot_general | solution.py:330
  6.4 1.5 %copy-done.1 = bf16[2,3584,128]{2,1,0:T(8,128)(2,1)S(1)} copy-done((bf16[2,3584,128]{2,1,0:T(8,128)(2,1)S(1)}, bf16[2,3584,128]{2,1,0:T(8,128)(2,1)}, u32[]{:S(2)}) %copy-start.1) | copy-done | bytes 1835032
  7.9 1.2 %copy-done.2 = bf16[3584,128]{1,0:T(8,128)(2,1)S(1)} copy-done((bf16[3584,128]{1,0:T(8,128)(2,1)S(1)}, bf16[3584,128]{1,0:T(8,128)(2,1)}, u32[]{:S(2)}) %copy-start.2) | copy-done | bytes 917528
  9.1 1.0 %copy-done.4 = bf16[512,448]{0,1:T(8,128)(2,1)S(1)} copy-done((bf16[512,448]{0,1:T(8,128)(2,1)S(1)}, bf16[512,448]{0,1:T(8,128)(2,1)}, u32[]{:S(2)}) %copy-start.4) | copy-done | bytes 458776
  10.1 0.6 shard_map.127.refs_5_
  10.7 3.1 %collective-permute-done.refs_0_ = bf16[448,512]{1,0:T(8,128)(2,1)} collective-permute-done((bf16[448,512]{1,0:T(8,128)(2,1)}, bf16[448,512]{1,0:T(8,128)(2,1)}, u32[]{:S(2)}, u32[]{:S(2)}) %collective-permute-start) | collective-permute-done | bytes 458784 | tf_op jit(solution)/shard_map/ppermute | solution.py:31
  13.8 1.8 %collective-permute-start.1 = (bf16[448,512]{1,0:T(8,128)(2,1)}, bf16[448,512]{1,0:T(8,128)(2,1)}, u32[]{:S(2)}, u32[]{:S(2)}) collective-permute-start(bf16[448,512]{1,0:T(8,128)(2,1)} %collective-permute-done.refs_0_), channel_id=1, source_target_pairs={{0,2},{2,4},{4,6},{6,7},{7,5},{5,3},{3,1},{1,0},{8,10},{10,12},{12... | collective-permute-start | bytes 1376264 | tf_op jit(solution)/shard_map/ppermute | solution.py:31
  15.6 0.2 collective-permute-start.5
  15.8 0.6 fusion
  16.4 0.1 slice.36
  16.5 0.1 broadcast_in_dim.27
  16.5 0.1 broadcast_in_dim_reshape.9.bias
  16.6 0.1 broadcast_in_dim.28
  16.7 0.1 broadcast_in_dim_reshape.10.rate
  16.9 0.1 broadcast_in_dim_reshape.11.skip.refs_5_
  16.9 0.1 pad_add_fusion
  17.1 3.0 %shard_map.128.refs_5_ = f32[512,512]{1,0:T(8,128)S(1)} custom-call(bf16[448,512]{1,0:T(8,128)(2,1)} %collective-permute-done.refs_0_, bf16[448,512]{1,0:T(8,128)(2,1)S(1)} %collective-permute-done.2.refs_1_, bf16[2,3584,128]{2,1,0:T(8,128)(2,1)} %refs_2_.7, bf16[3584,128]{1,0:T(8,128)(2,1)S(1)} %copy-done.3, ...), custom_call_target="tpu_custom_call" | custom-call | flops 1000000000 | bytes 2097152 | tf_op jit(solution)/shard_map/pallas_call | solution.py:367
  20.0 6.0 %collective-permute-done.1.refs_0_ = bf16[448,512]{1,0:T(8,128)(2,1)} collective-permute-done((bf16[448,512]{1,0:T(8,128)(2,1)}, bf16[448,512]{1,0:T(8,128)(2,1)}, u32[]{:S(2)}, u32[]{:S(2)}) %collective-permute-start.1) | collective-permute-done | bytes 458784 | tf_op jit(solution)/shard_map/ppermute | solution.py:31
  26.0 1.6 %collective-permute-start.4 = (bf16[448,512]{1,0:T(8,128)(2,1)}, bf16[448,512]{1,0:T(8,128)(2,1)S(1)}, u32[]{:S(2)}, u32[]{:S(2)}) collective-permute-start(bf16[448,512]{1,0:T(8,128)(2,1)} %collective-permute-done.1.refs_0_), channel_id=1, source_target_pairs={{0,2},{2,4},{4,6},{6,7},{7,5},{5,3},{3,1},{1,0},{8,10},{10,12},{12... | collective-permute-start | bytes 1376264 | tf_op jit(solution)/shard_map/ppermute | solution.py:31
  27.6 0.4 collective-permute-start.6
  28.1 0.1 multiply_convert_fusion.rest_0_
  28.2 1.6 %collective-permute-start.12 = (bf16[128,1792]{1,0:T(8,128)(2,1)S(1)}, bf16[128,1792]{1,0:T(8,128)(2,1)S(1)}, u32[]{:S(2)}, u32[]{:S(2)}) collective-permute-start(bf16[128,1792]{1,0:T(8,128)(2,1)S(1)} %multiply_convert_fusion.rest_0_), channel_id=1, source_target_pairs={{0,2},{2,4},{4,6},{6,7},{7,5},{5,3},{3,1},{1,0},{8,10},{10,12},{12... | collective-permute-start | bytes 1376264 | tf_op jit(solution)/shard_map/ppermute | solution.py:31
  29.9 0.4 collective-permute-start.13
  30.3 3.0 %shard_map.129.refs_5_ = f32[512,512]{1,0:T(8,128)S(1)} custom-call(bf16[448,512]{1,0:T(8,128)(2,1)} %collective-permute-done.1.refs_0_, bf16[448,512]{1,0:T(8,128)(2,1)} %collective-permute-done.5.refs_1_, bf16[2,3584,128]{2,1,0:T(8,128)(2,1)} %refs_2_.7, bf16[3584,128]{1,0:T(8,128)(2,1)S(1)} %copy-done.3, ...), custom_call_target="tpu_custom_call" | custom-call | flops 1000000000 | bytes 2097152 | tf_op jit(solution)/shard_map/pallas_call | solution.py:367
  33.3 6.4 %collective-permute-done.4.forth.refs_0_ = bf16[448,512]{1,0:T(8,128)(2,1)S(1)} collective-permute-done((bf16[448,512]{1,0:T(8,128)(2,1)}, bf16[448,512]{1,0:T(8,128)(2,1)S(1)}, u32[]{:S(2)}, u32[]{:S(2)}) %collective-permute-start.4) | collective-permute-done | bytes 458784 | tf_op jit(solution)/shard_map/ppermute | solution.py:31
  39.7 1.6 %collective-permute-done.6.back.refs_1_ = bf16[448,512]{1,0:T(8,128)(2,1)S(1)} collective-permute-done((bf16[448,512]{1,0:T(8,128)(2,1)}, bf16[448,512]{1,0:T(8,128)(2,1)S(1)}, u32[]{:S(2)}, u32[]{:S(2)}) %collective-permute-start.6) | collective-permute-done | bytes 458784 | tf_op jit(solution)/shard_map/ppermute | solution.py:31
  41.3 1.6 %collective-permute-start.7 = (bf16[224,512]{1,0:T(8,128)(2,1)S(1)}, bf16[224,512]{1,0:T(8,128)(2,1)S(1)}, u32[]{:S(2)}, u32[]{:S(2)}) collective-permute-start(bf16[224,512]{1,0:T(8,128)(2,1)S(1)} %get-tuple-element.42), channel_id=1, source_target_pairs={{0,2},{2,4},{4,6},{6,7},{7,5},{5,3},{3,1},{1,0},{8,10},{10,12},{12... | collective-permute-start | bytes 688136 | tf_op jit(solution)/shard_map/ppermute | solution.py:31
  43.0 0.5 collective-permute-start.8
  43.4 1.9 %shard_map.131 = (f32[512,512]{1,0:T(8,128)S(1)}, bf16[448,512]{1,0:T(8,128)(2,1)S(1)}) custom-call(bf16[448,512]{1,0:T(8,128)(2,1)S(1)} %collective-permute-done.4.forth.refs_0_, bf16[448,512]{1,0:T(8,128)(2,1)S(1)} %collective-permute-done.6.back.refs_1_, bf16[2,3584,128]{2,1,0:T(8,128)(2,1)} %refs_2_.7, bf16[3584,128]{1,0:T(8,128)(2,1)S(1)} %copy-done.3, ...), custom_call_target="tpu_custom_call" | custom-call | flops 1000000000 | bytes 2097152 | tf_op jit(solution)/shard_map/pallas_call | solution.py:367
  45.3 4.2 %collective-permute-done.12.rest_1_ = bf16[128,1792]{1,0:T(8,128)(2,1)S(1)} collective-permute-done((bf16[128,1792]{1,0:T(8,128)(2,1)S(1)}, bf16[128,1792]{1,0:T(8,128)(2,1)S(1)}, u32[]{:S(2)}, u32[]{:S(2)}) %collective-permute-start.12) | collective-permute-done | bytes 458784 | tf_op jit(solution)/shard_map/ppermute | solution.py:31
  49.5 1.1 %collective-permute-done.13.rest_2_ = bf16[128,1792]{1,0:T(8,128)(2,1)S(1)} collective-permute-done((bf16[128,1792]{1,0:T(8,128)(2,1)S(1)}, bf16[128,1792]{1,0:T(8,128)(2,1)S(1)}, u32[]{:S(2)}, u32[]{:S(2)}) %collective-permute-start.13) | collective-permute-done | bytes 458784 | tf_op jit(solution)/shard_map/ppermute | solution.py:31
  50.6 1.4 %collective-permute-done.7.top = bf16[224,512]{1,0:T(8,128)(2,1)S(1)} collective-permute-done((bf16[224,512]{1,0:T(8,128)(2,1)S(1)}, bf16[224,512]{1,0:T(8,128)(2,1)S(1)}, u32[]{:S(2)}, u32[]{:S(2)}) %collective-permute-start.7) | collective-permute-done | bytes 229408 | tf_op jit(solution)/shard_map/ppermute | solution.py:31
  52.0 1.0 %collective-permute-done.8.bottom = bf16[224,512]{1,0:T(8,128)(2,1)S(1)} collective-permute-done((bf16[224,512]{1,0:T(8,128)(2,1)S(1)}, bf16[224,512]{1,0:T(8,128)(2,1)S(1)}, u32[]{:S(2)}, u32[]{:S(2)}) %collective-permute-start.8) | collective-permute-done | bytes 229408 | tf_op jit(solution)/shard_map/ppermute | solution.py:31
  53.1 1.6 %collective-permute-start.14 = (bf16[128,1792]{1,0:T(8,128)(2,1)S(1)}, bf16[128,1792]{1,0:T(8,128)(2,1)}, u32[]{:S(2)}, u32[]{:S(2)}) collective-permute-start(bf16[128,1792]{1,0:T(8,128)(2,1)S(1)} %collective-permute-done.12.rest_1_), channel_id=1, source_target_pairs={{0,2},{2,4},{4,6},{6,7},{7,5},{5,3},{3,1},{1,0},{8,10},{10,12},{12... | collective-permute-start | bytes 1376264 | tf_op jit(solution)/shard_map/ppermute | solution.py:31
  54.7 0.5 collective-permute-start.15
  55.1 0.5 shard_map.132.proj.refs_6_
  55.6 1.3 %collective-permute-start.9 = (bf16[8,256]{1,0:T(8,128)(2,1)S(1)}, bf16[8,256]{1,0:T(8,128)(2,1)S(1)}, u32[]{:S(2)}, u32[]{:S(2)}) collective-permute-start(bf16[8,256]{1,0:T(8,128)(2,1)S(1)} %slice.44), channel_id=1, source_target_pairs={{0,8},{8,16},{16,24},{1,9},{9,17},{17,25},{2,10},{10,18},{18,26},{... | collective-permute-start | bytes 12296 | tf_op jit(solution)/shard_map/ppermute | solution.py:381
  56.9 0.1 copy.17.seg_ext
  57.1 0.1 copy.18.seg_ext.refs_3_
  57.2 1.0 %shard_map.133 = (f32[256,128]{1,0:T(8,128)S(1)}, f32[256,128]{1,0:T(8,128)S(1)}, f32[256,128]{1,0:T(8,128)S(1)}, f32[72,128]{1,0:T(8,128)S(1)}, f32[256,128]{1,0:T(8,128)S(1)}) custom-call(f32[512,512]{1,0:T(8,128)S(1)} %shard_map.132.proj.refs_6_, s32[264,1]{1,0:T(8,128)S(1)} %copy.17.seg_ext, s32[1,256]{1,0:T(1,128)S(1)} %bitcast.14, ...), custom_call_target="tpu_custom_call" | custom-call | flops 10000000 | bytes 2097152 | tf_op jit(solution)/shard_map/pallas_call | solution.py:386
  58.2 1.2 %shard_map.134 = (f32[256,128]{1,0:T(8,128)S(1)}, f32[256,128]{1,0:T(8,128)S(1)}, f32[256,128]{1,0:T(8,128)S(1)}, f32[256,128]{1,0:T(8,128)S(1)}, f32[256,128]{1...) custom-call(f32[512,512]{1,0:T(8,128)S(1)} %shard_map.132.proj.refs_6_, ...), custom_call_target="tpu_custom_call" | custom-call | flops 10000000 | bytes 2097152 | tf_op jit(solution)/shard_map/pallas_call | solution.py:391
  59.5 1.7 %collective-permute-start.10 = (bf16[80,128]{1,0:T(8,128)(2,1)S(1)}, bf16[80,128]{1,0:T(8,128)(2,1)S(1)}, u32[]{:S(2)}, u32[]{:S(2)}) collective-permute-start(bf16[80,128]{1,0:T(8,128)(2,1)S(1)} %get-tuple-element.47.first.refs_0_), channel_id=1, source_target_pairs={{0,8},{8,0},{16,24},{24,16},{1,9},{9,1},{17,25},{25,17},{2,10},{10... | collective-permute-start | bytes 61448 | tf_op jit(solution)/shard_map/ppermute | solution.py:397
  61.1 0.8 collective-permute-done.10.second.refs_1_
  62.0 1.9 %collective-permute-start.11 = (bf16[2,80,128]{2,1,0:T(8,128)(2,1)S(1)}, bf16[2,80,128]{2,1,0:T(8,128)(2,1)S(1)}, u32[]{:S(2)}, u32[]{:S(2)}) collective-permute-start(bf16[2,80,128]{2,1,0:T(8,128)(2,1)S(1)} %shard_map.135), channel_id=1, source_target_pairs={{0,16},{8,24},{16,0},{24,8},{1,17},{9,25},{17,1},{25,9},{2,18},{10... | collective-permute-start | bytes 122888 | tf_op jit(solution)/shard_map/ppermute | solution.py:399
  63.9 2.1 %collective-permute-done.11.refs_2_ = bf16[2,80,128]{2,1,0:T(8,128)(2,1)S(1)} collective-permute-done((bf16[2,80,128]{2,1,0:T(8,128)(2,1)S(1)}, bf16[2,80,128]{2,1,0:T(8,128)(2,1)S(1)}, u32[]{:S(2)}, u32[]{:S(2)}) %collective-permute-start.11) | collective-permute-done | bytes 40992 | tf_op jit(solution)/shard_map/ppermute | solution.py:399
  66.0 1.6 %collective-permute-start.17 = (bf16[128,1792]{1,0:T(8,128)(2,1)}, bf16[128,1792]{1,0:T(8,128)(2,1)S(1)}, u32[]{:S(2)}, u32[]{:S(2)}) collective-permute-start(bf16[128,1792]{1,0:T(8,128)(2,1)} %collective-permute-done.14.rest_3_), channel_id=1, source_target_pairs={{0,2},{2,4},{4,6},{6,7},{7,5},{5,3},{3,1},{1,0},{8,10},{10,12},{12... | collective-permute-start | bytes 1376264 | tf_op jit(solution)/shard_map/ppermute | solution.py:31
  67.6 0.4 collective-permute-start.18
  68.0 1.8 %shard_map.136 = bf16[512,128]{1,0:T(8,128)(2,1)} custom-call(s32[1,1]{1,0:T(1,128)} %bitcast.seg_first, bf16[80,128]{1,0:T(8,128)(2,1)S(1)} %get-tuple-element.47.first.refs_0_, bf16[80,128]{1,0:T(8,128)(2,1)S(1)} %collective-permute-done.10.second.refs_1_, bf16[2,80,128]{2,1,0:T(8,128)(2,1)S(1)} %collective-permute-done.11.refs_2_, ...), custom_call_target="tpu_custom_call" | custom-call | flops 10000000 | bytes 2097152 | tf_op jit(solution)/shard_map/pallas_call | solution.py:402
  69.8 5.0 %all-to-all-start = ((bf16[8,64,128]{2,1,0:T(8,128)(2,1)}), bf16[8,64,128]{2,1,0:T(8,128)(2,1)S(1)}, u32[]{:S(2)}, u32[]{:S(2)}) async-start(bf16[8,64,128]{2,1,0:T(8,128)(2,1)} %bitcast.6), calls=%async_computation | async-start | bytes 262144 | tf_op jit(solution)/shard_map/all_to_all | solution.py:420
  74.8 3.6 %collective-permute-done.17.rest_5_.forth = bf16[128,1792]{1,0:T(8,128)(2,1)S(1)} collective-permute-done((bf16[128,1792]{1,0:T(8,128)(2,1)}, bf16[128,1792]{1,0:T(8,128)(2,1)S(1)}, u32[]{:S(2)}, u32[]{:S(2)}) %collective-permute-start.17) | collective-permute-done | bytes 458784 | tf_op jit(solution)/shard_map/ppermute | solution.py:31
  78.4 1.7 %collective-permute-done.18.rest_6_.back = bf16[128,1792]{1,0:T(8,128)(2,1)S(1)} collective-permute-done((bf16[128,1792]{1,0:T(8,128)(2,1)}, bf16[128,1792]{1,0:T(8,128)(2,1)S(1)}, u32[]{:S(2)}, u32[]{:S(2)}) %collective-permute-start.18) | collective-permute-done | bytes 458784 | tf_op jit(solution)/shard_map/ppermute | solution.py:31
  80.0 2.2 %collective-permute-start.19 = (bf16[64,1792]{1,0:T(8,128)(2,1)S(1)}, bf16[64,1792]{1,0:T(8,128)(2,1)S(1)}, u32[]{:S(2)}, u32[]{:S(2)}) collective-permute-start(bf16[64,1792]{1,0:T(8,128)(2,1)S(1)} %get-tuple-element.65), channel_id=1, source_target_pairs={{0,2},{2,4},{4,6},{6,7},{7,5},{5,3},{3,1},{1,0},{8,10},{10,12},{12... | collective-permute-start | bytes 688136 | tf_op jit(solution)/shard_map/ppermute | solution.py:31
  82.2 1.4 %all-to-all-done.mine = bf16[8,64,128]{2,1,0:T(8,128)(2,1)S(1)} async-done(((bf16[8,64,128]{2,1,0:T(8,128)(2,1)}), bf16[8,64,128]{2,1,0:T(8,128)(2,1)S(1)}, u32[]{:S(2)}, u32[]{:S(2)}) %all-to-all-start) | async-done | bytes 131104 | tf_op jit(solution)/shard_map/all_to_all | solution.py:420
  83.6 1.3 %collective-permute-done.16.other = bf16[8,64,128]{2,1,0:T(8,128)(2,1)S(1)} collective-permute-done((bf16[8,64,128]{2,1,0:T(8,128)(2,1)S(1)}, bf16[8,64,128]{2,1,0:T(8,128)(2,1)S(1)}, u32[]{:S(2)}, u32[]{:S(2)}) %collective-permute-start.16) | collective-permute-done | bytes 131104 | tf_op jit(solution)/shard_map/ppermute | solution.py:422
  84.9 2.1 %shard_map.137.total = f32[128,1792]{1,0:T(8,128)S(1)} custom-call(bf16[8,64,128]{2,1,0:T(8,128)(2,1)S(1)} %all-to-all-done.mine, bf16[8,64,128]{2,1,0:T(8,128)(2,1)S(1)} %collective-permute-done.16.other, bf16[128,1792]{1,0:T(8,128)(2,1)S(1)} %multiply_convert_fusion.rest_0_, bf16[128,1792]{1,0:T(8,128)(2,1)S(1)} %collective-permute-done.12.rest_1_, ...), custom_call_target="tpu_custom_call" | custom-call | flops 1 | bytes 1 | tf_op jit(solution)/shard_map/pallas_call | solution.py:427
  87.1 1.1 %collective-permute-done.20.bottom = bf16[64,1792]{1,0:T(8,128)(2,1)S(1)} collective-permute-done((bf16[64,1792]{1,0:T(8,128)(2,1)S(1)}, bf16[64,1792]{1,0:T(8,128)(2,1)S(1)}, u32[]{:S(2)}, u32[]{:S(2)}) %collective-permute-start.20) | collective-permute-done | bytes 229408 | tf_op jit(solution)/shard_map/ppermute | solution.py:31
  88.2 0.2 shard_map.140
  88.4 0.1 collective-permute-start.21
  88.5 1.0 %shard_map.139.whole = bf16[64,3584]{1,0:T(8,128)(2,1)} custom-call(bf16[8,64,128]{2,1,0:T(8,128)(2,1)S(1)} %all-to-all-done.mine, f32[128,1792]{1,0:T(8,128)S(1)} %shard_map.137.total, bf16[64,1792]{1,0:T(8,128)(2,1)S(1)} %collective-permute-done.19.top, bf16[64,1792]{1,0:T(8,128)(2,1)S(1)} %collective-permute-done.20.bottom), custom_call_target="tpu_custom_call" | custom-call | flops 10000000 | bytes 2097152 | tf_op jit(solution)/shard_map/pallas_call | solution.py:434
  89.5 0.5 collective-permute-done.21.arrived
  90.0 0.7 shard_map.141
  (42 shorter events, 0.2 us)
Async XLA Ops:
  0.0 5.2 %copy-start = (bf16[3584,2]{0,1:T(2,128)(2,1)S(1)}, bf16[3584,2]{0,1:T(2,128)(2,1)}, u32[]{:S(2)}) copy-start(bf16[3584,2]{0,1:T(2,128)(2,1)} %param.16) | copy-start | bytes 43012
  0.0 13.8 %collective-permute-start = (bf16[448,512]{1,0:T(8,128)(2,1)}, bf16[448,512]{1,0:T(8,128)(2,1)}, u32[]{:S(2)}, u32[]{:S(2)}) collective-permute-start(bf16[448,512]{1,0:T(8,128)(2,1)} %bitcast.10), channel_id=1, source_target_pairs={{0,2},{2,4},{4,6},{6,7},{7,5},{5,3},{3,1},{1,0},{8,10},{10,12},{12... | collective-permute-start | bytes 1376264 | tf_op jit(solution)/shard_map/ppermute | solution.py:31
  3.0 12.6 %collective-permute-start.2 = (bf16[448,512]{1,0:T(8,128)(2,1)}, bf16[448,512]{1,0:T(8,128)(2,1)S(1)}, u32[]{:S(2)}, u32[]{:S(2)}) collective-permute-start(bf16[448,512]{1,0:T(8,128)(2,1)} %bitcast.11), channel_id=1, source_target_pairs={{0,1},{2,0},{4,2},{6,4},{7,6},{5,7},{3,5},{1,3},{8,9},{10,8},{12,1... | collective-permute-start | bytes 1376264 | tf_op jit(solution)/shard_map/ppermute | solution.py:31
  3.8 13.2 %collective-permute-start.3 = (s32[8]{0:T(128)S(1)}, s32[8]{0:T(128)S(1)}, u32[]{:S(2)}, u32[]{:S(2)}) collective-permute-start(s32[8]{0:T(128)S(1)} %slice.33), channel_id=1, source_target_pairs={{0,8},{8,16},{16,24},{1,9},{9,17},{17,25},{2,10},{10,18},{18,26},{... | collective-permute-start | bytes 104 | tf_op jit(solution)/shard_map/ppermute | solution.py:339
  6.4 1.5 %copy-start.1 = (bf16[2,3584,128]{2,1,0:T(8,128)(2,1)S(1)}, bf16[2,3584,128]{2,1,0:T(8,128)(2,1)}, u32[]{:S(2)}) copy-start(bf16[2,3584,128]{2,1,0:T(8,128)(2,1)} %refs_2_.7) | copy-start | bytes 5505028
  7.9 1.2 %copy-start.2 = (bf16[3584,128]{1,0:T(8,128)(2,1)S(1)}, bf16[3584,128]{1,0:T(8,128)(2,1)}, u32[]{:S(2)}) copy-start(bf16[3584,128]{1,0:T(8,128)(2,1)} %refs_3_.5) | copy-start | bytes 2752516
  9.1 1.0 %copy-start.4 = (bf16[512,448]{0,1:T(8,128)(2,1)S(1)}, bf16[512,448]{0,1:T(8,128)(2,1)}, u32[]{:S(2)}) copy-start(bf16[512,448]{0,1:T(8,128)(2,1)} %param.13) | copy-start | bytes 1376260
  10.1 5.7 %copy-start.8 = (s32[512]{0:T(512)S(1)}, s32[512]{0:T(512)}, u32[]{:S(2)}) copy-start(s32[512]{0:T(512)} %param.24) | copy-start | bytes 6148
  10.1 6.4 %copy-start.10 = (f32[2]{0:T(128)S(1)}, f32[2]{0:T(128)}, u32[]{:S(2)}) copy-start(f32[2]{0:T(128)} %param.17) | copy-start | bytes 28
  10.1 6.6 %copy-start.11 = (f32[2]{0:T(128)S(1)}, f32[2]{0:T(128)}, u32[]{:S(2)}) copy-start(f32[2]{0:T(128)} %param.18) | copy-start | bytes 28
  10.1 6.7 %copy-start.12 = (f32[2]{0:T(128)S(1)}, f32[2]{0:T(128)}, u32[]{:S(2)}) copy-start(f32[2]{0:T(128)} %param.19) | copy-start | bytes 28
  10.1 7.0 %copy-start.3 = (bf16[3584,128]{1,0:T(8,128)(2,1)S(1)}, bf16[3584,128]{1,0:T(8,128)(2,1)}, u32[]{:S(2)}) copy-start(bf16[3584,128]{1,0:T(8,128)(2,1)} %refs_3_.5) | copy-start | bytes 2752516
  13.8 12.3 %collective-permute-start.1 = (bf16[448,512]{1,0:T(8,128)(2,1)}, bf16[448,512]{1,0:T(8,128)(2,1)}, u32[]{:S(2)}, u32[]{:S(2)}) collective-permute-start(bf16[448,512]{1,0:T(8,128)(2,1)} %collective-permute-done.refs_0_), channel_id=1, source_target_pairs={{0,2},{2,4},{4,6},{6,7},{7,5},{5,3},{3,1},{1,0},{8,10},{10,12},{12... | collective-permute-start | bytes 1376264 | tf_op jit(solution)/shard_map/ppermute | solution.py:31
  15.6 12.0 %collective-permute-start.5 = (bf16[448,512]{1,0:T(8,128)(2,1)S(1)}, bf16[448,512]{1,0:T(8,128)(2,1)}, u32[]{:S(2)}, u32[]{:S(2)}) collective-permute-start(bf16[448,512]{1,0:T(8,128)(2,1)S(1)} %collective-permute-done.2.refs_1_), channel_id=1, source_target_pairs={{0,1},{2,0},{4,2},{6,4},{7,6},{5,7},{3,5},{1,3},{8,9},{10,8},{12,1... | collective-permute-start | bytes 1376264 | tf_op jit(solution)/shard_map/ppermute | solution.py:31
  17.0 11.0 %copy-start.7 = (bf16[128,3584]{1,0:T(8,128)(2,1)S(1)}, bf16[128,3584]{1,0:T(8,128)(2,1)}, u32[]{:S(2)}) copy-start(bf16[128,3584]{1,0:T(8,128)(2,1)} %param.23) | copy-start | bytes 2752516
  17.0 11.0 %copy-start.9 = (f32[128]{0:T(128)S(1)}, f32[128]{0:T(128)}, u32[]{:S(2)}) copy-start(f32[128]{0:T(128)} %param.22) | copy-start | bytes 1540
  26.0 13.7 %collective-permute-start.4 = (bf16[448,512]{1,0:T(8,128)(2,1)}, bf16[448,512]{1,0:T(8,128)(2,1)S(1)}, u32[]{:S(2)}, u32[]{:S(2)}) collective-permute-start(bf16[448,512]{1,0:T(8,128)(2,1)} %collective-permute-done.1.refs_0_), channel_id=1, source_target_pairs={{0,2},{2,4},{4,6},{6,7},{7,5},{5,3},{3,1},{1,0},{8,10},{10,12},{12... | collective-permute-start | bytes 1376264 | tf_op jit(solution)/shard_map/ppermute | solution.py:31
  27.6 13.7 %collective-permute-start.6 = (bf16[448,512]{1,0:T(8,128)(2,1)}, bf16[448,512]{1,0:T(8,128)(2,1)S(1)}, u32[]{:S(2)}, u32[]{:S(2)}) collective-permute-start(bf16[448,512]{1,0:T(8,128)(2,1)} %collective-permute-done.5.refs_1_), channel_id=1, source_target_pairs={{0,1},{2,0},{4,2},{6,4},{7,6},{5,7},{3,5},{1,3},{8,9},{10,8},{12,1... | collective-permute-start | bytes 1376264 | tf_op jit(solution)/shard_map/ppermute | solution.py:31
  28.2 21.3 %collective-permute-start.12 = (bf16[128,1792]{1,0:T(8,128)(2,1)S(1)}, bf16[128,1792]{1,0:T(8,128)(2,1)S(1)}, u32[]{:S(2)}, u32[]{:S(2)}) collective-permute-start(bf16[128,1792]{1,0:T(8,128)(2,1)S(1)} %multiply_convert_fusion.rest_0_), channel_id=1, source_target_pairs={{0,2},{2,4},{4,6},{6,7},{7,5},{5,3},{3,1},{1,0},{8,10},{10,12},{12... | collective-permute-start | bytes 1376264 | tf_op jit(solution)/shard_map/ppermute | solution.py:31
  29.9 20.8 %collective-permute-start.13 = (bf16[128,1792]{1,0:T(8,128)(2,1)S(1)}, bf16[128,1792]{1,0:T(8,128)(2,1)S(1)}, u32[]{:S(2)}, u32[]{:S(2)}) collective-permute-start(bf16[128,1792]{1,0:T(8,128)(2,1)S(1)} %multiply_convert_fusion.rest_0_), channel_id=1, source_target_pairs={{0,1},{2,0},{4,2},{6,4},{7,6},{5,7},{3,5},{1,3},{8,9},{10,8},{12,1... | collective-permute-start | bytes 1376264 | tf_op jit(solution)/shard_map/ppermute | solution.py:31
  41.3 10.7 %collective-permute-start.7 = (bf16[224,512]{1,0:T(8,128)(2,1)S(1)}, bf16[224,512]{1,0:T(8,128)(2,1)S(1)}, u32[]{:S(2)}, u32[]{:S(2)}) collective-permute-start(bf16[224,512]{1,0:T(8,128)(2,1)S(1)} %get-tuple-element.42), channel_id=1, source_target_pairs={{0,2},{2,4},{4,6},{6,7},{7,5},{5,3},{3,1},{1,0},{8,10},{10,12},{12... | collective-permute-start | bytes 688136 | tf_op jit(solution)/shard_map/ppermute | solution.py:31
  43.0 10.1 %collective-permute-start.8 = (bf16[224,512]{1,0:T(8,128)(2,1)S(1)}, bf16[224,512]{1,0:T(8,128)(2,1)S(1)}, u32[]{:S(2)}, u32[]{:S(2)}) collective-permute-start(bf16[224,512]{1,0:T(8,128)(2,1)S(1)} %get-tuple-element.43), channel_id=1, source_target_pairs={{0,1},{2,0},{4,2},{6,4},{7,6},{5,7},{3,5},{1,3},{8,9},{10,8},{12,1... | collective-permute-start | bytes 688136 | tf_op jit(solution)/shard_map/ppermute | solution.py:31
  53.1 12.9 %collective-permute-start.14 = (bf16[128,1792]{1,0:T(8,128)(2,1)S(1)}, bf16[128,1792]{1,0:T(8,128)(2,1)}, u32[]{:S(2)}, u32[]{:S(2)}) collective-permute-start(bf16[128,1792]{1,0:T(8,128)(2,1)S(1)} %collective-permute-done.12.rest_1_), channel_id=1, source_target_pairs={{0,2},{2,4},{4,6},{6,7},{7,5},{5,3},{3,1},{1,0},{8,10},{10,12},{12... | collective-permute-start | bytes 1376264 | tf_op jit(solution)/shard_map/ppermute | solution.py:31
  54.7 11.3 %collective-permute-start.15 = (bf16[128,1792]{1,0:T(8,128)(2,1)S(1)}, bf16[128,1792]{1,0:T(8,128)(2,1)}, u32[]{:S(2)}, u32[]{:S(2)}) collective-permute-start(bf16[128,1792]{1,0:T(8,128)(2,1)S(1)} %collective-permute-done.13.rest_2_), channel_id=1, source_target_pairs={{0,1},{2,0},{4,2},{6,4},{7,6},{5,7},{3,5},{1,3},{8,9},{10,8},{12,1... | collective-permute-start | bytes 1376264 | tf_op jit(solution)/shard_map/ppermute | solution.py:31
  55.1 2.1 %copy-start.5 = (f32[4,128]{1,0:T(4,128)S(1)}, f32[4,128]{1,0:T(4,128)}, u32[]{:S(2)}) copy-start(f32[4,128]{1,0:T(4,128)} %taps_x.3) | copy-start | bytes 6148
  55.1 2.1 %copy-start.6 = (f32[4,128]{1,0:T(4,128)S(1)}, f32[4,128]{1,0:T(4,128)}, u32[]{:S(2)}) copy-start(f32[4,128]{1,0:T(4,128)} %taps_bc.3) | copy-start | bytes 6148
  55.6 2.6 %collective-permute-start.9 = (bf16[8,256]{1,0:T(8,128)(2,1)S(1)}, bf16[8,256]{1,0:T(8,128)(2,1)S(1)}, u32[]{:S(2)}, u32[]{:S(2)}) collective-permute-start(bf16[8,256]{1,0:T(8,128)(2,1)S(1)} %slice.44), channel_id=1, source_target_pairs={{0,8},{8,16},{16,24},{1,9},{9,17},{17,25},{2,10},{10,18},{18,26},{... | collective-permute-start | bytes 12296 | tf_op jit(solution)/shard_map/ppermute | solution.py:381
  59.5 2.5 %collective-permute-start.10 = (bf16[80,128]{1,0:T(8,128)(2,1)S(1)}, bf16[80,128]{1,0:T(8,128)(2,1)S(1)}, u32[]{:S(2)}, u32[]{:S(2)}) collective-permute-start(bf16[80,128]{1,0:T(8,128)(2,1)S(1)} %get-tuple-element.47.first.refs_0_), channel_id=1, source_target_pairs={{0,8},{8,0},{16,24},{24,16},{1,9},{9,1},{17,25},{25,17},{2,10},{10... | collective-permute-start | bytes 61448 | tf_op jit(solution)/shard_map/ppermute | solution.py:397
  62.0 4.0 %collective-permute-start.11 = (bf16[2,80,128]{2,1,0:T(8,128)(2,1)S(1)}, bf16[2,80,128]{2,1,0:T(8,128)(2,1)S(1)}, u32[]{:S(2)}, u32[]{:S(2)}) collective-permute-start(bf16[2,80,128]{2,1,0:T(8,128)(2,1)S(1)} %shard_map.135), channel_id=1, source_target_pairs={{0,16},{8,24},{16,0},{24,8},{1,17},{9,25},{17,1},{25,9},{2,18},{10... | collective-permute-start | bytes 122888 | tf_op jit(solution)/shard_map/ppermute | solution.py:399
  66.0 12.4 %collective-permute-start.17 = (bf16[128,1792]{1,0:T(8,128)(2,1)}, bf16[128,1792]{1,0:T(8,128)(2,1)S(1)}, u32[]{:S(2)}, u32[]{:S(2)}) collective-permute-start(bf16[128,1792]{1,0:T(8,128)(2,1)} %collective-permute-done.14.rest_3_), channel_id=1, source_target_pairs={{0,2},{2,4},{4,6},{6,7},{7,5},{5,3},{3,1},{1,0},{8,10},{10,12},{12... | collective-permute-start | bytes 1376264 | tf_op jit(solution)/shard_map/ppermute | solution.py:31
  67.6 12.4 %collective-permute-start.18 = (bf16[128,1792]{1,0:T(8,128)(2,1)}, bf16[128,1792]{1,0:T(8,128)(2,1)S(1)}, u32[]{:S(2)}, u32[]{:S(2)}) collective-permute-start(bf16[128,1792]{1,0:T(8,128)(2,1)} %collective-permute-done.15.rest_4_), channel_id=1, source_target_pairs={{0,1},{2,0},{4,2},{6,4},{7,6},{5,7},{3,5},{1,3},{8,9},{10,8},{12,1... | collective-permute-start | bytes 1376264 | tf_op jit(solution)/shard_map/ppermute | solution.py:31
  69.8 13.8 %all-to-all-start = ((bf16[8,64,128]{2,1,0:T(8,128)(2,1)}), bf16[8,64,128]{2,1,0:T(8,128)(2,1)S(1)}, u32[]{:S(2)}, u32[]{:S(2)}) async-start(bf16[8,64,128]{2,1,0:T(8,128)(2,1)} %bitcast.6), calls=%async_computation | async-start | bytes 262144 | tf_op jit(solution)/shard_map/all_to_all | solution.py:420
  80.0 7.1 %collective-permute-start.19 = (bf16[64,1792]{1,0:T(8,128)(2,1)S(1)}, bf16[64,1792]{1,0:T(8,128)(2,1)S(1)}, u32[]{:S(2)}, u32[]{:S(2)}) collective-permute-start(bf16[64,1792]{1,0:T(8,128)(2,1)S(1)} %get-tuple-element.65), channel_id=1, source_target_pairs={{0,2},{2,4},{4,6},{6,7},{7,5},{5,3},{3,1},{1,0},{8,10},{10,12},{12... | collective-permute-start | bytes 688136 | tf_op jit(solution)/shard_map/ppermute | solution.py:31
  82.2 6.0 %collective-permute-start.20 = (bf16[64,1792]{1,0:T(8,128)(2,1)S(1)}, bf16[64,1792]{1,0:T(8,128)(2,1)S(1)}, u32[]{:S(2)}, u32[]{:S(2)}) collective-permute-start(bf16[64,1792]{1,0:T(8,128)(2,1)S(1)} %get-tuple-element.66), channel_id=1, source_target_pairs={{0,1},{2,0},{4,2},{6,4},{7,6},{5,7},{3,5},{1,3},{8,9},{10,8},{12,1... | collective-permute-start | bytes 688136 | tf_op jit(solution)/shard_map/ppermute | solution.py:31
  83.6 1.3 %collective-permute-start.16 = (bf16[8,64,128]{2,1,0:T(8,128)(2,1)S(1)}, bf16[8,64,128]{2,1,0:T(8,128)(2,1)S(1)}, u32[]{:S(2)}, u32[]{:S(2)}) collective-permute-start(bf16[8,64,128]{2,1,0:T(8,128)(2,1)S(1)} %all-to-all-done.mine), channel_id=1, source_target_pairs={{0,8},{8,0},{16,24},{24,16},{1,9},{9,1},{17,25},{25,17},{2,10},{10... | collective-permute-start | bytes 393224 | tf_op jit(solution)/shard_map/ppermute | solution.py:422
  88.4 1.6 %collective-permute-start.21 = (bf16[64,1792]{1,0:T(8,128)(2,1)S(1)}, bf16[64,1792]{1,0:T(8,128)(2,1)S(1)}, u32[]{:S(2)}, u32[]{:S(2)}) collective-permute-start(bf16[64,1792]{1,0:T(8,128)(2,1)S(1)} %shard_map.140), channel_id=1, source_target_pairs={{0,8},{8,0},{16,24},{24,16},{1,9},{9,1},{17,25},{25,17},{2,10},{10... | collective-permute-start | bytes 688136 | tf_op jit(solution)/shard_map/ppermute | solution.py:433
